TPU v7x, 32 devices: a whole 2x2x4 slice. The times are simulated.
32 devices in a mesh: ctx: 8 (over z, y), tp: 4 (over x, core).
Axes of the slice: x: 2, y: 2, z: 4, core: 2. Of those that a mesh axis runs over, the one named last changes fastest.
Arguments:
- queries: bfloat16 [4096, 4096], P('ctx', 'tp'), may hold values from -6 to 6
- keys: bfloat16 [4096, 512], P('ctx', 'tp'), may hold values from -6 to 6
- values: bfloat16 [4096, 512], P('ctx', 'tp'), may hold values from -6 to 6
- out_weight: bfloat16 [4096, 8192], P('tp'), may hold values from -0.75 to 0.75
- vertical: int32 [32, 16], P('tp'), may hold values from 0 to 63, as said below
- slash: int32 [32, 8], P('tp'), may hold values from 0 to 15, as said below
Outputs:
- projected: bfloat16 [4096, 8192], P(('ctx', 'tp'))
Inputs may be any that keep to these rules, and one draw needn't show every extreme that they name: `vertical`: each head's 16 blocks are distinct. For each index of tp, the blocks named by its 8 heads include at most 2 blocks of any one ctx shard of 512 tokens, and exactly 2 of some shard. `slash`: each head's first offset is 0 and its 8 offsets are distinct.
All inputs are finite; a program needn't handle non-finite values.
Results may differ from a plain program's by a relative error of at most 0.013.
Values may be sent and summed in bfloat16 or wider, within the bound.
No kernel may reach another device: no remote copies, remote signals or barrier semaphores. Data moves between devices by JAX's collectives and lax.ppermute only.
A program may use at most 128 MiB of HBM per device.

v0:
```python
import jax
import jax.numpy as jnp
from jax import lax
from jax.sharding import PartitionSpec as P

HS = 128
BLK = 64


def slot_table(vert_row, slash_row, query_blocks):
    block_count = query_blocks.shape[0]
    column_ids = query_blocks[:, None]
    vert_blocks = jnp.broadcast_to(vert_row[None, :], (block_count, vert_row.shape[0]))
    vert_ok = vert_blocks <= column_ids
    slash_blocks = column_ids - slash_row[None, :]
    repeated = jnp.any(slash_blocks[:, :, None] == vert_row[None, None, :], axis=2)
    slash_ok = (slash_blocks >= 0) & jnp.logical_not(repeated)
    blocks = jnp.concatenate([vert_blocks, slash_blocks], axis=1)
    usable = jnp.concatenate([vert_ok, slash_ok], axis=1)
    return (blocks, usable)


def attend(head_query, key_tiles, value_tiles, blocks, usable, query_blocks):
    block_len = head_query.shape[1]
    score_scale = 1.0 / jnp.sqrt(jnp.float32(head_query.shape[2]))
    scores = (
        jnp.einsum("ibd,isjd->ibsj", head_query, key_tiles, preferred_element_type=jnp.float32)
        * score_scale
    )
    diagonal = blocks == query_blocks[:, None]
    positions = jnp.arange(block_len, dtype=jnp.int32)
    above_diag = positions[None, :] > positions[:, None]
    blocked = (
        jnp.logical_not(usable)[:, None, :, None]
        | diagonal[:, None, :, None] & above_diag[None, :, None, :]
    )
    scores = jnp.where(blocked, jnp.float32(-1e30), scores)
    row_max = jnp.max(scores, axis=(2, 3), keepdims=True)
    weights = jnp.exp(scores - row_max)
    row_total = jnp.sum(weights, axis=(2, 3))
    rounded_probs = weights.astype(jnp.bfloat16)
    attended = jnp.einsum(
        "ibsj,isjd->ibd", rounded_probs, value_tiles, preferred_element_type=jnp.float32
    )
    return (attended / row_total[:, :, None]).astype(jnp.bfloat16)


def shards(queries, keys, values, out_weight, vertical, slash):
    local_rows = queries.shape[0]
    local_heads = vertical.shape[0]
    local_blocks = local_rows // BLK
    ctx_rank = lax.axis_index("ctx")
    keyvals = jnp.concatenate([keys, values], axis=1).reshape(local_blocks, BLK, 2 * HS)
    first_block = ctx_rank * local_blocks
    query_blocks = first_block + jnp.arange(local_blocks, dtype=jnp.int32)
    source = lax.all_gather(keyvals, "ctx", axis=0, tiled=True)

    def locate(blocks):
        return jnp.clip(blocks, 0, source.shape[0] - 1)

    head_queries = queries.reshape(local_blocks, BLK, local_heads, HS).transpose(2, 0, 1, 3)

    def one_head(inputs):
        head_query, vert_row, slash_row = inputs
        blocks, usable = slot_table(vert_row, slash_row, query_blocks)
        chosen = source[locate(blocks)]
        return attend(head_query, chosen[..., :HS], chosen[..., HS:], blocks, usable, query_blocks)

    heads_out = lax.map(one_head, (head_queries, vertical, slash))
    attended = heads_out.transpose(1, 2, 0, 3).reshape(local_rows, local_heads * HS)
    product = jnp.dot(attended, out_weight, preferred_element_type=jnp.float32)
    return lax.psum_scatter(
        lax.optimization_barrier(product.astype(jnp.bfloat16))
        .astype(jnp.float32)
        .astype(jnp.bfloat16),
        "tp",
        scatter_dimension=0,
        tiled=True,
    )


def solution(mesh):
    return jax.shard_map(
        shards,
        mesh=mesh,
        in_specs=(
            P("ctx", "tp"),
            P("ctx", "tp"),
            P("ctx", "tp"),
            P("tp", None),
            P("tp", None),
            P("tp", None),
        ),
        out_specs=P(("ctx", "tp"), None),
        check_vma=False,
    )
```

profile of v0, /device:TPU:16, one launch (start us, length us, event | category | flops | bytes accessed | tf_op | source)
XLA Modules:
  0.0 331.5 jit_solution(13588827198661412802)
XLA Ops:
  6.5 1.7 pad_maximum_fusion
  8.3 1.5 copy.21
  10.2 49.1 %all-gather.2.cloned.1.call-done = bf16[64,64,256]{2,1,0:T(8,128)(2,1)} async-done(((bf16[8,64,256]{2,1,0:T(8,128)(2,1)}), bf16[64,64,256]{2,1,0:T(8,128)(2,1)}) %all-gather.2.cloned.1.call-update) | async-done | bytes 2097168 | tf_op jit(solution)/shard_map/all_gather | solution.py:56
  59.3 176.9 %while.11 = (s32[]{:T(128)}, bf16[8,8,64,128]{3,2,1,0:T(8,128)(2,1)S(1)}, s32[8,16]{1,0:T(8,128)}, s32[8,8]{1,0:T(8,128)}, bf16[8,8,64,128]{3,2,1,0:T(8,128)(2,1...) while((s32[]{:T(128)}, bf16[8,8,64,128]{3,2,1,0:T(8,128)(2,1)S(1)}, ...), condition=%wide.region_4.5_spmd.clone, body=%wide.region_0.4_spmd.clone.sunk | while | flops 416161856 | bytes 50649856 | solution.py:69
  59.3 0.7 fusion.59
  61.4 9.6 %gather_fusion = bf16[192,64,256]{2,1,0:T(8,128)(2,1)} fusion(bf16[64,64,256]{2,1,0:T(8,128)(2,1)} %get-tuple-element.179, s32[1024]{0:T(1024)S(1)} %pad_clamp_fusion.2), kind=kCustom, calls=%fused_computation.clone.clone.1 | custom fusion | bytes 12583680 | tf_op jit(solution)/shard_map/while/body/eval_jaxpr/gather | solution.py:66
  71.1 4.4 %fusion.61 = (f32[8,64]{1,0:T(8,128)S(1)}, f32[8,64,24,64]{1,3,2,0:T(8,128)S(1)}) fusion(pred[64,64]{0,1:T(8,128)(4,1)S(1)} %iota_compare_fusion.2, pred[8,24]{1,0:T(8,128)(4,1)S(1)} %get-tuple-element.152, pred[8,24]{1,0:T(8,128)(4,1)S(1)} %get-tuple-element.153, bf16[8,24,64,256]{3,2,1,0:T(8,128)(2,1)} %bitcast.59, ...), kind=kOutput, calls=%fused_computation.6.clone.1 | convolution fusion | flops 205258240 | bytes 6435328 | tf_op jit(solution)/shard_map/while/body/eval_jaxpr/ibd,isjd->ibsj/dot_general | solution.py:27
  75.5 2.5 fusion.62
  78.0 3.4 %fusion.63 = bf16[8,8,64,128]{3,2,1,0:T(8,128)(2,1)S(1)} fusion(bf16[8,8,64,128]{3,2,1,0:T(8,128)(2,1)S(1)} %get-tuple-element.166, s32[]{:T(128)} %get-tuple-element.165, bf16[8,24,64,256]{3,2,1,0:T(8,128)(2,1)S(1)} %bitcast.62, f32[8,64,24,64]{1,3,2,0:T(8,128)S(1)} %get-tuple-element.154, f32[8,64]{1,0:T(8,128)S(1)} %get-tuple-element.155, ...), kind=kOutput, calls=%fused_computation.20.clone.1 | convolution fusion | flops 206176256 | bytes 9586692 | tf_op jit(solution)/shard_map/while/body/eval_jaxpr/ibsj,isjd->ibd/dot_general | solution.py:42
  81.4 0.7 fusion.59
  82.2 0.7 fusion.60
  83.6 9.6 %gather_fusion = bf16[192,64,256]{2,1,0:T(8,128)(2,1)} fusion(bf16[64,64,256]{2,1,0:T(8,128)(2,1)} %get-tuple-element.179, s32[1024]{0:T(1024)S(1)} %pad_clamp_fusion.2), kind=kCustom, calls=%fused_computation.clone.clone.1 | custom fusion | bytes 12583680 | tf_op jit(solution)/shard_map/while/body/eval_jaxpr/gather | solution.py:66
  93.2 4.4 %fusion.61 = (f32[8,64]{1,0:T(8,128)S(1)}, f32[8,64,24,64]{1,3,2,0:T(8,128)S(1)}) fusion(pred[64,64]{0,1:T(8,128)(4,1)S(1)} %iota_compare_fusion.2, pred[8,24]{1,0:T(8,128)(4,1)S(1)} %get-tuple-element.152, pred[8,24]{1,0:T(8,128)(4,1)S(1)} %get-tuple-element.153, bf16[8,24,64,256]{3,2,1,0:T(8,128)(2,1)} %bitcast.59, ...), kind=kOutput, calls=%fused_computation.6.clone.1 | convolution fusion | flops 205258240 | bytes 6435328 | tf_op jit(solution)/shard_map/while/body/eval_jaxpr/ibd,isjd->ibsj/dot_general | solution.py:27
  97.6 2.5 fusion.62
  100.1 3.4 %fusion.63 = bf16[8,8,64,128]{3,2,1,0:T(8,128)(2,1)S(1)} fusion(bf16[8,8,64,128]{3,2,1,0:T(8,128)(2,1)S(1)} %get-tuple-element.166, s32[]{:T(128)} %get-tuple-element.165, bf16[8,24,64,256]{3,2,1,0:T(8,128)(2,1)S(1)} %bitcast.62, f32[8,64,24,64]{1,3,2,0:T(8,128)S(1)} %get-tuple-element.154, f32[8,64]{1,0:T(8,128)S(1)} %get-tuple-element.155, ...), kind=kOutput, calls=%fused_computation.20.clone.1 | convolution fusion | flops 206176256 | bytes 9586692 | tf_op jit(solution)/shard_map/while/body/eval_jaxpr/ibsj,isjd->ibd/dot_general | solution.py:42
  103.5 0.7 fusion.59
  105.7 9.6 %gather_fusion = bf16[192,64,256]{2,1,0:T(8,128)(2,1)} fusion(bf16[64,64,256]{2,1,0:T(8,128)(2,1)} %get-tuple-element.179, s32[1024]{0:T(1024)S(1)} %pad_clamp_fusion.2), kind=kCustom, calls=%fused_computation.clone.clone.1 | custom fusion | bytes 12583680 | tf_op jit(solution)/shard_map/while/body/eval_jaxpr/gather | solution.py:66
  115.4 4.4 %fusion.61 = (f32[8,64]{1,0:T(8,128)S(1)}, f32[8,64,24,64]{1,3,2,0:T(8,128)S(1)}) fusion(pred[64,64]{0,1:T(8,128)(4,1)S(1)} %iota_compare_fusion.2, pred[8,24]{1,0:T(8,128)(4,1)S(1)} %get-tuple-element.152, pred[8,24]{1,0:T(8,128)(4,1)S(1)} %get-tuple-element.153, bf16[8,24,64,256]{3,2,1,0:T(8,128)(2,1)} %bitcast.59, ...), kind=kOutput, calls=%fused_computation.6.clone.1 | convolution fusion | flops 205258240 | bytes 6435328 | tf_op jit(solution)/shard_map/while/body/eval_jaxpr/ibd,isjd->ibsj/dot_general | solution.py:27
  119.7 2.5 fusion.62
  122.3 3.4 %fusion.63 = bf16[8,8,64,128]{3,2,1,0:T(8,128)(2,1)S(1)} fusion(bf16[8,8,64,128]{3,2,1,0:T(8,128)(2,1)S(1)} %get-tuple-element.166, s32[]{:T(128)} %get-tuple-element.165, bf16[8,24,64,256]{3,2,1,0:T(8,128)(2,1)S(1)} %bitcast.62, f32[8,64,24,64]{1,3,2,0:T(8,128)S(1)} %get-tuple-element.154, f32[8,64]{1,0:T(8,128)S(1)} %get-tuple-element.155, ...), kind=kOutput, calls=%fused_computation.20.clone.1 | convolution fusion | flops 206176256 | bytes 9586692 | tf_op jit(solution)/shard_map/while/body/eval_jaxpr/ibsj,isjd->ibd/dot_general | solution.py:42
  125.6 0.7 fusion.59
  127.8 9.6 %gather_fusion = bf16[192,64,256]{2,1,0:T(8,128)(2,1)} fusion(bf16[64,64,256]{2,1,0:T(8,128)(2,1)} %get-tuple-element.179, s32[1024]{0:T(1024)S(1)} %pad_clamp_fusion.2), kind=kCustom, calls=%fused_computation.clone.clone.1 | custom fusion | bytes 12583680 | tf_op jit(solution)/shard_map/while/body/eval_jaxpr/gather | solution.py:66
  137.5 4.4 %fusion.61 = (f32[8,64]{1,0:T(8,128)S(1)}, f32[8,64,24,64]{1,3,2,0:T(8,128)S(1)}) fusion(pred[64,64]{0,1:T(8,128)(4,1)S(1)} %iota_compare_fusion.2, pred[8,24]{1,0:T(8,128)(4,1)S(1)} %get-tuple-element.152, pred[8,24]{1,0:T(8,128)(4,1)S(1)} %get-tuple-element.153, bf16[8,24,64,256]{3,2,1,0:T(8,128)(2,1)} %bitcast.59, ...), kind=kOutput, calls=%fused_computation.6.clone.1 | convolution fusion | flops 205258240 | bytes 6435328 | tf_op jit(solution)/shard_map/while/body/eval_jaxpr/ibd,isjd->ibsj/dot_general | solution.py:27
  141.9 2.5 fusion.62
  144.4 3.4 %fusion.63 = bf16[8,8,64,128]{3,2,1,0:T(8,128)(2,1)S(1)} fusion(bf16[8,8,64,128]{3,2,1,0:T(8,128)(2,1)S(1)} %get-tuple-element.166, s32[]{:T(128)} %get-tuple-element.165, bf16[8,24,64,256]{3,2,1,0:T(8,128)(2,1)S(1)} %bitcast.62, f32[8,64,24,64]{1,3,2,0:T(8,128)S(1)} %get-tuple-element.154, f32[8,64]{1,0:T(8,128)S(1)} %get-tuple-element.155, ...), kind=kOutput, calls=%fused_computation.20.clone.1 | convolution fusion | flops 206176256 | bytes 9586692 | tf_op jit(solution)/shard_map/while/body/eval_jaxpr/ibsj,isjd->ibd/dot_general | solution.py:42
  147.7 0.7 fusion.59
  149.9 9.6 %gather_fusion = bf16[192,64,256]{2,1,0:T(8,128)(2,1)} fusion(bf16[64,64,256]{2,1,0:T(8,128)(2,1)} %get-tuple-element.179, s32[1024]{0:T(1024)S(1)} %pad_clamp_fusion.2), kind=kCustom, calls=%fused_computation.clone.clone.1 | custom fusion | bytes 12583680 | tf_op jit(solution)/shard_map/while/body/eval_jaxpr/gather | solution.py:66
  159.6 4.4 %fusion.61 = (f32[8,64]{1,0:T(8,128)S(1)}, f32[8,64,24,64]{1,3,2,0:T(8,128)S(1)}) fusion(pred[64,64]{0,1:T(8,128)(4,1)S(1)} %iota_compare_fusion.2, pred[8,24]{1,0:T(8,128)(4,1)S(1)} %get-tuple-element.152, pred[8,24]{1,0:T(8,128)(4,1)S(1)} %get-tuple-element.153, bf16[8,24,64,256]{3,2,1,0:T(8,128)(2,1)} %bitcast.59, ...), kind=kOutput, calls=%fused_computation.6.clone.1 | convolution fusion | flops 205258240 | bytes 6435328 | tf_op jit(solution)/shard_map/while/body/eval_jaxpr/ibd,isjd->ibsj/dot_general | solution.py:27
  164.0 2.5 fusion.62
  166.5 3.4 %fusion.63 = bf16[8,8,64,128]{3,2,1,0:T(8,128)(2,1)S(1)} fusion(bf16[8,8,64,128]{3,2,1,0:T(8,128)(2,1)S(1)} %get-tuple-element.166, s32[]{:T(128)} %get-tuple-element.165, bf16[8,24,64,256]{3,2,1,0:T(8,128)(2,1)S(1)} %bitcast.62, f32[8,64,24,64]{1,3,2,0:T(8,128)S(1)} %get-tuple-element.154, f32[8,64]{1,0:T(8,128)S(1)} %get-tuple-element.155, ...), kind=kOutput, calls=%fused_computation.20.clone.1 | convolution fusion | flops 206176256 | bytes 9586692 | tf_op jit(solution)/shard_map/while/body/eval_jaxpr/ibsj,isjd->ibd/dot_general | solution.py:42
  169.9 0.7 fusion.59
  172.0 9.6 %gather_fusion = bf16[192,64,256]{2,1,0:T(8,128)(2,1)} fusion(bf16[64,64,256]{2,1,0:T(8,128)(2,1)} %get-tuple-element.179, s32[1024]{0:T(1024)S(1)} %pad_clamp_fusion.2), kind=kCustom, calls=%fused_computation.clone.clone.1 | custom fusion | bytes 12583680 | tf_op jit(solution)/shard_map/while/body/eval_jaxpr/gather | solution.py:66
  181.7 4.4 %fusion.61 = (f32[8,64]{1,0:T(8,128)S(1)}, f32[8,64,24,64]{1,3,2,0:T(8,128)S(1)}) fusion(pred[64,64]{0,1:T(8,128)(4,1)S(1)} %iota_compare_fusion.2, pred[8,24]{1,0:T(8,128)(4,1)S(1)} %get-tuple-element.152, pred[8,24]{1,0:T(8,128)(4,1)S(1)} %get-tuple-element.153, bf16[8,24,64,256]{3,2,1,0:T(8,128)(2,1)} %bitcast.59, ...), kind=kOutput, calls=%fused_computation.6.clone.1 | convolution fusion | flops 205258240 | bytes 6435328 | tf_op jit(solution)/shard_map/while/body/eval_jaxpr/ibd,isjd->ibsj/dot_general | solution.py:27
  186.1 2.5 fusion.62
  188.6 3.4 %fusion.63 = bf16[8,8,64,128]{3,2,1,0:T(8,128)(2,1)S(1)} fusion(bf16[8,8,64,128]{3,2,1,0:T(8,128)(2,1)S(1)} %get-tuple-element.166, s32[]{:T(128)} %get-tuple-element.165, bf16[8,24,64,256]{3,2,1,0:T(8,128)(2,1)S(1)} %bitcast.62, f32[8,64,24,64]{1,3,2,0:T(8,128)S(1)} %get-tuple-element.154, f32[8,64]{1,0:T(8,128)S(1)} %get-tuple-element.155, ...), kind=kOutput, calls=%fused_computation.20.clone.1 | convolution fusion | flops 206176256 | bytes 9586692 | tf_op jit(solution)/shard_map/while/body/eval_jaxpr/ibsj,isjd->ibd/dot_general | solution.py:42
  192.0 0.7 fusion.59
  194.2 9.6 %gather_fusion = bf16[192,64,256]{2,1,0:T(8,128)(2,1)} fusion(bf16[64,64,256]{2,1,0:T(8,128)(2,1)} %get-tuple-element.179, s32[1024]{0:T(1024)S(1)} %pad_clamp_fusion.2), kind=kCustom, calls=%fused_computation.clone.clone.1 | custom fusion | bytes 12583680 | tf_op jit(solution)/shard_map/while/body/eval_jaxpr/gather | solution.py:66
  203.8 4.4 %fusion.61 = (f32[8,64]{1,0:T(8,128)S(1)}, f32[8,64,24,64]{1,3,2,0:T(8,128)S(1)}) fusion(pred[64,64]{0,1:T(8,128)(4,1)S(1)} %iota_compare_fusion.2, pred[8,24]{1,0:T(8,128)(4,1)S(1)} %get-tuple-element.152, pred[8,24]{1,0:T(8,128)(4,1)S(1)} %get-tuple-element.153, bf16[8,24,64,256]{3,2,1,0:T(8,128)(2,1)} %bitcast.59, ...), kind=kOutput, calls=%fused_computation.6.clone.1 | convolution fusion | flops 205258240 | bytes 6435328 | tf_op jit(solution)/shard_map/while/body/eval_jaxpr/ibd,isjd->ibsj/dot_general | solution.py:27
  208.2 2.5 fusion.62
  210.7 3.4 %fusion.63 = bf16[8,8,64,128]{3,2,1,0:T(8,128)(2,1)S(1)} fusion(bf16[8,8,64,128]{3,2,1,0:T(8,128)(2,1)S(1)} %get-tuple-element.166, s32[]{:T(128)} %get-tuple-element.165, bf16[8,24,64,256]{3,2,1,0:T(8,128)(2,1)S(1)} %bitcast.62, f32[8,64,24,64]{1,3,2,0:T(8,128)S(1)} %get-tuple-element.154, f32[8,64]{1,0:T(8,128)S(1)} %get-tuple-element.155, ...), kind=kOutput, calls=%fused_computation.20.clone.1 | convolution fusion | flops 206176256 | bytes 9586692 | tf_op jit(solution)/shard_map/while/body/eval_jaxpr/ibsj,isjd->ibd/dot_general | solution.py:42
  214.1 0.7 fusion.59
  216.3 9.6 %gather_fusion = bf16[192,64,256]{2,1,0:T(8,128)(2,1)} fusion(bf16[64,64,256]{2,1,0:T(8,128)(2,1)} %get-tuple-element.179, s32[1024]{0:T(1024)S(1)} %pad_clamp_fusion.2), kind=kCustom, calls=%fused_computation.clone.clone.1 | custom fusion | bytes 12583680 | tf_op jit(solution)/shard_map/while/body/eval_jaxpr/gather | solution.py:66
  225.9 4.4 %fusion.61 = (f32[8,64]{1,0:T(8,128)S(1)}, f32[8,64,24,64]{1,3,2,0:T(8,128)S(1)}) fusion(pred[64,64]{0,1:T(8,128)(4,1)S(1)} %iota_compare_fusion.2, pred[8,24]{1,0:T(8,128)(4,1)S(1)} %get-tuple-element.152, pred[8,24]{1,0:T(8,128)(4,1)S(1)} %get-tuple-element.153, bf16[8,24,64,256]{3,2,1,0:T(8,128)(2,1)} %bitcast.59, ...), kind=kOutput, calls=%fused_computation.6.clone.1 | convolution fusion | flops 205258240 | bytes 6435328 | tf_op jit(solution)/shard_map/while/body/eval_jaxpr/ibd,isjd->ibsj/dot_general | solution.py:27
  230.3 2.5 fusion.62
  232.8 3.4 %fusion.63 = bf16[8,8,64,128]{3,2,1,0:T(8,128)(2,1)S(1)} fusion(bf16[8,8,64,128]{3,2,1,0:T(8,128)(2,1)S(1)} %get-tuple-element.166, s32[]{:T(128)} %get-tuple-element.165, bf16[8,24,64,256]{3,2,1,0:T(8,128)(2,1)S(1)} %bitcast.62, f32[8,64,24,64]{1,3,2,0:T(8,128)S(1)} %get-tuple-element.154, f32[8,64]{1,0:T(8,128)S(1)} %get-tuple-element.155, ...), kind=kOutput, calls=%fused_computation.20.clone.1 | convolution fusion | flops 206176256 | bytes 9586692 | tf_op jit(solution)/shard_map/while/body/eval_jaxpr/ibsj,isjd->ibd/dot_general | solution.py:42
  236.2 0.7 copy.17
  236.9 16.8 %convolution_convert_fusion = bf16[512,8192]{1,0:T(8,128)(2,1)} fusion(bf16[1024,8192]{1,0:T(8,128)(2,1)} %param.11, bf16[64,8,8,128]{3,2,1,0:T(8,128)(2,1)S(1)} %bitcast.66), kind=kOutput, calls=%fused_computation.42 | convolution fusion | flops 8594128896 | bytes 26214400 | tf_op jit(solution)/shard_map/dot_general | solution.py:71
  253.8 70.9 %reduce-scatter.2.cloned.1.call-done = bf16[128,8192]{1,0:T(8,128)(2,1)} async-done(((bf16[512,8192]{1,0:T(8,128)(2,1)}), bf16[128,8192]{1,0:T(8,128)(2,1)}) %reduce-scatter.2.cloned.1.call-update) | async-done | bytes 2097168 | tf_op jit(solution)/shard_map/reduce_scatter | solution.py:72
  (150 shorter events, 11.6 us)
Async XLA Ops:
  6.5 52.7 %all-gather.2.cloned.1.call-start = ((), (), s32[]{:S(2)}) async-start(), calls=%async_computation.1 | async-start | bytes 2359296 | tf_op jit(solution)/shard_map/all_gather | solution.py:56
  8.3 316.4 %reduce-scatter.2.cloned.1.call-start = ((), (), s32[]{:S(2)}) async-start(), calls=%async_computation.2 | async-start | bytes 10485760 | tf_op jit(solution)/shard_map/reduce_scatter | solution.py:72
  71.1 6.9 %slice-start = ((s8[6291456]{0:T(1024)(128)(4,1)}), s8[4194304]{0:T(1024)(128)(4,1)S(1)}, s32[]{:S(2)}) async-start(s8[6291456]{0:T(1024)(128)(4,1)} %bitcast.60), calls=%async_computation.3 | async-start | bytes 8388608 | tf_op jit(solution)/shard_map/while
  71.1 6.9 %slice-start.1 = ((s8[6291456]{0:T(1024)(128)(4,1)}), s8[2097152]{0:T(1024)(128)(4,1)S(1)}, s32[]{:S(2)}) async-start(s8[6291456]{0:T(1024)(128)(4,1)} %bitcast.60), calls=%async_computation.4 | async-start | bytes 4194304 | tf_op jit(solution)/shard_map/while
  93.2 6.9 %slice-start = ((s8[6291456]{0:T(1024)(128)(4,1)}), s8[4194304]{0:T(1024)(128)(4,1)S(1)}, s32[]{:S(2)}) async-start(s8[6291456]{0:T(1024)(128)(4,1)} %bitcast.60), calls=%async_computation.3 | async-start | bytes 8388608 | tf_op jit(solution)/shard_map/while
  93.2 6.9 %slice-start.1 = ((s8[6291456]{0:T(1024)(128)(4,1)}), s8[2097152]{0:T(1024)(128)(4,1)S(1)}, s32[]{:S(2)}) async-start(s8[6291456]{0:T(1024)(128)(4,1)} %bitcast.60), calls=%async_computation.4 | async-start | bytes 4194304 | tf_op jit(solution)/shard_map/while
  115.3 6.9 %slice-start = ((s8[6291456]{0:T(1024)(128)(4,1)}), s8[4194304]{0:T(1024)(128)(4,1)S(1)}, s32[]{:S(2)}) async-start(s8[6291456]{0:T(1024)(128)(4,1)} %bitcast.60), calls=%async_computation.3 | async-start | bytes 8388608 | tf_op jit(solution)/shard_map/while
  115.3 6.9 %slice-start.1 = ((s8[6291456]{0:T(1024)(128)(4,1)}), s8[2097152]{0:T(1024)(128)(4,1)S(1)}, s32[]{:S(2)}) async-start(s8[6291456]{0:T(1024)(128)(4,1)} %bitcast.60), calls=%async_computation.4 | async-start | bytes 4194304 | tf_op jit(solution)/shard_map/while
  137.5 6.9 %slice-start = ((s8[6291456]{0:T(1024)(128)(4,1)}), s8[4194304]{0:T(1024)(128)(4,1)S(1)}, s32[]{:S(2)}) async-start(s8[6291456]{0:T(1024)(128)(4,1)} %bitcast.60), calls=%async_computation.3 | async-start | bytes 8388608 | tf_op jit(solution)/shard_map/while
  137.5 6.9 %slice-start.1 = ((s8[6291456]{0:T(1024)(128)(4,1)}), s8[2097152]{0:T(1024)(128)(4,1)S(1)}, s32[]{:S(2)}) async-start(s8[6291456]{0:T(1024)(128)(4,1)} %bitcast.60), calls=%async_computation.4 | async-start | bytes 4194304 | tf_op jit(solution)/shard_map/while
  159.6 6.9 %slice-start = ((s8[6291456]{0:T(1024)(128)(4,1)}), s8[4194304]{0:T(1024)(128)(4,1)S(1)}, s32[]{:S(2)}) async-start(s8[6291456]{0:T(1024)(128)(4,1)} %bitcast.60), calls=%async_computation.3 | async-start | bytes 8388608 | tf_op jit(solution)/shard_map/while
  159.6 6.9 %slice-start.1 = ((s8[6291456]{0:T(1024)(128)(4,1)}), s8[2097152]{0:T(1024)(128)(4,1)S(1)}, s32[]{:S(2)}) async-start(s8[6291456]{0:T(1024)(128)(4,1)} %bitcast.60), calls=%async_computation.4 | async-start | bytes 4194304 | tf_op jit(solution)/shard_map/while
  181.7 6.9 %slice-start = ((s8[6291456]{0:T(1024)(128)(4,1)}), s8[4194304]{0:T(1024)(128)(4,1)S(1)}, s32[]{:S(2)}) async-start(s8[6291456]{0:T(1024)(128)(4,1)} %bitcast.60), calls=%async_computation.3 | async-start | bytes 8388608 | tf_op jit(solution)/shard_map/while
  181.7 6.9 %slice-start.1 = ((s8[6291456]{0:T(1024)(128)(4,1)}), s8[2097152]{0:T(1024)(128)(4,1)S(1)}, s32[]{:S(2)}) async-start(s8[6291456]{0:T(1024)(128)(4,1)} %bitcast.60), calls=%async_computation.4 | async-start | bytes 4194304 | tf_op jit(solution)/shard_map/while
  203.8 6.9 %slice-start = ((s8[6291456]{0:T(1024)(128)(4,1)}), s8[4194304]{0:T(1024)(128)(4,1)S(1)}, s32[]{:S(2)}) async-start(s8[6291456]{0:T(1024)(128)(4,1)} %bitcast.60), calls=%async_computation.3 | async-start | bytes 8388608 | tf_op jit(solution)/shard_map/while
  203.8 6.9 %slice-start.1 = ((s8[6291456]{0:T(1024)(128)(4,1)}), s8[2097152]{0:T(1024)(128)(4,1)S(1)}, s32[]{:S(2)}) async-start(s8[6291456]{0:T(1024)(128)(4,1)} %bitcast.60), calls=%async_computation.4 | async-start | bytes 4194304 | tf_op jit(solution)/shard_map/while
  225.9 6.9 %slice-start = ((s8[6291456]{0:T(1024)(128)(4,1)}), s8[4194304]{0:T(1024)(128)(4,1)S(1)}, s32[]{:S(2)}) async-start(s8[6291456]{0:T(1024)(128)(4,1)} %bitcast.60), calls=%async_computation.3 | async-start | bytes 8388608 | tf_op jit(solution)/shard_map/while
  225.9 6.9 %slice-start.1 = ((s8[6291456]{0:T(1024)(128)(4,1)}), s8[2097152]{0:T(1024)(128)(4,1)S(1)}, s32[]{:S(2)}) async-start(s8[6291456]{0:T(1024)(128)(4,1)} %bitcast.60), calls=%async_computation.4 | async-start | bytes 4194304 | tf_op jit(solution)/shard_map/while
Sparse Core Ops, SparseCore 0:
  9.5 49.7 all-gather.1
  253.9 70.7 reduce-scatter.1
where the time goes:
time: 334 us; the launch traced here: 332 us
  waiting for transfers between devices  120 us (36%)
  local copies, waits for them, and re-layouts  91.5 us (27%)
  matrix products  78.7 us (24%)
  other arithmetic  27 us (8%)
  between operations  13.5 us (4%)
    gather x8, local copies, waits for them, and re-layouts, one_head(): chosen = source[locate(blocks)]  77.1 us
    reduce_scatter x1, waiting for transfers between devices, shards(): lax.psum_scatter(lax.optimization_barrier(product.astype(jnp.bfloat16)).a...  70.9 us
    all_gather x1, waiting for transfers between devices, shards(): source = lax.all_gather(keyvals, 'ctx', axis=0, tiled=True)  49.1 us
    dot_general x8, matrix products, attend(): jnp.einsum('ibd,isjd->ibsj', head_query, key_tiles, preferred_element_typ...  35.1 us
    dot_general x8, matrix products, attend(): jnp.einsum('ibsj,isjd->ibd', rounded_probs, value_tiles, preferred_elemen...  26.8 us
    reduce_sum x8, other arithmetic, attend(): row_total = jnp.sum(weights, axis=(2, 3))  19.8 us
    dot_general x1, matrix products, shards(): product = jnp.dot(attended, out_weight, preferred_element_type=jnp.float32)  16.8 us
  transfers between devices with their start and end apart: 2, of which 2 were waited for; matrix products, arithmetic and copies ran while one was open for 1% of the time, Pallas kernels for 0%

commit v1 on v0

v1 whole, which is shorter than its diff:
```python
import functools

import jax
import jax.numpy as jnp
from jax import lax
from jax.experimental import pallas as pl
from jax.experimental.pallas import tpu as pltpu
from jax.sharding import PartitionSpec as P

HS = 128
BLK = 64
SPAN = 16
VMOST = 2
LANES = 128
MASKED = -1e30
EXP_SCALE = 1.4426950408889634 / (HS**0.5)
CHUNKS = 4
TILE = 512
VMEM_LIMIT = 56 * 1024 * 1024


def vmem():
    return pl.BlockSpec(memory_space=pltpu.VMEM)


def smem():
    return pl.BlockSpec(memory_space=pltpu.SMEM)


def params():
    return pltpu.CompilerParams(vmem_limit_bytes=VMEM_LIMIT)


def pick_kernel(rank_ref, vert_ref, k_ref, v_ref, out_ref):
    local_blocks = k_ref.shape[0] // BLK
    heads, count = vert_ref.shape
    base = rank_ref[0] * local_blocks
    used = jnp.int32(0)
    for head in range(heads):
        for slot in range(count):
            block = vert_ref[head, slot] - base
            inside = (block >= 0) & (block < local_blocks)
            bit = jnp.left_shift(jnp.int32(1), jnp.clip(block, 0, local_blocks - 1))
            used = used | jnp.where(inside, bit, 0)
    first = jnp.int32(local_blocks)
    second = jnp.int32(local_blocks)
    for block in reversed(range(local_blocks)):
        here = ((used >> block) & 1) == 1
        second = jnp.where(here, first, second)
        first = jnp.where(here, block, first)
    for slot, block in enumerate((first, second)):
        start = pl.multiple_of(jnp.minimum(block, local_blocks - 1) * BLK, BLK)
        out_ref[slot * BLK : (slot + 1) * BLK, :HS] = k_ref[pl.ds(start, BLK), :]
        out_ref[slot * BLK : (slot + 1) * BLK, HS:] = v_ref[pl.ds(start, BLK), :]


def pick(rank, vertical, keys, values):
    return pl.pallas_call(
        pick_kernel,
        out_shape=jax.ShapeDtypeStruct((VMOST * BLK, 2 * HS), keys.dtype),
        in_specs=[smem(), smem(), vmem(), vmem()],
        out_specs=vmem(),
        compiler_params=params(),
        name="pick",
    )(rank, vertical, keys, values)


def mask_kernel(local_blocks, rank_ref, vert_ref, slash_ref, win_ref, pool_ref):
    heads, vert_count = vert_ref.shape
    slash_count = slash_ref.shape[1]
    rank = rank_ref[0]
    lane = lax.broadcasted_iota(jnp.int32, (heads, LANES), 1)
    vert = [vert_ref[:, s : s + 1] for s in range(vert_count)]
    zero = jnp.zeros((heads, LANES), jnp.float32)

    def member(columns, blocks):
        found = columns[0] == blocks
        for column in columns[1:]:
            found = found | (column == blocks)
        return found

    offset_ok = member([slash_ref[:, s : s + 1] for s in range(slash_count)], SPAN - 1 - lane)
    shard = rank - 2 - lane // VMOST
    first = jnp.full((1, LANES), local_blocks, jnp.int32)
    second = first
    for j in reversed(range(local_blocks)):
        here = member(vert, shard * local_blocks + j)
        here = jnp.max(jnp.where(here, 1, 0), axis=0, keepdims=True) == 1
        second = jnp.where(here, first, second)
        first = jnp.where(here, j, first)
    picked = jnp.where(lane % VMOST == 0, first, second)
    block = shard * local_blocks + picked
    pool_ok = (picked < local_blocks) & (shard >= 0) & member(vert, block)
    for i in range(local_blocks):
        row = rank * local_blocks + i
        seen = row - (SPAN - 1) + lane
        ok = (seen >= 0) & (offset_ok | member(vert, seen))
        win_ref[i] = jnp.where(ok | (lane >= SPAN), zero, MASKED)
        pool_ref[i] = jnp.where(pool_ok & (block < row - (SPAN - 1)), zero, MASKED)


def masks(rank, vertical, slash, local_blocks):
    heads = vertical.shape[0]
    shape = jax.ShapeDtypeStruct((local_blocks, heads, LANES), jnp.float32)
    return pl.pallas_call(
        functools.partial(mask_kernel, local_blocks),
        out_shape=(shape, shape),
        in_specs=[smem(), vmem(), vmem()],
        out_specs=(vmem(), vmem()),
        compiler_params=params(),
        name="masks",
    )(rank, vertical, slash)


def attend_kernel(near, pools, ids_ref, q_ref, win_ref, pool_ref, *refs):
    kv_refs = refs[: 2 * near]
    pool_kv = refs[2 * near : 2 * near + pools]
    out_ref = refs[-7]
    k_win, v_win, e_win, k_pool, v_pool, e_pool = refs[-6:]
    step = pl.program_id(0)
    heads = win_ref.shape[1]
    rows = kv_refs[0].shape[0]

    @pl.when(step == 0)
    def _():
        for s in range(near):
            k_win[s * rows : (s + 1) * rows, :] = kv_refs[2 * s][...]
            v_win[s * rows : (s + 1) * rows, :] = kv_refs[2 * s + 1][...]
        for s in range(pools):
            at = slice(s * VMOST * BLK, (s + 1) * VMOST * BLK)
            k_pool[at, :] = pool_kv[s][:, :HS]
            v_pool[at, :] = pool_kv[s][:, HS:]
        key = lax.broadcasted_iota(jnp.int32, e_win.shape, 0)
        lane = lax.broadcasted_iota(jnp.int32, e_win.shape, 1)
        last = (key // BLK == SPAN - 1) & (key % BLK == lane - BLK)
        e_win[...] = jnp.where((key // BLK == lane) | last, 1.0, 0.0).astype(e_win.dtype)
        key = lax.broadcasted_iota(jnp.int32, e_pool.shape, 0)
        lane = lax.broadcasted_iota(jnp.int32, e_pool.shape, 1)
        e_pool[...] = jnp.where(key // BLK == lane, 1.0, 0.0).astype(e_pool.dtype)

    here = ids_ref[step]
    q = q_ref[...]
    q = jnp.concatenate([q[:, h * HS : (h + 1) * HS] for h in range(heads)], axis=0)
    row = lax.broadcasted_iota(jnp.int32, (BLK, LANES), 0)
    lane = lax.broadcasted_iota(jnp.int32, (BLK, LANES), 1)
    above = jnp.where(lane - BLK > row, MASKED, 0.0).astype(jnp.float32)
    win_mask = win_ref[0][:, None, :] + above[None]
    win_mask = win_mask.reshape(heads * BLK, LANES).astype(q.dtype)
    pool_mask = jnp.broadcast_to(pool_ref[0][:, None, :], (heads, BLK, LANES))
    pool_mask = pool_mask.reshape(heads * BLK, LANES).astype(q.dtype)

    start = pl.multiple_of((here + 1) * BLK, BLK)
    keys = jnp.concatenate([k_win[pl.ds(start, SPAN * BLK), :], e_win[...]], axis=1)
    contract = (((1,), (1,)), ((), ()))
    near_scores = lax.dot_general(
        jnp.concatenate([q, win_mask], axis=1), keys, contract, preferred_element_type=jnp.float32
    )
    far_keys = jnp.concatenate([k_pool[...], e_pool[...]], axis=1)
    far_scores = lax.dot_general(
        jnp.concatenate([q, pool_mask], axis=1),
        far_keys,
        contract,
        preferred_element_type=jnp.float32,
    )
    top = jnp.maximum(
        jnp.max(near_scores, axis=1, keepdims=True), jnp.max(far_scores, axis=1, keepdims=True)
    )
    near_probs = jnp.exp2((near_scores - top) * EXP_SCALE).astype(q.dtype)
    far_probs = jnp.exp2((far_scores - top) * EXP_SCALE).astype(q.dtype)
    near_values = jnp.concatenate(
        [v_win[pl.ds(start, SPAN * BLK), :], jnp.ones((SPAN * BLK, LANES), q.dtype)], axis=1
    )
    far_values = jnp.concatenate(
        [v_pool[...], jnp.ones((v_pool.shape[0], LANES), q.dtype)], axis=1
    )
    summed = jnp.dot(near_probs, near_values, preferred_element_type=jnp.float32)
    summed = summed + jnp.dot(far_probs, far_values, preferred_element_type=jnp.float32)
    out = (summed[:, :HS] / summed[:, HS:]).astype(out_ref.dtype)
    for h in range(heads):
        out_ref[:, h * HS : (h + 1) * HS] = out[h * BLK : (h + 1) * BLK]


def attend(ids, queries, win, pool, near_kv, pool_kv, after):
    steps = ids.shape[0]
    width = queries.shape[1]
    heads = win.shape[1]
    near, pools = len(near_kv), len(pool_kv)
    rows = near_kv[0][0].shape[0]
    dtype = queries.dtype

    def whole(x):
        return pl.BlockSpec(x.shape, lambda g, ids: (0,) * x.ndim)

    flat = [x for pair in near_kv for x in pair] + list(pool_kv)
    table = pl.BlockSpec((1, heads, LANES), lambda g, ids: (ids[g], 0, 0))
    keys_seen = SPAN * BLK + pools * VMOST * BLK
    flops = steps * heads * BLK * keys_seen * 256 * 4
    return pl.pallas_call(
        functools.partial(attend_kernel, near, pools),
        out_shape=jax.ShapeDtypeStruct((steps * BLK, width), dtype),
        grid_spec=pltpu.PrefetchScalarGridSpec(
            num_scalar_prefetch=1,
            grid=(steps,),
            in_specs=[pl.BlockSpec((BLK, width), lambda g, ids: (ids[g], 0)), table, table]
            + [whole(x) for x in flat]
            + [pl.BlockSpec(memory_space=pl.ANY) for _ in after],
            out_specs=pl.BlockSpec((BLK, width), lambda g, ids: (g, 0)),
            scratch_shapes=[
                pltpu.VMEM((near * rows, HS), dtype),
                pltpu.VMEM((near * rows, HS), dtype),
                pltpu.VMEM((SPAN * BLK, LANES), dtype),
                pltpu.VMEM((pools * VMOST * BLK, HS), dtype),
                pltpu.VMEM((pools * VMOST * BLK, HS), dtype),
                pltpu.VMEM((pools * VMOST * BLK, LANES), dtype),
            ],
        ),
        compiler_params=params(),
        cost_estimate=pl.CostEstimate(
            flops=flops, bytes_accessed=steps * BLK * width * 4, transcendentals=0
        ),
        name="attend",
    )(ids, queries, win, pool, *flat, *after)


def project_kernel(a_ref, w_ref, *refs):
    send_ref, keep_ref = refs[-2:]
    half = send_ref.shape[0]
    product = jnp.dot(a_ref[...], w_ref[...], preferred_element_type=jnp.float32)
    product = product.astype(send_ref.dtype)
    send_ref[...] = product[:half]
    keep_ref[...] = product[half:]


def project(attended, out_weight, chunk, after):
    rows, depth = attended.shape
    columns = out_weight.shape[1] // CHUNKS
    tiles = columns // TILE
    half = jax.ShapeDtypeStruct((rows // 2, columns), attended.dtype)
    return pl.pallas_call(
        project_kernel,
        out_shape=(half, half),
        grid=(tiles,),
        in_specs=[
            pl.BlockSpec((rows, depth), lambda g: (0, 0)),
            pl.BlockSpec((depth, TILE), lambda g: (0, chunk * tiles + g)),
        ]
        + [pl.BlockSpec(memory_space=pl.ANY) for _ in after],
        out_specs=(
            pl.BlockSpec((rows // 2, TILE), lambda g: (0, g)),
            pl.BlockSpec((rows // 2, TILE), lambda g: (0, g)),
        ),
        compiler_params=params(),
        cost_estimate=pl.CostEstimate(
            flops=2 * rows * depth * columns,
            bytes_accessed=2 * columns * (depth + rows),
            transcendentals=0,
        ),
        name="project",
    )(attended, out_weight, *after)


def add(*terms):
    total = terms[0].astype(jnp.float32)
    for term in terms[1:]:
        total = total + term.astype(jnp.float32)
    return total.astype(terms[0].dtype)


def shards(ctx_size, queries, keys, values, out_weight, vertical, slash):
    local_blocks = queries.shape[0] // BLK
    near = 1 + -(-(SPAN - 1) // local_blocks)
    ctx_rank = lax.axis_index("ctx")
    tp_rank = lax.axis_index("tp")
    rank = jnp.reshape(ctx_rank, (1,)).astype(jnp.int32)

    def shifted(x, by):
        return lax.ppermute(x, "ctx", [(r, r + by) for r in range(ctx_size - by)])

    near_kv = [(shifted(keys, s), shifted(values, s)) for s in range(near - 1, 0, -1)]
    near_kv.append((keys, values))
    own = pick(rank, vertical, keys, values)
    pool_kv = [shifted(own, s) for s in range(2, ctx_size)]
    win, pool = masks(rank, vertical, slash, local_blocks)

    quarter = local_blocks // 4
    inner = jnp.arange(quarter, dtype=jnp.int32)

    def blocks_of(first, second):
        return jnp.concatenate([first * quarter + inner, second * quarter + inner])

    def sibling(x):
        return lax.ppermute(x, "tp", [(j, j ^ 1) for j in range(4)])

    def across(x):
        return lax.ppermute(x, "tp", [(j, j ^ 2) for j in range(4)])

    other_ids = blocks_of(tp_rank ^ 3, tp_rank ^ 2)
    attended = attend(other_ids, queries, win, pool, near_kv, pool_kv, ())
    arrived = []
    after = ()
    for c in range(CHUNKS):
        send, keep = project(attended, out_weight, c, after)
        after = (send,)
        arrived.append(across(add(keep, sibling(send))))
    own_ids = blocks_of(tp_rank ^ 1, tp_rank)
    attended = attend(own_ids, queries, win, pool, near_kv, pool_kv, after)
    outs = []
    after = ()
    for c in range(CHUNKS):
        send, keep = project(attended, out_weight, c, after)
        after = (send,)
        outs.append(add(keep, sibling(send), arrived[c]))
    return jnp.concatenate(outs, axis=1)


def solution(mesh):
    assert mesh.shape["tp"] == 4
    return jax.shard_map(
        functools.partial(shards, mesh.shape["ctx"]),
        mesh=mesh,
        in_specs=(
            P("ctx", "tp"),
            P("ctx", "tp"),
            P("ctx", "tp"),
            P("tp", None),
            P("tp", None),
            P("tp", None),
        ),
        out_specs=P(("ctx", "tp"), None),
        check_vma=False,
    )
```

time: 334 us -> 151 us (0.45)
  local copies, waits for them, and re-layouts: 91.5 us -> 0.79 us
  matrix products: 78.7 us -> 0 us
  waiting for transfers between devices: 120 us -> 46.5 us
  Pallas kernels: 0 us -> 67.1 us
  starting transfers between devices: 0.04 us -> 29.5 us
  other arithmetic: 27 us -> 4.29 us
  between operations: 13.5 us -> 0.46 us
    dot_general x17 -> x0, matrix products: 78.7 us -> none  [the longest x8 35.1 us: attend(): jnp.einsum('ibd,isjd->ibsj', head_query, key_tiles, preferred_element_typ...]
    gather x8 -> x0, local copies, waits for them, and re-layouts: 77.1 us -> none  [one_head(): chosen = source[locate(blocks)]]
    reduce_scatter x1 -> x0, waiting for transfers between devices: 70.9 us -> none  [shards(): lax.psum_scatter(lax.optimization_barrier(product.astype(jnp.bfloat16)).a...]
    pallas_call x0 -> x12, Pallas kernels: none -> 67.1 us  [the longest x8 39.8 us: project(): pl.pallas_call(project_kernel, out_shape=(half, half), grid=(tiles,), in_...]
    all_gather x1 -> x0, waiting for transfers between devices: 49.1 us -> none  [shards(): source = lax.all_gather(keyvals, 'ctx', axis=0, tiled=True)]
    ppermute x0 -> x22, waiting for transfers between devices: none -> 46.5 us  [the longest x4 42.6 us: across(): return lax.ppermute(x, 'tp', [(j, j ^ 2) for j in range(4)])]
    ppermute x0 -> x22, starting transfers between devices: none -> 29.5 us  [the longest x10 23.5 us: shifted(): return lax.ppermute(x, 'ctx', [(r, r + by) for r in range(ctx_size - by)])]
    reduce_sum x8 -> x0, other arithmetic: 19.8 us -> none  [attend(): row_total = jnp.sum(weights, axis=(2, 3))]
  transfers between devices with their start and end apart: 2 -> 22, of which waited for: 2 -> 5; matrix products, arithmetic and copies ran while one was open for 1% -> 2% of each run, Pallas kernels for 0% -> 32%
where the time goes in v1:
time: 151 us; the launch traced here: 149 us
  Pallas kernels  67.1 us (44%)
  waiting for transfers between devices  46.5 us (31%)
  starting transfers between devices  29.5 us (20%)
  other arithmetic  4.29 us (3%)
    ppermute x4, waiting for transfers between devices, across(): return lax.ppermute(x, 'tp', [(j, j ^ 2) for j in range(4)])  42.6 us
    pallas_call x8, Pallas kernels, project(): pl.pallas_call(project_kernel, out_shape=(half, half), grid=(tiles,), in_...  39.8 us
    pallas_call x2, Pallas kernels, attend(): pl.pallas_call(functools.partial(attend_kernel, near, pools), out_shape=j...  23.7 us
    ppermute x10, starting transfers between devices, shifted(): return lax.ppermute(x, 'ctx', [(r, r + by) for r in range(ctx_size - by)])  23.5 us
    ppermute x4, starting transfers between devices, across(): return lax.ppermute(x, 'tp', [(j, j ^ 2) for j in range(4)])  4.25 us
    ppermute x10, waiting for transfers between devices, shifted(): return lax.ppermute(x, 'ctx', [(r, r + by) for r in range(ctx_size - by)])  3.82 us
  transfers between devices with their start and end apart: 22, of which 5 were waited for; matrix products, arithmetic and copies ran while one was open for 2% of the time, Pallas kernels for 32%

profile of v1, /device:TPU:16, one launch (start us, length us, event | category | flops | bytes accessed | tf_op | source)
XLA Modules:
  0.0 148.6 jit_solution(265999648023417145)
XLA Ops:
  0.0 2.0 %pick.1 = bf16[128,256]{1,0:T(8,128)(2,1)} custom-call(s32[1]{0:T(128)} %bitcast.rank_ref, s32[8,16]{1,0:T(8,128)} %vert_ref.3, bf16[512,128]{1,0:T(8,128)(2,1)} %refs_4_.3, bf16[512,128]{1,0:T(8,128)(2,1)} %refs_5_.3), custom_call_target="tpu_custom_call" | custom-call | tf_op jit(solution)/shard_map/pick/pallas_call | solution.py:58
  2.0 0.7 collective-permute-start.9
  2.7 0.7 collective-permute-start.8
  3.4 0.7 collective-permute-start.7
  4.0 1.3 collective-permute-start.6
  5.3 6.3 %collective-permute-start.5 = (bf16[128,256]{1,0:T(8,128)(2,1)}, bf16[128,256]{1,0:T(8,128)(2,1)S(1)}, u32[]{:S(2)}, u32[]{:S(2)}) collective-permute-start(bf16[128,256]{1,0:T(8,128)(2,1)} %pick.1), channel_id=1, source_target_pairs={{0,12},{4,16},{8,20},{12,24},{16,28},{1,13},{5,17},{9,21},{13,25},... | collective-permute-start | bytes 196616 | tf_op jit(solution)/shard_map/ppermute | solution.py:277
  11.7 1.9 %collective-permute-start.2 = (bf16[512,128]{1,0:T(8,128)(2,1)}, bf16[512,128]{1,0:T(8,128)(2,1)S(1)}, u32[]{:S(2)}, u32[]{:S(2)}) collective-permute-start(bf16[512,128]{1,0:T(8,128)(2,1)} %refs_4_.3), channel_id=1, source_target_pairs={{0,4},{4,8},{8,12},{12,16},{16,20},{20,24},{24,28},{1,5},{5,9},{9,... | collective-permute-start | bytes 393224 | tf_op jit(solution)/shard_map/ppermute | solution.py:277
  13.7 5.0 %collective-permute-start = (bf16[512,128]{1,0:T(8,128)(2,1)}, bf16[512,128]{1,0:T(8,128)(2,1)S(1)}, u32[]{:S(2)}, u32[]{:S(2)}) collective-permute-start(bf16[512,128]{1,0:T(8,128)(2,1)} %refs_4_.3), channel_id=1, source_target_pairs={{0,8},{4,12},{8,16},{12,20},{16,24},{20,28},{1,9},{5,13},{9,17},{1... | collective-permute-start | bytes 393224 | tf_op jit(solution)/shard_map/ppermute | solution.py:277
  18.7 1.9 %collective-permute-start.3 = (bf16[512,128]{1,0:T(8,128)(2,1)}, bf16[512,128]{1,0:T(8,128)(2,1)S(1)}, u32[]{:S(2)}, u32[]{:S(2)}) collective-permute-start(bf16[512,128]{1,0:T(8,128)(2,1)} %refs_5_.3), channel_id=1, source_target_pairs={{0,4},{4,8},{8,12},{12,16},{16,20},{20,24},{24,28},{1,5},{5,9},{9,... | collective-permute-start | bytes 393224 | tf_op jit(solution)/shard_map/ppermute | solution.py:277
  20.6 3.2 %collective-permute-start.1 = (bf16[512,128]{1,0:T(8,128)(2,1)}, bf16[512,128]{1,0:T(8,128)(2,1)S(1)}, u32[]{:S(2)}, u32[]{:S(2)}) collective-permute-start(bf16[512,128]{1,0:T(8,128)(2,1)} %refs_5_.3), channel_id=1, source_target_pairs={{0,8},{4,12},{8,16},{12,20},{16,24},{20,28},{1,9},{5,13},{9,17},{1... | collective-permute-start | bytes 393224 | tf_op jit(solution)/shard_map/ppermute | solution.py:277
  23.8 0.7 pad_add_fusion.ids_ref
  24.5 1.6 %masks.1 = (f32[8,8,128]{2,1,0:T(8,128)}, f32[8,8,128]{2,1,0:T(8,128)}) custom-call(s32[1]{0:T(128)} %bitcast.rank_ref, s32[8,16]{1,0:T(8,128)} %vert_ref.3, s32[8,8]{1,0:T(8,128)} %slash_ref.1), custom_call_target="tpu_custom_call" | custom-call | tf_op jit(solution)/shard_map/masks/pallas_call | solution.py:105
  26.0 1.9 %collective-permute-start.4 = (bf16[128,256]{1,0:T(8,128)(2,1)}, bf16[128,256]{1,0:T(8,128)(2,1)S(1)}, u32[]{:S(2)}, u32[]{:S(2)}) collective-permute-start(bf16[128,256]{1,0:T(8,128)(2,1)} %pick.1), channel_id=1, source_target_pairs={{0,8},{4,12},{8,16},{12,20},{16,24},{20,28},{1,9},{5,13},{9,17},{1... | collective-permute-start | bytes 196616 | tf_op jit(solution)/shard_map/ppermute | solution.py:277
  27.9 0.6 pad_add_fusion.1.ids_ref
  28.6 3.8 %collective-permute-done.4.refs_6_ = bf16[128,256]{1,0:T(8,128)(2,1)S(1)} collective-permute-done((bf16[128,256]{1,0:T(8,128)(2,1)}, bf16[128,256]{1,0:T(8,128)(2,1)S(1)}, u32[]{:S(2)}, u32[]{:S(2)}) %collective-permute-start.4) | collective-permute-done | bytes 65568 | tf_op jit(solution)/shard_map/ppermute | solution.py:277
  32.5 0.5 copy-done.21
  33.2 11.8 %attend.2.a_ref = bf16[256,1024]{1,0:T(8,128)(2,1)} custom-call(s32[4]{0:T(128)} %pad_add_fusion.1.ids_ref, bf16[512,1024]{1,0:T(8,128)(2,1)} %q_ref.3, f32[8,8,128]{2,1,0:T(8,128)} %get-tuple-element.23.win_ref, f32[8,8,128]{2,1,0:T(8,128)} %get-tuple-element.24.pool_ref, bf16[512,128]{1,0:T(8,128)(2,1)} %copy-done.13, bf16[512,128]{1,0:T(8,128)(2,1)} %copy-done.15, ...), custom_call_target="tpu_custom_call" | custom-call | flops 3758096384 | bytes 1048576 | tf_op jit(solution)/shard_map/attend/pallas_call | solution.py:198
  45.0 4.9 %project.8 = (bf16[128,2048]{1,0:T(8,128)(2,1)}, bf16[128,2048]{1,0:T(8,128)(2,1)}) custom-call(bf16[256,1024]{1,0:T(8,128)(2,1)} %attend.2.a_ref, bf16[1024,8192]{1,0:T(8,128)(2,1)} %w_ref.15), custom_call_target="tpu_custom_call" | custom-call | flops 1073741824 | bytes 5242880 | tf_op jit(solution)/shard_map/project/pallas_call | solution.py:239
  50.0 5.0 %project.9 = (bf16[128,2048]{1,0:T(8,128)(2,1)}, bf16[128,2048]{1,0:T(8,128)(2,1)}) custom-call(bf16[256,1024]{1,0:T(8,128)(2,1)} %attend.2.a_ref, bf16[1024,8192]{1,0:T(8,128)(2,1)} %w_ref.15, bf16[128,2048]{1,0:T(8,128)(2,1)} %get-tuple-element.25.refs_0_), custom_call_target="tpu_custom_call" | custom-call | flops 1073741824 | bytes 5242880 | tf_op jit(solution)/shard_map/project/pallas_call | solution.py:239
  54.9 0.5 collective-permute-start.14
  55.4 4.9 %project.10 = (bf16[128,2048]{1,0:T(8,128)(2,1)}, bf16[128,2048]{1,0:T(8,128)(2,1)}) custom-call(bf16[256,1024]{1,0:T(8,128)(2,1)} %attend.2.a_ref, bf16[1024,8192]{1,0:T(8,128)(2,1)} %w_ref.15, bf16[128,2048]{1,0:T(8,128)(2,1)} %get-tuple-element.26.refs_0_), custom_call_target="tpu_custom_call" | custom-call | flops 1073741824 | bytes 5242880 | tf_op jit(solution)/shard_map/project/pallas_call | solution.py:239
  60.4 5.0 %project.11 = (bf16[128,2048]{1,0:T(8,128)(2,1)}, bf16[128,2048]{1,0:T(8,128)(2,1)}) custom-call(bf16[256,1024]{1,0:T(8,128)(2,1)} %attend.2.a_ref, bf16[1024,8192]{1,0:T(8,128)(2,1)} %w_ref.15, bf16[128,2048]{1,0:T(8,128)(2,1)} %get-tuple-element.27.refs_0_), custom_call_target="tpu_custom_call" | custom-call | flops 1073741824 | bytes 5242880 | tf_op jit(solution)/shard_map/project/pallas_call | solution.py:239
  65.4 0.5 collective-permute-start.20
  65.9 11.8 %attend.3.a_ref = bf16[256,1024]{1,0:T(8,128)(2,1)} custom-call(s32[4]{0:T(128)} %pad_add_fusion.ids_ref, bf16[512,1024]{1,0:T(8,128)(2,1)} %q_ref.3, f32[8,8,128]{2,1,0:T(8,128)} %get-tuple-element.23.win_ref, f32[8,8,128]{2,1,0:T(8,128)} %get-tuple-element.24.pool_ref, bf16[512,128]{1,0:T(8,128)(2,1)} %copy-done.13, bf16[512,128]{1,0:T(8,128)(2,1)} %copy-done.15, ...), custom_call_target="tpu_custom_call" | custom-call | flops 3758096384 | bytes 1048576 | tf_op jit(solution)/shard_map/attend/pallas_call | solution.py:198
  77.7 5.0 %project.12 = (bf16[128,2048]{1,0:T(8,128)(2,1)}, bf16[128,2048]{1,0:T(8,128)(2,1)}) custom-call(bf16[256,1024]{1,0:T(8,128)(2,1)} %attend.3.a_ref, bf16[1024,8192]{1,0:T(8,128)(2,1)} %w_ref.15), custom_call_target="tpu_custom_call" | custom-call | flops 1073741824 | bytes 5242880 | tf_op jit(solution)/shard_map/project/pallas_call | solution.py:239
  82.8 4.9 %project.13 = (bf16[128,2048]{1,0:T(8,128)(2,1)}, bf16[128,2048]{1,0:T(8,128)(2,1)}) custom-call(bf16[256,1024]{1,0:T(8,128)(2,1)} %attend.3.a_ref, bf16[1024,8192]{1,0:T(8,128)(2,1)} %w_ref.15, bf16[128,2048]{1,0:T(8,128)(2,1)} %get-tuple-element.30.refs_0_), custom_call_target="tpu_custom_call" | custom-call | flops 1073741824 | bytes 5242880 | tf_op jit(solution)/shard_map/project/pallas_call | solution.py:239
  87.7 4.9 %project.14 = (bf16[128,2048]{1,0:T(8,128)(2,1)}, bf16[128,2048]{1,0:T(8,128)(2,1)}) custom-call(bf16[256,1024]{1,0:T(8,128)(2,1)} %attend.3.a_ref, bf16[1024,8192]{1,0:T(8,128)(2,1)} %w_ref.15, bf16[128,2048]{1,0:T(8,128)(2,1)} %get-tuple-element.33.refs_0_), custom_call_target="tpu_custom_call" | custom-call | flops 1073741824 | bytes 5242880 | tf_op jit(solution)/shard_map/project/pallas_call | solution.py:239
  92.7 5.1 %project.15 = (bf16[128,2048]{1,0:T(8,128)(2,1)}, bf16[128,2048]{1,0:T(8,128)(2,1)}) custom-call(bf16[256,1024]{1,0:T(8,128)(2,1)} %attend.3.a_ref, bf16[1024,8192]{1,0:T(8,128)(2,1)} %w_ref.15, bf16[128,2048]{1,0:T(8,128)(2,1)} %get-tuple-element.36.refs_0_), custom_call_target="tpu_custom_call" | custom-call | flops 1073741824 | bytes 5242880 | tf_op jit(solution)/shard_map/project/pallas_call | solution.py:239
  97.8 0.5 collective-permute-start.13
  98.3 0.1 add_convert_fusion.7
  98.5 0.1 collective-permute-start.16
  98.6 0.1 add_convert_fusion.5
  98.8 1.6 %collective-permute-start.12 = (bf16[128,2048]{1,0:T(8,128)(2,1)S(1)}, bf16[128,2048]{1,0:T(8,128)(2,1)S(1)}, u32[]{:S(2)}, u32[]{:S(2)}) collective-permute-start(bf16[128,2048]{1,0:T(8,128)(2,1)S(1)} %add_convert_fusion.7), channel_id=1, source_target_pairs={{0,2},{1,3},{2,0},{3,1},{4,6},{5,7},{6,4},{7,5},{8,10},{9,11},{10,... | collective-permute-start | bytes 1572872 | tf_op jit(solution)/shard_map/ppermute | solution.py:295
  100.3 0.1 add_convert_fusion.1
  100.5 0.6 collective-permute-start.15
  101.1 0.1 add_convert_fusion.3
  101.2 0.1 collective-permute-start.19
  101.3 12.3 %collective-permute-done.12 = bf16[128,2048]{1,0:T(8,128)(2,1)S(1)} collective-permute-done((bf16[128,2048]{1,0:T(8,128)(2,1)S(1)}, bf16[128,2048]{1,0:T(8,128)(2,1)S(1)}, u32[]{:S(2)}, u32[]{:S(2)}) %collective-permute-start.12) | collective-permute-done | bytes 524320 | tf_op jit(solution)/shard_map/ppermute | solution.py:295
  113.6 1.5 %collective-permute-start.21 = (bf16[128,2048]{1,0:T(8,128)(2,1)S(1)}, bf16[128,2048]{1,0:T(8,128)(2,1)S(1)}, u32[]{:S(2)}, u32[]{:S(2)}) collective-permute-start(bf16[128,2048]{1,0:T(8,128)(2,1)S(1)} %add_convert_fusion.1), channel_id=1, source_target_pairs={{0,2},{1,3},{2,0},{3,1},{4,6},{5,7},{6,4},{7,5},{8,10},{9,11},{10,... | collective-permute-start | bytes 1572872 | tf_op jit(solution)/shard_map/ppermute | solution.py:295
  115.1 0.2 add_convert_fusion.6
  115.3 0.6 collective-permute-start.18
  115.9 8.9 %collective-permute-done.15 = bf16[128,2048]{1,0:T(8,128)(2,1)S(1)} collective-permute-done((bf16[128,2048]{1,0:T(8,128)(2,1)S(1)}, bf16[128,2048]{1,0:T(8,128)(2,1)S(1)}, u32[]{:S(2)}, u32[]{:S(2)}) %collective-permute-start.15) | collective-permute-done | bytes 524320 | tf_op jit(solution)/shard_map/ppermute | solution.py:295
  124.8 0.2 add_convert_fusion.4
  125.1 11.0 %collective-permute-done.21 = bf16[128,2048]{1,0:T(8,128)(2,1)S(1)} collective-permute-done((bf16[128,2048]{1,0:T(8,128)(2,1)S(1)}, bf16[128,2048]{1,0:T(8,128)(2,1)S(1)}, u32[]{:S(2)}, u32[]{:S(2)}) %collective-permute-start.21) | collective-permute-done | bytes 524320 | tf_op jit(solution)/shard_map/ppermute | solution.py:295
  136.0 0.2 add_convert_fusion
  136.3 10.5 %collective-permute-done.18 = bf16[128,2048]{1,0:T(8,128)(2,1)S(1)} collective-permute-done((bf16[128,2048]{1,0:T(8,128)(2,1)S(1)}, bf16[128,2048]{1,0:T(8,128)(2,1)S(1)}, u32[]{:S(2)}, u32[]{:S(2)}) %collective-permute-start.18) | collective-permute-done | bytes 524320 | tf_op jit(solution)/shard_map/ppermute | solution.py:295
  146.8 0.2 add_convert_fusion.2
  147.1 1.5 %pad_maximum_fusion = bf16[128,8192]{1,0:T(8,128)(2,1)} fusion(bf16[128,2048]{1,0:T(8,128)(2,1)S(1)} %add_convert_fusion, bf16[128,2048]{1,0:T(8,128)(2,1)S(1)} %add_convert_fusion.2, bf16[128,2048]{1,0:T(8,128)(2,1)S(1)} %add_convert_fusion.4, bf16[128,2048]{1,0:T(8,128)(2,1)S(1)} %add_convert_fusion.6), kind=kLoop, calls=%fused_computation | loop fusion | flops 8388608 | bytes 4194304 | tf_op jit(solution)/shard_map/concatenate | solution.py:313
  (65 shorter events, 0.4 us)
Async XLA Ops:
  2.0 9.7 %collective-permute-start.9 = (bf16[128,256]{1,0:T(8,128)(2,1)}, bf16[128,256]{1,0:T(8,128)(2,1)S(1)}, u32[]{:S(2)}, u32[]{:S(2)}) collective-permute-start(bf16[128,256]{1,0:T(8,128)(2,1)} %pick.1), channel_id=1, source_target_pairs={{0,28},{1,29},{2,30},{3,31}} | collective-permute-start | bytes 196616 | tf_op jit(solution)/shard_map/ppermute | solution.py:277
  2.7 11.0 %collective-permute-start.8 = (bf16[128,256]{1,0:T(8,128)(2,1)}, bf16[128,256]{1,0:T(8,128)(2,1)S(1)}, u32[]{:S(2)}, u32[]{:S(2)}) collective-permute-start(bf16[128,256]{1,0:T(8,128)(2,1)} %pick.1), channel_id=1, source_target_pairs={{0,24},{4,28},{1,25},{5,29},{2,26},{6,30},{3,27},{7,31}} | collective-permute-start | bytes 196616 | tf_op jit(solution)/shard_map/ppermute | solution.py:277
  3.4 15.3 %collective-permute-start.7 = (bf16[128,256]{1,0:T(8,128)(2,1)}, bf16[128,256]{1,0:T(8,128)(2,1)S(1)}, u32[]{:S(2)}, u32[]{:S(2)}) collective-permute-start(bf16[128,256]{1,0:T(8,128)(2,1)} %pick.1), channel_id=1, source_target_pairs={{0,20},{4,24},{8,28},{1,21},{5,25},{9,29},{2,22},{6,26},{10,30},{3... | collective-permute-start | bytes 196616 | tf_op jit(solution)/shard_map/ppermute | solution.py:277
  4.0 16.5 %collective-permute-start.6 = (bf16[128,256]{1,0:T(8,128)(2,1)}, bf16[128,256]{1,0:T(8,128)(2,1)S(1)}, u32[]{:S(2)}, u32[]{:S(2)}) collective-permute-start(bf16[128,256]{1,0:T(8,128)(2,1)} %pick.1), channel_id=1, source_target_pairs={{0,16},{4,20},{8,24},{12,28},{1,17},{5,21},{9,25},{13,29},{2,18},{... | collective-permute-start | bytes 196616 | tf_op jit(solution)/shard_map/ppermute | solution.py:277
  5.3 20.7 %collective-permute-start.5 = (bf16[128,256]{1,0:T(8,128)(2,1)}, bf16[128,256]{1,0:T(8,128)(2,1)S(1)}, u32[]{:S(2)}, u32[]{:S(2)}) collective-permute-start(bf16[128,256]{1,0:T(8,128)(2,1)} %pick.1), channel_id=1, source_target_pairs={{0,12},{4,16},{8,20},{12,24},{16,28},{1,13},{5,17},{9,21},{13,25},... | collective-permute-start | bytes 196616 | tf_op jit(solution)/shard_map/ppermute | solution.py:277
  11.7 20.7 %copy-start.16 = (bf16[128,256]{1,0:T(8,128)(2,1)}, bf16[128,256]{1,0:T(8,128)(2,1)S(1)}, u32[]{:S(2)}) copy-start(bf16[128,256]{1,0:T(8,128)(2,1)S(1)} %collective-permute-done.9.refs_11_) | copy-start | bytes 196612
  11.7 20.7 %collective-permute-start.2 = (bf16[512,128]{1,0:T(8,128)(2,1)}, bf16[512,128]{1,0:T(8,128)(2,1)S(1)}, u32[]{:S(2)}, u32[]{:S(2)}) collective-permute-start(bf16[512,128]{1,0:T(8,128)(2,1)} %refs_4_.3), channel_id=1, source_target_pairs={{0,4},{4,8},{8,12},{12,16},{16,20},{20,24},{24,28},{1,5},{5,9},{9,... | collective-permute-start | bytes 393224 | tf_op jit(solution)/shard_map/ppermute | solution.py:277
  13.7 18.8 %copy-start.17 = (bf16[128,256]{1,0:T(8,128)(2,1)}, bf16[128,256]{1,0:T(8,128)(2,1)S(1)}, u32[]{:S(2)}) copy-start(bf16[128,256]{1,0:T(8,128)(2,1)S(1)} %collective-permute-done.8.refs_10_) | copy-start | bytes 196612
  13.7 18.7 %collective-permute-start = (bf16[512,128]{1,0:T(8,128)(2,1)}, bf16[512,128]{1,0:T(8,128)(2,1)S(1)}, u32[]{:S(2)}, u32[]{:S(2)}) collective-permute-start(bf16[512,128]{1,0:T(8,128)(2,1)} %refs_4_.3), channel_id=1, source_target_pairs={{0,8},{4,12},{8,16},{12,20},{16,24},{20,28},{1,9},{5,13},{9,17},{1... | collective-permute-start | bytes 393224 | tf_op jit(solution)/shard_map/ppermute | solution.py:277
  18.7 13.8 %copy-start.18 = (bf16[128,256]{1,0:T(8,128)(2,1)}, bf16[128,256]{1,0:T(8,128)(2,1)S(1)}, u32[]{:S(2)}) copy-start(bf16[128,256]{1,0:T(8,128)(2,1)S(1)} %collective-permute-done.7.refs_9_) | copy-start | bytes 196612
  18.7 13.7 %collective-permute-start.3 = (bf16[512,128]{1,0:T(8,128)(2,1)}, bf16[512,128]{1,0:T(8,128)(2,1)S(1)}, u32[]{:S(2)}, u32[]{:S(2)}) collective-permute-start(bf16[512,128]{1,0:T(8,128)(2,1)} %refs_5_.3), channel_id=1, source_target_pairs={{0,4},{4,8},{8,12},{12,16},{16,20},{20,24},{24,28},{1,5},{5,9},{9,... | collective-permute-start | bytes 393224 | tf_op jit(solution)/shard_map/ppermute | solution.py:277
  20.6 11.9 %copy-start.19 = (bf16[128,256]{1,0:T(8,128)(2,1)}, bf16[128,256]{1,0:T(8,128)(2,1)S(1)}, u32[]{:S(2)}) copy-start(bf16[128,256]{1,0:T(8,128)(2,1)S(1)} %collective-permute-done.6.refs_8_) | copy-start | bytes 196612
  20.6 11.8 %collective-permute-start.1 = (bf16[512,128]{1,0:T(8,128)(2,1)}, bf16[512,128]{1,0:T(8,128)(2,1)S(1)}, u32[]{:S(2)}, u32[]{:S(2)}) collective-permute-start(bf16[512,128]{1,0:T(8,128)(2,1)} %refs_5_.3), channel_id=1, source_target_pairs={{0,8},{4,12},{8,16},{12,20},{16,24},{20,28},{1,9},{5,13},{9,17},{1... | collective-permute-start | bytes 393224 | tf_op jit(solution)/shard_map/ppermute | solution.py:277
  26.0 6.5 %copy-start.20 = (bf16[128,256]{1,0:T(8,128)(2,1)}, bf16[128,256]{1,0:T(8,128)(2,1)S(1)}, u32[]{:S(2)}) copy-start(bf16[128,256]{1,0:T(8,128)(2,1)S(1)} %collective-permute-done.5.refs_7_) | copy-start | bytes 196612
  26.0 6.4 %collective-permute-start.4 = (bf16[128,256]{1,0:T(8,128)(2,1)}, bf16[128,256]{1,0:T(8,128)(2,1)S(1)}, u32[]{:S(2)}, u32[]{:S(2)}) collective-permute-start(bf16[128,256]{1,0:T(8,128)(2,1)} %pick.1), channel_id=1, source_target_pairs={{0,8},{4,12},{8,16},{12,20},{16,24},{20,28},{1,9},{5,13},{9,17},{1... | collective-permute-start | bytes 196616 | tf_op jit(solution)/shard_map/ppermute | solution.py:277
  32.4 0.6 copy-start.21
  32.4 0.7 copy-start.12
  32.4 0.7 copy-start.13
  32.4 0.8 copy-start.14
  32.4 0.8 copy-start.15
  50.0 47.8 %collective-permute-start.11 = (bf16[128,2048]{1,0:T(8,128)(2,1)}, bf16[128,2048]{1,0:T(8,128)(2,1)S(1)}, u32[]{:S(2)}, u32[]{:S(2)}) collective-permute-start(bf16[128,2048]{1,0:T(8,128)(2,1)} %get-tuple-element.25.refs_0_), channel_id=1, source_target_pairs={{0,1},{1,0},{2,3},{3,2},{4,5},{5,4},{6,7},{7,6},{8,9},{9,8},{10,11... | collective-permute-start | bytes 1572872 | tf_op jit(solution)/shard_map/ppermute | solution.py:292
  54.9 43.5 %collective-permute-start.14 = (bf16[128,2048]{1,0:T(8,128)(2,1)}, bf16[128,2048]{1,0:T(8,128)(2,1)S(1)}, u32[]{:S(2)}, u32[]{:S(2)}) collective-permute-start(bf16[128,2048]{1,0:T(8,128)(2,1)} %get-tuple-element.26.refs_0_), channel_id=1, source_target_pairs={{0,1},{1,0},{2,3},{3,2},{4,5},{5,4},{6,7},{7,6},{8,9},{9,8},{10,11... | collective-permute-start | bytes 1572872 | tf_op jit(solution)/shard_map/ppermute | solution.py:292
  60.4 5.0 %copy-start.2 = (bf16[128,2048]{1,0:T(8,128)(2,1)S(1)}, bf16[128,2048]{1,0:T(8,128)(2,1)}, u32[]{:S(2)}) copy-start(bf16[128,2048]{1,0:T(8,128)(2,1)} %get-tuple-element.27.refs_0_) | copy-start | bytes 1572868
  65.4 35.1 %collective-permute-start.17 = (bf16[128,2048]{1,0:T(8,128)(2,1)S(1)}, bf16[128,2048]{1,0:T(8,128)(2,1)S(1)}, u32[]{:S(2)}, u32[]{:S(2)}) collective-permute-start(bf16[128,2048]{1,0:T(8,128)(2,1)S(1)} %copy-done.2), channel_id=1, source_target_pairs={{0,1},{1,0},{2,3},{3,2},{4,5},{5,4},{6,7},{7,6},{8,9},{9,8},{10,11... | collective-permute-start | bytes 1572872 | tf_op jit(solution)/shard_map/ppermute | solution.py:292
  65.4 33.4 %collective-permute-start.20 = (bf16[128,2048]{1,0:T(8,128)(2,1)}, bf16[128,2048]{1,0:T(8,128)(2,1)S(1)}, u32[]{:S(2)}, u32[]{:S(2)}) collective-permute-start(bf16[128,2048]{1,0:T(8,128)(2,1)} %get-tuple-element.28.refs_12_), channel_id=1, source_target_pairs={{0,1},{1,0},{2,3},{3,2},{4,5},{5,4},{6,7},{7,6},{8,9},{9,8},{10,11... | collective-permute-start | bytes 1572872 | tf_op jit(solution)/shard_map/ppermute | solution.py:292
  82.7 18.5 %collective-permute-start.10 = (bf16[128,2048]{1,0:T(8,128)(2,1)}, bf16[128,2048]{1,0:T(8,128)(2,1)S(1)}, u32[]{:S(2)}, u32[]{:S(2)}) collective-permute-start(bf16[128,2048]{1,0:T(8,128)(2,1)} %get-tuple-element.30.refs_0_), channel_id=1, source_target_pairs={{0,1},{1,0},{2,3},{3,2},{4,5},{5,4},{6,7},{7,6},{8,9},{9,8},{10,11... | collective-permute-start | bytes 1572872 | tf_op jit(solution)/shard_map/ppermute | solution.py:292
  92.7 5.2 %copy-start.3 = (bf16[128,2048]{1,0:T(8,128)(2,1)S(1)}, bf16[128,2048]{1,0:T(8,128)(2,1)}, u32[]{:S(2)}) copy-start(bf16[128,2048]{1,0:T(8,128)(2,1)} %get-tuple-element.33.refs_0_) | copy-start | bytes 1572868
  92.7 5.7 %copy-start.6 = (bf16[128,2048]{1,0:T(8,128)(2,1)S(1)}, bf16[128,2048]{1,0:T(8,128)(2,1)}, u32[]{:S(2)}) copy-start(bf16[128,2048]{1,0:T(8,128)(2,1)} %get-tuple-element.31) | copy-start | bytes 1572868
  92.7 5.8 %copy-start = (bf16[128,2048]{1,0:T(8,128)(2,1)S(1)}, bf16[128,2048]{1,0:T(8,128)(2,1)}, u32[]{:S(2)}) copy-start(bf16[128,2048]{1,0:T(8,128)(2,1)} %get-tuple-element.36.refs_0_) | copy-start | bytes 1572868
  92.7 6.0 %copy-start.5 = (bf16[128,2048]{1,0:T(8,128)(2,1)S(1)}, bf16[128,2048]{1,0:T(8,128)(2,1)}, u32[]{:S(2)}) copy-start(bf16[128,2048]{1,0:T(8,128)(2,1)} %get-tuple-element.34) | copy-start | bytes 1572868
  92.7 7.7 %copy-start.4 = (bf16[128,2048]{1,0:T(8,128)(2,1)S(1)}, bf16[128,2048]{1,0:T(8,128)(2,1)}, u32[]{:S(2)}) copy-start(bf16[128,2048]{1,0:T(8,128)(2,1)} %get-tuple-element.40) | copy-start | bytes 1572868
  97.8 3.3 %copy-start.1 = (bf16[128,2048]{1,0:T(8,128)(2,1)S(1)}, bf16[128,2048]{1,0:T(8,128)(2,1)}, u32[]{:S(2)}) copy-start(bf16[128,2048]{1,0:T(8,128)(2,1)} %get-tuple-element.37) | copy-start | bytes 1572868
  97.8 3.4 %copy-start.11 = (bf16[128,2048]{1,0:T(8,128)(2,1)S(1)}, bf16[128,2048]{1,0:T(8,128)(2,1)}, u32[]{:S(2)}) copy-start(bf16[128,2048]{1,0:T(8,128)(2,1)} %get-tuple-element.39) | copy-start | bytes 1572868
  97.8 17.3 %copy-start.10 = (bf16[128,2048]{1,0:T(8,128)(2,1)S(1)}, bf16[128,2048]{1,0:T(8,128)(2,1)}, u32[]{:S(2)}) copy-start(bf16[128,2048]{1,0:T(8,128)(2,1)} %get-tuple-element.29) | copy-start | bytes 1572868
  97.8 17.5 %collective-permute-start.13 = (bf16[128,2048]{1,0:T(8,128)(2,1)S(1)}, bf16[128,2048]{1,0:T(8,128)(2,1)S(1)}, u32[]{:S(2)}, u32[]{:S(2)}) collective-permute-start(bf16[128,2048]{1,0:T(8,128)(2,1)S(1)} %copy-done.3), channel_id=1, source_target_pairs={{0,1},{1,0},{2,3},{3,2},{4,5},{5,4},{6,7},{7,6},{8,9},{9,8},{10,11... | collective-permute-start | bytes 1572872 | tf_op jit(solution)/shard_map/ppermute | solution.py:292
  98.3 26.5 %copy-start.9 = (bf16[128,2048]{1,0:T(8,128)(2,1)S(1)}, bf16[128,2048]{1,0:T(8,128)(2,1)}, u32[]{:S(2)}) copy-start(bf16[128,2048]{1,0:T(8,128)(2,1)} %get-tuple-element.32) | copy-start | bytes 1572868
  98.5 37.8 %collective-permute-start.16 = (bf16[128,2048]{1,0:T(8,128)(2,1)S(1)}, bf16[128,2048]{1,0:T(8,128)(2,1)S(1)}, u32[]{:S(2)}, u32[]{:S(2)}) collective-permute-start(bf16[128,2048]{1,0:T(8,128)(2,1)S(1)} %copy-done), channel_id=1, source_target_pairs={{0,1},{1,0},{2,3},{3,2},{4,5},{5,4},{6,7},{7,6},{8,9},{9,8},{10,11... | collective-permute-start | bytes 1572872 | tf_op jit(solution)/shard_map/ppermute | solution.py:292
  98.6 37.4 %copy-start.8 = (bf16[128,2048]{1,0:T(8,128)(2,1)S(1)}, bf16[128,2048]{1,0:T(8,128)(2,1)}, u32[]{:S(2)}) copy-start(bf16[128,2048]{1,0:T(8,128)(2,1)} %get-tuple-element.38) | copy-start | bytes 1572868
  98.8 14.8 %collective-permute-start.12 = (bf16[128,2048]{1,0:T(8,128)(2,1)S(1)}, bf16[128,2048]{1,0:T(8,128)(2,1)S(1)}, u32[]{:S(2)}, u32[]{:S(2)}) collective-permute-start(bf16[128,2048]{1,0:T(8,128)(2,1)S(1)} %add_convert_fusion.7), channel_id=1, source_target_pairs={{0,2},{1,3},{2,0},{3,1},{4,6},{5,7},{6,4},{7,5},{8,10},{9,11},{10,... | collective-permute-start | bytes 1572872 | tf_op jit(solution)/shard_map/ppermute | solution.py:295
  100.5 46.3 %copy-start.7 = (bf16[128,2048]{1,0:T(8,128)(2,1)S(1)}, bf16[128,2048]{1,0:T(8,128)(2,1)}, u32[]{:S(2)}) copy-start(bf16[128,2048]{1,0:T(8,128)(2,1)} %get-tuple-element.35) | copy-start | bytes 1572868
  100.5 24.3 %collective-permute-start.15 = (bf16[128,2048]{1,0:T(8,128)(2,1)S(1)}, bf16[128,2048]{1,0:T(8,128)(2,1)S(1)}, u32[]{:S(2)}, u32[]{:S(2)}) collective-permute-start(bf16[128,2048]{1,0:T(8,128)(2,1)S(1)} %add_convert_fusion.5), channel_id=1, source_target_pairs={{0,2},{1,3},{2,0},{3,1},{4,6},{5,7},{6,4},{7,5},{8,10},{9,11},{10,... | collective-permute-start | bytes 1572872 | tf_op jit(solution)/shard_map/ppermute | solution.py:295
  101.2 23.8 %collective-permute-start.19 = (bf16[128,2048]{1,0:T(8,128)(2,1)S(1)}, bf16[128,2048]{1,0:T(8,128)(2,1)S(1)}, u32[]{:S(2)}, u32[]{:S(2)}) collective-permute-start(bf16[128,2048]{1,0:T(8,128)(2,1)S(1)} %copy-done.11), channel_id=1, source_target_pairs={{0,1},{1,0},{2,3},{3,2},{4,5},{5,4},{6,7},{7,6},{8,9},{9,8},{10,11... | collective-permute-start | bytes 1572872 | tf_op jit(solution)/shard_map/ppermute | solution.py:292
  113.6 22.5 %collective-permute-start.21 = (bf16[128,2048]{1,0:T(8,128)(2,1)S(1)}, bf16[128,2048]{1,0:T(8,128)(2,1)S(1)}, u32[]{:S(2)}, u32[]{:S(2)}) collective-permute-start(bf16[128,2048]{1,0:T(8,128)(2,1)S(1)} %add_convert_fusion.1), channel_id=1, source_target_pairs={{0,2},{1,3},{2,0},{3,1},{4,6},{5,7},{6,4},{7,5},{8,10},{9,11},{10,... | collective-permute-start | bytes 1572872 | tf_op jit(solution)/shard_map/ppermute | solution.py:295
  115.3 31.5 %collective-permute-start.18 = (bf16[128,2048]{1,0:T(8,128)(2,1)S(1)}, bf16[128,2048]{1,0:T(8,128)(2,1)S(1)}, u32[]{:S(2)}, u32[]{:S(2)}) collective-permute-start(bf16[128,2048]{1,0:T(8,128)(2,1)S(1)} %add_convert_fusion.3), channel_id=1, source_target_pairs={{0,2},{1,3},{2,0},{3,1},{4,6},{5,7},{6,4},{7,5},{8,10},{9,11},{10,... | collective-permute-start | bytes 1572872 | tf_op jit(solution)/shard_map/ppermute | solution.py:295

commit v2 on v1

--- a/solution.py
+++ b/solution.py
@@ -15,8 +15,9 @@
 MASKED = -1e30
 EXP_SCALE = 1.4426950408889634 / (HS**0.5)
 CHUNKS = 4
-TILE = 512
-VMEM_LIMIT = 56 * 1024 * 1024
+TILE = 1024
+WEIGHT_PARTS = 4
+MIB = 1024 * 1024
 
 
 def vmem():
@@ -27,11 +28,11 @@
     return pl.BlockSpec(memory_space=pltpu.SMEM)
 
 
-def params():
-    return pltpu.CompilerParams(vmem_limit_bytes=VMEM_LIMIT)
-
-
-def pick_kernel(rank_ref, vert_ref, k_ref, v_ref, out_ref):
+def params(mib):
+    return pltpu.CompilerParams(vmem_limit_bytes=mib * MIB)
+
+
+def pick_kernel(rank_ref, vert_ref, k_ref, v_ref, both_ref, out_ref):
     local_blocks = k_ref.shape[0] // BLK
     heads, count = vert_ref.shape
     base = rank_ref[0] * local_blocks
@@ -48,19 +49,25 @@
         here = ((used >> block) & 1) == 1
         second = jnp.where(here, first, second)
         first = jnp.where(here, block, first)
+    both_ref[:, :HS] = k_ref[...]
+    both_ref[:, HS:] = v_ref[...]
     for slot, block in enumerate((first, second)):
         start = pl.multiple_of(jnp.minimum(block, local_blocks - 1) * BLK, BLK)
-        out_ref[slot * BLK : (slot + 1) * BLK, :HS] = k_ref[pl.ds(start, BLK), :]
-        out_ref[slot * BLK : (slot + 1) * BLK, HS:] = v_ref[pl.ds(start, BLK), :]
-
-
-def pick(rank, vertical, keys, values):
+        rows = jnp.concatenate([k_ref[pl.ds(start, BLK), :], v_ref[pl.ds(start, BLK), :]], axis=1)
+        for copy in range(out_ref.shape[0]):
+            out_ref[copy, slot * BLK : (slot + 1) * BLK, :] = rows
+
+
+def pick(rank, vertical, keys, values, copies):
     return pl.pallas_call(
         pick_kernel,
-        out_shape=jax.ShapeDtypeStruct((VMOST * BLK, 2 * HS), keys.dtype),
+        out_shape=(
+            jax.ShapeDtypeStruct((keys.shape[0], 2 * HS), keys.dtype),
+            jax.ShapeDtypeStruct((copies, VMOST * BLK, 2 * HS), keys.dtype),
+        ),
         in_specs=[smem(), smem(), vmem(), vmem()],
-        out_specs=vmem(),
-        compiler_params=params(),
+        out_specs=(vmem(), vmem()),
+        compiler_params=params(8),
         name="pick",
     )(rank, vertical, keys, values)
 
@@ -80,7 +87,7 @@
         return found
 
     offset_ok = member([slash_ref[:, s : s + 1] for s in range(slash_count)], SPAN - 1 - lane)
-    shard = rank - 2 - lane // VMOST
+    shard = lane // VMOST
     first = jnp.full((1, LANES), local_blocks, jnp.int32)
     second = first
     for j in reversed(range(local_blocks)):
@@ -90,7 +97,7 @@
         first = jnp.where(here, j, first)
     picked = jnp.where(lane % VMOST == 0, first, second)
     block = shard * local_blocks + picked
-    pool_ok = (picked < local_blocks) & (shard >= 0) & member(vert, block)
+    pool_ok = (picked < local_blocks) & member(vert, block)
     for i in range(local_blocks):
         row = rank * local_blocks + i
         seen = row - (SPAN - 1) + lane
@@ -107,14 +114,14 @@
         out_shape=(shape, shape),
         in_specs=[smem(), vmem(), vmem()],
         out_specs=(vmem(), vmem()),
-        compiler_params=params(),
+        compiler_params=params(8),
         name="masks",
     )(rank, vertical, slash)
 
 
 def attend_kernel(near, pools, ids_ref, q_ref, win_ref, pool_ref, *refs):
-    kv_refs = refs[: 2 * near]
-    pool_kv = refs[2 * near : 2 * near + pools]
+    kv_refs = refs[:near]
+    pool_kv = refs[near]
     out_ref = refs[-7]
     k_win, v_win, e_win, k_pool, v_pool, e_pool = refs[-6:]
     step = pl.program_id(0)
@@ -124,12 +131,12 @@
     @pl.when(step == 0)
     def _():
         for s in range(near):
-            k_win[s * rows : (s + 1) * rows, :] = kv_refs[2 * s][...]
-            v_win[s * rows : (s + 1) * rows, :] = kv_refs[2 * s + 1][...]
+            k_win[s * rows : (s + 1) * rows, :] = kv_refs[s][:, :HS]
+            v_win[s * rows : (s + 1) * rows, :] = kv_refs[s][:, HS:]
         for s in range(pools):
             at = slice(s * VMOST * BLK, (s + 1) * VMOST * BLK)
-            k_pool[at, :] = pool_kv[s][:, :HS]
-            v_pool[at, :] = pool_kv[s][:, HS:]
+            k_pool[at, :] = pool_kv[s, :, :HS]
+            v_pool[at, :] = pool_kv[s, :, HS:]
         key = lax.broadcasted_iota(jnp.int32, e_win.shape, 0)
         lane = lax.broadcasted_iota(jnp.int32, e_win.shape, 1)
         last = (key // BLK == SPAN - 1) & (key % BLK == lane - BLK)
@@ -184,14 +191,14 @@
     steps = ids.shape[0]
     width = queries.shape[1]
     heads = win.shape[1]
-    near, pools = len(near_kv), len(pool_kv)
-    rows = near_kv[0][0].shape[0]
+    near, pools = len(near_kv), pool_kv.shape[0] - 2
+    rows = near_kv[0].shape[0]
     dtype = queries.dtype
 
     def whole(x):
         return pl.BlockSpec(x.shape, lambda g, ids: (0,) * x.ndim)
 
-    flat = [x for pair in near_kv for x in pair] + list(pool_kv)
+    flat = [*near_kv, pool_kv]
     table = pl.BlockSpec((1, heads, LANES), lambda g, ids: (ids[g], 0, 0))
     keys_seen = SPAN * BLK + pools * VMOST * BLK
     flops = steps * heads * BLK * keys_seen * 256 * 4
@@ -202,7 +209,8 @@
             num_scalar_prefetch=1,
             grid=(steps,),
             in_specs=[pl.BlockSpec((BLK, width), lambda g, ids: (ids[g], 0)), table, table]
-            + [whole(x) for x in flat]
+            + [whole(x) for x in near_kv]
+            + [pl.BlockSpec((pools,) + pool_kv.shape[1:], lambda g, ids: (0, 0, 0))]
             + [pl.BlockSpec(memory_space=pl.ANY) for _ in after],
             out_specs=pl.BlockSpec((BLK, width), lambda g, ids: (g, 0)),
             scratch_shapes=[
@@ -214,7 +222,7 @@
                 pltpu.VMEM((pools * VMOST * BLK, LANES), dtype),
             ],
         ),
-        compiler_params=params(),
+        compiler_params=params(28),
         cost_estimate=pl.CostEstimate(
             flops=flops, bytes_accessed=steps * BLK * width * 4, transcendentals=0
         ),
@@ -222,10 +230,17 @@
     )(ids, queries, win, pool, *flat, *after)
 
 
-def project_kernel(a_ref, w_ref, *refs):
+def project_kernel(a_ref, *refs):
     send_ref, keep_ref = refs[-2:]
     half = send_ref.shape[0]
-    product = jnp.dot(a_ref[...], w_ref[...], preferred_element_type=jnp.float32)
+    product = None
+    for part in range(WEIGHT_PARTS):
+        w = refs[part][...]
+        depth = w.shape[0]
+        term = jnp.dot(
+            a_ref[:, part * depth : (part + 1) * depth], w, preferred_element_type=jnp.float32
+        )
+        product = term if product is None else product + term
     product = product.astype(send_ref.dtype)
     send_ref[...] = product[:half]
     keep_ref[...] = product[half:]
@@ -236,27 +251,29 @@
     columns = out_weight.shape[1] // CHUNKS
     tiles = columns // TILE
     half = jax.ShapeDtypeStruct((rows // 2, columns), attended.dtype)
+
+    def weight(part):
+        return pl.BlockSpec((depth // WEIGHT_PARTS, TILE), lambda g: (part, chunk * tiles + g))
+
     return pl.pallas_call(
         project_kernel,
         out_shape=(half, half),
         grid=(tiles,),
-        in_specs=[
-            pl.BlockSpec((rows, depth), lambda g: (0, 0)),
-            pl.BlockSpec((depth, TILE), lambda g: (0, chunk * tiles + g)),
-        ]
+        in_specs=[pl.BlockSpec((rows, depth), lambda g: (0, 0))]
+        + [weight(part) for part in range(WEIGHT_PARTS)]
         + [pl.BlockSpec(memory_space=pl.ANY) for _ in after],
         out_specs=(
             pl.BlockSpec((rows // 2, TILE), lambda g: (0, g)),
             pl.BlockSpec((rows // 2, TILE), lambda g: (0, g)),
         ),
-        compiler_params=params(),
+        compiler_params=params(16),
         cost_estimate=pl.CostEstimate(
             flops=2 * rows * depth * columns,
             bytes_accessed=2 * columns * (depth + rows),
             transcendentals=0,
         ),
         name="project",
-    )(attended, out_weight, *after)
+    )(attended, *[out_weight] * WEIGHT_PARTS, *after)
 
 
 def add(*terms):
@@ -276,10 +293,9 @@
     def shifted(x, by):
         return lax.ppermute(x, "ctx", [(r, r + by) for r in range(ctx_size - by)])
 
-    near_kv = [(shifted(keys, s), shifted(values, s)) for s in range(near - 1, 0, -1)]
-    near_kv.append((keys, values))
-    own = pick(rank, vertical, keys, values)
-    pool_kv = [shifted(own, s) for s in range(2, ctx_size)]
+    own, pair = pick(rank, vertical, keys, values, ctx_size)
+    near_kv = [shifted(own, s) for s in range(near - 1, 0, -1)] + [own]
+    pool_kv = lax.all_to_all(pair, "ctx", split_axis=0, concat_axis=0, tiled=True)
     win, pool = masks(rank, vertical, slash, local_blocks)
 
     quarter = local_blocks // 4
@@ -297,19 +313,19 @@
     other_ids = blocks_of(tp_rank ^ 3, tp_rank ^ 2)
     attended = attend(other_ids, queries, win, pool, near_kv, pool_kv, ())
     arrived = []
-    after = ()
+    sums = []
+    for c in range(CHUNKS):
+        send, keep = project(attended, out_weight, c, sums[c - 2 : c - 1] if c > 1 else ())
+        sums.append(add(keep, sibling(send)))
+        arrived.append(across(sums[c]))
+    own_ids = blocks_of(tp_rank ^ 1, tp_rank)
+    attended = attend(own_ids, queries, win, pool, near_kv, pool_kv, (sums[-2],))
+    outs = []
+    after = (sums[-1],)
     for c in range(CHUNKS):
         send, keep = project(attended, out_weight, c, after)
         after = (send,)
-        arrived.append(across(add(keep, sibling(send))))
-    own_ids = blocks_of(tp_rank ^ 1, tp_rank)
-    attended = attend(own_ids, queries, win, pool, near_kv, pool_kv, after)
-    outs = []
-    after = ()
-    for c in range(CHUNKS):
-        send, keep = project(attended, out_weight, c, after)
-        after = (send,)
-        outs.append(add(keep, sibling(send), arrived[c]))
+        outs.append(add(add(keep, sibling(send)), arrived[c]))
     return jnp.concatenate(outs, axis=1)
 
 

time: 151 us -> 119 us (0.79)
  Pallas kernels: 67.1 us -> 35.7 us
  local copies, waits for them, and re-layouts: 0.79 us -> 16.6 us
  starting transfers between devices: 29.5 us -> 19.1 us
  waiting for transfers between devices: 46.5 us -> 43.1 us
    pallas_call x8, Pallas kernels: 39.8 us -> 14.4 us  [project(): pl.pallas_call(project_kernel, out_shape=(half, half), grid=(tiles,), in_...]
    ppermute x10 -> x2, starting transfers between devices: 23.5 us -> 6.73 us  [shifted(): return lax.ppermute(x, 'ctx', [(r, r + by) for r in range(ctx_size - by)])]
    unnamed x44 -> x26, local copies, waits for them, and re-layouts: 0.79 us -> 16.6 us
    ppermute x4, waiting for transfers between devices: 42.6 us -> 27.2 us  [across(): return lax.ppermute(x, 'tp', [(j, j ^ 2) for j in range(4)])]
    ppermute x10 -> x2, waiting for transfers between devices: 3.82 us -> 15.9 us  [shifted(): return lax.ppermute(x, 'ctx', [(r, r + by) for r in range(ctx_size - by)])]
    all_to_all x0 -> x1, starting transfers between devices: none -> 6.17 us  [shards(): lax.all_to_all(pair, 'ctx', split_axis=0, concat_axis=0, tiled=True)]
    pallas_call x2, Pallas kernels: 23.7 us -> 19.2 us  [attend(): pl.pallas_call(functools.partial(attend_kernel, near, pools), out_shape=j...]
  transfers between devices with their start and end apart: 22 -> 15, of which waited for: 5 -> 5; matrix products, arithmetic and copies ran while one was open for 2% -> 1% of each run, Pallas kernels for 32% -> 19%
where the time goes in v2:
time: 119 us; the launch traced here: 118 us
  waiting for transfers between devices  43.1 us (36%)
  Pallas kernels  35.7 us (30%)
  starting transfers between devices  19.1 us (16%)
  local copies, waits for them, and re-layouts  16.6 us (14%)
  other arithmetic  3.16 us (3%)
    ppermute x4, waiting for transfers between devices, across(): return lax.ppermute(x, 'tp', [(j, j ^ 2) for j in range(4)])  27.2 us
    pallas_call x2, Pallas kernels, attend(): pl.pallas_call(functools.partial(attend_kernel, near, pools), out_shape=j...  19.2 us
    unnamed x26, local copies, waits for them, and re-layouts  16.6 us
    ppermute x2, waiting for transfers between devices, shifted(): return lax.ppermute(x, 'ctx', [(r, r + by) for r in range(ctx_size - by)])  15.9 us
    pallas_call x8, Pallas kernels, project(): pl.pallas_call(project_kernel, out_shape=(half, half), grid=(tiles,), in_...  14.4 us
    ppermute x2, starting transfers between devices, shifted(): return lax.ppermute(x, 'ctx', [(r, r + by) for r in range(ctx_size - by)])  6.73 us
    all_to_all x1, starting transfers between devices, shards(): lax.all_to_all(pair, 'ctx', split_axis=0, concat_axis=0, tiled=True)  6.17 us
    ppermute x4, starting transfers between devices, across(): return lax.ppermute(x, 'tp', [(j, j ^ 2) for j in range(4)])  4.24 us
  transfers between devices with their start and end apart: 15, of which 5 were waited for; matrix products, arithmetic and copies ran while one was open for 1% of the time, Pallas kernels for 19%

profile of v2, /device:TPU:16, one launch (start us, length us, event | category | flops | bytes accessed | tf_op | source)
XLA Modules:
  0.0 118.1 jit_solution(16074755263087671636)
XLA Ops:
  0.0 0.9 copy-done.2
  0.9 0.9 copy-done.3
  1.8 0.7 copy-done.4
  2.5 1.9 %pick.1 = (bf16[512,256]{1,0:T(8,128)(2,1)S(1)}, bf16[8,128,256]{2,1,0:T(8,128)(2,1)}) custom-call(s32[1]{0:T(128)} %bitcast.rank_ref, s32[8,16]{1,0:T(8,128)S(1)} %copy-done.4, bf16[512,128]{1,0:T(8,128)(2,1)S(1)} %copy-done.2, bf16[512,128]{1,0:T(8,128)(2,1)S(1)} %copy-done.3), custom_call_target="tpu_custom_call" | custom-call | tf_op jit(solution)/shard_map/pick/pallas_call | solution.py:62
  4.3 6.2 %all-to-all-start = ((bf16[8,128,256]{2,1,0:T(8,128)(2,1)}), bf16[8,128,256]{2,1,0:T(8,128)(2,1)S(1)}, u32[]{:S(2)}, u32[]{:S(2)}) async-start(bf16[8,128,256]{2,1,0:T(8,128)(2,1)} %get-tuple-element.28), calls=%async_computation | async-start | bytes 1048576 | tf_op jit(solution)/shard_map/all_to_all | solution.py:298
  10.5 3.4 %collective-permute-start = (bf16[512,256]{1,0:T(8,128)(2,1)S(1)}, bf16[512,256]{1,0:T(8,128)(2,1)S(1)}, u32[]{:S(2)}, u32[]{:S(2)}) collective-permute-start(bf16[512,256]{1,0:T(8,128)(2,1)S(1)} %get-tuple-element.27.refs_2_), channel_id=1, source_target_pairs={{0,8},{4,12},{8,16},{12,20},{16,24},{20,28},{1,9},{5,13},{9,17},{1... | collective-permute-start | bytes 786440 | tf_op jit(solution)/shard_map/ppermute | solution.py:294
  13.9 3.4 %collective-permute-start.1 = (bf16[512,256]{1,0:T(8,128)(2,1)S(1)}, bf16[512,256]{1,0:T(8,128)(2,1)S(1)}, u32[]{:S(2)}, u32[]{:S(2)}) collective-permute-start(bf16[512,256]{1,0:T(8,128)(2,1)S(1)} %get-tuple-element.27.refs_2_), channel_id=1, source_target_pairs={{0,4},{4,8},{8,12},{12,16},{16,20},{20,24},{24,28},{1,5},{5,9},{9,... | collective-permute-start | bytes 786440 | tf_op jit(solution)/shard_map/ppermute | solution.py:294
  17.3 0.7 copy-done.5
  18.0 0.7 copy-done.6
  18.6 0.2 masks.1
  18.9 0.1 pad_add_fusion.1.ids_ref
  19.0 9.0 %collective-permute-done.refs_0_ = bf16[512,256]{1,0:T(8,128)(2,1)S(1)} collective-permute-done((bf16[512,256]{1,0:T(8,128)(2,1)S(1)}, bf16[512,256]{1,0:T(8,128)(2,1)S(1)}, u32[]{:S(2)}, u32[]{:S(2)}) %collective-permute-start) | collective-permute-done | bytes 262176 | tf_op jit(solution)/shard_map/ppermute | solution.py:294
  28.0 6.8 %collective-permute-done.1.refs_1_ = bf16[512,256]{1,0:T(8,128)(2,1)S(1)} collective-permute-done((bf16[512,256]{1,0:T(8,128)(2,1)S(1)}, bf16[512,256]{1,0:T(8,128)(2,1)S(1)}, u32[]{:S(2)}, u32[]{:S(2)}) %collective-permute-start.1) | collective-permute-done | bytes 262176 | tf_op jit(solution)/shard_map/ppermute | solution.py:294
  34.8 1.2 %copy-done.7 = bf16[512,1024]{1,0:T(8,128)(2,1)S(1)} copy-done((bf16[512,1024]{1,0:T(8,128)(2,1)S(1)}, bf16[512,1024]{1,0:T(8,128)(2,1)}, u32[]{:S(2)}) %copy-start.7) | copy-done | bytes 1048600
  36.1 9.6 %attend.2.a_ref = bf16[256,1024]{1,0:T(8,128)(2,1)S(1)} custom-call(s32[4]{0:T(128)S(1)} %pad_add_fusion.1.ids_ref, bf16[512,1024]{1,0:T(8,128)(2,1)S(1)} %copy-done.7, f32[8,8,128]{2,1,0:T(8,128)S(1)} %get-tuple-element.25.win_ref, f32[8,8,128]{2,1,0:T(8,128)S(1)} %get-tuple-element.26.pool_ref, bf16[512,256]{1,0:T(8,128)(2,1)S(1)} %collective-permute-done.refs_0_, ...), custom_call_target="tpu_custom_call" | custom-call | flops 3758096384 | bytes 1048576 | tf_op jit(solution)/shard_map/attend/pallas_call | solution.py:205
  45.7 5.8 %copy-done = bf16[1024,8192]{1,0:T(8,128)(2,1)S(1)} copy-done((bf16[1024,8192]{1,0:T(8,128)(2,1)S(1)}, bf16[1024,8192]{1,0:T(8,128)(2,1)}, u32[]{:S(2)}) %copy-start) | copy-done | bytes 16777240
  51.4 1.8 %project.8 = (bf16[128,2048]{1,0:T(8,128)(2,1)S(1)}, bf16[128,2048]{1,0:T(8,128)(2,1)S(1)}) custom-call(bf16[256,1024]{1,0:T(8,128)(2,1)S(1)} %attend.2.a_ref, bf16[1024,8192]{1,0:T(8,128)(2,1)S(1)} %copy-done, bf16[1024,8192]{1,0:T(8,128)(2,1)S(1)} %copy-done, bf16[1024,8192]{1,0:T(8,128)(2,1)S(1)} %copy-done, bf16[1024,8192]{1,0:T(8,128)(2,1)S(1)} %copy-done), custom_call_target="tpu_custom_call" | custom-call | flops 1073741824 | bytes 5242880 | tf_op jit(solution)/shard_map/project/pallas_call | solution.py:258
  53.2 0.1 collective-permute-start.2
  53.4 5.8 %copy-done.1 = bf16[1024,8192]{1,0:T(8,128)(2,1)S(1)} copy-done((bf16[1024,8192]{1,0:T(8,128)(2,1)S(1)}, bf16[1024,8192]{1,0:T(8,128)(2,1)}, u32[]{:S(2)}) %copy-start.1) | copy-done | bytes 16777240
  59.2 1.8 %project.10 = (bf16[128,2048]{1,0:T(8,128)(2,1)S(1)}, bf16[128,2048]{1,0:T(8,128)(2,1)S(1)}) custom-call(bf16[256,1024]{1,0:T(8,128)(2,1)S(1)} %attend.2.a_ref, bf16[1024,8192]{1,0:T(8,128)(2,1)S(1)} %copy-done.1, bf16[1024,8192]{1,0:T(8,128)(2,1)S(1)} %copy-done.1, bf16[1024,8192]{1,0:T(8,128)(2,1)S(1)} %copy-done.1, bf16[1024,8192]{1,0:T(8,128)(2,1)S(1)} %copy-done.1), custom_call_target="tpu_custom_call" | custom-call | flops 1073741824 | bytes 5242880 | tf_op jit(solution)/shard_map/project/pallas_call | solution.py:258
  61.0 0.6 collective-permute-start.4
  61.5 0.1 add_convert_fusion.11.refs_4_
  61.7 1.6 %collective-permute-start.7 = (bf16[128,2048]{1,0:T(8,128)(2,1)S(1)}, bf16[128,2048]{1,0:T(8,128)(2,1)S(1)}, u32[]{:S(2)}, u32[]{:S(2)}) collective-permute-start(bf16[128,2048]{1,0:T(8,128)(2,1)S(1)} %add_convert_fusion.11.refs_4_), channel_id=1, source_target_pairs={{0,2},{1,3},{2,0},{3,1},{4,6},{5,7},{6,4},{7,5},{8,10},{9,11},{10,... | collective-permute-start | bytes 1572872 | tf_op jit(solution)/shard_map/ppermute | solution.py:311
  63.2 1.8 %project.9 = (bf16[128,2048]{1,0:T(8,128)(2,1)S(1)}, bf16[128,2048]{1,0:T(8,128)(2,1)S(1)}) custom-call(bf16[256,1024]{1,0:T(8,128)(2,1)S(1)} %attend.2.a_ref, bf16[1024,8192]{1,0:T(8,128)(2,1)S(1)} %copy-done.1, bf16[1024,8192]{1,0:T(8,128)(2,1)S(1)} %copy-done.1, bf16[1024,8192]{1,0:T(8,128)(2,1)S(1)} %copy-done.1, bf16[1024,8192]{1,0:T(8,128)(2,1)S(1)} %copy-done.1, ...), custom_call_target="tpu_custom_call" | custom-call | flops 1073741824 | bytes 5242880 | tf_op jit(solution)/shard_map/project/pallas_call | solution.py:258
  65.1 0.1 add_convert_fusion.9.refs_4_
  65.3 1.8 %project.11 = (bf16[128,2048]{1,0:T(8,128)(2,1)S(1)}, bf16[128,2048]{1,0:T(8,128)(2,1)S(1)}) custom-call(bf16[256,1024]{1,0:T(8,128)(2,1)S(1)} %attend.2.a_ref, bf16[1024,8192]{1,0:T(8,128)(2,1)S(1)} %copy-done.1, bf16[1024,8192]{1,0:T(8,128)(2,1)S(1)} %copy-done.1, bf16[1024,8192]{1,0:T(8,128)(2,1)S(1)} %copy-done.1, bf16[1024,8192]{1,0:T(8,128)(2,1)S(1)} %copy-done.1, ...), custom_call_target="tpu_custom_call" | custom-call | flops 1073741824 | bytes 5242880 | tf_op jit(solution)/shard_map/project/pallas_call | solution.py:258
  67.1 0.6 collective-permute-start.5
  67.7 0.1 add_convert_fusion.10.refs_4_
  67.8 9.6 %attend.3.a_ref = bf16[256,1024]{1,0:T(8,128)(2,1)S(1)} custom-call(s32[4]{0:T(128)S(1)} %pad_add_fusion.ids_ref, bf16[512,1024]{1,0:T(8,128)(2,1)S(1)} %copy-done.8, f32[8,8,128]{2,1,0:T(8,128)S(1)} %get-tuple-element.25.win_ref, f32[8,8,128]{2,1,0:T(8,128)S(1)} %get-tuple-element.26.pool_ref, bf16[512,256]{1,0:T(8,128)(2,1)S(1)} %collective-permute-done.refs_0_, ...), custom_call_target="tpu_custom_call" | custom-call | flops 3758096384 | bytes 1048576 | tf_op jit(solution)/shard_map/attend/pallas_call | solution.py:205
  77.4 0.1 add_convert_fusion.8.refs_4_
  77.6 1.8 %project.12 = (bf16[128,2048]{1,0:T(8,128)(2,1)S(1)}, bf16[128,2048]{1,0:T(8,128)(2,1)S(1)}) custom-call(bf16[256,1024]{1,0:T(8,128)(2,1)S(1)} %attend.3.a_ref, bf16[1024,8192]{1,0:T(8,128)(2,1)S(1)} %bitcast.2, bf16[1024,8192]{1,0:T(8,128)(2,1)S(1)} %bitcast.2, bf16[1024,8192]{1,0:T(8,128)(2,1)S(1)} %bitcast.2, bf16[1024,8192]{1,0:T(8,128)(2,1)S(1)} %bitcast.2, ...), custom_call_target="tpu_custom_call" | custom-call | flops 1073741824 | bytes 5242880 | tf_op jit(solution)/shard_map/project/pallas_call | solution.py:258
  79.4 0.1 collective-permute-start.6
  79.5 0.6 collective-permute-start.9
  80.1 1.8 %project.13 = (bf16[128,2048]{1,0:T(8,128)(2,1)S(1)}, bf16[128,2048]{1,0:T(8,128)(2,1)S(1)}) custom-call(bf16[256,1024]{1,0:T(8,128)(2,1)S(1)} %attend.3.a_ref, bf16[1024,8192]{1,0:T(8,128)(2,1)S(1)} %bitcast.2, bf16[1024,8192]{1,0:T(8,128)(2,1)S(1)} %bitcast.2, bf16[1024,8192]{1,0:T(8,128)(2,1)S(1)} %bitcast.2, bf16[1024,8192]{1,0:T(8,128)(2,1)S(1)} %bitcast.2, ...), custom_call_target="tpu_custom_call" | custom-call | flops 1073741824 | bytes 5242880 | tf_op jit(solution)/shard_map/project/pallas_call | solution.py:258
  81.9 0.2 collective-permute-start.8
  82.2 1.8 %project.14 = (bf16[128,2048]{1,0:T(8,128)(2,1)S(1)}, bf16[128,2048]{1,0:T(8,128)(2,1)S(1)}) custom-call(bf16[256,1024]{1,0:T(8,128)(2,1)S(1)} %attend.3.a_ref, bf16[1024,8192]{1,0:T(8,128)(2,1)S(1)} %bitcast.2, bf16[1024,8192]{1,0:T(8,128)(2,1)S(1)} %bitcast.2, bf16[1024,8192]{1,0:T(8,128)(2,1)S(1)} %bitcast.2, bf16[1024,8192]{1,0:T(8,128)(2,1)S(1)} %bitcast.2, ...), custom_call_target="tpu_custom_call" | custom-call | flops 1073741824 | bytes 5242880 | tf_op jit(solution)/shard_map/project/pallas_call | solution.py:258
  84.0 0.4 collective-permute-start.10
  84.4 1.8 %project.15 = (bf16[128,2048]{1,0:T(8,128)(2,1)S(1)}, bf16[128,2048]{1,0:T(8,128)(2,1)S(1)}) custom-call(bf16[256,1024]{1,0:T(8,128)(2,1)S(1)} %attend.3.a_ref, bf16[1024,8192]{1,0:T(8,128)(2,1)S(1)} %bitcast.2, bf16[1024,8192]{1,0:T(8,128)(2,1)S(1)} %bitcast.2, bf16[1024,8192]{1,0:T(8,128)(2,1)S(1)} %bitcast.2, bf16[1024,8192]{1,0:T(8,128)(2,1)S(1)} %bitcast.2, ...), custom_call_target="tpu_custom_call" | custom-call | flops 1073741824 | bytes 5242880 | tf_op jit(solution)/shard_map/project/pallas_call | solution.py:258
  86.2 1.6 %collective-permute-start.11 = (bf16[128,2048]{1,0:T(8,128)(2,1)S(1)}, bf16[128,2048]{1,0:T(8,128)(2,1)S(1)}, u32[]{:S(2)}, u32[]{:S(2)}) collective-permute-start(bf16[128,2048]{1,0:T(8,128)(2,1)S(1)} %add_convert_fusion.10.refs_4_), channel_id=1, source_target_pairs={{0,2},{1,3},{2,0},{3,1},{4,6},{5,7},{6,4},{7,5},{8,10},{9,11},{10,... | collective-permute-start | bytes 1572872 | tf_op jit(solution)/shard_map/ppermute | solution.py:311
  87.8 0.5 collective-permute-start.13
  88.3 0.3 add_convert_fusion.6
  88.6 5.7 %collective-permute-done.9 = bf16[128,2048]{1,0:T(8,128)(2,1)S(1)} collective-permute-done((bf16[128,2048]{1,0:T(8,128)(2,1)S(1)}, bf16[128,2048]{1,0:T(8,128)(2,1)S(1)}, u32[]{:S(2)}, u32[]{:S(2)}) %collective-permute-start.9) | collective-permute-done | bytes 524320 | tf_op jit(solution)/shard_map/ppermute | solution.py:311
  94.3 0.2 add_convert_fusion.4
  94.6 11.0 %collective-permute-done.11 = bf16[128,2048]{1,0:T(8,128)(2,1)S(1)} collective-permute-done((bf16[128,2048]{1,0:T(8,128)(2,1)S(1)}, bf16[128,2048]{1,0:T(8,128)(2,1)S(1)}, u32[]{:S(2)}, u32[]{:S(2)}) %collective-permute-start.11) | collective-permute-done | bytes 524320 | tf_op jit(solution)/shard_map/ppermute | solution.py:311
  105.5 0.3 add_convert_fusion.2
  105.8 10.5 %collective-permute-done.13 = bf16[128,2048]{1,0:T(8,128)(2,1)S(1)} collective-permute-done((bf16[128,2048]{1,0:T(8,128)(2,1)S(1)}, bf16[128,2048]{1,0:T(8,128)(2,1)S(1)}, u32[]{:S(2)}, u32[]{:S(2)}) %collective-permute-start.13) | collective-permute-done | bytes 524320 | tf_op jit(solution)/shard_map/ppermute | solution.py:311
  116.3 0.2 add_convert_fusion
  116.6 1.5 %pad_maximum_fusion = bf16[128,8192]{1,0:T(8,128)(2,1)} fusion(bf16[128,2048]{1,0:T(8,128)(2,1)S(1)} %add_convert_fusion, bf16[128,2048]{1,0:T(8,128)(2,1)S(1)} %add_convert_fusion.2, bf16[128,2048]{1,0:T(8,128)(2,1)S(1)} %add_convert_fusion.4, bf16[128,2048]{1,0:T(8,128)(2,1)S(1)} %add_convert_fusion.6), kind=kLoop, calls=%fused_computation | loop fusion | flops 8388608 | bytes 4194304 | tf_op jit(solution)/shard_map/concatenate | solution.py:329
  (34 shorter events, 0.2 us)
Async XLA Ops:
  0.0 0.9 copy-start.2
  0.9 0.9 copy-start.3
  1.8 0.7 copy-start.4
  4.3 30.5 %all-to-all-start = ((bf16[8,128,256]{2,1,0:T(8,128)(2,1)}), bf16[8,128,256]{2,1,0:T(8,128)(2,1)S(1)}, u32[]{:S(2)}, u32[]{:S(2)}) async-start(bf16[8,128,256]{2,1,0:T(8,128)(2,1)} %get-tuple-element.28), calls=%async_computation | async-start | bytes 1048576 | tf_op jit(solution)/shard_map/all_to_all | solution.py:298
  10.5 17.5 %collective-permute-start = (bf16[512,256]{1,0:T(8,128)(2,1)S(1)}, bf16[512,256]{1,0:T(8,128)(2,1)S(1)}, u32[]{:S(2)}, u32[]{:S(2)}) collective-permute-start(bf16[512,256]{1,0:T(8,128)(2,1)S(1)} %get-tuple-element.27.refs_2_), channel_id=1, source_target_pairs={{0,8},{4,12},{8,16},{12,20},{16,24},{20,28},{1,9},{5,13},{9,17},{1... | collective-permute-start | bytes 786440 | tf_op jit(solution)/shard_map/ppermute | solution.py:294
  13.9 20.9 %collective-permute-start.1 = (bf16[512,256]{1,0:T(8,128)(2,1)S(1)}, bf16[512,256]{1,0:T(8,128)(2,1)S(1)}, u32[]{:S(2)}, u32[]{:S(2)}) collective-permute-start(bf16[512,256]{1,0:T(8,128)(2,1)S(1)} %get-tuple-element.27.refs_2_), channel_id=1, source_target_pairs={{0,4},{4,8},{8,12},{12,16},{16,20},{20,24},{24,28},{1,5},{5,9},{9,... | collective-permute-start | bytes 786440 | tf_op jit(solution)/shard_map/ppermute | solution.py:294
  17.3 0.7 copy-start.5
  18.0 0.7 copy-start.6
  34.8 1.2 %copy-start.7 = (bf16[512,1024]{1,0:T(8,128)(2,1)S(1)}, bf16[512,1024]{1,0:T(8,128)(2,1)}, u32[]{:S(2)}) copy-start(bf16[512,1024]{1,0:T(8,128)(2,1)} %q_ref.3) | copy-start | bytes 3145732
  45.6 5.8 %copy-start = (bf16[1024,8192]{1,0:T(8,128)(2,1)S(1)}, bf16[1024,8192]{1,0:T(8,128)(2,1)}, u32[]{:S(2)}) copy-start(bf16[1024,8192]{1,0:T(8,128)(2,1)} %refs_3_.15) | copy-start | bytes 50331652
  53.2 8.3 %collective-permute-start.2 = (bf16[128,2048]{1,0:T(8,128)(2,1)S(1)}, bf16[128,2048]{1,0:T(8,128)(2,1)S(1)}, u32[]{:S(2)}, u32[]{:S(2)}) collective-permute-start(bf16[128,2048]{1,0:T(8,128)(2,1)S(1)} %get-tuple-element.30), channel_id=1, source_target_pairs={{0,1},{1,0},{2,3},{3,2},{4,5},{5,4},{6,7},{7,6},{8,9},{9,8},{10,11... | collective-permute-start | bytes 1572872 | tf_op jit(solution)/shard_map/ppermute | solution.py:308
  53.4 5.8 %copy-start.1 = (bf16[1024,8192]{1,0:T(8,128)(2,1)S(1)}, bf16[1024,8192]{1,0:T(8,128)(2,1)}, u32[]{:S(2)}) copy-start(bf16[1024,8192]{1,0:T(8,128)(2,1)} %refs_3_.15) | copy-start | bytes 50331652
  61.0 4.1 %collective-permute-start.4 = (bf16[128,2048]{1,0:T(8,128)(2,1)S(1)}, bf16[128,2048]{1,0:T(8,128)(2,1)S(1)}, u32[]{:S(2)}, u32[]{:S(2)}) collective-permute-start(bf16[128,2048]{1,0:T(8,128)(2,1)S(1)} %get-tuple-element.34), channel_id=1, source_target_pairs={{0,1},{1,0},{2,3},{3,2},{4,5},{5,4},{6,7},{7,6},{8,9},{9,8},{10,11... | collective-permute-start | bytes 1572872 | tf_op jit(solution)/shard_map/ppermute | solution.py:308
  61.7 24.6 %collective-permute-start.7 = (bf16[128,2048]{1,0:T(8,128)(2,1)S(1)}, bf16[128,2048]{1,0:T(8,128)(2,1)S(1)}, u32[]{:S(2)}, u32[]{:S(2)}) collective-permute-start(bf16[128,2048]{1,0:T(8,128)(2,1)S(1)} %add_convert_fusion.11.refs_4_), channel_id=1, source_target_pairs={{0,2},{1,3},{2,0},{3,1},{4,6},{5,7},{6,4},{7,5},{8,10},{9,11},{10,... | collective-permute-start | bytes 1572872 | tf_op jit(solution)/shard_map/ppermute | solution.py:311
  63.2 14.3 %slice-start = ((s8[16777216]{0:T(1024)(128)(4,1)}), s8[4194304]{0:T(1024)(128)(4,1)S(1)}, s32[]{:S(2)}) async-start(s8[16777216]{0:T(1024)(128)(4,1)} %bitcast.1), calls=%async_computation.1 | async-start | bytes 8388608
  63.2 14.4 %slice-start.1 = ((s8[16777216]{0:T(1024)(128)(4,1)}), s8[4194304]{0:T(1024)(128)(4,1)S(1)}, s32[]{:S(2)}) async-start(s8[16777216]{0:T(1024)(128)(4,1)} %bitcast.1), calls=%async_computation.2 | async-start | bytes 8388608
  65.0 2.6 %collective-permute-start.3 = (bf16[128,2048]{1,0:T(8,128)(2,1)S(1)}, bf16[128,2048]{1,0:T(8,128)(2,1)S(1)}, u32[]{:S(2)}, u32[]{:S(2)}) collective-permute-start(bf16[128,2048]{1,0:T(8,128)(2,1)S(1)} %get-tuple-element.32), channel_id=1, source_target_pairs={{0,1},{1,0},{2,3},{3,2},{4,5},{5,4},{6,7},{7,6},{8,9},{9,8},{10,11... | collective-permute-start | bytes 1572872 | tf_op jit(solution)/shard_map/ppermute | solution.py:308
  65.2 2.6 %copy-start.8 = (bf16[512,1024]{1,0:T(8,128)(2,1)S(1)}, bf16[512,1024]{1,0:T(8,128)(2,1)}, u32[]{:S(2)}) copy-start(bf16[512,1024]{1,0:T(8,128)(2,1)} %q_ref.3) | copy-start | bytes 3145732
  65.3 12.3 %slice-start.2 = ((s8[16777216]{0:T(1024)(128)(4,1)}), s8[4194304]{0:T(1024)(128)(4,1)S(1)}, s32[]{:S(2)}) async-start(s8[16777216]{0:T(1024)(128)(4,1)} %bitcast.1), calls=%async_computation.3 | async-start | bytes 8388608
  65.3 12.3 %slice-start.3 = ((s8[16777216]{0:T(1024)(128)(4,1)}), s8[4194304]{0:T(1024)(128)(4,1)S(1)}, s32[]{:S(2)}) async-start(s8[16777216]{0:T(1024)(128)(4,1)} %bitcast.1), calls=%async_computation.4 | async-start | bytes 8388608
  67.1 10.3 %collective-permute-start.5 = (bf16[128,2048]{1,0:T(8,128)(2,1)S(1)}, bf16[128,2048]{1,0:T(8,128)(2,1)S(1)}, u32[]{:S(2)}, u32[]{:S(2)}) collective-permute-start(bf16[128,2048]{1,0:T(8,128)(2,1)S(1)} %get-tuple-element.36), channel_id=1, source_target_pairs={{0,1},{1,0},{2,3},{3,2},{4,5},{5,4},{6,7},{7,6},{8,9},{9,8},{10,11... | collective-permute-start | bytes 1572872 | tf_op jit(solution)/shard_map/ppermute | solution.py:308
  79.4 8.3 %collective-permute-start.6 = (bf16[128,2048]{1,0:T(8,128)(2,1)S(1)}, bf16[128,2048]{1,0:T(8,128)(2,1)S(1)}, u32[]{:S(2)}, u32[]{:S(2)}) collective-permute-start(bf16[128,2048]{1,0:T(8,128)(2,1)S(1)} %get-tuple-element.38.refs_4_), channel_id=1, source_target_pairs={{0,1},{1,0},{2,3},{3,2},{4,5},{5,4},{6,7},{7,6},{8,9},{9,8},{10,11... | collective-permute-start | bytes 1572872 | tf_op jit(solution)/shard_map/ppermute | solution.py:308
  79.5 14.8 %collective-permute-start.9 = (bf16[128,2048]{1,0:T(8,128)(2,1)S(1)}, bf16[128,2048]{1,0:T(8,128)(2,1)S(1)}, u32[]{:S(2)}, u32[]{:S(2)}) collective-permute-start(bf16[128,2048]{1,0:T(8,128)(2,1)S(1)} %add_convert_fusion.9.refs_4_), channel_id=1, source_target_pairs={{0,2},{1,3},{2,0},{3,1},{4,6},{5,7},{6,4},{7,5},{8,10},{9,11},{10,... | collective-permute-start | bytes 1572872 | tf_op jit(solution)/shard_map/ppermute | solution.py:311
  81.9 12.4 %collective-permute-start.8 = (bf16[128,2048]{1,0:T(8,128)(2,1)S(1)}, bf16[128,2048]{1,0:T(8,128)(2,1)S(1)}, u32[]{:S(2)}, u32[]{:S(2)}) collective-permute-start(bf16[128,2048]{1,0:T(8,128)(2,1)S(1)} %get-tuple-element.40.refs_4_), channel_id=1, source_target_pairs={{0,1},{1,0},{2,3},{3,2},{4,5},{5,4},{6,7},{7,6},{8,9},{9,8},{10,11... | collective-permute-start | bytes 1572872 | tf_op jit(solution)/shard_map/ppermute | solution.py:308
  84.0 10.6 %collective-permute-start.10 = (bf16[128,2048]{1,0:T(8,128)(2,1)S(1)}, bf16[128,2048]{1,0:T(8,128)(2,1)S(1)}, u32[]{:S(2)}, u32[]{:S(2)}) collective-permute-start(bf16[128,2048]{1,0:T(8,128)(2,1)S(1)} %get-tuple-element.42.refs_4_), channel_id=1, source_target_pairs={{0,1},{1,0},{2,3},{3,2},{4,5},{5,4},{6,7},{7,6},{8,9},{9,8},{10,11... | collective-permute-start | bytes 1572872 | tf_op jit(solution)/shard_map/ppermute | solution.py:308
  86.2 19.3 %collective-permute-start.11 = (bf16[128,2048]{1,0:T(8,128)(2,1)S(1)}, bf16[128,2048]{1,0:T(8,128)(2,1)S(1)}, u32[]{:S(2)}, u32[]{:S(2)}) collective-permute-start(bf16[128,2048]{1,0:T(8,128)(2,1)S(1)} %add_convert_fusion.10.refs_4_), channel_id=1, source_target_pairs={{0,2},{1,3},{2,0},{3,1},{4,6},{5,7},{6,4},{7,5},{8,10},{9,11},{10,... | collective-permute-start | bytes 1572872 | tf_op jit(solution)/shard_map/ppermute | solution.py:311
  87.8 28.5 %collective-permute-start.13 = (bf16[128,2048]{1,0:T(8,128)(2,1)S(1)}, bf16[128,2048]{1,0:T(8,128)(2,1)S(1)}, u32[]{:S(2)}, u32[]{:S(2)}) collective-permute-start(bf16[128,2048]{1,0:T(8,128)(2,1)S(1)} %add_convert_fusion.8.refs_4_), channel_id=1, source_target_pairs={{0,2},{1,3},{2,0},{3,1},{4,6},{5,7},{6,4},{7,5},{8,10},{9,11},{10,... | collective-permute-start | bytes 1572872 | tf_op jit(solution)/shard_map/ppermute | solution.py:311
  94.3 11.5 %collective-permute-start.12 = (bf16[128,2048]{1,0:T(8,128)(2,1)S(1)}, bf16[128,2048]{1,0:T(8,128)(2,1)S(1)}, u32[]{:S(2)}, u32[]{:S(2)}) collective-permute-start(bf16[128,2048]{1,0:T(8,128)(2,1)S(1)} %get-tuple-element.44), channel_id=1, source_target_pairs={{0,1},{1,0},{2,3},{3,2},{4,5},{5,4},{6,7},{7,6},{8,9},{9,8},{10,11... | collective-permute-start | bytes 1572872 | tf_op jit(solution)/shard_map/ppermute | solution.py:308

commit v3 on v2

v3 whole, which is shorter than its diff:
```python
import functools

import jax
import jax.numpy as jnp
from jax import lax
from jax.experimental import pallas as pl
from jax.experimental.pallas import tpu as pltpu
from jax.sharding import PartitionSpec as P

HS = 128
BLK = 64
SPAN = 16
VMOST = 2
LANES = 128
MASKED = -1e30
EXP_SCALE = 1.4426950408889634 / (HS**0.5)
TILE = 1024
ACROSS = ((0, 2), (4, 4), (2, 2))
WEIGHT_PARTS = 4
MIB = 1024 * 1024


SHORT = pl.CostEstimate(flops=0, bytes_accessed=0, transcendentals=0)


def vmem():
    return pl.BlockSpec(memory_space=pltpu.VMEM)


def smem():
    return pl.BlockSpec(memory_space=pltpu.SMEM)


def anywhere():
    return pl.BlockSpec(memory_space=pl.ANY)


def params(mib):
    return pltpu.CompilerParams(vmem_limit_bytes=mib * MIB)


def pick_kernel(rank_ref, vert_ref, k_ref, v_ref, _, out_ref):
    local_blocks = k_ref.shape[0] // BLK
    block = vert_ref[...] - rank_ref[0] * local_blocks
    block = jnp.where((block >= 0) & (block < local_blocks), block, local_blocks)
    first = jnp.min(block)
    second = jnp.min(jnp.where(block > first, block, local_blocks))
    for slot, block in enumerate((first, second)):
        start = pl.multiple_of(jnp.minimum(block, local_blocks - 1) * BLK, BLK)
        out_ref[slot * BLK : (slot + 1) * BLK, :HS] = k_ref[pl.ds(start, BLK), :]
        out_ref[slot * BLK : (slot + 1) * BLK, HS:] = v_ref[pl.ds(start, BLK), :]


def pick(rank, vertical, keys, values, after):
    return pl.pallas_call(
        pick_kernel,
        out_shape=jax.ShapeDtypeStruct((VMOST * BLK, 2 * HS), keys.dtype),
        in_specs=[smem(), vmem(), vmem(), vmem(), anywhere()],
        out_specs=vmem(),
        compiler_params=params(56),
        name="pick",
    )(rank, vertical, keys, values, after)


def mask_kernel(local_blocks, near, rank_ref, vert_ref, slash_ref, win_ref, pool_ref):
    heads, vert_count = vert_ref.shape
    slash_count = slash_ref.shape[1]
    rank = rank_ref[0]
    lane = lax.broadcasted_iota(jnp.int32, (heads, LANES), 1)
    vert = [vert_ref[:, s : s + 1] for s in range(vert_count)]
    zero = jnp.zeros((heads, LANES), jnp.float32)

    def member(columns, blocks):
        found = columns[0] == blocks
        for column in columns[1:]:
            found = found | (column == blocks)
        return found

    offset_ok = member([slash_ref[:, s : s + 1] for s in range(slash_count)], SPAN - 1 - lane)
    shard = rank - (near - 1) - lane // VMOST
    first = jnp.full((1, LANES), local_blocks, jnp.int32)
    second = first
    for j in reversed(range(local_blocks)):
        here = member(vert, shard * local_blocks + j)
        here = jnp.max(jnp.where(here, 1, 0), axis=0, keepdims=True) == 1
        second = jnp.where(here, first, second)
        first = jnp.where(here, j, first)
    picked = jnp.where(lane % VMOST == 0, first, second)
    block = shard * local_blocks + picked
    pool_ok = (picked < local_blocks) & (shard >= 0) & member(vert, block)
    for i in range(local_blocks):
        row = rank * local_blocks + i
        seen = row - (SPAN - 1) + lane
        ok = (seen >= 0) & (offset_ok | member(vert, seen))
        win_ref[i] = jnp.where(ok | (lane >= SPAN), zero, MASKED)
        pool_ref[i] = jnp.where(pool_ok & (block < row - (SPAN - 1)), zero, MASKED)


def masks(rank, vertical, slash, local_blocks, near):
    heads = vertical.shape[0]
    shape = jax.ShapeDtypeStruct((local_blocks, heads, LANES), jnp.float32)
    return pl.pallas_call(
        functools.partial(mask_kernel, local_blocks, near),
        out_shape=(shape, shape),
        in_specs=[smem(), vmem(), vmem()],
        out_specs=(vmem(), vmem()),
        compiler_params=params(56),
        name="masks",
    )(rank, vertical, slash)


def attend_kernel(near, pools, with_rows, ids_ref, q_ref, win_ref, pool_ref, *refs):
    kv_refs = refs[: 2 * near]
    pair_refs = refs[2 * near : 2 * near + pools]
    w_hbm = refs[2 * near + pools]
    k_win, v_win, e_win, k_pool, v_pool, e_pool, attended, weight, arrival = refs[-9:]
    step = pl.program_id(0)
    heads = win_ref.shape[1]
    rows = kv_refs[0].shape[0]
    tiles, _, tile = weight.shape
    outs = refs[-9 - 2 * tiles - with_rows : -9]

    def fetch(t):
        return pltpu.make_async_copy(
            w_hbm.at[:, pl.ds(t * tile, tile)], weight.at[t], arrival.at[t]
        )

    @pl.when(step == 0)
    def _():
        for t in range(tiles):
            fetch(t).start()
        for s in range(near):
            k_win[s * rows : (s + 1) * rows, :] = kv_refs[2 * s][...]
            v_win[s * rows : (s + 1) * rows, :] = kv_refs[2 * s + 1][...]
        for s in range(pools):
            at = slice(s * VMOST * BLK, (s + 1) * VMOST * BLK)
            k_pool[at, :] = pair_refs[s][:, :HS]
            v_pool[at, :] = pair_refs[s][:, HS:]
        key = lax.broadcasted_iota(jnp.int32, e_win.shape, 0)
        lane = lax.broadcasted_iota(jnp.int32, e_win.shape, 1)
        last = (key // BLK == SPAN - 1) & (key % BLK == lane - BLK)
        e_win[...] = jnp.where((key // BLK == lane) | last, 1.0, 0.0).astype(e_win.dtype)
        key = lax.broadcasted_iota(jnp.int32, e_pool.shape, 0)
        lane = lax.broadcasted_iota(jnp.int32, e_pool.shape, 1)
        e_pool[...] = jnp.where(key // BLK == lane, 1.0, 0.0).astype(e_pool.dtype)

    here = ids_ref[step]
    q = q_ref[...]
    q = jnp.concatenate([q[:, h * HS : (h + 1) * HS] for h in range(heads)], axis=0)
    row = lax.broadcasted_iota(jnp.int32, (BLK, LANES), 0)
    lane = lax.broadcasted_iota(jnp.int32, (BLK, LANES), 1)
    above = jnp.where(lane - BLK > row, MASKED, 0.0).astype(jnp.float32)
    win_mask = win_ref[0][:, None, :] + above[None]
    win_mask = win_mask.reshape(heads * BLK, LANES).astype(q.dtype)
    pool_mask = jnp.broadcast_to(pool_ref[0][:, None, :], (heads, BLK, LANES))
    pool_mask = pool_mask.reshape(heads * BLK, LANES).astype(q.dtype)

    start = pl.multiple_of((here + 1) * BLK, BLK)
    keys = jnp.concatenate([k_win[pl.ds(start, SPAN * BLK), :], e_win[...]], axis=1)
    contract = (((1,), (1,)), ((), ()))
    near_scores = lax.dot_general(
        jnp.concatenate([q, win_mask], axis=1), keys, contract, preferred_element_type=jnp.float32
    )
    far_keys = jnp.concatenate([k_pool[...], e_pool[...]], axis=1)
    far_scores = lax.dot_general(
        jnp.concatenate([q, pool_mask], axis=1),
        far_keys,
        contract,
        preferred_element_type=jnp.float32,
    )
    top = jnp.maximum(
        jnp.max(near_scores, axis=1, keepdims=True), jnp.max(far_scores, axis=1, keepdims=True)
    )
    near_probs = jnp.exp2((near_scores - top) * EXP_SCALE).astype(q.dtype)
    far_probs = jnp.exp2((far_scores - top) * EXP_SCALE).astype(q.dtype)
    near_values = jnp.concatenate(
        [v_win[pl.ds(start, SPAN * BLK), :], jnp.ones((SPAN * BLK, LANES), q.dtype)], axis=1
    )
    far_values = jnp.concatenate(
        [v_pool[...], jnp.ones((v_pool.shape[0], LANES), q.dtype)], axis=1
    )
    summed = jnp.dot(near_probs, near_values, preferred_element_type=jnp.float32)
    summed = summed + jnp.dot(far_probs, far_values, preferred_element_type=jnp.float32)
    out = (summed[:, :HS] / summed[:, HS:]).astype(q.dtype)
    out_rows = pl.ds(pl.multiple_of(step * BLK, BLK), BLK)
    for h in range(heads):
        attended[out_rows, h * HS : (h + 1) * HS] = out[h * BLK : (h + 1) * BLK]

    @pl.when(step == pl.num_programs(0) - 1)
    def _():
        half = outs[0].shape[0]
        if with_rows:
            outs[-1][...] = attended[...]
        for t in range(tiles):
            fetch(t).wait()
            product = jnp.dot(attended[...], weight[t], preferred_element_type=jnp.float32)
            product = product.astype(q.dtype)
            outs[t][...] = product[:half]
            outs[tiles + t][...] = product[half:]


def attend(ids, queries, win, pool, near_kv, pairs, out_weight, tiles, with_rows, after):
    steps = ids.shape[0]
    width = queries.shape[1]
    heads = win.shape[1]
    near, pools = len(near_kv) // 2, len(pairs)
    rows = near_kv[0].shape[0]
    dtype = queries.dtype
    far = pools * VMOST * BLK

    def whole(shape):
        return pl.BlockSpec(shape, lambda g, ids: (0,) * len(shape))

    table = pl.BlockSpec((1, heads, LANES), lambda g, ids: (ids[g], 0, 0))
    out_shapes = [(steps * BLK // 2, TILE)] * (2 * tiles)
    if with_rows:
        out_shapes.append((steps * BLK, width))
    return pl.pallas_call(
        functools.partial(attend_kernel, near, pools, with_rows),
        out_shape=[jax.ShapeDtypeStruct(shape, dtype) for shape in out_shapes],
        grid_spec=pltpu.PrefetchScalarGridSpec(
            num_scalar_prefetch=1,
            grid=(steps,),
            in_specs=[pl.BlockSpec((BLK, width), lambda g, ids: (ids[g], 0)), table, table]
            + [whole(x.shape) for x in [*near_kv, *pairs]]
            + [anywhere() for _ in range(1 + len(after))],
            out_specs=[whole(shape) for shape in out_shapes],
            scratch_shapes=[
                pltpu.VMEM((near * rows, HS), dtype),
                pltpu.VMEM((near * rows, HS), dtype),
                pltpu.VMEM((SPAN * BLK, LANES), dtype),
                pltpu.VMEM((far, HS), dtype),
                pltpu.VMEM((far, HS), dtype),
                pltpu.VMEM((far, LANES), dtype),
                pltpu.VMEM((steps * BLK, width), dtype),
                pltpu.VMEM((tiles, out_weight.shape[0], TILE), dtype),
                pltpu.SemaphoreType.DMA((tiles,)),
            ],
        ),
        compiler_params=params(58),
        cost_estimate=SHORT,
        name="attend",
    )(ids, queries, win, pool, *near_kv, *pairs, out_weight, *after)


def project_kernel(a_ref, *refs):
    send_ref, keep_ref = refs[-2:]
    half = send_ref.shape[0]
    product = None
    for part in range(WEIGHT_PARTS):
        w = refs[part][...]
        depth = w.shape[0]
        term = jnp.dot(
            a_ref[:, part * depth : (part + 1) * depth], w, preferred_element_type=jnp.float32
        )
        product = term if product is None else product + term
    product = product.astype(send_ref.dtype)
    send_ref[...] = product[:half]
    keep_ref[...] = product[half:]


def project(attended, out_weight, tile, after):
    rows, depth = attended.shape
    half = jax.ShapeDtypeStruct((rows // 2, TILE), attended.dtype)

    def weight(part):
        return pl.BlockSpec((depth // WEIGHT_PARTS, TILE), lambda g: (part, tile))

    return pl.pallas_call(
        project_kernel,
        out_shape=(half, half),
        grid=(1,),
        in_specs=[pl.BlockSpec((rows, depth), lambda g: (0, 0))]
        + [weight(part) for part in range(WEIGHT_PARTS)]
        + [anywhere() for _ in after],
        out_specs=(vmem(), vmem()),
        compiler_params=params(50),
        cost_estimate=SHORT,
        name="project",
    )(attended, *[out_weight] * WEIGHT_PARTS, *after)


def add_kernel(*refs):
    out_ref = refs[-1]
    tiles = len(refs) // 2
    for t in range(tiles):
        total = refs[t][...].astype(jnp.float32) + refs[tiles + t][...].astype(jnp.float32)
        out_ref[:, t * TILE : (t + 1) * TILE] = total.astype(out_ref.dtype)


def add(keep, got):
    rows = keep[0].shape[0]
    return pl.pallas_call(
        add_kernel,
        out_shape=jax.ShapeDtypeStruct((rows, len(keep) * TILE), keep[0].dtype),
        in_specs=[vmem()] * (2 * len(keep)),
        out_specs=vmem(),
        compiler_params=params(50),
        cost_estimate=SHORT,
        name="add",
    )(*keep, *got)


def finish_kernel(tiles, *refs):
    arrived_ref, out_ref = refs[2 * tiles], refs[-1]
    for t in range(tiles):
        at = slice(t * TILE, (t + 1) * TILE)
        total = refs[t][...].astype(jnp.float32) + refs[tiles + t][...].astype(jnp.float32)
        out_ref[:, at] = (total + arrived_ref[:, at].astype(jnp.float32)).astype(out_ref.dtype)


def finish(keep, got, arrived, place, width, out):
    rows, columns = arrived.shape
    before = [] if out is None else [out]
    return pl.pallas_call(
        functools.partial(finish_kernel, len(keep)),
        out_shape=jax.ShapeDtypeStruct((rows, width), arrived.dtype),
        grid=(1,),
        in_specs=[vmem()] * (2 * len(keep) + 1) + [anywhere() for _ in before],
        out_specs=pl.BlockSpec((rows, columns), lambda g: (0, place)),
        input_output_aliases={2 * len(keep) + 1: 0} if before else {},
        compiler_params=params(50),
        cost_estimate=SHORT,
        name="finish",
    )(*keep, *got, arrived, *before)


def shards(ctx_size, queries, keys, values, out_weight, vertical, slash):
    local_blocks = queries.shape[0] // BLK
    near = 1 + -(-(SPAN - 1) // local_blocks)
    assert near == 3 and ctx_size % 2 == 0
    ctx_rank = lax.axis_index("ctx")
    tp_rank = lax.axis_index("tp")
    rank = jnp.reshape(ctx_rank, (1,)).astype(jnp.int32)
    odd = ctx_rank % 2 == 1

    def shifted(x, by):
        return lax.ppermute(x, "ctx", [(r, r + by) for r in range(ctx_size - by)])

    def swapped(x):
        return lax.ppermute(x, "ctx", [(r, r ^ 1) for r in range(ctx_size)])

    keys_2, values_2 = shifted(keys, 2), shifted(values, 2)
    keys_1 = swapped(jnp.where(odd, keys_2, keys))
    values_1 = swapped(jnp.where(odd, values_2, values))
    near_kv = [keys_2, values_2, keys_1, values_1, keys, values]
    own = pick(rank, vertical, keys, values, keys_2)
    pairs = [pick(rank - 2, vertical, keys_2, values_2, own)]
    pairs += [shifted(own, s) for s in range(near, ctx_size)]
    win, pool = masks(rank, vertical, slash, local_blocks, near)

    quarter = local_blocks // 4
    inner = jnp.arange(quarter, dtype=jnp.int32)

    def blocks_of(first, second):
        return jnp.concatenate([first * quarter + inner, second * quarter + inner])

    def sibling(x):
        return lax.ppermute(x, "tp", [(j, j ^ 1) for j in range(4)])

    def across(x):
        return lax.ppermute(x, "tp", [(j, j ^ 2) for j in range(4)])

    def attention(first, second, tiles, with_rows, after):
        ids = blocks_of(first, second)
        return attend(ids, queries, win, pool, near_kv, pairs, out_weight, tiles, with_rows, after)

    width = out_weight.shape[1]
    tiles = width // TILE
    head = ACROSS[0][1]
    assert ACROSS[0][0] == 0 and sum(count for _, count in ACROSS) == tiles
    *parts, attended = attention(tp_rank ^ 3, tp_rank ^ 2, head, True, ())
    keep = parts[head:]
    total = add(keep, [sibling(x) for x in parts[:head]])
    arrived = [across(total)]
    after = (total,)
    for first, count in ACROSS[1:]:
        keep, got = [], []
        for t in range(first, first + count):
            send, mine = project(attended, out_weight, t, after)
            keep.append(mine)
            got.append(sibling(send))
        total = add(keep, got)
        arrived.append(across(total))
        after = (total, arrived[0])
    parts = attention(tp_rank ^ 1, tp_rank, tiles, False, (total,))
    keep = parts[tiles:]
    got = [sibling(x) for x in parts[:tiles]]
    out = None
    for part, (first, count) in zip(arrived, ACROSS):
        assert first % count == 0
        at = slice(first, first + count)
        out = finish(keep[at], got[at], part, first // count, width, out)
    return out


def solution(mesh):
    assert mesh.shape["tp"] == 4
    return jax.shard_map(
        functools.partial(shards, mesh.shape["ctx"]),
        mesh=mesh,
        in_specs=(
            P("ctx", "tp"),
            P("ctx", "tp"),
            P("ctx", "tp"),
            P("tp", None),
            P("tp", None),
            P("tp", None),
        ),
        out_specs=P(("ctx", "tp"), None),
        check_vma=False,
    )
```

time: 119 us -> 115 us (0.966)
  the two profiles are of different devices: /device:TPU:16 before, /device:TPU:0 now
where the time goes in v3:
time: 115 us
  Pallas kernels  59.4 us (52%)
  starting transfers between devices  32.3 us (28%)
  waiting for transfers between devices  12.1 us (11%)
  local copies, waits for them, and re-layouts  7.41 us (6%)
  other arithmetic  3.06 us (3%)
    pallas_call x2, Pallas kernels, attend(): pl.pallas_call(functools.partial(attend_kernel, near, pools, with_rows),...  34.3 us
    ppermute x7, starting transfers between devices, shifted(): return lax.ppermute(x, 'ctx', [(r, r + by) for r in range(ctx_size - by)])  23.4 us
    pallas_call x6, Pallas kernels, project(): pl.pallas_call(project_kernel, out_shape=(half, half), grid=(1,), in_spec...  14.7 us
    ppermute x3, waiting for transfers between devices, across(): return lax.ppermute(x, 'tp', [(j, j ^ 2) for j in range(4)])  8.04 us
    unnamed x44, local copies, waits for them, and re-layouts  7.41 us
    ppermute x16, starting transfers between devices, sibling(): return lax.ppermute(x, 'tp', [(j, j ^ 1) for j in range(4)])  4.15 us
    ppermute x16, waiting for transfers between devices, sibling(): return lax.ppermute(x, 'tp', [(j, j ^ 1) for j in range(4)])  4.06 us
    pallas_call x2, Pallas kernels, pick(): pl.pallas_call(pick_kernel, out_shape=jax.ShapeDtypeStruct((VMOST * BLK,...  4.04 us
  transfers between devices with their start and end apart: 28, of which 9 were waited for; matrix products, arithmetic and copies ran while one was open for 3% of the time, Pallas kernels for 36%

profile of v3, /device:TPU:0, one launch (start us, length us, event | category | flops | bytes accessed | tf_op | source)
XLA Modules:
  0.0 114.6 jit_solution(5582988888554622031)
XLA Ops:
  0.0 4.9 %collective-permute-start = (bf16[512,128]{1,0:T(8,128)(2,1)}, bf16[512,128]{1,0:T(8,128)(2,1)S(1)}, u32[]{:S(2)}, u32[]{:S(2)}) collective-permute-start(bf16[512,128]{1,0:T(8,128)(2,1)} %refs_4_.3), channel_id=1, source_target_pairs={{0,8},{4,12},{8,16},{12,20},{16,24},{20,28},{1,9},{5,13},{9,17},{1... | collective-permute-start | bytes 393224 | tf_op jit(solution)/shard_map/ppermute | solution.py:338
  4.9 3.5 %collective-permute-start.1 = (bf16[512,128]{1,0:T(8,128)(2,1)}, bf16[512,128]{1,0:T(8,128)(2,1)S(1)}, u32[]{:S(2)}, u32[]{:S(2)}) collective-permute-start(bf16[512,128]{1,0:T(8,128)(2,1)} %refs_5_.3), channel_id=1, source_target_pairs={{0,8},{4,12},{8,16},{12,20},{16,24},{20,28},{1,9},{5,13},{9,17},{1... | collective-permute-start | bytes 393224 | tf_op jit(solution)/shard_map/ppermute | solution.py:338
  8.5 0.6 copy-done.13
  9.1 2.0 %pick.2._ = bf16[128,256]{1,0:T(8,128)(2,1)} custom-call(s32[1]{0:T(128)} %bitcast.rank_ref, s32[8,16]{1,0:T(8,128)} %vert_ref.5, bf16[512,128]{1,0:T(8,128)(2,1)} %refs_4_.3, bf16[512,128]{1,0:T(8,128)(2,1)} %refs_5_.3, bf16[512,128]{1,0:T(8,128)(2,1)} %copy-done.13), custom_call_target="tpu_custom_call" | custom-call | tf_op jit(solution)/shard_map/pick/pallas_call | solution.py:55
  11.1 7.7 %collective-permute-start.8 = (bf16[128,256]{1,0:T(8,128)(2,1)}, bf16[128,256]{1,0:T(8,128)(2,1)S(1)}, u32[]{:S(2)}, u32[]{:S(2)}) collective-permute-start(bf16[128,256]{1,0:T(8,128)(2,1)} %pick.2._), channel_id=1, source_target_pairs={{0,28},{1,29},{2,30},{3,31}} | collective-permute-start | bytes 196616 | tf_op jit(solution)/shard_map/ppermute | solution.py:338
  18.8 1.3 %collective-permute-start.7 = (bf16[128,256]{1,0:T(8,128)(2,1)}, bf16[128,256]{1,0:T(8,128)(2,1)S(1)}, u32[]{:S(2)}, u32[]{:S(2)}) collective-permute-start(bf16[128,256]{1,0:T(8,128)(2,1)} %pick.2._), channel_id=1, source_target_pairs={{0,24},{4,28},{1,25},{5,29},{2,26},{6,30},{3,27},{7,31}} | collective-permute-start | bytes 196616 | tf_op jit(solution)/shard_map/ppermute | solution.py:338
  20.1 0.9 broadcast_select_fusion.1
  21.1 0.6 collective-permute-start.2
  21.7 1.0 broadcast_select_fusion
  22.7 0.6 collective-permute-start.3
  23.2 1.6 %masks.1 = (f32[8,8,128]{2,1,0:T(8,128)}, f32[8,8,128]{2,1,0:T(8,128)}) custom-call(s32[1]{0:T(128)} %bitcast.rank_ref, s32[8,16]{1,0:T(8,128)} %vert_ref.5, s32[8,8]{1,0:T(8,128)} %slash_ref.1), custom_call_target="tpu_custom_call" | custom-call | tf_op jit(solution)/shard_map/masks/pallas_call | solution.py:102
  24.8 1.3 %collective-permute-start.6 = (bf16[128,256]{1,0:T(8,128)(2,1)}, bf16[128,256]{1,0:T(8,128)(2,1)S(1)}, u32[]{:S(2)}, u32[]{:S(2)}) collective-permute-start(bf16[128,256]{1,0:T(8,128)(2,1)} %pick.2._), channel_id=1, source_target_pairs={{0,20},{4,24},{8,28},{1,21},{5,25},{9,29},{2,22},{6,26},{10,30},{3... | collective-permute-start | bytes 196616 | tf_op jit(solution)/shard_map/ppermute | solution.py:338
  26.1 1.3 %collective-permute-start.5 = (bf16[128,256]{1,0:T(8,128)(2,1)}, bf16[128,256]{1,0:T(8,128)(2,1)S(1)}, u32[]{:S(2)}, u32[]{:S(2)}) collective-permute-start(bf16[128,256]{1,0:T(8,128)(2,1)} %pick.2._), channel_id=1, source_target_pairs={{0,16},{4,20},{8,24},{12,28},{1,17},{5,21},{9,25},{13,29},{2,18},{... | collective-permute-start | bytes 196616 | tf_op jit(solution)/shard_map/ppermute | solution.py:338
  27.4 3.4 %collective-permute-start.4 = (bf16[128,256]{1,0:T(8,128)(2,1)}, bf16[128,256]{1,0:T(8,128)(2,1)S(1)}, u32[]{:S(2)}, u32[]{:S(2)}) collective-permute-start(bf16[128,256]{1,0:T(8,128)(2,1)} %pick.2._), channel_id=1, source_target_pairs={{0,12},{4,16},{8,20},{12,24},{16,28},{1,13},{5,17},{9,21},{13,25},... | collective-permute-start | bytes 196616 | tf_op jit(solution)/shard_map/ppermute | solution.py:338
  30.9 0.6 pad_add_fusion.1.ids_ref
  31.4 2.0 %pick.3.refs_6_ = bf16[128,256]{1,0:T(8,128)(2,1)} custom-call(s32[1]{0:T(128)S(6)} %sub.3.rank_ref, s32[8,16]{1,0:T(8,128)} %vert_ref.5, bf16[512,128]{1,0:T(8,128)(2,1)} %copy-done.13, bf16[512,128]{1,0:T(8,128)(2,1)} %copy-done.14, bf16[128,256]{1,0:T(8,128)(2,1)} %pick.2._), custom_call_target="tpu_custom_call" | custom-call | tf_op jit(solution)/shard_map/pick/pallas_call | solution.py:55
  33.5 0.5 copy-done.19
  34.3 13.8 %attend.2 = (bf16[128,1024]{1,0:T(8,128)(2,1)}, bf16[128,1024]{1,0:T(8,128)(2,1)}, bf16[128,1024]{1,0:T(8,128)(2,1)}, bf16[128,1024]{1,0:T(8,128)(2,1)}, bf16[256,1024]{1,0:T(8,128)(2,1)}) custom-call(s32[4]{0:T(128)} %pad_add_fusion.1.ids_ref, bf16[512,1024]{1,0:T(8,128)(2,1)} %q_ref.3, f32[8,8,128]{2,1,0:T(8,128)} %get-tuple-element.40.win_ref, ...), custom_call_target="tpu_custom_call" | custom-call | tf_op jit(solution)/shard_map/attend/pallas_call | solution.py:218
  48.2 0.5 collective-permute-start.10
  48.7 1.2 %collective-permute-done.9.refs_2_ = bf16[128,1024]{1,0:T(8,128)(2,1)S(1)} collective-permute-done((bf16[128,1024]{1,0:T(8,128)(2,1)}, bf16[128,1024]{1,0:T(8,128)(2,1)S(1)}, u32[]{:S(2)}, u32[]{:S(2)}) %collective-permute-start.9) | collective-permute-done | bytes 262176 | tf_op jit(solution)/shard_map/ppermute | solution.py:359
  50.3 0.9 copy-done.11
  51.2 0.9 copy-done.12
  52.3 1.6 %collective-permute-start.15 = (bf16[128,2048]{1,0:T(8,128)(2,1)S(1)}, bf16[128,2048]{1,0:T(8,128)(2,1)S(1)}, u32[]{:S(2)}, u32[]{:S(2)}) collective-permute-start(bf16[128,2048]{1,0:T(8,128)(2,1)S(1)} %add.53.refs_4_), channel_id=1, source_target_pairs={{0,2},{1,3},{2,0},{3,1},{4,6},{5,7},{6,4},{7,5},{8,10},{9,11},{10,... | collective-permute-start | bytes 1572872 | tf_op jit(solution)/shard_map/ppermute | solution.py:362
  53.8 1.0 copy-done
  54.9 2.2 %project.9 = (bf16[128,1024]{1,0:T(8,128)(2,1)S(1)}, bf16[128,1024]{1,0:T(8,128)(2,1)S(1)}) custom-call(bf16[256,1024]{1,0:T(8,128)(2,1)S(1)} %copy-done, bf16[1024,8192]{1,0:T(8,128)(2,1)} %refs_12_.3, bf16[1024,8192]{1,0:T(8,128)(2,1)} %refs_12_.3, bf16[1024,8192]{1,0:T(8,128)(2,1)} %refs_12_.3, bf16[1024,8192]{1,0:T(8,128)(2,1)} %refs_12_.3, ...), custom_call_target="tpu_custom_call" | custom-call | tf_op jit(solution)/shard_map/project/pallas_call | solution.py:269
  57.1 2.2 %project.8 = (bf16[128,1024]{1,0:T(8,128)(2,1)S(1)}, bf16[128,1024]{1,0:T(8,128)(2,1)S(1)}) custom-call(bf16[256,1024]{1,0:T(8,128)(2,1)S(1)} %copy-done, bf16[1024,8192]{1,0:T(8,128)(2,1)} %refs_12_.3, bf16[1024,8192]{1,0:T(8,128)(2,1)} %refs_12_.3, bf16[1024,8192]{1,0:T(8,128)(2,1)} %refs_12_.3, bf16[1024,8192]{1,0:T(8,128)(2,1)} %refs_12_.3, ...), custom_call_target="tpu_custom_call" | custom-call | tf_op jit(solution)/shard_map/project/pallas_call | solution.py:269
  59.4 2.2 %project.7 = (bf16[128,1024]{1,0:T(8,128)(2,1)S(1)}, bf16[128,1024]{1,0:T(8,128)(2,1)S(1)}) custom-call(bf16[256,1024]{1,0:T(8,128)(2,1)S(1)} %copy-done, bf16[1024,8192]{1,0:T(8,128)(2,1)} %refs_12_.3, bf16[1024,8192]{1,0:T(8,128)(2,1)} %refs_12_.3, bf16[1024,8192]{1,0:T(8,128)(2,1)} %refs_12_.3, bf16[1024,8192]{1,0:T(8,128)(2,1)} %refs_12_.3, ...), custom_call_target="tpu_custom_call" | custom-call | tf_op jit(solution)/shard_map/project/pallas_call | solution.py:269
  61.6 2.2 %project.6 = (bf16[128,1024]{1,0:T(8,128)(2,1)S(1)}, bf16[128,1024]{1,0:T(8,128)(2,1)S(1)}) custom-call(bf16[256,1024]{1,0:T(8,128)(2,1)S(1)} %copy-done, bf16[1024,8192]{1,0:T(8,128)(2,1)} %refs_12_.3, bf16[1024,8192]{1,0:T(8,128)(2,1)} %refs_12_.3, bf16[1024,8192]{1,0:T(8,128)(2,1)} %refs_12_.3, bf16[1024,8192]{1,0:T(8,128)(2,1)} %refs_12_.3, ...), custom_call_target="tpu_custom_call" | custom-call | tf_op jit(solution)/shard_map/project/pallas_call | solution.py:269
  63.9 0.5 collective-permute-start.13
  64.5 0.4 collective-permute-start.11
  64.9 0.5 collective-permute-done.14.refs_7_
  65.8 0.4 collective-permute-done.12.refs_5_
  66.8 2.9 %project.10 = (bf16[128,1024]{1,0:T(8,128)(2,1)}, bf16[128,1024]{1,0:T(8,128)(2,1)S(1)}) custom-call(bf16[256,1024]{1,0:T(8,128)(2,1)S(1)} %copy-done.1, bf16[1024,8192]{1,0:T(8,128)(2,1)} %refs_12_.3, bf16[1024,8192]{1,0:T(8,128)(2,1)} %refs_12_.3, bf16[1024,8192]{1,0:T(8,128)(2,1)} %refs_12_.3, bf16[1024,8192]{1,0:T(8,128)(2,1)} %refs_12_.3, ...), custom_call_target="tpu_custom_call" | custom-call | tf_op jit(solution)/shard_map/project/pallas_call | solution.py:269
  69.9 2.9 %project.11 = (bf16[128,1024]{1,0:T(8,128)(2,1)}, bf16[128,1024]{1,0:T(8,128)(2,1)S(1)}) custom-call(bf16[256,1024]{1,0:T(8,128)(2,1)S(1)} %copy-done.1, bf16[1024,8192]{1,0:T(8,128)(2,1)} %refs_12_.3, bf16[1024,8192]{1,0:T(8,128)(2,1)} %refs_12_.3, bf16[1024,8192]{1,0:T(8,128)(2,1)} %refs_12_.3, bf16[1024,8192]{1,0:T(8,128)(2,1)} %refs_12_.3, ...), custom_call_target="tpu_custom_call" | custom-call | tf_op jit(solution)/shard_map/project/pallas_call | solution.py:269
  73.2 1.0 collective-permute-start.25
  74.1 0.6 pad_add_fusion.ids_ref
  74.7 1.1 add.55.refs_13_
  75.8 0.8 copy-done.2
  76.6 20.5 %attend.3 = (bf16[128,1024]{1,0:T(8,128)(2,1)}, bf16[128,1024]{1,0:T(8,128)(2,1)}, bf16[128,1024]{1,0:T(8,128)(2,1)}, bf16[128,1024]{1,0:T(8,128)(2,1)}, bf16[12...) custom-call(s32[4]{0:T(128)} %pad_add_fusion.ids_ref, ...), custom_call_target="tpu_custom_call" | custom-call | tf_op jit(solution)/shard_map/attend/pallas_call | solution.py:218
  98.2 0.7 collective-permute-done.21.refs_4_
  99.3 1.1 collective-permute-start.20
  100.4 0.5 collective-permute-start.18
  101.0 0.9 copy-done.3
  101.9 0.9 copy-done.4
  102.9 1.0 finish.3.refs_9_
  104.3 1.3 %finish.4.refs_5_ = bf16[128,8192]{1,0:T(8,128)(2,1)} custom-call(bf16[128,1024]{1,0:T(8,128)(2,1)S(1)} %copy-done.7, bf16[128,1024]{1,0:T(8,128)(2,1)S(1)} %copy-done.8, bf16[128,1024]{1,0:T(8,128)(2,1)S(1)} %copy-done.9, bf16[128,1024]{1,0:T(8,128)(2,1)S(1)} %copy-done.10, ...), custom_call_target="tpu_custom_call", output_to_operand_aliasing={{}: (9, {})} | custom-call | tf_op jit(solution)/shard_map/finish/pallas_call | solution.py:315
  105.6 8.0 %collective-permute-done.20.refs_4_ = bf16[128,2048]{1,0:T(8,128)(2,1)S(1)} collective-permute-done((bf16[128,2048]{1,0:T(8,128)(2,1)}, bf16[128,2048]{1,0:T(8,128)(2,1)S(1)}, u32[]{:S(2)}, u32[]{:S(2)}) %collective-permute-start.20) | collective-permute-done | bytes 524320 | tf_op jit(solution)/shard_map/ppermute | solution.py:362
  113.6 1.0 finish.5
  (75 shorter events, 4.4 us)
Async XLA Ops:
  0.0 8.4 %collective-permute-start = (bf16[512,128]{1,0:T(8,128)(2,1)}, bf16[512,128]{1,0:T(8,128)(2,1)S(1)}, u32[]{:S(2)}, u32[]{:S(2)}) collective-permute-start(bf16[512,128]{1,0:T(8,128)(2,1)} %refs_4_.3), channel_id=1, source_target_pairs={{0,8},{4,12},{8,16},{12,20},{16,24},{20,28},{1,9},{5,13},{9,17},{1... | collective-permute-start | bytes 393224 | tf_op jit(solution)/shard_map/ppermute | solution.py:338
  4.9 16.7 %collective-permute-start.1 = (bf16[512,128]{1,0:T(8,128)(2,1)}, bf16[512,128]{1,0:T(8,128)(2,1)S(1)}, u32[]{:S(2)}, u32[]{:S(2)}) collective-permute-start(bf16[512,128]{1,0:T(8,128)(2,1)} %refs_5_.3), channel_id=1, source_target_pairs={{0,8},{4,12},{8,16},{12,20},{16,24},{20,28},{1,9},{5,13},{9,17},{1... | collective-permute-start | bytes 393224 | tf_op jit(solution)/shard_map/ppermute | solution.py:338
  11.1 15.0 %collective-permute-start.8 = (bf16[128,256]{1,0:T(8,128)(2,1)}, bf16[128,256]{1,0:T(8,128)(2,1)S(1)}, u32[]{:S(2)}, u32[]{:S(2)}) collective-permute-start(bf16[128,256]{1,0:T(8,128)(2,1)} %pick.2._), channel_id=1, source_target_pairs={{0,28},{1,29},{2,30},{3,31}} | collective-permute-start | bytes 196616 | tf_op jit(solution)/shard_map/ppermute | solution.py:338
  18.8 8.6 %collective-permute-start.7 = (bf16[128,256]{1,0:T(8,128)(2,1)}, bf16[128,256]{1,0:T(8,128)(2,1)S(1)}, u32[]{:S(2)}, u32[]{:S(2)}) collective-permute-start(bf16[128,256]{1,0:T(8,128)(2,1)} %pick.2._), channel_id=1, source_target_pairs={{0,24},{4,28},{1,25},{5,29},{2,26},{6,30},{3,27},{7,31}} | collective-permute-start | bytes 196616 | tf_op jit(solution)/shard_map/ppermute | solution.py:338
  21.1 12.4 %collective-permute-start.2 = (bf16[512,128]{1,0:T(8,128)(2,1)S(1)}, bf16[512,128]{1,0:T(8,128)(2,1)S(1)}, u32[]{:S(2)}, u32[]{:S(2)}) collective-permute-start(bf16[512,128]{1,0:T(8,128)(2,1)S(1)} %broadcast_select_fusion.1), channel_id=1, source_target_pairs={{0,4},{4,0},{8,12},{12,8},{16,20},{20,16},{24,28},{28,24},{1,5},{5... | collective-permute-start | bytes 393224 | tf_op jit(solution)/shard_map/ppermute | solution.py:341
  21.7 9.7 %copy-start.14 = (bf16[512,128]{1,0:T(8,128)(2,1)}, bf16[512,128]{1,0:T(8,128)(2,1)S(1)}, u32[]{:S(2)}) copy-start(bf16[512,128]{1,0:T(8,128)(2,1)S(1)} %collective-permute-done.1.v_ref.refs_1_) | copy-start | bytes 393220
  22.7 10.9 %collective-permute-start.3 = (bf16[512,128]{1,0:T(8,128)(2,1)S(1)}, bf16[512,128]{1,0:T(8,128)(2,1)S(1)}, u32[]{:S(2)}, u32[]{:S(2)}) collective-permute-start(bf16[512,128]{1,0:T(8,128)(2,1)S(1)} %broadcast_select_fusion), channel_id=1, source_target_pairs={{0,4},{4,0},{8,12},{12,8},{16,20},{20,16},{24,28},{28,24},{1,5},{5... | collective-permute-start | bytes 393224 | tf_op jit(solution)/shard_map/ppermute | solution.py:341
  24.8 8.6 %collective-permute-start.6 = (bf16[128,256]{1,0:T(8,128)(2,1)}, bf16[128,256]{1,0:T(8,128)(2,1)S(1)}, u32[]{:S(2)}, u32[]{:S(2)}) collective-permute-start(bf16[128,256]{1,0:T(8,128)(2,1)} %pick.2._), channel_id=1, source_target_pairs={{0,20},{4,24},{8,28},{1,21},{5,25},{9,29},{2,22},{6,26},{10,30},{3... | collective-permute-start | bytes 196616 | tf_op jit(solution)/shard_map/ppermute | solution.py:338
  26.1 7.4 %copy-start.17 = (bf16[128,256]{1,0:T(8,128)(2,1)}, bf16[128,256]{1,0:T(8,128)(2,1)S(1)}, u32[]{:S(2)}) copy-start(bf16[128,256]{1,0:T(8,128)(2,1)S(1)} %collective-permute-done.8.refs_11_) | copy-start | bytes 196612
  26.1 7.3 %collective-permute-start.5 = (bf16[128,256]{1,0:T(8,128)(2,1)}, bf16[128,256]{1,0:T(8,128)(2,1)S(1)}, u32[]{:S(2)}, u32[]{:S(2)}) collective-permute-start(bf16[128,256]{1,0:T(8,128)(2,1)} %pick.2._), channel_id=1, source_target_pairs={{0,16},{4,20},{8,24},{12,28},{1,17},{5,21},{9,25},{13,29},{2,18},{... | collective-permute-start | bytes 196616 | tf_op jit(solution)/shard_map/ppermute | solution.py:338
  27.4 6.1 %copy-start.18 = (bf16[128,256]{1,0:T(8,128)(2,1)}, bf16[128,256]{1,0:T(8,128)(2,1)S(1)}, u32[]{:S(2)}) copy-start(bf16[128,256]{1,0:T(8,128)(2,1)S(1)} %collective-permute-done.7.refs_10_) | copy-start | bytes 196612
  27.4 6.0 %collective-permute-start.4 = (bf16[128,256]{1,0:T(8,128)(2,1)}, bf16[128,256]{1,0:T(8,128)(2,1)S(1)}, u32[]{:S(2)}, u32[]{:S(2)}) collective-permute-start(bf16[128,256]{1,0:T(8,128)(2,1)} %pick.2._), channel_id=1, source_target_pairs={{0,12},{4,16},{8,20},{12,24},{16,28},{1,13},{5,17},{9,21},{13,25},... | collective-permute-start | bytes 196616 | tf_op jit(solution)/shard_map/ppermute | solution.py:338
  33.5 0.7 copy-start.20
  33.5 0.6 copy-start.21
  33.5 0.7 copy-start.15
  33.5 0.7 copy-start.16
  48.1 1.8 %collective-permute-start.9 = (bf16[128,1024]{1,0:T(8,128)(2,1)}, bf16[128,1024]{1,0:T(8,128)(2,1)S(1)}, u32[]{:S(2)}, u32[]{:S(2)}) collective-permute-start(bf16[128,1024]{1,0:T(8,128)(2,1)} %get-tuple-element.45), channel_id=1, source_target_pairs={{0,1},{1,0},{2,3},{3,2},{4,5},{5,4},{6,7},{7,6},{8,9},{9,8},{10,11... | collective-permute-start | bytes 786440 | tf_op jit(solution)/shard_map/ppermute | solution.py:359
  48.2 2.1 %collective-permute-start.10 = (bf16[128,1024]{1,0:T(8,128)(2,1)}, bf16[128,1024]{1,0:T(8,128)(2,1)S(1)}, u32[]{:S(2)}, u32[]{:S(2)}) collective-permute-start(bf16[128,1024]{1,0:T(8,128)(2,1)} %get-tuple-element.46), channel_id=1, source_target_pairs={{0,1},{1,0},{2,3},{3,2},{4,5},{5,4},{6,7},{7,6},{8,9},{9,8},{10,11... | collective-permute-start | bytes 786440 | tf_op jit(solution)/shard_map/ppermute | solution.py:359
  50.3 1.0 copy-start.11
  51.2 0.9 copy-start.12
  52.3 14.5 %collective-permute-start.15 = (bf16[128,2048]{1,0:T(8,128)(2,1)S(1)}, bf16[128,2048]{1,0:T(8,128)(2,1)S(1)}, u32[]{:S(2)}, u32[]{:S(2)}) collective-permute-start(bf16[128,2048]{1,0:T(8,128)(2,1)S(1)} %add.53.refs_4_), channel_id=1, source_target_pairs={{0,2},{1,3},{2,0},{3,1},{4,6},{5,7},{6,4},{7,5},{8,10},{9,11},{10,... | collective-permute-start | bytes 1572872 | tf_op jit(solution)/shard_map/ppermute | solution.py:362
  53.8 1.0 copy-start
  63.8 3.0 %copy-start.1 = (bf16[256,1024]{1,0:T(8,128)(2,1)S(1)}, bf16[256,1024]{1,0:T(8,128)(2,1)}, u32[]{:S(2)}) copy-start(bf16[256,1024]{1,0:T(8,128)(2,1)} %get-tuple-element.42.a_ref) | copy-start | bytes 1572868
  63.8 1.6 %collective-permute-start.14 = (bf16[128,1024]{1,0:T(8,128)(2,1)S(1)}, bf16[128,1024]{1,0:T(8,128)(2,1)S(1)}, u32[]{:S(2)}, u32[]{:S(2)}) collective-permute-start(bf16[128,1024]{1,0:T(8,128)(2,1)S(1)} %get-tuple-element.54), channel_id=1, source_target_pairs={{0,1},{1,0},{2,3},{3,2},{4,5},{5,4},{6,7},{7,6},{8,9},{9,8},{10,11... | collective-permute-start | bytes 786440 | tf_op jit(solution)/shard_map/ppermute | solution.py:359
  63.9 1.9 %collective-permute-start.13 = (bf16[128,1024]{1,0:T(8,128)(2,1)S(1)}, bf16[128,1024]{1,0:T(8,128)(2,1)S(1)}, u32[]{:S(2)}, u32[]{:S(2)}) collective-permute-start(bf16[128,1024]{1,0:T(8,128)(2,1)S(1)} %get-tuple-element.53), channel_id=1, source_target_pairs={{0,1},{1,0},{2,3},{3,2},{4,5},{5,4},{6,7},{7,6},{8,9},{9,8},{10,11... | collective-permute-start | bytes 786440 | tf_op jit(solution)/shard_map/ppermute | solution.py:359
  64.4 1.8 %collective-permute-start.12 = (bf16[128,1024]{1,0:T(8,128)(2,1)S(1)}, bf16[128,1024]{1,0:T(8,128)(2,1)S(1)}, u32[]{:S(2)}, u32[]{:S(2)}) collective-permute-start(bf16[128,1024]{1,0:T(8,128)(2,1)S(1)} %get-tuple-element.52), channel_id=1, source_target_pairs={{0,1},{1,0},{2,3},{3,2},{4,5},{5,4},{6,7},{7,6},{8,9},{9,8},{10,11... | collective-permute-start | bytes 786440 | tf_op jit(solution)/shard_map/ppermute | solution.py:359
  64.5 2.1 %collective-permute-start.11 = (bf16[128,1024]{1,0:T(8,128)(2,1)S(1)}, bf16[128,1024]{1,0:T(8,128)(2,1)S(1)}, u32[]{:S(2)}, u32[]{:S(2)}) collective-permute-start(bf16[128,1024]{1,0:T(8,128)(2,1)S(1)} %get-tuple-element.51), channel_id=1, source_target_pairs={{0,1},{1,0},{2,3},{3,2},{4,5},{5,4},{6,7},{7,6},{8,9},{9,8},{10,11... | collective-permute-start | bytes 786440 | tf_op jit(solution)/shard_map/ppermute | solution.py:359
  69.7 5.0 %collective-permute-start.16 = (bf16[128,1024]{1,0:T(8,128)(2,1)}, bf16[128,1024]{1,0:T(8,128)(2,1)S(1)}, u32[]{:S(2)}, u32[]{:S(2)}) collective-permute-start(bf16[128,1024]{1,0:T(8,128)(2,1)} %get-tuple-element.57), channel_id=1, source_target_pairs={{0,1},{1,0},{2,3},{3,2},{4,5},{5,4},{6,7},{7,6},{8,9},{9,8},{10,11... | collective-permute-start | bytes 786440 | tf_op jit(solution)/shard_map/ppermute | solution.py:359
  72.8 1.9 %collective-permute-start.17 = (bf16[128,1024]{1,0:T(8,128)(2,1)}, bf16[128,1024]{1,0:T(8,128)(2,1)}, u32[]{:S(2)}, u32[]{:S(2)}) collective-permute-start(bf16[128,1024]{1,0:T(8,128)(2,1)} %get-tuple-element.58), channel_id=1, source_target_pairs={{0,1},{1,0},{2,3},{3,2},{4,5},{5,4},{6,7},{7,6},{8,9},{9,8},{10,11... | collective-permute-start | bytes 786440 | tf_op jit(solution)/shard_map/ppermute | solution.py:359
  73.2 30.7 %collective-permute-start.25 = (bf16[128,4096]{1,0:T(8,128)(2,1)S(1)}, bf16[128,4096]{1,0:T(8,128)(2,1)S(1)}, u32[]{:S(2)}, u32[]{:S(2)}) collective-permute-start(bf16[128,4096]{1,0:T(8,128)(2,1)S(1)} %add.54.refs_4_), channel_id=1, source_target_pairs={{0,2},{1,3},{2,0},{3,1},{4,6},{5,7},{6,4},{7,5},{8,10},{9,11},{10,... | collective-permute-start | bytes 3145736 | tf_op jit(solution)/shard_map/ppermute | solution.py:362
  75.8 0.8 copy-start.2
  97.1 1.8 %collective-permute-start.21 = (bf16[128,1024]{1,0:T(8,128)(2,1)}, bf16[128,1024]{1,0:T(8,128)(2,1)S(1)}, u32[]{:S(2)}, u32[]{:S(2)}) collective-permute-start(bf16[128,1024]{1,0:T(8,128)(2,1)} %get-tuple-element.67), channel_id=1, source_target_pairs={{0,1},{1,0},{2,3},{3,2},{4,5},{5,4},{6,7},{7,6},{8,9},{9,8},{10,11... | collective-permute-start | bytes 786440 | tf_op jit(solution)/shard_map/ppermute | solution.py:359
  97.5 1.8 %collective-permute-start.22 = (bf16[128,1024]{1,0:T(8,128)(2,1)}, bf16[128,1024]{1,0:T(8,128)(2,1)S(1)}, u32[]{:S(2)}, u32[]{:S(2)}) collective-permute-start(bf16[128,1024]{1,0:T(8,128)(2,1)} %get-tuple-element.68), channel_id=1, source_target_pairs={{0,1},{1,0},{2,3},{3,2},{4,5},{5,4},{6,7},{7,6},{8,9},{9,8},{10,11... | collective-permute-start | bytes 786440 | tf_op jit(solution)/shard_map/ppermute | solution.py:359
  97.7 2.7 %collective-permute-start.23 = (bf16[128,1024]{1,0:T(8,128)(2,1)}, bf16[128,1024]{1,0:T(8,128)(2,1)S(1)}, u32[]{:S(2)}, u32[]{:S(2)}) collective-permute-start(bf16[128,1024]{1,0:T(8,128)(2,1)} %get-tuple-element.69), channel_id=1, source_target_pairs={{0,1},{1,0},{2,3},{3,2},{4,5},{5,4},{6,7},{7,6},{8,9},{9,8},{10,11... | collective-permute-start | bytes 786440 | tf_op jit(solution)/shard_map/ppermute | solution.py:359
  98.0 2.4 %collective-permute-start.26 = (bf16[128,1024]{1,0:T(8,128)(2,1)}, bf16[128,1024]{1,0:T(8,128)(2,1)S(1)}, u32[]{:S(2)}, u32[]{:S(2)}) collective-permute-start(bf16[128,1024]{1,0:T(8,128)(2,1)} %get-tuple-element.73), channel_id=1, source_target_pairs={{0,1},{1,0},{2,3},{3,2},{4,5},{5,4},{6,7},{7,6},{8,9},{9,8},{10,11... | collective-permute-start | bytes 786440 | tf_op jit(solution)/shard_map/ppermute | solution.py:359
  98.9 2.0 %collective-permute-start.27 = (bf16[128,1024]{1,0:T(8,128)(2,1)}, bf16[128,1024]{1,0:T(8,128)(2,1)S(1)}, u32[]{:S(2)}, u32[]{:S(2)}) collective-permute-start(bf16[128,1024]{1,0:T(8,128)(2,1)} %get-tuple-element.74), channel_id=1, source_target_pairs={{0,1},{1,0},{2,3},{3,2},{4,5},{5,4},{6,7},{7,6},{8,9},{9,8},{10,11... | collective-permute-start | bytes 786440 | tf_op jit(solution)/shard_map/ppermute | solution.py:359
  99.3 14.3 %collective-permute-start.20 = (bf16[128,2048]{1,0:T(8,128)(2,1)}, bf16[128,2048]{1,0:T(8,128)(2,1)S(1)}, u32[]{:S(2)}, u32[]{:S(2)}) collective-permute-start(bf16[128,2048]{1,0:T(8,128)(2,1)} %copy-done.2), channel_id=1, source_target_pairs={{0,2},{1,3},{2,0},{3,1},{4,6},{5,7},{6,4},{7,5},{8,10},{9,11},{10,... | collective-permute-start | bytes 1572872 | tf_op jit(solution)/shard_map/ppermute | solution.py:362
  100.4 3.5 %collective-permute-start.24 = (bf16[128,1024]{1,0:T(8,128)(2,1)}, bf16[128,1024]{1,0:T(8,128)(2,1)S(1)}, u32[]{:S(2)}, u32[]{:S(2)}) collective-permute-start(bf16[128,1024]{1,0:T(8,128)(2,1)} %get-tuple-element.70), channel_id=1, source_target_pairs={{0,1},{1,0},{2,3},{3,2},{4,5},{5,4},{6,7},{7,6},{8,9},{9,8},{10,11... | collective-permute-start | bytes 786440 | tf_op jit(solution)/shard_map/ppermute | solution.py:359
  100.4 5.2 %collective-permute-start.18 = (bf16[128,1024]{1,0:T(8,128)(2,1)}, bf16[128,1024]{1,0:T(8,128)(2,1)S(1)}, u32[]{:S(2)}, u32[]{:S(2)}) collective-permute-start(bf16[128,1024]{1,0:T(8,128)(2,1)} %get-tuple-element.61), channel_id=1, source_target_pairs={{0,1},{1,0},{2,3},{3,2},{4,5},{5,4},{6,7},{7,6},{8,9},{9,8},{10,11... | collective-permute-start | bytes 786440 | tf_op jit(solution)/shard_map/ppermute | solution.py:359
  100.9 4.7 %collective-permute-start.19 = (bf16[128,1024]{1,0:T(8,128)(2,1)}, bf16[128,1024]{1,0:T(8,128)(2,1)S(1)}, u32[]{:S(2)}, u32[]{:S(2)}) collective-permute-start(bf16[128,1024]{1,0:T(8,128)(2,1)} %get-tuple-element.62), channel_id=1, source_target_pairs={{0,1},{1,0},{2,3},{3,2},{4,5},{5,4},{6,7},{7,6},{8,9},{9,8},{10,11... | collective-permute-start | bytes 786440 | tf_op jit(solution)/shard_map/ppermute | solution.py:359
  101.0 0.9 copy-start.3
  101.9 0.9 copy-start.4
  102.9 1.0 copy-start.7
  102.9 1.0 copy-start.8
  102.9 1.2 %copy-start.9 = (bf16[128,1024]{1,0:T(8,128)(2,1)S(1)}, bf16[128,1024]{1,0:T(8,128)(2,1)}, u32[]{:S(2)}) copy-start(bf16[128,1024]{1,0:T(8,128)(2,1)} %get-tuple-element.65.refs_2_) | copy-start | bytes 786436
  102.9 1.4 %copy-start.10 = (bf16[128,1024]{1,0:T(8,128)(2,1)S(1)}, bf16[128,1024]{1,0:T(8,128)(2,1)}, u32[]{:S(2)}) copy-start(bf16[128,1024]{1,0:T(8,128)(2,1)} %get-tuple-element.66.refs_3_) | copy-start | bytes 786436
  104.3 9.4 %copy-start.5 = (bf16[128,1024]{1,0:T(8,128)(2,1)S(1)}, bf16[128,1024]{1,0:T(8,128)(2,1)}, u32[]{:S(2)}) copy-start(bf16[128,1024]{1,0:T(8,128)(2,1)} %get-tuple-element.59.refs_0_) | copy-start | bytes 786436
  104.3 9.4 %copy-start.6 = (bf16[128,1024]{1,0:T(8,128)(2,1)S(1)}, bf16[128,1024]{1,0:T(8,128)(2,1)}, u32[]{:S(2)}) copy-start(bf16[128,1024]{1,0:T(8,128)(2,1)} %get-tuple-element.60.refs_1_) | copy-start | bytes 786436
  (2 other events, 1.3 us)

commit v4 on v3

--- a/solution.py
+++ b/solution.py
@@ -16,7 +16,6 @@
 EXP_SCALE = 1.4426950408889634 / (HS**0.5)
 TILE = 1024
 ACROSS = ((0, 2), (4, 4), (2, 2))
-WEIGHT_PARTS = 4
 MIB = 1024 * 1024
 
 
@@ -39,27 +38,37 @@
     return pltpu.CompilerParams(vmem_limit_bytes=mib * MIB)
 
 
-def pick_kernel(rank_ref, vert_ref, k_ref, v_ref, _, out_ref):
-    local_blocks = k_ref.shape[0] // BLK
-    block = vert_ref[...] - rank_ref[0] * local_blocks
+def picked_blocks(vertical, shard, local_blocks):
+    block = vertical - shard * local_blocks
     block = jnp.where((block >= 0) & (block < local_blocks), block, local_blocks)
     first = jnp.min(block)
     second = jnp.min(jnp.where(block > first, block, local_blocks))
-    for slot, block in enumerate((first, second)):
-        start = pl.multiple_of(jnp.minimum(block, local_blocks - 1) * BLK, BLK)
-        out_ref[slot * BLK : (slot + 1) * BLK, :HS] = k_ref[pl.ds(start, BLK), :]
-        out_ref[slot * BLK : (slot + 1) * BLK, HS:] = v_ref[pl.ds(start, BLK), :]
-
-
-def pick(rank, vertical, keys, values, after):
+    return [
+        pl.ds(pl.multiple_of(jnp.minimum(x, local_blocks - 1) * BLK, BLK), BLK)
+        for x in (first, second)
+    ]
+
+
+def pick_kernel(rank_ref, vert_ref, k_ref, v_ref, both_ref, pair_ref):
+    both_ref[:, :HS] = k_ref[...]
+    both_ref[:, HS:] = v_ref[...]
+    blocks = picked_blocks(vert_ref[...], rank_ref[0], k_ref.shape[0] // BLK)
+    for slot, rows in enumerate(blocks):
+        pair_ref[slot * BLK : (slot + 1) * BLK, :] = both_ref[rows, :]
+
+
+def pick(rank, vertical, keys, values):
     return pl.pallas_call(
         pick_kernel,
-        out_shape=jax.ShapeDtypeStruct((VMOST * BLK, 2 * HS), keys.dtype),
-        in_specs=[smem(), vmem(), vmem(), vmem(), anywhere()],
-        out_specs=vmem(),
-        compiler_params=params(56),
+        out_shape=(
+            jax.ShapeDtypeStruct((keys.shape[0], 2 * HS), keys.dtype),
+            jax.ShapeDtypeStruct((VMOST * BLK, 2 * HS), keys.dtype),
+        ),
+        in_specs=[smem(), vmem(), vmem(), vmem()],
+        out_specs=(vmem(), vmem()),
+        compiler_params=params(60),
         name="pick",
-    )(rank, vertical, keys, values, after)
+    )(rank, vertical, keys, values)
 
 
 def mask_kernel(local_blocks, near, rank_ref, vert_ref, slash_ref, win_ref, pool_ref):
@@ -104,15 +113,17 @@
         out_shape=(shape, shape),
         in_specs=[smem(), vmem(), vmem()],
         out_specs=(vmem(), vmem()),
-        compiler_params=params(56),
+        compiler_params=params(60),
         name="masks",
     )(rank, vertical, slash)
 
 
-def attend_kernel(near, pools, with_rows, ids_ref, q_ref, win_ref, pool_ref, *refs):
-    kv_refs = refs[: 2 * near]
-    pair_refs = refs[2 * near : 2 * near + pools]
-    w_hbm = refs[2 * near + pools]
+def attend_kernel(
+    near, pools, with_rows, here_of, tp_ref, ctx_ref, q_ref, win_ref, pool_ref, vert_ref, *refs
+):
+    kv_refs = refs[:near]
+    pair_refs = refs[near : near + pools - 1]
+    w_hbm = refs[near + pools - 1]
     k_win, v_win, e_win, k_pool, v_pool, e_pool, attended, weight, arrival = refs[-9:]
     step = pl.program_id(0)
     heads = win_ref.shape[1]
@@ -130,12 +141,16 @@
         for t in range(tiles):
             fetch(t).start()
         for s in range(near):
-            k_win[s * rows : (s + 1) * rows, :] = kv_refs[2 * s][...]
-            v_win[s * rows : (s + 1) * rows, :] = kv_refs[2 * s + 1][...]
-        for s in range(pools):
+            k_win[s * rows : (s + 1) * rows, :] = kv_refs[s][:, :HS]
+            v_win[s * rows : (s + 1) * rows, :] = kv_refs[s][:, HS:]
+        blocks = picked_blocks(vert_ref[...], ctx_ref[0] - (near - 1), rows // BLK)
+        for slot, block in enumerate(blocks):
+            k_pool[slot * BLK : (slot + 1) * BLK, :] = kv_refs[0][block, :HS]
+            v_pool[slot * BLK : (slot + 1) * BLK, :] = kv_refs[0][block, HS:]
+        for s in range(1, pools):
             at = slice(s * VMOST * BLK, (s + 1) * VMOST * BLK)
-            k_pool[at, :] = pair_refs[s][:, :HS]
-            v_pool[at, :] = pair_refs[s][:, HS:]
+            k_pool[at, :] = pair_refs[s - 1][:, :HS]
+            v_pool[at, :] = pair_refs[s - 1][:, HS:]
         key = lax.broadcasted_iota(jnp.int32, e_win.shape, 0)
         lane = lax.broadcasted_iota(jnp.int32, e_win.shape, 1)
         last = (key // BLK == SPAN - 1) & (key % BLK == lane - BLK)
@@ -144,7 +159,7 @@
         lane = lax.broadcasted_iota(jnp.int32, e_pool.shape, 1)
         e_pool[...] = jnp.where(key // BLK == lane, 1.0, 0.0).astype(e_pool.dtype)
 
-    here = ids_ref[step]
+    here = here_of(step, tp_ref)
     q = q_ref[...]
     q = jnp.concatenate([q[:, h * HS : (h + 1) * HS] for h in range(heads)], axis=0)
     row = lax.broadcasted_iota(jnp.int32, (BLK, LANES), 0)
@@ -199,30 +214,36 @@
             outs[tiles + t][...] = product[half:]
 
 
-def attend(ids, queries, win, pool, near_kv, pairs, out_weight, tiles, with_rows, after):
-    steps = ids.shape[0]
+def attend(flips, tp, ctx, queries, win, pool, vertical, near_kv, pairs, out_weight, tiles, with_rows, after):
     width = queries.shape[1]
-    heads = win.shape[1]
-    near, pools = len(near_kv) // 2, len(pairs)
+    local_blocks, heads, _ = win.shape
+    quarter = local_blocks // 4
+    steps = len(flips) * quarter
+    near, pools = len(near_kv), len(pairs) + 1
     rows = near_kv[0].shape[0]
     dtype = queries.dtype
     far = pools * VMOST * BLK
 
+    def here_of(step, tp_ref):
+        owner = tp_ref[0] ^ jnp.where(step < quarter, flips[0], flips[1])
+        return owner * quarter + step % quarter
+
     def whole(shape):
-        return pl.BlockSpec(shape, lambda g, ids: (0,) * len(shape))
-
-    table = pl.BlockSpec((1, heads, LANES), lambda g, ids: (ids[g], 0, 0))
+        return pl.BlockSpec(shape, lambda g, tp, ctx: (0,) * len(shape))
+
+    table = pl.BlockSpec((1, heads, LANES), lambda g, tp, ctx: (here_of(g, tp), 0, 0))
     out_shapes = [(steps * BLK // 2, TILE)] * (2 * tiles)
     if with_rows:
         out_shapes.append((steps * BLK, width))
     return pl.pallas_call(
-        functools.partial(attend_kernel, near, pools, with_rows),
+        functools.partial(attend_kernel, near, pools, with_rows, here_of),
         out_shape=[jax.ShapeDtypeStruct(shape, dtype) for shape in out_shapes],
         grid_spec=pltpu.PrefetchScalarGridSpec(
-            num_scalar_prefetch=1,
+            num_scalar_prefetch=2,
             grid=(steps,),
-            in_specs=[pl.BlockSpec((BLK, width), lambda g, ids: (ids[g], 0)), table, table]
-            + [whole(x.shape) for x in [*near_kv, *pairs]]
+            in_specs=[pl.BlockSpec((BLK, width), lambda g, tp, ctx: (here_of(g, tp), 0))]
+            + [table, table]
+            + [whole(x.shape) for x in [vertical, *near_kv, *pairs]]
             + [anywhere() for _ in range(1 + len(after))],
             out_specs=[whole(shape) for shape in out_shapes],
             scratch_shapes=[
@@ -237,47 +258,49 @@
                 pltpu.SemaphoreType.DMA((tiles,)),
             ],
         ),
-        compiler_params=params(58),
+        compiler_params=params(60),
         cost_estimate=SHORT,
         name="attend",
-    )(ids, queries, win, pool, *near_kv, *pairs, out_weight, *after)
-
-
-def project_kernel(a_ref, *refs):
-    send_ref, keep_ref = refs[-2:]
-    half = send_ref.shape[0]
-    product = None
-    for part in range(WEIGHT_PARTS):
-        w = refs[part][...]
-        depth = w.shape[0]
-        term = jnp.dot(
-            a_ref[:, part * depth : (part + 1) * depth], w, preferred_element_type=jnp.float32
+    )(tp, ctx, queries, win, pool, vertical, *near_kv, *pairs, out_weight, *after)
+
+
+def project_kernel(first, a_ref, w_hbm, *refs):
+    weight, arrival = refs[-2:]
+    tiles, _, tile = weight.shape
+    outs = refs[-2 - 2 * tiles : -2]
+    half = outs[0].shape[0]
+
+    def fetch(t):
+        return pltpu.make_async_copy(
+            w_hbm.at[:, pl.ds((first + t) * tile, tile)], weight.at[t], arrival.at[t]
         )
-        product = term if product is None else product + term
-    product = product.astype(send_ref.dtype)
-    send_ref[...] = product[:half]
-    keep_ref[...] = product[half:]
-
-
-def project(attended, out_weight, tile, after):
+
+    for t in range(tiles):
+        fetch(t).start()
+    for t in range(tiles):
+        fetch(t).wait()
+        product = jnp.dot(a_ref[...], weight[t], preferred_element_type=jnp.float32)
+        product = product.astype(a_ref.dtype)
+        outs[t][...] = product[:half]
+        outs[tiles + t][...] = product[half:]
+
+
+def project(attended, out_weight, first, tiles, after):
     rows, depth = attended.shape
     half = jax.ShapeDtypeStruct((rows // 2, TILE), attended.dtype)
-
-    def weight(part):
-        return pl.BlockSpec((depth // WEIGHT_PARTS, TILE), lambda g: (part, tile))
-
-    return pl.pallas_call(
-        project_kernel,
-        out_shape=(half, half),
-        grid=(1,),
-        in_specs=[pl.BlockSpec((rows, depth), lambda g: (0, 0))]
-        + [weight(part) for part in range(WEIGHT_PARTS)]
-        + [anywhere() for _ in after],
-        out_specs=(vmem(), vmem()),
-        compiler_params=params(50),
+    return pl.pallas_call(
+        functools.partial(project_kernel, first),
+        out_shape=[half] * (2 * tiles),
+        in_specs=[vmem(), anywhere()] + [anywhere() for _ in after],
+        out_specs=[vmem()] * (2 * tiles),
+        scratch_shapes=[
+            pltpu.VMEM((tiles, depth, TILE), attended.dtype),
+            pltpu.SemaphoreType.DMA((tiles,)),
+        ],
+        compiler_params=params(60),
         cost_estimate=SHORT,
         name="project",
-    )(attended, *[out_weight] * WEIGHT_PARTS, *after)
+    )(attended, out_weight, *after)
 
 
 def add_kernel(*refs):
@@ -295,7 +318,7 @@
         out_shape=jax.ShapeDtypeStruct((rows, len(keep) * TILE), keep[0].dtype),
         in_specs=[vmem()] * (2 * len(keep)),
         out_specs=vmem(),
-        compiler_params=params(50),
+        compiler_params=params(60),
         cost_estimate=SHORT,
         name="add",
     )(*keep, *got)
@@ -319,7 +342,7 @@
         in_specs=[vmem()] * (2 * len(keep) + 1) + [anywhere() for _ in before],
         out_specs=pl.BlockSpec((rows, columns), lambda g: (0, place)),
         input_output_aliases={2 * len(keep) + 1: 0} if before else {},
-        compiler_params=params(50),
+        compiler_params=params(16),
         cost_estimate=SHORT,
         name="finish",
     )(*keep, *got, arrived, *before)
@@ -328,32 +351,16 @@
 def shards(ctx_size, queries, keys, values, out_weight, vertical, slash):
     local_blocks = queries.shape[0] // BLK
     near = 1 + -(-(SPAN - 1) // local_blocks)
-    assert near == 3 and ctx_size % 2 == 0
-    ctx_rank = lax.axis_index("ctx")
-    tp_rank = lax.axis_index("tp")
-    rank = jnp.reshape(ctx_rank, (1,)).astype(jnp.int32)
-    odd = ctx_rank % 2 == 1
+    ctx = jnp.reshape(lax.axis_index("ctx"), (1,)).astype(jnp.int32)
+    tp = jnp.reshape(lax.axis_index("tp"), (1,)).astype(jnp.int32)
 
     def shifted(x, by):
         return lax.ppermute(x, "ctx", [(r, r + by) for r in range(ctx_size - by)])
 
-    def swapped(x):
-        return lax.ppermute(x, "ctx", [(r, r ^ 1) for r in range(ctx_size)])
-
-    keys_2, values_2 = shifted(keys, 2), shifted(values, 2)
-    keys_1 = swapped(jnp.where(odd, keys_2, keys))
-    values_1 = swapped(jnp.where(odd, values_2, values))
-    near_kv = [keys_2, values_2, keys_1, values_1, keys, values]
-    own = pick(rank, vertical, keys, values, keys_2)
-    pairs = [pick(rank - 2, vertical, keys_2, values_2, own)]
-    pairs += [shifted(own, s) for s in range(near, ctx_size)]
-    win, pool = masks(rank, vertical, slash, local_blocks, near)
-
-    quarter = local_blocks // 4
-    inner = jnp.arange(quarter, dtype=jnp.int32)
-
-    def blocks_of(first, second):
-        return jnp.concatenate([first * quarter + inner, second * quarter + inner])
+    own, pair = pick(ctx, vertical, keys, values)
+    near_kv = [shifted(own, s) for s in range(near - 1, 0, -1)] + [own]
+    pairs = [shifted(pair, s) for s in range(near, ctx_size)]
+    win, pool = masks(ctx, vertical, slash, local_blocks, near)
 
     def sibling(x):
         return lax.ppermute(x, "tp", [(j, j ^ 1) for j in range(4)])
@@ -361,29 +368,28 @@
     def across(x):
         return lax.ppermute(x, "tp", [(j, j ^ 2) for j in range(4)])
 
-    def attention(first, second, tiles, with_rows, after):
-        ids = blocks_of(first, second)
-        return attend(ids, queries, win, pool, near_kv, pairs, out_weight, tiles, with_rows, after)
+    def attention(flips, tiles, with_rows, after):
+        return attend(
+            flips, tp, ctx, queries, win, pool, vertical, near_kv, pairs, out_weight, tiles, with_rows, after
+        )
 
     width = out_weight.shape[1]
     tiles = width // TILE
     head = ACROSS[0][1]
     assert ACROSS[0][0] == 0 and sum(count for _, count in ACROSS) == tiles
-    *parts, attended = attention(tp_rank ^ 3, tp_rank ^ 2, head, True, ())
+    *parts, attended = attention((3, 2), head, True, ())
     keep = parts[head:]
-    total = add(keep, [sibling(x) for x in parts[:head]])
+    got = [sibling(x) for x in parts[:head]]
+    total = add(keep, got)
     arrived = [across(total)]
-    after = (total,)
+    rest = tiles - head
+    parts = project(attended, out_weight, head, rest, (total,))
+    keep += parts[rest:]
+    got += [sibling(x) for x in parts[:rest]]
     for first, count in ACROSS[1:]:
-        keep, got = [], []
-        for t in range(first, first + count):
-            send, mine = project(attended, out_weight, t, after)
-            keep.append(mine)
-            got.append(sibling(send))
-        total = add(keep, got)
+        total = add(keep[first : first + count], got[first : first + count])
         arrived.append(across(total))
-        after = (total, arrived[0])
-    parts = attention(tp_rank ^ 1, tp_rank, tiles, False, (total,))
+    parts = attention((1, 0), tiles, False, (total, arrived[0]))
     keep = parts[tiles:]
     got = [sibling(x) for x in parts[:tiles]]
     out = None

time: 115 us -> 111 us (0.965)
  waiting for transfers between devices: 12.1 us -> 16.7 us
  Pallas kernels: 59.4 us -> 55.1 us
  other arithmetic: 3.06 us -> 0 us
  starting transfers between devices: 32.3 us -> 31.1 us
    pallas_call x10 -> x4, Pallas kernels: 53.1 us -> 43.2 us  [the longest x2 33.2 us: attend(): pl.pallas_call(functools.partial(attend_kernel, near, pools, with_rows, h...]
    pallas_call x3, Pallas kernels: 1.43 us -> 6.96 us  [add(): pl.pallas_call(add_kernel, out_shape=jax.ShapeDtypeStruct((rows, len(keep...]
    ppermute x7, waiting for transfers between devices: 0.02 us -> 3.89 us  [shifted(): return lax.ppermute(x, 'ctx', [(r, r + by) for r in range(ctx_size - by)])]
    select_n x2 -> x0, other arithmetic: 1.9 us -> none  [the longest x1 0.97 us: shards(): values_1 = swapped(jnp.where(odd, values_2, values))]
    ppermute x3, waiting for transfers between devices: 8.04 us -> 9.89 us  [across(): return lax.ppermute(x, 'tp', [(j, j ^ 2) for j in range(4)])]
    ppermute x2 -> x0, starting transfers between devices: 1.21 us -> none  [swapped(): return lax.ppermute(x, 'ctx', [(r, r ^ 1) for r in range(ctx_size)])]
    ppermute x16, waiting for transfers between devices: 4.06 us -> 2.91 us  [sibling(): return lax.ppermute(x, 'tp', [(j, j ^ 1) for j in range(4)])]
    concatenate x2 -> x0, other arithmetic: 1.15 us -> none  [blocks_of(): return jnp.concatenate([first * quarter + inner, second * quarter + inner])]
  transfers between devices with their start and end apart: 28 -> 26, of which waited for: 9 -> 9; matrix products, arithmetic and copies ran while one was open for 3% -> 0% of each run, Pallas kernels for 36% -> 26%
where the time goes in v4:
time: 111 us; the launch traced here: 110 us
  Pallas kernels  55.1 us (50%)
  starting transfers between devices  31.1 us (28%)
  waiting for transfers between devices  16.7 us (15%)
  local copies, waits for them, and re-layouts  7.17 us (6%)
    pallas_call x2, Pallas kernels, attend(): pl.pallas_call(functools.partial(attend_kernel, near, pools, with_rows, h...  33.2 us
    ppermute x7, starting transfers between devices, shifted(): return lax.ppermute(x, 'ctx', [(r, r + by) for r in range(ctx_size - by)])  23.1 us
    ppermute x3, waiting for transfers between devices, across(): return lax.ppermute(x, 'tp', [(j, j ^ 2) for j in range(4)])  9.89 us
    pallas_call x1, Pallas kernels, project(): pl.pallas_call(functools.partial(project_kernel, first), out_shape=[half]...  8.01 us
    unnamed x54, local copies, waits for them, and re-layouts  7.17 us
    pallas_call x3, Pallas kernels, add(): pl.pallas_call(add_kernel, out_shape=jax.ShapeDtypeStruct((rows, len(keep...  6.96 us
    ppermute x3, starting transfers between devices, across(): return lax.ppermute(x, 'tp', [(j, j ^ 2) for j in range(4)])  4.21 us
    ppermute x7, waiting for transfers between devices, shifted(): return lax.ppermute(x, 'ctx', [(r, r + by) for r in range(ctx_size - by)])  3.89 us
  transfers between devices with their start and end apart: 26, of which 9 were waited for; matrix products, arithmetic and copies ran while one was open for 0% of the time, Pallas kernels for 26%

profile of v4, /device:TPU:0, one launch (start us, length us, event | category | flops | bytes accessed | tf_op | source)
XLA Modules:
  0.0 110.3 jit_solution(1967174273502217826)
XLA Ops:
  0.0 2.0 %pick.1 = (bf16[512,256]{1,0:T(8,128)(2,1)}, bf16[128,256]{1,0:T(8,128)(2,1)}) custom-call(s32[1]{0:T(128)} %bitcast.1.rank_ref.ctx_ref, s32[8,16]{1,0:T(8,128)} %vert_ref.7, bf16[512,128]{1,0:T(8,128)(2,1)} %k_ref.1, bf16[512,128]{1,0:T(8,128)(2,1)} %v_ref.1), custom_call_target="tpu_custom_call" | custom-call | tf_op jit(solution)/shard_map/pick/pallas_call | solution.py:61
  2.0 4.9 %collective-permute-start.1 = (bf16[512,256]{1,0:T(8,128)(2,1)}, bf16[512,256]{1,0:T(8,128)(2,1)S(1)}, u32[]{:S(2)}, u32[]{:S(2)}) collective-permute-start(bf16[512,256]{1,0:T(8,128)(2,1)} %get-tuple-element.44.refs_2_), channel_id=1, source_target_pairs={{0,4},{4,8},{8,12},{12,16},{16,20},{20,24},{24,28},{1,5},{5,9},{9,... | collective-permute-start | bytes 786440 | tf_op jit(solution)/shard_map/ppermute | solution.py:358
  6.9 3.5 %collective-permute-start = (bf16[512,256]{1,0:T(8,128)(2,1)}, bf16[512,256]{1,0:T(8,128)(2,1)S(1)}, u32[]{:S(2)}, u32[]{:S(2)}) collective-permute-start(bf16[512,256]{1,0:T(8,128)(2,1)} %get-tuple-element.44.refs_2_), channel_id=1, source_target_pairs={{0,8},{4,12},{8,16},{12,20},{16,24},{20,28},{1,9},{5,13},{9,17},{1... | collective-permute-start | bytes 786440 | tf_op jit(solution)/shard_map/ppermute | solution.py:358
  10.4 2.1 %collective-permute-start.6 = (bf16[128,256]{1,0:T(8,128)(2,1)}, bf16[128,256]{1,0:T(8,128)(2,1)S(1)}, u32[]{:S(2)}, u32[]{:S(2)}) collective-permute-start(bf16[128,256]{1,0:T(8,128)(2,1)} %get-tuple-element.45), channel_id=1, source_target_pairs={{0,28},{1,29},{2,30},{3,31}} | collective-permute-start | bytes 196616 | tf_op jit(solution)/shard_map/ppermute | solution.py:358
  12.5 1.8 %collective-permute-start.5 = (bf16[128,256]{1,0:T(8,128)(2,1)}, bf16[128,256]{1,0:T(8,128)(2,1)S(1)}, u32[]{:S(2)}, u32[]{:S(2)}) collective-permute-start(bf16[128,256]{1,0:T(8,128)(2,1)} %get-tuple-element.45), channel_id=1, source_target_pairs={{0,24},{4,28},{1,25},{5,29},{2,26},{6,30},{3,27},{7,31}} | collective-permute-start | bytes 196616 | tf_op jit(solution)/shard_map/ppermute | solution.py:358
  14.4 1.3 %collective-permute-start.4 = (bf16[128,256]{1,0:T(8,128)(2,1)}, bf16[128,256]{1,0:T(8,128)(2,1)S(1)}, u32[]{:S(2)}, u32[]{:S(2)}) collective-permute-start(bf16[128,256]{1,0:T(8,128)(2,1)} %get-tuple-element.45), channel_id=1, source_target_pairs={{0,20},{4,24},{8,28},{1,21},{5,25},{9,29},{2,22},{6,26},{10,30},{3... | collective-permute-start | bytes 196616 | tf_op jit(solution)/shard_map/ppermute | solution.py:358
  15.7 3.2 %collective-permute-done.6.refs_7_ = bf16[128,256]{1,0:T(8,128)(2,1)S(1)} collective-permute-done((bf16[128,256]{1,0:T(8,128)(2,1)}, bf16[128,256]{1,0:T(8,128)(2,1)S(1)}, u32[]{:S(2)}, u32[]{:S(2)}) %collective-permute-start.6) | collective-permute-done | bytes 65568 | tf_op jit(solution)/shard_map/ppermute | solution.py:358
  18.9 1.3 %collective-permute-start.3 = (bf16[128,256]{1,0:T(8,128)(2,1)}, bf16[128,256]{1,0:T(8,128)(2,1)S(1)}, u32[]{:S(2)}, u32[]{:S(2)}) collective-permute-start(bf16[128,256]{1,0:T(8,128)(2,1)} %get-tuple-element.45), channel_id=1, source_target_pairs={{0,16},{4,20},{8,24},{12,28},{1,17},{5,21},{9,25},{13,29},{2,18},{... | collective-permute-start | bytes 196616 | tf_op jit(solution)/shard_map/ppermute | solution.py:358
  20.2 8.2 %collective-permute-start.2 = (bf16[128,256]{1,0:T(8,128)(2,1)}, bf16[128,256]{1,0:T(8,128)(2,1)S(1)}, u32[]{:S(2)}, u32[]{:S(2)}) collective-permute-start(bf16[128,256]{1,0:T(8,128)(2,1)} %get-tuple-element.45), channel_id=1, source_target_pairs={{0,12},{4,16},{8,20},{12,24},{16,28},{1,13},{5,17},{9,21},{13,25},... | collective-permute-start | bytes 196616 | tf_op jit(solution)/shard_map/ppermute | solution.py:358
  28.4 1.5 %masks.1 = (f32[8,8,128]{2,1,0:T(8,128)}, f32[8,8,128]{2,1,0:T(8,128)}) custom-call(s32[1]{0:T(128)} %bitcast.1.rank_ref.ctx_ref, s32[8,16]{1,0:T(8,128)} %vert_ref.7, s32[8,8]{1,0:T(8,128)} %slash_ref.1), custom_call_target="tpu_custom_call" | custom-call | tf_op jit(solution)/shard_map/masks/pallas_call | solution.py:111
  30.0 0.6 collective-permute-done.2.refs_3_
  30.7 0.6 copy-done.18
  31.4 13.3 %attend.2 = (bf16[128,1024]{1,0:T(8,128)(2,1)}, bf16[128,1024]{1,0:T(8,128)(2,1)}, bf16[128,1024]{1,0:T(8,128)(2,1)}, bf16[128,1024]{1,0:T(8,128)(2,1)}, bf16[256,1024]{1,0:T(8,128)(2,1)}) custom-call(s32[1]{0:T(128)} %bitcast.tp_ref, s32[1]{0:T(128)} %bitcast.1.rank_ref.ctx_ref, bf16[512,1024]{1,0:T(8,128)(2,1)} %q_ref.3, ...), custom_call_target="tpu_custom_call" | custom-call | tf_op jit(solution)/shard_map/attend/pallas_call | solution.py:238
  44.8 0.5 collective-permute-start.8
  45.3 1.2 %collective-permute-done.7.refs_2_ = bf16[128,1024]{1,0:T(8,128)(2,1)S(1)} collective-permute-done((bf16[128,1024]{1,0:T(8,128)(2,1)}, bf16[128,1024]{1,0:T(8,128)(2,1)S(1)}, u32[]{:S(2)}, u32[]{:S(2)}) %collective-permute-start.7) | collective-permute-done | bytes 262176 | tf_op jit(solution)/shard_map/ppermute | solution.py:366
  46.6 0.4 collective-permute-done.8.refs_3_
  47.0 0.3 copy-done.25
  47.3 0.4 copy-done.26
  47.7 2.1 %add.3.refs_0_ = bf16[128,2048]{1,0:T(8,128)(2,1)} custom-call(bf16[128,1024]{1,0:T(8,128)(2,1)} %get-tuple-element.47.refs_0_, bf16[128,1024]{1,0:T(8,128)(2,1)} %get-tuple-element.48.refs_1_, bf16[128,1024]{1,0:T(8,128)(2,1)} %copy-done.25, bf16[128,1024]{1,0:T(8,128)(2,1)} %copy-done.26), custom_call_target="tpu_custom_call" | custom-call | tf_op jit(solution)/shard_map/add/pallas_call | solution.py:316
  49.8 8.0 %project.1 = (bf16[128,1024]{1,0:T(8,128)(2,1)}, bf16[128,1024]{1,0:T(8,128)(2,1)}, bf16[128,1024]{1,0:T(8,128)(2,1)}, bf16[128,1024]{1,0:T(8,128)(2,1)}, bf16[1...) custom-call(bf16[256,1024]{1,0:T(8,128)(2,1)} %get-tuple-element.46., ...), custom_call_target="tpu_custom_call" | custom-call | tf_op jit(solution)/shard_map/project/pallas_call | solution.py:291
  57.8 0.2 collective-permute-start.19
  58.0 0.4 collective-permute-start.20
  58.5 0.4 collective-permute-start.22
  58.9 1.5 %collective-permute-start.11 = (bf16[128,2048]{1,0:T(8,128)(2,1)S(1)}, bf16[128,2048]{1,0:T(8,128)(2,1)S(1)}, u32[]{:S(2)}, u32[]{:S(2)}) collective-permute-start(bf16[128,2048]{1,0:T(8,128)(2,1)S(1)} %copy-done.11), channel_id=1, source_target_pairs={{0,2},{1,3},{2,0},{3,1},{4,6},{5,7},{6,4},{7,5},{8,10},{9,11},{10,... | collective-permute-start | bytes 1572872 | tf_op jit(solution)/shard_map/ppermute | solution.py:369
  60.4 0.5 collective-permute-start.10
  61.2 0.4 copy-done.21
  61.7 2.8 %add.5 = bf16[128,4096]{1,0:T(8,128)(2,1)} custom-call(bf16[128,1024]{1,0:T(8,128)(2,1)} %get-tuple-element.67.refs_0_, bf16[128,1024]{1,0:T(8,128)(2,1)} %get-tuple-element.68.refs_1_, bf16[128,1024]{1,0:T(8,128)(2,1)} %get-tuple-element.69.refs_2_, bf16[128,1024]{1,0:T(8,128)(2,1)} %get-tuple-element.70.refs_3_, bf16[128,1024]{1,0:T(8,128)(2,1)} %copy-done.19, ...), custom_call_target="tpu_custom_call" | custom-call | tf_op jit(solution)/shard_map/add/pallas_call | solution.py:316
  64.5 1.2 %collective-permute-start.23 = (bf16[128,4096]{1,0:T(8,128)(2,1)}, bf16[128,4096]{1,0:T(8,128)(2,1)S(1)}, u32[]{:S(2)}, u32[]{:S(2)}) collective-permute-start(bf16[128,4096]{1,0:T(8,128)(2,1)} %add.5), channel_id=1, source_target_pairs={{0,2},{1,3},{2,0},{3,1},{4,6},{5,7},{6,4},{7,5},{8,10},{9,11},{10,... | collective-permute-start | bytes 3145736 | tf_op jit(solution)/shard_map/ppermute | solution.py:369
  65.7 0.7 copy-done.23
  66.5 2.1 %add.4.refs_9_ = bf16[128,2048]{1,0:T(8,128)(2,1)} custom-call(bf16[128,1024]{1,0:T(8,128)(2,1)} %get-tuple-element.51.refs_0_, bf16[128,1024]{1,0:T(8,128)(2,1)} %get-tuple-element.52.refs_1_, bf16[128,1024]{1,0:T(8,128)(2,1)} %copy-done.23, bf16[128,1024]{1,0:T(8,128)(2,1)} %copy-done.24), custom_call_target="tpu_custom_call" | custom-call | tf_op jit(solution)/shard_map/add/pallas_call | solution.py:316
  68.6 5.1 %collective-permute-done.11.refs_10_.refs_4_ = bf16[128,2048]{1,0:T(8,128)(2,1)S(1)} collective-permute-done((bf16[128,2048]{1,0:T(8,128)(2,1)S(1)}, bf16[128,2048]{1,0:T(8,128)(2,1)S(1)}, u32[]{:S(2)}, u32[]{:S(2)}) %collective-permute-start.11) | collective-permute-done | bytes 524320 | tf_op jit(solution)/shard_map/ppermute | solution.py:369
  73.6 0.8 copy-done
  74.4 19.9 %attend.3 = (bf16[128,1024]{1,0:T(8,128)(2,1)}, bf16[128,1024]{1,0:T(8,128)(2,1)}, bf16[128,1024]{1,0:T(8,128)(2,1)}, bf16[128,1024]{1,0:T(8,128)(2,1)}, bf16[12...) custom-call(s32[1]{0:T(128)} %bitcast.tp_ref, ...), custom_call_target="tpu_custom_call" | custom-call | tf_op jit(solution)/shard_map/attend/pallas_call | solution.py:238
  94.4 0.5 collective-permute-start.16
  95.0 1.5 %collective-permute-start.14 = (bf16[128,2048]{1,0:T(8,128)(2,1)S(1)}, bf16[128,2048]{1,0:T(8,128)(2,1)S(1)}, u32[]{:S(2)}, u32[]{:S(2)}) collective-permute-start(bf16[128,2048]{1,0:T(8,128)(2,1)S(1)} %copy-done.10), channel_id=1, source_target_pairs={{0,2},{1,3},{2,0},{3,1},{4,6},{5,7},{6,4},{7,5},{8,10},{9,11},{10,... | collective-permute-start | bytes 1572872 | tf_op jit(solution)/shard_map/ppermute | solution.py:369
  96.5 0.2 collective-permute-start.24
  96.7 0.3 collective-permute-start.25
  97.0 0.2 collective-permute-start.18
  97.2 1.1 collective-permute-done.24.refs_2_
  98.4 0.2 collective-permute-done.25.refs_3_
  98.8 1.0 copy-done.1
  99.8 0.9 copy-done.2
  100.8 0.9 copy-done.3
  101.7 1.0 finish.3.refs_9_
  102.9 0.2 copy-done.9
  103.1 1.3 %finish.4.refs_5_ = bf16[128,8192]{1,0:T(8,128)(2,1)} custom-call(bf16[128,1024]{1,0:T(8,128)(2,1)S(1)} %copy-done.6, bf16[128,1024]{1,0:T(8,128)(2,1)S(1)} %copy-done.7, bf16[128,1024]{1,0:T(8,128)(2,1)S(1)} %copy-done.8, bf16[128,1024]{1,0:T(8,128)(2,1)S(1)} %copy-done.9, ...), custom_call_target="tpu_custom_call", output_to_operand_aliasing={{}: (9, {})} | custom-call | tf_op jit(solution)/shard_map/finish/pallas_call | solution.py:338
  104.4 4.8 %collective-permute-done.14.refs_4_ = bf16[128,2048]{1,0:T(8,128)(2,1)S(1)} collective-permute-done((bf16[128,2048]{1,0:T(8,128)(2,1)S(1)}, bf16[128,2048]{1,0:T(8,128)(2,1)S(1)}, u32[]{:S(2)}, u32[]{:S(2)}) %collective-permute-start.14) | collective-permute-done | bytes 524320 | tf_op jit(solution)/shard_map/ppermute | solution.py:369
  109.3 1.0 finish.5
  (69 shorter events, 1.7 us)
Async XLA Ops:
  2.0 28.6 %collective-permute-start.1 = (bf16[512,256]{1,0:T(8,128)(2,1)}, bf16[512,256]{1,0:T(8,128)(2,1)S(1)}, u32[]{:S(2)}, u32[]{:S(2)}) collective-permute-start(bf16[512,256]{1,0:T(8,128)(2,1)} %get-tuple-element.44.refs_2_), channel_id=1, source_target_pairs={{0,4},{4,8},{8,12},{12,16},{16,20},{20,24},{24,28},{1,5},{5,9},{9,... | collective-permute-start | bytes 786440 | tf_op jit(solution)/shard_map/ppermute | solution.py:358
  6.9 23.7 %collective-permute-start = (bf16[512,256]{1,0:T(8,128)(2,1)}, bf16[512,256]{1,0:T(8,128)(2,1)S(1)}, u32[]{:S(2)}, u32[]{:S(2)}) collective-permute-start(bf16[512,256]{1,0:T(8,128)(2,1)} %get-tuple-element.44.refs_2_), channel_id=1, source_target_pairs={{0,8},{4,12},{8,16},{12,20},{16,24},{20,28},{1,9},{5,13},{9,17},{1... | collective-permute-start | bytes 786440 | tf_op jit(solution)/shard_map/ppermute | solution.py:358
  10.4 8.5 %collective-permute-start.6 = (bf16[128,256]{1,0:T(8,128)(2,1)}, bf16[128,256]{1,0:T(8,128)(2,1)S(1)}, u32[]{:S(2)}, u32[]{:S(2)}) collective-permute-start(bf16[128,256]{1,0:T(8,128)(2,1)} %get-tuple-element.45), channel_id=1, source_target_pairs={{0,28},{1,29},{2,30},{3,31}} | collective-permute-start | bytes 196616 | tf_op jit(solution)/shard_map/ppermute | solution.py:358
  12.5 7.7 %collective-permute-start.5 = (bf16[128,256]{1,0:T(8,128)(2,1)}, bf16[128,256]{1,0:T(8,128)(2,1)S(1)}, u32[]{:S(2)}, u32[]{:S(2)}) collective-permute-start(bf16[128,256]{1,0:T(8,128)(2,1)} %get-tuple-element.45), channel_id=1, source_target_pairs={{0,24},{4,28},{1,25},{5,29},{2,26},{6,30},{3,27},{7,31}} | collective-permute-start | bytes 196616 | tf_op jit(solution)/shard_map/ppermute | solution.py:358
  14.4 15.6 %collective-permute-start.4 = (bf16[128,256]{1,0:T(8,128)(2,1)}, bf16[128,256]{1,0:T(8,128)(2,1)S(1)}, u32[]{:S(2)}, u32[]{:S(2)}) collective-permute-start(bf16[128,256]{1,0:T(8,128)(2,1)} %get-tuple-element.45), channel_id=1, source_target_pairs={{0,20},{4,24},{8,28},{1,21},{5,25},{9,29},{2,22},{6,26},{10,30},{3... | collective-permute-start | bytes 196616 | tf_op jit(solution)/shard_map/ppermute | solution.py:358
  18.9 11.8 %copy-start.14 = (bf16[128,256]{1,0:T(8,128)(2,1)}, bf16[128,256]{1,0:T(8,128)(2,1)S(1)}, u32[]{:S(2)}) copy-start(bf16[128,256]{1,0:T(8,128)(2,1)S(1)} %collective-permute-done.6.refs_7_) | copy-start | bytes 196612
  18.9 11.1 %collective-permute-start.3 = (bf16[128,256]{1,0:T(8,128)(2,1)}, bf16[128,256]{1,0:T(8,128)(2,1)S(1)}, u32[]{:S(2)}, u32[]{:S(2)}) collective-permute-start(bf16[128,256]{1,0:T(8,128)(2,1)} %get-tuple-element.45), channel_id=1, source_target_pairs={{0,16},{4,20},{8,24},{12,28},{1,17},{5,21},{9,25},{13,29},{2,18},{... | collective-permute-start | bytes 196616 | tf_op jit(solution)/shard_map/ppermute | solution.py:358
  20.2 10.4 %copy-start.15 = (bf16[128,256]{1,0:T(8,128)(2,1)}, bf16[128,256]{1,0:T(8,128)(2,1)S(1)}, u32[]{:S(2)}) copy-start(bf16[128,256]{1,0:T(8,128)(2,1)S(1)} %collective-permute-done.5.refs_6_) | copy-start | bytes 196612
  20.2 10.4 %collective-permute-start.2 = (bf16[128,256]{1,0:T(8,128)(2,1)}, bf16[128,256]{1,0:T(8,128)(2,1)S(1)}, u32[]{:S(2)}, u32[]{:S(2)}) collective-permute-start(bf16[128,256]{1,0:T(8,128)(2,1)} %get-tuple-element.45), channel_id=1, source_target_pairs={{0,12},{4,16},{8,20},{12,24},{16,28},{1,13},{5,17},{9,21},{13,25},... | collective-permute-start | bytes 196616 | tf_op jit(solution)/shard_map/ppermute | solution.py:358
  30.6 0.7 copy-start.12
  30.6 0.8 copy-start.13
  44.8 1.8 %collective-permute-start.7 = (bf16[128,1024]{1,0:T(8,128)(2,1)}, bf16[128,1024]{1,0:T(8,128)(2,1)S(1)}, u32[]{:S(2)}, u32[]{:S(2)}) collective-permute-start(bf16[128,1024]{1,0:T(8,128)(2,1)} %get-tuple-element.49), channel_id=1, source_target_pairs={{0,1},{1,0},{2,3},{3,2},{4,5},{5,4},{6,7},{7,6},{8,9},{9,8},{10,11... | collective-permute-start | bytes 786440 | tf_op jit(solution)/shard_map/ppermute | solution.py:366
  44.8 2.1 %collective-permute-start.8 = (bf16[128,1024]{1,0:T(8,128)(2,1)}, bf16[128,1024]{1,0:T(8,128)(2,1)S(1)}, u32[]{:S(2)}, u32[]{:S(2)}) collective-permute-start(bf16[128,1024]{1,0:T(8,128)(2,1)} %get-tuple-element.50), channel_id=1, source_target_pairs={{0,1},{1,0},{2,3},{3,2},{4,5},{5,4},{6,7},{7,6},{8,9},{9,8},{10,11... | collective-permute-start | bytes 786440 | tf_op jit(solution)/shard_map/ppermute | solution.py:366
  46.6 0.7 copy-start.25
  47.0 0.7 copy-start.26
  49.8 9.1 %copy-start.11 = (bf16[128,2048]{1,0:T(8,128)(2,1)S(1)}, bf16[128,2048]{1,0:T(8,128)(2,1)}, u32[]{:S(2)}) copy-start(bf16[128,2048]{1,0:T(8,128)(2,1)} %add.3.refs_0_) | copy-start | bytes 1572868
  57.8 2.6 %collective-permute-start.19 = (bf16[128,1024]{1,0:T(8,128)(2,1)}, bf16[128,1024]{1,0:T(8,128)(2,1)S(1)}, u32[]{:S(2)}, u32[]{:S(2)}) collective-permute-start(bf16[128,1024]{1,0:T(8,128)(2,1)} %get-tuple-element.71), channel_id=1, source_target_pairs={{0,1},{1,0},{2,3},{3,2},{4,5},{5,4},{6,7},{7,6},{8,9},{9,8},{10,11... | collective-permute-start | bytes 786440 | tf_op jit(solution)/shard_map/ppermute | solution.py:366
  58.0 2.4 %collective-permute-start.20 = (bf16[128,1024]{1,0:T(8,128)(2,1)}, bf16[128,1024]{1,0:T(8,128)(2,1)S(1)}, u32[]{:S(2)}, u32[]{:S(2)}) collective-permute-start(bf16[128,1024]{1,0:T(8,128)(2,1)} %get-tuple-element.72), channel_id=1, source_target_pairs={{0,1},{1,0},{2,3},{3,2},{4,5},{5,4},{6,7},{7,6},{8,9},{9,8},{10,11... | collective-permute-start | bytes 786440 | tf_op jit(solution)/shard_map/ppermute | solution.py:366
  58.4 2.5 %collective-permute-start.21 = (bf16[128,1024]{1,0:T(8,128)(2,1)}, bf16[128,1024]{1,0:T(8,128)(2,1)S(1)}, u32[]{:S(2)}, u32[]{:S(2)}) collective-permute-start(bf16[128,1024]{1,0:T(8,128)(2,1)} %get-tuple-element.73), channel_id=1, source_target_pairs={{0,1},{1,0},{2,3},{3,2},{4,5},{5,4},{6,7},{7,6},{8,9},{9,8},{10,11... | collective-permute-start | bytes 786440 | tf_op jit(solution)/shard_map/ppermute | solution.py:366
  58.5 2.4 %collective-permute-start.22 = (bf16[128,1024]{1,0:T(8,128)(2,1)}, bf16[128,1024]{1,0:T(8,128)(2,1)S(1)}, u32[]{:S(2)}, u32[]{:S(2)}) collective-permute-start(bf16[128,1024]{1,0:T(8,128)(2,1)} %get-tuple-element.74), channel_id=1, source_target_pairs={{0,1},{1,0},{2,3},{3,2},{4,5},{5,4},{6,7},{7,6},{8,9},{9,8},{10,11... | collective-permute-start | bytes 786440 | tf_op jit(solution)/shard_map/ppermute | solution.py:366
  58.9 14.8 %collective-permute-start.11 = (bf16[128,2048]{1,0:T(8,128)(2,1)S(1)}, bf16[128,2048]{1,0:T(8,128)(2,1)S(1)}, u32[]{:S(2)}, u32[]{:S(2)}) collective-permute-start(bf16[128,2048]{1,0:T(8,128)(2,1)S(1)} %copy-done.11), channel_id=1, source_target_pairs={{0,2},{1,3},{2,0},{3,1},{4,6},{5,7},{6,4},{7,5},{8,10},{9,11},{10,... | collective-permute-start | bytes 1572872 | tf_op jit(solution)/shard_map/ppermute | solution.py:369
  60.4 0.7 copy-start.19
  60.4 5.3 %collective-permute-start.9 = (bf16[128,1024]{1,0:T(8,128)(2,1)}, bf16[128,1024]{1,0:T(8,128)(2,1)S(1)}, u32[]{:S(2)}, u32[]{:S(2)}) collective-permute-start(bf16[128,1024]{1,0:T(8,128)(2,1)} %get-tuple-element.53), channel_id=1, source_target_pairs={{0,1},{1,0},{2,3},{3,2},{4,5},{5,4},{6,7},{7,6},{8,9},{9,8},{10,11... | collective-permute-start | bytes 786440 | tf_op jit(solution)/shard_map/ppermute | solution.py:366
  60.4 0.8 copy-start.20
  60.4 5.3 %collective-permute-start.10 = (bf16[128,1024]{1,0:T(8,128)(2,1)}, bf16[128,1024]{1,0:T(8,128)(2,1)S(1)}, u32[]{:S(2)}, u32[]{:S(2)}) collective-permute-start(bf16[128,1024]{1,0:T(8,128)(2,1)} %get-tuple-element.54), channel_id=1, source_target_pairs={{0,1},{1,0},{2,3},{3,2},{4,5},{5,4},{6,7},{7,6},{8,9},{9,8},{10,11... | collective-permute-start | bytes 786440 | tf_op jit(solution)/shard_map/ppermute | solution.py:366
  60.9 0.8 copy-start.22
  64.5 38.3 %collective-permute-start.23 = (bf16[128,4096]{1,0:T(8,128)(2,1)}, bf16[128,4096]{1,0:T(8,128)(2,1)S(1)}, u32[]{:S(2)}, u32[]{:S(2)}) collective-permute-start(bf16[128,4096]{1,0:T(8,128)(2,1)} %add.5), channel_id=1, source_target_pairs={{0,2},{1,3},{2,0},{3,1},{4,6},{5,7},{6,4},{7,5},{8,10},{9,11},{10,... | collective-permute-start | bytes 3145736 | tf_op jit(solution)/shard_map/ppermute | solution.py:369
  65.7 0.8 copy-start.24
  68.6 26.4 %copy-start.10 = (bf16[128,2048]{1,0:T(8,128)(2,1)S(1)}, bf16[128,2048]{1,0:T(8,128)(2,1)}, u32[]{:S(2)}) copy-start(bf16[128,2048]{1,0:T(8,128)(2,1)} %add.4.refs_9_) | copy-start | bytes 1572868
  73.6 0.8 copy-start
  94.3 2.1 %collective-permute-start.15 = (bf16[128,1024]{1,0:T(8,128)(2,1)}, bf16[128,1024]{1,0:T(8,128)(2,1)S(1)}, u32[]{:S(2)}, u32[]{:S(2)}) collective-permute-start(bf16[128,1024]{1,0:T(8,128)(2,1)} %get-tuple-element.63), channel_id=1, source_target_pairs={{0,1},{1,0},{2,3},{3,2},{4,5},{5,4},{6,7},{7,6},{8,9},{9,8},{10,11... | collective-permute-start | bytes 786440 | tf_op jit(solution)/shard_map/ppermute | solution.py:366
  94.4 2.2 %collective-permute-start.16 = (bf16[128,1024]{1,0:T(8,128)(2,1)}, bf16[128,1024]{1,0:T(8,128)(2,1)S(1)}, u32[]{:S(2)}, u32[]{:S(2)}) collective-permute-start(bf16[128,1024]{1,0:T(8,128)(2,1)} %get-tuple-element.64), channel_id=1, source_target_pairs={{0,1},{1,0},{2,3},{3,2},{4,5},{5,4},{6,7},{7,6},{8,9},{9,8},{10,11... | collective-permute-start | bytes 786440 | tf_op jit(solution)/shard_map/ppermute | solution.py:366
  94.9 2.1 %collective-permute-start.17 = (bf16[128,1024]{1,0:T(8,128)(2,1)}, bf16[128,1024]{1,0:T(8,128)(2,1)S(1)}, u32[]{:S(2)}, u32[]{:S(2)}) collective-permute-start(bf16[128,1024]{1,0:T(8,128)(2,1)} %get-tuple-element.65), channel_id=1, source_target_pairs={{0,1},{1,0},{2,3},{3,2},{4,5},{5,4},{6,7},{7,6},{8,9},{9,8},{10,11... | collective-permute-start | bytes 786440 | tf_op jit(solution)/shard_map/ppermute | solution.py:366
  95.0 14.3 %collective-permute-start.14 = (bf16[128,2048]{1,0:T(8,128)(2,1)S(1)}, bf16[128,2048]{1,0:T(8,128)(2,1)S(1)}, u32[]{:S(2)}, u32[]{:S(2)}) collective-permute-start(bf16[128,2048]{1,0:T(8,128)(2,1)S(1)} %copy-done.10), channel_id=1, source_target_pairs={{0,2},{1,3},{2,0},{3,1},{4,6},{5,7},{6,4},{7,5},{8,10},{9,11},{10,... | collective-permute-start | bytes 1572872 | tf_op jit(solution)/shard_map/ppermute | solution.py:369
  96.5 1.7 %collective-permute-start.24 = (bf16[128,1024]{1,0:T(8,128)(2,1)}, bf16[128,1024]{1,0:T(8,128)(2,1)S(1)}, u32[]{:S(2)}, u32[]{:S(2)}) collective-permute-start(bf16[128,1024]{1,0:T(8,128)(2,1)} %get-tuple-element.77), channel_id=1, source_target_pairs={{0,1},{1,0},{2,3},{3,2},{4,5},{5,4},{6,7},{7,6},{8,9},{9,8},{10,11... | collective-permute-start | bytes 786440 | tf_op jit(solution)/shard_map/ppermute | solution.py:366
  96.7 2.0 %collective-permute-start.25 = (bf16[128,1024]{1,0:T(8,128)(2,1)}, bf16[128,1024]{1,0:T(8,128)(2,1)S(1)}, u32[]{:S(2)}, u32[]{:S(2)}) collective-permute-start(bf16[128,1024]{1,0:T(8,128)(2,1)} %get-tuple-element.78), channel_id=1, source_target_pairs={{0,1},{1,0},{2,3},{3,2},{4,5},{5,4},{6,7},{7,6},{8,9},{9,8},{10,11... | collective-permute-start | bytes 786440 | tf_op jit(solution)/shard_map/ppermute | solution.py:366
  97.0 5.7 %collective-permute-start.18 = (bf16[128,1024]{1,0:T(8,128)(2,1)}, bf16[128,1024]{1,0:T(8,128)(2,1)S(1)}, u32[]{:S(2)}, u32[]{:S(2)}) collective-permute-start(bf16[128,1024]{1,0:T(8,128)(2,1)} %get-tuple-element.66), channel_id=1, source_target_pairs={{0,1},{1,0},{2,3},{3,2},{4,5},{5,4},{6,7},{7,6},{8,9},{9,8},{10,11... | collective-permute-start | bytes 786440 | tf_op jit(solution)/shard_map/ppermute | solution.py:366
  98.2 11.0 %collective-permute-start.12 = (bf16[128,1024]{1,0:T(8,128)(2,1)}, bf16[128,1024]{1,0:T(8,128)(2,1)S(1)}, u32[]{:S(2)}, u32[]{:S(2)}) collective-permute-start(bf16[128,1024]{1,0:T(8,128)(2,1)} %get-tuple-element.57), channel_id=1, source_target_pairs={{0,1},{1,0},{2,3},{3,2},{4,5},{5,4},{6,7},{7,6},{8,9},{9,8},{10,11... | collective-permute-start | bytes 786440 | tf_op jit(solution)/shard_map/ppermute | solution.py:366
  98.6 10.7 %collective-permute-start.13 = (bf16[128,1024]{1,0:T(8,128)(2,1)}, bf16[128,1024]{1,0:T(8,128)(2,1)S(1)}, u32[]{:S(2)}, u32[]{:S(2)}) collective-permute-start(bf16[128,1024]{1,0:T(8,128)(2,1)} %get-tuple-element.58), channel_id=1, source_target_pairs={{0,1},{1,0},{2,3},{3,2},{4,5},{5,4},{6,7},{7,6},{8,9},{9,8},{10,11... | collective-permute-start | bytes 786440 | tf_op jit(solution)/shard_map/ppermute | solution.py:366
  98.8 1.0 copy-start.1
  99.8 0.9 copy-start.2
  100.8 0.9 copy-start.3
  101.7 1.0 copy-start.6
  101.7 1.0 copy-start.7
  101.7 1.2 %copy-start.8 = (bf16[128,1024]{1,0:T(8,128)(2,1)S(1)}, bf16[128,1024]{1,0:T(8,128)(2,1)}, u32[]{:S(2)}) copy-start(bf16[128,1024]{1,0:T(8,128)(2,1)} %get-tuple-element.61.refs_2_) | copy-start | bytes 786436
  101.7 1.4 %copy-start.9 = (bf16[128,1024]{1,0:T(8,128)(2,1)S(1)}, bf16[128,1024]{1,0:T(8,128)(2,1)}, u32[]{:S(2)}) copy-start(bf16[128,1024]{1,0:T(8,128)(2,1)} %get-tuple-element.62.refs_3_) | copy-start | bytes 786436
  103.1 6.2 %copy-start.4 = (bf16[128,1024]{1,0:T(8,128)(2,1)S(1)}, bf16[128,1024]{1,0:T(8,128)(2,1)}, u32[]{:S(2)}) copy-start(bf16[128,1024]{1,0:T(8,128)(2,1)} %get-tuple-element.55.refs_0_) | copy-start | bytes 786436
  103.1 6.2 %copy-start.5 = (bf16[128,1024]{1,0:T(8,128)(2,1)S(1)}, bf16[128,1024]{1,0:T(8,128)(2,1)}, u32[]{:S(2)}) copy-start(bf16[128,1024]{1,0:T(8,128)(2,1)} %get-tuple-element.56.refs_1_) | copy-start | bytes 786436
  (5 other events, 3.4 us)

commit v5 on v4

--- a/solution.py
+++ b/solution.py
@@ -11,11 +11,13 @@
 BLK = 64
 SPAN = 16
 VMOST = 2
+NEAR = 3
 LANES = 128
 MASKED = -1e30
 EXP_SCALE = 1.4426950408889634 / (HS**0.5)
 TILE = 1024
-ACROSS = ((0, 2), (4, 4), (2, 2))
+PIECE = 2
+ACROSS = 4
 MIB = 1024 * 1024
 
 
@@ -71,7 +73,7 @@
     )(rank, vertical, keys, values)
 
 
-def mask_kernel(local_blocks, near, rank_ref, vert_ref, slash_ref, win_ref, pool_ref):
+def mask_kernel(local_blocks, slots, rank_ref, vert_ref, slash_ref, win_ref, pool_ref):
     heads, vert_count = vert_ref.shape
     slash_count = slash_ref.shape[1]
     rank = rank_ref[0]
@@ -86,7 +88,9 @@
         return found
 
     offset_ok = member([slash_ref[:, s : s + 1] for s in range(slash_count)], SPAN - 1 - lane)
-    shard = rank - (near - 1) - lane // VMOST
+    shard = jnp.full((heads, LANES), -1, jnp.int32)
+    for slot, (back, back_odd) in enumerate(slots):
+        shard = jnp.where(lane // VMOST == slot, rank - back - back_odd * (rank & 1), shard)
     first = jnp.full((1, LANES), local_blocks, jnp.int32)
     second = first
     for j in reversed(range(local_blocks)):
@@ -105,11 +109,11 @@
         pool_ref[i] = jnp.where(pool_ok & (block < row - (SPAN - 1)), zero, MASKED)
 
 
-def masks(rank, vertical, slash, local_blocks, near):
+def masks(rank, vertical, slash, local_blocks, slots):
     heads = vertical.shape[0]
     shape = jax.ShapeDtypeStruct((local_blocks, heads, LANES), jnp.float32)
     return pl.pallas_call(
-        functools.partial(mask_kernel, local_blocks, near),
+        functools.partial(mask_kernel, local_blocks, slots),
         out_shape=(shape, shape),
         in_specs=[smem(), vmem(), vmem()],
         out_specs=(vmem(), vmem()),
@@ -119,38 +123,54 @@
 
 
 def attend_kernel(
-    near, pools, with_rows, here_of, tp_ref, ctx_ref, q_ref, win_ref, pool_ref, vert_ref, *refs
+    pools, tiles, here_of, tp_ref, ctx_ref, q_ref, win_ref, pool_ref, vert_ref, *refs
 ):
-    kv_refs = refs[:near]
-    pair_refs = refs[near : near + pools - 1]
-    w_hbm = refs[near + pools - 1]
-    k_win, v_win, e_win, k_pool, v_pool, e_pool, attended, weight, arrival = refs[-9:]
+    own_kv, kv_2, kv_even, kv_back = refs[:4]
+    pair_refs = refs[4 : 4 + pools - 2]
+    w_hbm = refs[4 + pools - 2]
+    k_win, v_win, e_win, k_pool, v_pool, e_pool, attended = refs[-9:-2]
+    weight, arrival = refs[-2:]
+    outs = refs[-12:-9] if tiles else refs[-10:-9]
     step = pl.program_id(0)
     heads = win_ref.shape[1]
-    rows = kv_refs[0].shape[0]
-    tiles, _, tile = weight.shape
-    outs = refs[-9 - 2 * tiles - with_rows : -9]
+    rows = own_kv.shape[0]
 
     def fetch(t):
         return pltpu.make_async_copy(
-            w_hbm.at[:, pl.ds(t * tile, tile)], weight.at[t], arrival.at[t]
+            w_hbm.at[:, pl.ds(t * TILE, TILE)], weight.at[t], arrival.at[t]
         )
 
     @pl.when(step == 0)
     def _():
         for t in range(tiles):
             fetch(t).start()
-        for s in range(near):
-            k_win[s * rows : (s + 1) * rows, :] = kv_refs[s][:, :HS]
-            v_win[s * rows : (s + 1) * rows, :] = kv_refs[s][:, HS:]
-        blocks = picked_blocks(vert_ref[...], ctx_ref[0] - (near - 1), rows // BLK)
-        for slot, block in enumerate(blocks):
-            k_pool[slot * BLK : (slot + 1) * BLK, :] = kv_refs[0][block, :HS]
-            v_pool[slot * BLK : (slot + 1) * BLK, :] = kv_refs[0][block, HS:]
-        for s in range(1, pools):
+        odd = (ctx_ref[0] & 1) == 1
+
+        def place(s, ref):
+            k_win[s * rows : (s + 1) * rows, :] = ref[:, :HS]
+            v_win[s * rows : (s + 1) * rows, :] = ref[:, HS:]
+
+        place(0, kv_2)
+        place(2, own_kv)
+
+        @pl.when(odd)
+        def _():
+            place(1, kv_even)
+
+        @pl.when(jnp.logical_not(odd))
+        def _():
+            place(1, kv_back)
+
+        for s, (ref, back) in enumerate(((kv_2, 2), (kv_back, jnp.where(odd, 3, 1)))):
+            blocks = picked_blocks(vert_ref[...], ctx_ref[0] - back, rows // BLK)
+            for slot, block in enumerate(blocks):
+                at = pl.ds((s * VMOST + slot) * BLK, BLK)
+                k_pool[at, :] = ref[block, :HS]
+                v_pool[at, :] = ref[block, HS:]
+        for s in range(2, pools):
             at = slice(s * VMOST * BLK, (s + 1) * VMOST * BLK)
-            k_pool[at, :] = pair_refs[s - 1][:, :HS]
-            v_pool[at, :] = pair_refs[s - 1][:, HS:]
+            k_pool[at, :] = pair_refs[s - 2][:, :HS]
+            v_pool[at, :] = pair_refs[s - 2][:, HS:]
         key = lax.broadcasted_iota(jnp.int32, e_win.shape, 0)
         lane = lax.broadcasted_iota(jnp.int32, e_win.shape, 1)
         last = (key // BLK == SPAN - 1) & (key % BLK == lane - BLK)
@@ -203,23 +223,22 @@
 
     @pl.when(step == pl.num_programs(0) - 1)
     def _():
-        half = outs[0].shape[0]
-        if with_rows:
-            outs[-1][...] = attended[...]
+        outs[-1][...] = attended[...]
+        half = attended.shape[0] // 2
         for t in range(tiles):
             fetch(t).wait()
             product = jnp.dot(attended[...], weight[t], preferred_element_type=jnp.float32)
             product = product.astype(q.dtype)
-            outs[t][...] = product[:half]
-            outs[tiles + t][...] = product[half:]
-
-
-def attend(flips, tp, ctx, queries, win, pool, vertical, near_kv, pairs, out_weight, tiles, with_rows, after):
+            outs[0][:, t * TILE : (t + 1) * TILE] = product[:half]
+            outs[1][:, t * TILE : (t + 1) * TILE] = product[half:]
+
+
+def attend(flips, tp, ctx, queries, win, pool, vertical, near_kv, pairs, out_weight, tiles, after):
     width = queries.shape[1]
     local_blocks, heads, _ = win.shape
     quarter = local_blocks // 4
     steps = len(flips) * quarter
-    near, pools = len(near_kv), len(pairs) + 1
+    pools = len(pairs) + 2
     rows = near_kv[0].shape[0]
     dtype = queries.dtype
     far = pools * VMOST * BLK
@@ -232,11 +251,10 @@
         return pl.BlockSpec(shape, lambda g, tp, ctx: (0,) * len(shape))
 
     table = pl.BlockSpec((1, heads, LANES), lambda g, tp, ctx: (here_of(g, tp), 0, 0))
-    out_shapes = [(steps * BLK // 2, TILE)] * (2 * tiles)
-    if with_rows:
-        out_shapes.append((steps * BLK, width))
+    out_shapes = [(steps * BLK // 2, tiles * TILE)] * 2 if tiles else []
+    out_shapes.append((steps * BLK, width))
     return pl.pallas_call(
-        functools.partial(attend_kernel, near, pools, with_rows, here_of),
+        functools.partial(attend_kernel, pools, tiles, here_of),
         out_shape=[jax.ShapeDtypeStruct(shape, dtype) for shape in out_shapes],
         grid_spec=pltpu.PrefetchScalarGridSpec(
             num_scalar_prefetch=2,
@@ -247,15 +265,15 @@
             + [anywhere() for _ in range(1 + len(after))],
             out_specs=[whole(shape) for shape in out_shapes],
             scratch_shapes=[
-                pltpu.VMEM((near * rows, HS), dtype),
-                pltpu.VMEM((near * rows, HS), dtype),
+                pltpu.VMEM((NEAR * rows, HS), dtype),
+                pltpu.VMEM((NEAR * rows, HS), dtype),
                 pltpu.VMEM((SPAN * BLK, LANES), dtype),
                 pltpu.VMEM((far, HS), dtype),
                 pltpu.VMEM((far, HS), dtype),
                 pltpu.VMEM((far, LANES), dtype),
                 pltpu.VMEM((steps * BLK, width), dtype),
-                pltpu.VMEM((tiles, out_weight.shape[0], TILE), dtype),
-                pltpu.SemaphoreType.DMA((tiles,)),
+                pltpu.VMEM((max(tiles, 1), out_weight.shape[0], TILE), dtype),
+                pltpu.SemaphoreType.DMA((max(tiles, 1),)),
             ],
         ),
         compiler_params=params(60),
@@ -266,13 +284,14 @@
 
 def project_kernel(first, a_ref, w_hbm, *refs):
     weight, arrival = refs[-2:]
-    tiles, _, tile = weight.shape
-    outs = refs[-2 - 2 * tiles : -2]
+    tiles = weight.shape[0]
+    pieces = tiles // PIECE
+    outs = refs[-2 - 2 * pieces : -2]
     half = outs[0].shape[0]
 
     def fetch(t):
         return pltpu.make_async_copy(
-            w_hbm.at[:, pl.ds((first + t) * tile, tile)], weight.at[t], arrival.at[t]
+            w_hbm.at[:, pl.ds((first + t) * TILE, TILE)], weight.at[t], arrival.at[t]
         )
 
     for t in range(tiles):
@@ -281,18 +300,20 @@
         fetch(t).wait()
         product = jnp.dot(a_ref[...], weight[t], preferred_element_type=jnp.float32)
         product = product.astype(a_ref.dtype)
-        outs[t][...] = product[:half]
-        outs[tiles + t][...] = product[half:]
+        at = slice(t % PIECE * TILE, (t % PIECE + 1) * TILE)
+        outs[t // PIECE][:, at] = product[:half]
+        outs[pieces + t // PIECE][:, at] = product[half:]
 
 
 def project(attended, out_weight, first, tiles, after):
     rows, depth = attended.shape
-    half = jax.ShapeDtypeStruct((rows // 2, TILE), attended.dtype)
-    return pl.pallas_call(
+    pieces = tiles // PIECE
+    part = jax.ShapeDtypeStruct((rows // 2, PIECE * TILE), attended.dtype)
+    outs = pl.pallas_call(
         functools.partial(project_kernel, first),
-        out_shape=[half] * (2 * tiles),
+        out_shape=[part] * (2 * pieces),
         in_specs=[vmem(), anywhere()] + [anywhere() for _ in after],
-        out_specs=[vmem()] * (2 * tiles),
+        out_specs=[vmem()] * (2 * pieces),
         scratch_shapes=[
             pltpu.VMEM((tiles, depth, TILE), attended.dtype),
             pltpu.SemaphoreType.DMA((tiles,)),
@@ -301,6 +322,7 @@
         cost_estimate=SHORT,
         name="project",
     )(attended, out_weight, *after)
+    return outs[:pieces], outs[pieces:]
 
 
 def add_kernel(*refs):
@@ -308,14 +330,14 @@
     tiles = len(refs) // 2
     for t in range(tiles):
         total = refs[t][...].astype(jnp.float32) + refs[tiles + t][...].astype(jnp.float32)
-        out_ref[:, t * TILE : (t + 1) * TILE] = total.astype(out_ref.dtype)
+        out_ref[:, t * PIECE * TILE : (t + 1) * PIECE * TILE] = total.astype(out_ref.dtype)
 
 
 def add(keep, got):
     rows = keep[0].shape[0]
     return pl.pallas_call(
         add_kernel,
-        out_shape=jax.ShapeDtypeStruct((rows, len(keep) * TILE), keep[0].dtype),
+        out_shape=jax.ShapeDtypeStruct((rows, len(keep) * PIECE * TILE), keep[0].dtype),
         in_specs=[vmem()] * (2 * len(keep)),
         out_specs=vmem(),
         compiler_params=params(60),
@@ -327,7 +349,7 @@
 def finish_kernel(tiles, *refs):
     arrived_ref, out_ref = refs[2 * tiles], refs[-1]
     for t in range(tiles):
-        at = slice(t * TILE, (t + 1) * TILE)
+        at = slice(t * PIECE * TILE, (t + 1) * PIECE * TILE)
         total = refs[t][...].astype(jnp.float32) + refs[tiles + t][...].astype(jnp.float32)
         out_ref[:, at] = (total + arrived_ref[:, at].astype(jnp.float32)).astype(out_ref.dtype)
 
@@ -350,17 +372,25 @@
 
 def shards(ctx_size, queries, keys, values, out_weight, vertical, slash):
     local_blocks = queries.shape[0] // BLK
-    near = 1 + -(-(SPAN - 1) // local_blocks)
+    assert ctx_size % 2 == 0 and (NEAR - 1) * local_blocks >= SPAN - 1
     ctx = jnp.reshape(lax.axis_index("ctx"), (1,)).astype(jnp.int32)
     tp = jnp.reshape(lax.axis_index("tp"), (1,)).astype(jnp.int32)
 
     def shifted(x, by):
         return lax.ppermute(x, "ctx", [(r, r + by) for r in range(ctx_size - by)])
 
+    def swapped(x):
+        return lax.ppermute(x, "ctx", [(r, r ^ 1) for r in range(ctx_size)])
+
     own, pair = pick(ctx, vertical, keys, values)
-    near_kv = [shifted(own, s) for s in range(near - 1, 0, -1)] + [own]
-    pairs = [shifted(pair, s) for s in range(near, ctx_size)]
-    win, pool = masks(ctx, vertical, slash, local_blocks, near)
+    kv_2 = shifted(own, 2)
+    kv_even = lax.ppermute(own, "ctx", [(r, r + 1) for r in range(0, ctx_size, 2)])
+    steps = range(4, ctx_size, 2)
+    pairs = [shifted(pair, s) for s in steps]
+    near_kv = [own, kv_2, kv_even, swapped(kv_2)]
+    pairs += [swapped(x) for x in pairs]
+    slots = [(2, 0), (1, 2)] + [(s, 0) for s in steps] + [(s - 1, 2) for s in steps]
+    win, pool = masks(ctx, vertical, slash, local_blocks, slots)
 
     def sibling(x):
         return lax.ppermute(x, "tp", [(j, j ^ 1) for j in range(4)])
@@ -368,35 +398,28 @@
     def across(x):
         return lax.ppermute(x, "tp", [(j, j ^ 2) for j in range(4)])
 
-    def attention(flips, tiles, with_rows, after):
+    def attention(flips, tiles, after):
         return attend(
-            flips, tp, ctx, queries, win, pool, vertical, near_kv, pairs, out_weight, tiles, with_rows, after
+            flips, tp, ctx, queries, win, pool, vertical, near_kv, pairs, out_weight, tiles, after
         )
 
     width = out_weight.shape[1]
     tiles = width // TILE
-    head = ACROSS[0][1]
-    assert ACROSS[0][0] == 0 and sum(count for _, count in ACROSS) == tiles
-    *parts, attended = attention((3, 2), head, True, ())
-    keep = parts[head:]
-    got = [sibling(x) for x in parts[:head]]
-    total = add(keep, got)
+    assert tiles == 2 * ACROSS
+    send, keep, attended = attention((3, 2), ACROSS, ())
+    total = keep.astype(jnp.float32) + sibling(send).astype(jnp.float32)
+    total = total.astype(keep.dtype)
     arrived = [across(total)]
-    rest = tiles - head
-    parts = project(attended, out_weight, head, rest, (total,))
-    keep += parts[rest:]
-    got += [sibling(x) for x in parts[:rest]]
-    for first, count in ACROSS[1:]:
-        total = add(keep[first : first + count], got[first : first + count])
-        arrived.append(across(total))
-    parts = attention((1, 0), tiles, False, (total, arrived[0]))
-    keep = parts[tiles:]
-    got = [sibling(x) for x in parts[:tiles]]
+    send, keep = project(attended, out_weight, ACROSS, ACROSS, (total,))
+    total = add(keep, [sibling(x) for x in send])
+    arrived.append(across(total))
+    (attended,) = attention((1, 0), 0, (total,))
+    send, keep = project(attended, out_weight, 0, tiles, (arrived[0],))
+    got = [sibling(x) for x in send]
     out = None
-    for part, (first, count) in zip(arrived, ACROSS):
-        assert first % count == 0
-        at = slice(first, first + count)
-        out = finish(keep[at], got[at], part, first // count, width, out)
+    for place, part in enumerate(arrived):
+        at = slice(place * ACROSS // PIECE, (place + 1) * ACROSS // PIECE)
+        out = finish(keep[at], got[at], part, place, width, out)
     return out
 
 

time: 111 us -> 98.9 us (0.89)
  the two profiles are of different devices: /device:TPU:0 before, /device:TPU:16 now
where the time goes in v5:
time: 98.9 us; the launch traced here: 97.5 us
  Pallas kernels  52.8 us (53%)
  waiting for transfers between devices  21.6 us (22%)
  starting transfers between devices  15.6 us (16%)
  local copies, waits for them, and re-layouts  5.87 us (6%)
  other arithmetic  1.47 us (1%)
    pallas_call x2, Pallas kernels, attend(): pl.pallas_call(functools.partial(attend_kernel, pools, tiles, here_of), o...  27.4 us
    pallas_call x2, Pallas kernels, project(): pl.pallas_call(functools.partial(project_kernel, first), out_shape=[part]...  16.3 us
    ppermute x3, waiting for transfers between devices, shifted(): return lax.ppermute(x, 'ctx', [(r, r + by) for r in range(ctx_size - by)])  10.3 us
    ppermute x7, waiting for transfers between devices, sibling(): return lax.ppermute(x, 'tp', [(j, j ^ 1) for j in range(4)])  7.07 us
    unnamed x32, local copies, waits for them, and re-layouts  5.87 us
    ppermute x3, starting transfers between devices, shifted(): return lax.ppermute(x, 'ctx', [(r, r + by) for r in range(ctx_size - by)])  5.42 us
    ppermute x1, starting transfers between devices, shards(): lax.ppermute(own, 'ctx', [(r, r + 1) for r in range(0, ctx_size, 2)])  3.44 us
    pallas_call x1, Pallas kernels, add(): pl.pallas_call(add_kernel, out_shape=jax.ShapeDtypeStruct((rows, len(keep...  2.73 us
  transfers between devices with their start and end apart: 16, of which 9 were waited for; matrix products, arithmetic and copies ran while one was open for 0% of the time, Pallas kernels for 35%

profile of v5, /device:TPU:16, one launch (start us, length us, event | category | flops | bytes accessed | tf_op | source)
XLA Modules:
  0.0 97.5 jit_solution(17593094958504637814)
XLA Ops:
  0.0 2.0 %pick.1 = (bf16[512,256]{1,0:T(8,128)(2,1)}, bf16[128,256]{1,0:T(8,128)(2,1)}) custom-call(s32[1]{0:T(128)} %bitcast.1.rank_ref.ctx_ref, s32[8,16]{1,0:T(8,128)} %vert_ref.7, bf16[512,128]{1,0:T(8,128)(2,1)} %k_ref.1, bf16[512,128]{1,0:T(8,128)(2,1)} %v_ref.1), custom_call_target="tpu_custom_call" | custom-call | tf_op jit(solution)/shard_map/pick/pallas_call | solution.py:63
  2.0 3.5 %collective-permute-start = (bf16[512,256]{1,0:T(8,128)(2,1)}, bf16[512,256]{1,0:T(8,128)(2,1)S(1)}, u32[]{:S(2)}, u32[]{:S(2)}) collective-permute-start(bf16[512,256]{1,0:T(8,128)(2,1)} %get-tuple-element.26.refs_0_), channel_id=1, source_target_pairs={{0,8},{4,12},{8,16},{12,20},{16,24},{20,28},{1,9},{5,13},{9,17},{1... | collective-permute-start | bytes 786440 | tf_op jit(solution)/shard_map/ppermute | solution.py:380
  5.5 3.4 %collective-permute-start.1 = (bf16[512,256]{1,0:T(8,128)(2,1)}, bf16[512,256]{1,0:T(8,128)(2,1)S(1)}, u32[]{:S(2)}, u32[]{:S(2)}) collective-permute-start(bf16[512,256]{1,0:T(8,128)(2,1)} %get-tuple-element.26.refs_0_), channel_id=1, source_target_pairs={{0,4},{8,12},{16,20},{24,28},{1,5},{9,13},{17,21},{25,29},{2,6},{1... | collective-permute-start | bytes 786440 | tf_op jit(solution)/shard_map/ppermute | solution.py:387
  8.9 3.2 %collective-permute-done.refs_1_ = bf16[512,256]{1,0:T(8,128)(2,1)S(1)} collective-permute-done((bf16[512,256]{1,0:T(8,128)(2,1)}, bf16[512,256]{1,0:T(8,128)(2,1)S(1)}, u32[]{:S(2)}, u32[]{:S(2)}) %collective-permute-start) | collective-permute-done | bytes 262176 | tf_op jit(solution)/shard_map/ppermute | solution.py:380
  12.2 1.5 %collective-permute-start.2 = (bf16[512,256]{1,0:T(8,128)(2,1)S(1)}, bf16[512,256]{1,0:T(8,128)(2,1)S(1)}, u32[]{:S(2)}, u32[]{:S(2)}) collective-permute-start(bf16[512,256]{1,0:T(8,128)(2,1)S(1)} %collective-permute-done.refs_1_), channel_id=1, source_target_pairs={{0,4},{4,0},{8,12},{12,8},{16,20},{20,16},{24,28},{28,24},{1,5},{5... | collective-permute-start | bytes 786440 | tf_op jit(solution)/shard_map/ppermute | solution.py:383
  13.7 0.7 collective-permute-start.4
  14.3 1.3 %collective-permute-start.3 = (bf16[128,256]{1,0:T(8,128)(2,1)}, bf16[128,256]{1,0:T(8,128)(2,1)S(1)}, u32[]{:S(2)}, u32[]{:S(2)}) collective-permute-start(bf16[128,256]{1,0:T(8,128)(2,1)} %get-tuple-element.27), channel_id=1, source_target_pairs={{0,16},{4,20},{8,24},{12,28},{1,17},{5,21},{9,25},{13,29},{2,18},{... | collective-permute-start | bytes 196616 | tf_op jit(solution)/shard_map/ppermute | solution.py:380
  15.6 0.0 collective-permute-done.4.refs_5_
  15.7 0.6 collective-permute-start.6
  16.2 7.1 %collective-permute-done.3.refs_4_ = bf16[128,256]{1,0:T(8,128)(2,1)S(1)} collective-permute-done((bf16[128,256]{1,0:T(8,128)(2,1)}, bf16[128,256]{1,0:T(8,128)(2,1)S(1)}, u32[]{:S(2)}, u32[]{:S(2)}) %collective-permute-start.3) | collective-permute-done | bytes 65568 | tf_op jit(solution)/shard_map/ppermute | solution.py:380
  23.4 0.5 collective-permute-start.5
  23.9 1.6 %masks.1 = (f32[8,8,128]{2,1,0:T(8,128)}, f32[8,8,128]{2,1,0:T(8,128)}) custom-call(s32[1]{0:T(128)} %bitcast.1.rank_ref.ctx_ref, s32[8,16]{1,0:T(8,128)} %vert_ref.7, s32[8,8]{1,0:T(8,128)} %slash_ref.1), custom_call_target="tpu_custom_call" | custom-call | tf_op jit(solution)/shard_map/masks/pallas_call | solution.py:115
  25.4 0.0 collective-permute-done.6.refs_7_
  25.4 2.2 %collective-permute-done.5.refs_6_ = bf16[128,256]{1,0:T(8,128)(2,1)S(1)} collective-permute-done((bf16[128,256]{1,0:T(8,128)(2,1)S(1)}, bf16[128,256]{1,0:T(8,128)(2,1)S(1)}, u32[]{:S(2)}, u32[]{:S(2)}) %collective-permute-start.5) | collective-permute-done | bytes 65568 | tf_op jit(solution)/shard_map/ppermute | solution.py:383
  27.7 0.6 copy-done.15
  28.2 0.1 copy-done.8
  28.3 0.1 copy-done.9
  28.4 15.5 %attend.2 = (bf16[128,4096]{1,0:T(8,128)(2,1)}, bf16[128,4096]{1,0:T(8,128)(2,1)}, bf16[256,1024]{1,0:T(8,128)(2,1)}) custom-call(s32[1]{0:T(128)} %bitcast.tp_ref, s32[1]{0:T(128)} %bitcast.1.rank_ref.ctx_ref, bf16[512,1024]{1,0:T(8,128)(2,1)} %q_ref.3, f32[8,8,128]{2,1,0:T(8,128)} %get-tuple-element.24.win_ref, f32[8,8,128]{2,1,0:T(8,128)} %get-tuple-element.25.pool_ref, ...), custom_call_target="tpu_custom_call" | custom-call | tf_op jit(solution)/shard_map/attend/pallas_call | solution.py:256
  44.0 0.1 collective-permute-start.7
  44.0 2.9 %collective-permute-done.7 = bf16[128,4096]{1,0:T(8,128)(2,1)S(1)} collective-permute-done((bf16[128,4096]{1,0:T(8,128)(2,1)}, bf16[128,4096]{1,0:T(8,128)(2,1)S(1)}, u32[]{:S(2)}, u32[]{:S(2)}) %collective-permute-start.7) | collective-permute-done | bytes 1048608 | tf_op jit(solution)/shard_map/ppermute | solution.py:396
  46.9 1.5 %add_convert_fusion.refs_0_ = bf16[128,4096]{1,0:T(8,128)(2,1)S(1)} fusion(bf16[128,4096]{1,0:T(8,128)(2,1)S(1)} %collective-permute-done.7, bf16[128,4096]{1,0:T(8,128)(2,1)} %get-tuple-element.29), kind=kLoop, calls=%fused_computation | loop fusion | flops 2097152 | bytes 3145728 | tf_op jit(solution)/shard_map/convert_element_type | solution.py:411
  48.4 0.0 copy-start.6
  48.4 1.6 %collective-permute-start.10 = (bf16[128,4096]{1,0:T(8,128)(2,1)S(1)}, bf16[128,4096]{1,0:T(8,128)(2,1)S(1)}, u32[]{:S(2)}, u32[]{:S(2)}) collective-permute-start(bf16[128,4096]{1,0:T(8,128)(2,1)S(1)} %add_convert_fusion.refs_0_), channel_id=1, source_target_pairs={{0,2},{1,3},{2,0},{3,1},{4,6},{5,7},{6,4},{7,5},{8,10},{9,11},{10,... | collective-permute-start | bytes 3145736 | tf_op jit(solution)/shard_map/ppermute | solution.py:399
  50.0 6.7 %project.2 = (bf16[128,2048]{1,0:T(8,128)(2,1)}, bf16[128,2048]{1,0:T(8,128)(2,1)}, bf16[128,2048]{1,0:T(8,128)(2,1)}, bf16[128,2048]{1,0:T(8,128)(2,1)}) custom-call(bf16[256,1024]{1,0:T(8,128)(2,1)} %get-tuple-element.28.a_ref, bf16[1024,8192]{1,0:T(8,128)(2,1)} %w_hbm.3, bf16[128,4096]{1,0:T(8,128)(2,1)} %copy-done.6), custom_call_target="tpu_custom_call" | custom-call | tf_op jit(solution)/shard_map/project/pallas_call | solution.py:312
  56.6 0.1 collective-permute-start.8
  56.7 0.5 collective-permute-start.9
  57.2 1.6 %collective-permute-done.8.refs_2_ = bf16[128,2048]{1,0:T(8,128)(2,1)S(1)} collective-permute-done((bf16[128,2048]{1,0:T(8,128)(2,1)}, bf16[128,2048]{1,0:T(8,128)(2,1)S(1)}, u32[]{:S(2)}, u32[]{:S(2)}) %collective-permute-start.8) | collective-permute-done | bytes 524320 | tf_op jit(solution)/shard_map/ppermute | solution.py:396
  58.8 0.7 collective-permute-done.9.refs_3_
  59.6 0.0 copy-done.10
  59.6 0.8 copy-done.11
  60.4 2.7 %add.6.refs_9_ = bf16[128,4096]{1,0:T(8,128)(2,1)} custom-call(bf16[128,2048]{1,0:T(8,128)(2,1)} %get-tuple-element.31.refs_0_, bf16[128,2048]{1,0:T(8,128)(2,1)} %get-tuple-element.32.refs_1_, bf16[128,2048]{1,0:T(8,128)(2,1)} %copy-done.10, bf16[128,2048]{1,0:T(8,128)(2,1)} %copy-done.11), custom_call_target="tpu_custom_call" | custom-call | tf_op jit(solution)/shard_map/add/pallas_call | solution.py:338
  63.1 0.9 collective-permute-start.13
  64.0 11.9 %attend.3.a_ref = bf16[256,1024]{1,0:T(8,128)(2,1)} custom-call(s32[1]{0:T(128)} %bitcast.tp_ref, s32[1]{0:T(128)} %bitcast.1.rank_ref.ctx_ref, bf16[512,1024]{1,0:T(8,128)(2,1)} %q_ref.3, f32[8,8,128]{2,1,0:T(8,128)} %get-tuple-element.24.win_ref, f32[8,8,128]{2,1,0:T(8,128)} %get-tuple-element.25.pool_ref, s32[8,16]{1,0:T(8,128)} %vert_ref.7, ...), custom_call_target="tpu_custom_call" | custom-call | tf_op jit(solution)/shard_map/attend/pallas_call | solution.py:256
  75.9 0.0 copy-start
  76.0 1.0 copy-done
  76.9 9.7 %project.3 = (bf16[128,2048]{1,0:T(8,128)(2,1)}, bf16[128,2048]{1,0:T(8,128)(2,1)}, bf16[128,2048]{1,0:T(8,128)(2,1)}, bf16[128,2048]{1,0:T(8,128)(2,1)}, bf16[1...) custom-call(bf16[256,1024]{1,0:T(8,128)(2,1)} %attend.3.a_ref, ...), custom_call_target="tpu_custom_call" | custom-call | tf_op jit(solution)/shard_map/project/pallas_call | solution.py:312
  86.6 0.1 collective-permute-start.14
  86.7 0.5 collective-permute-start.15
  87.2 0.1 collective-permute-start.11
  87.2 0.4 collective-permute-start.12
  87.7 1.1 %collective-permute-done.14.refs_2_ = bf16[128,2048]{1,0:T(8,128)(2,1)S(1)} collective-permute-done((bf16[128,2048]{1,0:T(8,128)(2,1)}, bf16[128,2048]{1,0:T(8,128)(2,1)S(1)}, u32[]{:S(2)}, u32[]{:S(2)}) %collective-permute-start.14) | collective-permute-done | bytes 524320 | tf_op jit(solution)/shard_map/ppermute | solution.py:396
  88.8 0.7 collective-permute-done.15.refs_3_
  89.5 1.2 %copy-done.1 = bf16[128,4096]{1,0:T(8,128)(2,1)S(1)} copy-done((bf16[128,4096]{1,0:T(8,128)(2,1)S(1)}, bf16[128,4096]{1,0:T(8,128)(2,1)}, u32[]{:S(2)}) %copy-start.1) | copy-done | bytes 1048600
  90.8 1.0 %copy-done.4 = bf16[128,2048]{1,0:T(8,128)(2,1)S(1)} copy-done((bf16[128,2048]{1,0:T(8,128)(2,1)S(1)}, bf16[128,2048]{1,0:T(8,128)(2,1)}, u32[]{:S(2)}) %copy-start.4) | copy-done | bytes 524312
  91.8 1.0 %copy-done.5 = bf16[128,2048]{1,0:T(8,128)(2,1)S(1)} copy-done((bf16[128,2048]{1,0:T(8,128)(2,1)S(1)}, bf16[128,2048]{1,0:T(8,128)(2,1)}, u32[]{:S(2)}) %copy-start.5) | copy-done | bytes 524312
  92.8 1.3 %finish.2.refs_5_ = bf16[128,8192]{1,0:T(8,128)(2,1)} custom-call(bf16[128,2048]{1,0:T(8,128)(2,1)S(1)} %copy-done.4, bf16[128,2048]{1,0:T(8,128)(2,1)S(1)} %copy-done.5, bf16[128,2048]{1,0:T(8,128)(2,1)S(1)} %collective-permute-done.14.refs_2_, bf16[128,2048]{1,0:T(8,128)(2,1)S(1)} %collective-permute-done.15.refs_3_, bf16[128,4096]{1,0:T(8,128)(2,1)S(1)} %copy-done.1), custom_call_target="tpu_custom_call" | custom-call | tf_op jit(solution)/shard_map/finish/pallas_call | solution.py:360
  94.2 1.9 %collective-permute-done.13.refs_4_ = bf16[128,4096]{1,0:T(8,128)(2,1)S(1)} collective-permute-done((bf16[128,4096]{1,0:T(8,128)(2,1)}, bf16[128,4096]{1,0:T(8,128)(2,1)S(1)}, u32[]{:S(2)}, u32[]{:S(2)}) %collective-permute-start.13) | collective-permute-done | bytes 1048608 | tf_op jit(solution)/shard_map/ppermute | solution.py:399
  96.2 1.3 %finish.3 = bf16[128,8192]{1,0:T(8,128)(2,1)} custom-call(bf16[128,2048]{1,0:T(8,128)(2,1)S(1)} %copy-done.2, bf16[128,2048]{1,0:T(8,128)(2,1)S(1)} %copy-done.3, bf16[128,2048]{1,0:T(8,128)(2,1)S(1)} %collective-permute-done.11.refs_2_, bf16[128,2048]{1,0:T(8,128)(2,1)S(1)} %collective-permute-done.12.refs_3_, ...), custom_call_target="tpu_custom_call", output_to_operand_aliasing={{}: (5, {})} | custom-call | tf_op jit(solution)/shard_map/finish/pallas_call | solution.py:360
  (26 shorter events, 0.1 us)
Async XLA Ops:
  2.0 10.1 %collective-permute-start = (bf16[512,256]{1,0:T(8,128)(2,1)}, bf16[512,256]{1,0:T(8,128)(2,1)S(1)}, u32[]{:S(2)}, u32[]{:S(2)}) collective-permute-start(bf16[512,256]{1,0:T(8,128)(2,1)} %get-tuple-element.26.refs_0_), channel_id=1, source_target_pairs={{0,8},{4,12},{8,16},{12,20},{16,24},{20,28},{1,9},{5,13},{9,17},{1... | collective-permute-start | bytes 786440 | tf_op jit(solution)/shard_map/ppermute | solution.py:380
  5.5 22.1 %collective-permute-start.1 = (bf16[512,256]{1,0:T(8,128)(2,1)}, bf16[512,256]{1,0:T(8,128)(2,1)S(1)}, u32[]{:S(2)}, u32[]{:S(2)}) collective-permute-start(bf16[512,256]{1,0:T(8,128)(2,1)} %get-tuple-element.26.refs_0_), channel_id=1, source_target_pairs={{0,4},{8,12},{16,20},{24,28},{1,5},{9,13},{17,21},{25,29},{2,6},{1... | collective-permute-start | bytes 786440 | tf_op jit(solution)/shard_map/ppermute | solution.py:387
  12.2 15.5 %copy-start.7 = (bf16[512,256]{1,0:T(8,128)(2,1)}, bf16[512,256]{1,0:T(8,128)(2,1)S(1)}, u32[]{:S(2)}) copy-start(bf16[512,256]{1,0:T(8,128)(2,1)S(1)} %collective-permute-done.refs_1_) | copy-start | bytes 786436
  12.2 15.5 %collective-permute-start.2 = (bf16[512,256]{1,0:T(8,128)(2,1)S(1)}, bf16[512,256]{1,0:T(8,128)(2,1)S(1)}, u32[]{:S(2)}, u32[]{:S(2)}) collective-permute-start(bf16[512,256]{1,0:T(8,128)(2,1)S(1)} %collective-permute-done.refs_1_), channel_id=1, source_target_pairs={{0,4},{4,0},{8,12},{12,8},{16,20},{20,16},{24,28},{28,24},{1,5},{5... | collective-permute-start | bytes 786440 | tf_op jit(solution)/shard_map/ppermute | solution.py:383
  13.7 2.0 %collective-permute-start.4 = (bf16[128,256]{1,0:T(8,128)(2,1)}, bf16[128,256]{1,0:T(8,128)(2,1)S(1)}, u32[]{:S(2)}, u32[]{:S(2)}) collective-permute-start(bf16[128,256]{1,0:T(8,128)(2,1)} %get-tuple-element.27), channel_id=1, source_target_pairs={{0,24},{4,28},{1,25},{5,29},{2,26},{6,30},{3,27},{7,31}} | collective-permute-start | bytes 196616 | tf_op jit(solution)/shard_map/ppermute | solution.py:380
  14.3 9.0 %collective-permute-start.3 = (bf16[128,256]{1,0:T(8,128)(2,1)}, bf16[128,256]{1,0:T(8,128)(2,1)S(1)}, u32[]{:S(2)}, u32[]{:S(2)}) collective-permute-start(bf16[128,256]{1,0:T(8,128)(2,1)} %get-tuple-element.27), channel_id=1, source_target_pairs={{0,16},{4,20},{8,24},{12,28},{1,17},{5,21},{9,25},{13,29},{2,18},{... | collective-permute-start | bytes 196616 | tf_op jit(solution)/shard_map/ppermute | solution.py:380
  15.6 12.0 %copy-start.12 = (bf16[128,256]{1,0:T(8,128)(2,1)}, bf16[128,256]{1,0:T(8,128)(2,1)S(1)}, u32[]{:S(2)}) copy-start(bf16[128,256]{1,0:T(8,128)(2,1)S(1)} %collective-permute-done.4.refs_5_) | copy-start | bytes 196612
  15.7 9.8 %collective-permute-start.6 = (bf16[128,256]{1,0:T(8,128)(2,1)S(1)}, bf16[128,256]{1,0:T(8,128)(2,1)S(1)}, u32[]{:S(2)}, u32[]{:S(2)}) collective-permute-start(bf16[128,256]{1,0:T(8,128)(2,1)S(1)} %collective-permute-done.4.refs_5_), channel_id=1, source_target_pairs={{0,4},{4,0},{8,12},{12,8},{16,20},{20,16},{24,28},{28,24},{1,5},{5... | collective-permute-start | bytes 196616 | tf_op jit(solution)/shard_map/ppermute | solution.py:383
  23.3 4.3 %copy-start.13 = (bf16[128,256]{1,0:T(8,128)(2,1)}, bf16[128,256]{1,0:T(8,128)(2,1)S(1)}, u32[]{:S(2)}) copy-start(bf16[128,256]{1,0:T(8,128)(2,1)S(1)} %collective-permute-done.3.refs_4_) | copy-start | bytes 196612
  23.4 4.3 %collective-permute-start.5 = (bf16[128,256]{1,0:T(8,128)(2,1)S(1)}, bf16[128,256]{1,0:T(8,128)(2,1)S(1)}, u32[]{:S(2)}, u32[]{:S(2)}) collective-permute-start(bf16[128,256]{1,0:T(8,128)(2,1)S(1)} %collective-permute-done.3.refs_4_), channel_id=1, source_target_pairs={{0,4},{4,0},{8,12},{12,8},{16,20},{20,16},{24,28},{28,24},{1,5},{5... | collective-permute-start | bytes 196616 | tf_op jit(solution)/shard_map/ppermute | solution.py:383
  25.4 2.3 %copy-start.14 = (bf16[128,256]{1,0:T(8,128)(2,1)}, bf16[128,256]{1,0:T(8,128)(2,1)S(1)}, u32[]{:S(2)}) copy-start(bf16[128,256]{1,0:T(8,128)(2,1)S(1)} %collective-permute-done.6.refs_7_) | copy-start | bytes 196612
  27.6 0.6 copy-start.15
  27.6 0.7 copy-start.8
  27.6 0.8 copy-start.9
  44.0 2.9 %collective-permute-start.7 = (bf16[128,4096]{1,0:T(8,128)(2,1)}, bf16[128,4096]{1,0:T(8,128)(2,1)S(1)}, u32[]{:S(2)}, u32[]{:S(2)}) collective-permute-start(bf16[128,4096]{1,0:T(8,128)(2,1)} %get-tuple-element.30), channel_id=1, source_target_pairs={{0,1},{1,0},{2,3},{3,2},{4,5},{5,4},{6,7},{7,6},{8,9},{9,8},{10,11... | collective-permute-start | bytes 3145736 | tf_op jit(solution)/shard_map/ppermute | solution.py:396
  48.4 1.6 %copy-start.6 = (bf16[128,4096]{1,0:T(8,128)(2,1)}, bf16[128,4096]{1,0:T(8,128)(2,1)S(1)}, u32[]{:S(2)}) copy-start(bf16[128,4096]{1,0:T(8,128)(2,1)S(1)} %add_convert_fusion.refs_0_) | copy-start | bytes 3145732
  48.4 27.5 %collective-permute-start.10 = (bf16[128,4096]{1,0:T(8,128)(2,1)S(1)}, bf16[128,4096]{1,0:T(8,128)(2,1)S(1)}, u32[]{:S(2)}, u32[]{:S(2)}) collective-permute-start(bf16[128,4096]{1,0:T(8,128)(2,1)S(1)} %add_convert_fusion.refs_0_), channel_id=1, source_target_pairs={{0,2},{1,3},{2,0},{3,1},{4,6},{5,7},{6,4},{7,5},{8,10},{9,11},{10,... | collective-permute-start | bytes 3145736 | tf_op jit(solution)/shard_map/ppermute | solution.py:399
  56.6 2.2 %collective-permute-start.8 = (bf16[128,2048]{1,0:T(8,128)(2,1)}, bf16[128,2048]{1,0:T(8,128)(2,1)S(1)}, u32[]{:S(2)}, u32[]{:S(2)}) collective-permute-start(bf16[128,2048]{1,0:T(8,128)(2,1)} %get-tuple-element.33), channel_id=1, source_target_pairs={{0,1},{1,0},{2,3},{3,2},{4,5},{5,4},{6,7},{7,6},{8,9},{9,8},{10,11... | collective-permute-start | bytes 1572872 | tf_op jit(solution)/shard_map/ppermute | solution.py:396
  56.7 2.9 %collective-permute-start.9 = (bf16[128,2048]{1,0:T(8,128)(2,1)}, bf16[128,2048]{1,0:T(8,128)(2,1)S(1)}, u32[]{:S(2)}, u32[]{:S(2)}) collective-permute-start(bf16[128,2048]{1,0:T(8,128)(2,1)} %get-tuple-element.34), channel_id=1, source_target_pairs={{0,1},{1,0},{2,3},{3,2},{4,5},{5,4},{6,7},{7,6},{8,9},{9,8},{10,11... | collective-permute-start | bytes 1572872 | tf_op jit(solution)/shard_map/ppermute | solution.py:396
  58.8 0.8 copy-start.10
  59.6 0.8 copy-start.11
  63.1 33.0 %collective-permute-start.13 = (bf16[128,4096]{1,0:T(8,128)(2,1)}, bf16[128,4096]{1,0:T(8,128)(2,1)S(1)}, u32[]{:S(2)}, u32[]{:S(2)}) collective-permute-start(bf16[128,4096]{1,0:T(8,128)(2,1)} %add.6.refs_9_), channel_id=1, source_target_pairs={{0,2},{1,3},{2,0},{3,1},{4,6},{5,7},{6,4},{7,5},{8,10},{9,11},{10,... | collective-permute-start | bytes 3145736 | tf_op jit(solution)/shard_map/ppermute | solution.py:399
  75.9 1.0 copy-start
  86.6 2.2 %collective-permute-start.14 = (bf16[128,2048]{1,0:T(8,128)(2,1)}, bf16[128,2048]{1,0:T(8,128)(2,1)S(1)}, u32[]{:S(2)}, u32[]{:S(2)}) collective-permute-start(bf16[128,2048]{1,0:T(8,128)(2,1)} %get-tuple-element.41), channel_id=1, source_target_pairs={{0,1},{1,0},{2,3},{3,2},{4,5},{5,4},{6,7},{7,6},{8,9},{9,8},{10,11... | collective-permute-start | bytes 1572872 | tf_op jit(solution)/shard_map/ppermute | solution.py:396
  86.7 2.9 %collective-permute-start.15 = (bf16[128,2048]{1,0:T(8,128)(2,1)}, bf16[128,2048]{1,0:T(8,128)(2,1)S(1)}, u32[]{:S(2)}, u32[]{:S(2)}) collective-permute-start(bf16[128,2048]{1,0:T(8,128)(2,1)} %get-tuple-element.42), channel_id=1, source_target_pairs={{0,1},{1,0},{2,3},{3,2},{4,5},{5,4},{6,7},{7,6},{8,9},{9,8},{10,11... | collective-permute-start | bytes 1572872 | tf_op jit(solution)/shard_map/ppermute | solution.py:396
  87.2 9.0 %collective-permute-start.11 = (bf16[128,2048]{1,0:T(8,128)(2,1)}, bf16[128,2048]{1,0:T(8,128)(2,1)S(1)}, u32[]{:S(2)}, u32[]{:S(2)}) collective-permute-start(bf16[128,2048]{1,0:T(8,128)(2,1)} %get-tuple-element.37), channel_id=1, source_target_pairs={{0,1},{1,0},{2,3},{3,2},{4,5},{5,4},{6,7},{7,6},{8,9},{9,8},{10,11... | collective-permute-start | bytes 1572872 | tf_op jit(solution)/shard_map/ppermute | solution.py:396
  87.2 8.9 %collective-permute-start.12 = (bf16[128,2048]{1,0:T(8,128)(2,1)}, bf16[128,2048]{1,0:T(8,128)(2,1)S(1)}, u32[]{:S(2)}, u32[]{:S(2)}) collective-permute-start(bf16[128,2048]{1,0:T(8,128)(2,1)} %get-tuple-element.38), channel_id=1, source_target_pairs={{0,1},{1,0},{2,3},{3,2},{4,5},{5,4},{6,7},{7,6},{8,9},{9,8},{10,11... | collective-permute-start | bytes 1572872 | tf_op jit(solution)/shard_map/ppermute | solution.py:396
  89.5 1.2 %copy-start.1 = (bf16[128,4096]{1,0:T(8,128)(2,1)S(1)}, bf16[128,4096]{1,0:T(8,128)(2,1)}, u32[]{:S(2)}) copy-start(bf16[128,4096]{1,0:T(8,128)(2,1)} %copy-done) | copy-start | bytes 3145732
  90.8 1.0 %copy-start.4 = (bf16[128,2048]{1,0:T(8,128)(2,1)S(1)}, bf16[128,2048]{1,0:T(8,128)(2,1)}, u32[]{:S(2)}) copy-start(bf16[128,2048]{1,0:T(8,128)(2,1)} %get-tuple-element.39.refs_0_) | copy-start | bytes 1572868
  91.8 1.0 %copy-start.5 = (bf16[128,2048]{1,0:T(8,128)(2,1)S(1)}, bf16[128,2048]{1,0:T(8,128)(2,1)}, u32[]{:S(2)}) copy-start(bf16[128,2048]{1,0:T(8,128)(2,1)} %get-tuple-element.40.refs_1_) | copy-start | bytes 1572868
  92.8 3.3 %copy-start.2 = (bf16[128,2048]{1,0:T(8,128)(2,1)S(1)}, bf16[128,2048]{1,0:T(8,128)(2,1)}, u32[]{:S(2)}) copy-start(bf16[128,2048]{1,0:T(8,128)(2,1)} %get-tuple-element.35.refs_0_) | copy-start | bytes 1572868
  92.8 3.3 %copy-start.3 = (bf16[128,2048]{1,0:T(8,128)(2,1)S(1)}, bf16[128,2048]{1,0:T(8,128)(2,1)}, u32[]{:S(2)}) copy-start(bf16[128,2048]{1,0:T(8,128)(2,1)} %get-tuple-element.36.refs_1_) | copy-start | bytes 1572868

commit v6 on v5

--- a/solution.py
+++ b/solution.py
@@ -89,8 +89,8 @@
 
     offset_ok = member([slash_ref[:, s : s + 1] for s in range(slash_count)], SPAN - 1 - lane)
     shard = jnp.full((heads, LANES), -1, jnp.int32)
-    for slot, (back, back_odd) in enumerate(slots):
-        shard = jnp.where(lane // VMOST == slot, rank - back - back_odd * (rank & 1), shard)
+    for slot, back in enumerate(slots):
+        shard = jnp.where(lane // VMOST == slot, rank - back, shard)
     first = jnp.full((1, LANES), local_blocks, jnp.int32)
     second = first
     for j in reversed(range(local_blocks)):
@@ -122,126 +122,122 @@
     )(rank, vertical, slash)
 
 
-def attend_kernel(
-    pools, tiles, here_of, tp_ref, ctx_ref, q_ref, win_ref, pool_ref, vert_ref, *refs
-):
-    own_kv, kv_2, kv_even, kv_back = refs[:4]
-    pair_refs = refs[4 : 4 + pools - 2]
-    w_hbm = refs[4 + pools - 2]
-    k_win, v_win, e_win, k_pool, v_pool, e_pool, attended = refs[-9:-2]
-    weight, arrival = refs[-2:]
-    outs = refs[-12:-9] if tiles else refs[-10:-9]
+def attend_kernel(names, tiles, here_of, tp_ref, ctx_ref, *refs):
+    ref = dict(zip(names, refs))
+    near, far = "win" in ref, "pool" in ref
+    q_ref = ref["q"]
     step = pl.program_id(0)
-    heads = win_ref.shape[1]
-    rows = own_kv.shape[0]
+    heads = q_ref.shape[1] // HS
+    dtype = q_ref.dtype
 
     def fetch(t):
         return pltpu.make_async_copy(
-            w_hbm.at[:, pl.ds(t * TILE, TILE)], weight.at[t], arrival.at[t]
+            ref["w"].at[:, pl.ds(t * TILE, TILE)], ref["weight"].at[t], ref["arrival"].at[t]
         )
 
     @pl.when(step == 0)
     def _():
         for t in range(tiles):
             fetch(t).start()
-        odd = (ctx_ref[0] & 1) == 1
-
-        def place(s, ref):
-            k_win[s * rows : (s + 1) * rows, :] = ref[:, :HS]
-            v_win[s * rows : (s + 1) * rows, :] = ref[:, HS:]
-
-        place(0, kv_2)
-        place(2, own_kv)
-
-        @pl.when(odd)
-        def _():
-            place(1, kv_even)
-
-        @pl.when(jnp.logical_not(odd))
-        def _():
-            place(1, kv_back)
-
-        for s, (ref, back) in enumerate(((kv_2, 2), (kv_back, jnp.where(odd, 3, 1)))):
-            blocks = picked_blocks(vert_ref[...], ctx_ref[0] - back, rows // BLK)
+        rows = ref["kv_2"].shape[0]
+        if near:
+            for s, name in enumerate(("kv_2", "kv_1", "own")):
+                ref["k_win"][s * rows : (s + 1) * rows, :] = ref[name][:, :HS]
+                ref["v_win"][s * rows : (s + 1) * rows, :] = ref[name][:, HS:]
+            e_win = ref["e_win"]
+            key = lax.broadcasted_iota(jnp.int32, e_win.shape, 0)
+            lane = lax.broadcasted_iota(jnp.int32, e_win.shape, 1)
+            last = (key // BLK == SPAN - 1) & (key % BLK == lane - BLK)
+            e_win[...] = jnp.where((key // BLK == lane) | last, 1.0, 0.0).astype(dtype)
+        if far:
+            blocks = picked_blocks(ref["vert"][...], ctx_ref[0] - (NEAR - 1), rows // BLK)
             for slot, block in enumerate(blocks):
-                at = pl.ds((s * VMOST + slot) * BLK, BLK)
-                k_pool[at, :] = ref[block, :HS]
-                v_pool[at, :] = ref[block, HS:]
-        for s in range(2, pools):
-            at = slice(s * VMOST * BLK, (s + 1) * VMOST * BLK)
-            k_pool[at, :] = pair_refs[s - 2][:, :HS]
-            v_pool[at, :] = pair_refs[s - 2][:, HS:]
-        key = lax.broadcasted_iota(jnp.int32, e_win.shape, 0)
-        lane = lax.broadcasted_iota(jnp.int32, e_win.shape, 1)
-        last = (key // BLK == SPAN - 1) & (key % BLK == lane - BLK)
-        e_win[...] = jnp.where((key // BLK == lane) | last, 1.0, 0.0).astype(e_win.dtype)
-        key = lax.broadcasted_iota(jnp.int32, e_pool.shape, 0)
-        lane = lax.broadcasted_iota(jnp.int32, e_pool.shape, 1)
-        e_pool[...] = jnp.where(key // BLK == lane, 1.0, 0.0).astype(e_pool.dtype)
-
-    here = here_of(step, tp_ref)
+                at = slice(slot * BLK, (slot + 1) * BLK)
+                ref["k_pool"][at, :] = ref["kv_2"][block, :HS]
+                ref["v_pool"][at, :] = ref["kv_2"][block, HS:]
+            e_pool = ref["e_pool"]
+            for s in range(1, e_pool.shape[0] // (VMOST * BLK)):
+                at = slice(s * VMOST * BLK, (s + 1) * VMOST * BLK)
+                ref["k_pool"][at, :] = ref["pair", s][:, :HS]
+                ref["v_pool"][at, :] = ref["pair", s][:, HS:]
+            key = lax.broadcasted_iota(jnp.int32, e_pool.shape, 0)
+            lane = lax.broadcasted_iota(jnp.int32, e_pool.shape, 1)
+            e_pool[...] = jnp.where(key // BLK == lane, 1.0, 0.0).astype(dtype)
+
     q = q_ref[...]
     q = jnp.concatenate([q[:, h * HS : (h + 1) * HS] for h in range(heads)], axis=0)
-    row = lax.broadcasted_iota(jnp.int32, (BLK, LANES), 0)
-    lane = lax.broadcasted_iota(jnp.int32, (BLK, LANES), 1)
-    above = jnp.where(lane - BLK > row, MASKED, 0.0).astype(jnp.float32)
-    win_mask = win_ref[0][:, None, :] + above[None]
-    win_mask = win_mask.reshape(heads * BLK, LANES).astype(q.dtype)
-    pool_mask = jnp.broadcast_to(pool_ref[0][:, None, :], (heads, BLK, LANES))
-    pool_mask = pool_mask.reshape(heads * BLK, LANES).astype(q.dtype)
-
-    start = pl.multiple_of((here + 1) * BLK, BLK)
-    keys = jnp.concatenate([k_win[pl.ds(start, SPAN * BLK), :], e_win[...]], axis=1)
-    contract = (((1,), (1,)), ((), ()))
-    near_scores = lax.dot_general(
-        jnp.concatenate([q, win_mask], axis=1), keys, contract, preferred_element_type=jnp.float32
-    )
-    far_keys = jnp.concatenate([k_pool[...], e_pool[...]], axis=1)
-    far_scores = lax.dot_general(
-        jnp.concatenate([q, pool_mask], axis=1),
-        far_keys,
-        contract,
-        preferred_element_type=jnp.float32,
-    )
-    top = jnp.maximum(
-        jnp.max(near_scores, axis=1, keepdims=True), jnp.max(far_scores, axis=1, keepdims=True)
-    )
-    near_probs = jnp.exp2((near_scores - top) * EXP_SCALE).astype(q.dtype)
-    far_probs = jnp.exp2((far_scores - top) * EXP_SCALE).astype(q.dtype)
-    near_values = jnp.concatenate(
-        [v_win[pl.ds(start, SPAN * BLK), :], jnp.ones((SPAN * BLK, LANES), q.dtype)], axis=1
-    )
-    far_values = jnp.concatenate(
-        [v_pool[...], jnp.ones((v_pool.shape[0], LANES), q.dtype)], axis=1
-    )
-    summed = jnp.dot(near_probs, near_values, preferred_element_type=jnp.float32)
-    summed = summed + jnp.dot(far_probs, far_values, preferred_element_type=jnp.float32)
-    out = (summed[:, :HS] / summed[:, HS:]).astype(q.dtype)
+
+    def scores_of(mask, keys, lanes):
+        mask = mask.reshape(heads * BLK, LANES).astype(dtype)
+        return lax.dot_general(
+            jnp.concatenate([q, mask], axis=1),
+            jnp.concatenate([keys, lanes], axis=1),
+            (((1,), (1,)), ((), ())),
+            preferred_element_type=jnp.float32,
+        )
+
+    def weigh(scores, top, values):
+        probs = jnp.exp2((scores - top) * EXP_SCALE).astype(dtype)
+        values = jnp.concatenate([values, jnp.ones((values.shape[0], LANES), dtype)], axis=1)
+        return jnp.dot(probs, values, preferred_element_type=jnp.float32)
+
+    if near:
+        row = lax.broadcasted_iota(jnp.int32, (BLK, LANES), 0)
+        lane = lax.broadcasted_iota(jnp.int32, (BLK, LANES), 1)
+        above = jnp.where(lane - BLK > row, MASKED, 0.0).astype(jnp.float32)
+        start = pl.multiple_of((here_of(step, tp_ref) + 1) * BLK, BLK)
+        window = pl.ds(start, SPAN * BLK)
+        near_scores = scores_of(
+            ref["win"][0][:, None, :] + above[None], ref["k_win"][window, :], ref["e_win"][...]
+        )
+        top = jnp.max(near_scores, axis=1, keepdims=True)
+    if far:
+        mask = jnp.broadcast_to(ref["pool"][0][:, None, :], (heads, BLK, LANES))
+        far_scores = scores_of(mask, ref["k_pool"][...], ref["e_pool"][...])
+        far_top = jnp.max(far_scores, axis=1, keepdims=True)
+        if near:
+            top = jnp.maximum(top, far_top)
+        else:
+            near_top = ref["top"][...]
+            top = jnp.maximum(near_top[:, :1], far_top)
+            shrink = jnp.exp2((near_top - top) * EXP_SCALE)
+            summed = ref["sum"][...] * jnp.concatenate([shrink, shrink], axis=1)
+    if near:
+        summed = weigh(near_scores, top, ref["v_win"][window, :])
+    if far:
+        summed = summed + weigh(far_scores, top, ref["v_pool"][...])
+    else:
+        ref["sum_out"][...] = summed
+        ref["top_out"][...] = jnp.broadcast_to(top, (heads * BLK, LANES))
+        return
+
+    out = (summed[:, :HS] / summed[:, HS:]).astype(dtype)
+    attended = ref["attended"]
     out_rows = pl.ds(pl.multiple_of(step * BLK, BLK), BLK)
     for h in range(heads):
         attended[out_rows, h * HS : (h + 1) * HS] = out[h * BLK : (h + 1) * BLK]
 
     @pl.when(step == pl.num_programs(0) - 1)
     def _():
-        outs[-1][...] = attended[...]
+        ref["rows_out"][...] = attended[...]
         half = attended.shape[0] // 2
         for t in range(tiles):
             fetch(t).wait()
-            product = jnp.dot(attended[...], weight[t], preferred_element_type=jnp.float32)
-            product = product.astype(q.dtype)
-            outs[0][:, t * TILE : (t + 1) * TILE] = product[:half]
-            outs[1][:, t * TILE : (t + 1) * TILE] = product[half:]
-
-
-def attend(flips, tp, ctx, queries, win, pool, vertical, near_kv, pairs, out_weight, tiles, after):
+            product = jnp.dot(attended[...], ref["weight"][t], preferred_element_type=jnp.float32)
+            product = product.astype(dtype)
+            ref["send"][:, t * TILE : (t + 1) * TILE] = product[:half]
+            ref["keep"][:, t * TILE : (t + 1) * TILE] = product[half:]
+
+
+def attend(flips, tp, ctx, arrays, near, far, tiles, after):
+    queries, win, dtype = arrays["q"], arrays["win"], arrays["q"].dtype
     width = queries.shape[1]
     local_blocks, heads, _ = win.shape
     quarter = local_blocks // 4
     steps = len(flips) * quarter
-    pools = len(pairs) + 2
-    rows = near_kv[0].shape[0]
-    dtype = queries.dtype
-    far = pools * VMOST * BLK
+    rows = arrays["own"].shape[0]
+    pairs = [name for name in arrays if isinstance(name, tuple)]
+    far_rows = (len(pairs) + 1) * VMOST * BLK
 
     def here_of(step, tp_ref):
         owner = tp_ref[0] ^ jnp.where(step < quarter, flips[0], flips[1])
@@ -250,36 +246,57 @@
     def whole(shape):
         return pl.BlockSpec(shape, lambda g, tp, ctx: (0,) * len(shape))
 
+    def stepped(*block):
+        return pl.BlockSpec(block, lambda g, tp, ctx: (g, 0))
+
     table = pl.BlockSpec((1, heads, LANES), lambda g, tp, ctx: (here_of(g, tp), 0, 0))
-    out_shapes = [(steps * BLK // 2, tiles * TILE)] * 2 if tiles else []
-    out_shapes.append((steps * BLK, width))
+    inputs = {"q": pl.BlockSpec((BLK, width), lambda g, tp, ctx: (here_of(g, tp), 0))}
+    inputs["kv_2"] = whole(arrays["kv_2"].shape)
+    outputs, scratch = {}, {}
+    if near:
+        inputs["win"] = table
+        inputs["kv_1"] = inputs["own"] = inputs["kv_2"]
+        scratch["k_win"] = scratch["v_win"] = pltpu.VMEM((NEAR * rows, HS), dtype)
+        scratch["e_win"] = pltpu.VMEM((SPAN * BLK, LANES), dtype)
+    if far:
+        inputs["pool"] = table
+        inputs["vert"] = whole(arrays["vert"].shape)
+        inputs.update((name, whole(arrays[name].shape)) for name in pairs)
+        scratch["k_pool"] = scratch["v_pool"] = pltpu.VMEM((far_rows, HS), dtype)
+        scratch["e_pool"] = pltpu.VMEM((far_rows, LANES), dtype)
+        scratch["attended"] = pltpu.VMEM((steps * BLK, width), dtype)
+        outputs["rows_out"] = (jax.ShapeDtypeStruct((steps * BLK, width), dtype), None)
+        if not near:
+            inputs["sum"] = stepped(heads * BLK, 2 * LANES)
+            inputs["top"] = stepped(heads * BLK, LANES)
+    else:
+        shape = (steps * heads * BLK, 2 * LANES)
+        outputs["sum_out"] = (jax.ShapeDtypeStruct(shape, jnp.float32), stepped(heads * BLK, 2 * LANES))
+        shape = (steps * heads * BLK, LANES)
+        outputs["top_out"] = (jax.ShapeDtypeStruct(shape, jnp.float32), stepped(heads * BLK, LANES))
+    if tiles:
+        inputs["w"] = anywhere()
+        part = jax.ShapeDtypeStruct((steps * BLK // 2, tiles * TILE), dtype)
+        outputs["send"] = outputs["keep"] = (part, None)
+        scratch["weight"] = pltpu.VMEM((tiles, width, TILE), dtype)
+        scratch["arrival"] = pltpu.SemaphoreType.DMA((tiles,))
+    for place, x in enumerate(after):
+        inputs["after", place] = anywhere()
+        arrays = {**arrays, ("after", place): x}
     return pl.pallas_call(
-        functools.partial(attend_kernel, pools, tiles, here_of),
-        out_shape=[jax.ShapeDtypeStruct(shape, dtype) for shape in out_shapes],
+        functools.partial(attend_kernel, [*inputs, *outputs, *scratch], tiles, here_of),
+        out_shape=[shape for shape, _ in outputs.values()],
         grid_spec=pltpu.PrefetchScalarGridSpec(
             num_scalar_prefetch=2,
             grid=(steps,),
-            in_specs=[pl.BlockSpec((BLK, width), lambda g, tp, ctx: (here_of(g, tp), 0))]
-            + [table, table]
-            + [whole(x.shape) for x in [vertical, *near_kv, *pairs]]
-            + [anywhere() for _ in range(1 + len(after))],
-            out_specs=[whole(shape) for shape in out_shapes],
-            scratch_shapes=[
-                pltpu.VMEM((NEAR * rows, HS), dtype),
-                pltpu.VMEM((NEAR * rows, HS), dtype),
-                pltpu.VMEM((SPAN * BLK, LANES), dtype),
-                pltpu.VMEM((far, HS), dtype),
-                pltpu.VMEM((far, HS), dtype),
-                pltpu.VMEM((far, LANES), dtype),
-                pltpu.VMEM((steps * BLK, width), dtype),
-                pltpu.VMEM((max(tiles, 1), out_weight.shape[0], TILE), dtype),
-                pltpu.SemaphoreType.DMA((max(tiles, 1),)),
-            ],
+            in_specs=list(inputs.values()),
+            out_specs=[spec or whole(shape.shape) for shape, spec in outputs.values()],
+            scratch_shapes=list(scratch.values()),
         ),
         compiler_params=params(60),
         cost_estimate=SHORT,
         name="attend",
-    )(tp, ctx, queries, win, pool, vertical, *near_kv, *pairs, out_weight, *after)
+    )(tp, ctx, *[arrays[name] for name in inputs])
 
 
 def project_kernel(first, a_ref, w_hbm, *refs):
@@ -379,41 +396,32 @@
     def shifted(x, by):
         return lax.ppermute(x, "ctx", [(r, r + by) for r in range(ctx_size - by)])
 
-    def swapped(x):
-        return lax.ppermute(x, "ctx", [(r, r ^ 1) for r in range(ctx_size)])
-
     own, pair = pick(ctx, vertical, keys, values)
-    kv_2 = shifted(own, 2)
-    kv_even = lax.ppermute(own, "ctx", [(r, r + 1) for r in range(0, ctx_size, 2)])
-    steps = range(4, ctx_size, 2)
-    pairs = [shifted(pair, s) for s in steps]
-    near_kv = [own, kv_2, kv_even, swapped(kv_2)]
-    pairs += [swapped(x) for x in pairs]
-    slots = [(2, 0), (1, 2)] + [(s, 0) for s in steps] + [(s - 1, 2) for s in steps]
+    slots = range(NEAR - 1, ctx_size)
     win, pool = masks(ctx, vertical, slash, local_blocks, slots)
+    arrays = {"q": queries, "own": own, "win": win, "pool": pool, "vert": vertical, "w": out_weight}
+    arrays["kv_1"], arrays["kv_2"] = shifted(own, 1), shifted(own, 2)
+    for slot, back in list(enumerate(slots))[1:]:
+        arrays["pair", slot] = shifted(pair, back)
 
     def sibling(x):
         return lax.ppermute(x, "tp", [(j, j ^ 1) for j in range(4)])
 
     def across(x):
         return lax.ppermute(x, "tp", [(j, j ^ 2) for j in range(4)])
-
-    def attention(flips, tiles, after):
-        return attend(
-            flips, tp, ctx, queries, win, pool, vertical, near_kv, pairs, out_weight, tiles, after
-        )
 
     width = out_weight.shape[1]
     tiles = width // TILE
     assert tiles == 2 * ACROSS
-    send, keep, attended = attention((3, 2), ACROSS, ())
+    arrays["sum"], arrays["top"] = attend((3, 2), tp, ctx, arrays, True, False, 0, ())
+    attended, send, keep = attend((3, 2), tp, ctx, arrays, False, True, ACROSS, ())
     total = keep.astype(jnp.float32) + sibling(send).astype(jnp.float32)
     total = total.astype(keep.dtype)
     arrived = [across(total)]
     send, keep = project(attended, out_weight, ACROSS, ACROSS, (total,))
     total = add(keep, [sibling(x) for x in send])
     arrived.append(across(total))
-    (attended,) = attention((1, 0), 0, (total,))
+    (attended,) = attend((1, 0), tp, ctx, arrays, True, True, 0, (total,))
     send, keep = project(attended, out_weight, 0, tiles, (arrived[0],))
     got = [sibling(x) for x in send]
     out = None

time: 98.9 us -> 106 us (1.072)
  the two profiles are of different devices: /device:TPU:16 before, /device:TPU:0 now
where the time goes in v6:
time: 106 us; the launch traced here: 105 us
  Pallas kernels  57.4 us (54%)
  starting transfers between devices  30.8 us (29%)
  waiting for transfers between devices  9.41 us (9%)
  local copies, waits for them, and re-layouts  5.73 us (5%)
  other arithmetic  1.47 us (1%)
    pallas_call x3, Pallas kernels, attend(): pl.pallas_call(functools.partial(attend_kernel, [*inputs, *outputs, *scra...  32 us
    ppermute x7, starting transfers between devices, shifted(): return lax.ppermute(x, 'ctx', [(r, r + by) for r in range(ctx_size - by)])  26.6 us
    pallas_call x2, Pallas kernels, project(): pl.pallas_call(functools.partial(project_kernel, first), out_shape=[part]...  16.4 us
    ppermute x7, waiting for transfers between devices, sibling(): return lax.ppermute(x, 'tp', [(j, j ^ 1) for j in range(4)])  7.07 us
    unnamed x32, local copies, waits for them, and re-layouts  5.73 us
    pallas_call x1, Pallas kernels, add(): pl.pallas_call(add_kernel, out_shape=jax.ShapeDtypeStruct((rows, len(keep...  2.73 us
    pallas_call x2, Pallas kernels, finish(): pl.pallas_call(functools.partial(finish_kernel, len(keep)), out_shape=jax...  2.69 us
    ppermute x2, starting transfers between devices, across(): return lax.ppermute(x, 'tp', [(j, j ^ 2) for j in range(4)])  2.44 us
  transfers between devices with their start and end apart: 16, of which 6 were waited for; matrix products, arithmetic and copies ran while one was open for 0% of the time, Pallas kernels for 39%

profile of v6, /device:TPU:0, one launch (start us, length us, event | category | flops | bytes accessed | tf_op | source)
XLA Modules:
  0.0 105.0 jit_solution(12009547338455464970)
XLA Ops:
  0.0 2.0 %pick.1 = (bf16[512,256]{1,0:T(8,128)(2,1)}, bf16[128,256]{1,0:T(8,128)(2,1)}) custom-call(s32[1]{0:T(128)} %bitcast.1.rank_ref.ctx_ref, s32[8,16]{1,0:T(8,128)} %refs_6_.1, bf16[512,128]{1,0:T(8,128)(2,1)} %k_ref.1, bf16[512,128]{1,0:T(8,128)(2,1)} %v_ref.1), custom_call_target="tpu_custom_call" | custom-call | tf_op jit(solution)/shard_map/pick/pallas_call | solution.py:63
  2.0 4.9 %collective-permute-start.1 = (bf16[512,256]{1,0:T(8,128)(2,1)}, bf16[512,256]{1,0:T(8,128)(2,1)S(1)}, u32[]{:S(2)}, u32[]{:S(2)}) collective-permute-start(bf16[512,256]{1,0:T(8,128)(2,1)} %get-tuple-element.26.refs_4_), channel_id=1, source_target_pairs={{0,4},{4,8},{8,12},{12,16},{16,20},{20,24},{24,28},{1,5},{5,9},{9,... | collective-permute-start | bytes 786440 | tf_op jit(solution)/shard_map/ppermute | solution.py:397
  6.9 3.5 %collective-permute-start = (bf16[512,256]{1,0:T(8,128)(2,1)}, bf16[512,256]{1,0:T(8,128)(2,1)S(1)}, u32[]{:S(2)}, u32[]{:S(2)}) collective-permute-start(bf16[512,256]{1,0:T(8,128)(2,1)} %get-tuple-element.26.refs_4_), channel_id=1, source_target_pairs={{0,8},{4,12},{8,16},{12,20},{16,24},{20,28},{1,9},{5,13},{9,17},{1... | collective-permute-start | bytes 786440 | tf_op jit(solution)/shard_map/ppermute | solution.py:397
  10.4 2.1 %collective-permute-start.6 = (bf16[128,256]{1,0:T(8,128)(2,1)}, bf16[128,256]{1,0:T(8,128)(2,1)S(1)}, u32[]{:S(2)}, u32[]{:S(2)}) collective-permute-start(bf16[128,256]{1,0:T(8,128)(2,1)} %get-tuple-element.29), channel_id=1, source_target_pairs={{0,28},{1,29},{2,30},{3,31}} | collective-permute-start | bytes 196616 | tf_op jit(solution)/shard_map/ppermute | solution.py:397
  12.5 1.8 %collective-permute-start.5 = (bf16[128,256]{1,0:T(8,128)(2,1)}, bf16[128,256]{1,0:T(8,128)(2,1)S(1)}, u32[]{:S(2)}, u32[]{:S(2)}) collective-permute-start(bf16[128,256]{1,0:T(8,128)(2,1)} %get-tuple-element.29), channel_id=1, source_target_pairs={{0,24},{4,28},{1,25},{5,29},{2,26},{6,30},{3,27},{7,31}} | collective-permute-start | bytes 196616 | tf_op jit(solution)/shard_map/ppermute | solution.py:397
  14.4 1.3 %collective-permute-start.4 = (bf16[128,256]{1,0:T(8,128)(2,1)}, bf16[128,256]{1,0:T(8,128)(2,1)S(1)}, u32[]{:S(2)}, u32[]{:S(2)}) collective-permute-start(bf16[128,256]{1,0:T(8,128)(2,1)} %get-tuple-element.29), channel_id=1, source_target_pairs={{0,20},{4,24},{8,28},{1,21},{5,25},{9,29},{2,22},{6,26},{10,30},{3... | collective-permute-start | bytes 196616 | tf_op jit(solution)/shard_map/ppermute | solution.py:397
  15.7 4.4 %collective-permute-start.3 = (bf16[128,256]{1,0:T(8,128)(2,1)}, bf16[128,256]{1,0:T(8,128)(2,1)S(1)}, u32[]{:S(2)}, u32[]{:S(2)}) collective-permute-start(bf16[128,256]{1,0:T(8,128)(2,1)} %get-tuple-element.29), channel_id=1, source_target_pairs={{0,16},{4,20},{8,24},{12,28},{1,17},{5,21},{9,25},{13,29},{2,18},{... | collective-permute-start | bytes 196616 | tf_op jit(solution)/shard_map/ppermute | solution.py:397
  20.2 8.6 %collective-permute-start.2 = (bf16[128,256]{1,0:T(8,128)(2,1)}, bf16[128,256]{1,0:T(8,128)(2,1)S(1)}, u32[]{:S(2)}, u32[]{:S(2)}) collective-permute-start(bf16[128,256]{1,0:T(8,128)(2,1)} %get-tuple-element.29), channel_id=1, source_target_pairs={{0,12},{4,16},{8,20},{12,24},{16,28},{1,13},{5,17},{9,21},{13,25},... | collective-permute-start | bytes 196616 | tf_op jit(solution)/shard_map/ppermute | solution.py:397
  28.7 1.5 %masks.1 = (f32[8,8,128]{2,1,0:T(8,128)}, f32[8,8,128]{2,1,0:T(8,128)}) custom-call(s32[1]{0:T(128)} %bitcast.1.rank_ref.ctx_ref, s32[8,16]{1,0:T(8,128)} %refs_6_.1, s32[8,8]{1,0:T(8,128)} %slash_ref.1), custom_call_target="tpu_custom_call" | custom-call | tf_op jit(solution)/shard_map/masks/pallas_call | solution.py:115
  30.3 7.8 %attend.3 = (f32[2048,256]{1,0:T(8,128)}, f32[2048,128]{1,0:T(8,128)}) custom-call(s32[1]{0:T(128)} %bitcast.tp_ref, s32[1]{0:T(128)} %bitcast.1.rank_ref.ctx_ref, bf16[512,1024]{1,0:T(8,128)(2,1)} %refs_0_.5, bf16[512,256]{1,0:T(8,128)(2,1)} %copy-done.7, f32[8,8,128]{2,1,0:T(8,128)} %get-tuple-element.27.refs_2_, bf16[512,256]{1,0:T(8,128)(2,1)} %copy-done.8, ...), custom_call_target="tpu_custom_call" | custom-call | tf_op jit(solution)/shard_map/attend/pallas_call | solution.py:286
  38.0 0.0 collective-permute-done.6.refs_8_.refs_11_
  38.1 0.0 collective-permute-done.4.refs_6_.refs_9_
  38.1 0.5 copy-done.11
  38.7 0.0 copy-done.12
  38.7 0.0 copy-done.13
  38.7 0.0 copy-done.14
  38.8 0.0 copy-done.15
  38.8 12.7 %attend.4 = (bf16[256,1024]{1,0:T(8,128)(2,1)}, bf16[128,4096]{1,0:T(8,128)(2,1)}, bf16[128,4096]{1,0:T(8,128)(2,1)}) custom-call(s32[1]{0:T(128)} %bitcast.tp_ref, s32[1]{0:T(128)} %bitcast.1.rank_ref.ctx_ref, bf16[512,1024]{1,0:T(8,128)(2,1)} %refs_0_.5, bf16[512,256]{1,0:T(8,128)(2,1)} %copy-done.7, f32[8,8,128]{2,1,0:T(8,128)} %get-tuple-element.28.refs_2_.refs_5_, ...), custom_call_target="tpu_custom_call" | custom-call | tf_op jit(solution)/shard_map/attend/pallas_call | solution.py:286
  51.5 0.1 collective-permute-start.7
  51.6 2.9 %collective-permute-done.7 = bf16[128,4096]{1,0:T(8,128)(2,1)S(1)} collective-permute-done((bf16[128,4096]{1,0:T(8,128)(2,1)}, bf16[128,4096]{1,0:T(8,128)(2,1)S(1)}, u32[]{:S(2)}, u32[]{:S(2)}) %collective-permute-start.7) | collective-permute-done | bytes 1048608 | tf_op jit(solution)/shard_map/ppermute | solution.py:408
  54.4 1.5 %add_convert_fusion.refs_0_ = bf16[128,4096]{1,0:T(8,128)(2,1)S(1)} fusion(bf16[128,4096]{1,0:T(8,128)(2,1)S(1)} %collective-permute-done.7, bf16[128,4096]{1,0:T(8,128)(2,1)} %get-tuple-element.33), kind=kLoop, calls=%fused_computation | loop fusion | flops 2097152 | bytes 3145728 | tf_op jit(solution)/shard_map/convert_element_type | solution.py:419
  55.9 0.0 copy-start.6
  55.9 1.6 %collective-permute-start.10 = (bf16[128,4096]{1,0:T(8,128)(2,1)S(1)}, bf16[128,4096]{1,0:T(8,128)(2,1)S(1)}, u32[]{:S(2)}, u32[]{:S(2)}) collective-permute-start(bf16[128,4096]{1,0:T(8,128)(2,1)S(1)} %add_convert_fusion.refs_0_), channel_id=1, source_target_pairs={{0,2},{1,3},{2,0},{3,1},{4,6},{5,7},{6,4},{7,5},{8,10},{9,11},{10,... | collective-permute-start | bytes 3145736 | tf_op jit(solution)/shard_map/ppermute | solution.py:411
  57.5 6.7 %project.2 = (bf16[128,2048]{1,0:T(8,128)(2,1)}, bf16[128,2048]{1,0:T(8,128)(2,1)}, bf16[128,2048]{1,0:T(8,128)(2,1)}, bf16[128,2048]{1,0:T(8,128)(2,1)}) custom-call(bf16[256,1024]{1,0:T(8,128)(2,1)} %get-tuple-element.32.a_ref, bf16[1024,8192]{1,0:T(8,128)(2,1)} %w_hbm.3, bf16[128,4096]{1,0:T(8,128)(2,1)} %copy-done.6), custom_call_target="tpu_custom_call" | custom-call | tf_op jit(solution)/shard_map/project/pallas_call | solution.py:329
  64.2 0.1 collective-permute-start.8
  64.3 0.5 collective-permute-start.9
  64.8 1.6 %collective-permute-done.8.refs_2_ = bf16[128,2048]{1,0:T(8,128)(2,1)S(1)} collective-permute-done((bf16[128,2048]{1,0:T(8,128)(2,1)}, bf16[128,2048]{1,0:T(8,128)(2,1)S(1)}, u32[]{:S(2)}, u32[]{:S(2)}) %collective-permute-start.8) | collective-permute-done | bytes 524320 | tf_op jit(solution)/shard_map/ppermute | solution.py:408
  66.4 0.7 collective-permute-done.9.refs_3_
  67.1 0.0 copy-done.9
  67.2 0.8 copy-done.10
  67.9 2.7 %add.6.refs_12_ = bf16[128,4096]{1,0:T(8,128)(2,1)} custom-call(bf16[128,2048]{1,0:T(8,128)(2,1)} %get-tuple-element.35.refs_0_, bf16[128,2048]{1,0:T(8,128)(2,1)} %get-tuple-element.36.refs_1_, bf16[128,2048]{1,0:T(8,128)(2,1)} %copy-done.9, bf16[128,2048]{1,0:T(8,128)(2,1)} %copy-done.10), custom_call_target="tpu_custom_call" | custom-call | tf_op jit(solution)/shard_map/add/pallas_call | solution.py:355
  70.6 0.9 collective-permute-start.13
  71.5 11.5 %attend.5.a_ref = bf16[256,1024]{1,0:T(8,128)(2,1)} custom-call(s32[1]{0:T(128)} %bitcast.tp_ref, s32[1]{0:T(128)} %bitcast.1.rank_ref.ctx_ref, bf16[512,1024]{1,0:T(8,128)(2,1)} %refs_0_.5, bf16[512,256]{1,0:T(8,128)(2,1)} %copy-done.7, f32[8,8,128]{2,1,0:T(8,128)} %get-tuple-element.27.refs_2_, bf16[512,256]{1,0:T(8,128)(2,1)} %copy-done.8, ...), custom_call_target="tpu_custom_call" | custom-call | tf_op jit(solution)/shard_map/attend/pallas_call | solution.py:286
  83.1 0.0 copy-start
  83.1 1.0 copy-done
  84.0 9.7 %project.3 = (bf16[128,2048]{1,0:T(8,128)(2,1)}, bf16[128,2048]{1,0:T(8,128)(2,1)}, bf16[128,2048]{1,0:T(8,128)(2,1)}, bf16[128,2048]{1,0:T(8,128)(2,1)}, bf16[1...) custom-call(bf16[256,1024]{1,0:T(8,128)(2,1)} %attend.5.a_ref, ...), custom_call_target="tpu_custom_call" | custom-call | tf_op jit(solution)/shard_map/project/pallas_call | solution.py:329
  93.7 0.1 collective-permute-start.14
  93.8 0.5 collective-permute-start.15
  94.3 0.1 collective-permute-start.11
  94.4 0.4 collective-permute-start.12
  94.8 1.1 %collective-permute-done.14.refs_2_ = bf16[128,2048]{1,0:T(8,128)(2,1)S(1)} collective-permute-done((bf16[128,2048]{1,0:T(8,128)(2,1)}, bf16[128,2048]{1,0:T(8,128)(2,1)S(1)}, u32[]{:S(2)}, u32[]{:S(2)}) %collective-permute-start.14) | collective-permute-done | bytes 524320 | tf_op jit(solution)/shard_map/ppermute | solution.py:408
  95.9 0.7 collective-permute-done.15.refs_3_
  96.7 1.2 %copy-done.1 = bf16[128,4096]{1,0:T(8,128)(2,1)S(1)} copy-done((bf16[128,4096]{1,0:T(8,128)(2,1)S(1)}, bf16[128,4096]{1,0:T(8,128)(2,1)}, u32[]{:S(2)}) %copy-start.1) | copy-done | bytes 1048600
  97.9 1.0 copy-done.4
  99.0 1.0 copy-done.5
  100.0 1.3 %finish.2.refs_5_ = bf16[128,8192]{1,0:T(8,128)(2,1)} custom-call(bf16[128,2048]{1,0:T(8,128)(2,1)S(1)} %copy-done.4, bf16[128,2048]{1,0:T(8,128)(2,1)S(1)} %copy-done.5, bf16[128,2048]{1,0:T(8,128)(2,1)S(1)} %collective-permute-done.14.refs_2_, bf16[128,2048]{1,0:T(8,128)(2,1)S(1)} %collective-permute-done.15.refs_3_, bf16[128,4096]{1,0:T(8,128)(2,1)S(1)} %copy-done.1), custom_call_target="tpu_custom_call" | custom-call | tf_op jit(solution)/shard_map/finish/pallas_call | solution.py:377
  101.4 2.3 %collective-permute-done.13.refs_4_ = bf16[128,4096]{1,0:T(8,128)(2,1)S(1)} collective-permute-done((bf16[128,4096]{1,0:T(8,128)(2,1)}, bf16[128,4096]{1,0:T(8,128)(2,1)S(1)}, u32[]{:S(2)}, u32[]{:S(2)}) %collective-permute-start.13) | collective-permute-done | bytes 1048608 | tf_op jit(solution)/shard_map/ppermute | solution.py:411
  103.7 1.3 %finish.3 = bf16[128,8192]{1,0:T(8,128)(2,1)} custom-call(bf16[128,2048]{1,0:T(8,128)(2,1)S(1)} %copy-done.2, bf16[128,2048]{1,0:T(8,128)(2,1)S(1)} %copy-done.3, bf16[128,2048]{1,0:T(8,128)(2,1)S(1)} %collective-permute-done.11.refs_2_, bf16[128,2048]{1,0:T(8,128)(2,1)S(1)} %collective-permute-done.12.refs_3_, ...), custom_call_target="tpu_custom_call", output_to_operand_aliasing={{}: (5, {})} | custom-call | tf_op jit(solution)/shard_map/finish/pallas_call | solution.py:377
  (27 shorter events, 0.1 us)
Async XLA Ops:
  2.0 13.7 %collective-permute-start.1 = (bf16[512,256]{1,0:T(8,128)(2,1)}, bf16[512,256]{1,0:T(8,128)(2,1)S(1)}, u32[]{:S(2)}, u32[]{:S(2)}) collective-permute-start(bf16[512,256]{1,0:T(8,128)(2,1)} %get-tuple-element.26.refs_4_), channel_id=1, source_target_pairs={{0,4},{4,8},{8,12},{12,16},{16,20},{20,24},{24,28},{1,5},{5,9},{9,... | collective-permute-start | bytes 786440 | tf_op jit(solution)/shard_map/ppermute | solution.py:397
  6.9 13.2 %collective-permute-start = (bf16[512,256]{1,0:T(8,128)(2,1)}, bf16[512,256]{1,0:T(8,128)(2,1)S(1)}, u32[]{:S(2)}, u32[]{:S(2)}) collective-permute-start(bf16[512,256]{1,0:T(8,128)(2,1)} %get-tuple-element.26.refs_4_), channel_id=1, source_target_pairs={{0,8},{4,12},{8,16},{12,20},{16,24},{20,28},{1,9},{5,13},{9,17},{1... | collective-permute-start | bytes 786440 | tf_op jit(solution)/shard_map/ppermute | solution.py:397
  10.4 27.7 %collective-permute-start.6 = (bf16[128,256]{1,0:T(8,128)(2,1)}, bf16[128,256]{1,0:T(8,128)(2,1)S(1)}, u32[]{:S(2)}, u32[]{:S(2)}) collective-permute-start(bf16[128,256]{1,0:T(8,128)(2,1)} %get-tuple-element.29), channel_id=1, source_target_pairs={{0,28},{1,29},{2,30},{3,31}} | collective-permute-start | bytes 196616 | tf_op jit(solution)/shard_map/ppermute | solution.py:397
  12.5 25.5 %collective-permute-start.5 = (bf16[128,256]{1,0:T(8,128)(2,1)}, bf16[128,256]{1,0:T(8,128)(2,1)S(1)}, u32[]{:S(2)}, u32[]{:S(2)}) collective-permute-start(bf16[128,256]{1,0:T(8,128)(2,1)} %get-tuple-element.29), channel_id=1, source_target_pairs={{0,24},{4,28},{1,25},{5,29},{2,26},{6,30},{3,27},{7,31}} | collective-permute-start | bytes 196616 | tf_op jit(solution)/shard_map/ppermute | solution.py:397
  14.4 23.7 %collective-permute-start.4 = (bf16[128,256]{1,0:T(8,128)(2,1)}, bf16[128,256]{1,0:T(8,128)(2,1)S(1)}, u32[]{:S(2)}, u32[]{:S(2)}) collective-permute-start(bf16[128,256]{1,0:T(8,128)(2,1)} %get-tuple-element.29), channel_id=1, source_target_pairs={{0,20},{4,24},{8,28},{1,21},{5,25},{9,29},{2,22},{6,26},{10,30},{3... | collective-permute-start | bytes 196616 | tf_op jit(solution)/shard_map/ppermute | solution.py:397
  15.7 14.6 %copy-start.8 = (bf16[512,256]{1,0:T(8,128)(2,1)}, bf16[512,256]{1,0:T(8,128)(2,1)S(1)}, u32[]{:S(2)}) copy-start(bf16[512,256]{1,0:T(8,128)(2,1)S(1)} %collective-permute-done.1.refs_3_) | copy-start | bytes 786436
  15.7 22.4 %collective-permute-start.3 = (bf16[128,256]{1,0:T(8,128)(2,1)}, bf16[128,256]{1,0:T(8,128)(2,1)S(1)}, u32[]{:S(2)}, u32[]{:S(2)}) collective-permute-start(bf16[128,256]{1,0:T(8,128)(2,1)} %get-tuple-element.29), channel_id=1, source_target_pairs={{0,16},{4,20},{8,24},{12,28},{1,17},{5,21},{9,25},{13,29},{2,18},{... | collective-permute-start | bytes 196616 | tf_op jit(solution)/shard_map/ppermute | solution.py:397
  20.1 10.1 %copy-start.7 = (bf16[512,256]{1,0:T(8,128)(2,1)}, bf16[512,256]{1,0:T(8,128)(2,1)S(1)}, u32[]{:S(2)}) copy-start(bf16[512,256]{1,0:T(8,128)(2,1)S(1)} %collective-permute-done.refs_1_) | copy-start | bytes 786436
  20.2 18.0 %collective-permute-start.2 = (bf16[128,256]{1,0:T(8,128)(2,1)}, bf16[128,256]{1,0:T(8,128)(2,1)S(1)}, u32[]{:S(2)}, u32[]{:S(2)}) collective-permute-start(bf16[128,256]{1,0:T(8,128)(2,1)} %get-tuple-element.29), channel_id=1, source_target_pairs={{0,12},{4,16},{8,20},{12,24},{16,28},{1,13},{5,17},{9,21},{13,25},... | collective-permute-start | bytes 196616 | tf_op jit(solution)/shard_map/ppermute | solution.py:397
  38.0 0.6 copy-start.11
  38.1 0.6 copy-start.12
  38.1 0.6 copy-start.13
  38.1 0.7 copy-start.14
  38.1 0.6 copy-start.15
  51.5 2.9 %collective-permute-start.7 = (bf16[128,4096]{1,0:T(8,128)(2,1)}, bf16[128,4096]{1,0:T(8,128)(2,1)S(1)}, u32[]{:S(2)}, u32[]{:S(2)}) collective-permute-start(bf16[128,4096]{1,0:T(8,128)(2,1)} %get-tuple-element.34), channel_id=1, source_target_pairs={{0,1},{1,0},{2,3},{3,2},{4,5},{5,4},{6,7},{7,6},{8,9},{9,8},{10,11... | collective-permute-start | bytes 3145736 | tf_op jit(solution)/shard_map/ppermute | solution.py:408
  55.9 1.6 %copy-start.6 = (bf16[128,4096]{1,0:T(8,128)(2,1)}, bf16[128,4096]{1,0:T(8,128)(2,1)S(1)}, u32[]{:S(2)}) copy-start(bf16[128,4096]{1,0:T(8,128)(2,1)S(1)} %add_convert_fusion.refs_0_) | copy-start | bytes 3145732
  55.9 27.1 %collective-permute-start.10 = (bf16[128,4096]{1,0:T(8,128)(2,1)S(1)}, bf16[128,4096]{1,0:T(8,128)(2,1)S(1)}, u32[]{:S(2)}, u32[]{:S(2)}) collective-permute-start(bf16[128,4096]{1,0:T(8,128)(2,1)S(1)} %add_convert_fusion.refs_0_), channel_id=1, source_target_pairs={{0,2},{1,3},{2,0},{3,1},{4,6},{5,7},{6,4},{7,5},{8,10},{9,11},{10,... | collective-permute-start | bytes 3145736 | tf_op jit(solution)/shard_map/ppermute | solution.py:411
  64.2 2.2 %collective-permute-start.8 = (bf16[128,2048]{1,0:T(8,128)(2,1)}, bf16[128,2048]{1,0:T(8,128)(2,1)S(1)}, u32[]{:S(2)}, u32[]{:S(2)}) collective-permute-start(bf16[128,2048]{1,0:T(8,128)(2,1)} %get-tuple-element.37), channel_id=1, source_target_pairs={{0,1},{1,0},{2,3},{3,2},{4,5},{5,4},{6,7},{7,6},{8,9},{9,8},{10,11... | collective-permute-start | bytes 1572872 | tf_op jit(solution)/shard_map/ppermute | solution.py:408
  64.3 2.9 %collective-permute-start.9 = (bf16[128,2048]{1,0:T(8,128)(2,1)}, bf16[128,2048]{1,0:T(8,128)(2,1)S(1)}, u32[]{:S(2)}, u32[]{:S(2)}) collective-permute-start(bf16[128,2048]{1,0:T(8,128)(2,1)} %get-tuple-element.38), channel_id=1, source_target_pairs={{0,1},{1,0},{2,3},{3,2},{4,5},{5,4},{6,7},{7,6},{8,9},{9,8},{10,11... | collective-permute-start | bytes 1572872 | tf_op jit(solution)/shard_map/ppermute | solution.py:408
  66.4 0.8 copy-start.9
  67.1 0.8 copy-start.10
  70.6 33.0 %collective-permute-start.13 = (bf16[128,4096]{1,0:T(8,128)(2,1)}, bf16[128,4096]{1,0:T(8,128)(2,1)S(1)}, u32[]{:S(2)}, u32[]{:S(2)}) collective-permute-start(bf16[128,4096]{1,0:T(8,128)(2,1)} %add.6.refs_12_), channel_id=1, source_target_pairs={{0,2},{1,3},{2,0},{3,1},{4,6},{5,7},{6,4},{7,5},{8,10},{9,11},{10,... | collective-permute-start | bytes 3145736 | tf_op jit(solution)/shard_map/ppermute | solution.py:411
  83.1 1.0 copy-start
  93.7 2.2 %collective-permute-start.14 = (bf16[128,2048]{1,0:T(8,128)(2,1)}, bf16[128,2048]{1,0:T(8,128)(2,1)S(1)}, u32[]{:S(2)}, u32[]{:S(2)}) collective-permute-start(bf16[128,2048]{1,0:T(8,128)(2,1)} %get-tuple-element.45), channel_id=1, source_target_pairs={{0,1},{1,0},{2,3},{3,2},{4,5},{5,4},{6,7},{7,6},{8,9},{9,8},{10,11... | collective-permute-start | bytes 1572872 | tf_op jit(solution)/shard_map/ppermute | solution.py:408
  93.8 2.9 %collective-permute-start.15 = (bf16[128,2048]{1,0:T(8,128)(2,1)}, bf16[128,2048]{1,0:T(8,128)(2,1)S(1)}, u32[]{:S(2)}, u32[]{:S(2)}) collective-permute-start(bf16[128,2048]{1,0:T(8,128)(2,1)} %get-tuple-element.46), channel_id=1, source_target_pairs={{0,1},{1,0},{2,3},{3,2},{4,5},{5,4},{6,7},{7,6},{8,9},{9,8},{10,11... | collective-permute-start | bytes 1572872 | tf_op jit(solution)/shard_map/ppermute | solution.py:408
  94.3 7.0 %collective-permute-start.11 = (bf16[128,2048]{1,0:T(8,128)(2,1)}, bf16[128,2048]{1,0:T(8,128)(2,1)S(1)}, u32[]{:S(2)}, u32[]{:S(2)}) collective-permute-start(bf16[128,2048]{1,0:T(8,128)(2,1)} %get-tuple-element.41), channel_id=1, source_target_pairs={{0,1},{1,0},{2,3},{3,2},{4,5},{5,4},{6,7},{7,6},{8,9},{9,8},{10,11... | collective-permute-start | bytes 1572872 | tf_op jit(solution)/shard_map/ppermute | solution.py:408
  94.4 6.9 %collective-permute-start.12 = (bf16[128,2048]{1,0:T(8,128)(2,1)}, bf16[128,2048]{1,0:T(8,128)(2,1)S(1)}, u32[]{:S(2)}, u32[]{:S(2)}) collective-permute-start(bf16[128,2048]{1,0:T(8,128)(2,1)} %get-tuple-element.42), channel_id=1, source_target_pairs={{0,1},{1,0},{2,3},{3,2},{4,5},{5,4},{6,7},{7,6},{8,9},{9,8},{10,11... | collective-permute-start | bytes 1572872 | tf_op jit(solution)/shard_map/ppermute | solution.py:408
  96.7 1.2 %copy-start.1 = (bf16[128,4096]{1,0:T(8,128)(2,1)S(1)}, bf16[128,4096]{1,0:T(8,128)(2,1)}, u32[]{:S(2)}) copy-start(bf16[128,4096]{1,0:T(8,128)(2,1)} %copy-done) | copy-start | bytes 3145732
  97.9 1.0 copy-start.4
  99.0 1.0 copy-start.5
  100.0 3.7 %copy-start.2 = (bf16[128,2048]{1,0:T(8,128)(2,1)S(1)}, bf16[128,2048]{1,0:T(8,128)(2,1)}, u32[]{:S(2)}) copy-start(bf16[128,2048]{1,0:T(8,128)(2,1)} %get-tuple-element.39.refs_0_) | copy-start | bytes 1572868
  100.0 3.7 %copy-start.3 = (bf16[128,2048]{1,0:T(8,128)(2,1)S(1)}, bf16[128,2048]{1,0:T(8,128)(2,1)}, u32[]{:S(2)}) copy-start(bf16[128,2048]{1,0:T(8,128)(2,1)} %get-tuple-element.40.refs_1_) | copy-start | bytes 1572868

commit v7 on v5

v7 whole, which is shorter than its diff:
```python
import functools

import jax
import jax.numpy as jnp
from jax import lax
from jax.experimental import pallas as pl
from jax.experimental.pallas import tpu as pltpu
from jax.sharding import PartitionSpec as P

HS = 128
BLK = 64
SPAN = 16
VMOST = 2
NEAR = 3
LANES = 128
MASKED = -1e30
EXP_SCALE = 1.4426950408889634 / (HS**0.5)
TILE = 1024
PIECE = 2
HEAD = 4
MIB = 1024 * 1024


SHORT = pl.CostEstimate(flops=0, bytes_accessed=0, transcendentals=0)


def vmem():
    return pl.BlockSpec(memory_space=pltpu.VMEM)


def smem():
    return pl.BlockSpec(memory_space=pltpu.SMEM)


def anywhere():
    return pl.BlockSpec(memory_space=pl.ANY)


def params(mib):
    return pltpu.CompilerParams(vmem_limit_bytes=mib * MIB)


def picked_blocks(vertical, shard, local_blocks):
    block = vertical - shard * local_blocks
    block = jnp.where((block >= 0) & (block < local_blocks), block, local_blocks)
    first = jnp.min(block)
    second = jnp.min(jnp.where(block > first, block, local_blocks))
    return [
        pl.ds(pl.multiple_of(jnp.minimum(x, local_blocks - 1) * BLK, BLK), BLK)
        for x in (first, second)
    ]


def pick_kernel(rank_ref, vert_ref, k_ref, v_ref, both_ref, pair_ref):
    both_ref[:, :HS] = k_ref[...]
    both_ref[:, HS:] = v_ref[...]
    blocks = picked_blocks(vert_ref[...], rank_ref[0], k_ref.shape[0] // BLK)
    for slot, rows in enumerate(blocks):
        pair_ref[slot * BLK : (slot + 1) * BLK, :] = both_ref[rows, :]


def pick(rank, vertical, keys, values):
    return pl.pallas_call(
        pick_kernel,
        out_shape=(
            jax.ShapeDtypeStruct((keys.shape[0], 2 * HS), keys.dtype),
            jax.ShapeDtypeStruct((VMOST * BLK, 2 * HS), keys.dtype),
        ),
        in_specs=[smem(), vmem(), vmem(), vmem()],
        out_specs=(vmem(), vmem()),
        compiler_params=params(60),
        name="pick",
    )(rank, vertical, keys, values)


def member(table, blocks):
    found = table[:, :1] == blocks
    for column in range(1, table.shape[1]):
        found = found | (table[:, column : column + 1] == blocks)
    return found


def pool_blocks(vertical, rank, slots, local_blocks):
    lane = lax.broadcasted_iota(jnp.int32, (vertical.shape[0], LANES), 1)
    shard = jnp.where(lane // VMOST < slots, rank - (NEAR - 1) - lane // VMOST, -1)
    first = jnp.full((1, LANES), local_blocks, jnp.int32)
    second = first
    for j in reversed(range(local_blocks)):
        here = member(vertical, shard * local_blocks + j)
        here = jnp.max(jnp.where(here, 1, 0), axis=0, keepdims=True) == 1
        second = jnp.where(here, first, second)
        first = jnp.where(here, j, first)
    picked = jnp.where(lane % VMOST == 0, first, second)
    return jnp.where((picked < local_blocks) & (shard >= 0), shard * local_blocks + picked, -1)


def attend_kernel(
    slots, tiles, flips, tp_ref, ctx_ref, q_ref, vert_ref, slash_ref, own, kv_1, kv_2, *refs
):
    pairs = refs[: slots - 1]
    w_hbm = refs[slots - 1]
    kv_win, e_win, kv_pool, e_pool, blocks_ref, attended, weight, arrival, landed = refs[-9:]
    outs = refs[-12:-9] if tiles else refs[-10:-9]
    step = pl.program_id(0)
    heads = vert_ref.shape[0]
    rows = own.shape[0]
    local_blocks = rows // BLK
    quarter = local_blocks // 4
    pair_rows = VMOST * BLK
    dtype = q_ref.dtype
    rank = ctx_ref[0]

    def fetch(t):
        return pltpu.make_async_copy(
            w_hbm.at[:, pl.ds(t * TILE, TILE)], weight.at[t], arrival.at[t]
        )

    @pl.when(step == 0)
    def _():
        copies = [
            pltpu.make_async_copy(x, kv_win.at[pl.ds(s * rows, rows), :], landed.at[s])
            for s, x in enumerate((kv_2, kv_1, own))
        ]
        copies += [
            pltpu.make_async_copy(
                x, kv_pool.at[pl.ds((s + 1) * pair_rows, pair_rows), :], landed.at[NEAR + s]
            )
            for s, x in enumerate(pairs)
        ]
        for copy in copies:
            copy.start()
        for t in range(tiles):
            fetch(t).start()
        key = lax.broadcasted_iota(jnp.int32, e_win.shape, 0)
        lane = lax.broadcasted_iota(jnp.int32, e_win.shape, 1)
        last = (key - (SPAN - 1) * BLK == lane - BLK) & (lane >= BLK)
        e_win[...] = jnp.where((key // BLK == lane) | last, 1.0, 0.0).astype(dtype)
        key = lax.broadcasted_iota(jnp.int32, e_pool.shape, 0)
        lane = lax.broadcasted_iota(jnp.int32, e_pool.shape, 1)
        e_pool[...] = jnp.where(key // BLK == lane, 1.0, 0.0).astype(dtype)
        blocks_ref[...] = pool_blocks(vert_ref[...], rank, slots, local_blocks)
        picked = picked_blocks(vert_ref[...], rank - (NEAR - 1), local_blocks)
        for copy in copies:
            copy.wait()
        for slot, block in enumerate(picked):
            kv_pool[slot * BLK : (slot + 1) * BLK, :] = kv_win[block, :]

    owner = tp_ref[0] ^ jnp.where(step == 0, flips[0], flips[1])
    lane = lax.broadcasted_iota(jnp.int32, (heads, LANES), 1)
    row = lax.broadcasted_iota(jnp.int32, (BLK, LANES), 0)
    above = lax.broadcasted_iota(jnp.int32, (BLK, LANES), 1) - BLK > row
    above = jnp.where(above, MASKED, 0.0).astype(jnp.float32)
    offset_ok = member(slash_ref[...], SPAN - 1 - lane)
    block = blocks_ref[...]
    pool_ok = member(vert_ref[...], block) & (block >= 0)
    contract = (((1,), (1,)), ((), ()))

    def with_ones(values):
        return jnp.concatenate([values, jnp.ones((values.shape[0], LANES), dtype)], axis=1)

    near, far_q, windows = [], [], []
    for u in range(quarter):
        here = owner * quarter + u
        q = q_ref[u * BLK : (u + 1) * BLK, :]
        q = jnp.concatenate([q[:, h * HS : (h + 1) * HS] for h in range(heads)], axis=0)
        first = rank * local_blocks + here - (SPAN - 1)
        seen = first + lane
        ok = (seen >= 0) & (offset_ok | member(vert_ref[...], seen))
        mask = jnp.where(ok | (lane >= SPAN), 0.0, MASKED).astype(jnp.float32)
        mask = (mask[:, None, :] + above[None]).reshape(heads * BLK, LANES).astype(dtype)
        far_mask = jnp.where(pool_ok & (block < first), 0.0, MASKED).astype(jnp.float32)
        far_mask = jnp.broadcast_to(far_mask[:, None, :], (heads, BLK, LANES))
        far_mask = far_mask.reshape(heads * BLK, LANES).astype(dtype)
        far_q.append(jnp.concatenate([q, far_mask], axis=1))
        window = pl.ds(pl.multiple_of((here + 1) * BLK, BLK), SPAN * BLK)
        windows.append(window)
        keys = jnp.concatenate([kv_win[window, :HS], e_win[...]], axis=1)
        near.append(
            lax.dot_general(
                jnp.concatenate([q, mask], axis=1),
                keys,
                contract,
                preferred_element_type=jnp.float32,
            )
        )
    far = lax.dot_general(
        jnp.concatenate(far_q, axis=0),
        jnp.concatenate([kv_pool[:, :HS], e_pool[...]], axis=1),
        contract,
        preferred_element_type=jnp.float32,
    )
    far_values = with_ones(kv_pool[:, HS:])
    for u in range(quarter):
        far_u = far[u * heads * BLK : (u + 1) * heads * BLK]
        top = jnp.maximum(
            jnp.max(near[u], axis=1, keepdims=True), jnp.max(far_u, axis=1, keepdims=True)
        )
        probs = jnp.exp2((near[u] - top) * EXP_SCALE).astype(dtype)
        values = with_ones(kv_win[windows[u], HS:])
        summed = jnp.dot(probs, values, preferred_element_type=jnp.float32)
        probs = jnp.exp2((far_u - top) * EXP_SCALE).astype(dtype)
        summed = summed + jnp.dot(probs, far_values, preferred_element_type=jnp.float32)
        out = (summed[:, :HS] / summed[:, HS:]).astype(dtype)
        at = pl.ds(pl.multiple_of((step * quarter + u) * BLK, BLK), BLK)
        for h in range(heads):
            attended[at, h * HS : (h + 1) * HS] = out[h * BLK : (h + 1) * BLK]

    @pl.when(step == pl.num_programs(0) - 1)
    def _():
        outs[0][...] = attended[...]
        half = attended.shape[0] // 2
        for t in range(tiles):
            fetch(t).wait()
            product = jnp.dot(attended[...], weight[t], preferred_element_type=jnp.float32)
            product = product.astype(dtype)
            outs[1][:, t * TILE : (t + 1) * TILE] = product[:half]
            outs[2][:, t * TILE : (t + 1) * TILE] = product[half:]


def attend(flips, tp, ctx, queries, vertical, slash, near_kv, pairs, out_weight, tiles, after):
    width = queries.shape[1]
    rows = near_kv[0].shape[0]
    quarter = rows // 4
    steps = len(flips)
    slots = len(pairs) + 1
    dtype = queries.dtype
    far = slots * VMOST * BLK

    def place(g, tp, ctx):
        return (tp[0] ^ jnp.where(g == 0, flips[0], flips[1]), 0)

    def whole(shape):
        return pl.BlockSpec(shape, lambda g, tp, ctx: (0,) * len(shape))

    out_shapes = [(steps * quarter, width)]
    if tiles:
        out_shapes += [(steps * quarter // 2, tiles * TILE)] * 2
    return pl.pallas_call(
        functools.partial(attend_kernel, slots, tiles, flips),
        out_shape=[jax.ShapeDtypeStruct(shape, dtype) for shape in out_shapes],
        grid_spec=pltpu.PrefetchScalarGridSpec(
            num_scalar_prefetch=2,
            grid=(steps,),
            in_specs=[pl.BlockSpec((quarter, width), place)]
            + [whole(vertical.shape), whole(slash.shape)]
            + [anywhere() for _ in [*near_kv, *pairs, out_weight, *after]],
            out_specs=[whole(shape) for shape in out_shapes],
            scratch_shapes=[
                pltpu.VMEM((NEAR * rows, 2 * HS), dtype),
                pltpu.VMEM((SPAN * BLK, LANES), dtype),
                pltpu.VMEM((far, 2 * HS), dtype),
                pltpu.VMEM((far, LANES), dtype),
                pltpu.VMEM((vertical.shape[0], LANES), jnp.int32),
                pltpu.VMEM((steps * quarter, width), dtype),
                pltpu.VMEM((max(tiles, 1), out_weight.shape[0], TILE), dtype),
                pltpu.SemaphoreType.DMA((max(tiles, 1),)),
                pltpu.SemaphoreType.DMA((NEAR + len(pairs),)),
            ],
        ),
        compiler_params=params(60),
        cost_estimate=SHORT,
        name="attend",
    )(tp, ctx, queries, vertical, slash, *near_kv, *pairs, out_weight, *after)


def project_kernel(first, a_ref, w_hbm, *refs):
    weight, arrival = refs[-2:]
    tiles = weight.shape[0]
    pieces = tiles // PIECE
    outs = refs[-2 - 2 * pieces : -2]
    half = outs[0].shape[0]

    def fetch(t):
        return pltpu.make_async_copy(
            w_hbm.at[:, pl.ds((first + t) * TILE, TILE)], weight.at[t], arrival.at[t]
        )

    for t in range(tiles):
        fetch(t).start()
    for t in range(tiles):
        fetch(t).wait()
        product = jnp.dot(a_ref[...], weight[t], preferred_element_type=jnp.float32)
        product = product.astype(a_ref.dtype)
        at = slice(t % PIECE * TILE, (t % PIECE + 1) * TILE)
        outs[t // PIECE][:, at] = product[:half]
        outs[pieces + t // PIECE][:, at] = product[half:]


def project(attended, out_weight, first, tiles, after):
    rows, depth = attended.shape
    pieces = tiles // PIECE
    part = jax.ShapeDtypeStruct((rows // 2, PIECE * TILE), attended.dtype)
    outs = pl.pallas_call(
        functools.partial(project_kernel, first),
        out_shape=[part] * (2 * pieces),
        in_specs=[vmem(), anywhere()] + [anywhere() for _ in after],
        out_specs=[vmem()] * (2 * pieces),
        scratch_shapes=[
            pltpu.VMEM((tiles, depth, TILE), attended.dtype),
            pltpu.SemaphoreType.DMA((tiles,)),
        ],
        compiler_params=params(60),
        cost_estimate=SHORT,
        name="project",
    )(attended, out_weight, *after)
    return outs[:pieces], outs[pieces:]


def add_kernel(*refs):
    out_ref = refs[-1]
    tiles = len(refs) // 2
    for t in range(tiles):
        total = refs[t][...].astype(jnp.float32) + refs[tiles + t][...].astype(jnp.float32)
        out_ref[:, t * PIECE * TILE : (t + 1) * PIECE * TILE] = total.astype(out_ref.dtype)


def add(keep, got):
    rows = keep[0].shape[0]
    return pl.pallas_call(
        add_kernel,
        out_shape=jax.ShapeDtypeStruct((rows, len(keep) * PIECE * TILE), keep[0].dtype),
        in_specs=[vmem()] * (2 * len(keep)),
        out_specs=vmem(),
        compiler_params=params(60),
        cost_estimate=SHORT,
        name="add",
    )(*keep, *got)


def finish_kernel(pieces, *refs):
    arrived_ref, out_ref = refs[2 * pieces], refs[-1]
    step = pl.program_id(0)
    for t in range(pieces * PIECE):

        @pl.when(step == t)
        def _():
            part = slice(t % PIECE * TILE, (t % PIECE + 1) * TILE)
            total = refs[t // PIECE][:, part].astype(jnp.float32)
            total = total + refs[pieces + t // PIECE][:, part].astype(jnp.float32)
            total = total + arrived_ref[:, t * TILE : (t + 1) * TILE].astype(jnp.float32)
            out_ref[...] = total.astype(out_ref.dtype)


def finish(keep, got, arrived, first, width, out):
    rows = arrived.shape[0]
    before = [] if out is None else [out]
    return pl.pallas_call(
        functools.partial(finish_kernel, len(keep)),
        out_shape=jax.ShapeDtypeStruct((rows, width), arrived.dtype),
        grid=(len(keep) * PIECE,),
        in_specs=[vmem()] * (2 * len(keep) + 1) + [anywhere() for _ in before],
        out_specs=pl.BlockSpec((rows, TILE), lambda g: (0, first + g)),
        input_output_aliases={2 * len(keep) + 1: 0} if before else {},
        compiler_params=params(16),
        cost_estimate=SHORT,
        name="finish",
    )(*keep, *got, arrived, *before)


def shards(ctx_size, queries, keys, values, out_weight, vertical, slash):
    local_blocks = queries.shape[0] // BLK
    assert ctx_size % 2 == 0 and (NEAR - 1) * local_blocks >= SPAN - 1
    ctx = jnp.reshape(lax.axis_index("ctx"), (1,)).astype(jnp.int32)
    tp = jnp.reshape(lax.axis_index("tp"), (1,)).astype(jnp.int32)

    def shifted(x, by):
        return lax.ppermute(x, "ctx", [(r, r + by) for r in range(ctx_size - by)])

    own, pair = pick(ctx, vertical, keys, values)
    near_kv = [own, shifted(own, 1), shifted(own, 2)]
    pairs = [shifted(pair, s) for s in range(NEAR, ctx_size)]

    def sibling(x):
        return lax.ppermute(x, "tp", [(j, j ^ 1) for j in range(4)])

    def across(x):
        return lax.ppermute(x, "tp", [(j, j ^ 2) for j in range(4)])

    def attention(flips, tiles, after):
        return attend(
            flips, tp, ctx, queries, vertical, slash, near_kv, pairs, out_weight, tiles, after
        )

    width = out_weight.shape[1]
    tiles = width // TILE
    attended, send, keep = attention((3, 2), HEAD, ())
    total = keep.astype(jnp.float32) + sibling(send).astype(jnp.float32)
    total = total.astype(keep.dtype)
    arrived = [across(total)]
    send, keep = project(attended, out_weight, HEAD, tiles - HEAD, (total,))
    total = add(keep, [sibling(x) for x in send])
    arrived.append(across(total))
    (attended,) = attention((1, 0), 0, (total,))
    send, keep = project(attended, out_weight, 0, tiles, (arrived[0],))
    got = [sibling(x) for x in send]
    cut = HEAD // PIECE
    out = finish(keep[:cut], got[:cut], arrived[0], 0, width, None)
    return finish(keep[cut:], got[cut:], arrived[1], HEAD, width, out)


def solution(mesh):
    assert mesh.shape["tp"] == 4
    return jax.shard_map(
        functools.partial(shards, mesh.shape["ctx"]),
        mesh=mesh,
        in_specs=(
            P("ctx", "tp"),
            P("ctx", "tp"),
            P("ctx", "tp"),
            P("tp", None),
            P("tp", None),
            P("tp", None),
        ),
        out_specs=P(("ctx", "tp"), None),
        check_vma=False,
    )
```

time: 98.9 us -> 96 us (0.971)
  starting transfers between devices: 15.6 us -> 26.7 us
  Pallas kernels: 52.8 us -> 45.5 us
  waiting for transfers between devices: 21.6 us -> 15 us
    ppermute x3 -> x7, starting transfers between devices: 5.42 us -> 22.5 us  [shifted(): return lax.ppermute(x, 'ctx', [(r, r + by) for r in range(ctx_size - by)])]
    ppermute x3 -> x7, waiting for transfers between devices: 10.3 us -> 2.17 us  [shifted(): return lax.ppermute(x, 'ctx', [(r, r + by) for r in range(ctx_size - by)])]
    pallas_call x3 -> x2, Pallas kernels: 29 us -> 20.8 us  [attend(): pl.pallas_call(functools.partial(attend_kernel, slots, tiles, flips), out...]
    ppermute x4 -> x0, starting transfers between devices: 6.04 us -> none  [the longest x1 3.44 us: shards(): lax.ppermute(own, 'ctx', [(r, r + 1) for r in range(0, ctx_size, 2)])]
    ppermute x2, waiting for transfers between devices: 1.95 us -> 5.71 us  [across(): return lax.ppermute(x, 'tp', [(j, j ^ 2) for j in range(4)])]
    ppermute x4 -> x0, waiting for transfers between devices: 2.21 us -> none  [the longest x3 2.2 us: swapped(): return lax.ppermute(x, 'ctx', [(r, r ^ 1) for r in range(ctx_size)])]
  transfers between devices with their start and end apart: 16 -> 16, of which waited for: 9 -> 8; matrix products, arithmetic and copies ran while one was open for 0% -> 0% of each run, Pallas kernels for 35% -> 30%
where the time goes in v7:
time: 96 us; the launch traced here: 94.7 us
  Pallas kernels  45.5 us (47%)
  starting transfers between devices  26.7 us (28%)
  waiting for transfers between devices  15 us (16%)
  local copies, waits for them, and re-layouts  5.87 us (6%)
  other arithmetic  1.47 us (2%)
    ppermute x7, starting transfers between devices, shifted(): return lax.ppermute(x, 'ctx', [(r, r + by) for r in range(ctx_size - by)])  22.5 us
    pallas_call x2, Pallas kernels, attend(): pl.pallas_call(functools.partial(attend_kernel, slots, tiles, flips), out...  20.8 us
    pallas_call x2, Pallas kernels, project(): pl.pallas_call(functools.partial(project_kernel, first), out_shape=[part]...  16.4 us
    ppermute x7, waiting for transfers between devices, sibling(): return lax.ppermute(x, 'tp', [(j, j ^ 1) for j in range(4)])  7.07 us
    unnamed x32, local copies, waits for them, and re-layouts  5.87 us
    ppermute x2, waiting for transfers between devices, across(): return lax.ppermute(x, 'tp', [(j, j ^ 2) for j in range(4)])  5.71 us
    pallas_call x2, Pallas kernels, finish(): pl.pallas_call(functools.partial(finish_kernel, len(keep)), out_shape=jax...  3.47 us
    pallas_call x1, Pallas kernels, add(): pl.pallas_call(add_kernel, out_shape=jax.ShapeDtypeStruct((rows, len(keep...  2.73 us
  transfers between devices with their start and end apart: 16, of which 8 were waited for; matrix products, arithmetic and copies ran while one was open for 0% of the time, Pallas kernels for 30%

profile of v7, /device:TPU:16, one launch (start us, length us, event | category | flops | bytes accessed | tf_op | source)
XLA Modules:
  0.0 94.7 jit_solution(13943794020300015677)
XLA Ops:
  0.0 2.0 %pick.1 = (bf16[512,256]{1,0:T(8,128)(2,1)}, bf16[128,256]{1,0:T(8,128)(2,1)}) custom-call(s32[1]{0:T(128)} %bitcast.1.rank_ref.ctx_ref, s32[8,16]{1,0:T(8,128)} %vert_ref.5, bf16[512,128]{1,0:T(8,128)(2,1)} %k_ref.1, bf16[512,128]{1,0:T(8,128)(2,1)} %v_ref.1), custom_call_target="tpu_custom_call" | custom-call | tf_op jit(solution)/shard_map/pick/pallas_call | solution.py:63
  2.0 3.5 %collective-permute-start.1 = (bf16[512,256]{1,0:T(8,128)(2,1)}, bf16[512,256]{1,0:T(8,128)(2,1)S(1)}, u32[]{:S(2)}, u32[]{:S(2)}) collective-permute-start(bf16[512,256]{1,0:T(8,128)(2,1)} %get-tuple-element.22.own), channel_id=1, source_target_pairs={{0,8},{4,12},{8,16},{12,20},{16,24},{20,28},{1,9},{5,13},{9,17},{1... | collective-permute-start | bytes 786440 | tf_op jit(solution)/shard_map/ppermute | solution.py:367
  5.5 3.4 %collective-permute-start = (bf16[512,256]{1,0:T(8,128)(2,1)}, bf16[512,256]{1,0:T(8,128)(2,1)S(1)}, u32[]{:S(2)}, u32[]{:S(2)}) collective-permute-start(bf16[512,256]{1,0:T(8,128)(2,1)} %get-tuple-element.22.own), channel_id=1, source_target_pairs={{0,4},{4,8},{8,12},{12,16},{16,20},{20,24},{24,28},{1,5},{5,9},{9,... | collective-permute-start | bytes 786440 | tf_op jit(solution)/shard_map/ppermute | solution.py:367
  8.9 0.7 collective-permute-start.6
  9.6 0.7 collective-permute-start.5
  10.3 0.7 collective-permute-start.4
  10.9 0.0 collective-permute-done.6.refs_4_
  11.0 1.3 %collective-permute-start.3 = (bf16[128,256]{1,0:T(8,128)(2,1)}, bf16[128,256]{1,0:T(8,128)(2,1)S(1)}, u32[]{:S(2)}, u32[]{:S(2)}) collective-permute-start(bf16[128,256]{1,0:T(8,128)(2,1)} %get-tuple-element.23), channel_id=1, source_target_pairs={{0,16},{4,20},{8,24},{12,28},{1,17},{5,21},{9,25},{13,29},{2,18},{... | collective-permute-start | bytes 196616 | tf_op jit(solution)/shard_map/ppermute | solution.py:367
  12.3 0.0 collective-permute-done.5.refs_3_
  12.3 12.3 %collective-permute-start.2 = (bf16[128,256]{1,0:T(8,128)(2,1)}, bf16[128,256]{1,0:T(8,128)(2,1)S(1)}, u32[]{:S(2)}, u32[]{:S(2)}) collective-permute-start(bf16[128,256]{1,0:T(8,128)(2,1)} %get-tuple-element.23), channel_id=1, source_target_pairs={{0,12},{4,16},{8,20},{12,24},{16,28},{1,13},{5,17},{9,21},{13,25},... | collective-permute-start | bytes 196616 | tf_op jit(solution)/shard_map/ppermute | solution.py:367
  24.6 0.0 collective-permute-done.4.refs_2_
  24.7 2.2 %collective-permute-done.2.refs_0_ = bf16[128,256]{1,0:T(8,128)(2,1)S(1)} collective-permute-done((bf16[128,256]{1,0:T(8,128)(2,1)}, bf16[128,256]{1,0:T(8,128)(2,1)S(1)}, u32[]{:S(2)}, u32[]{:S(2)}) %collective-permute-start.2) | collective-permute-done | bytes 65568 | tf_op jit(solution)/shard_map/ppermute | solution.py:367
  26.8 0.0 collective-permute-done.1.kv_2
  26.9 0.6 copy-done.15
  27.5 0.1 copy-done.7
  27.6 0.1 copy-done.8
  27.6 13.1 %attend.2 = (bf16[256,1024]{1,0:T(8,128)(2,1)}, bf16[128,4096]{1,0:T(8,128)(2,1)}, bf16[128,4096]{1,0:T(8,128)(2,1)}) custom-call(s32[1]{0:T(128)} %bitcast.tp_ref, s32[1]{0:T(128)} %bitcast.1.rank_ref.ctx_ref, bf16[512,1024]{1,0:T(8,128)(2,1)} %q_ref.3, s32[8,16]{1,0:T(8,128)} %vert_ref.5, s32[8,8]{1,0:T(8,128)} %slash_ref.3, ...), custom_call_target="tpu_custom_call" | custom-call | tf_op jit(solution)/shard_map/attend/pallas_call | solution.py:238
  40.8 0.1 collective-permute-start.7
  40.9 2.9 %collective-permute-done.7 = bf16[128,4096]{1,0:T(8,128)(2,1)S(1)} collective-permute-done((bf16[128,4096]{1,0:T(8,128)(2,1)}, bf16[128,4096]{1,0:T(8,128)(2,1)S(1)}, u32[]{:S(2)}, u32[]{:S(2)}) %collective-permute-start.7) | collective-permute-done | bytes 1048608 | tf_op jit(solution)/shard_map/ppermute | solution.py:374
  43.7 1.5 %add_convert_fusion.refs_0_ = bf16[128,4096]{1,0:T(8,128)(2,1)S(1)} fusion(bf16[128,4096]{1,0:T(8,128)(2,1)S(1)} %collective-permute-done.7, bf16[128,4096]{1,0:T(8,128)(2,1)} %get-tuple-element.25), kind=kLoop, calls=%fused_computation | loop fusion | flops 2097152 | bytes 3145728 | tf_op jit(solution)/shard_map/convert_element_type | solution.py:388
  45.2 0.0 copy-start.6
  45.2 1.6 %collective-permute-start.10 = (bf16[128,4096]{1,0:T(8,128)(2,1)S(1)}, bf16[128,4096]{1,0:T(8,128)(2,1)S(1)}, u32[]{:S(2)}, u32[]{:S(2)}) collective-permute-start(bf16[128,4096]{1,0:T(8,128)(2,1)S(1)} %add_convert_fusion.refs_0_), channel_id=1, source_target_pairs={{0,2},{1,3},{2,0},{3,1},{4,6},{5,7},{6,4},{7,5},{8,10},{9,11},{10,... | collective-permute-start | bytes 3145736 | tf_op jit(solution)/shard_map/ppermute | solution.py:377
  46.8 6.7 %project.2 = (bf16[128,2048]{1,0:T(8,128)(2,1)}, bf16[128,2048]{1,0:T(8,128)(2,1)}, bf16[128,2048]{1,0:T(8,128)(2,1)}, bf16[128,2048]{1,0:T(8,128)(2,1)}) custom-call(bf16[256,1024]{1,0:T(8,128)(2,1)} %get-tuple-element.24.a_ref, bf16[1024,8192]{1,0:T(8,128)(2,1)} %w_hbm.3, bf16[128,4096]{1,0:T(8,128)(2,1)} %copy-done.6), custom_call_target="tpu_custom_call" | custom-call | tf_op jit(solution)/shard_map/project/pallas_call | solution.py:293
  53.5 0.1 collective-permute-start.8
  53.5 0.5 collective-permute-start.9
  54.0 1.6 %collective-permute-done.8.refs_2_ = bf16[128,2048]{1,0:T(8,128)(2,1)S(1)} collective-permute-done((bf16[128,2048]{1,0:T(8,128)(2,1)}, bf16[128,2048]{1,0:T(8,128)(2,1)S(1)}, u32[]{:S(2)}, u32[]{:S(2)}) %collective-permute-start.8) | collective-permute-done | bytes 524320 | tf_op jit(solution)/shard_map/ppermute | solution.py:374
  55.7 0.7 collective-permute-done.9.refs_3_
  56.4 0.0 copy-done.9
  56.4 0.8 copy-done.10
  57.2 2.7 %add.6.refs_6_ = bf16[128,4096]{1,0:T(8,128)(2,1)} custom-call(bf16[128,2048]{1,0:T(8,128)(2,1)} %get-tuple-element.27.refs_0_, bf16[128,2048]{1,0:T(8,128)(2,1)} %get-tuple-element.28.refs_1_, bf16[128,2048]{1,0:T(8,128)(2,1)} %copy-done.9, bf16[128,2048]{1,0:T(8,128)(2,1)} %copy-done.10), custom_call_target="tpu_custom_call" | custom-call | tf_op jit(solution)/shard_map/add/pallas_call | solution.py:319
  60.0 0.9 collective-permute-start.13
  60.8 7.7 %attend.3.a_ref = bf16[256,1024]{1,0:T(8,128)(2,1)} custom-call(s32[1]{0:T(128)} %bitcast.tp_ref, s32[1]{0:T(128)} %bitcast.1.rank_ref.ctx_ref, bf16[512,1024]{1,0:T(8,128)(2,1)} %q_ref.3, s32[8,16]{1,0:T(8,128)} %vert_ref.5, s32[8,8]{1,0:T(8,128)} %slash_ref.3, bf16[512,256]{1,0:T(8,128)(2,1)} %get-tuple-element.22.own, bf16[512,256]{1,0:T(8,128)(2,1)} %copy-done.8, ...), custom_call_target="tpu_custom_call" | custom-call | tf_op jit(solution)/shard_map/attend/pallas_call | solution.py:238
  68.5 2.8 %collective-permute-done.10.refs_0_.refs_4_ = bf16[128,4096]{1,0:T(8,128)(2,1)S(1)} collective-permute-done((bf16[128,4096]{1,0:T(8,128)(2,1)S(1)}, bf16[128,4096]{1,0:T(8,128)(2,1)S(1)}, u32[]{:S(2)}, u32[]{:S(2)}) %collective-permute-start.10) | collective-permute-done | bytes 1048608 | tf_op jit(solution)/shard_map/ppermute | solution.py:377
  71.3 1.0 %copy-done = bf16[128,4096]{1,0:T(8,128)(2,1)} copy-done((bf16[128,4096]{1,0:T(8,128)(2,1)}, bf16[128,4096]{1,0:T(8,128)(2,1)S(1)}, u32[]{:S(2)}) %copy-start) | copy-done | bytes 1048600
  72.3 9.7 %project.3 = (bf16[128,2048]{1,0:T(8,128)(2,1)}, bf16[128,2048]{1,0:T(8,128)(2,1)}, bf16[128,2048]{1,0:T(8,128)(2,1)}, bf16[128,2048]{1,0:T(8,128)(2,1)}, bf16[1...) custom-call(bf16[256,1024]{1,0:T(8,128)(2,1)} %attend.3.a_ref, ...), custom_call_target="tpu_custom_call" | custom-call | tf_op jit(solution)/shard_map/project/pallas_call | solution.py:293
  82.0 0.1 collective-permute-start.14
  82.1 0.5 collective-permute-start.15
  82.6 0.1 collective-permute-start.11
  82.7 0.4 collective-permute-start.12
  83.1 1.1 %collective-permute-done.14.refs_2_ = bf16[128,2048]{1,0:T(8,128)(2,1)S(1)} collective-permute-done((bf16[128,2048]{1,0:T(8,128)(2,1)}, bf16[128,2048]{1,0:T(8,128)(2,1)S(1)}, u32[]{:S(2)}, u32[]{:S(2)}) %collective-permute-start.14) | collective-permute-done | bytes 524320 | tf_op jit(solution)/shard_map/ppermute | solution.py:374
  84.2 0.7 collective-permute-done.15.refs_3_
  85.0 1.2 %copy-done.1 = bf16[128,4096]{1,0:T(8,128)(2,1)S(1)} copy-done((bf16[128,4096]{1,0:T(8,128)(2,1)S(1)}, bf16[128,4096]{1,0:T(8,128)(2,1)}, u32[]{:S(2)}) %copy-start.1) | copy-done | bytes 1048600
  86.2 1.0 %copy-done.4 = bf16[128,2048]{1,0:T(8,128)(2,1)S(1)} copy-done((bf16[128,2048]{1,0:T(8,128)(2,1)S(1)}, bf16[128,2048]{1,0:T(8,128)(2,1)}, u32[]{:S(2)}) %copy-start.4) | copy-done | bytes 524312
  87.2 1.0 %copy-done.5 = bf16[128,2048]{1,0:T(8,128)(2,1)S(1)} copy-done((bf16[128,2048]{1,0:T(8,128)(2,1)S(1)}, bf16[128,2048]{1,0:T(8,128)(2,1)}, u32[]{:S(2)}) %copy-start.5) | copy-done | bytes 524312
  88.3 1.7 %finish.2.refs_5_ = bf16[128,8192]{1,0:T(8,128)(2,1)} custom-call(bf16[128,2048]{1,0:T(8,128)(2,1)S(1)} %copy-done.4, bf16[128,2048]{1,0:T(8,128)(2,1)S(1)} %copy-done.5, bf16[128,2048]{1,0:T(8,128)(2,1)S(1)} %collective-permute-done.14.refs_2_, bf16[128,2048]{1,0:T(8,128)(2,1)S(1)} %collective-permute-done.15.refs_3_, bf16[128,4096]{1,0:T(8,128)(2,1)S(1)} %copy-done.1), custom_call_target="tpu_custom_call" | custom-call | tf_op jit(solution)/shard_map/finish/pallas_call | solution.py:347
  90.0 0.0 collective-permute-done.12.refs_3_
  90.0 3.0 %collective-permute-done.13.refs_4_ = bf16[128,4096]{1,0:T(8,128)(2,1)S(1)} collective-permute-done((bf16[128,4096]{1,0:T(8,128)(2,1)}, bf16[128,4096]{1,0:T(8,128)(2,1)S(1)}, u32[]{:S(2)}, u32[]{:S(2)}) %collective-permute-start.13) | collective-permute-done | bytes 1048608 | tf_op jit(solution)/shard_map/ppermute | solution.py:377
  93.0 1.7 %finish.3 = bf16[128,8192]{1,0:T(8,128)(2,1)} custom-call(bf16[128,2048]{1,0:T(8,128)(2,1)S(1)} %copy-done.2, bf16[128,2048]{1,0:T(8,128)(2,1)S(1)} %copy-done.3, bf16[128,2048]{1,0:T(8,128)(2,1)S(1)} %collective-permute-done.11.refs_2_, bf16[128,2048]{1,0:T(8,128)(2,1)S(1)} %collective-permute-done.12.refs_3_, ...), custom_call_target="tpu_custom_call", output_to_operand_aliasing={{}: (5, {})} | custom-call | tf_op jit(solution)/shard_map/finish/pallas_call | solution.py:347
  (25 shorter events, 0.0 us)
Async XLA Ops:
  2.0 24.8 %collective-permute-start.1 = (bf16[512,256]{1,0:T(8,128)(2,1)}, bf16[512,256]{1,0:T(8,128)(2,1)S(1)}, u32[]{:S(2)}, u32[]{:S(2)}) collective-permute-start(bf16[512,256]{1,0:T(8,128)(2,1)} %get-tuple-element.22.own), channel_id=1, source_target_pairs={{0,8},{4,12},{8,16},{12,20},{16,24},{20,28},{1,9},{5,13},{9,17},{1... | collective-permute-start | bytes 786440 | tf_op jit(solution)/shard_map/ppermute | solution.py:367
  5.5 21.4 %collective-permute-start = (bf16[512,256]{1,0:T(8,128)(2,1)}, bf16[512,256]{1,0:T(8,128)(2,1)S(1)}, u32[]{:S(2)}, u32[]{:S(2)}) collective-permute-start(bf16[512,256]{1,0:T(8,128)(2,1)} %get-tuple-element.22.own), channel_id=1, source_target_pairs={{0,4},{4,8},{8,12},{12,16},{16,20},{20,24},{24,28},{1,5},{5,9},{9,... | collective-permute-start | bytes 786440 | tf_op jit(solution)/shard_map/ppermute | solution.py:367
  8.9 2.0 %collective-permute-start.6 = (bf16[128,256]{1,0:T(8,128)(2,1)}, bf16[128,256]{1,0:T(8,128)(2,1)S(1)}, u32[]{:S(2)}, u32[]{:S(2)}) collective-permute-start(bf16[128,256]{1,0:T(8,128)(2,1)} %get-tuple-element.23), channel_id=1, source_target_pairs={{0,28},{1,29},{2,30},{3,31}} | collective-permute-start | bytes 196616 | tf_op jit(solution)/shard_map/ppermute | solution.py:367
  9.6 2.7 %collective-permute-start.5 = (bf16[128,256]{1,0:T(8,128)(2,1)}, bf16[128,256]{1,0:T(8,128)(2,1)S(1)}, u32[]{:S(2)}, u32[]{:S(2)}) collective-permute-start(bf16[128,256]{1,0:T(8,128)(2,1)} %get-tuple-element.23), channel_id=1, source_target_pairs={{0,24},{4,28},{1,25},{5,29},{2,26},{6,30},{3,27},{7,31}} | collective-permute-start | bytes 196616 | tf_op jit(solution)/shard_map/ppermute | solution.py:367
  10.3 14.4 %collective-permute-start.4 = (bf16[128,256]{1,0:T(8,128)(2,1)}, bf16[128,256]{1,0:T(8,128)(2,1)S(1)}, u32[]{:S(2)}, u32[]{:S(2)}) collective-permute-start(bf16[128,256]{1,0:T(8,128)(2,1)} %get-tuple-element.23), channel_id=1, source_target_pairs={{0,20},{4,24},{8,28},{1,21},{5,25},{9,29},{2,22},{6,26},{10,30},{3... | collective-permute-start | bytes 196616 | tf_op jit(solution)/shard_map/ppermute | solution.py:367
  11.0 15.9 %copy-start.11 = (bf16[128,256]{1,0:T(8,128)(2,1)}, bf16[128,256]{1,0:T(8,128)(2,1)S(1)}, u32[]{:S(2)}) copy-start(bf16[128,256]{1,0:T(8,128)(2,1)S(1)} %collective-permute-done.6.refs_4_) | copy-start | bytes 196612
  11.0 13.7 %collective-permute-start.3 = (bf16[128,256]{1,0:T(8,128)(2,1)}, bf16[128,256]{1,0:T(8,128)(2,1)S(1)}, u32[]{:S(2)}, u32[]{:S(2)}) collective-permute-start(bf16[128,256]{1,0:T(8,128)(2,1)} %get-tuple-element.23), channel_id=1, source_target_pairs={{0,16},{4,20},{8,24},{12,28},{1,17},{5,21},{9,25},{13,29},{2,18},{... | collective-permute-start | bytes 196616 | tf_op jit(solution)/shard_map/ppermute | solution.py:367
  12.3 14.6 %copy-start.12 = (bf16[128,256]{1,0:T(8,128)(2,1)}, bf16[128,256]{1,0:T(8,128)(2,1)S(1)}, u32[]{:S(2)}) copy-start(bf16[128,256]{1,0:T(8,128)(2,1)S(1)} %collective-permute-done.5.refs_3_) | copy-start | bytes 196612
  12.3 14.5 %collective-permute-start.2 = (bf16[128,256]{1,0:T(8,128)(2,1)}, bf16[128,256]{1,0:T(8,128)(2,1)S(1)}, u32[]{:S(2)}, u32[]{:S(2)}) collective-permute-start(bf16[128,256]{1,0:T(8,128)(2,1)} %get-tuple-element.23), channel_id=1, source_target_pairs={{0,12},{4,16},{8,20},{12,24},{16,28},{1,13},{5,17},{9,21},{13,25},... | collective-permute-start | bytes 196616 | tf_op jit(solution)/shard_map/ppermute | solution.py:367
  24.6 2.2 %copy-start.13 = (bf16[128,256]{1,0:T(8,128)(2,1)}, bf16[128,256]{1,0:T(8,128)(2,1)S(1)}, u32[]{:S(2)}) copy-start(bf16[128,256]{1,0:T(8,128)(2,1)S(1)} %collective-permute-done.4.refs_2_) | copy-start | bytes 196612
  24.7 2.2 %copy-start.14 = (bf16[128,256]{1,0:T(8,128)(2,1)}, bf16[128,256]{1,0:T(8,128)(2,1)S(1)}, u32[]{:S(2)}) copy-start(bf16[128,256]{1,0:T(8,128)(2,1)S(1)} %collective-permute-done.3.refs_1_) | copy-start | bytes 196612
  26.8 0.6 copy-start.15
  26.8 0.7 copy-start.7
  26.8 0.8 copy-start.8
  40.8 2.9 %collective-permute-start.7 = (bf16[128,4096]{1,0:T(8,128)(2,1)}, bf16[128,4096]{1,0:T(8,128)(2,1)S(1)}, u32[]{:S(2)}, u32[]{:S(2)}) collective-permute-start(bf16[128,4096]{1,0:T(8,128)(2,1)} %get-tuple-element.26), channel_id=1, source_target_pairs={{0,1},{1,0},{2,3},{3,2},{4,5},{5,4},{6,7},{7,6},{8,9},{9,8},{10,11... | collective-permute-start | bytes 3145736 | tf_op jit(solution)/shard_map/ppermute | solution.py:374
  45.2 1.6 %copy-start.6 = (bf16[128,4096]{1,0:T(8,128)(2,1)}, bf16[128,4096]{1,0:T(8,128)(2,1)S(1)}, u32[]{:S(2)}) copy-start(bf16[128,4096]{1,0:T(8,128)(2,1)S(1)} %add_convert_fusion.refs_0_) | copy-start | bytes 3145732
  45.2 26.1 %collective-permute-start.10 = (bf16[128,4096]{1,0:T(8,128)(2,1)S(1)}, bf16[128,4096]{1,0:T(8,128)(2,1)S(1)}, u32[]{:S(2)}, u32[]{:S(2)}) collective-permute-start(bf16[128,4096]{1,0:T(8,128)(2,1)S(1)} %add_convert_fusion.refs_0_), channel_id=1, source_target_pairs={{0,2},{1,3},{2,0},{3,1},{4,6},{5,7},{6,4},{7,5},{8,10},{9,11},{10,... | collective-permute-start | bytes 3145736 | tf_op jit(solution)/shard_map/ppermute | solution.py:377
  53.5 2.2 %collective-permute-start.8 = (bf16[128,2048]{1,0:T(8,128)(2,1)}, bf16[128,2048]{1,0:T(8,128)(2,1)S(1)}, u32[]{:S(2)}, u32[]{:S(2)}) collective-permute-start(bf16[128,2048]{1,0:T(8,128)(2,1)} %get-tuple-element.29), channel_id=1, source_target_pairs={{0,1},{1,0},{2,3},{3,2},{4,5},{5,4},{6,7},{7,6},{8,9},{9,8},{10,11... | collective-permute-start | bytes 1572872 | tf_op jit(solution)/shard_map/ppermute | solution.py:374
  53.5 2.9 %collective-permute-start.9 = (bf16[128,2048]{1,0:T(8,128)(2,1)}, bf16[128,2048]{1,0:T(8,128)(2,1)S(1)}, u32[]{:S(2)}, u32[]{:S(2)}) collective-permute-start(bf16[128,2048]{1,0:T(8,128)(2,1)} %get-tuple-element.30), channel_id=1, source_target_pairs={{0,1},{1,0},{2,3},{3,2},{4,5},{5,4},{6,7},{7,6},{8,9},{9,8},{10,11... | collective-permute-start | bytes 1572872 | tf_op jit(solution)/shard_map/ppermute | solution.py:374
  55.7 0.8 copy-start.9
  56.4 0.8 copy-start.10
  60.0 33.0 %collective-permute-start.13 = (bf16[128,4096]{1,0:T(8,128)(2,1)}, bf16[128,4096]{1,0:T(8,128)(2,1)S(1)}, u32[]{:S(2)}, u32[]{:S(2)}) collective-permute-start(bf16[128,4096]{1,0:T(8,128)(2,1)} %add.6.refs_6_), channel_id=1, source_target_pairs={{0,2},{1,3},{2,0},{3,1},{4,6},{5,7},{6,4},{7,5},{8,10},{9,11},{10,... | collective-permute-start | bytes 3145736 | tf_op jit(solution)/shard_map/ppermute | solution.py:377
  71.3 1.0 %copy-start = (bf16[128,4096]{1,0:T(8,128)(2,1)}, bf16[128,4096]{1,0:T(8,128)(2,1)S(1)}, u32[]{:S(2)}) copy-start(bf16[128,4096]{1,0:T(8,128)(2,1)S(1)} %collective-permute-done.10.refs_0_.refs_4_) | copy-start | bytes 3145732
  82.0 2.2 %collective-permute-start.14 = (bf16[128,2048]{1,0:T(8,128)(2,1)}, bf16[128,2048]{1,0:T(8,128)(2,1)S(1)}, u32[]{:S(2)}, u32[]{:S(2)}) collective-permute-start(bf16[128,2048]{1,0:T(8,128)(2,1)} %get-tuple-element.37), channel_id=1, source_target_pairs={{0,1},{1,0},{2,3},{3,2},{4,5},{5,4},{6,7},{7,6},{8,9},{9,8},{10,11... | collective-permute-start | bytes 1572872 | tf_op jit(solution)/shard_map/ppermute | solution.py:374
  82.1 2.9 %collective-permute-start.15 = (bf16[128,2048]{1,0:T(8,128)(2,1)}, bf16[128,2048]{1,0:T(8,128)(2,1)S(1)}, u32[]{:S(2)}, u32[]{:S(2)}) collective-permute-start(bf16[128,2048]{1,0:T(8,128)(2,1)} %get-tuple-element.38), channel_id=1, source_target_pairs={{0,1},{1,0},{2,3},{3,2},{4,5},{5,4},{6,7},{7,6},{8,9},{9,8},{10,11... | collective-permute-start | bytes 1572872 | tf_op jit(solution)/shard_map/ppermute | solution.py:374
  82.6 7.4 %collective-permute-start.11 = (bf16[128,2048]{1,0:T(8,128)(2,1)}, bf16[128,2048]{1,0:T(8,128)(2,1)S(1)}, u32[]{:S(2)}, u32[]{:S(2)}) collective-permute-start(bf16[128,2048]{1,0:T(8,128)(2,1)} %get-tuple-element.33), channel_id=1, source_target_pairs={{0,1},{1,0},{2,3},{3,2},{4,5},{5,4},{6,7},{7,6},{8,9},{9,8},{10,11... | collective-permute-start | bytes 1572872 | tf_op jit(solution)/shard_map/ppermute | solution.py:374
  82.7 7.3 %collective-permute-start.12 = (bf16[128,2048]{1,0:T(8,128)(2,1)}, bf16[128,2048]{1,0:T(8,128)(2,1)S(1)}, u32[]{:S(2)}, u32[]{:S(2)}) collective-permute-start(bf16[128,2048]{1,0:T(8,128)(2,1)} %get-tuple-element.34), channel_id=1, source_target_pairs={{0,1},{1,0},{2,3},{3,2},{4,5},{5,4},{6,7},{7,6},{8,9},{9,8},{10,11... | collective-permute-start | bytes 1572872 | tf_op jit(solution)/shard_map/ppermute | solution.py:374
  85.0 1.2 %copy-start.1 = (bf16[128,4096]{1,0:T(8,128)(2,1)S(1)}, bf16[128,4096]{1,0:T(8,128)(2,1)}, u32[]{:S(2)}) copy-start(bf16[128,4096]{1,0:T(8,128)(2,1)} %copy-done) | copy-start | bytes 3145732
  86.2 1.0 %copy-start.4 = (bf16[128,2048]{1,0:T(8,128)(2,1)S(1)}, bf16[128,2048]{1,0:T(8,128)(2,1)}, u32[]{:S(2)}) copy-start(bf16[128,2048]{1,0:T(8,128)(2,1)} %get-tuple-element.35.refs_0_) | copy-start | bytes 1572868
  87.2 1.0 %copy-start.5 = (bf16[128,2048]{1,0:T(8,128)(2,1)S(1)}, bf16[128,2048]{1,0:T(8,128)(2,1)}, u32[]{:S(2)}) copy-start(bf16[128,2048]{1,0:T(8,128)(2,1)} %get-tuple-element.36.refs_1_) | copy-start | bytes 1572868
  88.3 4.7 %copy-start.2 = (bf16[128,2048]{1,0:T(8,128)(2,1)S(1)}, bf16[128,2048]{1,0:T(8,128)(2,1)}, u32[]{:S(2)}) copy-start(bf16[128,2048]{1,0:T(8,128)(2,1)} %get-tuple-element.31.refs_0_) | copy-start | bytes 1572868
  88.3 4.7 %copy-start.3 = (bf16[128,2048]{1,0:T(8,128)(2,1)S(1)}, bf16[128,2048]{1,0:T(8,128)(2,1)}, u32[]{:S(2)}) copy-start(bf16[128,2048]{1,0:T(8,128)(2,1)} %get-tuple-element.32.refs_1_) | copy-start | bytes 1572868

commit v8 on v7

--- a/solution.py
+++ b/solution.py
@@ -56,15 +56,17 @@
     both_ref[:, HS:] = v_ref[...]
     blocks = picked_blocks(vert_ref[...], rank_ref[0], k_ref.shape[0] // BLK)
     for slot, rows in enumerate(blocks):
-        pair_ref[slot * BLK : (slot + 1) * BLK, :] = both_ref[rows, :]
-
-
-def pick(rank, vertical, keys, values):
+        picked = both_ref[rows, :]
+        for copy in range(pair_ref.shape[0]):
+            pair_ref[copy, slot * BLK : (slot + 1) * BLK, :] = picked
+
+
+def pick(rank, vertical, keys, values, copies):
     return pl.pallas_call(
         pick_kernel,
         out_shape=(
             jax.ShapeDtypeStruct((keys.shape[0], 2 * HS), keys.dtype),
-            jax.ShapeDtypeStruct((VMOST * BLK, 2 * HS), keys.dtype),
+            jax.ShapeDtypeStruct((copies, VMOST * BLK, 2 * HS), keys.dtype),
         ),
         in_specs=[smem(), vmem(), vmem(), vmem()],
         out_specs=(vmem(), vmem()),
@@ -82,7 +84,9 @@
 
 def pool_blocks(vertical, rank, slots, local_blocks):
     lane = lax.broadcasted_iota(jnp.int32, (vertical.shape[0], LANES), 1)
-    shard = jnp.where(lane // VMOST < slots, rank - (NEAR - 1) - lane // VMOST, -1)
+    slot = lane // VMOST
+    shard = jnp.where(slot < slots, 2 * slot + (rank & 1), 2 * (slot - slots) + 1 - (rank & 1))
+    shard = jnp.where(slot < 2 * slots, shard, -1)
     first = jnp.full((1, LANES), local_blocks, jnp.int32)
     second = first
     for j in reversed(range(local_blocks)):
@@ -97,8 +101,8 @@
 def attend_kernel(
     slots, tiles, flips, tp_ref, ctx_ref, q_ref, vert_ref, slash_ref, own, kv_1, kv_2, *refs
 ):
-    pairs = refs[: slots - 1]
-    w_hbm = refs[slots - 1]
+    pairs = refs[:2]
+    w_hbm = refs[2]
     kv_win, e_win, kv_pool, e_pool, blocks_ref, attended, weight, arrival, landed = refs[-9:]
     outs = refs[-12:-9] if tiles else refs[-10:-9]
     step = pl.program_id(0)
@@ -123,9 +127,12 @@
         ]
         copies += [
             pltpu.make_async_copy(
-                x, kv_pool.at[pl.ds((s + 1) * pair_rows, pair_rows), :], landed.at[NEAR + s]
+                x.at[s],
+                kv_pool.at[pl.ds((p * slots + s) * pair_rows, pair_rows), :],
+                landed.at[NEAR + p * slots + s],
             )
-            for s, x in enumerate(pairs)
+            for p, x in enumerate(pairs)
+            for s in range(slots)
         ]
         for copy in copies:
             copy.start()
@@ -139,11 +146,8 @@
         lane = lax.broadcasted_iota(jnp.int32, e_pool.shape, 1)
         e_pool[...] = jnp.where(key // BLK == lane, 1.0, 0.0).astype(dtype)
         blocks_ref[...] = pool_blocks(vert_ref[...], rank, slots, local_blocks)
-        picked = picked_blocks(vert_ref[...], rank - (NEAR - 1), local_blocks)
         for copy in copies:
             copy.wait()
-        for slot, block in enumerate(picked):
-            kv_pool[slot * BLK : (slot + 1) * BLK, :] = kv_win[block, :]
 
     owner = tp_ref[0] ^ jnp.where(step == 0, flips[0], flips[1])
     lane = lax.broadcasted_iota(jnp.int32, (heads, LANES), 1)
@@ -222,9 +226,9 @@
     rows = near_kv[0].shape[0]
     quarter = rows // 4
     steps = len(flips)
-    slots = len(pairs) + 1
+    slots = pairs[0].shape[0] - 1
     dtype = queries.dtype
-    far = slots * VMOST * BLK
+    far = 2 * slots * VMOST * BLK
 
     def place(g, tp, ctx):
         return (tp[0] ^ jnp.where(g == 0, flips[0], flips[1]), 0)
@@ -254,10 +258,10 @@
                 pltpu.VMEM((steps * quarter, width), dtype),
                 pltpu.VMEM((max(tiles, 1), out_weight.shape[0], TILE), dtype),
                 pltpu.SemaphoreType.DMA((max(tiles, 1),)),
-                pltpu.SemaphoreType.DMA((NEAR + len(pairs),)),
+                pltpu.SemaphoreType.DMA((NEAR + 2 * slots,)),
             ],
         ),
-        compiler_params=params(60),
+        compiler_params=params(50),
         cost_estimate=SHORT,
         name="attend",
     )(tp, ctx, queries, vertical, slash, *near_kv, *pairs, out_weight, *after)
@@ -299,32 +303,16 @@
             pltpu.VMEM((tiles, depth, TILE), attended.dtype),
             pltpu.SemaphoreType.DMA((tiles,)),
         ],
-        compiler_params=params(60),
+        compiler_params=params(50),
         cost_estimate=SHORT,
         name="project",
     )(attended, out_weight, *after)
     return outs[:pieces], outs[pieces:]
 
 
-def add_kernel(*refs):
-    out_ref = refs[-1]
-    tiles = len(refs) // 2
-    for t in range(tiles):
-        total = refs[t][...].astype(jnp.float32) + refs[tiles + t][...].astype(jnp.float32)
-        out_ref[:, t * PIECE * TILE : (t + 1) * PIECE * TILE] = total.astype(out_ref.dtype)
-
-
 def add(keep, got):
-    rows = keep[0].shape[0]
-    return pl.pallas_call(
-        add_kernel,
-        out_shape=jax.ShapeDtypeStruct((rows, len(keep) * PIECE * TILE), keep[0].dtype),
-        in_specs=[vmem()] * (2 * len(keep)),
-        out_specs=vmem(),
-        compiler_params=params(60),
-        cost_estimate=SHORT,
-        name="add",
-    )(*keep, *got)
+    sums = [k.astype(jnp.float32) + g.astype(jnp.float32) for k, g in zip(keep, got)]
+    return jnp.concatenate([x.astype(keep[0].dtype) for x in sums], axis=1)
 
 
 def finish_kernel(pieces, *refs):
@@ -366,9 +354,11 @@
     def shifted(x, by):
         return lax.ppermute(x, "ctx", [(r, r + by) for r in range(ctx_size - by)])
 
-    own, pair = pick(ctx, vertical, keys, values)
+    own, pair = pick(ctx, vertical, keys, values, ctx_size // 2)
     near_kv = [own, shifted(own, 1), shifted(own, 2)]
-    pairs = [shifted(pair, s) for s in range(NEAR, ctx_size)]
+    parities = [list(range(odd, ctx_size, 2)) for odd in (0, 1)]
+    pairs = [lax.all_to_all(pair, "ctx", 0, 0, axis_index_groups=parities, tiled=True)]
+    pairs.append(lax.ppermute(pairs[0], "ctx", [(r, r ^ 1) for r in range(ctx_size)]))
 
     def sibling(x):
         return lax.ppermute(x, "tp", [(j, j ^ 1) for j in range(4)])
@@ -384,8 +374,7 @@
     width = out_weight.shape[1]
     tiles = width // TILE
     attended, send, keep = attention((3, 2), HEAD, ())
-    total = keep.astype(jnp.float32) + sibling(send).astype(jnp.float32)
-    total = total.astype(keep.dtype)
+    total = add([keep], [sibling(send)])
     arrived = [across(total)]
     send, keep = project(attended, out_weight, HEAD, tiles - HEAD, (total,))
     total = add(keep, [sibling(x) for x in send])

time: 96 us -> 96.5 us (level)
  waiting for transfers between devices: 15 us -> 38.1 us
  Pallas kernels: 45.5 us -> 34.5 us
  starting transfers between devices: 26.7 us -> 17.3 us
    ppermute x7 -> x2, starting transfers between devices: 22.5 us -> 6.79 us  [shifted(): return lax.ppermute(x, 'ctx', [(r, r + by) for r in range(ctx_size - by)])]
    ppermute x2, waiting for transfers between devices: 5.71 us -> 21.3 us  [across(): return lax.ppermute(x, 'tp', [(j, j ^ 2) for j in range(4)])]
    ppermute x7 -> x2, waiting for transfers between devices: 2.17 us -> 11.4 us  [shifted(): return lax.ppermute(x, 'ctx', [(r, r + by) for r in range(ctx_size - by)])]
    pallas_call x2, Pallas kernels: 20.8 us -> 15.2 us  [attend(): pl.pallas_call(functools.partial(attend_kernel, slots, tiles, flips), out...]
    all_to_all x0 -> x1, starting transfers between devices: none -> 5.2 us  [shards(): lax.all_to_all(pair, 'ctx', 0, 0, axis_index_groups=parities, tiled=True)]
    pallas_call x1 -> x0, Pallas kernels: 2.73 us -> none  [add(): pl.pallas_call(add_kernel, out_shape=jax.ShapeDtypeStruct((rows, len(keep...]
    pallas_call x2, Pallas kernels: 16.4 us -> 13.7 us  [project(): pl.pallas_call(functools.partial(project_kernel, first), out_shape=[part]...]
    ppermute x7, waiting for transfers between devices: 7.07 us -> 4.78 us  [sibling(): return lax.ppermute(x, 'tp', [(j, j ^ 1) for j in range(4)])]
  transfers between devices with their start and end apart: 16 -> 13, of which waited for: 8 -> 9; matrix products, arithmetic and copies ran while one was open for 0% -> 0% of each run, Pallas kernels for 30% -> 17%
where the time goes in v8:
time: 96.5 us; the launch traced here: 96 us
  waiting for transfers between devices  38.1 us (39%)
  Pallas kernels  34.5 us (36%)
  starting transfers between devices  17.3 us (18%)
  local copies, waits for them, and re-layouts  5.34 us (6%)
    ppermute x2, waiting for transfers between devices, across(): return lax.ppermute(x, 'tp', [(j, j ^ 2) for j in range(4)])  21.3 us
    pallas_call x2, Pallas kernels, attend(): pl.pallas_call(functools.partial(attend_kernel, slots, tiles, flips), out...  15.2 us
    pallas_call x2, Pallas kernels, project(): pl.pallas_call(functools.partial(project_kernel, first), out_shape=[part]...  13.7 us
    ppermute x2, waiting for transfers between devices, shifted(): return lax.ppermute(x, 'ctx', [(r, r + by) for r in range(ctx_size - by)])  11.4 us
    ppermute x2, starting transfers between devices, shifted(): return lax.ppermute(x, 'ctx', [(r, r + by) for r in range(ctx_size - by)])  6.79 us
    unnamed x20, local copies, waits for them, and re-layouts  5.34 us
    all_to_all x1, starting transfers between devices, shards(): lax.all_to_all(pair, 'ctx', 0, 0, axis_index_groups=parities, tiled=True)  5.2 us
    ppermute x7, waiting for transfers between devices, sibling(): return lax.ppermute(x, 'tp', [(j, j ^ 1) for j in range(4)])  4.78 us
  transfers between devices with their start and end apart: 13, of which 9 were waited for; matrix products, arithmetic and copies ran while one was open for 0% of the time, Pallas kernels for 17%

profile of v8, /device:TPU:16, one launch (start us, length us, event | category | flops | bytes accessed | tf_op | source)
XLA Modules:
  0.0 96.0 jit_solution(12729843676351312146)
XLA Ops:
  0.0 2.1 %pick.1 = (bf16[512,256]{1,0:T(8,128)(2,1)}, bf16[4,128,256]{2,1,0:T(8,128)(2,1)}) custom-call(s32[1]{0:T(128)} %bitcast.1.rank_ref.ctx_ref, s32[8,16]{1,0:T(8,128)} %vert_ref.5, bf16[512,128]{1,0:T(8,128)(2,1)} %k_ref.1, bf16[512,128]{1,0:T(8,128)(2,1)} %v_ref.1), custom_call_target="tpu_custom_call" | custom-call | tf_op jit(solution)/shard_map/pick/pallas_call | solution.py:65
  2.1 5.2 %all-to-all-start = ((bf16[4,128,256]{2,1,0:T(8,128)(2,1)}), bf16[4,128,256]{2,1,0:T(8,128)(2,1)S(1)}, u32[]{:S(2)}, u32[]{:S(2)}) async-start(bf16[4,128,256]{2,1,0:T(8,128)(2,1)} %get-tuple-element.23), calls=%async_computation | async-start | bytes 524288 | tf_op jit(solution)/shard_map/all_to_all | solution.py:360
  7.3 3.4 %collective-permute-start.1 = (bf16[512,256]{1,0:T(8,128)(2,1)}, bf16[512,256]{1,0:T(8,128)(2,1)S(1)}, u32[]{:S(2)}, u32[]{:S(2)}) collective-permute-start(bf16[512,256]{1,0:T(8,128)(2,1)} %get-tuple-element.22.own), channel_id=1, source_target_pairs={{0,8},{4,12},{8,16},{12,20},{16,24},{20,28},{1,9},{5,13},{9,17},{1... | collective-permute-start | bytes 786440 | tf_op jit(solution)/shard_map/ppermute | solution.py:355
  10.7 3.4 %collective-permute-start = (bf16[512,256]{1,0:T(8,128)(2,1)}, bf16[512,256]{1,0:T(8,128)(2,1)S(1)}, u32[]{:S(2)}, u32[]{:S(2)}) collective-permute-start(bf16[512,256]{1,0:T(8,128)(2,1)} %get-tuple-element.22.own), channel_id=1, source_target_pairs={{0,4},{4,8},{8,12},{12,16},{16,20},{20,24},{24,28},{1,5},{5,9},{9,... | collective-permute-start | bytes 786440 | tf_op jit(solution)/shard_map/ppermute | solution.py:355
  14.1 0.0 all-to-all-done.refs_0_
  14.1 0.6 collective-permute-start.2
  14.7 4.8 %collective-permute-done.1.kv_2 = bf16[512,256]{1,0:T(8,128)(2,1)S(1)} collective-permute-done((bf16[512,256]{1,0:T(8,128)(2,1)}, bf16[512,256]{1,0:T(8,128)(2,1)S(1)}, u32[]{:S(2)}, u32[]{:S(2)}) %collective-permute-start.1) | collective-permute-done | bytes 262176 | tf_op jit(solution)/shard_map/ppermute | solution.py:355
  19.4 6.7 %collective-permute-done.kv_1 = bf16[512,256]{1,0:T(8,128)(2,1)S(1)} collective-permute-done((bf16[512,256]{1,0:T(8,128)(2,1)}, bf16[512,256]{1,0:T(8,128)(2,1)S(1)}, u32[]{:S(2)}, u32[]{:S(2)}) %collective-permute-start) | collective-permute-done | bytes 262176 | tf_op jit(solution)/shard_map/ppermute | solution.py:355
  26.1 0.6 collective-permute-done.2.refs_1_
  26.7 0.9 copy-done.4
  27.7 0.7 copy-done.7
  28.4 0.7 copy-done.8
  29.0 9.4 %attend.2 = (bf16[256,1024]{1,0:T(8,128)(2,1)S(1)}, bf16[128,4096]{1,0:T(8,128)(2,1)S(1)}, bf16[128,4096]{1,0:T(8,128)(2,1)S(1)}) custom-call(s32[1]{0:T(128)} %bitcast.tp_ref, s32[1]{0:T(128)} %bitcast.1.rank_ref.ctx_ref, bf16[512,1024]{1,0:T(8,128)(2,1)} %q_ref.3, s32[8,16]{1,0:T(8,128)S(1)} %copy-done.7, s32[8,8]{1,0:T(8,128)S(1)} %copy-done.8, ...), custom_call_target="tpu_custom_call" | custom-call | tf_op jit(solution)/shard_map/attend/pallas_call | solution.py:242
  38.5 0.1 collective-permute-start.3
  38.6 2.6 %collective-permute-done.3 = bf16[128,4096]{1,0:T(8,128)(2,1)S(1)} collective-permute-done((bf16[128,4096]{1,0:T(8,128)(2,1)S(1)}, bf16[128,4096]{1,0:T(8,128)(2,1)S(1)}, u32[]{:S(2)}, u32[]{:S(2)}) %collective-permute-start.3) | collective-permute-done | bytes 1048608 | tf_op jit(solution)/shard_map/ppermute | solution.py:364
  41.2 0.2 add_convert_fusion.refs_0_
  41.5 4.5 %project.2 = (bf16[128,2048]{1,0:T(8,128)(2,1)S(1)}, bf16[128,2048]{1,0:T(8,128)(2,1)S(1)}, bf16[128,2048]{1,0:T(8,128)(2,1)S(1)}, bf16[128,2048]{1,0:T(8,128)(2,1)S(1)}) custom-call(bf16[256,1024]{1,0:T(8,128)(2,1)S(1)} %get-tuple-element.24.a_ref, bf16[1024,8192]{1,0:T(8,128)(2,1)} %w_hbm.3, bf16[128,4096]{1,0:T(8,128)(2,1)S(1)} %add_convert_fusion.refs_0_), custom_call_target="tpu_custom_call" | custom-call | tf_op jit(solution)/shard_map/project/pallas_call | solution.py:297
  45.9 0.2 collective-permute-start.4
  46.1 0.4 collective-permute-start.5
  46.5 1.5 %collective-permute-start.6 = (bf16[128,4096]{1,0:T(8,128)(2,1)S(1)}, bf16[128,4096]{1,0:T(8,128)(2,1)S(1)}, u32[]{:S(2)}, u32[]{:S(2)}) collective-permute-start(bf16[128,4096]{1,0:T(8,128)(2,1)S(1)} %add_convert_fusion.refs_0_), channel_id=1, source_target_pairs={{0,2},{1,3},{2,0},{3,1},{4,6},{5,7},{6,4},{7,5},{8,10},{9,11},{10,... | collective-permute-start | bytes 3145736 | tf_op jit(solution)/shard_map/ppermute | solution.py:367
  48.0 0.0 collective-permute-done.4
  48.0 0.1 add_convert_fusion.2
  48.1 0.0 copy-start
  48.2 0.0 copy-start.5
  48.2 0.0 copy-start.9
  48.2 0.5 collective-permute-done.5
  48.7 0.1 add_convert_fusion.1
  48.8 0.1 pad_maximum_fusion.refs_3_
  48.9 1.6 %collective-permute-start.9 = (bf16[128,4096]{1,0:T(8,128)(2,1)S(1)}, bf16[128,4096]{1,0:T(8,128)(2,1)S(1)}, u32[]{:S(2)}, u32[]{:S(2)}) collective-permute-start(bf16[128,4096]{1,0:T(8,128)(2,1)S(1)} %pad_maximum_fusion.refs_3_), channel_id=1, source_target_pairs={{0,2},{1,3},{2,0},{3,1},{4,6},{5,7},{6,4},{7,5},{8,10},{9,11},{10,... | collective-permute-start | bytes 3145736 | tf_op jit(solution)/shard_map/ppermute | solution.py:367
  50.5 0.0 copy-done
  50.5 0.0 copy-done.5
  50.5 5.8 %attend.3.a_ref = bf16[256,1024]{1,0:T(8,128)(2,1)S(1)} custom-call(s32[1]{0:T(128)} %bitcast.tp_ref, s32[1]{0:T(128)} %bitcast.1.rank_ref.ctx_ref, bf16[512,1024]{1,0:T(8,128)(2,1)S(1)} %copy-done, s32[8,16]{1,0:T(8,128)S(1)} %copy-done.7, s32[8,8]{1,0:T(8,128)S(1)} %copy-done.9, bf16[512,256]{1,0:T(8,128)(2,1)S(1)} %copy-done.5, ...), custom_call_target="tpu_custom_call" | custom-call | tf_op jit(solution)/shard_map/attend/pallas_call | solution.py:242
  56.3 0.8 copy-done.3
  57.1 15.5 %collective-permute-done.6.refs_0_.refs_4_ = bf16[128,4096]{1,0:T(8,128)(2,1)S(1)} collective-permute-done((bf16[128,4096]{1,0:T(8,128)(2,1)S(1)}, bf16[128,4096]{1,0:T(8,128)(2,1)S(1)}, u32[]{:S(2)}, u32[]{:S(2)}) %collective-permute-start.6) | collective-permute-done | bytes 1048608 | tf_op jit(solution)/shard_map/ppermute | solution.py:367
  72.5 1.0 %copy-done.1 = bf16[128,4096]{1,0:T(8,128)(2,1)} copy-done((bf16[128,4096]{1,0:T(8,128)(2,1)}, bf16[128,4096]{1,0:T(8,128)(2,1)S(1)}, u32[]{:S(2)}) %copy-start.1) | copy-done | bytes 1048600
  73.5 9.2 %project.3 = (bf16[128,2048]{1,0:T(8,128)(2,1)S(1)}, bf16[128,2048]{1,0:T(8,128)(2,1)S(1)}, bf16[128,2048]{1,0:T(8,128)(2,1)S(1)}, bf16[128,2048]{1,0:T(8,128)(2...) custom-call(bf16[256,1024]{1,0:T(8,128)(2,1)} %copy-done.3, ...), custom_call_target="tpu_custom_call" | custom-call | tf_op jit(solution)/shard_map/project/pallas_call | solution.py:297
  82.7 0.1 collective-permute-start.10
  82.8 0.5 collective-permute-start.11
  83.3 0.1 collective-permute-start.7
  83.4 0.4 collective-permute-start.8
  83.8 0.9 collective-permute-done.10.refs_2_
  84.7 0.7 collective-permute-done.11.refs_3_
  85.4 1.2 %copy-done.2 = bf16[128,4096]{1,0:T(8,128)(2,1)S(1)} copy-done((bf16[128,4096]{1,0:T(8,128)(2,1)S(1)}, bf16[128,4096]{1,0:T(8,128)(2,1)}, u32[]{:S(2)}) %copy-start.2) | copy-done | bytes 1048600
  86.7 1.7 %finish.2.refs_5_ = bf16[128,8192]{1,0:T(8,128)(2,1)} custom-call(bf16[128,2048]{1,0:T(8,128)(2,1)S(1)} %get-tuple-element.35.refs_0_, bf16[128,2048]{1,0:T(8,128)(2,1)S(1)} %get-tuple-element.36.refs_1_, bf16[128,2048]{1,0:T(8,128)(2,1)S(1)} %collective-permute-done.10.refs_2_, bf16[128,2048]{1,0:T(8,128)(2,1)S(1)} %collective-permute-done.11.refs_3_, ...), custom_call_target="tpu_custom_call" | custom-call | tf_op jit(solution)/shard_map/finish/pallas_call | solution.py:335
  88.4 5.8 %collective-permute-done.9.refs_4_ = bf16[128,4096]{1,0:T(8,128)(2,1)S(1)} collective-permute-done((bf16[128,4096]{1,0:T(8,128)(2,1)S(1)}, bf16[128,4096]{1,0:T(8,128)(2,1)S(1)}, u32[]{:S(2)}, u32[]{:S(2)}) %collective-permute-start.9) | collective-permute-done | bytes 1048608 | tf_op jit(solution)/shard_map/ppermute | solution.py:367
  94.2 0.0 collective-permute-done.7.refs_2_
  94.2 0.0 collective-permute-done.8.refs_3_
  94.2 1.8 %finish.3 = bf16[128,8192]{1,0:T(8,128)(2,1)} custom-call(bf16[128,2048]{1,0:T(8,128)(2,1)S(1)} %get-tuple-element.31.refs_0_, bf16[128,2048]{1,0:T(8,128)(2,1)S(1)} %copy-done.6, bf16[128,2048]{1,0:T(8,128)(2,1)S(1)} %collective-permute-done.7.refs_2_, bf16[128,2048]{1,0:T(8,128)(2,1)S(1)} %collective-permute-done.8.refs_3_, ...), custom_call_target="tpu_custom_call", output_to_operand_aliasing={{}: (5, {})} | custom-call | tf_op jit(solution)/shard_map/finish/pallas_call | solution.py:335
  (9 shorter events, 0.0 us)
Async XLA Ops:
  2.1 12.0 %all-to-all-start = ((bf16[4,128,256]{2,1,0:T(8,128)(2,1)}), bf16[4,128,256]{2,1,0:T(8,128)(2,1)S(1)}, u32[]{:S(2)}, u32[]{:S(2)}) async-start(bf16[4,128,256]{2,1,0:T(8,128)(2,1)} %get-tuple-element.23), calls=%async_computation | async-start | bytes 524288 | tf_op jit(solution)/shard_map/all_to_all | solution.py:360
  7.3 12.1 %collective-permute-start.1 = (bf16[512,256]{1,0:T(8,128)(2,1)}, bf16[512,256]{1,0:T(8,128)(2,1)S(1)}, u32[]{:S(2)}, u32[]{:S(2)}) collective-permute-start(bf16[512,256]{1,0:T(8,128)(2,1)} %get-tuple-element.22.own), channel_id=1, source_target_pairs={{0,8},{4,12},{8,16},{12,20},{16,24},{20,28},{1,9},{5,13},{9,17},{1... | collective-permute-start | bytes 786440 | tf_op jit(solution)/shard_map/ppermute | solution.py:355
  10.7 15.4 %collective-permute-start = (bf16[512,256]{1,0:T(8,128)(2,1)}, bf16[512,256]{1,0:T(8,128)(2,1)S(1)}, u32[]{:S(2)}, u32[]{:S(2)}) collective-permute-start(bf16[512,256]{1,0:T(8,128)(2,1)} %get-tuple-element.22.own), channel_id=1, source_target_pairs={{0,4},{4,8},{8,12},{12,16},{16,20},{20,24},{24,28},{1,5},{5,9},{9,... | collective-permute-start | bytes 786440 | tf_op jit(solution)/shard_map/ppermute | solution.py:355
  14.1 12.6 %collective-permute-start.2 = (bf16[4,128,256]{2,1,0:T(8,128)(2,1)S(1)}, bf16[4,128,256]{2,1,0:T(8,128)(2,1)S(1)}, u32[]{:S(2)}, u32[]{:S(2)}) collective-permute-start(bf16[4,128,256]{2,1,0:T(8,128)(2,1)S(1)} %all-to-all-done.refs_0_), channel_id=1, source_target_pairs={{0,4},{4,0},{8,12},{12,8},{16,20},{20,16},{24,28},{28,24},{1,5},{5... | collective-permute-start | bytes 786440 | tf_op jit(solution)/shard_map/ppermute | solution.py:361
  26.7 1.0 copy-start.4
  27.7 0.7 copy-start.7
  28.4 0.7 copy-start.8
  38.5 2.7 %collective-permute-start.3 = (bf16[128,4096]{1,0:T(8,128)(2,1)S(1)}, bf16[128,4096]{1,0:T(8,128)(2,1)S(1)}, u32[]{:S(2)}, u32[]{:S(2)}) collective-permute-start(bf16[128,4096]{1,0:T(8,128)(2,1)S(1)} %get-tuple-element.26), channel_id=1, source_target_pairs={{0,1},{1,0},{2,3},{3,2},{4,5},{5,4},{6,7},{7,6},{8,9},{9,8},{10,11... | collective-permute-start | bytes 3145736 | tf_op jit(solution)/shard_map/ppermute | solution.py:364
  45.9 2.1 %collective-permute-start.4 = (bf16[128,2048]{1,0:T(8,128)(2,1)S(1)}, bf16[128,2048]{1,0:T(8,128)(2,1)S(1)}, u32[]{:S(2)}, u32[]{:S(2)}) collective-permute-start(bf16[128,2048]{1,0:T(8,128)(2,1)S(1)} %get-tuple-element.28), channel_id=1, source_target_pairs={{0,1},{1,0},{2,3},{3,2},{4,5},{5,4},{6,7},{7,6},{8,9},{9,8},{10,11... | collective-permute-start | bytes 1572872 | tf_op jit(solution)/shard_map/ppermute | solution.py:364
  46.1 2.5 %collective-permute-start.5 = (bf16[128,2048]{1,0:T(8,128)(2,1)S(1)}, bf16[128,2048]{1,0:T(8,128)(2,1)S(1)}, u32[]{:S(2)}, u32[]{:S(2)}) collective-permute-start(bf16[128,2048]{1,0:T(8,128)(2,1)S(1)} %get-tuple-element.30), channel_id=1, source_target_pairs={{0,1},{1,0},{2,3},{3,2},{4,5},{5,4},{6,7},{7,6},{8,9},{9,8},{10,11... | collective-permute-start | bytes 1572872 | tf_op jit(solution)/shard_map/ppermute | solution.py:364
  46.5 26.0 %collective-permute-start.6 = (bf16[128,4096]{1,0:T(8,128)(2,1)S(1)}, bf16[128,4096]{1,0:T(8,128)(2,1)S(1)}, u32[]{:S(2)}, u32[]{:S(2)}) collective-permute-start(bf16[128,4096]{1,0:T(8,128)(2,1)S(1)} %add_convert_fusion.refs_0_), channel_id=1, source_target_pairs={{0,2},{1,3},{2,0},{3,1},{4,6},{5,7},{6,4},{7,5},{8,10},{9,11},{10,... | collective-permute-start | bytes 3145736 | tf_op jit(solution)/shard_map/ppermute | solution.py:367
  48.1 2.3 %copy-start = (bf16[512,1024]{1,0:T(8,128)(2,1)S(1)}, bf16[512,1024]{1,0:T(8,128)(2,1)}, u32[]{:S(2)}) copy-start(bf16[512,1024]{1,0:T(8,128)(2,1)} %q_ref.3) | copy-start | bytes 3145732
  48.2 2.3 %copy-start.5 = (bf16[512,256]{1,0:T(8,128)(2,1)S(1)}, bf16[512,256]{1,0:T(8,128)(2,1)}, u32[]{:S(2)}) copy-start(bf16[512,256]{1,0:T(8,128)(2,1)} %get-tuple-element.22.own) | copy-start | bytes 786436
  48.2 2.3 %copy-start.9 = (s32[8,8]{1,0:T(8,128)S(1)}, s32[8,8]{1,0:T(8,128)}, u32[]{:S(2)}) copy-start(s32[8,8]{1,0:T(8,128)} %slash_ref.3) | copy-start | bytes 772
  48.9 45.3 %collective-permute-start.9 = (bf16[128,4096]{1,0:T(8,128)(2,1)S(1)}, bf16[128,4096]{1,0:T(8,128)(2,1)S(1)}, u32[]{:S(2)}, u32[]{:S(2)}) collective-permute-start(bf16[128,4096]{1,0:T(8,128)(2,1)S(1)} %pad_maximum_fusion.refs_3_), channel_id=1, source_target_pairs={{0,2},{1,3},{2,0},{3,1},{4,6},{5,7},{6,4},{7,5},{8,10},{9,11},{10,... | collective-permute-start | bytes 3145736 | tf_op jit(solution)/shard_map/ppermute | solution.py:367
  56.3 0.8 copy-start.3
  72.5 1.0 %copy-start.1 = (bf16[128,4096]{1,0:T(8,128)(2,1)}, bf16[128,4096]{1,0:T(8,128)(2,1)S(1)}, u32[]{:S(2)}) copy-start(bf16[128,4096]{1,0:T(8,128)(2,1)S(1)} %collective-permute-done.6.refs_0_.refs_4_) | copy-start | bytes 3145732
  82.7 2.0 %collective-permute-start.10 = (bf16[128,2048]{1,0:T(8,128)(2,1)S(1)}, bf16[128,2048]{1,0:T(8,128)(2,1)S(1)}, u32[]{:S(2)}, u32[]{:S(2)}) collective-permute-start(bf16[128,2048]{1,0:T(8,128)(2,1)S(1)} %get-tuple-element.37), channel_id=1, source_target_pairs={{0,1},{1,0},{2,3},{3,2},{4,5},{5,4},{6,7},{7,6},{8,9},{9,8},{10,11... | collective-permute-start | bytes 1572872 | tf_op jit(solution)/shard_map/ppermute | solution.py:364
  82.8 2.6 %collective-permute-start.11 = (bf16[128,2048]{1,0:T(8,128)(2,1)S(1)}, bf16[128,2048]{1,0:T(8,128)(2,1)S(1)}, u32[]{:S(2)}, u32[]{:S(2)}) collective-permute-start(bf16[128,2048]{1,0:T(8,128)(2,1)S(1)} %get-tuple-element.38), channel_id=1, source_target_pairs={{0,1},{1,0},{2,3},{3,2},{4,5},{5,4},{6,7},{7,6},{8,9},{9,8},{10,11... | collective-permute-start | bytes 1572872 | tf_op jit(solution)/shard_map/ppermute | solution.py:364
  83.3 10.9 %collective-permute-start.7 = (bf16[128,2048]{1,0:T(8,128)(2,1)S(1)}, bf16[128,2048]{1,0:T(8,128)(2,1)S(1)}, u32[]{:S(2)}, u32[]{:S(2)}) collective-permute-start(bf16[128,2048]{1,0:T(8,128)(2,1)S(1)} %get-tuple-element.33), channel_id=1, source_target_pairs={{0,1},{1,0},{2,3},{3,2},{4,5},{5,4},{6,7},{7,6},{8,9},{9,8},{10,11... | collective-permute-start | bytes 1572872 | tf_op jit(solution)/shard_map/ppermute | solution.py:364
  83.4 10.8 %collective-permute-start.8 = (bf16[128,2048]{1,0:T(8,128)(2,1)S(1)}, bf16[128,2048]{1,0:T(8,128)(2,1)S(1)}, u32[]{:S(2)}, u32[]{:S(2)}) collective-permute-start(bf16[128,2048]{1,0:T(8,128)(2,1)S(1)} %get-tuple-element.34), channel_id=1, source_target_pairs={{0,1},{1,0},{2,3},{3,2},{4,5},{5,4},{6,7},{7,6},{8,9},{9,8},{10,11... | collective-permute-start | bytes 1572872 | tf_op jit(solution)/shard_map/ppermute | solution.py:364
  85.4 1.2 %copy-start.2 = (bf16[128,4096]{1,0:T(8,128)(2,1)S(1)}, bf16[128,4096]{1,0:T(8,128)(2,1)}, u32[]{:S(2)}) copy-start(bf16[128,4096]{1,0:T(8,128)(2,1)} %copy-done.1) | copy-start | bytes 3145732
  86.6 7.5 %copy-start.6 = (bf16[128,2048]{1,0:T(8,128)(2,1)S(1)}, bf16[128,2048]{1,0:T(8,128)(2,1)}, u32[]{:S(2)}) copy-start(bf16[128,2048]{1,0:T(8,128)(2,1)} %get-tuple-element.32.refs_1_) | copy-start | bytes 1572868

commit v9 on v7

--- a/solution.py
+++ b/solution.py
@@ -13,10 +13,11 @@
 VMOST = 2
 NEAR = 3
 LANES = 128
+NOWHERE = 1 << 20
 MASKED = -1e30
 EXP_SCALE = 1.4426950408889634 / (HS**0.5)
 TILE = 1024
-PIECE = 2
+PIECE = 1
 HEAD = 4
 MIB = 1024 * 1024
 
@@ -82,7 +83,10 @@
 
 def pool_blocks(vertical, rank, slots, local_blocks):
     lane = lax.broadcasted_iota(jnp.int32, (vertical.shape[0], LANES), 1)
-    shard = jnp.where(lane // VMOST < slots, rank - (NEAR - 1) - lane // VMOST, -1)
+    shard = jnp.full(lane.shape, -1, jnp.int32)
+    for slot, (even, odd) in enumerate(slots):
+        back = jnp.where(rank & 1 == 1, odd, even)
+        shard = jnp.where(lane // VMOST == slot, rank - back, shard)
     first = jnp.full((1, LANES), local_blocks, jnp.int32)
     second = first
     for j in reversed(range(local_blocks)):
@@ -97,8 +101,8 @@
 def attend_kernel(
     slots, tiles, flips, tp_ref, ctx_ref, q_ref, vert_ref, slash_ref, own, kv_1, kv_2, *refs
 ):
-    pairs = refs[: slots - 1]
-    w_hbm = refs[slots - 1]
+    pairs = refs[: len(slots) - 1]
+    w_hbm = refs[len(slots) - 1]
     kv_win, e_win, kv_pool, e_pool, blocks_ref, attended, weight, arrival, landed = refs[-9:]
     outs = refs[-12:-9] if tiles else refs[-10:-9]
     step = pl.program_id(0)
@@ -217,14 +221,13 @@
             outs[2][:, t * TILE : (t + 1) * TILE] = product[half:]
 
 
-def attend(flips, tp, ctx, queries, vertical, slash, near_kv, pairs, out_weight, tiles, after):
+def attend(flips, tp, ctx, queries, vertical, slash, near_kv, pairs, slots, out_weight, tiles, after):
     width = queries.shape[1]
     rows = near_kv[0].shape[0]
     quarter = rows // 4
     steps = len(flips)
-    slots = len(pairs) + 1
     dtype = queries.dtype
-    far = slots * VMOST * BLK
+    far = len(slots) * VMOST * BLK
 
     def place(g, tp, ctx):
         return (tp[0] ^ jnp.where(g == 0, flips[0], flips[1]), 0)
@@ -257,7 +260,7 @@
                 pltpu.SemaphoreType.DMA((NEAR + len(pairs),)),
             ],
         ),
-        compiler_params=params(60),
+        compiler_params=params(50),
         cost_estimate=SHORT,
         name="attend",
     )(tp, ctx, queries, vertical, slash, *near_kv, *pairs, out_weight, *after)
@@ -299,7 +302,7 @@
             pltpu.VMEM((tiles, depth, TILE), attended.dtype),
             pltpu.SemaphoreType.DMA((tiles,)),
         ],
-        compiler_params=params(60),
+        compiler_params=params(50),
         cost_estimate=SHORT,
         name="project",
     )(attended, out_weight, *after)
@@ -308,49 +311,57 @@
 
 def add_kernel(*refs):
     out_ref = refs[-1]
-    tiles = len(refs) // 2
-    for t in range(tiles):
-        total = refs[t][...].astype(jnp.float32) + refs[tiles + t][...].astype(jnp.float32)
-        out_ref[:, t * PIECE * TILE : (t + 1) * PIECE * TILE] = total.astype(out_ref.dtype)
+    pieces = len(refs) // 2
+    for t in range(pieces):
+        total = refs[t][...].astype(jnp.float32) + refs[pieces + t][...].astype(jnp.float32)
+        columns = total.shape[1]
+        out_ref[:, t * columns : (t + 1) * columns] = total.astype(out_ref.dtype)
 
 
 def add(keep, got):
-    rows = keep[0].shape[0]
+    rows, columns = keep[0].shape
     return pl.pallas_call(
         add_kernel,
-        out_shape=jax.ShapeDtypeStruct((rows, len(keep) * PIECE * TILE), keep[0].dtype),
+        out_shape=jax.ShapeDtypeStruct((rows, len(keep) * columns), keep[0].dtype),
         in_specs=[vmem()] * (2 * len(keep)),
         out_specs=vmem(),
-        compiler_params=params(60),
+        compiler_params=params(16),
         cost_estimate=SHORT,
         name="add",
     )(*keep, *got)
 
 
-def finish_kernel(pieces, *refs):
-    arrived_ref, out_ref = refs[2 * pieces], refs[-1]
-    step = pl.program_id(0)
+def finish_kernel(pieces, first, *refs):
+    arrived_ref = refs[2 * pieces]
+    out_ref, tiles_ref, sent = refs[-3:]
+    copies = []
     for t in range(pieces * PIECE):
-
-        @pl.when(step == t)
-        def _():
-            part = slice(t % PIECE * TILE, (t % PIECE + 1) * TILE)
-            total = refs[t // PIECE][:, part].astype(jnp.float32)
-            total = total + refs[pieces + t // PIECE][:, part].astype(jnp.float32)
-            total = total + arrived_ref[:, t * TILE : (t + 1) * TILE].astype(jnp.float32)
-            out_ref[...] = total.astype(out_ref.dtype)
+        part = slice(t % PIECE * TILE, (t % PIECE + 1) * TILE)
+        total = refs[t // PIECE][:, part].astype(jnp.float32)
+        total = total + refs[pieces + t // PIECE][:, part].astype(jnp.float32)
+        total = total + arrived_ref[:, t * TILE : (t + 1) * TILE].astype(jnp.float32)
+        tiles_ref[t] = total.astype(out_ref.dtype)
+        columns = pl.ds((first + t) * TILE, TILE)
+        copies.append(pltpu.make_async_copy(tiles_ref.at[t], out_ref.at[:, columns], sent.at[t]))
+        copies[-1].start()
+    for copy in copies:
+        copy.wait()
 
 
 def finish(keep, got, arrived, first, width, out):
     rows = arrived.shape[0]
+    tiles = len(keep) * PIECE
     before = [] if out is None else [out]
     return pl.pallas_call(
-        functools.partial(finish_kernel, len(keep)),
+        functools.partial(finish_kernel, len(keep), first),
         out_shape=jax.ShapeDtypeStruct((rows, width), arrived.dtype),
-        grid=(len(keep) * PIECE,),
         in_specs=[vmem()] * (2 * len(keep) + 1) + [anywhere() for _ in before],
-        out_specs=pl.BlockSpec((rows, TILE), lambda g: (0, first + g)),
+        out_specs=anywhere(),
         input_output_aliases={2 * len(keep) + 1: 0} if before else {},
+        scratch_shapes=[
+            pltpu.VMEM((tiles, rows, TILE), arrived.dtype),
+            pltpu.SemaphoreType.DMA((tiles,)),
+        ],
         compiler_params=params(16),
         cost_estimate=SHORT,
         name="finish",
@@ -366,9 +377,16 @@
     def shifted(x, by):
         return lax.ppermute(x, "ctx", [(r, r + by) for r in range(ctx_size - by)])
 
+    def swapped(x):
+        return lax.ppermute(x, "ctx", [(r, r ^ 1) for r in range(ctx_size)])
+
     own, pair = pick(ctx, vertical, keys, values)
     near_kv = [own, shifted(own, 1), shifted(own, 2)]
-    pairs = [shifted(pair, s) for s in range(NEAR, ctx_size)]
+    backs = range(4, ctx_size, 2)
+    pairs = [shifted(pair, s) for s in backs]
+    third = lax.ppermute(pair, "ctx", [(r, r + 3) for r in range(0, ctx_size - 3, 2)])
+    pairs += [third] + [swapped(x) for x in pairs]
+    slots = [(2, 2)] + [(s, s) for s in backs] + [(NOWHERE, 3)] + [(s - 1, s + 1) for s in backs]
 
     def sibling(x):
         return lax.ppermute(x, "tp", [(j, j ^ 1) for j in range(4)])
@@ -378,14 +396,13 @@
 
     def attention(flips, tiles, after):
         return attend(
-            flips, tp, ctx, queries, vertical, slash, near_kv, pairs, out_weight, tiles, after
+            flips, tp, ctx, queries, vertical, slash, near_kv, pairs, slots, out_weight, tiles, after
         )
 
     width = out_weight.shape[1]
     tiles = width // TILE
     attended, send, keep = attention((3, 2), HEAD, ())
-    total = keep.astype(jnp.float32) + sibling(send).astype(jnp.float32)
-    total = total.astype(keep.dtype)
+    total = (keep.astype(jnp.float32) + sibling(send).astype(jnp.float32)).astype(keep.dtype)
     arrived = [across(total)]
     send, keep = project(attended, out_weight, HEAD, tiles - HEAD, (total,))
     total = add(keep, [sibling(x) for x in send])

time: 96 us -> 90.7 us (0.945)
  the two profiles are of different devices: /device:TPU:16 before, /device:TPU:0 now
where the time goes in v9:
time: 90.7 us; the launch traced here: 90.3 us
  Pallas kernels  33.6 us (37%)
  starting transfers between devices  25.7 us (28%)
  waiting for transfers between devices  25 us (28%)
  local copies, waits for them, and re-layouts  5.31 us (6%)
    ppermute x2, waiting for transfers between devices, across(): return lax.ppermute(x, 'tp', [(j, j ^ 2) for j in range(4)])  16 us
    pallas_call x2, Pallas kernels, attend(): pl.pallas_call(functools.partial(attend_kernel, slots, tiles, flips), out...  15.6 us
    pallas_call x2, Pallas kernels, project(): pl.pallas_call(functools.partial(project_kernel, first), out_shape=[part]...  13.6 us
    ppermute x4, starting transfers between devices, shifted(): return lax.ppermute(x, 'ctx', [(r, r + by) for r in range(ctx_size - by)])  13.5 us
    ppermute x2, starting transfers between devices, swapped(): return lax.ppermute(x, 'ctx', [(r, r ^ 1) for r in range(ctx_size)])  5.96 us
    ppermute x13, waiting for transfers between devices, sibling(): return lax.ppermute(x, 'tp', [(j, j ^ 1) for j in range(4)])  5.51 us
    unnamed x20, local copies, waits for them, and re-layouts  5.31 us
    ppermute x2, waiting for transfers between devices, swapped(): return lax.ppermute(x, 'ctx', [(r, r ^ 1) for r in range(ctx_size)])  3.52 us
  transfers between devices with their start and end apart: 22, of which 13 were waited for; matrix products, arithmetic and copies ran while one was open for 0% of the time, Pallas kernels for 23%

profile of v9, /device:TPU:0, one launch (start us, length us, event | category | flops | bytes accessed | tf_op | source)
XLA Modules:
  0.0 90.3 jit_solution(9430584637581632319)
XLA Ops:
  0.0 2.0 %pick.1 = (bf16[512,256]{1,0:T(8,128)(2,1)}, bf16[128,256]{1,0:T(8,128)(2,1)}) custom-call(s32[1]{0:T(128)} %bitcast.1.rank_ref.ctx_ref, s32[8,16]{1,0:T(8,128)} %vert_ref.5, bf16[512,128]{1,0:T(8,128)(2,1)} %k_ref.1, bf16[512,128]{1,0:T(8,128)(2,1)} %v_ref.1), custom_call_target="tpu_custom_call" | custom-call | tf_op jit(solution)/shard_map/pick/pallas_call | solution.py:64
  2.0 4.9 %collective-permute-start.1 = (bf16[512,256]{1,0:T(8,128)(2,1)}, bf16[512,256]{1,0:T(8,128)(2,1)S(1)}, u32[]{:S(2)}, u32[]{:S(2)}) collective-permute-start(bf16[512,256]{1,0:T(8,128)(2,1)} %get-tuple-element.34.own), channel_id=1, source_target_pairs={{0,8},{4,12},{8,16},{12,20},{16,24},{20,28},{1,9},{5,13},{9,17},{1... | collective-permute-start | bytes 786440 | tf_op jit(solution)/shard_map/ppermute | solution.py:378
  6.9 3.4 %collective-permute-start = (bf16[512,256]{1,0:T(8,128)(2,1)}, bf16[512,256]{1,0:T(8,128)(2,1)S(1)}, u32[]{:S(2)}, u32[]{:S(2)}) collective-permute-start(bf16[512,256]{1,0:T(8,128)(2,1)} %get-tuple-element.34.own), channel_id=1, source_target_pairs={{0,4},{4,8},{8,12},{12,16},{16,20},{20,24},{24,28},{1,5},{5,9},{9,... | collective-permute-start | bytes 786440 | tf_op jit(solution)/shard_map/ppermute | solution.py:378
  10.4 3.3 %collective-permute-start.3 = (bf16[128,256]{1,0:T(8,128)(2,1)}, bf16[128,256]{1,0:T(8,128)(2,1)S(1)}, u32[]{:S(2)}, u32[]{:S(2)}) collective-permute-start(bf16[128,256]{1,0:T(8,128)(2,1)} %get-tuple-element.35), channel_id=1, source_target_pairs={{0,24},{4,28},{1,25},{5,29},{2,26},{6,30},{3,27},{7,31}} | collective-permute-start | bytes 196616 | tf_op jit(solution)/shard_map/ppermute | solution.py:378
  13.7 1.8 %collective-permute-start.2 = (bf16[128,256]{1,0:T(8,128)(2,1)}, bf16[128,256]{1,0:T(8,128)(2,1)S(1)}, u32[]{:S(2)}, u32[]{:S(2)}) collective-permute-start(bf16[128,256]{1,0:T(8,128)(2,1)} %get-tuple-element.35), channel_id=1, source_target_pairs={{0,16},{4,20},{8,24},{12,28},{1,17},{5,21},{9,25},{13,29},{2,18},{... | collective-permute-start | bytes 196616 | tf_op jit(solution)/shard_map/ppermute | solution.py:378
  15.5 1.3 %collective-permute-start.4 = (bf16[128,256]{1,0:T(8,128)(2,1)}, bf16[128,256]{1,0:T(8,128)(2,1)S(1)}, u32[]{:S(2)}, u32[]{:S(2)}) collective-permute-start(bf16[128,256]{1,0:T(8,128)(2,1)} %get-tuple-element.35), channel_id=1, source_target_pairs={{0,12},{8,20},{16,28},{1,13},{9,21},{17,29},{2,14},{10,22},{18,30}... | collective-permute-start | bytes 196616 | tf_op jit(solution)/shard_map/ppermute | solution.py:387
  16.9 5.2 %collective-permute-start.6 = (bf16[128,256]{1,0:T(8,128)(2,1)S(1)}, bf16[128,256]{1,0:T(8,128)(2,1)S(1)}, u32[]{:S(2)}, u32[]{:S(2)}) collective-permute-start(bf16[128,256]{1,0:T(8,128)(2,1)S(1)} %collective-permute-done.3.refs_1_), channel_id=1, source_target_pairs={{0,4},{4,0},{8,12},{12,8},{16,20},{20,16},{24,28},{28,24},{1,5},{5... | collective-permute-start | bytes 196616 | tf_op jit(solution)/shard_map/ppermute | solution.py:381
  22.1 0.7 collective-permute-start.5
  22.8 1.5 %collective-permute-done.6.refs_4_ = bf16[128,256]{1,0:T(8,128)(2,1)S(1)} collective-permute-done((bf16[128,256]{1,0:T(8,128)(2,1)S(1)}, bf16[128,256]{1,0:T(8,128)(2,1)S(1)}, u32[]{:S(2)}, u32[]{:S(2)}) %collective-permute-start.6) | collective-permute-done | bytes 65568 | tf_op jit(solution)/shard_map/ppermute | solution.py:381
  24.3 2.0 %collective-permute-done.5.refs_3_ = bf16[128,256]{1,0:T(8,128)(2,1)S(1)} collective-permute-done((bf16[128,256]{1,0:T(8,128)(2,1)S(1)}, bf16[128,256]{1,0:T(8,128)(2,1)S(1)}, u32[]{:S(2)}, u32[]{:S(2)}) %collective-permute-start.5) | collective-permute-done | bytes 65568 | tf_op jit(solution)/shard_map/ppermute | solution.py:381
  26.3 0.9 %copy-done.4 = bf16[512,256]{1,0:T(8,128)(2,1)S(1)} copy-done((bf16[512,256]{1,0:T(8,128)(2,1)S(1)}, bf16[512,256]{1,0:T(8,128)(2,1)}, u32[]{:S(2)}) %copy-start.4) | copy-done | bytes 262168
  27.3 0.7 copy-done.7
  28.0 0.7 copy-done.8
  28.7 9.6 %attend.2 = (bf16[256,1024]{1,0:T(8,128)(2,1)S(1)}, bf16[128,4096]{1,0:T(8,128)(2,1)S(1)}, bf16[128,4096]{1,0:T(8,128)(2,1)S(1)}) custom-call(s32[1]{0:T(128)} %bitcast.tp_ref, s32[1]{0:T(128)} %bitcast.1.rank_ref.ctx_ref, bf16[512,1024]{1,0:T(8,128)(2,1)} %q_ref.3, s32[8,16]{1,0:T(8,128)S(1)} %copy-done.7, s32[8,8]{1,0:T(8,128)S(1)} %copy-done.8, ...), custom_call_target="tpu_custom_call" | custom-call | tf_op jit(solution)/shard_map/attend/pallas_call | solution.py:241
  38.3 0.1 collective-permute-start.7
  38.4 2.6 %collective-permute-done.7 = bf16[128,4096]{1,0:T(8,128)(2,1)S(1)} collective-permute-done((bf16[128,4096]{1,0:T(8,128)(2,1)S(1)}, bf16[128,4096]{1,0:T(8,128)(2,1)S(1)}, u32[]{:S(2)}, u32[]{:S(2)}) %collective-permute-start.7) | collective-permute-done | bytes 1048608 | tf_op jit(solution)/shard_map/ppermute | solution.py:392
  41.0 0.2 add_convert_fusion.refs_0_
  41.3 1.6 %collective-permute-start.12 = (bf16[128,4096]{1,0:T(8,128)(2,1)S(1)}, bf16[128,4096]{1,0:T(8,128)(2,1)S(1)}, u32[]{:S(2)}, u32[]{:S(2)}) collective-permute-start(bf16[128,4096]{1,0:T(8,128)(2,1)S(1)} %add_convert_fusion.refs_0_), channel_id=1, source_target_pairs={{0,2},{1,3},{2,0},{3,1},{4,6},{5,7},{6,4},{7,5},{8,10},{9,11},{10,... | collective-permute-start | bytes 3145736 | tf_op jit(solution)/shard_map/ppermute | solution.py:395
  42.8 4.5 %project.2 = (bf16[128,1024]{1,0:T(8,128)(2,1)S(1)}, bf16[128,1024]{1,0:T(8,128)(2,1)S(1)}, bf16[128,1024]{1,0:T(8,128)(2,1)S(1)}, bf16[128,1024]{1,0:T(8,128)(2...) custom-call(bf16[256,1024]{1,0:T(8,128)(2,1)S(1)} %get-tuple-element, ...), custom_call_target="tpu_custom_call" | custom-call | tf_op jit(solution)/shard_map/project/pallas_call | solution.py:296
  47.4 0.5 collective-permute-start.9
  47.9 0.1 collective-permute-start.10
  48.0 0.4 collective-permute-start.11
  48.5 0.5 collective-permute-done.8.refs_4_
  49.0 0.4 collective-permute-done.9.refs_5_
  49.3 0.4 collective-permute-done.10.refs_6_
  49.7 0.4 collective-permute-done.11.refs_7_
  50.1 0.2 add.6.refs_6_
  50.3 0.6 collective-permute-start.17
  50.9 5.9 %attend.3.a_ref = bf16[256,1024]{1,0:T(8,128)(2,1)S(1)} custom-call(s32[1]{0:T(128)} %bitcast.tp_ref, s32[1]{0:T(128)} %bitcast.1.rank_ref.ctx_ref, bf16[512,1024]{1,0:T(8,128)(2,1)S(1)} %copy-done, s32[8,16]{1,0:T(8,128)S(1)} %copy-done.7, s32[8,8]{1,0:T(8,128)S(1)} %copy-done.9, bf16[512,256]{1,0:T(8,128)(2,1)S(1)} %copy-done.5, ...), custom_call_target="tpu_custom_call" | custom-call | tf_op jit(solution)/shard_map/attend/pallas_call | solution.py:241
  56.9 0.8 copy-done.3
  57.7 9.7 %collective-permute-done.12.refs_0_.refs_8_ = bf16[128,4096]{1,0:T(8,128)(2,1)S(1)} collective-permute-done((bf16[128,4096]{1,0:T(8,128)(2,1)S(1)}, bf16[128,4096]{1,0:T(8,128)(2,1)S(1)}, u32[]{:S(2)}, u32[]{:S(2)}) %collective-permute-start.12) | collective-permute-done | bytes 1048608 | tf_op jit(solution)/shard_map/ppermute | solution.py:395
  67.3 1.0 %copy-done.1 = bf16[128,4096]{1,0:T(8,128)(2,1)} copy-done((bf16[128,4096]{1,0:T(8,128)(2,1)}, bf16[128,4096]{1,0:T(8,128)(2,1)S(1)}, u32[]{:S(2)}) %copy-start.1) | copy-done | bytes 1048600
  68.3 9.1 %project.3 = (bf16[128,1024]{1,0:T(8,128)(2,1)S(1)}, bf16[128,1024]{1,0:T(8,128)(2,1)S(1)}, bf16[128,1024]{1,0:T(8,128)(2,1)S(1)}, bf16[128,1024]{1,0:T(8,128)(2...) custom-call(bf16[256,1024]{1,0:T(8,128)(2,1)} %copy-done.3, ...), custom_call_target="tpu_custom_call" | custom-call | tf_op jit(solution)/shard_map/project/pallas_call | solution.py:296
  77.5 0.5 collective-permute-start.19
  78.0 0.1 collective-permute-start.20
  78.1 0.4 collective-permute-start.21
  78.5 0.5 collective-permute-done.18.refs_4_
  79.0 0.1 collective-permute-start.13
  79.2 0.2 collective-permute-done.19.refs_5_
  79.4 0.1 collective-permute-start.14
  79.5 0.2 collective-permute-done.20.refs_6_
  79.8 0.1 collective-permute-start.15
  79.9 0.2 collective-permute-done.21.refs_7_
  80.1 0.1 collective-permute-start.16
  80.3 1.2 %copy-done.2 = bf16[128,4096]{1,0:T(8,128)(2,1)S(1)} copy-done((bf16[128,4096]{1,0:T(8,128)(2,1)S(1)}, bf16[128,4096]{1,0:T(8,128)(2,1)}, u32[]{:S(2)}) %copy-start.2) | copy-done | bytes 1048600
  81.5 1.1 %finish.2.refs_9_ = bf16[128,8192]{1,0:T(8,128)(2,1)} custom-call(bf16[128,1024]{1,0:T(8,128)(2,1)S(1)} %get-tuple-element.55.refs_0_, bf16[128,1024]{1,0:T(8,128)(2,1)S(1)} %get-tuple-element.56.refs_1_, bf16[128,1024]{1,0:T(8,128)(2,1)S(1)} %get-tuple-element.57.refs_2_, bf16[128,1024]{1,0:T(8,128)(2,1)S(1)} %get-tuple-element.58.refs_3_, ...), custom_call_target="tpu_custom_call" | custom-call | tf_op jit(solution)/shard_map/finish/pallas_call | solution.py:355
  82.7 6.3 %collective-permute-done.17.refs_8_ = bf16[128,4096]{1,0:T(8,128)(2,1)S(1)} collective-permute-done((bf16[128,4096]{1,0:T(8,128)(2,1)S(1)}, bf16[128,4096]{1,0:T(8,128)(2,1)S(1)}, u32[]{:S(2)}, u32[]{:S(2)}) %collective-permute-start.17) | collective-permute-done | bytes 1048608 | tf_op jit(solution)/shard_map/ppermute | solution.py:395
  89.0 1.1 %finish.3 = bf16[128,8192]{1,0:T(8,128)(2,1)} custom-call(bf16[128,1024]{1,0:T(8,128)(2,1)S(1)} %get-tuple-element.47.refs_0_, bf16[128,1024]{1,0:T(8,128)(2,1)S(1)} %get-tuple-element.48.refs_1_, bf16[128,1024]{1,0:T(8,128)(2,1)S(1)} %get-tuple-element.49.refs_2_, bf16[128,1024]{1,0:T(8,128)(2,1)S(1)} %copy-done.6, ...), custom_call_target="tpu_custom_call", output_to_operand_aliasing={{}: (9, {})} | custom-call | tf_op jit(solution)/shard_map/finish/pallas_call | solution.py:355
  (25 shorter events, 0.2 us)
Async XLA Ops:
  2.0 24.3 %collective-permute-start.1 = (bf16[512,256]{1,0:T(8,128)(2,1)}, bf16[512,256]{1,0:T(8,128)(2,1)S(1)}, u32[]{:S(2)}, u32[]{:S(2)}) collective-permute-start(bf16[512,256]{1,0:T(8,128)(2,1)} %get-tuple-element.34.own), channel_id=1, source_target_pairs={{0,8},{4,12},{8,16},{12,20},{16,24},{20,28},{1,9},{5,13},{9,17},{1... | collective-permute-start | bytes 786440 | tf_op jit(solution)/shard_map/ppermute | solution.py:378
  6.9 19.4 %collective-permute-start = (bf16[512,256]{1,0:T(8,128)(2,1)}, bf16[512,256]{1,0:T(8,128)(2,1)S(1)}, u32[]{:S(2)}, u32[]{:S(2)}) collective-permute-start(bf16[512,256]{1,0:T(8,128)(2,1)} %get-tuple-element.34.own), channel_id=1, source_target_pairs={{0,4},{4,8},{8,12},{12,16},{16,20},{20,24},{24,28},{1,5},{5,9},{9,... | collective-permute-start | bytes 786440 | tf_op jit(solution)/shard_map/ppermute | solution.py:378
  10.4 6.5 %collective-permute-start.3 = (bf16[128,256]{1,0:T(8,128)(2,1)}, bf16[128,256]{1,0:T(8,128)(2,1)S(1)}, u32[]{:S(2)}, u32[]{:S(2)}) collective-permute-start(bf16[128,256]{1,0:T(8,128)(2,1)} %get-tuple-element.35), channel_id=1, source_target_pairs={{0,24},{4,28},{1,25},{5,29},{2,26},{6,30},{3,27},{7,31}} | collective-permute-start | bytes 196616 | tf_op jit(solution)/shard_map/ppermute | solution.py:378
  13.7 8.4 %collective-permute-start.2 = (bf16[128,256]{1,0:T(8,128)(2,1)}, bf16[128,256]{1,0:T(8,128)(2,1)S(1)}, u32[]{:S(2)}, u32[]{:S(2)}) collective-permute-start(bf16[128,256]{1,0:T(8,128)(2,1)} %get-tuple-element.35), channel_id=1, source_target_pairs={{0,16},{4,20},{8,24},{12,28},{1,17},{5,21},{9,25},{13,29},{2,18},{... | collective-permute-start | bytes 196616 | tf_op jit(solution)/shard_map/ppermute | solution.py:378
  15.5 7.3 %collective-permute-start.4 = (bf16[128,256]{1,0:T(8,128)(2,1)}, bf16[128,256]{1,0:T(8,128)(2,1)S(1)}, u32[]{:S(2)}, u32[]{:S(2)}) collective-permute-start(bf16[128,256]{1,0:T(8,128)(2,1)} %get-tuple-element.35), channel_id=1, source_target_pairs={{0,12},{8,20},{16,28},{1,13},{9,21},{17,29},{2,14},{10,22},{18,30}... | collective-permute-start | bytes 196616 | tf_op jit(solution)/shard_map/ppermute | solution.py:387
  16.9 7.5 %collective-permute-start.6 = (bf16[128,256]{1,0:T(8,128)(2,1)S(1)}, bf16[128,256]{1,0:T(8,128)(2,1)S(1)}, u32[]{:S(2)}, u32[]{:S(2)}) collective-permute-start(bf16[128,256]{1,0:T(8,128)(2,1)S(1)} %collective-permute-done.3.refs_1_), channel_id=1, source_target_pairs={{0,4},{4,0},{8,12},{12,8},{16,20},{20,16},{24,28},{28,24},{1,5},{5... | collective-permute-start | bytes 196616 | tf_op jit(solution)/shard_map/ppermute | solution.py:381
  22.1 4.3 %collective-permute-start.5 = (bf16[128,256]{1,0:T(8,128)(2,1)S(1)}, bf16[128,256]{1,0:T(8,128)(2,1)S(1)}, u32[]{:S(2)}, u32[]{:S(2)}) collective-permute-start(bf16[128,256]{1,0:T(8,128)(2,1)S(1)} %collective-permute-done.2.refs_0_), channel_id=1, source_target_pairs={{0,4},{4,0},{8,12},{12,8},{16,20},{20,16},{24,28},{28,24},{1,5},{5... | collective-permute-start | bytes 196616 | tf_op jit(solution)/shard_map/ppermute | solution.py:381
  26.3 1.0 %copy-start.4 = (bf16[512,256]{1,0:T(8,128)(2,1)S(1)}, bf16[512,256]{1,0:T(8,128)(2,1)}, u32[]{:S(2)}) copy-start(bf16[512,256]{1,0:T(8,128)(2,1)} %get-tuple-element.34.own) | copy-start | bytes 786436
  27.3 0.7 copy-start.7
  28.0 0.7 copy-start.8
  38.3 2.7 %collective-permute-start.7 = (bf16[128,4096]{1,0:T(8,128)(2,1)S(1)}, bf16[128,4096]{1,0:T(8,128)(2,1)S(1)}, u32[]{:S(2)}, u32[]{:S(2)}) collective-permute-start(bf16[128,4096]{1,0:T(8,128)(2,1)S(1)} %get-tuple-element.38), channel_id=1, source_target_pairs={{0,1},{1,0},{2,3},{3,2},{4,5},{5,4},{6,7},{7,6},{8,9},{9,8},{10,11... | collective-permute-start | bytes 3145736 | tf_op jit(solution)/shard_map/ppermute | solution.py:392
  41.3 26.1 %collective-permute-start.12 = (bf16[128,4096]{1,0:T(8,128)(2,1)S(1)}, bf16[128,4096]{1,0:T(8,128)(2,1)S(1)}, u32[]{:S(2)}, u32[]{:S(2)}) collective-permute-start(bf16[128,4096]{1,0:T(8,128)(2,1)S(1)} %add_convert_fusion.refs_0_), channel_id=1, source_target_pairs={{0,2},{1,3},{2,0},{3,1},{4,6},{5,7},{6,4},{7,5},{8,10},{9,11},{10,... | collective-permute-start | bytes 3145736 | tf_op jit(solution)/shard_map/ppermute | solution.py:395
  47.3 3.6 %copy-start = (bf16[512,1024]{1,0:T(8,128)(2,1)S(1)}, bf16[512,1024]{1,0:T(8,128)(2,1)}, u32[]{:S(2)}) copy-start(bf16[512,1024]{1,0:T(8,128)(2,1)} %q_ref.3) | copy-start | bytes 3145732
  47.3 3.6 %copy-start.5 = (bf16[512,256]{1,0:T(8,128)(2,1)S(1)}, bf16[512,256]{1,0:T(8,128)(2,1)}, u32[]{:S(2)}) copy-start(bf16[512,256]{1,0:T(8,128)(2,1)} %get-tuple-element.34.own) | copy-start | bytes 786436
  47.4 3.6 %copy-start.9 = (s32[8,8]{1,0:T(8,128)S(1)}, s32[8,8]{1,0:T(8,128)}, u32[]{:S(2)}) copy-start(s32[8,8]{1,0:T(8,128)} %slash_ref.3) | copy-start | bytes 772
  47.4 1.6 %collective-permute-start.8 = (bf16[128,1024]{1,0:T(8,128)(2,1)S(1)}, bf16[128,1024]{1,0:T(8,128)(2,1)S(1)}, u32[]{:S(2)}, u32[]{:S(2)}) collective-permute-start(bf16[128,1024]{1,0:T(8,128)(2,1)S(1)} %get-tuple-element.43), channel_id=1, source_target_pairs={{0,1},{1,0},{2,3},{3,2},{4,5},{5,4},{6,7},{7,6},{8,9},{9,8},{10,11... | collective-permute-start | bytes 786440 | tf_op jit(solution)/shard_map/ppermute | solution.py:392
  47.4 1.9 %collective-permute-start.9 = (bf16[128,1024]{1,0:T(8,128)(2,1)S(1)}, bf16[128,1024]{1,0:T(8,128)(2,1)S(1)}, u32[]{:S(2)}, u32[]{:S(2)}) collective-permute-start(bf16[128,1024]{1,0:T(8,128)(2,1)S(1)} %get-tuple-element.44), channel_id=1, source_target_pairs={{0,1},{1,0},{2,3},{3,2},{4,5},{5,4},{6,7},{7,6},{8,9},{9,8},{10,11... | collective-permute-start | bytes 786440 | tf_op jit(solution)/shard_map/ppermute | solution.py:392
  47.9 1.8 %collective-permute-start.10 = (bf16[128,1024]{1,0:T(8,128)(2,1)S(1)}, bf16[128,1024]{1,0:T(8,128)(2,1)S(1)}, u32[]{:S(2)}, u32[]{:S(2)}) collective-permute-start(bf16[128,1024]{1,0:T(8,128)(2,1)S(1)} %get-tuple-element.45), channel_id=1, source_target_pairs={{0,1},{1,0},{2,3},{3,2},{4,5},{5,4},{6,7},{7,6},{8,9},{9,8},{10,11... | collective-permute-start | bytes 786440 | tf_op jit(solution)/shard_map/ppermute | solution.py:392
  48.0 2.1 %collective-permute-start.11 = (bf16[128,1024]{1,0:T(8,128)(2,1)S(1)}, bf16[128,1024]{1,0:T(8,128)(2,1)S(1)}, u32[]{:S(2)}, u32[]{:S(2)}) collective-permute-start(bf16[128,1024]{1,0:T(8,128)(2,1)S(1)} %get-tuple-element.46), channel_id=1, source_target_pairs={{0,1},{1,0},{2,3},{3,2},{4,5},{5,4},{6,7},{7,6},{8,9},{9,8},{10,11... | collective-permute-start | bytes 786440 | tf_op jit(solution)/shard_map/ppermute | solution.py:392
  50.3 38.7 %collective-permute-start.17 = (bf16[128,4096]{1,0:T(8,128)(2,1)S(1)}, bf16[128,4096]{1,0:T(8,128)(2,1)S(1)}, u32[]{:S(2)}, u32[]{:S(2)}) collective-permute-start(bf16[128,4096]{1,0:T(8,128)(2,1)S(1)} %add.6.refs_6_), channel_id=1, source_target_pairs={{0,2},{1,3},{2,0},{3,1},{4,6},{5,7},{6,4},{7,5},{8,10},{9,11},{10,... | collective-permute-start | bytes 3145736 | tf_op jit(solution)/shard_map/ppermute | solution.py:395
  56.9 0.8 copy-start.3
  67.3 1.0 %copy-start.1 = (bf16[128,4096]{1,0:T(8,128)(2,1)}, bf16[128,4096]{1,0:T(8,128)(2,1)S(1)}, u32[]{:S(2)}) copy-start(bf16[128,4096]{1,0:T(8,128)(2,1)S(1)} %collective-permute-done.12.refs_0_.refs_8_) | copy-start | bytes 3145732
  77.4 1.6 %collective-permute-start.18 = (bf16[128,1024]{1,0:T(8,128)(2,1)S(1)}, bf16[128,1024]{1,0:T(8,128)(2,1)S(1)}, u32[]{:S(2)}, u32[]{:S(2)}) collective-permute-start(bf16[128,1024]{1,0:T(8,128)(2,1)S(1)} %get-tuple-element.59), channel_id=1, source_target_pairs={{0,1},{1,0},{2,3},{3,2},{4,5},{5,4},{6,7},{7,6},{8,9},{9,8},{10,11... | collective-permute-start | bytes 786440 | tf_op jit(solution)/shard_map/ppermute | solution.py:392
  77.5 1.9 %collective-permute-start.19 = (bf16[128,1024]{1,0:T(8,128)(2,1)S(1)}, bf16[128,1024]{1,0:T(8,128)(2,1)S(1)}, u32[]{:S(2)}, u32[]{:S(2)}) collective-permute-start(bf16[128,1024]{1,0:T(8,128)(2,1)S(1)} %get-tuple-element.60), channel_id=1, source_target_pairs={{0,1},{1,0},{2,3},{3,2},{4,5},{5,4},{6,7},{7,6},{8,9},{9,8},{10,11... | collective-permute-start | bytes 786440 | tf_op jit(solution)/shard_map/ppermute | solution.py:392
  78.0 1.8 %collective-permute-start.20 = (bf16[128,1024]{1,0:T(8,128)(2,1)S(1)}, bf16[128,1024]{1,0:T(8,128)(2,1)S(1)}, u32[]{:S(2)}, u32[]{:S(2)}) collective-permute-start(bf16[128,1024]{1,0:T(8,128)(2,1)S(1)} %get-tuple-element.61), channel_id=1, source_target_pairs={{0,1},{1,0},{2,3},{3,2},{4,5},{5,4},{6,7},{7,6},{8,9},{9,8},{10,11... | collective-permute-start | bytes 786440 | tf_op jit(solution)/shard_map/ppermute | solution.py:392
  78.1 2.1 %collective-permute-start.21 = (bf16[128,1024]{1,0:T(8,128)(2,1)S(1)}, bf16[128,1024]{1,0:T(8,128)(2,1)S(1)}, u32[]{:S(2)}, u32[]{:S(2)}) collective-permute-start(bf16[128,1024]{1,0:T(8,128)(2,1)S(1)} %get-tuple-element.62), channel_id=1, source_target_pairs={{0,1},{1,0},{2,3},{3,2},{4,5},{5,4},{6,7},{7,6},{8,9},{9,8},{10,11... | collective-permute-start | bytes 786440 | tf_op jit(solution)/shard_map/ppermute | solution.py:392
  79.0 3.6 %collective-permute-start.13 = (bf16[128,1024]{1,0:T(8,128)(2,1)S(1)}, bf16[128,1024]{1,0:T(8,128)(2,1)S(1)}, u32[]{:S(2)}, u32[]{:S(2)}) collective-permute-start(bf16[128,1024]{1,0:T(8,128)(2,1)S(1)} %get-tuple-element.51), channel_id=1, source_target_pairs={{0,1},{1,0},{2,3},{3,2},{4,5},{5,4},{6,7},{7,6},{8,9},{9,8},{10,11... | collective-permute-start | bytes 786440 | tf_op jit(solution)/shard_map/ppermute | solution.py:392
  79.4 3.2 %collective-permute-start.14 = (bf16[128,1024]{1,0:T(8,128)(2,1)S(1)}, bf16[128,1024]{1,0:T(8,128)(2,1)S(1)}, u32[]{:S(2)}, u32[]{:S(2)}) collective-permute-start(bf16[128,1024]{1,0:T(8,128)(2,1)S(1)} %get-tuple-element.52), channel_id=1, source_target_pairs={{0,1},{1,0},{2,3},{3,2},{4,5},{5,4},{6,7},{7,6},{8,9},{9,8},{10,11... | collective-permute-start | bytes 786440 | tf_op jit(solution)/shard_map/ppermute | solution.py:392
  79.8 2.9 %collective-permute-start.15 = (bf16[128,1024]{1,0:T(8,128)(2,1)S(1)}, bf16[128,1024]{1,0:T(8,128)(2,1)S(1)}, u32[]{:S(2)}, u32[]{:S(2)}) collective-permute-start(bf16[128,1024]{1,0:T(8,128)(2,1)S(1)} %get-tuple-element.53), channel_id=1, source_target_pairs={{0,1},{1,0},{2,3},{3,2},{4,5},{5,4},{6,7},{7,6},{8,9},{9,8},{10,11... | collective-permute-start | bytes 786440 | tf_op jit(solution)/shard_map/ppermute | solution.py:392
  80.1 2.5 %collective-permute-start.16 = (bf16[128,1024]{1,0:T(8,128)(2,1)S(1)}, bf16[128,1024]{1,0:T(8,128)(2,1)S(1)}, u32[]{:S(2)}, u32[]{:S(2)}) collective-permute-start(bf16[128,1024]{1,0:T(8,128)(2,1)S(1)} %get-tuple-element.54), channel_id=1, source_target_pairs={{0,1},{1,0},{2,3},{3,2},{4,5},{5,4},{6,7},{7,6},{8,9},{9,8},{10,11... | collective-permute-start | bytes 786440 | tf_op jit(solution)/shard_map/ppermute | solution.py:392
  80.3 1.2 %copy-start.2 = (bf16[128,4096]{1,0:T(8,128)(2,1)S(1)}, bf16[128,4096]{1,0:T(8,128)(2,1)}, u32[]{:S(2)}) copy-start(bf16[128,4096]{1,0:T(8,128)(2,1)} %copy-done.1) | copy-start | bytes 3145732
  81.5 7.5 %copy-start.6 = (bf16[128,1024]{1,0:T(8,128)(2,1)S(1)}, bf16[128,1024]{1,0:T(8,128)(2,1)}, u32[]{:S(2)}) copy-start(bf16[128,1024]{1,0:T(8,128)(2,1)} %get-tuple-element.50.refs_3_) | copy-start | bytes 786436

commit v10 on v9

--- a/solution.py
+++ b/solution.py
@@ -17,8 +17,8 @@
 MASKED = -1e30
 EXP_SCALE = 1.4426950408889634 / (HS**0.5)
 TILE = 1024
-PIECE = 1
 HEAD = 4
+REST = (1, 1, 1, 1)
 MIB = 1024 * 1024
 
 
@@ -72,6 +72,19 @@
         compiler_params=params(60),
         name="pick",
     )(rank, vertical, keys, values)
+
+
+def hold(x, others):
+    return pl.pallas_call(
+        lambda *refs: None,
+        out_shape=jax.ShapeDtypeStruct(x.shape, x.dtype),
+        in_specs=[anywhere() for _ in [x, *others]],
+        out_specs=anywhere(),
+        input_output_aliases={0: 0},
+        compiler_params=params(1),
+        cost_estimate=SHORT,
+        name="hold",
+    )(x, *others)
 
 
 def member(table, blocks):
@@ -98,21 +111,48 @@
     return jnp.where((picked < local_blocks) & (shard >= 0), shard * local_blocks + picked, -1)
 
 
+def tables_kernel(slots, rank_ref, vert_ref, slash_ref, own_ref, table_ref, copy_ref):
+    copy_ref[...] = own_ref[...]
+    local_blocks = own_ref.shape[0] // BLK
+    table_ref[0, :, : vert_ref.shape[1]] = vert_ref[...]
+    table_ref[1, :, : slash_ref.shape[1]] = slash_ref[...]
+    table_ref[2] = pool_blocks(vert_ref[...], rank_ref[0], slots, local_blocks)
+
+
+def tables(rank, vertical, slash, own, slots):
+    shape = (3, vertical.shape[0], LANES)
+    return pl.pallas_call(
+        functools.partial(tables_kernel, slots),
+        out_shape=(
+            jax.ShapeDtypeStruct(shape, jnp.int32),
+            jax.ShapeDtypeStruct(own.shape, own.dtype),
+        ),
+        in_specs=[smem(), vmem(), vmem(), vmem()],
+        out_specs=(vmem(), vmem()),
+        compiler_params=params(4),
+        cost_estimate=SHORT,
+        name="tables",
+    )(rank, vertical, slash, own)
+
+
 def attend_kernel(
-    slots, tiles, flips, tp_ref, ctx_ref, q_ref, vert_ref, slash_ref, own, kv_1, kv_2, *refs
+    slots, tiles, sizes, flips, tp_ref, ctx_ref, q_ref, table_ref, own, kv_1, kv_2, *refs
 ):
     pairs = refs[: len(slots) - 1]
     w_hbm = refs[len(slots) - 1]
-    kv_win, e_win, kv_pool, e_pool, blocks_ref, attended, weight, arrival, landed = refs[-9:]
-    outs = refs[-12:-9] if tiles else refs[-10:-9]
+    kv_win, e_win, kv_pool, e_pool, attended, weight, arrival, landed = refs[-8:]
+    outs = refs[-11:-8] if tiles else refs[-9:-8]
     step = pl.program_id(0)
-    heads = vert_ref.shape[0]
+    heads = table_ref.shape[1]
     rows = own.shape[0]
     local_blocks = rows // BLK
     quarter = local_blocks // 4
     pair_rows = VMOST * BLK
     dtype = q_ref.dtype
     rank = ctx_ref[0]
+    vert = table_ref[0][:, : sizes[0]]
+    slash = table_ref[1][:, : sizes[1]]
+    block = table_ref[2]
 
     def fetch(t):
         return pltpu.make_async_copy(
@@ -142,8 +182,7 @@
         key = lax.broadcasted_iota(jnp.int32, e_pool.shape, 0)
         lane = lax.broadcasted_iota(jnp.int32, e_pool.shape, 1)
         e_pool[...] = jnp.where(key // BLK == lane, 1.0, 0.0).astype(dtype)
-        blocks_ref[...] = pool_blocks(vert_ref[...], rank, slots, local_blocks)
-        picked = picked_blocks(vert_ref[...], rank - (NEAR - 1), local_blocks)
+        picked = picked_blocks(vert, rank - (NEAR - 1), local_blocks)
         for copy in copies:
             copy.wait()
         for slot, block in enumerate(picked):
@@ -154,9 +193,8 @@
     row = lax.broadcasted_iota(jnp.int32, (BLK, LANES), 0)
     above = lax.broadcasted_iota(jnp.int32, (BLK, LANES), 1) - BLK > row
     above = jnp.where(above, MASKED, 0.0).astype(jnp.float32)
-    offset_ok = member(slash_ref[...], SPAN - 1 - lane)
-    block = blocks_ref[...]
-    pool_ok = member(vert_ref[...], block) & (block >= 0)
+    offset_ok = member(slash, SPAN - 1 - lane)
+    pool_ok = member(vert, block) & (block >= 0)
     contract = (((1,), (1,)), ((), ()))
 
     def with_ones(values):
@@ -169,7 +207,7 @@
         q = jnp.concatenate([q[:, h * HS : (h + 1) * HS] for h in range(heads)], axis=0)
         first = rank * local_blocks + here - (SPAN - 1)
         seen = first + lane
-        ok = (seen >= 0) & (offset_ok | member(vert_ref[...], seen))
+        ok = (seen >= 0) & (offset_ok | member(vert, seen))
         mask = jnp.where(ok | (lane >= SPAN), 0.0, MASKED).astype(jnp.float32)
         mask = (mask[:, None, :] + above[None]).reshape(heads * BLK, LANES).astype(dtype)
         far_mask = jnp.where(pool_ok & (block < first), 0.0, MASKED).astype(jnp.float32)
@@ -221,7 +259,7 @@
             outs[2][:, t * TILE : (t + 1) * TILE] = product[half:]
 
 
-def attend(flips, tp, ctx, queries, vertical, slash, near_kv, pairs, slots, out_weight, tiles, after):
+def attend(flips, tp, ctx, queries, table, near_kv, pairs, slots, sizes, out_weight, tiles, after):
     width = queries.shape[1]
     rows = near_kv[0].shape[0]
     quarter = rows // 4
@@ -239,13 +277,13 @@
     if tiles:
         out_shapes += [(steps * quarter // 2, tiles * TILE)] * 2
     return pl.pallas_call(
-        functools.partial(attend_kernel, slots, tiles, flips),
+        functools.partial(attend_kernel, slots, tiles, sizes, flips),
         out_shape=[jax.ShapeDtypeStruct(shape, dtype) for shape in out_shapes],
         grid_spec=pltpu.PrefetchScalarGridSpec(
             num_scalar_prefetch=2,
             grid=(steps,),
             in_specs=[pl.BlockSpec((quarter, width), place)]
-            + [whole(vertical.shape), whole(slash.shape)]
+            + [whole(table.shape)]
             + [anywhere() for _ in [*near_kv, *pairs, out_weight, *after]],
             out_specs=[whole(shape) for shape in out_shapes],
             scratch_shapes=[
@@ -253,7 +291,6 @@
                 pltpu.VMEM((SPAN * BLK, LANES), dtype),
                 pltpu.VMEM((far, 2 * HS), dtype),
                 pltpu.VMEM((far, LANES), dtype),
-                pltpu.VMEM((vertical.shape[0], LANES), jnp.int32),
                 pltpu.VMEM((steps * quarter, width), dtype),
                 pltpu.VMEM((max(tiles, 1), out_weight.shape[0], TILE), dtype),
                 pltpu.SemaphoreType.DMA((max(tiles, 1),)),
@@ -263,14 +300,12 @@
         compiler_params=params(50),
         cost_estimate=SHORT,
         name="attend",
-    )(tp, ctx, queries, vertical, slash, *near_kv, *pairs, out_weight, *after)
-
-
-def project_kernel(first, a_ref, w_hbm, *refs):
+    )(tp, ctx, queries, table, *near_kv, *pairs, out_weight, *after)
+
+
+def project_kernel(first, sizes, a_ref, w_hbm, *refs):
     weight, arrival = refs[-2:]
-    tiles = weight.shape[0]
-    pieces = tiles // PIECE
-    outs = refs[-2 - 2 * pieces : -2]
+    outs = refs[-2 - 2 * len(sizes) : -2]
     half = outs[0].shape[0]
 
     def fetch(t):
@@ -278,51 +313,57 @@
             w_hbm.at[:, pl.ds((first + t) * TILE, TILE)], weight.at[t], arrival.at[t]
         )
 
-    for t in range(tiles):
+    for t in range(sum(sizes)):
         fetch(t).start()
-    for t in range(tiles):
-        fetch(t).wait()
-        product = jnp.dot(a_ref[...], weight[t], preferred_element_type=jnp.float32)
-        product = product.astype(a_ref.dtype)
-        at = slice(t % PIECE * TILE, (t % PIECE + 1) * TILE)
-        outs[t // PIECE][:, at] = product[:half]
-        outs[pieces + t // PIECE][:, at] = product[half:]
-
-
-def project(attended, out_weight, first, tiles, after):
+    t = 0
+    for piece, size in enumerate(sizes):
+        for place in range(size):
+            fetch(t).wait()
+            product = jnp.dot(a_ref[...], weight[t], preferred_element_type=jnp.float32)
+            product = product.astype(a_ref.dtype)
+            at = slice(place * TILE, (place + 1) * TILE)
+            outs[piece][:, at] = product[:half]
+            outs[len(sizes) + piece][:, at] = product[half:]
+            t += 1
+
+
+def project(attended, out_weight, first, sizes, after):
     rows, depth = attended.shape
-    pieces = tiles // PIECE
-    part = jax.ShapeDtypeStruct((rows // 2, PIECE * TILE), attended.dtype)
+    parts = [
+        jax.ShapeDtypeStruct((rows // 2, size * TILE), attended.dtype) for size in sizes
+    ]
     outs = pl.pallas_call(
-        functools.partial(project_kernel, first),
-        out_shape=[part] * (2 * pieces),
+        functools.partial(project_kernel, first, sizes),
+        out_shape=parts + parts,
         in_specs=[vmem(), anywhere()] + [anywhere() for _ in after],
-        out_specs=[vmem()] * (2 * pieces),
+        out_specs=[vmem()] * (2 * len(sizes)),
         scratch_shapes=[
-            pltpu.VMEM((tiles, depth, TILE), attended.dtype),
-            pltpu.SemaphoreType.DMA((tiles,)),
+            pltpu.VMEM((sum(sizes), depth, TILE), attended.dtype),
+            pltpu.SemaphoreType.DMA((sum(sizes),)),
         ],
         compiler_params=params(50),
         cost_estimate=SHORT,
         name="project",
     )(attended, out_weight, *after)
-    return outs[:pieces], outs[pieces:]
+    return outs[: len(sizes)], outs[len(sizes) :]
 
 
 def add_kernel(*refs):
     out_ref = refs[-1]
     pieces = len(refs) // 2
+    first = 0
     for t in range(pieces):
         total = refs[t][...].astype(jnp.float32) + refs[pieces + t][...].astype(jnp.float32)
-        columns = total.shape[1]
-        out_ref[:, t * columns : (t + 1) * columns] = total.astype(out_ref.dtype)
+        last = first + total.shape[1]
+        out_ref[:, first:last] = total.astype(out_ref.dtype)
+        first = last
 
 
 def add(keep, got):
-    rows, columns = keep[0].shape
+    rows, columns = keep[0].shape[0], sum(x.shape[1] for x in keep)
     return pl.pallas_call(
         add_kernel,
-        out_shape=jax.ShapeDtypeStruct((rows, len(keep) * columns), keep[0].dtype),
+        out_shape=jax.ShapeDtypeStruct((rows, columns), keep[0].dtype),
         in_specs=[vmem()] * (2 * len(keep)),
         out_specs=vmem(),
         compiler_params=params(16),
@@ -335,10 +376,8 @@
     arrived_ref = refs[2 * pieces]
     out_ref, tiles_ref, sent = refs[-3:]
     copies = []
-    for t in range(pieces * PIECE):
-        part = slice(t % PIECE * TILE, (t % PIECE + 1) * TILE)
-        total = refs[t // PIECE][:, part].astype(jnp.float32)
-        total = total + refs[pieces + t // PIECE][:, part].astype(jnp.float32)
+    for t in range(pieces):
+        total = refs[t][...].astype(jnp.float32) + refs[pieces + t][...].astype(jnp.float32)
         total = total + arrived_ref[:, t * TILE : (t + 1) * TILE].astype(jnp.float32)
         tiles_ref[t] = total.astype(out_ref.dtype)
         columns = pl.ds((first + t) * TILE, TILE)
@@ -350,7 +389,7 @@
 
 def finish(keep, got, arrived, first, width, out):
     rows = arrived.shape[0]
-    tiles = len(keep) * PIECE
+    tiles = len(keep)
     before = [] if out is None else [out]
     return pl.pallas_call(
         functools.partial(finish_kernel, len(keep), first),
@@ -381,12 +420,14 @@
         return lax.ppermute(x, "ctx", [(r, r ^ 1) for r in range(ctx_size)])
 
     own, pair = pick(ctx, vertical, keys, values)
-    near_kv = [own, shifted(own, 1), shifted(own, 2)]
     backs = range(4, ctx_size, 2)
     pairs = [shifted(pair, s) for s in backs]
     third = lax.ppermute(pair, "ctx", [(r, r + 3) for r in range(0, ctx_size - 3, 2)])
+    slots = [(2, 2)] + [(s, s) for s in backs] + [(NOWHERE, 3)] + [(s - 1, s + 1) for s in backs]
+    table, own_copy = tables(ctx, vertical, slash, own, slots)
+    own = hold(own, [*pairs, third, table])
+    near_kv = [own_copy, shifted(own, 1), shifted(own, 2)]
     pairs += [third] + [swapped(x) for x in pairs]
-    slots = [(2, 2)] + [(s, s) for s in backs] + [(NOWHERE, 3)] + [(s - 1, s + 1) for s in backs]
 
     def sibling(x):
         return lax.ppermute(x, "tp", [(j, j ^ 1) for j in range(4)])
@@ -395,24 +436,25 @@
         return lax.ppermute(x, "tp", [(j, j ^ 2) for j in range(4)])
 
     def attention(flips, tiles, after):
+        sizes = (vertical.shape[1], slash.shape[1])
         return attend(
-            flips, tp, ctx, queries, vertical, slash, near_kv, pairs, slots, out_weight, tiles, after
+            flips, tp, ctx, queries, table, near_kv, pairs, slots, sizes, out_weight, tiles, after
         )
 
     width = out_weight.shape[1]
     tiles = width // TILE
+    assert HEAD + sum(REST) == tiles
     attended, send, keep = attention((3, 2), HEAD, ())
     total = (keep.astype(jnp.float32) + sibling(send).astype(jnp.float32)).astype(keep.dtype)
     arrived = [across(total)]
-    send, keep = project(attended, out_weight, HEAD, tiles - HEAD, (total,))
+    send, keep = project(attended, out_weight, HEAD, REST, (total,))
     total = add(keep, [sibling(x) for x in send])
     arrived.append(across(total))
     (attended,) = attention((1, 0), 0, (total,))
-    send, keep = project(attended, out_weight, 0, tiles, (arrived[0],))
+    send, keep = project(attended, out_weight, 0, (1,) * tiles, (arrived[0],))
     got = [sibling(x) for x in send]
-    cut = HEAD // PIECE
-    out = finish(keep[:cut], got[:cut], arrived[0], 0, width, None)
-    return finish(keep[cut:], got[cut:], arrived[1], HEAD, width, out)
+    out = finish(keep[:HEAD], got[:HEAD], arrived[0], 0, width, None)
+    return finish(keep[HEAD:], got[HEAD:], arrived[1], HEAD, width, out)
 
 
 def solution(mesh):

time: 90.7 us -> 92.8 us (1.023)
  the two profiles are of different devices: /device:TPU:0 before, /device:TPU:16 now
where the time goes in v10:
time: 92.8 us; the launch traced here: 92.4 us
  Pallas kernels  34.7 us (37%)
  waiting for transfers between devices  33 us (36%)
  starting transfers between devices  19.8 us (21%)
  local copies, waits for them, and re-layouts  4.35 us (5%)
    ppermute x2, waiting for transfers between devices, across(): return lax.ppermute(x, 'tp', [(j, j ^ 2) for j in range(4)])  16.1 us
    pallas_call x2, Pallas kernels, attend(): pl.pallas_call(functools.partial(attend_kernel, slots, tiles, sizes, flip...  15.5 us
    pallas_call x2, Pallas kernels, project(): pl.pallas_call(functools.partial(project_kernel, first, sizes), out_shape...  13.6 us
    ppermute x4, starting transfers between devices, shifted(): return lax.ppermute(x, 'ctx', [(r, r + by) for r in range(ctx_size - by)])  8.31 us
    ppermute x2, waiting for transfers between devices, swapped(): return lax.ppermute(x, 'ctx', [(r, r ^ 1) for r in range(ctx_size)])  7.94 us
    ppermute x13, waiting for transfers between devices, sibling(): return lax.ppermute(x, 'tp', [(j, j ^ 1) for j in range(4)])  5.51 us
    ppermute x1, starting transfers between devices, shards(): lax.ppermute(pair, 'ctx', [(r, r + 3) for r in range(0, ctx_size - 3, 2)])  4.43 us
    unnamed x14, local copies, waits for them, and re-layouts  4.35 us
  transfers between devices with their start and end apart: 22, of which 14 were waited for; matrix products, arithmetic and copies ran while one was open for 0% of the time, Pallas kernels for 24%

profile of v10, /device:TPU:16, one launch (start us, length us, event | category | flops | bytes accessed | tf_op | source)
XLA Modules:
  0.0 92.4 jit_solution(8072976215806005546)
XLA Ops:
  0.0 2.0 %pick.1 = (bf16[512,256]{1,0:T(8,128)(2,1)}, bf16[128,256]{1,0:T(8,128)(2,1)}) custom-call(s32[1]{0:T(128)} %bitcast.1.rank_ref.ctx_ref, s32[8,16]{1,0:T(8,128)} %vert_ref.3, bf16[512,128]{1,0:T(8,128)(2,1)} %k_ref.1, bf16[512,128]{1,0:T(8,128)(2,1)} %v_ref.1), custom_call_target="tpu_custom_call" | custom-call | tf_op jit(solution)/shard_map/pick/pallas_call | solution.py:64
  2.0 4.4 %collective-permute-start.2 = (bf16[128,256]{1,0:T(8,128)(2,1)}, bf16[128,256]{1,0:T(8,128)(2,1)S(1)}, u32[]{:S(2)}, u32[]{:S(2)}) collective-permute-start(bf16[128,256]{1,0:T(8,128)(2,1)} %get-tuple-element.39), channel_id=1, source_target_pairs={{0,12},{8,20},{16,28},{1,13},{9,21},{17,29},{2,14},{10,22},{18,30}... | collective-permute-start | bytes 196616 | tf_op jit(solution)/shard_map/ppermute | solution.py:425
  6.4 0.7 collective-permute-start.1
  7.1 1.3 %collective-permute-start = (bf16[128,256]{1,0:T(8,128)(2,1)}, bf16[128,256]{1,0:T(8,128)(2,1)S(1)}, u32[]{:S(2)}, u32[]{:S(2)}) collective-permute-start(bf16[128,256]{1,0:T(8,128)(2,1)} %get-tuple-element.39), channel_id=1, source_target_pairs={{0,16},{4,20},{8,24},{12,28},{1,17},{5,21},{9,25},{13,29},{2,18},{... | collective-permute-start | bytes 196616 | tf_op jit(solution)/shard_map/ppermute | solution.py:417
  8.4 0.7 copy-done.5
  9.1 0.7 copy-done.6
  9.8 1.1 %tables.1 = (s32[3,8,128]{2,1,0:T(8,128)S(1)}, bf16[512,256]{1,0:T(8,128)(2,1)S(1)}) custom-call(s32[1]{0:T(128)} %bitcast.1.rank_ref.ctx_ref, s32[8,16]{1,0:T(8,128)S(1)} %copy-done.5, s32[8,8]{1,0:T(8,128)S(1)} %copy-done.6, bf16[512,256]{1,0:T(8,128)(2,1)} %get-tuple-element.36.own_ref.refs_0_), custom_call_target="tpu_custom_call" | custom-call | tf_op jit(solution)/shard_map/tables/pallas_call | solution.py:124
  10.9 3.5 %collective-permute-done.refs_1_.refs_0_ = bf16[128,256]{1,0:T(8,128)(2,1)S(1)} collective-permute-done((bf16[128,256]{1,0:T(8,128)(2,1)}, bf16[128,256]{1,0:T(8,128)(2,1)S(1)}, u32[]{:S(2)}, u32[]{:S(2)}) %collective-permute-start) | collective-permute-done | bytes 65568 | tf_op jit(solution)/shard_map/ppermute | solution.py:417
  14.4 1.9 %collective-permute-start.4 = (bf16[512,256]{1,0:T(8,128)(2,1)}, bf16[512,256]{1,0:T(8,128)(2,1)S(1)}, u32[]{:S(2)}, u32[]{:S(2)}) collective-permute-start(bf16[512,256]{1,0:T(8,128)(2,1)} %hold.1), channel_id=1, source_target_pairs={{0,8},{4,12},{8,16},{12,20},{16,24},{20,28},{1,9},{5,13},{9,17},{1... | collective-permute-start | bytes 786440 | tf_op jit(solution)/shard_map/ppermute | solution.py:417
  16.3 4.4 %collective-permute-start.3 = (bf16[512,256]{1,0:T(8,128)(2,1)}, bf16[512,256]{1,0:T(8,128)(2,1)S(1)}, u32[]{:S(2)}, u32[]{:S(2)}) collective-permute-start(bf16[512,256]{1,0:T(8,128)(2,1)} %hold.1), channel_id=1, source_target_pairs={{0,4},{4,8},{8,12},{12,16},{16,20},{20,24},{24,28},{1,5},{5,9},{9,... | collective-permute-start | bytes 786440 | tf_op jit(solution)/shard_map/ppermute | solution.py:417
  20.8 0.1 collective-permute-start.6
  20.8 2.0 %collective-permute-start.5 = (bf16[128,256]{1,0:T(8,128)(2,1)S(1)}, bf16[128,256]{1,0:T(8,128)(2,1)S(1)}, u32[]{:S(2)}, u32[]{:S(2)}) collective-permute-start(bf16[128,256]{1,0:T(8,128)(2,1)S(1)} %collective-permute-done.refs_1_.refs_0_), channel_id=1, source_target_pairs={{0,4},{4,0},{8,12},{12,8},{16,20},{20,16},{24,28},{28,24},{1,5},{5... | collective-permute-start | bytes 196616 | tf_op jit(solution)/shard_map/ppermute | solution.py:420
  22.8 7.2 %collective-permute-done.6.refs_4_ = bf16[128,256]{1,0:T(8,128)(2,1)S(1)} collective-permute-done((bf16[128,256]{1,0:T(8,128)(2,1)S(1)}, bf16[128,256]{1,0:T(8,128)(2,1)S(1)}, u32[]{:S(2)}, u32[]{:S(2)}) %collective-permute-start.6) | collective-permute-done | bytes 65568 | tf_op jit(solution)/shard_map/ppermute | solution.py:420
  30.1 0.7 collective-permute-done.5.refs_3_
  30.8 9.6 %attend.2 = (bf16[256,1024]{1,0:T(8,128)(2,1)S(1)}, bf16[128,4096]{1,0:T(8,128)(2,1)S(1)}, bf16[128,4096]{1,0:T(8,128)(2,1)S(1)}) custom-call(s32[1]{0:T(128)} %bitcast.tp_ref, s32[1]{0:T(128)} %bitcast.1.rank_ref.ctx_ref, bf16[512,1024]{1,0:T(8,128)(2,1)} %q_ref.3, s32[3,8,128]{2,1,0:T(8,128)S(1)} %get-tuple-element.37.refs_4_.table_ref, ...), custom_call_target="tpu_custom_call" | custom-call | tf_op jit(solution)/shard_map/attend/pallas_call | solution.py:279
  40.5 2.6 %collective-permute-done.7 = bf16[128,4096]{1,0:T(8,128)(2,1)S(1)} collective-permute-done((bf16[128,4096]{1,0:T(8,128)(2,1)S(1)}, bf16[128,4096]{1,0:T(8,128)(2,1)S(1)}, u32[]{:S(2)}, u32[]{:S(2)}) %collective-permute-start.7) | collective-permute-done | bytes 1048608 | tf_op jit(solution)/shard_map/ppermute | solution.py:433
  43.1 0.2 add_convert_fusion.refs_0_
  43.4 1.6 %collective-permute-start.12 = (bf16[128,4096]{1,0:T(8,128)(2,1)S(1)}, bf16[128,4096]{1,0:T(8,128)(2,1)S(1)}, u32[]{:S(2)}, u32[]{:S(2)}) collective-permute-start(bf16[128,4096]{1,0:T(8,128)(2,1)S(1)} %add_convert_fusion.refs_0_), channel_id=1, source_target_pairs={{0,2},{1,3},{2,0},{3,1},{4,6},{5,7},{6,4},{7,5},{8,10},{9,11},{10,... | collective-permute-start | bytes 3145736 | tf_op jit(solution)/shard_map/ppermute | solution.py:436
  44.9 4.5 %project.2 = (bf16[128,1024]{1,0:T(8,128)(2,1)S(1)}, bf16[128,1024]{1,0:T(8,128)(2,1)S(1)}, bf16[128,1024]{1,0:T(8,128)(2,1)S(1)}, bf16[128,1024]{1,0:T(8,128)(2...) custom-call(bf16[256,1024]{1,0:T(8,128)(2,1)S(1)} %get-tuple-element, ...), custom_call_target="tpu_custom_call" | custom-call | tf_op jit(solution)/shard_map/project/pallas_call | solution.py:335
  49.5 0.5 collective-permute-start.9
  50.0 0.1 collective-permute-start.10
  50.1 0.4 collective-permute-start.11
  50.5 0.5 collective-permute-done.8.refs_4_
  51.0 0.4 collective-permute-done.9.refs_5_
  51.4 0.4 collective-permute-done.10.refs_6_
  51.8 0.4 collective-permute-done.11.refs_7_
  52.2 0.3 add.6.refs_6_
  52.4 0.6 collective-permute-start.17
  53.0 5.9 %attend.3.a_ref = bf16[256,1024]{1,0:T(8,128)(2,1)S(1)} custom-call(s32[1]{0:T(128)} %bitcast.tp_ref, s32[1]{0:T(128)} %bitcast.1.rank_ref.ctx_ref, bf16[512,1024]{1,0:T(8,128)(2,1)S(1)} %copy-done.2, s32[3,8,128]{2,1,0:T(8,128)S(1)} %get-tuple-element.37.refs_4_.table_ref, bf16[512,256]{1,0:T(8,128)(2,1)S(1)} %get-tuple-element.38.own, ...), custom_call_target="tpu_custom_call" | custom-call | tf_op jit(solution)/shard_map/attend/pallas_call | solution.py:279
  58.9 0.8 copy-done.3
  59.7 9.7 %collective-permute-done.12.refs_0_.refs_8_ = bf16[128,4096]{1,0:T(8,128)(2,1)S(1)} collective-permute-done((bf16[128,4096]{1,0:T(8,128)(2,1)S(1)}, bf16[128,4096]{1,0:T(8,128)(2,1)S(1)}, u32[]{:S(2)}, u32[]{:S(2)}) %collective-permute-start.12) | collective-permute-done | bytes 1048608 | tf_op jit(solution)/shard_map/ppermute | solution.py:436
  69.4 1.0 %copy-done = bf16[128,4096]{1,0:T(8,128)(2,1)} copy-done((bf16[128,4096]{1,0:T(8,128)(2,1)}, bf16[128,4096]{1,0:T(8,128)(2,1)S(1)}, u32[]{:S(2)}) %copy-start) | copy-done | bytes 1048600
  70.4 9.1 %project.3 = (bf16[128,1024]{1,0:T(8,128)(2,1)S(1)}, bf16[128,1024]{1,0:T(8,128)(2,1)S(1)}, bf16[128,1024]{1,0:T(8,128)(2,1)S(1)}, bf16[128,1024]{1,0:T(8,128)(2...) custom-call(bf16[256,1024]{1,0:T(8,128)(2,1)} %copy-done.3, ...), custom_call_target="tpu_custom_call" | custom-call | tf_op jit(solution)/shard_map/project/pallas_call | solution.py:335
  79.6 0.5 collective-permute-start.19
  80.1 0.1 collective-permute-start.20
  80.2 0.4 collective-permute-start.21
  80.6 0.5 collective-permute-done.18.refs_4_
  81.1 0.1 collective-permute-start.13
  81.3 0.2 collective-permute-done.19.refs_5_
  81.5 0.1 collective-permute-start.14
  81.7 0.2 collective-permute-done.20.refs_6_
  81.9 0.1 collective-permute-start.15
  82.0 0.2 collective-permute-done.21.refs_7_
  82.3 0.1 collective-permute-start.16
  82.4 1.2 %copy-done.1 = bf16[128,4096]{1,0:T(8,128)(2,1)S(1)} copy-done((bf16[128,4096]{1,0:T(8,128)(2,1)S(1)}, bf16[128,4096]{1,0:T(8,128)(2,1)}, u32[]{:S(2)}) %copy-start.1) | copy-done | bytes 1048600
  83.6 1.1 %finish.2.refs_9_ = bf16[128,8192]{1,0:T(8,128)(2,1)} custom-call(bf16[128,1024]{1,0:T(8,128)(2,1)S(1)} %get-tuple-element.59.refs_0_, bf16[128,1024]{1,0:T(8,128)(2,1)S(1)} %get-tuple-element.60.refs_1_, bf16[128,1024]{1,0:T(8,128)(2,1)S(1)} %get-tuple-element.61.refs_2_, bf16[128,1024]{1,0:T(8,128)(2,1)S(1)} %get-tuple-element.62.refs_3_, ...), custom_call_target="tpu_custom_call" | custom-call | tf_op jit(solution)/shard_map/finish/pallas_call | solution.py:394
  84.8 6.3 %collective-permute-done.17.refs_8_ = bf16[128,4096]{1,0:T(8,128)(2,1)S(1)} collective-permute-done((bf16[128,4096]{1,0:T(8,128)(2,1)S(1)}, bf16[128,4096]{1,0:T(8,128)(2,1)S(1)}, u32[]{:S(2)}, u32[]{:S(2)}) %collective-permute-start.17) | collective-permute-done | bytes 1048608 | tf_op jit(solution)/shard_map/ppermute | solution.py:436
  91.1 1.1 %finish.3 = bf16[128,8192]{1,0:T(8,128)(2,1)} custom-call(bf16[128,1024]{1,0:T(8,128)(2,1)S(1)} %get-tuple-element.51.refs_0_, bf16[128,1024]{1,0:T(8,128)(2,1)S(1)} %get-tuple-element.52.refs_1_, bf16[128,1024]{1,0:T(8,128)(2,1)S(1)} %get-tuple-element.53.refs_2_, bf16[128,1024]{1,0:T(8,128)(2,1)S(1)} %copy-done.4, ...), custom_call_target="tpu_custom_call", output_to_operand_aliasing={{}: (9, {})} | custom-call | tf_op jit(solution)/shard_map/finish/pallas_call | solution.py:394
  (21 shorter events, 0.3 us)
Async XLA Ops:
  2.0 8.9 %collective-permute-start.2 = (bf16[128,256]{1,0:T(8,128)(2,1)}, bf16[128,256]{1,0:T(8,128)(2,1)S(1)}, u32[]{:S(2)}, u32[]{:S(2)}) collective-permute-start(bf16[128,256]{1,0:T(8,128)(2,1)} %get-tuple-element.39), channel_id=1, source_target_pairs={{0,12},{8,20},{16,28},{1,13},{9,21},{17,29},{2,14},{10,22},{18,30}... | collective-permute-start | bytes 196616 | tf_op jit(solution)/shard_map/ppermute | solution.py:425
  6.4 4.5 %collective-permute-start.1 = (bf16[128,256]{1,0:T(8,128)(2,1)}, bf16[128,256]{1,0:T(8,128)(2,1)S(1)}, u32[]{:S(2)}, u32[]{:S(2)}) collective-permute-start(bf16[128,256]{1,0:T(8,128)(2,1)} %get-tuple-element.39), channel_id=1, source_target_pairs={{0,24},{4,28},{1,25},{5,29},{2,26},{6,30},{3,27},{7,31}} | collective-permute-start | bytes 196616 | tf_op jit(solution)/shard_map/ppermute | solution.py:417
  7.1 7.3 %collective-permute-start = (bf16[128,256]{1,0:T(8,128)(2,1)}, bf16[128,256]{1,0:T(8,128)(2,1)S(1)}, u32[]{:S(2)}, u32[]{:S(2)}) collective-permute-start(bf16[128,256]{1,0:T(8,128)(2,1)} %get-tuple-element.39), channel_id=1, source_target_pairs={{0,16},{4,20},{8,24},{12,28},{1,17},{5,21},{9,25},{13,29},{2,18},{... | collective-permute-start | bytes 196616 | tf_op jit(solution)/shard_map/ppermute | solution.py:417
  8.4 0.7 copy-start.5
  9.1 0.7 copy-start.6
  14.4 16.4 %collective-permute-start.4 = (bf16[512,256]{1,0:T(8,128)(2,1)}, bf16[512,256]{1,0:T(8,128)(2,1)S(1)}, u32[]{:S(2)}, u32[]{:S(2)}) collective-permute-start(bf16[512,256]{1,0:T(8,128)(2,1)} %hold.1), channel_id=1, source_target_pairs={{0,8},{4,12},{8,16},{12,20},{16,24},{20,28},{1,9},{5,13},{9,17},{1... | collective-permute-start | bytes 786440 | tf_op jit(solution)/shard_map/ppermute | solution.py:417
  16.3 14.5 %collective-permute-start.3 = (bf16[512,256]{1,0:T(8,128)(2,1)}, bf16[512,256]{1,0:T(8,128)(2,1)S(1)}, u32[]{:S(2)}, u32[]{:S(2)}) collective-permute-start(bf16[512,256]{1,0:T(8,128)(2,1)} %hold.1), channel_id=1, source_target_pairs={{0,4},{4,8},{8,12},{12,16},{16,20},{20,24},{24,28},{1,5},{5,9},{9,... | collective-permute-start | bytes 786440 | tf_op jit(solution)/shard_map/ppermute | solution.py:417
  20.8 9.3 %collective-permute-start.6 = (bf16[128,256]{1,0:T(8,128)(2,1)S(1)}, bf16[128,256]{1,0:T(8,128)(2,1)S(1)}, u32[]{:S(2)}, u32[]{:S(2)}) collective-permute-start(bf16[128,256]{1,0:T(8,128)(2,1)S(1)} %collective-permute-done.1.refs_2_.refs_1_), channel_id=1, source_target_pairs={{0,4},{4,0},{8,12},{12,8},{16,20},{20,16},{24,28},{28,24},{1,5},{5... | collective-permute-start | bytes 196616 | tf_op jit(solution)/shard_map/ppermute | solution.py:420
  20.8 10.0 %collective-permute-start.5 = (bf16[128,256]{1,0:T(8,128)(2,1)S(1)}, bf16[128,256]{1,0:T(8,128)(2,1)S(1)}, u32[]{:S(2)}, u32[]{:S(2)}) collective-permute-start(bf16[128,256]{1,0:T(8,128)(2,1)S(1)} %collective-permute-done.refs_1_.refs_0_), channel_id=1, source_target_pairs={{0,4},{4,0},{8,12},{12,8},{16,20},{20,16},{24,28},{28,24},{1,5},{5... | collective-permute-start | bytes 196616 | tf_op jit(solution)/shard_map/ppermute | solution.py:420
  40.4 2.7 %collective-permute-start.7 = (bf16[128,4096]{1,0:T(8,128)(2,1)S(1)}, bf16[128,4096]{1,0:T(8,128)(2,1)S(1)}, u32[]{:S(2)}, u32[]{:S(2)}) collective-permute-start(bf16[128,4096]{1,0:T(8,128)(2,1)S(1)} %get-tuple-element.42), channel_id=1, source_target_pairs={{0,1},{1,0},{2,3},{3,2},{4,5},{5,4},{6,7},{7,6},{8,9},{9,8},{10,11... | collective-permute-start | bytes 3145736 | tf_op jit(solution)/shard_map/ppermute | solution.py:433
  43.4 26.1 %collective-permute-start.12 = (bf16[128,4096]{1,0:T(8,128)(2,1)S(1)}, bf16[128,4096]{1,0:T(8,128)(2,1)S(1)}, u32[]{:S(2)}, u32[]{:S(2)}) collective-permute-start(bf16[128,4096]{1,0:T(8,128)(2,1)S(1)} %add_convert_fusion.refs_0_), channel_id=1, source_target_pairs={{0,2},{1,3},{2,0},{3,1},{4,6},{5,7},{6,4},{7,5},{8,10},{9,11},{10,... | collective-permute-start | bytes 3145736 | tf_op jit(solution)/shard_map/ppermute | solution.py:436
  49.4 3.6 %copy-start.2 = (bf16[512,1024]{1,0:T(8,128)(2,1)S(1)}, bf16[512,1024]{1,0:T(8,128)(2,1)}, u32[]{:S(2)}) copy-start(bf16[512,1024]{1,0:T(8,128)(2,1)} %q_ref.3) | copy-start | bytes 3145732
  49.4 1.6 %collective-permute-start.8 = (bf16[128,1024]{1,0:T(8,128)(2,1)S(1)}, bf16[128,1024]{1,0:T(8,128)(2,1)S(1)}, u32[]{:S(2)}, u32[]{:S(2)}) collective-permute-start(bf16[128,1024]{1,0:T(8,128)(2,1)S(1)} %get-tuple-element.47), channel_id=1, source_target_pairs={{0,1},{1,0},{2,3},{3,2},{4,5},{5,4},{6,7},{7,6},{8,9},{9,8},{10,11... | collective-permute-start | bytes 786440 | tf_op jit(solution)/shard_map/ppermute | solution.py:433
  49.5 1.9 %collective-permute-start.9 = (bf16[128,1024]{1,0:T(8,128)(2,1)S(1)}, bf16[128,1024]{1,0:T(8,128)(2,1)S(1)}, u32[]{:S(2)}, u32[]{:S(2)}) collective-permute-start(bf16[128,1024]{1,0:T(8,128)(2,1)S(1)} %get-tuple-element.48), channel_id=1, source_target_pairs={{0,1},{1,0},{2,3},{3,2},{4,5},{5,4},{6,7},{7,6},{8,9},{9,8},{10,11... | collective-permute-start | bytes 786440 | tf_op jit(solution)/shard_map/ppermute | solution.py:433
  50.0 1.8 %collective-permute-start.10 = (bf16[128,1024]{1,0:T(8,128)(2,1)S(1)}, bf16[128,1024]{1,0:T(8,128)(2,1)S(1)}, u32[]{:S(2)}, u32[]{:S(2)}) collective-permute-start(bf16[128,1024]{1,0:T(8,128)(2,1)S(1)} %get-tuple-element.49), channel_id=1, source_target_pairs={{0,1},{1,0},{2,3},{3,2},{4,5},{5,4},{6,7},{7,6},{8,9},{9,8},{10,11... | collective-permute-start | bytes 786440 | tf_op jit(solution)/shard_map/ppermute | solution.py:433
  50.1 2.1 %collective-permute-start.11 = (bf16[128,1024]{1,0:T(8,128)(2,1)S(1)}, bf16[128,1024]{1,0:T(8,128)(2,1)S(1)}, u32[]{:S(2)}, u32[]{:S(2)}) collective-permute-start(bf16[128,1024]{1,0:T(8,128)(2,1)S(1)} %get-tuple-element.50), channel_id=1, source_target_pairs={{0,1},{1,0},{2,3},{3,2},{4,5},{5,4},{6,7},{7,6},{8,9},{9,8},{10,11... | collective-permute-start | bytes 786440 | tf_op jit(solution)/shard_map/ppermute | solution.py:433
  52.4 38.7 %collective-permute-start.17 = (bf16[128,4096]{1,0:T(8,128)(2,1)S(1)}, bf16[128,4096]{1,0:T(8,128)(2,1)S(1)}, u32[]{:S(2)}, u32[]{:S(2)}) collective-permute-start(bf16[128,4096]{1,0:T(8,128)(2,1)S(1)} %add.6.refs_6_), channel_id=1, source_target_pairs={{0,2},{1,3},{2,0},{3,1},{4,6},{5,7},{6,4},{7,5},{8,10},{9,11},{10,... | collective-permute-start | bytes 3145736 | tf_op jit(solution)/shard_map/ppermute | solution.py:436
  58.9 0.8 copy-start.3
  69.4 1.0 %copy-start = (bf16[128,4096]{1,0:T(8,128)(2,1)}, bf16[128,4096]{1,0:T(8,128)(2,1)S(1)}, u32[]{:S(2)}) copy-start(bf16[128,4096]{1,0:T(8,128)(2,1)S(1)} %collective-permute-done.12.refs_0_.refs_8_) | copy-start | bytes 3145732
  79.5 1.6 %collective-permute-start.18 = (bf16[128,1024]{1,0:T(8,128)(2,1)S(1)}, bf16[128,1024]{1,0:T(8,128)(2,1)S(1)}, u32[]{:S(2)}, u32[]{:S(2)}) collective-permute-start(bf16[128,1024]{1,0:T(8,128)(2,1)S(1)} %get-tuple-element.63), channel_id=1, source_target_pairs={{0,1},{1,0},{2,3},{3,2},{4,5},{5,4},{6,7},{7,6},{8,9},{9,8},{10,11... | collective-permute-start | bytes 786440 | tf_op jit(solution)/shard_map/ppermute | solution.py:433
  79.6 1.9 %collective-permute-start.19 = (bf16[128,1024]{1,0:T(8,128)(2,1)S(1)}, bf16[128,1024]{1,0:T(8,128)(2,1)S(1)}, u32[]{:S(2)}, u32[]{:S(2)}) collective-permute-start(bf16[128,1024]{1,0:T(8,128)(2,1)S(1)} %get-tuple-element.64), channel_id=1, source_target_pairs={{0,1},{1,0},{2,3},{3,2},{4,5},{5,4},{6,7},{7,6},{8,9},{9,8},{10,11... | collective-permute-start | bytes 786440 | tf_op jit(solution)/shard_map/ppermute | solution.py:433
  80.1 1.8 %collective-permute-start.20 = (bf16[128,1024]{1,0:T(8,128)(2,1)S(1)}, bf16[128,1024]{1,0:T(8,128)(2,1)S(1)}, u32[]{:S(2)}, u32[]{:S(2)}) collective-permute-start(bf16[128,1024]{1,0:T(8,128)(2,1)S(1)} %get-tuple-element.65), channel_id=1, source_target_pairs={{0,1},{1,0},{2,3},{3,2},{4,5},{5,4},{6,7},{7,6},{8,9},{9,8},{10,11... | collective-permute-start | bytes 786440 | tf_op jit(solution)/shard_map/ppermute | solution.py:433
  80.2 2.1 %collective-permute-start.21 = (bf16[128,1024]{1,0:T(8,128)(2,1)S(1)}, bf16[128,1024]{1,0:T(8,128)(2,1)S(1)}, u32[]{:S(2)}, u32[]{:S(2)}) collective-permute-start(bf16[128,1024]{1,0:T(8,128)(2,1)S(1)} %get-tuple-element.66), channel_id=1, source_target_pairs={{0,1},{1,0},{2,3},{3,2},{4,5},{5,4},{6,7},{7,6},{8,9},{9,8},{10,11... | collective-permute-start | bytes 786440 | tf_op jit(solution)/shard_map/ppermute | solution.py:433
  81.1 3.6 %collective-permute-start.13 = (bf16[128,1024]{1,0:T(8,128)(2,1)S(1)}, bf16[128,1024]{1,0:T(8,128)(2,1)S(1)}, u32[]{:S(2)}, u32[]{:S(2)}) collective-permute-start(bf16[128,1024]{1,0:T(8,128)(2,1)S(1)} %get-tuple-element.55), channel_id=1, source_target_pairs={{0,1},{1,0},{2,3},{3,2},{4,5},{5,4},{6,7},{7,6},{8,9},{9,8},{10,11... | collective-permute-start | bytes 786440 | tf_op jit(solution)/shard_map/ppermute | solution.py:433
  81.5 3.2 %collective-permute-start.14 = (bf16[128,1024]{1,0:T(8,128)(2,1)S(1)}, bf16[128,1024]{1,0:T(8,128)(2,1)S(1)}, u32[]{:S(2)}, u32[]{:S(2)}) collective-permute-start(bf16[128,1024]{1,0:T(8,128)(2,1)S(1)} %get-tuple-element.56), channel_id=1, source_target_pairs={{0,1},{1,0},{2,3},{3,2},{4,5},{5,4},{6,7},{7,6},{8,9},{9,8},{10,11... | collective-permute-start | bytes 786440 | tf_op jit(solution)/shard_map/ppermute | solution.py:433
  81.9 2.9 %collective-permute-start.15 = (bf16[128,1024]{1,0:T(8,128)(2,1)S(1)}, bf16[128,1024]{1,0:T(8,128)(2,1)S(1)}, u32[]{:S(2)}, u32[]{:S(2)}) collective-permute-start(bf16[128,1024]{1,0:T(8,128)(2,1)S(1)} %get-tuple-element.57), channel_id=1, source_target_pairs={{0,1},{1,0},{2,3},{3,2},{4,5},{5,4},{6,7},{7,6},{8,9},{9,8},{10,11... | collective-permute-start | bytes 786440 | tf_op jit(solution)/shard_map/ppermute | solution.py:433
  82.3 2.5 %collective-permute-start.16 = (bf16[128,1024]{1,0:T(8,128)(2,1)S(1)}, bf16[128,1024]{1,0:T(8,128)(2,1)S(1)}, u32[]{:S(2)}, u32[]{:S(2)}) collective-permute-start(bf16[128,1024]{1,0:T(8,128)(2,1)S(1)} %get-tuple-element.58), channel_id=1, source_target_pairs={{0,1},{1,0},{2,3},{3,2},{4,5},{5,4},{6,7},{7,6},{8,9},{9,8},{10,11... | collective-permute-start | bytes 786440 | tf_op jit(solution)/shard_map/ppermute | solution.py:433
  82.4 1.2 %copy-start.1 = (bf16[128,4096]{1,0:T(8,128)(2,1)S(1)}, bf16[128,4096]{1,0:T(8,128)(2,1)}, u32[]{:S(2)}) copy-start(bf16[128,4096]{1,0:T(8,128)(2,1)} %copy-done) | copy-start | bytes 3145732
  83.6 7.5 %copy-start.4 = (bf16[128,1024]{1,0:T(8,128)(2,1)S(1)}, bf16[128,1024]{1,0:T(8,128)(2,1)}, u32[]{:S(2)}) copy-start(bf16[128,1024]{1,0:T(8,128)(2,1)} %get-tuple-element.54.refs_3_) | copy-start | bytes 786436

commit v11 on v10

--- a/solution.py
+++ b/solution.py
@@ -13,12 +13,10 @@
 VMOST = 2
 NEAR = 3
 LANES = 128
-NOWHERE = 1 << 20
 MASKED = -1e30
 EXP_SCALE = 1.4426950408889634 / (HS**0.5)
 TILE = 1024
-HEAD = 4
-REST = (1, 1, 1, 1)
+ACROSS = (3, 4, 1)
 MIB = 1024 * 1024
 
 
@@ -57,15 +55,17 @@
     both_ref[:, HS:] = v_ref[...]
     blocks = picked_blocks(vert_ref[...], rank_ref[0], k_ref.shape[0] // BLK)
     for slot, rows in enumerate(blocks):
-        pair_ref[slot * BLK : (slot + 1) * BLK, :] = both_ref[rows, :]
-
-
-def pick(rank, vertical, keys, values):
+        picked = both_ref[rows, :]
+        for copy in range(pair_ref.shape[0]):
+            pair_ref[copy, slot * BLK : (slot + 1) * BLK, :] = picked
+
+
+def pick(rank, vertical, keys, values, copies):
     return pl.pallas_call(
         pick_kernel,
         out_shape=(
             jax.ShapeDtypeStruct((keys.shape[0], 2 * HS), keys.dtype),
-            jax.ShapeDtypeStruct((VMOST * BLK, 2 * HS), keys.dtype),
+            jax.ShapeDtypeStruct((copies, VMOST * BLK, 2 * HS), keys.dtype),
         ),
         in_specs=[smem(), vmem(), vmem(), vmem()],
         out_specs=(vmem(), vmem()),
@@ -74,19 +74,6 @@
     )(rank, vertical, keys, values)
 
 
-def hold(x, others):
-    return pl.pallas_call(
-        lambda *refs: None,
-        out_shape=jax.ShapeDtypeStruct(x.shape, x.dtype),
-        in_specs=[anywhere() for _ in [x, *others]],
-        out_specs=anywhere(),
-        input_output_aliases={0: 0},
-        compiler_params=params(1),
-        cost_estimate=SHORT,
-        name="hold",
-    )(x, *others)
-
-
 def member(table, blocks):
     found = table[:, :1] == blocks
     for column in range(1, table.shape[1]):
@@ -96,10 +83,9 @@
 
 def pool_blocks(vertical, rank, slots, local_blocks):
     lane = lax.broadcasted_iota(jnp.int32, (vertical.shape[0], LANES), 1)
-    shard = jnp.full(lane.shape, -1, jnp.int32)
-    for slot, (even, odd) in enumerate(slots):
-        back = jnp.where(rank & 1 == 1, odd, even)
-        shard = jnp.where(lane // VMOST == slot, rank - back, shard)
+    slot = lane // VMOST
+    shard = jnp.where(slot < slots, 2 * slot + (rank & 1), 2 * (slot - slots) + 1 - (rank & 1))
+    shard = jnp.where(slot < 2 * slots, shard, -1)
     first = jnp.full((1, LANES), local_blocks, jnp.int32)
     second = first
     for j in reversed(range(local_blocks)):
@@ -138,8 +124,8 @@
 def attend_kernel(
     slots, tiles, sizes, flips, tp_ref, ctx_ref, q_ref, table_ref, own, kv_1, kv_2, *refs
 ):
-    pairs = refs[: len(slots) - 1]
-    w_hbm = refs[len(slots) - 1]
+    pairs = refs[:2]
+    w_hbm = refs[2]
     kv_win, e_win, kv_pool, e_pool, attended, weight, arrival, landed = refs[-8:]
     outs = refs[-11:-8] if tiles else refs[-9:-8]
     step = pl.program_id(0)
@@ -147,7 +133,7 @@
     rows = own.shape[0]
     local_blocks = rows // BLK
     quarter = local_blocks // 4
-    pair_rows = VMOST * BLK
+    far_rows = e_pool.shape[0]
     dtype = q_ref.dtype
     rank = ctx_ref[0]
     vert = table_ref[0][:, : sizes[0]]
@@ -167,9 +153,9 @@
         ]
         copies += [
             pltpu.make_async_copy(
-                x, kv_pool.at[pl.ds((s + 1) * pair_rows, pair_rows), :], landed.at[NEAR + s]
+                x.at[pl.ds(0, slots)], kv_pool.at[pl.ds(p * slots, slots)], landed.at[NEAR + p]
             )
-            for s, x in enumerate(pairs)
+            for p, x in enumerate(pairs)
         ]
         for copy in copies:
             copy.start()
@@ -182,11 +168,8 @@
         key = lax.broadcasted_iota(jnp.int32, e_pool.shape, 0)
         lane = lax.broadcasted_iota(jnp.int32, e_pool.shape, 1)
         e_pool[...] = jnp.where(key // BLK == lane, 1.0, 0.0).astype(dtype)
-        picked = picked_blocks(vert, rank - (NEAR - 1), local_blocks)
         for copy in copies:
             copy.wait()
-        for slot, block in enumerate(picked):
-            kv_pool[slot * BLK : (slot + 1) * BLK, :] = kv_win[block, :]
 
     owner = tp_ref[0] ^ jnp.where(step == 0, flips[0], flips[1])
     lane = lax.broadcasted_iota(jnp.int32, (heads, LANES), 1)
@@ -227,11 +210,11 @@
         )
     far = lax.dot_general(
         jnp.concatenate(far_q, axis=0),
-        jnp.concatenate([kv_pool[:, :HS], e_pool[...]], axis=1),
+        jnp.concatenate([kv_pool[:, :, :HS].reshape(far_rows, HS), e_pool[...]], axis=1),
         contract,
         preferred_element_type=jnp.float32,
     )
-    far_values = with_ones(kv_pool[:, HS:])
+    far_values = with_ones(kv_pool[:, :, HS:].reshape(far_rows, HS))
     for u in range(quarter):
         far_u = far[u * heads * BLK : (u + 1) * heads * BLK]
         top = jnp.maximum(
@@ -259,13 +242,14 @@
             outs[2][:, t * TILE : (t + 1) * TILE] = product[half:]
 
 
-def attend(flips, tp, ctx, queries, table, near_kv, pairs, slots, sizes, out_weight, tiles, after):
+def attend(flips, tp, ctx, queries, table, near_kv, pairs, sizes, out_weight, tiles, after):
     width = queries.shape[1]
     rows = near_kv[0].shape[0]
     quarter = rows // 4
     steps = len(flips)
+    slots = pairs[1].shape[0]
     dtype = queries.dtype
-    far = len(slots) * VMOST * BLK
+    far = 2 * slots * VMOST * BLK
 
     def place(g, tp, ctx):
         return (tp[0] ^ jnp.where(g == 0, flips[0], flips[1]), 0)
@@ -289,12 +273,12 @@
             scratch_shapes=[
                 pltpu.VMEM((NEAR * rows, 2 * HS), dtype),
                 pltpu.VMEM((SPAN * BLK, LANES), dtype),
-                pltpu.VMEM((far, 2 * HS), dtype),
+                pltpu.VMEM((2 * slots, VMOST * BLK, 2 * HS), dtype),
                 pltpu.VMEM((far, LANES), dtype),
                 pltpu.VMEM((steps * quarter, width), dtype),
                 pltpu.VMEM((max(tiles, 1), out_weight.shape[0], TILE), dtype),
                 pltpu.SemaphoreType.DMA((max(tiles, 1),)),
-                pltpu.SemaphoreType.DMA((NEAR + len(pairs),)),
+                pltpu.SemaphoreType.DMA((NEAR + 2,)),
             ],
         ),
         compiler_params=params(50),
@@ -303,9 +287,10 @@
     )(tp, ctx, queries, table, *near_kv, *pairs, out_weight, *after)
 
 
-def project_kernel(first, sizes, a_ref, w_hbm, *refs):
+def project_kernel(first, a_ref, w_hbm, *refs):
     weight, arrival = refs[-2:]
-    outs = refs[-2 - 2 * len(sizes) : -2]
+    tiles = weight.shape[0]
+    outs = refs[-2 - 2 * tiles : -2]
     half = outs[0].shape[0]
 
     def fetch(t):
@@ -313,39 +298,33 @@
             w_hbm.at[:, pl.ds((first + t) * TILE, TILE)], weight.at[t], arrival.at[t]
         )
 
-    for t in range(sum(sizes)):
+    for t in range(tiles):
         fetch(t).start()
-    t = 0
-    for piece, size in enumerate(sizes):
-        for place in range(size):
-            fetch(t).wait()
-            product = jnp.dot(a_ref[...], weight[t], preferred_element_type=jnp.float32)
-            product = product.astype(a_ref.dtype)
-            at = slice(place * TILE, (place + 1) * TILE)
-            outs[piece][:, at] = product[:half]
-            outs[len(sizes) + piece][:, at] = product[half:]
-            t += 1
-
-
-def project(attended, out_weight, first, sizes, after):
+    for t in range(tiles):
+        fetch(t).wait()
+        product = jnp.dot(a_ref[...], weight[t], preferred_element_type=jnp.float32)
+        product = product.astype(a_ref.dtype)
+        outs[t][...] = product[:half]
+        outs[tiles + t][...] = product[half:]
+
+
+def project(attended, out_weight, first, tiles, after):
     rows, depth = attended.shape
-    parts = [
-        jax.ShapeDtypeStruct((rows // 2, size * TILE), attended.dtype) for size in sizes
-    ]
+    part = jax.ShapeDtypeStruct((rows // 2, TILE), attended.dtype)
     outs = pl.pallas_call(
-        functools.partial(project_kernel, first, sizes),
-        out_shape=parts + parts,
+        functools.partial(project_kernel, first),
+        out_shape=[part] * (2 * tiles),
         in_specs=[vmem(), anywhere()] + [anywhere() for _ in after],
-        out_specs=[vmem()] * (2 * len(sizes)),
+        out_specs=[vmem()] * (2 * tiles),
         scratch_shapes=[
-            pltpu.VMEM((sum(sizes), depth, TILE), attended.dtype),
-            pltpu.SemaphoreType.DMA((sum(sizes),)),
+            pltpu.VMEM((tiles, depth, TILE), attended.dtype),
+            pltpu.SemaphoreType.DMA((tiles,)),
         ],
         compiler_params=params(50),
         cost_estimate=SHORT,
         name="project",
     )(attended, out_weight, *after)
-    return outs[: len(sizes)], outs[len(sizes) :]
+    return outs[:tiles], outs[tiles:]
 
 
 def add_kernel(*refs):
@@ -416,18 +395,14 @@
     def shifted(x, by):
         return lax.ppermute(x, "ctx", [(r, r + by) for r in range(ctx_size - by)])
 
-    def swapped(x):
-        return lax.ppermute(x, "ctx", [(r, r ^ 1) for r in range(ctx_size)])
-
-    own, pair = pick(ctx, vertical, keys, values)
-    backs = range(4, ctx_size, 2)
-    pairs = [shifted(pair, s) for s in backs]
-    third = lax.ppermute(pair, "ctx", [(r, r + 3) for r in range(0, ctx_size - 3, 2)])
-    slots = [(2, 2)] + [(s, s) for s in backs] + [(NOWHERE, 3)] + [(s - 1, s + 1) for s in backs]
-    table, own_copy = tables(ctx, vertical, slash, own, slots)
-    own = hold(own, [*pairs, third, table])
+    half = ctx_size // 2
+    own, pair = pick(ctx, vertical, keys, values, half)
+    parities = [list(range(odd, ctx_size, 2)) for odd in (0, 1)]
+    pairs = [lax.all_to_all(pair, "ctx", 0, 0, axis_index_groups=parities, tiled=True)]
+    needed = pairs[0][: half - 1]
+    pairs.append(lax.ppermute(needed, "ctx", [(r, r ^ 1) for r in range(ctx_size)]))
+    table, own_copy = tables(ctx, vertical, slash, own, half - 1)
     near_kv = [own_copy, shifted(own, 1), shifted(own, 2)]
-    pairs += [third] + [swapped(x) for x in pairs]
 
     def sibling(x):
         return lax.ppermute(x, "tp", [(j, j ^ 1) for j in range(4)])
@@ -438,23 +413,33 @@
     def attention(flips, tiles, after):
         sizes = (vertical.shape[1], slash.shape[1])
         return attend(
-            flips, tp, ctx, queries, table, near_kv, pairs, slots, sizes, out_weight, tiles, after
+            flips, tp, ctx, queries, table, near_kv, pairs, sizes, out_weight, tiles, after
         )
 
     width = out_weight.shape[1]
     tiles = width // TILE
-    assert HEAD + sum(REST) == tiles
-    attended, send, keep = attention((3, 2), HEAD, ())
+    assert sum(ACROSS) == tiles
+    starts = [sum(ACROSS[:n]) for n in range(len(ACROSS))]
+
+    def send_chunk(chunk, after):
+        send, keep = project(attended, out_weight, starts[chunk], ACROSS[chunk], after)
+        return add(keep, [sibling(x) for x in send])
+
+    attended, send, keep = attention((3, 2), ACROSS[0], ())
     total = (keep.astype(jnp.float32) + sibling(send).astype(jnp.float32)).astype(keep.dtype)
     arrived = [across(total)]
-    send, keep = project(attended, out_weight, HEAD, REST, (total,))
-    total = add(keep, [sibling(x) for x in send])
+    total = send_chunk(1, (total,))
     arrived.append(across(total))
-    (attended,) = attention((1, 0), 0, (total,))
-    send, keep = project(attended, out_weight, 0, (1,) * tiles, (arrived[0],))
+    (own_attended,) = attention((1, 0), 0, (total,))
+    total = send_chunk(2, (own_attended,))
+    arrived.append(across(total))
+    send, keep = project(own_attended, out_weight, 0, tiles, (total, arrived[0]))
     got = [sibling(x) for x in send]
-    out = finish(keep[:HEAD], got[:HEAD], arrived[0], 0, width, None)
-    return finish(keep[HEAD:], got[HEAD:], arrived[1], HEAD, width, out)
+    out = None
+    for part, first, count in zip(arrived, starts, ACROSS):
+        at = slice(first, first + count)
+        out = finish(keep[at], got[at], part, first, width, out)
+    return out
 
 
 def solution(mesh):

time: 92.8 us -> 87 us (0.938)
  waiting for transfers between devices: 33 us -> 26 us
  Pallas kernels: 34.7 us -> 35.8 us
    ppermute x3 -> x1, waiting for transfers between devices: 7.94 us -> 0.01 us  [shards(): lax.ppermute(needed, 'ctx', [(r, r ^ 1) for r in range(ctx_size)])]
    ppermute x3 -> x1, starting transfers between devices: 6.52 us -> 0.62 us  [shards(): lax.ppermute(needed, 'ctx', [(r, r ^ 1) for r in range(ctx_size)])]
    ppermute x4 -> x2, waiting for transfers between devices: 3.46 us -> 8.77 us  [shifted(): return lax.ppermute(x, 'ctx', [(r, r + by) for r in range(ctx_size - by)])]
    all_to_all x0 -> x1, starting transfers between devices: none -> 5.2 us  [shards(): lax.all_to_all(pair, 'ctx', 0, 0, axis_index_groups=parities, tiled=True)]
    ppermute x2 -> x3, waiting for transfers between devices: 16.1 us -> 11.2 us  [across(): return lax.ppermute(x, 'tp', [(j, j ^ 2) for j in range(4)])]
    pallas_call x3, Pallas kernels: 13.6 us -> 16.2 us  [project(): pl.pallas_call(functools.partial(project_kernel, first), out_shape=[part]...]
    ppermute x2 -> x3, starting transfers between devices: 2.16 us -> 3.71 us  [across(): return lax.ppermute(x, 'tp', [(j, j ^ 2) for j in range(4)])]
    ppermute x4 -> x2, starting transfers between devices: 8.31 us -> 6.79 us  [shifted(): return lax.ppermute(x, 'ctx', [(r, r + by) for r in range(ctx_size - by)])]
  transfers between devices with their start and end apart: 22 -> 21, of which waited for: 14 -> 14; matrix products, arithmetic and copies ran while one was open for 0% -> 0% of each run, Pallas kernels for 24% -> 28%
where the time goes in v11:
time: 87 us; the launch traced here: 86.6 us
  Pallas kernels  35.8 us (41%)
  waiting for transfers between devices  26 us (30%)
  starting transfers between devices  19.2 us (22%)
  local copies, waits for them, and re-layouts  5.05 us (6%)
    pallas_call x3, Pallas kernels, project(): pl.pallas_call(functools.partial(project_kernel, first), out_shape=[part]...  16.2 us
    pallas_call x2, Pallas kernels, attend(): pl.pallas_call(functools.partial(attend_kernel, slots, tiles, sizes, flip...  14.1 us
    ppermute x3, waiting for transfers between devices, across(): return lax.ppermute(x, 'tp', [(j, j ^ 2) for j in range(4)])  11.2 us
    ppermute x2, waiting for transfers between devices, shifted(): return lax.ppermute(x, 'ctx', [(r, r + by) for r in range(ctx_size - by)])  8.77 us
    ppermute x2, starting transfers between devices, shifted(): return lax.ppermute(x, 'ctx', [(r, r + by) for r in range(ctx_size - by)])  6.79 us
    ppermute x14, waiting for transfers between devices, sibling(): return lax.ppermute(x, 'tp', [(j, j ^ 1) for j in range(4)])  6.03 us
    all_to_all x1, starting transfers between devices, shards(): lax.all_to_all(pair, 'ctx', 0, 0, axis_index_groups=parities, tiled=True)  5.2 us
    unnamed x20, local copies, waits for them, and re-layouts  5.04 us
  transfers between devices with their start and end apart: 21, of which 14 were waited for; matrix products, arithmetic and copies ran while one was open for 0% of the time, Pallas kernels for 28%

profile of v11, /device:TPU:16, one launch (start us, length us, event | category | flops | bytes accessed | tf_op | source)
XLA Modules:
  0.0 86.6 jit_solution(8122387818938238758)
XLA Ops:
  0.0 2.1 %pick.1 = (bf16[512,256]{1,0:T(8,128)(2,1)}, bf16[4,128,256]{2,1,0:T(8,128)(2,1)}) custom-call(s32[1]{0:T(128)} %bitcast.1.rank_ref.ctx_ref, s32[8,16]{1,0:T(8,128)} %vert_ref.3, bf16[512,128]{1,0:T(8,128)(2,1)} %k_ref.1, bf16[512,128]{1,0:T(8,128)(2,1)} %v_ref.1), custom_call_target="tpu_custom_call" | custom-call | tf_op jit(solution)/shard_map/pick/pallas_call | solution.py:64
  2.1 5.2 %all-to-all-start = ((bf16[4,128,256]{2,1,0:T(8,128)(2,1)}), bf16[4,128,256]{2,1,0:T(8,128)(2,1)S(1)}, u32[]{:S(2)}, u32[]{:S(2)}) async-start(bf16[4,128,256]{2,1,0:T(8,128)(2,1)} %get-tuple-element.41), calls=%async_computation | async-start | bytes 524288 | tf_op jit(solution)/shard_map/all_to_all | solution.py:401
  7.3 3.4 %collective-permute-start.1 = (bf16[512,256]{1,0:T(8,128)(2,1)}, bf16[512,256]{1,0:T(8,128)(2,1)S(1)}, u32[]{:S(2)}, u32[]{:S(2)}) collective-permute-start(bf16[512,256]{1,0:T(8,128)(2,1)} %get-tuple-element.38.own_ref), channel_id=1, source_target_pairs={{0,8},{4,12},{8,16},{12,20},{16,24},{20,28},{1,9},{5,13},{9,17},{1... | collective-permute-start | bytes 786440 | tf_op jit(solution)/shard_map/ppermute | solution.py:396
  10.7 3.4 %collective-permute-start = (bf16[512,256]{1,0:T(8,128)(2,1)}, bf16[512,256]{1,0:T(8,128)(2,1)S(1)}, u32[]{:S(2)}, u32[]{:S(2)}) collective-permute-start(bf16[512,256]{1,0:T(8,128)(2,1)} %get-tuple-element.38.own_ref), channel_id=1, source_target_pairs={{0,4},{4,8},{8,12},{12,16},{16,20},{20,24},{24,28},{1,5},{5,9},{9,... | collective-permute-start | bytes 786440 | tf_op jit(solution)/shard_map/ppermute | solution.py:396
  14.1 0.6 collective-permute-start.2
  14.7 0.9 %copy-done.7 = bf16[512,256]{1,0:T(8,128)(2,1)S(1)} copy-done((bf16[512,256]{1,0:T(8,128)(2,1)S(1)}, bf16[512,256]{1,0:T(8,128)(2,1)}, u32[]{:S(2)}) %copy-start.7) | copy-done | bytes 262168
  15.7 0.7 copy-done.8
  16.4 0.7 copy-done.9
  17.1 0.1 tables.1
  17.2 2.2 %collective-permute-done.1.kv_2 = bf16[512,256]{1,0:T(8,128)(2,1)S(1)} collective-permute-done((bf16[512,256]{1,0:T(8,128)(2,1)}, bf16[512,256]{1,0:T(8,128)(2,1)S(1)}, u32[]{:S(2)}, u32[]{:S(2)}) %collective-permute-start.1) | collective-permute-done | bytes 262176 | tf_op jit(solution)/shard_map/ppermute | solution.py:396
  19.4 6.6 %collective-permute-done.kv_1 = bf16[512,256]{1,0:T(8,128)(2,1)S(1)} collective-permute-done((bf16[512,256]{1,0:T(8,128)(2,1)}, bf16[512,256]{1,0:T(8,128)(2,1)S(1)}, u32[]{:S(2)}, u32[]{:S(2)}) %collective-permute-start) | collective-permute-done | bytes 262176 | tf_op jit(solution)/shard_map/ppermute | solution.py:396
  26.0 8.5 %attend.2 = (bf16[256,1024]{1,0:T(8,128)(2,1)S(1)}, bf16[128,3072]{1,0:T(8,128)(2,1)S(1)}, bf16[128,3072]{1,0:T(8,128)(2,1)S(1)}) custom-call(s32[1]{0:T(128)} %bitcast.tp_ref, s32[1]{0:T(128)} %bitcast.1.rank_ref.ctx_ref, bf16[512,1024]{1,0:T(8,128)(2,1)} %q_ref.3, s32[3,8,128]{2,1,0:T(8,128)S(1)} %get-tuple-element.39.table_ref, ...), custom_call_target="tpu_custom_call" | custom-call | tf_op jit(solution)/shard_map/attend/pallas_call | solution.py:263
  34.6 2.3 %collective-permute-done.3 = bf16[128,3072]{1,0:T(8,128)(2,1)S(1)} collective-permute-done((bf16[128,3072]{1,0:T(8,128)(2,1)S(1)}, bf16[128,3072]{1,0:T(8,128)(2,1)S(1)}, u32[]{:S(2)}, u32[]{:S(2)}) %collective-permute-start.3) | collective-permute-done | bytes 786464 | tf_op jit(solution)/shard_map/ppermute | solution.py:408
  36.9 0.2 add_convert_fusion.refs_0_
  37.1 1.6 %collective-permute-start.9 = (bf16[128,3072]{1,0:T(8,128)(2,1)S(1)}, bf16[128,3072]{1,0:T(8,128)(2,1)S(1)}, u32[]{:S(2)}, u32[]{:S(2)}) collective-permute-start(bf16[128,3072]{1,0:T(8,128)(2,1)S(1)} %add_convert_fusion.refs_0_), channel_id=1, source_target_pairs={{0,2},{1,3},{2,0},{3,1},{4,6},{5,7},{6,4},{7,5},{8,10},{9,11},{10,... | collective-permute-start | bytes 2359304 | tf_op jit(solution)/shard_map/ppermute | solution.py:411
  38.6 4.6 %project.3 = (bf16[128,1024]{1,0:T(8,128)(2,1)S(1)}, bf16[128,1024]{1,0:T(8,128)(2,1)S(1)}, bf16[128,1024]{1,0:T(8,128)(2,1)S(1)}, bf16[128,1024]{1,0:T(8,128)(2...) custom-call(bf16[256,1024]{1,0:T(8,128)(2,1)S(1)} %get-tuple-element, ...), custom_call_target="tpu_custom_call" | custom-call | tf_op jit(solution)/shard_map/project/pallas_call | solution.py:314
  43.3 0.5 collective-permute-start.5
  43.9 0.4 collective-permute-start.7
  44.3 0.5 collective-permute-done.4.refs_4_
  44.8 0.4 collective-permute-done.5.refs_5_
  45.2 0.4 collective-permute-done.6.refs_6_
  45.6 0.4 collective-permute-done.7.refs_7_
  45.9 0.2 add.7.refs_3_
  46.2 5.6 %attend.3.refs_0_.a_ref = bf16[256,1024]{1,0:T(8,128)(2,1)S(1)} custom-call(s32[1]{0:T(128)} %bitcast.tp_ref, s32[1]{0:T(128)} %bitcast.1.rank_ref.ctx_ref, bf16[512,1024]{1,0:T(8,128)(2,1)S(1)} %copy-done.1, s32[3,8,128]{2,1,0:T(8,128)S(1)} %get-tuple-element.39.table_ref, bf16[512,256]{1,0:T(8,128)(2,1)S(1)} %get-tuple-element.40.own, ...), custom_call_target="tpu_custom_call" | custom-call | tf_op jit(solution)/shard_map/attend/pallas_call | solution.py:263
  51.8 2.5 %project.4 = (bf16[128,1024]{1,0:T(8,128)(2,1)S(1)}, bf16[128,1024]{1,0:T(8,128)(2,1)S(1)}) custom-call(bf16[256,1024]{1,0:T(8,128)(2,1)S(1)} %get-tuple-element.42.a_ref, bf16[1024,8192]{1,0:T(8,128)(2,1)} %w_hbm.5, bf16[256,1024]{1,0:T(8,128)(2,1)S(1)} %attend.3.refs_0_.a_ref), custom_call_target="tpu_custom_call" | custom-call | tf_op jit(solution)/shard_map/project/pallas_call | solution.py:314
  54.3 0.2 collective-permute-start.8
  54.5 0.5 collective-permute-start.16
  55.1 0.9 %collective-permute-done.8.refs_1_ = bf16[128,1024]{1,0:T(8,128)(2,1)S(1)} collective-permute-done((bf16[128,1024]{1,0:T(8,128)(2,1)S(1)}, bf16[128,1024]{1,0:T(8,128)(2,1)S(1)}, u32[]{:S(2)}, u32[]{:S(2)}) %collective-permute-start.8) | collective-permute-done | bytes 262176 | tf_op jit(solution)/shard_map/ppermute | solution.py:408
  56.0 0.7 copy-done.4
  56.7 0.9 %copy-done.2 = bf16[128,3072]{1,0:T(8,128)(2,1)} copy-done((bf16[128,3072]{1,0:T(8,128)(2,1)}, bf16[128,3072]{1,0:T(8,128)(2,1)S(1)}, u32[]{:S(2)}) %copy-start.2) | copy-done | bytes 786456
  57.6 9.1 %project.5 = (bf16[128,1024]{1,0:T(8,128)(2,1)S(1)}, bf16[128,1024]{1,0:T(8,128)(2,1)S(1)}, bf16[128,1024]{1,0:T(8,128)(2,1)S(1)}, bf16[128,1024]{1,0:T(8,128)(2...) custom-call(bf16[256,1024]{1,0:T(8,128)(2,1)} %copy-done, ...), custom_call_target="tpu_custom_call" | custom-call | tf_op jit(solution)/shard_map/project/pallas_call | solution.py:314
  66.7 0.2 collective-permute-start.12
  66.9 0.4 collective-permute-start.13
  67.4 0.4 collective-permute-start.18
  67.8 0.5 collective-permute-done.12.refs_4_
  68.3 0.1 collective-permute-start.19
  68.5 0.2 collective-permute-done.13.refs_5_
  68.7 0.1 collective-permute-start.14
  68.9 0.2 collective-permute-done.17.refs_3_
  69.1 0.1 collective-permute-start.15
  69.2 0.2 collective-permute-done.18.refs_4_
  69.5 1.6 %collective-permute-start.11 = (bf16[128,1024]{1,0:T(8,128)(2,1)S(1)}, bf16[128,1024]{1,0:T(8,128)(2,1)S(1)}, u32[]{:S(2)}, u32[]{:S(2)}) collective-permute-start(bf16[128,1024]{1,0:T(8,128)(2,1)S(1)} %copy-done.5), channel_id=1, source_target_pairs={{0,2},{1,3},{2,0},{3,1},{4,6},{5,7},{6,4},{7,5},{8,10},{9,11},{10,... | collective-permute-start | bytes 786440 | tf_op jit(solution)/shard_map/ppermute | solution.py:411
  71.1 1.1 %copy-done.3 = bf16[128,3072]{1,0:T(8,128)(2,1)S(1)} copy-done((bf16[128,3072]{1,0:T(8,128)(2,1)S(1)}, bf16[128,3072]{1,0:T(8,128)(2,1)}, u32[]{:S(2)}) %copy-start.3) | copy-done | bytes 786456
  72.3 1.0 %finish.3.refs_9_ = bf16[128,8192]{1,0:T(8,128)(2,1)} custom-call(bf16[128,1024]{1,0:T(8,128)(2,1)S(1)} %get-tuple-element.65.refs_0_, bf16[128,1024]{1,0:T(8,128)(2,1)S(1)} %get-tuple-element.66.refs_1_, bf16[128,1024]{1,0:T(8,128)(2,1)S(1)} %get-tuple-element.67.refs_2_, bf16[128,1024]{1,0:T(8,128)(2,1)S(1)} %collective-permute-done.17.refs_3_, ...), custom_call_target="tpu_custom_call" | custom-call | tf_op jit(solution)/shard_map/finish/pallas_call | solution.py:373
  73.3 7.2 %collective-permute-done.16.refs_8_ = bf16[128,4096]{1,0:T(8,128)(2,1)S(1)} collective-permute-done((bf16[128,4096]{1,0:T(8,128)(2,1)S(1)}, bf16[128,4096]{1,0:T(8,128)(2,1)S(1)}, u32[]{:S(2)}, u32[]{:S(2)}) %collective-permute-start.16) | collective-permute-done | bytes 1048608 | tf_op jit(solution)/shard_map/ppermute | solution.py:411
  80.5 1.1 %finish.4.refs_3_ = bf16[128,8192]{1,0:T(8,128)(2,1)} custom-call(bf16[128,1024]{1,0:T(8,128)(2,1)S(1)} %get-tuple-element.57.refs_0_, bf16[128,1024]{1,0:T(8,128)(2,1)S(1)} %get-tuple-element.58.refs_1_, bf16[128,1024]{1,0:T(8,128)(2,1)S(1)} %get-tuple-element.59.refs_2_, ...), custom_call_target="tpu_custom_call", output_to_operand_aliasing={{}: (9, {})} | custom-call | tf_op jit(solution)/shard_map/finish/pallas_call | solution.py:373
  81.7 3.9 %collective-permute-done.11.refs_2_ = bf16[128,1024]{1,0:T(8,128)(2,1)S(1)} collective-permute-done((bf16[128,1024]{1,0:T(8,128)(2,1)S(1)}, bf16[128,1024]{1,0:T(8,128)(2,1)S(1)}, u32[]{:S(2)}, u32[]{:S(2)}) %collective-permute-start.11) | collective-permute-done | bytes 262176 | tf_op jit(solution)/shard_map/ppermute | solution.py:411
  85.6 0.8 finish.5
  (28 shorter events, 0.5 us)
Async XLA Ops:
  2.1 12.0 %all-to-all-start = ((bf16[4,128,256]{2,1,0:T(8,128)(2,1)}), bf16[4,128,256]{2,1,0:T(8,128)(2,1)S(1)}, u32[]{:S(2)}, u32[]{:S(2)}) async-start(bf16[4,128,256]{2,1,0:T(8,128)(2,1)} %get-tuple-element.41), calls=%async_computation | async-start | bytes 524288 | tf_op jit(solution)/shard_map/all_to_all | solution.py:401
  7.3 12.1 %collective-permute-start.1 = (bf16[512,256]{1,0:T(8,128)(2,1)}, bf16[512,256]{1,0:T(8,128)(2,1)S(1)}, u32[]{:S(2)}, u32[]{:S(2)}) collective-permute-start(bf16[512,256]{1,0:T(8,128)(2,1)} %get-tuple-element.38.own_ref), channel_id=1, source_target_pairs={{0,8},{4,12},{8,16},{12,20},{16,24},{20,28},{1,9},{5,13},{9,17},{1... | collective-permute-start | bytes 786440 | tf_op jit(solution)/shard_map/ppermute | solution.py:396
  10.7 15.3 %collective-permute-start = (bf16[512,256]{1,0:T(8,128)(2,1)}, bf16[512,256]{1,0:T(8,128)(2,1)S(1)}, u32[]{:S(2)}, u32[]{:S(2)}) collective-permute-start(bf16[512,256]{1,0:T(8,128)(2,1)} %get-tuple-element.38.own_ref), channel_id=1, source_target_pairs={{0,4},{4,8},{8,12},{12,16},{16,20},{20,24},{24,28},{1,5},{5,9},{9,... | collective-permute-start | bytes 786440 | tf_op jit(solution)/shard_map/ppermute | solution.py:396
  14.1 11.9 %collective-permute-start.2 = (bf16[3,128,256]{2,1,0:T(8,128)(2,1)S(1)}, bf16[3,128,256]{2,1,0:T(8,128)(2,1)S(1)}, u32[]{:S(2)}, u32[]{:S(2)}) collective-permute-start(bf16[3,128,256]{2,1,0:T(8,128)(2,1)S(1)} %slice.4), channel_id=1, source_target_pairs={{0,4},{4,0},{8,12},{12,8},{16,20},{20,16},{24,28},{28,24},{1,5},{5... | collective-permute-start | bytes 589832 | tf_op jit(solution)/shard_map/ppermute | solution.py:403
  14.7 0.9 %copy-start.7 = (bf16[512,256]{1,0:T(8,128)(2,1)S(1)}, bf16[512,256]{1,0:T(8,128)(2,1)}, u32[]{:S(2)}) copy-start(bf16[512,256]{1,0:T(8,128)(2,1)} %get-tuple-element.38.own_ref) | copy-start | bytes 786436
  15.7 0.7 copy-start.8
  16.4 0.7 copy-start.9
  34.5 2.4 %collective-permute-start.3 = (bf16[128,3072]{1,0:T(8,128)(2,1)S(1)}, bf16[128,3072]{1,0:T(8,128)(2,1)S(1)}, u32[]{:S(2)}, u32[]{:S(2)}) collective-permute-start(bf16[128,3072]{1,0:T(8,128)(2,1)S(1)} %get-tuple-element.44), channel_id=1, source_target_pairs={{0,1},{1,0},{2,3},{3,2},{4,5},{5,4},{6,7},{7,6},{8,9},{9,8},{10,11... | collective-permute-start | bytes 2359304 | tf_op jit(solution)/shard_map/ppermute | solution.py:408
  37.1 19.6 %collective-permute-start.9 = (bf16[128,3072]{1,0:T(8,128)(2,1)S(1)}, bf16[128,3072]{1,0:T(8,128)(2,1)S(1)}, u32[]{:S(2)}, u32[]{:S(2)}) collective-permute-start(bf16[128,3072]{1,0:T(8,128)(2,1)S(1)} %add_convert_fusion.refs_0_), channel_id=1, source_target_pairs={{0,2},{1,3},{2,0},{3,1},{4,6},{5,7},{6,4},{7,5},{8,10},{9,11},{10,... | collective-permute-start | bytes 2359304 | tf_op jit(solution)/shard_map/ppermute | solution.py:411
  43.2 3.0 %copy-start.1 = (bf16[512,1024]{1,0:T(8,128)(2,1)S(1)}, bf16[512,1024]{1,0:T(8,128)(2,1)}, u32[]{:S(2)}) copy-start(bf16[512,1024]{1,0:T(8,128)(2,1)} %q_ref.3) | copy-start | bytes 3145732
  43.2 1.6 %collective-permute-start.4 = (bf16[128,1024]{1,0:T(8,128)(2,1)S(1)}, bf16[128,1024]{1,0:T(8,128)(2,1)S(1)}, u32[]{:S(2)}, u32[]{:S(2)}) collective-permute-start(bf16[128,1024]{1,0:T(8,128)(2,1)S(1)} %get-tuple-element.49), channel_id=1, source_target_pairs={{0,1},{1,0},{2,3},{3,2},{4,5},{5,4},{6,7},{7,6},{8,9},{9,8},{10,11... | collective-permute-start | bytes 786440 | tf_op jit(solution)/shard_map/ppermute | solution.py:408
  43.3 1.9 %collective-permute-start.5 = (bf16[128,1024]{1,0:T(8,128)(2,1)S(1)}, bf16[128,1024]{1,0:T(8,128)(2,1)S(1)}, u32[]{:S(2)}, u32[]{:S(2)}) collective-permute-start(bf16[128,1024]{1,0:T(8,128)(2,1)S(1)} %get-tuple-element.50), channel_id=1, source_target_pairs={{0,1},{1,0},{2,3},{3,2},{4,5},{5,4},{6,7},{7,6},{8,9},{9,8},{10,11... | collective-permute-start | bytes 786440 | tf_op jit(solution)/shard_map/ppermute | solution.py:408
  43.8 1.8 %collective-permute-start.6 = (bf16[128,1024]{1,0:T(8,128)(2,1)S(1)}, bf16[128,1024]{1,0:T(8,128)(2,1)S(1)}, u32[]{:S(2)}, u32[]{:S(2)}) collective-permute-start(bf16[128,1024]{1,0:T(8,128)(2,1)S(1)} %get-tuple-element.51), channel_id=1, source_target_pairs={{0,1},{1,0},{2,3},{3,2},{4,5},{5,4},{6,7},{7,6},{8,9},{9,8},{10,11... | collective-permute-start | bytes 786440 | tf_op jit(solution)/shard_map/ppermute | solution.py:408
  43.9 2.1 %collective-permute-start.7 = (bf16[128,1024]{1,0:T(8,128)(2,1)S(1)}, bf16[128,1024]{1,0:T(8,128)(2,1)S(1)}, u32[]{:S(2)}, u32[]{:S(2)}) collective-permute-start(bf16[128,1024]{1,0:T(8,128)(2,1)S(1)} %get-tuple-element.52), channel_id=1, source_target_pairs={{0,1},{1,0},{2,3},{3,2},{4,5},{5,4},{6,7},{7,6},{8,9},{9,8},{10,11... | collective-permute-start | bytes 786440 | tf_op jit(solution)/shard_map/ppermute | solution.py:408
  51.8 2.5 %copy-start = (bf16[256,1024]{1,0:T(8,128)(2,1)}, bf16[256,1024]{1,0:T(8,128)(2,1)S(1)}, u32[]{:S(2)}) copy-start(bf16[256,1024]{1,0:T(8,128)(2,1)S(1)} %attend.3.refs_0_.a_ref) | copy-start | bytes 1572868
  54.3 1.6 %collective-permute-start.8 = (bf16[128,1024]{1,0:T(8,128)(2,1)S(1)}, bf16[128,1024]{1,0:T(8,128)(2,1)S(1)}, u32[]{:S(2)}, u32[]{:S(2)}) collective-permute-start(bf16[128,1024]{1,0:T(8,128)(2,1)S(1)} %get-tuple-element.54), channel_id=1, source_target_pairs={{0,1},{1,0},{2,3},{3,2},{4,5},{5,4},{6,7},{7,6},{8,9},{9,8},{10,11... | collective-permute-start | bytes 786440 | tf_op jit(solution)/shard_map/ppermute | solution.py:408
  54.5 26.0 %collective-permute-start.16 = (bf16[128,4096]{1,0:T(8,128)(2,1)S(1)}, bf16[128,4096]{1,0:T(8,128)(2,1)S(1)}, u32[]{:S(2)}, u32[]{:S(2)}) collective-permute-start(bf16[128,4096]{1,0:T(8,128)(2,1)S(1)} %add.7.refs_3_), channel_id=1, source_target_pairs={{0,2},{1,3},{2,0},{3,1},{4,6},{5,7},{6,4},{7,5},{8,10},{9,11},{10,... | collective-permute-start | bytes 3145736 | tf_op jit(solution)/shard_map/ppermute | solution.py:411
  56.0 0.7 copy-start.4
  56.7 0.9 %copy-start.2 = (bf16[128,3072]{1,0:T(8,128)(2,1)}, bf16[128,3072]{1,0:T(8,128)(2,1)S(1)}, u32[]{:S(2)}) copy-start(bf16[128,3072]{1,0:T(8,128)(2,1)S(1)} %collective-permute-done.9.refs_1_.refs_6_) | copy-start | bytes 2359300
  57.6 11.9 %copy-start.5 = (bf16[128,1024]{1,0:T(8,128)(2,1)S(1)}, bf16[128,1024]{1,0:T(8,128)(2,1)}, u32[]{:S(2)}) copy-start(bf16[128,1024]{1,0:T(8,128)(2,1)} %copy-done.4) | copy-start | bytes 786436
  66.7 1.6 %collective-permute-start.12 = (bf16[128,1024]{1,0:T(8,128)(2,1)S(1)}, bf16[128,1024]{1,0:T(8,128)(2,1)S(1)}, u32[]{:S(2)}, u32[]{:S(2)}) collective-permute-start(bf16[128,1024]{1,0:T(8,128)(2,1)S(1)} %get-tuple-element.61), channel_id=1, source_target_pairs={{0,1},{1,0},{2,3},{3,2},{4,5},{5,4},{6,7},{7,6},{8,9},{9,8},{10,11... | collective-permute-start | bytes 786440 | tf_op jit(solution)/shard_map/ppermute | solution.py:408
  66.9 1.8 %collective-permute-start.13 = (bf16[128,1024]{1,0:T(8,128)(2,1)S(1)}, bf16[128,1024]{1,0:T(8,128)(2,1)S(1)}, u32[]{:S(2)}, u32[]{:S(2)}) collective-permute-start(bf16[128,1024]{1,0:T(8,128)(2,1)S(1)} %get-tuple-element.62), channel_id=1, source_target_pairs={{0,1},{1,0},{2,3},{3,2},{4,5},{5,4},{6,7},{7,6},{8,9},{9,8},{10,11... | collective-permute-start | bytes 786440 | tf_op jit(solution)/shard_map/ppermute | solution.py:408
  67.3 1.8 %collective-permute-start.17 = (bf16[128,1024]{1,0:T(8,128)(2,1)S(1)}, bf16[128,1024]{1,0:T(8,128)(2,1)S(1)}, u32[]{:S(2)}, u32[]{:S(2)}) collective-permute-start(bf16[128,1024]{1,0:T(8,128)(2,1)S(1)} %get-tuple-element.68), channel_id=1, source_target_pairs={{0,1},{1,0},{2,3},{3,2},{4,5},{5,4},{6,7},{7,6},{8,9},{9,8},{10,11... | collective-permute-start | bytes 786440 | tf_op jit(solution)/shard_map/ppermute | solution.py:408
  67.4 2.0 %collective-permute-start.18 = (bf16[128,1024]{1,0:T(8,128)(2,1)S(1)}, bf16[128,1024]{1,0:T(8,128)(2,1)S(1)}, u32[]{:S(2)}, u32[]{:S(2)}) collective-permute-start(bf16[128,1024]{1,0:T(8,128)(2,1)S(1)} %get-tuple-element.69), channel_id=1, source_target_pairs={{0,1},{1,0},{2,3},{3,2},{4,5},{5,4},{6,7},{7,6},{8,9},{9,8},{10,11... | collective-permute-start | bytes 786440 | tf_op jit(solution)/shard_map/ppermute | solution.py:408
  68.3 2.8 %collective-permute-start.19 = (bf16[128,1024]{1,0:T(8,128)(2,1)S(1)}, bf16[128,1024]{1,0:T(8,128)(2,1)S(1)}, u32[]{:S(2)}, u32[]{:S(2)}) collective-permute-start(bf16[128,1024]{1,0:T(8,128)(2,1)S(1)} %get-tuple-element.70), channel_id=1, source_target_pairs={{0,1},{1,0},{2,3},{3,2},{4,5},{5,4},{6,7},{7,6},{8,9},{9,8},{10,11... | collective-permute-start | bytes 786440 | tf_op jit(solution)/shard_map/ppermute | solution.py:408
  68.7 4.6 %collective-permute-start.14 = (bf16[128,1024]{1,0:T(8,128)(2,1)S(1)}, bf16[128,1024]{1,0:T(8,128)(2,1)S(1)}, u32[]{:S(2)}, u32[]{:S(2)}) collective-permute-start(bf16[128,1024]{1,0:T(8,128)(2,1)S(1)} %get-tuple-element.63), channel_id=1, source_target_pairs={{0,1},{1,0},{2,3},{3,2},{4,5},{5,4},{6,7},{7,6},{8,9},{9,8},{10,11... | collective-permute-start | bytes 786440 | tf_op jit(solution)/shard_map/ppermute | solution.py:408
  69.1 4.2 %collective-permute-start.15 = (bf16[128,1024]{1,0:T(8,128)(2,1)S(1)}, bf16[128,1024]{1,0:T(8,128)(2,1)S(1)}, u32[]{:S(2)}, u32[]{:S(2)}) collective-permute-start(bf16[128,1024]{1,0:T(8,128)(2,1)S(1)} %get-tuple-element.64), channel_id=1, source_target_pairs={{0,1},{1,0},{2,3},{3,2},{4,5},{5,4},{6,7},{7,6},{8,9},{9,8},{10,11... | collective-permute-start | bytes 786440 | tf_op jit(solution)/shard_map/ppermute | solution.py:408
  69.5 16.1 %collective-permute-start.11 = (bf16[128,1024]{1,0:T(8,128)(2,1)S(1)}, bf16[128,1024]{1,0:T(8,128)(2,1)S(1)}, u32[]{:S(2)}, u32[]{:S(2)}) collective-permute-start(bf16[128,1024]{1,0:T(8,128)(2,1)S(1)} %copy-done.5), channel_id=1, source_target_pairs={{0,2},{1,3},{2,0},{3,1},{4,6},{5,7},{6,4},{7,5},{8,10},{9,11},{10,... | collective-permute-start | bytes 786440 | tf_op jit(solution)/shard_map/ppermute | solution.py:411
  71.1 14.5 %collective-permute-start.10 = (bf16[128,1024]{1,0:T(8,128)(2,1)S(1)}, bf16[128,1024]{1,0:T(8,128)(2,1)S(1)}, u32[]{:S(2)}, u32[]{:S(2)}) collective-permute-start(bf16[128,1024]{1,0:T(8,128)(2,1)S(1)} %get-tuple-element.56), channel_id=1, source_target_pairs={{0,1},{1,0},{2,3},{3,2},{4,5},{5,4},{6,7},{7,6},{8,9},{9,8},{10,11... | collective-permute-start | bytes 786440 | tf_op jit(solution)/shard_map/ppermute | solution.py:408
  71.1 1.1 %copy-start.3 = (bf16[128,3072]{1,0:T(8,128)(2,1)S(1)}, bf16[128,3072]{1,0:T(8,128)(2,1)}, u32[]{:S(2)}) copy-start(bf16[128,3072]{1,0:T(8,128)(2,1)} %copy-done.2) | copy-start | bytes 2359300
  80.5 5.1 %copy-start.6 = (bf16[128,1024]{1,0:T(8,128)(2,1)S(1)}, bf16[128,1024]{1,0:T(8,128)(2,1)}, u32[]{:S(2)}) copy-start(bf16[128,1024]{1,0:T(8,128)(2,1)} %get-tuple-element.55.refs_0_) | copy-start | bytes 786436

commit v12 on v11

--- a/solution.py
+++ b/solution.py
@@ -16,7 +16,7 @@
 MASKED = -1e30
 EXP_SCALE = 1.4426950408889634 / (HS**0.5)
 TILE = 1024
-ACROSS = (3, 4, 1)
+HEAD = 2
 MIB = 1024 * 1024
 
 
@@ -122,7 +122,7 @@
 
 
 def attend_kernel(
-    slots, tiles, sizes, flips, tp_ref, ctx_ref, q_ref, table_ref, own, kv_1, kv_2, *refs
+    slots, tiles, sizes, place, tp_ref, ctx_ref, q_0, q_1, table_ref, own, kv_1, kv_2, *refs
 ):
     pairs = refs[:2]
     w_hbm = refs[2]
@@ -132,9 +132,8 @@
     heads = table_ref.shape[1]
     rows = own.shape[0]
     local_blocks = rows // BLK
-    quarter = local_blocks // 4
     far_rows = e_pool.shape[0]
-    dtype = q_ref.dtype
+    dtype = q_0.dtype
     rank = ctx_ref[0]
     vert = table_ref[0][:, : sizes[0]]
     slash = table_ref[1][:, : sizes[1]]
@@ -171,7 +170,6 @@
         for copy in copies:
             copy.wait()
 
-    owner = tp_ref[0] ^ jnp.where(step == 0, flips[0], flips[1])
     lane = lax.broadcasted_iota(jnp.int32, (heads, LANES), 1)
     row = lax.broadcasted_iota(jnp.int32, (BLK, LANES), 0)
     above = lax.broadcasted_iota(jnp.int32, (BLK, LANES), 1) - BLK > row
@@ -184,9 +182,9 @@
         return jnp.concatenate([values, jnp.ones((values.shape[0], LANES), dtype)], axis=1)
 
     near, far_q, windows = [], [], []
-    for u in range(quarter):
-        here = owner * quarter + u
-        q = q_ref[u * BLK : (u + 1) * BLK, :]
+    for u, q_ref in enumerate((q_0, q_1)):
+        here = place(u, step, tp_ref)
+        q = q_ref[...]
         q = jnp.concatenate([q[:, h * HS : (h + 1) * HS] for h in range(heads)], axis=0)
         first = rank * local_blocks + here - (SPAN - 1)
         seen = first + lane
@@ -215,7 +213,7 @@
         preferred_element_type=jnp.float32,
     )
     far_values = with_ones(kv_pool[:, :, HS:].reshape(far_rows, HS))
-    for u in range(quarter):
+    for u in range(2):
         far_u = far[u * heads * BLK : (u + 1) * heads * BLK]
         top = jnp.maximum(
             jnp.max(near[u], axis=1, keepdims=True), jnp.max(far_u, axis=1, keepdims=True)
@@ -226,7 +224,7 @@
         probs = jnp.exp2((far_u - top) * EXP_SCALE).astype(dtype)
         summed = summed + jnp.dot(probs, far_values, preferred_element_type=jnp.float32)
         out = (summed[:, :HS] / summed[:, HS:]).astype(dtype)
-        at = pl.ds(pl.multiple_of((step * quarter + u) * BLK, BLK), BLK)
+        at = pl.ds(pl.multiple_of((step * 2 + u) * BLK, BLK), BLK)
         for h in range(heads):
             attended[at, h * HS : (h + 1) * HS] = out[h * BLK : (h + 1) * BLK]
 
@@ -242,31 +240,38 @@
             outs[2][:, t * TILE : (t + 1) * TILE] = product[half:]
 
 
-def attend(flips, tp, ctx, queries, table, near_kv, pairs, sizes, out_weight, tiles, after):
+def attend(blocks, tp, ctx, queries, table, near_kv, pairs, sizes, out_weight, tiles, after):
     width = queries.shape[1]
     rows = near_kv[0].shape[0]
-    quarter = rows // 4
-    steps = len(flips)
+    quarter = rows // BLK // 4
+    steps = len(blocks)
     slots = pairs[1].shape[0]
     dtype = queries.dtype
     far = 2 * slots * VMOST * BLK
 
-    def place(g, tp, ctx):
-        return (tp[0] ^ jnp.where(g == 0, flips[0], flips[1]), 0)
+    def place(u, g, tp):
+        flip, block = blocks[-1][u]
+        for step in range(steps - 1):
+            flip = jnp.where(g == step, blocks[step][u][0], flip)
+            block = jnp.where(g == step, blocks[step][u][1], block)
+        return (tp[0] ^ flip) * quarter + block
 
     def whole(shape):
         return pl.BlockSpec(shape, lambda g, tp, ctx: (0,) * len(shape))
 
-    out_shapes = [(steps * quarter, width)]
+    out_shapes = [(steps * 2 * BLK, width)]
     if tiles:
-        out_shapes += [(steps * quarter // 2, tiles * TILE)] * 2
+        out_shapes += [(steps * BLK, tiles * TILE)] * 2
     return pl.pallas_call(
-        functools.partial(attend_kernel, slots, tiles, sizes, flips),
+        functools.partial(attend_kernel, slots, tiles, sizes, place),
         out_shape=[jax.ShapeDtypeStruct(shape, dtype) for shape in out_shapes],
         grid_spec=pltpu.PrefetchScalarGridSpec(
             num_scalar_prefetch=2,
             grid=(steps,),
-            in_specs=[pl.BlockSpec((quarter, width), place)]
+            in_specs=[
+                pl.BlockSpec((BLK, width), lambda g, tp, ctx: (place(0, g, tp), 0)),
+                pl.BlockSpec((BLK, width), lambda g, tp, ctx: (place(1, g, tp), 0)),
+            ]
             + [whole(table.shape)]
             + [anywhere() for _ in [*near_kv, *pairs, out_weight, *after]],
             out_specs=[whole(shape) for shape in out_shapes],
@@ -275,7 +280,7 @@
                 pltpu.VMEM((SPAN * BLK, LANES), dtype),
                 pltpu.VMEM((2 * slots, VMOST * BLK, 2 * HS), dtype),
                 pltpu.VMEM((far, LANES), dtype),
-                pltpu.VMEM((steps * quarter, width), dtype),
+                pltpu.VMEM((steps * 2 * BLK, width), dtype),
                 pltpu.VMEM((max(tiles, 1), out_weight.shape[0], TILE), dtype),
                 pltpu.SemaphoreType.DMA((max(tiles, 1),)),
                 pltpu.SemaphoreType.DMA((NEAR + 2,)),
@@ -284,18 +289,18 @@
         compiler_params=params(50),
         cost_estimate=SHORT,
         name="attend",
-    )(tp, ctx, queries, table, *near_kv, *pairs, out_weight, *after)
+    )(tp, ctx, queries, queries, table, *near_kv, *pairs, out_weight, *after)
 
 
 def project_kernel(first, a_ref, w_hbm, *refs):
     weight, arrival = refs[-2:]
-    tiles = weight.shape[0]
+    tiles, _, tile = weight.shape
     outs = refs[-2 - 2 * tiles : -2]
     half = outs[0].shape[0]
 
     def fetch(t):
         return pltpu.make_async_copy(
-            w_hbm.at[:, pl.ds((first + t) * TILE, TILE)], weight.at[t], arrival.at[t]
+            w_hbm.at[:, pl.ds(first + t * tile, tile)], weight.at[t], arrival.at[t]
         )
 
     for t in range(tiles):
@@ -310,14 +315,15 @@
 
 def project(attended, out_weight, first, tiles, after):
     rows, depth = attended.shape
-    part = jax.ShapeDtypeStruct((rows // 2, TILE), attended.dtype)
+    tile = (out_weight.shape[1] - first) // tiles
+    part = jax.ShapeDtypeStruct((rows // 2, tile), attended.dtype)
     outs = pl.pallas_call(
         functools.partial(project_kernel, first),
         out_shape=[part] * (2 * tiles),
         in_specs=[vmem(), anywhere()] + [anywhere() for _ in after],
         out_specs=[vmem()] * (2 * tiles),
         scratch_shapes=[
-            pltpu.VMEM((tiles, depth, TILE), attended.dtype),
+            pltpu.VMEM((tiles, depth, tile), attended.dtype),
             pltpu.SemaphoreType.DMA((tiles,)),
         ],
         compiler_params=params(50),
@@ -351,33 +357,35 @@
     )(*keep, *got)
 
 
-def finish_kernel(pieces, first, *refs):
-    arrived_ref = refs[2 * pieces]
+def finish_kernel(tiles, first, top, *refs):
+    arrived_ref = refs[2 * tiles]
     out_ref, tiles_ref, sent = refs[-3:]
+    rows = pl.ds(top, arrived_ref.shape[0])
     copies = []
-    for t in range(pieces):
-        total = refs[t][...].astype(jnp.float32) + refs[pieces + t][...].astype(jnp.float32)
+    for t in range(tiles):
+        total = refs[t][rows, :].astype(jnp.float32) + refs[tiles + t][rows, :].astype(jnp.float32)
         total = total + arrived_ref[:, t * TILE : (t + 1) * TILE].astype(jnp.float32)
         tiles_ref[t] = total.astype(out_ref.dtype)
         columns = pl.ds((first + t) * TILE, TILE)
-        copies.append(pltpu.make_async_copy(tiles_ref.at[t], out_ref.at[:, columns], sent.at[t]))
+        copies.append(
+            pltpu.make_async_copy(tiles_ref.at[t], out_ref.at[rows, columns], sent.at[t])
+        )
         copies[-1].start()
     for copy in copies:
         copy.wait()
 
 
-def finish(keep, got, arrived, first, width, out):
-    rows = arrived.shape[0]
+def finish(keep, got, arrived, first, top, shape, out):
     tiles = len(keep)
     before = [] if out is None else [out]
     return pl.pallas_call(
-        functools.partial(finish_kernel, len(keep), first),
-        out_shape=jax.ShapeDtypeStruct((rows, width), arrived.dtype),
-        in_specs=[vmem()] * (2 * len(keep) + 1) + [anywhere() for _ in before],
+        functools.partial(finish_kernel, tiles, first, top),
+        out_shape=jax.ShapeDtypeStruct(shape, arrived.dtype),
+        in_specs=[vmem()] * (2 * tiles + 1) + [anywhere() for _ in before],
         out_specs=anywhere(),
-        input_output_aliases={2 * len(keep) + 1: 0} if before else {},
+        input_output_aliases={2 * tiles + 1: 0} if before else {},
         scratch_shapes=[
-            pltpu.VMEM((tiles, rows, TILE), arrived.dtype),
+            pltpu.VMEM((tiles, arrived.shape[0], TILE), arrived.dtype),
             pltpu.SemaphoreType.DMA((tiles,)),
         ],
         compiler_params=params(16),
@@ -410,36 +418,33 @@
     def across(x):
         return lax.ppermute(x, "tp", [(j, j ^ 2) for j in range(4)])
 
-    def attention(flips, tiles, after):
+    def attention(blocks, tiles, after):
         sizes = (vertical.shape[1], slash.shape[1])
         return attend(
-            flips, tp, ctx, queries, table, near_kv, pairs, sizes, out_weight, tiles, after
-        )
+            blocks, tp, ctx, queries, table, near_kv, pairs, sizes, out_weight, tiles, after
+        )
+
+    def exchanged(send, keep):
+        return add(keep, [sibling(x) for x in send])
 
     width = out_weight.shape[1]
     tiles = width // TILE
-    assert sum(ACROSS) == tiles
-    starts = [sum(ACROSS[:n]) for n in range(len(ACROSS))]
-
-    def send_chunk(chunk, after):
-        send, keep = project(attended, out_weight, starts[chunk], ACROSS[chunk], after)
-        return add(keep, [sibling(x) for x in send])
-
-    attended, send, keep = attention((3, 2), ACROSS[0], ())
+    assert local_blocks == 8
+    attended, send, keep = attention((((3, 0), (2, 0)),), HEAD, ())
     total = (keep.astype(jnp.float32) + sibling(send).astype(jnp.float32)).astype(keep.dtype)
     arrived = [across(total)]
-    total = send_chunk(1, (total,))
+    total = exchanged(*project(attended, out_weight, HEAD * TILE, 4, (total,)))
     arrived.append(across(total))
-    (own_attended,) = attention((1, 0), 0, (total,))
-    total = send_chunk(2, (own_attended,))
+    (attended,) = attention((((3, 1), (2, 1)),), 0, (total,))
+    total = exchanged(*project(attended, out_weight, 0, 4, (arrived[0],)))
     arrived.append(across(total))
-    send, keep = project(own_attended, out_weight, 0, tiles, (total, arrived[0]))
+    (attended,) = attention((((1, 0), (1, 1)), ((0, 0), (0, 1))), 0, (total, arrived[1]))
+    send, keep = project(attended, out_weight, 0, tiles, ())
     got = [sibling(x) for x in send]
-    out = None
-    for part, first, count in zip(arrived, starts, ACROSS):
-        at = slice(first, first + count)
-        out = finish(keep[at], got[at], part, first, width, out)
-    return out
+    shape = (queries.shape[0] // 4, width)
+    out = finish(keep[:HEAD], got[:HEAD], arrived[0], 0, 0, shape, None)
+    out = finish(keep[HEAD:], got[HEAD:], arrived[1], HEAD, 0, shape, out)
+    return finish(keep, got, arrived[2], 0, BLK, shape, out)
 
 
 def solution(mesh):

time: 87 us -> 85.2 us (0.979)
  waiting for transfers between devices: 26 us -> 21.8 us
  Pallas kernels: 35.8 us -> 39.3 us
  local copies, waits for them, and re-layouts: 5.05 us -> 3.14 us
  starting transfers between devices: 19.2 us -> 20.2 us
    pallas_call x3, Pallas kernels: 16.2 us -> 21 us  [project(): pl.pallas_call(functools.partial(project_kernel, first), out_shape=[part]...]
    ppermute x3, waiting for transfers between devices: 11.2 us -> 6.77 us  [across(): return lax.ppermute(x, 'tp', [(j, j ^ 2) for j in range(4)])]
    unnamed x20 -> x14, local copies, waits for them, and re-layouts: 5.04 us -> 3.12 us
    pallas_call x5 -> x6, Pallas kernels: 17.1 us -> 15.5 us  [the longest x3 12.7 us: attend(): pl.pallas_call(functools.partial(attend_kernel, slots, tiles, sizes, plac...]
    ppermute x14 -> x17, starting transfers between devices: 2.85 us -> 3.86 us  [sibling(): return lax.ppermute(x, 'tp', [(j, j ^ 1) for j in range(4)])]
    ppermute x14 -> x17, waiting for transfers between devices: 6.03 us -> 6.25 us  [sibling(): return lax.ppermute(x, 'tp', [(j, j ^ 1) for j in range(4)])]
  transfers between devices with their start and end apart: 21 -> 24, of which waited for: 14 -> 19; matrix products, arithmetic and copies ran while one was open for 0% -> 0% of each run, Pallas kernels for 28% -> 37%
where the time goes in v12:
time: 85.2 us; the launch traced here: 84.9 us
  Pallas kernels  39.3 us (46%)
  waiting for transfers between devices  21.8 us (26%)
  starting transfers between devices  20.2 us (24%)
  local copies, waits for them, and re-layouts  3.14 us (4%)
    pallas_call x3, Pallas kernels, project(): pl.pallas_call(functools.partial(project_kernel, first), out_shape=[part]...  21 us
    pallas_call x3, Pallas kernels, attend(): pl.pallas_call(functools.partial(attend_kernel, slots, tiles, sizes, plac...  12.7 us
    ppermute x2, waiting for transfers between devices, shifted(): return lax.ppermute(x, 'ctx', [(r, r + by) for r in range(ctx_size - by)])  8.77 us
    ppermute x2, starting transfers between devices, shifted(): return lax.ppermute(x, 'ctx', [(r, r + by) for r in range(ctx_size - by)])  6.79 us
    ppermute x3, waiting for transfers between devices, across(): return lax.ppermute(x, 'tp', [(j, j ^ 2) for j in range(4)])  6.77 us
    ppermute x17, waiting for transfers between devices, sibling(): return lax.ppermute(x, 'tp', [(j, j ^ 1) for j in range(4)])  6.25 us
    all_to_all x1, starting transfers between devices, shards(): lax.all_to_all(pair, 'ctx', 0, 0, axis_index_groups=parities, tiled=True)  5.2 us
    ppermute x17, starting transfers between devices, sibling(): return lax.ppermute(x, 'tp', [(j, j ^ 1) for j in range(4)])  3.86 us
  transfers between devices with their start and end apart: 24, of which 19 were waited for; matrix products, arithmetic and copies ran while one was open for 0% of the time, Pallas kernels for 37%

profile of v12, /device:TPU:16, one launch (start us, length us, event | category | flops | bytes accessed | tf_op | source)
XLA Modules:
  0.0 84.9 jit_solution(15050376694794392266)
XLA Ops:
  0.0 2.2 %pick.1 = (bf16[512,256]{1,0:T(8,128)(2,1)}, bf16[4,128,256]{2,1,0:T(8,128)(2,1)}) custom-call(s32[1]{0:T(128)} %bitcast.1.rank_ref.ctx_ref, s32[8,16]{1,0:T(8,128)} %vert_ref.3, bf16[512,128]{1,0:T(8,128)(2,1)} %k_ref.1, bf16[512,128]{1,0:T(8,128)(2,1)} %v_ref.1), custom_call_target="tpu_custom_call" | custom-call | tf_op jit(solution)/shard_map/pick/pallas_call | solution.py:64
  2.2 5.2 %all-to-all-start = ((bf16[4,128,256]{2,1,0:T(8,128)(2,1)}), bf16[4,128,256]{2,1,0:T(8,128)(2,1)S(1)}, u32[]{:S(2)}, u32[]{:S(2)}) async-start(bf16[4,128,256]{2,1,0:T(8,128)(2,1)} %get-tuple-element.47), calls=%async_computation | async-start | bytes 524288 | tf_op jit(solution)/shard_map/all_to_all | solution.py:409
  7.4 3.4 %collective-permute-start.1 = (bf16[512,256]{1,0:T(8,128)(2,1)}, bf16[512,256]{1,0:T(8,128)(2,1)S(1)}, u32[]{:S(2)}, u32[]{:S(2)}) collective-permute-start(bf16[512,256]{1,0:T(8,128)(2,1)} %get-tuple-element.44.own_ref), channel_id=1, source_target_pairs={{0,8},{4,12},{8,16},{12,20},{16,24},{20,28},{1,9},{5,13},{9,17},{1... | collective-permute-start | bytes 786440 | tf_op jit(solution)/shard_map/ppermute | solution.py:404
  10.7 3.4 %collective-permute-start = (bf16[512,256]{1,0:T(8,128)(2,1)}, bf16[512,256]{1,0:T(8,128)(2,1)S(1)}, u32[]{:S(2)}, u32[]{:S(2)}) collective-permute-start(bf16[512,256]{1,0:T(8,128)(2,1)} %get-tuple-element.44.own_ref), channel_id=1, source_target_pairs={{0,4},{4,8},{8,12},{12,16},{16,20},{20,24},{24,28},{1,5},{5,9},{9,... | collective-permute-start | bytes 786440 | tf_op jit(solution)/shard_map/ppermute | solution.py:404
  14.2 0.6 collective-permute-start.2
  14.8 0.9 %copy-done.4 = bf16[512,256]{1,0:T(8,128)(2,1)S(1)} copy-done((bf16[512,256]{1,0:T(8,128)(2,1)S(1)}, bf16[512,256]{1,0:T(8,128)(2,1)}, u32[]{:S(2)}) %copy-start.4) | copy-done | bytes 262168
  15.8 0.7 copy-done.5
  16.5 0.7 copy-done.6
  17.3 2.2 %collective-permute-done.1.kv_2 = bf16[512,256]{1,0:T(8,128)(2,1)S(1)} collective-permute-done((bf16[512,256]{1,0:T(8,128)(2,1)}, bf16[512,256]{1,0:T(8,128)(2,1)S(1)}, u32[]{:S(2)}, u32[]{:S(2)}) %collective-permute-start.1) | collective-permute-done | bytes 262176 | tf_op jit(solution)/shard_map/ppermute | solution.py:404
  19.5 6.6 %collective-permute-done.kv_1 = bf16[512,256]{1,0:T(8,128)(2,1)S(1)} collective-permute-done((bf16[512,256]{1,0:T(8,128)(2,1)}, bf16[512,256]{1,0:T(8,128)(2,1)S(1)}, u32[]{:S(2)}, u32[]{:S(2)}) %collective-permute-start) | collective-permute-done | bytes 262176 | tf_op jit(solution)/shard_map/ppermute | solution.py:404
  26.1 4.2 %attend.3 = (bf16[128,1024]{1,0:T(8,128)(2,1)S(1)}, bf16[64,2048]{1,0:T(8,128)(2,1)S(1)}, bf16[64,2048]{1,0:T(8,128)(2,1)S(1)}) custom-call(s32[1]{0:T(128)} %bitcast.tp_ref, s32[1]{0:T(128)} %bitcast.1.rank_ref.ctx_ref, bf16[512,1024]{1,0:T(8,128)(2,1)S(1)} %copy-done, bf16[512,1024]{1,0:T(8,128)(2,1)S(1)} %copy-done, ...), custom_call_target="tpu_custom_call" | custom-call | tf_op jit(solution)/shard_map/attend/pallas_call | solution.py:265
  30.4 1.5 %collective-permute-done.3 = bf16[64,2048]{1,0:T(8,128)(2,1)S(1)} collective-permute-done((bf16[64,2048]{1,0:T(8,128)(2,1)S(1)}, bf16[64,2048]{1,0:T(8,128)(2,1)S(1)}, u32[]{:S(2)}, u32[]{:S(2)}) %collective-permute-start.3) | collective-permute-done | bytes 262176 | tf_op jit(solution)/shard_map/ppermute | solution.py:416
  32.0 1.6 %collective-permute-start.8 = (bf16[64,2048]{1,0:T(8,128)(2,1)S(1)}, bf16[64,2048]{1,0:T(8,128)(2,1)S(1)}, u32[]{:S(2)}, u32[]{:S(2)}) collective-permute-start(bf16[64,2048]{1,0:T(8,128)(2,1)S(1)} %add_convert_fusion.refs_0_), channel_id=1, source_target_pairs={{0,2},{1,3},{2,0},{3,1},{4,6},{5,7},{6,4},{7,5},{8,10},{9,11},{10,... | collective-permute-start | bytes 786440 | tf_op jit(solution)/shard_map/ppermute | solution.py:419
  33.5 5.3 %project.3 = (bf16[64,1536]{1,0:T(8,128)(2,1)S(1)}, bf16[64,1536]{1,0:T(8,128)(2,1)S(1)}, bf16[64,1536]{1,0:T(8,128)(2,1)S(1)}, bf16[64,1536]{1,0:T(8,128)(2,1)S...) custom-call(bf16[128,1024]{1,0:T(8,128)(2,1)S(1)} %get-tuple-element, ...), custom_call_target="tpu_custom_call" | custom-call | tf_op jit(solution)/shard_map/project/pallas_call | solution.py:320
  38.9 0.5 collective-permute-start.5
  39.5 0.4 collective-permute-start.7
  39.9 0.4 collective-permute-done.4.refs_4_
  40.4 0.3 collective-permute-done.5.refs_5_
  40.6 0.3 collective-permute-done.6.refs_6_
  40.9 0.3 collective-permute-done.7.refs_7_
  41.2 0.2 add.7.refs_3_
  41.4 0.6 collective-permute-start.13
  42.0 3.1 %attend.4.a_ref = bf16[128,1024]{1,0:T(8,128)(2,1)S(1)} custom-call(s32[1]{0:T(128)} %bitcast.tp_ref, s32[1]{0:T(128)} %bitcast.1.rank_ref.ctx_ref, bf16[512,1024]{1,0:T(8,128)(2,1)S(1)} %copy-done, bf16[512,1024]{1,0:T(8,128)(2,1)S(1)} %copy-done, s32[3,8,128]{2,1,0:T(8,128)S(1)} %get-tuple-element.45.table_ref, ...), custom_call_target="tpu_custom_call" | custom-call | tf_op jit(solution)/shard_map/attend/pallas_call | solution.py:265
  45.1 6.7 %project.4 = (bf16[64,2048]{1,0:T(8,128)(2,1)S(1)}, bf16[64,2048]{1,0:T(8,128)(2,1)S(1)}, bf16[64,2048]{1,0:T(8,128)(2,1)S(1)}, bf16[64,2048]{1,0:T(8,128)(2,1)S...) custom-call(bf16[128,1024]{1,0:T(8,128)(2,1)S(1)} %attend.4.a_ref, ...), custom_call_target="tpu_custom_call" | custom-call | tf_op jit(solution)/shard_map/project/pallas_call | solution.py:320
  51.8 0.5 collective-permute-start.10
  52.4 0.4 collective-permute-start.12
  52.8 0.5 collective-permute-done.9.refs_4_
  53.3 0.4 collective-permute-done.10.refs_5_
  53.7 0.4 collective-permute-done.11.refs_6_
  54.1 0.4 collective-permute-done.12.refs_7_
  54.4 0.2 add.8.refs_3_
  54.7 1.6 %collective-permute-start.22 = (bf16[64,8192]{1,0:T(8,128)(2,1)S(1)}, bf16[64,8192]{1,0:T(8,128)(2,1)S(1)}, u32[]{:S(2)}, u32[]{:S(2)}) collective-permute-start(bf16[64,8192]{1,0:T(8,128)(2,1)S(1)} %add.8.refs_3_), channel_id=1, source_target_pairs={{0,2},{1,3},{2,0},{3,1},{4,6},{5,7},{6,4},{7,5},{8,10},{9,11},{10,... | collective-permute-start | bytes 3145736 | tf_op jit(solution)/shard_map/ppermute | solution.py:419
  56.3 5.6 %collective-permute-done.13.refs_4_.refs_12_ = bf16[64,6144]{1,0:T(8,128)(2,1)S(1)} collective-permute-done((bf16[64,6144]{1,0:T(8,128)(2,1)S(1)}, bf16[64,6144]{1,0:T(8,128)(2,1)S(1)}, u32[]{:S(2)}, u32[]{:S(2)}) %collective-permute-start.13) | collective-permute-done | bytes 786464 | tf_op jit(solution)/shard_map/ppermute | solution.py:419
  61.8 5.4 %attend.5.a_ref = bf16[256,1024]{1,0:T(8,128)(2,1)S(1)} custom-call(s32[1]{0:T(128)} %bitcast.tp_ref, s32[1]{0:T(128)} %bitcast.1.rank_ref.ctx_ref, bf16[512,1024]{1,0:T(8,128)(2,1)S(1)} %copy-done, bf16[512,1024]{1,0:T(8,128)(2,1)S(1)} %copy-done, s32[3,8,128]{2,1,0:T(8,128)S(1)} %get-tuple-element.45.table_ref, ...), custom_call_target="tpu_custom_call" | custom-call | tf_op jit(solution)/shard_map/attend/pallas_call | solution.py:265
  67.3 0.8 copy-done.2
  68.0 9.1 %project.5 = (bf16[128,1024]{1,0:T(8,128)(2,1)S(1)}, bf16[128,1024]{1,0:T(8,128)(2,1)S(1)}, bf16[128,1024]{1,0:T(8,128)(2,1)S(1)}, bf16[128,1024]{1,0:T(8,128)(2...) custom-call(bf16[256,1024]{1,0:T(8,128)(2,1)} %copy-done.2, ...), custom_call_target="tpu_custom_call" | custom-call | tf_op jit(solution)/shard_map/project/pallas_call | solution.py:320
  77.2 0.5 collective-permute-start.15
  77.8 0.4 collective-permute-start.17
  78.2 0.5 collective-permute-done.14.refs_2_.refs_8_
  78.9 0.2 collective-permute-done.15.refs_3_.refs_9_
  79.3 0.2 collective-permute-done.16.refs_6_.refs_10_
  79.6 0.2 collective-permute-done.17.refs_7_.refs_11_
  80.0 0.8 finish.3.refs_13_
  80.8 0.2 collective-permute-done.20.refs_10_.refs_14_
  81.0 0.4 collective-permute-done.21.refs_11_.refs_15_
  81.4 1.0 %finish.4.refs_17_ = bf16[128,8192]{1,0:T(8,128)(2,1)} custom-call(bf16[128,1024]{1,0:T(8,128)(2,1)S(1)} %get-tuple-element.69.refs_0_.refs_2_, bf16[128,1024]{1,0:T(8,128)(2,1)S(1)} %get-tuple-element.70.refs_1_.refs_3_, bf16[128,1024]{1,0:T(8,128)(2,1)S(1)} %get-tuple-element.71.refs_2_.refs_4_, ...), custom_call_target="tpu_custom_call", output_to_operand_aliasing={{}: (13, {})} | custom-call | tf_op jit(solution)/shard_map/finish/pallas_call | solution.py:381
  82.4 1.2 %collective-permute-done.22.refs_16_ = bf16[64,8192]{1,0:T(8,128)(2,1)S(1)} collective-permute-done((bf16[64,8192]{1,0:T(8,128)(2,1)S(1)}, bf16[64,8192]{1,0:T(8,128)(2,1)S(1)}, u32[]{:S(2)}, u32[]{:S(2)}) %collective-permute-start.22) | collective-permute-done | bytes 1048608 | tf_op jit(solution)/shard_map/ppermute | solution.py:419
  83.6 1.1 %finish.5 = bf16[128,8192]{1,0:T(8,128)(2,1)} custom-call(bf16[128,1024]{1,0:T(8,128)(2,1)S(1)} %get-tuple-element.67.refs_0_, bf16[128,1024]{1,0:T(8,128)(2,1)S(1)} %get-tuple-element.68.refs_1_, bf16[128,1024]{1,0:T(8,128)(2,1)S(1)} %get-tuple-element.69.refs_0_.refs_2_, ...), custom_call_target="tpu_custom_call", output_to_operand_aliasing={{}: (17, {})} | custom-call | tf_op jit(solution)/shard_map/finish/pallas_call | solution.py:381
  (29 shorter events, 1.3 us)
Async XLA Ops:
  0.0 26.1 %copy-start = (bf16[512,1024]{1,0:T(8,128)(2,1)S(1)}, bf16[512,1024]{1,0:T(8,128)(2,1)}, u32[]{:S(2)}) copy-start(bf16[512,1024]{1,0:T(8,128)(2,1)} %q_1.5) | copy-start | bytes 3145732
  2.2 12.0 %all-to-all-start = ((bf16[4,128,256]{2,1,0:T(8,128)(2,1)}), bf16[4,128,256]{2,1,0:T(8,128)(2,1)S(1)}, u32[]{:S(2)}, u32[]{:S(2)}) async-start(bf16[4,128,256]{2,1,0:T(8,128)(2,1)} %get-tuple-element.47), calls=%async_computation | async-start | bytes 524288 | tf_op jit(solution)/shard_map/all_to_all | solution.py:409
  7.4 12.1 %collective-permute-start.1 = (bf16[512,256]{1,0:T(8,128)(2,1)}, bf16[512,256]{1,0:T(8,128)(2,1)S(1)}, u32[]{:S(2)}, u32[]{:S(2)}) collective-permute-start(bf16[512,256]{1,0:T(8,128)(2,1)} %get-tuple-element.44.own_ref), channel_id=1, source_target_pairs={{0,8},{4,12},{8,16},{12,20},{16,24},{20,28},{1,9},{5,13},{9,17},{1... | collective-permute-start | bytes 786440 | tf_op jit(solution)/shard_map/ppermute | solution.py:404
  10.7 15.3 %collective-permute-start = (bf16[512,256]{1,0:T(8,128)(2,1)}, bf16[512,256]{1,0:T(8,128)(2,1)S(1)}, u32[]{:S(2)}, u32[]{:S(2)}) collective-permute-start(bf16[512,256]{1,0:T(8,128)(2,1)} %get-tuple-element.44.own_ref), channel_id=1, source_target_pairs={{0,4},{4,8},{8,12},{12,16},{16,20},{20,24},{24,28},{1,5},{5,9},{9,... | collective-permute-start | bytes 786440 | tf_op jit(solution)/shard_map/ppermute | solution.py:404
  14.2 11.9 %collective-permute-start.2 = (bf16[3,128,256]{2,1,0:T(8,128)(2,1)S(1)}, bf16[3,128,256]{2,1,0:T(8,128)(2,1)S(1)}, u32[]{:S(2)}, u32[]{:S(2)}) collective-permute-start(bf16[3,128,256]{2,1,0:T(8,128)(2,1)S(1)} %slice.4), channel_id=1, source_target_pairs={{0,4},{4,0},{8,12},{12,8},{16,20},{20,16},{24,28},{28,24},{1,5},{5... | collective-permute-start | bytes 589832 | tf_op jit(solution)/shard_map/ppermute | solution.py:411
  14.8 0.9 %copy-start.4 = (bf16[512,256]{1,0:T(8,128)(2,1)S(1)}, bf16[512,256]{1,0:T(8,128)(2,1)}, u32[]{:S(2)}) copy-start(bf16[512,256]{1,0:T(8,128)(2,1)} %get-tuple-element.44.own_ref) | copy-start | bytes 786436
  15.8 0.7 copy-start.5
  16.5 0.7 copy-start.6
  30.3 1.6 %collective-permute-start.3 = (bf16[64,2048]{1,0:T(8,128)(2,1)S(1)}, bf16[64,2048]{1,0:T(8,128)(2,1)S(1)}, u32[]{:S(2)}, u32[]{:S(2)}) collective-permute-start(bf16[64,2048]{1,0:T(8,128)(2,1)S(1)} %get-tuple-element.50), channel_id=1, source_target_pairs={{0,1},{1,0},{2,3},{3,2},{4,5},{5,4},{6,7},{7,6},{8,9},{9,8},{10,11... | collective-permute-start | bytes 786440 | tf_op jit(solution)/shard_map/ppermute | solution.py:416
  32.0 13.1 %collective-permute-start.8 = (bf16[64,2048]{1,0:T(8,128)(2,1)S(1)}, bf16[64,2048]{1,0:T(8,128)(2,1)S(1)}, u32[]{:S(2)}, u32[]{:S(2)}) collective-permute-start(bf16[64,2048]{1,0:T(8,128)(2,1)S(1)} %add_convert_fusion.refs_0_), channel_id=1, source_target_pairs={{0,2},{1,3},{2,0},{3,1},{4,6},{5,7},{6,4},{7,5},{8,10},{9,11},{10,... | collective-permute-start | bytes 786440 | tf_op jit(solution)/shard_map/ppermute | solution.py:419
  38.8 1.5 %collective-permute-start.4 = (bf16[64,1536]{1,0:T(8,128)(2,1)S(1)}, bf16[64,1536]{1,0:T(8,128)(2,1)S(1)}, u32[]{:S(2)}, u32[]{:S(2)}) collective-permute-start(bf16[64,1536]{1,0:T(8,128)(2,1)S(1)} %get-tuple-element.55), channel_id=1, source_target_pairs={{0,1},{1,0},{2,3},{3,2},{4,5},{5,4},{6,7},{7,6},{8,9},{9,8},{10,11... | collective-permute-start | bytes 589832 | tf_op jit(solution)/shard_map/ppermute | solution.py:416
  38.9 1.7 %collective-permute-start.5 = (bf16[64,1536]{1,0:T(8,128)(2,1)S(1)}, bf16[64,1536]{1,0:T(8,128)(2,1)S(1)}, u32[]{:S(2)}, u32[]{:S(2)}) collective-permute-start(bf16[64,1536]{1,0:T(8,128)(2,1)S(1)} %get-tuple-element.56), channel_id=1, source_target_pairs={{0,1},{1,0},{2,3},{3,2},{4,5},{5,4},{6,7},{7,6},{8,9},{9,8},{10,11... | collective-permute-start | bytes 589832 | tf_op jit(solution)/shard_map/ppermute | solution.py:416
  39.4 1.5 %collective-permute-start.6 = (bf16[64,1536]{1,0:T(8,128)(2,1)S(1)}, bf16[64,1536]{1,0:T(8,128)(2,1)S(1)}, u32[]{:S(2)}, u32[]{:S(2)}) collective-permute-start(bf16[64,1536]{1,0:T(8,128)(2,1)S(1)} %get-tuple-element.57), channel_id=1, source_target_pairs={{0,1},{1,0},{2,3},{3,2},{4,5},{5,4},{6,7},{7,6},{8,9},{9,8},{10,11... | collective-permute-start | bytes 589832 | tf_op jit(solution)/shard_map/ppermute | solution.py:416
  39.5 1.7 %collective-permute-start.7 = (bf16[64,1536]{1,0:T(8,128)(2,1)S(1)}, bf16[64,1536]{1,0:T(8,128)(2,1)S(1)}, u32[]{:S(2)}, u32[]{:S(2)}) collective-permute-start(bf16[64,1536]{1,0:T(8,128)(2,1)S(1)} %get-tuple-element.58), channel_id=1, source_target_pairs={{0,1},{1,0},{2,3},{3,2},{4,5},{5,4},{6,7},{7,6},{8,9},{9,8},{10,11... | collective-permute-start | bytes 589832 | tf_op jit(solution)/shard_map/ppermute | solution.py:416
  41.4 20.4 %collective-permute-start.13 = (bf16[64,6144]{1,0:T(8,128)(2,1)S(1)}, bf16[64,6144]{1,0:T(8,128)(2,1)S(1)}, u32[]{:S(2)}, u32[]{:S(2)}) collective-permute-start(bf16[64,6144]{1,0:T(8,128)(2,1)S(1)} %add.7.refs_3_), channel_id=1, source_target_pairs={{0,2},{1,3},{2,0},{3,1},{4,6},{5,7},{6,4},{7,5},{8,10},{9,11},{10,... | collective-permute-start | bytes 2359304 | tf_op jit(solution)/shard_map/ppermute | solution.py:419
  51.7 1.6 %collective-permute-start.9 = (bf16[64,2048]{1,0:T(8,128)(2,1)S(1)}, bf16[64,2048]{1,0:T(8,128)(2,1)S(1)}, u32[]{:S(2)}, u32[]{:S(2)}) collective-permute-start(bf16[64,2048]{1,0:T(8,128)(2,1)S(1)} %get-tuple-element.63), channel_id=1, source_target_pairs={{0,1},{1,0},{2,3},{3,2},{4,5},{5,4},{6,7},{7,6},{8,9},{9,8},{10,11... | collective-permute-start | bytes 786440 | tf_op jit(solution)/shard_map/ppermute | solution.py:416
  51.8 1.9 %collective-permute-start.10 = (bf16[64,2048]{1,0:T(8,128)(2,1)S(1)}, bf16[64,2048]{1,0:T(8,128)(2,1)S(1)}, u32[]{:S(2)}, u32[]{:S(2)}) collective-permute-start(bf16[64,2048]{1,0:T(8,128)(2,1)S(1)} %get-tuple-element.64), channel_id=1, source_target_pairs={{0,1},{1,0},{2,3},{3,2},{4,5},{5,4},{6,7},{7,6},{8,9},{9,8},{10,11... | collective-permute-start | bytes 786440 | tf_op jit(solution)/shard_map/ppermute | solution.py:416
  52.3 1.8 %collective-permute-start.11 = (bf16[64,2048]{1,0:T(8,128)(2,1)S(1)}, bf16[64,2048]{1,0:T(8,128)(2,1)S(1)}, u32[]{:S(2)}, u32[]{:S(2)}) collective-permute-start(bf16[64,2048]{1,0:T(8,128)(2,1)S(1)} %get-tuple-element.65), channel_id=1, source_target_pairs={{0,1},{1,0},{2,3},{3,2},{4,5},{5,4},{6,7},{7,6},{8,9},{9,8},{10,11... | collective-permute-start | bytes 786440 | tf_op jit(solution)/shard_map/ppermute | solution.py:416
  52.4 2.1 %collective-permute-start.12 = (bf16[64,2048]{1,0:T(8,128)(2,1)S(1)}, bf16[64,2048]{1,0:T(8,128)(2,1)S(1)}, u32[]{:S(2)}, u32[]{:S(2)}) collective-permute-start(bf16[64,2048]{1,0:T(8,128)(2,1)S(1)} %get-tuple-element.66), channel_id=1, source_target_pairs={{0,1},{1,0},{2,3},{3,2},{4,5},{5,4},{6,7},{7,6},{8,9},{9,8},{10,11... | collective-permute-start | bytes 786440 | tf_op jit(solution)/shard_map/ppermute | solution.py:416
  54.7 7.1 %copy-start.1 = (bf16[64,8192]{1,0:T(8,128)(2,1)}, bf16[64,8192]{1,0:T(8,128)(2,1)S(1)}, u32[]{:S(2)}) copy-start(bf16[64,8192]{1,0:T(8,128)(2,1)S(1)} %add.8.refs_3_) | copy-start | bytes 3145732
  54.7 28.9 %collective-permute-start.22 = (bf16[64,8192]{1,0:T(8,128)(2,1)S(1)}, bf16[64,8192]{1,0:T(8,128)(2,1)S(1)}, u32[]{:S(2)}, u32[]{:S(2)}) collective-permute-start(bf16[64,8192]{1,0:T(8,128)(2,1)S(1)} %add.8.refs_3_), channel_id=1, source_target_pairs={{0,2},{1,3},{2,0},{3,1},{4,6},{5,7},{6,4},{7,5},{8,10},{9,11},{10,... | collective-permute-start | bytes 3145736 | tf_op jit(solution)/shard_map/ppermute | solution.py:419
  67.2 0.8 copy-start.2
  77.1 4.3 %copy-start.3 = (bf16[128,1024]{1,0:T(8,128)(2,1)S(1)}, bf16[128,1024]{1,0:T(8,128)(2,1)}, u32[]{:S(2)}) copy-start(bf16[128,1024]{1,0:T(8,128)(2,1)} %get-tuple-element.74.refs_5_.refs_7_) | copy-start | bytes 786436
  77.1 1.6 %collective-permute-start.14 = (bf16[128,1024]{1,0:T(8,128)(2,1)S(1)}, bf16[128,1024]{1,0:T(8,128)(2,1)S(1)}, u32[]{:S(2)}, u32[]{:S(2)}) collective-permute-start(bf16[128,1024]{1,0:T(8,128)(2,1)S(1)} %get-tuple-element.75), channel_id=1, source_target_pairs={{0,1},{1,0},{2,3},{3,2},{4,5},{5,4},{6,7},{7,6},{8,9},{9,8},{10,11... | collective-permute-start | bytes 786440 | tf_op jit(solution)/shard_map/ppermute | solution.py:416
  77.2 1.9 %collective-permute-start.15 = (bf16[128,1024]{1,0:T(8,128)(2,1)S(1)}, bf16[128,1024]{1,0:T(8,128)(2,1)S(1)}, u32[]{:S(2)}, u32[]{:S(2)}) collective-permute-start(bf16[128,1024]{1,0:T(8,128)(2,1)S(1)} %get-tuple-element.76), channel_id=1, source_target_pairs={{0,1},{1,0},{2,3},{3,2},{4,5},{5,4},{6,7},{7,6},{8,9},{9,8},{10,11... | collective-permute-start | bytes 786440 | tf_op jit(solution)/shard_map/ppermute | solution.py:416
  77.7 1.8 %collective-permute-start.16 = (bf16[128,1024]{1,0:T(8,128)(2,1)S(1)}, bf16[128,1024]{1,0:T(8,128)(2,1)S(1)}, u32[]{:S(2)}, u32[]{:S(2)}) collective-permute-start(bf16[128,1024]{1,0:T(8,128)(2,1)S(1)} %get-tuple-element.77), channel_id=1, source_target_pairs={{0,1},{1,0},{2,3},{3,2},{4,5},{5,4},{6,7},{7,6},{8,9},{9,8},{10,11... | collective-permute-start | bytes 786440 | tf_op jit(solution)/shard_map/ppermute | solution.py:416
  77.8 2.1 %collective-permute-start.17 = (bf16[128,1024]{1,0:T(8,128)(2,1)S(1)}, bf16[128,1024]{1,0:T(8,128)(2,1)S(1)}, u32[]{:S(2)}, u32[]{:S(2)}) collective-permute-start(bf16[128,1024]{1,0:T(8,128)(2,1)S(1)} %get-tuple-element.78), channel_id=1, source_target_pairs={{0,1},{1,0},{2,3},{3,2},{4,5},{5,4},{6,7},{7,6},{8,9},{9,8},{10,11... | collective-permute-start | bytes 786440 | tf_op jit(solution)/shard_map/ppermute | solution.py:416
  78.7 2.0 %collective-permute-start.18 = (bf16[128,1024]{1,0:T(8,128)(2,1)S(1)}, bf16[128,1024]{1,0:T(8,128)(2,1)S(1)}, u32[]{:S(2)}, u32[]{:S(2)}) collective-permute-start(bf16[128,1024]{1,0:T(8,128)(2,1)S(1)} %get-tuple-element.79), channel_id=1, source_target_pairs={{0,1},{1,0},{2,3},{3,2},{4,5},{5,4},{6,7},{7,6},{8,9},{9,8},{10,11... | collective-permute-start | bytes 786440 | tf_op jit(solution)/shard_map/ppermute | solution.py:416
  79.1 1.7 %collective-permute-start.19 = (bf16[128,1024]{1,0:T(8,128)(2,1)S(1)}, bf16[128,1024]{1,0:T(8,128)(2,1)S(1)}, u32[]{:S(2)}, u32[]{:S(2)}) collective-permute-start(bf16[128,1024]{1,0:T(8,128)(2,1)S(1)} %get-tuple-element.80), channel_id=1, source_target_pairs={{0,1},{1,0},{2,3},{3,2},{4,5},{5,4},{6,7},{7,6},{8,9},{9,8},{10,11... | collective-permute-start | bytes 786440 | tf_op jit(solution)/shard_map/ppermute | solution.py:416
  79.5 1.5 %collective-permute-start.20 = (bf16[128,1024]{1,0:T(8,128)(2,1)S(1)}, bf16[128,1024]{1,0:T(8,128)(2,1)S(1)}, u32[]{:S(2)}, u32[]{:S(2)}) collective-permute-start(bf16[128,1024]{1,0:T(8,128)(2,1)S(1)} %get-tuple-element.81), channel_id=1, source_target_pairs={{0,1},{1,0},{2,3},{3,2},{4,5},{5,4},{6,7},{7,6},{8,9},{9,8},{10,11... | collective-permute-start | bytes 786440 | tf_op jit(solution)/shard_map/ppermute | solution.py:416
  79.9 1.5 %collective-permute-start.21 = (bf16[128,1024]{1,0:T(8,128)(2,1)S(1)}, bf16[128,1024]{1,0:T(8,128)(2,1)S(1)}, u32[]{:S(2)}, u32[]{:S(2)}) collective-permute-start(bf16[128,1024]{1,0:T(8,128)(2,1)S(1)} %get-tuple-element.82), channel_id=1, source_target_pairs={{0,1},{1,0},{2,3},{3,2},{4,5},{5,4},{6,7},{7,6},{8,9},{9,8},{10,11... | collective-permute-start | bytes 786440 | tf_op jit(solution)/shard_map/ppermute | solution.py:416

commit v13 on v12

--- a/solution.py
+++ b/solution.py
@@ -122,7 +122,7 @@
 
 
 def attend_kernel(
-    slots, tiles, sizes, place, tp_ref, ctx_ref, q_0, q_1, table_ref, own, kv_1, kv_2, *refs
+    slots, tiles, sizes, place, tp_ref, ctx_ref, q_0, q_1, table_ref, own, kv_2, kv_1, *refs
 ):
     pairs = refs[:2]
     w_hbm = refs[2]
@@ -410,7 +410,7 @@
     needed = pairs[0][: half - 1]
     pairs.append(lax.ppermute(needed, "ctx", [(r, r ^ 1) for r in range(ctx_size)]))
     table, own_copy = tables(ctx, vertical, slash, own, half - 1)
-    near_kv = [own_copy, shifted(own, 1), shifted(own, 2)]
+    near_kv = [own_copy, shifted(own, 2), shifted(own, 1)]
 
     def sibling(x):
         return lax.ppermute(x, "tp", [(j, j ^ 1) for j in range(4)])

time: 85.2 us -> 84.3 us (0.989)
  waiting for transfers between devices: 21.8 us -> 20.4 us
    ppermute x2, waiting for transfers between devices: 8.77 us -> 3.95 us  [shifted(): return lax.ppermute(x, 'ctx', [(r, r + by) for r in range(ctx_size - by)])]
    ppermute x1, waiting for transfers between devices: 0.01 us -> 3.41 us  [shards(): lax.ppermute(needed, 'ctx', [(r, r ^ 1) for r in range(ctx_size)])]
  transfers between devices with their start and end apart: 24 -> 24, of which waited for: 19 -> 19; matrix products, arithmetic and copies ran while one was open for 0% -> 0% of each run, Pallas kernels for 37% -> 38%
where the time goes in v13:
time: 84.3 us; the launch traced here: 83.4 us
  Pallas kernels  39.3 us (47%)
  waiting for transfers between devices  20.4 us (24%)
  starting transfers between devices  20.2 us (24%)
  local copies, waits for them, and re-layouts  3.14 us (4%)
    pallas_call x3, Pallas kernels, project(): pl.pallas_call(functools.partial(project_kernel, first), out_shape=[part]...  21 us
    pallas_call x3, Pallas kernels, attend(): pl.pallas_call(functools.partial(attend_kernel, slots, tiles, sizes, plac...  12.7 us
    ppermute x2, starting transfers between devices, shifted(): return lax.ppermute(x, 'ctx', [(r, r + by) for r in range(ctx_size - by)])  6.79 us
    ppermute x3, waiting for transfers between devices, across(): return lax.ppermute(x, 'tp', [(j, j ^ 2) for j in range(4)])  6.77 us
    ppermute x17, waiting for transfers between devices, sibling(): return lax.ppermute(x, 'tp', [(j, j ^ 1) for j in range(4)])  6.25 us
    all_to_all x1, starting transfers between devices, shards(): lax.all_to_all(pair, 'ctx', 0, 0, axis_index_groups=parities, tiled=True)  5.2 us
    ppermute x2, waiting for transfers between devices, shifted(): return lax.ppermute(x, 'ctx', [(r, r + by) for r in range(ctx_size - by)])  3.95 us
    ppermute x17, starting transfers between devices, sibling(): return lax.ppermute(x, 'tp', [(j, j ^ 1) for j in range(4)])  3.87 us
  transfers between devices with their start and end apart: 24, of which 19 were waited for; matrix products, arithmetic and copies ran while one was open for 0% of the time, Pallas kernels for 38%

profile of v13, /device:TPU:16, one launch (start us, length us, event | category | flops | bytes accessed | tf_op | source)
XLA Modules:
  0.0 83.4 jit_solution(3208098074629890024)
XLA Ops:
  0.0 2.2 %pick.1 = (bf16[512,256]{1,0:T(8,128)(2,1)}, bf16[4,128,256]{2,1,0:T(8,128)(2,1)}) custom-call(s32[1]{0:T(128)} %bitcast.1.rank_ref.ctx_ref, s32[8,16]{1,0:T(8,128)} %vert_ref.3, bf16[512,128]{1,0:T(8,128)(2,1)} %k_ref.1, bf16[512,128]{1,0:T(8,128)(2,1)} %v_ref.1), custom_call_target="tpu_custom_call" | custom-call | tf_op jit(solution)/shard_map/pick/pallas_call | solution.py:64
  2.2 5.2 %all-to-all-start = ((bf16[4,128,256]{2,1,0:T(8,128)(2,1)}), bf16[4,128,256]{2,1,0:T(8,128)(2,1)S(1)}, u32[]{:S(2)}, u32[]{:S(2)}) async-start(bf16[4,128,256]{2,1,0:T(8,128)(2,1)} %get-tuple-element.47), calls=%async_computation | async-start | bytes 524288 | tf_op jit(solution)/shard_map/all_to_all | solution.py:409
  7.4 3.4 %collective-permute-start.1 = (bf16[512,256]{1,0:T(8,128)(2,1)}, bf16[512,256]{1,0:T(8,128)(2,1)S(1)}, u32[]{:S(2)}, u32[]{:S(2)}) collective-permute-start(bf16[512,256]{1,0:T(8,128)(2,1)} %get-tuple-element.44.own_ref), channel_id=1, source_target_pairs={{0,4},{4,8},{8,12},{12,16},{16,20},{20,24},{24,28},{1,5},{5,9},{9,... | collective-permute-start | bytes 786440 | tf_op jit(solution)/shard_map/ppermute | solution.py:404
  10.8 3.4 %collective-permute-start = (bf16[512,256]{1,0:T(8,128)(2,1)}, bf16[512,256]{1,0:T(8,128)(2,1)S(1)}, u32[]{:S(2)}, u32[]{:S(2)}) collective-permute-start(bf16[512,256]{1,0:T(8,128)(2,1)} %get-tuple-element.44.own_ref), channel_id=1, source_target_pairs={{0,8},{4,12},{8,16},{12,20},{16,24},{20,28},{1,9},{5,13},{9,17},{1... | collective-permute-start | bytes 786440 | tf_op jit(solution)/shard_map/ppermute | solution.py:404
  14.2 0.6 collective-permute-start.2
  14.8 0.9 %copy-done.4 = bf16[512,256]{1,0:T(8,128)(2,1)S(1)} copy-done((bf16[512,256]{1,0:T(8,128)(2,1)S(1)}, bf16[512,256]{1,0:T(8,128)(2,1)}, u32[]{:S(2)}) %copy-start.4) | copy-done | bytes 262168
  15.8 0.7 copy-done.5
  16.5 0.7 copy-done.6
  17.3 3.9 %collective-permute-done.1.kv_1 = bf16[512,256]{1,0:T(8,128)(2,1)S(1)} collective-permute-done((bf16[512,256]{1,0:T(8,128)(2,1)}, bf16[512,256]{1,0:T(8,128)(2,1)S(1)}, u32[]{:S(2)}, u32[]{:S(2)}) %collective-permute-start.1) | collective-permute-done | bytes 262176 | tf_op jit(solution)/shard_map/ppermute | solution.py:404
  21.3 3.4 %collective-permute-done.2.refs_1_ = bf16[3,128,256]{2,1,0:T(8,128)(2,1)S(1)} collective-permute-done((bf16[3,128,256]{2,1,0:T(8,128)(2,1)S(1)}, bf16[3,128,256]{2,1,0:T(8,128)(2,1)S(1)}, u32[]{:S(2)}, u32[]{:S(2)}) %collective-permute-start.2) | collective-permute-done | bytes 196640 | tf_op jit(solution)/shard_map/ppermute | solution.py:411
  24.7 4.2 %attend.3 = (bf16[128,1024]{1,0:T(8,128)(2,1)S(1)}, bf16[64,2048]{1,0:T(8,128)(2,1)S(1)}, bf16[64,2048]{1,0:T(8,128)(2,1)S(1)}) custom-call(s32[1]{0:T(128)} %bitcast.tp_ref, s32[1]{0:T(128)} %bitcast.1.rank_ref.ctx_ref, bf16[512,1024]{1,0:T(8,128)(2,1)S(1)} %copy-done, bf16[512,1024]{1,0:T(8,128)(2,1)S(1)} %copy-done, ...), custom_call_target="tpu_custom_call" | custom-call | tf_op jit(solution)/shard_map/attend/pallas_call | solution.py:265
  29.0 1.5 %collective-permute-done.3 = bf16[64,2048]{1,0:T(8,128)(2,1)S(1)} collective-permute-done((bf16[64,2048]{1,0:T(8,128)(2,1)S(1)}, bf16[64,2048]{1,0:T(8,128)(2,1)S(1)}, u32[]{:S(2)}, u32[]{:S(2)}) %collective-permute-start.3) | collective-permute-done | bytes 262176 | tf_op jit(solution)/shard_map/ppermute | solution.py:416
  30.6 1.6 %collective-permute-start.8 = (bf16[64,2048]{1,0:T(8,128)(2,1)S(1)}, bf16[64,2048]{1,0:T(8,128)(2,1)S(1)}, u32[]{:S(2)}, u32[]{:S(2)}) collective-permute-start(bf16[64,2048]{1,0:T(8,128)(2,1)S(1)} %add_convert_fusion.refs_0_), channel_id=1, source_target_pairs={{0,2},{1,3},{2,0},{3,1},{4,6},{5,7},{6,4},{7,5},{8,10},{9,11},{10,... | collective-permute-start | bytes 786440 | tf_op jit(solution)/shard_map/ppermute | solution.py:419
  32.1 5.3 %project.3 = (bf16[64,1536]{1,0:T(8,128)(2,1)S(1)}, bf16[64,1536]{1,0:T(8,128)(2,1)S(1)}, bf16[64,1536]{1,0:T(8,128)(2,1)S(1)}, bf16[64,1536]{1,0:T(8,128)(2,1)S...) custom-call(bf16[128,1024]{1,0:T(8,128)(2,1)S(1)} %get-tuple-element, ...), custom_call_target="tpu_custom_call" | custom-call | tf_op jit(solution)/shard_map/project/pallas_call | solution.py:320
  37.5 0.5 collective-permute-start.5
  38.1 0.4 collective-permute-start.7
  38.5 0.4 collective-permute-done.4.refs_4_
  38.9 0.3 collective-permute-done.5.refs_5_
  39.2 0.3 collective-permute-done.6.refs_6_
  39.5 0.3 collective-permute-done.7.refs_7_
  39.8 0.2 add.7.refs_3_
  40.0 0.6 collective-permute-start.13
  40.6 3.1 %attend.4.a_ref = bf16[128,1024]{1,0:T(8,128)(2,1)S(1)} custom-call(s32[1]{0:T(128)} %bitcast.tp_ref, s32[1]{0:T(128)} %bitcast.1.rank_ref.ctx_ref, bf16[512,1024]{1,0:T(8,128)(2,1)S(1)} %copy-done, bf16[512,1024]{1,0:T(8,128)(2,1)S(1)} %copy-done, s32[3,8,128]{2,1,0:T(8,128)S(1)} %get-tuple-element.45.table_ref, ...), custom_call_target="tpu_custom_call" | custom-call | tf_op jit(solution)/shard_map/attend/pallas_call | solution.py:265
  43.6 6.7 %project.4 = (bf16[64,2048]{1,0:T(8,128)(2,1)S(1)}, bf16[64,2048]{1,0:T(8,128)(2,1)S(1)}, bf16[64,2048]{1,0:T(8,128)(2,1)S(1)}, bf16[64,2048]{1,0:T(8,128)(2,1)S...) custom-call(bf16[128,1024]{1,0:T(8,128)(2,1)S(1)} %attend.4.a_ref, ...), custom_call_target="tpu_custom_call" | custom-call | tf_op jit(solution)/shard_map/project/pallas_call | solution.py:320
  50.4 0.5 collective-permute-start.10
  51.0 0.4 collective-permute-start.12
  51.4 0.5 collective-permute-done.9.refs_4_
  51.9 0.4 collective-permute-done.10.refs_5_
  52.3 0.4 collective-permute-done.11.refs_6_
  52.7 0.4 collective-permute-done.12.refs_7_
  53.0 0.2 add.8.refs_3_
  53.3 1.6 %collective-permute-start.22 = (bf16[64,8192]{1,0:T(8,128)(2,1)S(1)}, bf16[64,8192]{1,0:T(8,128)(2,1)S(1)}, u32[]{:S(2)}, u32[]{:S(2)}) collective-permute-start(bf16[64,8192]{1,0:T(8,128)(2,1)S(1)} %add.8.refs_3_), channel_id=1, source_target_pairs={{0,2},{1,3},{2,0},{3,1},{4,6},{5,7},{6,4},{7,5},{8,10},{9,11},{10,... | collective-permute-start | bytes 3145736 | tf_op jit(solution)/shard_map/ppermute | solution.py:419
  54.8 5.6 %collective-permute-done.13.refs_4_.refs_12_ = bf16[64,6144]{1,0:T(8,128)(2,1)S(1)} collective-permute-done((bf16[64,6144]{1,0:T(8,128)(2,1)S(1)}, bf16[64,6144]{1,0:T(8,128)(2,1)S(1)}, u32[]{:S(2)}, u32[]{:S(2)}) %collective-permute-start.13) | collective-permute-done | bytes 786464 | tf_op jit(solution)/shard_map/ppermute | solution.py:419
  60.4 5.4 %attend.5.a_ref = bf16[256,1024]{1,0:T(8,128)(2,1)S(1)} custom-call(s32[1]{0:T(128)} %bitcast.tp_ref, s32[1]{0:T(128)} %bitcast.1.rank_ref.ctx_ref, bf16[512,1024]{1,0:T(8,128)(2,1)S(1)} %copy-done, bf16[512,1024]{1,0:T(8,128)(2,1)S(1)} %copy-done, s32[3,8,128]{2,1,0:T(8,128)S(1)} %get-tuple-element.45.table_ref, ...), custom_call_target="tpu_custom_call" | custom-call | tf_op jit(solution)/shard_map/attend/pallas_call | solution.py:265
  65.8 0.8 copy-done.2
  66.6 9.1 %project.5 = (bf16[128,1024]{1,0:T(8,128)(2,1)S(1)}, bf16[128,1024]{1,0:T(8,128)(2,1)S(1)}, bf16[128,1024]{1,0:T(8,128)(2,1)S(1)}, bf16[128,1024]{1,0:T(8,128)(2...) custom-call(bf16[256,1024]{1,0:T(8,128)(2,1)} %copy-done.2, ...), custom_call_target="tpu_custom_call" | custom-call | tf_op jit(solution)/shard_map/project/pallas_call | solution.py:320
  75.8 0.5 collective-permute-start.15
  76.4 0.4 collective-permute-start.17
  76.8 0.5 collective-permute-done.14.refs_2_.refs_8_
  77.5 0.2 collective-permute-done.15.refs_3_.refs_9_
  77.8 0.2 collective-permute-done.16.refs_6_.refs_10_
  78.2 0.2 collective-permute-done.17.refs_7_.refs_11_
  78.6 0.8 finish.3.refs_13_
  79.4 0.2 collective-permute-done.20.refs_10_.refs_14_
  79.6 0.4 collective-permute-done.21.refs_11_.refs_15_
  80.0 1.0 %finish.4.refs_17_ = bf16[128,8192]{1,0:T(8,128)(2,1)} custom-call(bf16[128,1024]{1,0:T(8,128)(2,1)S(1)} %get-tuple-element.69.refs_0_.refs_2_, bf16[128,1024]{1,0:T(8,128)(2,1)S(1)} %get-tuple-element.70.refs_1_.refs_3_, bf16[128,1024]{1,0:T(8,128)(2,1)S(1)} %get-tuple-element.71.refs_2_.refs_4_, ...), custom_call_target="tpu_custom_call", output_to_operand_aliasing={{}: (13, {})} | custom-call | tf_op jit(solution)/shard_map/finish/pallas_call | solution.py:381
  81.0 1.2 %collective-permute-done.22.refs_16_ = bf16[64,8192]{1,0:T(8,128)(2,1)S(1)} collective-permute-done((bf16[64,8192]{1,0:T(8,128)(2,1)S(1)}, bf16[64,8192]{1,0:T(8,128)(2,1)S(1)}, u32[]{:S(2)}, u32[]{:S(2)}) %collective-permute-start.22) | collective-permute-done | bytes 1048608 | tf_op jit(solution)/shard_map/ppermute | solution.py:419
  82.2 1.1 %finish.5 = bf16[128,8192]{1,0:T(8,128)(2,1)} custom-call(bf16[128,1024]{1,0:T(8,128)(2,1)S(1)} %get-tuple-element.67.refs_0_, bf16[128,1024]{1,0:T(8,128)(2,1)S(1)} %get-tuple-element.68.refs_1_, bf16[128,1024]{1,0:T(8,128)(2,1)S(1)} %get-tuple-element.69.refs_0_.refs_2_, ...), custom_call_target="tpu_custom_call", output_to_operand_aliasing={{}: (17, {})} | custom-call | tf_op jit(solution)/shard_map/finish/pallas_call | solution.py:381
  (29 shorter events, 1.3 us)
Async XLA Ops:
  0.0 24.7 %copy-start = (bf16[512,1024]{1,0:T(8,128)(2,1)S(1)}, bf16[512,1024]{1,0:T(8,128)(2,1)}, u32[]{:S(2)}) copy-start(bf16[512,1024]{1,0:T(8,128)(2,1)} %q_1.5) | copy-start | bytes 3145732
  2.2 12.0 %all-to-all-start = ((bf16[4,128,256]{2,1,0:T(8,128)(2,1)}), bf16[4,128,256]{2,1,0:T(8,128)(2,1)S(1)}, u32[]{:S(2)}, u32[]{:S(2)}) async-start(bf16[4,128,256]{2,1,0:T(8,128)(2,1)} %get-tuple-element.47), calls=%async_computation | async-start | bytes 524288 | tf_op jit(solution)/shard_map/all_to_all | solution.py:409
  7.4 13.9 %collective-permute-start.1 = (bf16[512,256]{1,0:T(8,128)(2,1)}, bf16[512,256]{1,0:T(8,128)(2,1)S(1)}, u32[]{:S(2)}, u32[]{:S(2)}) collective-permute-start(bf16[512,256]{1,0:T(8,128)(2,1)} %get-tuple-element.44.own_ref), channel_id=1, source_target_pairs={{0,4},{4,8},{8,12},{12,16},{16,20},{20,24},{24,28},{1,5},{5,9},{9,... | collective-permute-start | bytes 786440 | tf_op jit(solution)/shard_map/ppermute | solution.py:404
  10.8 10.5 %collective-permute-start = (bf16[512,256]{1,0:T(8,128)(2,1)}, bf16[512,256]{1,0:T(8,128)(2,1)S(1)}, u32[]{:S(2)}, u32[]{:S(2)}) collective-permute-start(bf16[512,256]{1,0:T(8,128)(2,1)} %get-tuple-element.44.own_ref), channel_id=1, source_target_pairs={{0,8},{4,12},{8,16},{12,20},{16,24},{20,28},{1,9},{5,13},{9,17},{1... | collective-permute-start | bytes 786440 | tf_op jit(solution)/shard_map/ppermute | solution.py:404
  14.2 10.5 %collective-permute-start.2 = (bf16[3,128,256]{2,1,0:T(8,128)(2,1)S(1)}, bf16[3,128,256]{2,1,0:T(8,128)(2,1)S(1)}, u32[]{:S(2)}, u32[]{:S(2)}) collective-permute-start(bf16[3,128,256]{2,1,0:T(8,128)(2,1)S(1)} %slice.4), channel_id=1, source_target_pairs={{0,4},{4,0},{8,12},{12,8},{16,20},{20,16},{24,28},{28,24},{1,5},{5... | collective-permute-start | bytes 589832 | tf_op jit(solution)/shard_map/ppermute | solution.py:411
  14.8 0.9 %copy-start.4 = (bf16[512,256]{1,0:T(8,128)(2,1)S(1)}, bf16[512,256]{1,0:T(8,128)(2,1)}, u32[]{:S(2)}) copy-start(bf16[512,256]{1,0:T(8,128)(2,1)} %get-tuple-element.44.own_ref) | copy-start | bytes 786436
  15.8 0.7 copy-start.5
  16.5 0.7 copy-start.6
  28.9 1.6 %collective-permute-start.3 = (bf16[64,2048]{1,0:T(8,128)(2,1)S(1)}, bf16[64,2048]{1,0:T(8,128)(2,1)S(1)}, u32[]{:S(2)}, u32[]{:S(2)}) collective-permute-start(bf16[64,2048]{1,0:T(8,128)(2,1)S(1)} %get-tuple-element.50), channel_id=1, source_target_pairs={{0,1},{1,0},{2,3},{3,2},{4,5},{5,4},{6,7},{7,6},{8,9},{9,8},{10,11... | collective-permute-start | bytes 786440 | tf_op jit(solution)/shard_map/ppermute | solution.py:416
  30.6 13.1 %collective-permute-start.8 = (bf16[64,2048]{1,0:T(8,128)(2,1)S(1)}, bf16[64,2048]{1,0:T(8,128)(2,1)S(1)}, u32[]{:S(2)}, u32[]{:S(2)}) collective-permute-start(bf16[64,2048]{1,0:T(8,128)(2,1)S(1)} %add_convert_fusion.refs_0_), channel_id=1, source_target_pairs={{0,2},{1,3},{2,0},{3,1},{4,6},{5,7},{6,4},{7,5},{8,10},{9,11},{10,... | collective-permute-start | bytes 786440 | tf_op jit(solution)/shard_map/ppermute | solution.py:419
  37.4 1.5 %collective-permute-start.4 = (bf16[64,1536]{1,0:T(8,128)(2,1)S(1)}, bf16[64,1536]{1,0:T(8,128)(2,1)S(1)}, u32[]{:S(2)}, u32[]{:S(2)}) collective-permute-start(bf16[64,1536]{1,0:T(8,128)(2,1)S(1)} %get-tuple-element.55), channel_id=1, source_target_pairs={{0,1},{1,0},{2,3},{3,2},{4,5},{5,4},{6,7},{7,6},{8,9},{9,8},{10,11... | collective-permute-start | bytes 589832 | tf_op jit(solution)/shard_map/ppermute | solution.py:416
  37.5 1.7 %collective-permute-start.5 = (bf16[64,1536]{1,0:T(8,128)(2,1)S(1)}, bf16[64,1536]{1,0:T(8,128)(2,1)S(1)}, u32[]{:S(2)}, u32[]{:S(2)}) collective-permute-start(bf16[64,1536]{1,0:T(8,128)(2,1)S(1)} %get-tuple-element.56), channel_id=1, source_target_pairs={{0,1},{1,0},{2,3},{3,2},{4,5},{5,4},{6,7},{7,6},{8,9},{9,8},{10,11... | collective-permute-start | bytes 589832 | tf_op jit(solution)/shard_map/ppermute | solution.py:416
  38.0 1.5 %collective-permute-start.6 = (bf16[64,1536]{1,0:T(8,128)(2,1)S(1)}, bf16[64,1536]{1,0:T(8,128)(2,1)S(1)}, u32[]{:S(2)}, u32[]{:S(2)}) collective-permute-start(bf16[64,1536]{1,0:T(8,128)(2,1)S(1)} %get-tuple-element.57), channel_id=1, source_target_pairs={{0,1},{1,0},{2,3},{3,2},{4,5},{5,4},{6,7},{7,6},{8,9},{9,8},{10,11... | collective-permute-start | bytes 589832 | tf_op jit(solution)/shard_map/ppermute | solution.py:416
  38.1 1.7 %collective-permute-start.7 = (bf16[64,1536]{1,0:T(8,128)(2,1)S(1)}, bf16[64,1536]{1,0:T(8,128)(2,1)S(1)}, u32[]{:S(2)}, u32[]{:S(2)}) collective-permute-start(bf16[64,1536]{1,0:T(8,128)(2,1)S(1)} %get-tuple-element.58), channel_id=1, source_target_pairs={{0,1},{1,0},{2,3},{3,2},{4,5},{5,4},{6,7},{7,6},{8,9},{9,8},{10,11... | collective-permute-start | bytes 589832 | tf_op jit(solution)/shard_map/ppermute | solution.py:416
  40.0 20.4 %collective-permute-start.13 = (bf16[64,6144]{1,0:T(8,128)(2,1)S(1)}, bf16[64,6144]{1,0:T(8,128)(2,1)S(1)}, u32[]{:S(2)}, u32[]{:S(2)}) collective-permute-start(bf16[64,6144]{1,0:T(8,128)(2,1)S(1)} %add.7.refs_3_), channel_id=1, source_target_pairs={{0,2},{1,3},{2,0},{3,1},{4,6},{5,7},{6,4},{7,5},{8,10},{9,11},{10,... | collective-permute-start | bytes 2359304 | tf_op jit(solution)/shard_map/ppermute | solution.py:419
  50.3 1.6 %collective-permute-start.9 = (bf16[64,2048]{1,0:T(8,128)(2,1)S(1)}, bf16[64,2048]{1,0:T(8,128)(2,1)S(1)}, u32[]{:S(2)}, u32[]{:S(2)}) collective-permute-start(bf16[64,2048]{1,0:T(8,128)(2,1)S(1)} %get-tuple-element.63), channel_id=1, source_target_pairs={{0,1},{1,0},{2,3},{3,2},{4,5},{5,4},{6,7},{7,6},{8,9},{9,8},{10,11... | collective-permute-start | bytes 786440 | tf_op jit(solution)/shard_map/ppermute | solution.py:416
  50.4 1.9 %collective-permute-start.10 = (bf16[64,2048]{1,0:T(8,128)(2,1)S(1)}, bf16[64,2048]{1,0:T(8,128)(2,1)S(1)}, u32[]{:S(2)}, u32[]{:S(2)}) collective-permute-start(bf16[64,2048]{1,0:T(8,128)(2,1)S(1)} %get-tuple-element.64), channel_id=1, source_target_pairs={{0,1},{1,0},{2,3},{3,2},{4,5},{5,4},{6,7},{7,6},{8,9},{9,8},{10,11... | collective-permute-start | bytes 786440 | tf_op jit(solution)/shard_map/ppermute | solution.py:416
  50.9 1.8 %collective-permute-start.11 = (bf16[64,2048]{1,0:T(8,128)(2,1)S(1)}, bf16[64,2048]{1,0:T(8,128)(2,1)S(1)}, u32[]{:S(2)}, u32[]{:S(2)}) collective-permute-start(bf16[64,2048]{1,0:T(8,128)(2,1)S(1)} %get-tuple-element.65), channel_id=1, source_target_pairs={{0,1},{1,0},{2,3},{3,2},{4,5},{5,4},{6,7},{7,6},{8,9},{9,8},{10,11... | collective-permute-start | bytes 786440 | tf_op jit(solution)/shard_map/ppermute | solution.py:416
  51.0 2.1 %collective-permute-start.12 = (bf16[64,2048]{1,0:T(8,128)(2,1)S(1)}, bf16[64,2048]{1,0:T(8,128)(2,1)S(1)}, u32[]{:S(2)}, u32[]{:S(2)}) collective-permute-start(bf16[64,2048]{1,0:T(8,128)(2,1)S(1)} %get-tuple-element.66), channel_id=1, source_target_pairs={{0,1},{1,0},{2,3},{3,2},{4,5},{5,4},{6,7},{7,6},{8,9},{9,8},{10,11... | collective-permute-start | bytes 786440 | tf_op jit(solution)/shard_map/ppermute | solution.py:416
  53.3 7.1 %copy-start.1 = (bf16[64,8192]{1,0:T(8,128)(2,1)}, bf16[64,8192]{1,0:T(8,128)(2,1)S(1)}, u32[]{:S(2)}) copy-start(bf16[64,8192]{1,0:T(8,128)(2,1)S(1)} %add.8.refs_3_) | copy-start | bytes 3145732
  53.3 28.9 %collective-permute-start.22 = (bf16[64,8192]{1,0:T(8,128)(2,1)S(1)}, bf16[64,8192]{1,0:T(8,128)(2,1)S(1)}, u32[]{:S(2)}, u32[]{:S(2)}) collective-permute-start(bf16[64,8192]{1,0:T(8,128)(2,1)S(1)} %add.8.refs_3_), channel_id=1, source_target_pairs={{0,2},{1,3},{2,0},{3,1},{4,6},{5,7},{6,4},{7,5},{8,10},{9,11},{10,... | collective-permute-start | bytes 3145736 | tf_op jit(solution)/shard_map/ppermute | solution.py:419
  65.8 0.8 copy-start.2
  75.7 4.3 %copy-start.3 = (bf16[128,1024]{1,0:T(8,128)(2,1)S(1)}, bf16[128,1024]{1,0:T(8,128)(2,1)}, u32[]{:S(2)}) copy-start(bf16[128,1024]{1,0:T(8,128)(2,1)} %get-tuple-element.74.refs_5_.refs_7_) | copy-start | bytes 786436
  75.7 1.6 %collective-permute-start.14 = (bf16[128,1024]{1,0:T(8,128)(2,1)S(1)}, bf16[128,1024]{1,0:T(8,128)(2,1)S(1)}, u32[]{:S(2)}, u32[]{:S(2)}) collective-permute-start(bf16[128,1024]{1,0:T(8,128)(2,1)S(1)} %get-tuple-element.75), channel_id=1, source_target_pairs={{0,1},{1,0},{2,3},{3,2},{4,5},{5,4},{6,7},{7,6},{8,9},{9,8},{10,11... | collective-permute-start | bytes 786440 | tf_op jit(solution)/shard_map/ppermute | solution.py:416
  75.8 1.9 %collective-permute-start.15 = (bf16[128,1024]{1,0:T(8,128)(2,1)S(1)}, bf16[128,1024]{1,0:T(8,128)(2,1)S(1)}, u32[]{:S(2)}, u32[]{:S(2)}) collective-permute-start(bf16[128,1024]{1,0:T(8,128)(2,1)S(1)} %get-tuple-element.76), channel_id=1, source_target_pairs={{0,1},{1,0},{2,3},{3,2},{4,5},{5,4},{6,7},{7,6},{8,9},{9,8},{10,11... | collective-permute-start | bytes 786440 | tf_op jit(solution)/shard_map/ppermute | solution.py:416
  76.3 1.8 %collective-permute-start.16 = (bf16[128,1024]{1,0:T(8,128)(2,1)S(1)}, bf16[128,1024]{1,0:T(8,128)(2,1)S(1)}, u32[]{:S(2)}, u32[]{:S(2)}) collective-permute-start(bf16[128,1024]{1,0:T(8,128)(2,1)S(1)} %get-tuple-element.77), channel_id=1, source_target_pairs={{0,1},{1,0},{2,3},{3,2},{4,5},{5,4},{6,7},{7,6},{8,9},{9,8},{10,11... | collective-permute-start | bytes 786440 | tf_op jit(solution)/shard_map/ppermute | solution.py:416
  76.4 2.1 %collective-permute-start.17 = (bf16[128,1024]{1,0:T(8,128)(2,1)S(1)}, bf16[128,1024]{1,0:T(8,128)(2,1)S(1)}, u32[]{:S(2)}, u32[]{:S(2)}) collective-permute-start(bf16[128,1024]{1,0:T(8,128)(2,1)S(1)} %get-tuple-element.78), channel_id=1, source_target_pairs={{0,1},{1,0},{2,3},{3,2},{4,5},{5,4},{6,7},{7,6},{8,9},{9,8},{10,11... | collective-permute-start | bytes 786440 | tf_op jit(solution)/shard_map/ppermute | solution.py:416
  77.3 2.0 %collective-permute-start.18 = (bf16[128,1024]{1,0:T(8,128)(2,1)S(1)}, bf16[128,1024]{1,0:T(8,128)(2,1)S(1)}, u32[]{:S(2)}, u32[]{:S(2)}) collective-permute-start(bf16[128,1024]{1,0:T(8,128)(2,1)S(1)} %get-tuple-element.79), channel_id=1, source_target_pairs={{0,1},{1,0},{2,3},{3,2},{4,5},{5,4},{6,7},{7,6},{8,9},{9,8},{10,11... | collective-permute-start | bytes 786440 | tf_op jit(solution)/shard_map/ppermute | solution.py:416
  77.7 1.7 %collective-permute-start.19 = (bf16[128,1024]{1,0:T(8,128)(2,1)S(1)}, bf16[128,1024]{1,0:T(8,128)(2,1)S(1)}, u32[]{:S(2)}, u32[]{:S(2)}) collective-permute-start(bf16[128,1024]{1,0:T(8,128)(2,1)S(1)} %get-tuple-element.80), channel_id=1, source_target_pairs={{0,1},{1,0},{2,3},{3,2},{4,5},{5,4},{6,7},{7,6},{8,9},{9,8},{10,11... | collective-permute-start | bytes 786440 | tf_op jit(solution)/shard_map/ppermute | solution.py:416
  78.1 1.5 %collective-permute-start.20 = (bf16[128,1024]{1,0:T(8,128)(2,1)S(1)}, bf16[128,1024]{1,0:T(8,128)(2,1)S(1)}, u32[]{:S(2)}, u32[]{:S(2)}) collective-permute-start(bf16[128,1024]{1,0:T(8,128)(2,1)S(1)} %get-tuple-element.81), channel_id=1, source_target_pairs={{0,1},{1,0},{2,3},{3,2},{4,5},{5,4},{6,7},{7,6},{8,9},{9,8},{10,11... | collective-permute-start | bytes 786440 | tf_op jit(solution)/shard_map/ppermute | solution.py:416
  78.4 1.5 %collective-permute-start.21 = (bf16[128,1024]{1,0:T(8,128)(2,1)S(1)}, bf16[128,1024]{1,0:T(8,128)(2,1)S(1)}, u32[]{:S(2)}, u32[]{:S(2)}) collective-permute-start(bf16[128,1024]{1,0:T(8,128)(2,1)S(1)} %get-tuple-element.82), channel_id=1, source_target_pairs={{0,1},{1,0},{2,3},{3,2},{4,5},{5,4},{6,7},{7,6},{8,9},{9,8},{10,11... | collective-permute-start | bytes 786440 | tf_op jit(solution)/shard_map/ppermute | solution.py:416

commit v14 on v13

--- a/solution.py
+++ b/solution.py
@@ -50,9 +50,12 @@
     ]
 
 
-def pick_kernel(rank_ref, vert_ref, k_ref, v_ref, both_ref, pair_ref):
+def pick_kernel(rank_ref, vert_ref, k_ref, v_ref, both_ref, low_ref, high_ref, pair_ref):
     both_ref[:, :HS] = k_ref[...]
     both_ref[:, HS:] = v_ref[...]
+    half = low_ref.shape[0]
+    low_ref[...] = both_ref[:half, :]
+    high_ref[...] = both_ref[half:, :]
     blocks = picked_blocks(vert_ref[...], rank_ref[0], k_ref.shape[0] // BLK)
     for slot, rows in enumerate(blocks):
         picked = both_ref[rows, :]
@@ -65,10 +68,12 @@
         pick_kernel,
         out_shape=(
             jax.ShapeDtypeStruct((keys.shape[0], 2 * HS), keys.dtype),
+            jax.ShapeDtypeStruct((keys.shape[0] // 2, 2 * HS), keys.dtype),
+            jax.ShapeDtypeStruct((keys.shape[0] // 2, 2 * HS), keys.dtype),
             jax.ShapeDtypeStruct((copies, VMOST * BLK, 2 * HS), keys.dtype),
         ),
         in_specs=[smem(), vmem(), vmem(), vmem()],
-        out_specs=(vmem(), vmem()),
+        out_specs=(vmem(),) * 4,
         compiler_params=params(60),
         name="pick",
     )(rank, vertical, keys, values)
@@ -122,10 +127,11 @@
 
 
 def attend_kernel(
-    slots, tiles, sizes, place, tp_ref, ctx_ref, q_0, q_1, table_ref, own, kv_2, kv_1, *refs
+    slots, tiles, sizes, place, tp_ref, ctx_ref, q_0, q_1, table_ref, own, kv_2, *refs
 ):
-    pairs = refs[:2]
-    w_hbm = refs[2]
+    kv_1, kv_1_odd, kv_1_even = refs[:3]
+    pairs = refs[3:5]
+    w_hbm = refs[5]
     kv_win, e_win, kv_pool, e_pool, attended, weight, arrival, landed = refs[-8:]
     outs = refs[-11:-8] if tiles else refs[-9:-8]
     step = pl.program_id(0)
@@ -146,10 +152,24 @@
 
     @pl.when(step == 0)
     def _():
+        half = kv_1.shape[0]
+        places = ((kv_2, 0), (kv_1, rows), (own, 2 * rows))
         copies = [
-            pltpu.make_async_copy(x, kv_win.at[pl.ds(s * rows, rows), :], landed.at[s])
-            for s, x in enumerate((kv_2, kv_1, own))
+            pltpu.make_async_copy(x, kv_win.at[pl.ds(at, x.shape[0]), :], landed.at[s])
+            for s, (x, at) in enumerate(places)
         ]
+        second = kv_win.at[pl.ds(rows + half, half), :]
+        odd = (rank & 1) == 1
+
+        @pl.when(odd)
+        def _():
+            pltpu.make_async_copy(kv_1_odd, second, landed.at[NEAR + 2]).start()
+
+        @pl.when(jnp.logical_not(odd))
+        def _():
+            pltpu.make_async_copy(kv_1_even, second, landed.at[NEAR + 2]).start()
+
+        copies.append(pltpu.make_async_copy(kv_1_odd, second, landed.at[NEAR + 2]))
         copies += [
             pltpu.make_async_copy(
                 x.at[pl.ds(0, slots)], kv_pool.at[pl.ds(p * slots, slots)], landed.at[NEAR + p]
@@ -157,7 +177,8 @@
             for p, x in enumerate(pairs)
         ]
         for copy in copies:
-            copy.start()
+            if copy is not copies[NEAR]:
+                copy.start()
         for t in range(tiles):
             fetch(t).start()
         key = lax.broadcasted_iota(jnp.int32, e_win.shape, 0)
@@ -283,7 +304,7 @@
                 pltpu.VMEM((steps * 2 * BLK, width), dtype),
                 pltpu.VMEM((max(tiles, 1), out_weight.shape[0], TILE), dtype),
                 pltpu.SemaphoreType.DMA((max(tiles, 1),)),
-                pltpu.SemaphoreType.DMA((NEAR + 2,)),
+                pltpu.SemaphoreType.DMA((NEAR + 3,)),
             ],
         ),
         compiler_params=params(50),
@@ -404,13 +425,15 @@
         return lax.ppermute(x, "ctx", [(r, r + by) for r in range(ctx_size - by)])
 
     half = ctx_size // 2
-    own, pair = pick(ctx, vertical, keys, values, half)
+    own, low, high, pair = pick(ctx, vertical, keys, values, half)
     parities = [list(range(odd, ctx_size, 2)) for odd in (0, 1)]
     pairs = [lax.all_to_all(pair, "ctx", 0, 0, axis_index_groups=parities, tiled=True)]
     needed = pairs[0][: half - 1]
     pairs.append(lax.ppermute(needed, "ctx", [(r, r ^ 1) for r in range(ctx_size)]))
     table, own_copy = tables(ctx, vertical, slash, own, half - 1)
-    near_kv = [own_copy, shifted(own, 2), shifted(own, 1)]
+    kv_1_odd = lax.ppermute(high, "ctx", [(r, r ^ 1) for r in range(ctx_size)])
+    kv_1_even = lax.ppermute(kv_1_odd, "ctx", [(r, r + 2) for r in range(0, ctx_size - 2, 2)])
+    near_kv = [own_copy, shifted(own, 2), shifted(low, 1), kv_1_odd, kv_1_even]
 
     def sibling(x):
         return lax.ppermute(x, "tp", [(j, j ^ 1) for j in range(4)])

time: 84.3 us -> 85.6 us (1.015)
  the two profiles are of different devices: /device:TPU:16 before, /device:TPU:0 now
where the time goes in v14:
time: 85.6 us; the launch traced here: 85.2 us
  Pallas kernels  40.7 us (48%)
  starting transfers between devices  25.4 us (30%)
  waiting for transfers between devices  15.4 us (18%)
  local copies, waits for them, and re-layouts  3.13 us (4%)
    pallas_call x3, Pallas kernels, project(): pl.pallas_call(functools.partial(project_kernel, first), out_shape=[part]...  21 us
    pallas_call x3, Pallas kernels, attend(): pl.pallas_call(functools.partial(attend_kernel, slots, tiles, sizes, plac...  14.1 us
    ppermute x2, starting transfers between devices, shifted(): return lax.ppermute(x, 'ctx', [(r, r + by) for r in range(ctx_size - by)])  6.34 us
    all_to_all x1, starting transfers between devices, shards(): lax.all_to_all(pair, 'ctx', 0, 0, axis_index_groups=parities, tiled=True)  6.32 us
    ppermute x17, waiting for transfers between devices, sibling(): return lax.ppermute(x, 'tp', [(j, j ^ 1) for j in range(4)])  6.24 us
    ppermute x3, waiting for transfers between devices, across(): return lax.ppermute(x, 'tp', [(j, j ^ 2) for j in range(4)])  5.72 us
    ppermute x17, starting transfers between devices, sibling(): return lax.ppermute(x, 'tp', [(j, j ^ 1) for j in range(4)])  3.86 us
    ppermute x3, starting transfers between devices, across(): return lax.ppermute(x, 'tp', [(j, j ^ 2) for j in range(4)])  3.71 us
  transfers between devices with their start and end apart: 26, of which 18 were waited for; matrix products, arithmetic and copies ran while one was open for 0% of the time, Pallas kernels for 39%

profile of v14, /device:TPU:0, one launch (start us, length us, event | category | flops | bytes accessed | tf_op | source)
XLA Modules:
  0.0 85.2 jit_solution(17106210312925295294)
XLA Ops:
  0.0 2.2 %pick.1 = (bf16[512,256]{1,0:T(8,128)(2,1)}, bf16[256,256]{1,0:T(8,128)(2,1)}, bf16[256,256]{1,0:T(8,128)(2,1)}, bf16[4,128,256]{2,1,0:T(8,128)(2,1)}) custom-call(s32[1]{0:T(128)} %bitcast.1.rank_ref.ctx_ref, s32[8,16]{1,0:T(8,128)} %vert_ref.3, bf16[512,128]{1,0:T(8,128)(2,1)} %k_ref.1, bf16[512,128]{1,0:T(8,128)(2,1)} %v_ref.1), custom_call_target="tpu_custom_call" | custom-call | tf_op jit(solution)/shard_map/pick/pallas_call | solution.py:67
  2.2 6.3 %all-to-all-start = ((bf16[4,128,256]{2,1,0:T(8,128)(2,1)}), bf16[4,128,256]{2,1,0:T(8,128)(2,1)S(1)}, u32[]{:S(2)}, u32[]{:S(2)}) async-start(bf16[4,128,256]{2,1,0:T(8,128)(2,1)} %get-tuple-element.51), calls=%async_computation | async-start | bytes 524288 | tf_op jit(solution)/shard_map/all_to_all | solution.py:430
  8.5 1.5 %collective-permute-start.2 = (bf16[256,256]{1,0:T(8,128)(2,1)}, bf16[256,256]{1,0:T(8,128)(2,1)S(1)}, u32[]{:S(2)}, u32[]{:S(2)}) collective-permute-start(bf16[256,256]{1,0:T(8,128)(2,1)} %get-tuple-element.50), channel_id=1, source_target_pairs={{0,4},{4,0},{8,12},{12,8},{16,20},{20,16},{24,28},{28,24},{1,5},{5... | collective-permute-start | bytes 393224 | tf_op jit(solution)/shard_map/ppermute | solution.py:434
  10.0 3.9 %collective-permute-start = (bf16[512,256]{1,0:T(8,128)(2,1)}, bf16[512,256]{1,0:T(8,128)(2,1)S(1)}, u32[]{:S(2)}, u32[]{:S(2)}) collective-permute-start(bf16[512,256]{1,0:T(8,128)(2,1)} %get-tuple-element.46.own_ref), channel_id=1, source_target_pairs={{0,8},{4,12},{8,16},{12,20},{16,24},{20,28},{1,9},{5,13},{9,17},{1... | collective-permute-start | bytes 786440 | tf_op jit(solution)/shard_map/ppermute | solution.py:425
  14.0 3.5 %all-to-all-done.refs_3_ = bf16[4,128,256]{2,1,0:T(8,128)(2,1)S(1)} async-done(((bf16[4,128,256]{2,1,0:T(8,128)(2,1)}), bf16[4,128,256]{2,1,0:T(8,128)(2,1)S(1)}, u32[]{:S(2)}, u32[]{:S(2)}) %all-to-all-start) | async-done | bytes 262176 | tf_op jit(solution)/shard_map/all_to_all | solution.py:430
  17.4 1.6 %collective-permute-start.4 = (bf16[3,128,256]{2,1,0:T(8,128)(2,1)S(1)}, bf16[3,128,256]{2,1,0:T(8,128)(2,1)S(1)}, u32[]{:S(2)}, u32[]{:S(2)}) collective-permute-start(bf16[3,128,256]{2,1,0:T(8,128)(2,1)S(1)} %slice.4), channel_id=1, source_target_pairs={{0,4},{4,0},{8,12},{12,8},{16,20},{20,16},{24,28},{28,24},{1,5},{5... | collective-permute-start | bytes 589832 | tf_op jit(solution)/shard_map/ppermute | solution.py:432
  19.0 2.4 %collective-permute-start.1 = (bf16[256,256]{1,0:T(8,128)(2,1)}, bf16[256,256]{1,0:T(8,128)(2,1)S(1)}, u32[]{:S(2)}, u32[]{:S(2)}) collective-permute-start(bf16[256,256]{1,0:T(8,128)(2,1)} %get-tuple-element.49), channel_id=1, source_target_pairs={{0,4},{4,8},{8,12},{12,16},{16,20},{20,24},{24,28},{1,5},{5,9},{9,... | collective-permute-start | bytes 393224 | tf_op jit(solution)/shard_map/ppermute | solution.py:425
  21.4 2.1 %collective-permute-start.3 = (bf16[256,256]{1,0:T(8,128)(2,1)S(1)}, bf16[256,256]{1,0:T(8,128)(2,1)S(1)}, u32[]{:S(2)}, u32[]{:S(2)}) collective-permute-start(bf16[256,256]{1,0:T(8,128)(2,1)S(1)} %collective-permute-done.2.refs_1_), channel_id=1, source_target_pairs={{0,8},{8,16},{16,24},{1,9},{9,17},{17,25},{2,10},{10,18},{18,26},{... | collective-permute-start | bytes 393224 | tf_op jit(solution)/shard_map/ppermute | solution.py:435
  23.5 0.9 %copy-done.4 = bf16[512,256]{1,0:T(8,128)(2,1)S(1)} copy-done((bf16[512,256]{1,0:T(8,128)(2,1)S(1)}, bf16[512,256]{1,0:T(8,128)(2,1)}, u32[]{:S(2)}) %copy-start.4) | copy-done | bytes 262168
  24.5 0.7 copy-done.5
  25.2 0.7 copy-done.6
  26.1 4.6 %attend.3 = (bf16[128,1024]{1,0:T(8,128)(2,1)S(1)}, bf16[64,2048]{1,0:T(8,128)(2,1)S(1)}, bf16[64,2048]{1,0:T(8,128)(2,1)S(1)}) custom-call(s32[1]{0:T(128)} %bitcast.tp_ref, s32[1]{0:T(128)} %bitcast.1.rank_ref.ctx_ref, bf16[512,1024]{1,0:T(8,128)(2,1)S(1)} %copy-done, bf16[512,1024]{1,0:T(8,128)(2,1)S(1)} %copy-done, ...), custom_call_target="tpu_custom_call" | custom-call | tf_op jit(solution)/shard_map/attend/pallas_call | solution.py:286
  30.7 1.5 %collective-permute-done.5 = bf16[64,2048]{1,0:T(8,128)(2,1)S(1)} collective-permute-done((bf16[64,2048]{1,0:T(8,128)(2,1)S(1)}, bf16[64,2048]{1,0:T(8,128)(2,1)S(1)}, u32[]{:S(2)}, u32[]{:S(2)}) %collective-permute-start.5) | collective-permute-done | bytes 262176 | tf_op jit(solution)/shard_map/ppermute | solution.py:439
  32.3 1.6 %collective-permute-start.10 = (bf16[64,2048]{1,0:T(8,128)(2,1)S(1)}, bf16[64,2048]{1,0:T(8,128)(2,1)S(1)}, u32[]{:S(2)}, u32[]{:S(2)}) collective-permute-start(bf16[64,2048]{1,0:T(8,128)(2,1)S(1)} %add_convert_fusion.refs_0_), channel_id=1, source_target_pairs={{0,2},{1,3},{2,0},{3,1},{4,6},{5,7},{6,4},{7,5},{8,10},{9,11},{10,... | collective-permute-start | bytes 786440 | tf_op jit(solution)/shard_map/ppermute | solution.py:442
  33.9 5.3 %project.3 = (bf16[64,1536]{1,0:T(8,128)(2,1)S(1)}, bf16[64,1536]{1,0:T(8,128)(2,1)S(1)}, bf16[64,1536]{1,0:T(8,128)(2,1)S(1)}, bf16[64,1536]{1,0:T(8,128)(2,1)S...) custom-call(bf16[128,1024]{1,0:T(8,128)(2,1)S(1)} %get-tuple-element, ...), custom_call_target="tpu_custom_call" | custom-call | tf_op jit(solution)/shard_map/project/pallas_call | solution.py:341
  39.2 0.5 collective-permute-start.7
  39.8 0.4 collective-permute-start.9
  40.2 0.4 collective-permute-done.6.refs_4_
  40.7 0.3 collective-permute-done.7.refs_5_
  40.9 0.3 collective-permute-done.8.refs_6_
  41.2 0.3 collective-permute-done.9.refs_7_
  41.7 0.6 collective-permute-start.15
  42.3 3.5 %attend.4.a_ref = bf16[128,1024]{1,0:T(8,128)(2,1)S(1)} custom-call(s32[1]{0:T(128)} %bitcast.tp_ref, s32[1]{0:T(128)} %bitcast.1.rank_ref.ctx_ref, bf16[512,1024]{1,0:T(8,128)(2,1)S(1)} %copy-done, bf16[512,1024]{1,0:T(8,128)(2,1)S(1)} %copy-done, s32[3,8,128]{2,1,0:T(8,128)S(1)} %get-tuple-element.47.table_ref, ...), custom_call_target="tpu_custom_call" | custom-call | tf_op jit(solution)/shard_map/attend/pallas_call | solution.py:286
  45.8 6.7 %project.4 = (bf16[64,2048]{1,0:T(8,128)(2,1)S(1)}, bf16[64,2048]{1,0:T(8,128)(2,1)S(1)}, bf16[64,2048]{1,0:T(8,128)(2,1)S(1)}, bf16[64,2048]{1,0:T(8,128)(2,1)S...) custom-call(bf16[128,1024]{1,0:T(8,128)(2,1)S(1)} %attend.4.a_ref, ...), custom_call_target="tpu_custom_call" | custom-call | tf_op jit(solution)/shard_map/project/pallas_call | solution.py:341
  52.6 0.5 collective-permute-start.12
  53.2 0.4 collective-permute-start.14
  53.6 0.5 collective-permute-done.11.refs_4_
  54.1 0.4 collective-permute-done.12.refs_5_
  54.5 0.4 collective-permute-done.13.refs_6_
  54.9 0.4 collective-permute-done.14.refs_7_
  55.2 0.2 add.8.refs_6_
  55.5 1.6 %collective-permute-start.24 = (bf16[64,8192]{1,0:T(8,128)(2,1)S(1)}, bf16[64,8192]{1,0:T(8,128)(2,1)S(1)}, u32[]{:S(2)}, u32[]{:S(2)}) collective-permute-start(bf16[64,8192]{1,0:T(8,128)(2,1)S(1)} %add.8.refs_6_), channel_id=1, source_target_pairs={{0,2},{1,3},{2,0},{3,1},{4,6},{5,7},{6,4},{7,5},{8,10},{9,11},{10,... | collective-permute-start | bytes 3145736 | tf_op jit(solution)/shard_map/ppermute | solution.py:442
  57.0 5.1 %collective-permute-done.15.refs_7_.refs_12_ = bf16[64,6144]{1,0:T(8,128)(2,1)S(1)} collective-permute-done((bf16[64,6144]{1,0:T(8,128)(2,1)S(1)}, bf16[64,6144]{1,0:T(8,128)(2,1)S(1)}, u32[]{:S(2)}, u32[]{:S(2)}) %collective-permute-start.15) | collective-permute-done | bytes 786464 | tf_op jit(solution)/shard_map/ppermute | solution.py:442
  62.1 5.9 %attend.5.a_ref = bf16[256,1024]{1,0:T(8,128)(2,1)S(1)} custom-call(s32[1]{0:T(128)} %bitcast.tp_ref, s32[1]{0:T(128)} %bitcast.1.rank_ref.ctx_ref, bf16[512,1024]{1,0:T(8,128)(2,1)S(1)} %copy-done, bf16[512,1024]{1,0:T(8,128)(2,1)S(1)} %copy-done, s32[3,8,128]{2,1,0:T(8,128)S(1)} %get-tuple-element.47.table_ref, ...), custom_call_target="tpu_custom_call" | custom-call | tf_op jit(solution)/shard_map/attend/pallas_call | solution.py:286
  68.1 0.8 copy-done.2
  68.9 9.1 %project.5 = (bf16[128,1024]{1,0:T(8,128)(2,1)S(1)}, bf16[128,1024]{1,0:T(8,128)(2,1)S(1)}, bf16[128,1024]{1,0:T(8,128)(2,1)S(1)}, bf16[128,1024]{1,0:T(8,128)(2...) custom-call(bf16[256,1024]{1,0:T(8,128)(2,1)} %copy-done.2, ...), custom_call_target="tpu_custom_call" | custom-call | tf_op jit(solution)/shard_map/project/pallas_call | solution.py:341
  78.1 0.5 collective-permute-start.17
  78.6 0.4 collective-permute-start.19
  79.1 0.5 collective-permute-done.16.refs_2_.refs_8_
  79.7 0.2 collective-permute-done.17.refs_3_.refs_9_
  80.1 0.2 collective-permute-done.18.refs_6_.refs_10_
  80.5 0.2 collective-permute-done.19.refs_7_.refs_11_
  80.9 0.8 finish.3.refs_13_
  81.7 0.2 collective-permute-done.22.refs_10_.refs_14_
  81.9 0.4 collective-permute-done.23.refs_11_.refs_15_
  82.3 1.0 %finish.4.refs_17_ = bf16[128,8192]{1,0:T(8,128)(2,1)} custom-call(bf16[128,1024]{1,0:T(8,128)(2,1)S(1)} %get-tuple-element.73.refs_0_.refs_2_, bf16[128,1024]{1,0:T(8,128)(2,1)S(1)} %get-tuple-element.74.refs_1_.refs_3_, bf16[128,1024]{1,0:T(8,128)(2,1)S(1)} %get-tuple-element.75.refs_2_.refs_4_, ...), custom_call_target="tpu_custom_call", output_to_operand_aliasing={{}: (13, {})} | custom-call | tf_op jit(solution)/shard_map/finish/pallas_call | solution.py:402
  83.3 0.6 collective-permute-done.24.refs_16_
  83.9 1.1 %finish.5 = bf16[128,8192]{1,0:T(8,128)(2,1)} custom-call(bf16[128,1024]{1,0:T(8,128)(2,1)S(1)} %get-tuple-element.71.refs_0_, bf16[128,1024]{1,0:T(8,128)(2,1)S(1)} %get-tuple-element.72.refs_1_, bf16[128,1024]{1,0:T(8,128)(2,1)S(1)} %get-tuple-element.73.refs_0_.refs_2_, ...), custom_call_target="tpu_custom_call", output_to_operand_aliasing={{}: (17, {})} | custom-call | tf_op jit(solution)/shard_map/finish/pallas_call | solution.py:402
  (33 shorter events, 1.5 us)
Async XLA Ops:
  0.0 26.0 %copy-start = (bf16[512,1024]{1,0:T(8,128)(2,1)S(1)}, bf16[512,1024]{1,0:T(8,128)(2,1)}, u32[]{:S(2)}) copy-start(bf16[512,1024]{1,0:T(8,128)(2,1)} %q_1.5) | copy-start | bytes 3145732
  2.2 15.2 %all-to-all-start = ((bf16[4,128,256]{2,1,0:T(8,128)(2,1)}), bf16[4,128,256]{2,1,0:T(8,128)(2,1)S(1)}, u32[]{:S(2)}, u32[]{:S(2)}) async-start(bf16[4,128,256]{2,1,0:T(8,128)(2,1)} %get-tuple-element.51), calls=%async_computation | async-start | bytes 524288 | tf_op jit(solution)/shard_map/all_to_all | solution.py:430
  8.5 12.9 %collective-permute-start.2 = (bf16[256,256]{1,0:T(8,128)(2,1)}, bf16[256,256]{1,0:T(8,128)(2,1)S(1)}, u32[]{:S(2)}, u32[]{:S(2)}) collective-permute-start(bf16[256,256]{1,0:T(8,128)(2,1)} %get-tuple-element.50), channel_id=1, source_target_pairs={{0,4},{4,0},{8,12},{12,8},{16,20},{20,16},{24,28},{28,24},{1,5},{5... | collective-permute-start | bytes 393224 | tf_op jit(solution)/shard_map/ppermute | solution.py:434
  10.0 16.0 %collective-permute-start = (bf16[512,256]{1,0:T(8,128)(2,1)}, bf16[512,256]{1,0:T(8,128)(2,1)S(1)}, u32[]{:S(2)}, u32[]{:S(2)}) collective-permute-start(bf16[512,256]{1,0:T(8,128)(2,1)} %get-tuple-element.46.own_ref), channel_id=1, source_target_pairs={{0,8},{4,12},{8,16},{12,20},{16,24},{20,28},{1,9},{5,13},{9,17},{1... | collective-permute-start | bytes 786440 | tf_op jit(solution)/shard_map/ppermute | solution.py:425
  17.4 8.6 %collective-permute-start.4 = (bf16[3,128,256]{2,1,0:T(8,128)(2,1)S(1)}, bf16[3,128,256]{2,1,0:T(8,128)(2,1)S(1)}, u32[]{:S(2)}, u32[]{:S(2)}) collective-permute-start(bf16[3,128,256]{2,1,0:T(8,128)(2,1)S(1)} %slice.4), channel_id=1, source_target_pairs={{0,4},{4,0},{8,12},{12,8},{16,20},{20,16},{24,28},{28,24},{1,5},{5... | collective-permute-start | bytes 589832 | tf_op jit(solution)/shard_map/ppermute | solution.py:432
  19.0 7.0 %collective-permute-start.1 = (bf16[256,256]{1,0:T(8,128)(2,1)}, bf16[256,256]{1,0:T(8,128)(2,1)S(1)}, u32[]{:S(2)}, u32[]{:S(2)}) collective-permute-start(bf16[256,256]{1,0:T(8,128)(2,1)} %get-tuple-element.49), channel_id=1, source_target_pairs={{0,4},{4,8},{8,12},{12,16},{16,20},{20,24},{24,28},{1,5},{5,9},{9,... | collective-permute-start | bytes 393224 | tf_op jit(solution)/shard_map/ppermute | solution.py:425
  21.4 4.6 %collective-permute-start.3 = (bf16[256,256]{1,0:T(8,128)(2,1)S(1)}, bf16[256,256]{1,0:T(8,128)(2,1)S(1)}, u32[]{:S(2)}, u32[]{:S(2)}) collective-permute-start(bf16[256,256]{1,0:T(8,128)(2,1)S(1)} %collective-permute-done.2.refs_1_), channel_id=1, source_target_pairs={{0,8},{8,16},{16,24},{1,9},{9,17},{17,25},{2,10},{10,18},{18,26},{... | collective-permute-start | bytes 393224 | tf_op jit(solution)/shard_map/ppermute | solution.py:435
  23.5 1.0 %copy-start.4 = (bf16[512,256]{1,0:T(8,128)(2,1)S(1)}, bf16[512,256]{1,0:T(8,128)(2,1)}, u32[]{:S(2)}) copy-start(bf16[512,256]{1,0:T(8,128)(2,1)} %get-tuple-element.46.own_ref) | copy-start | bytes 786436
  24.5 0.7 copy-start.5
  25.2 0.7 copy-start.6
  30.6 1.6 %collective-permute-start.5 = (bf16[64,2048]{1,0:T(8,128)(2,1)S(1)}, bf16[64,2048]{1,0:T(8,128)(2,1)S(1)}, u32[]{:S(2)}, u32[]{:S(2)}) collective-permute-start(bf16[64,2048]{1,0:T(8,128)(2,1)S(1)} %get-tuple-element.54), channel_id=1, source_target_pairs={{0,1},{1,0},{2,3},{3,2},{4,5},{5,4},{6,7},{7,6},{8,9},{9,8},{10,11... | collective-permute-start | bytes 786440 | tf_op jit(solution)/shard_map/ppermute | solution.py:439
  32.3 13.5 %collective-permute-start.10 = (bf16[64,2048]{1,0:T(8,128)(2,1)S(1)}, bf16[64,2048]{1,0:T(8,128)(2,1)S(1)}, u32[]{:S(2)}, u32[]{:S(2)}) collective-permute-start(bf16[64,2048]{1,0:T(8,128)(2,1)S(1)} %add_convert_fusion.refs_0_), channel_id=1, source_target_pairs={{0,2},{1,3},{2,0},{3,1},{4,6},{5,7},{6,4},{7,5},{8,10},{9,11},{10,... | collective-permute-start | bytes 786440 | tf_op jit(solution)/shard_map/ppermute | solution.py:442
  39.2 1.5 %collective-permute-start.6 = (bf16[64,1536]{1,0:T(8,128)(2,1)S(1)}, bf16[64,1536]{1,0:T(8,128)(2,1)S(1)}, u32[]{:S(2)}, u32[]{:S(2)}) collective-permute-start(bf16[64,1536]{1,0:T(8,128)(2,1)S(1)} %get-tuple-element.59), channel_id=1, source_target_pairs={{0,1},{1,0},{2,3},{3,2},{4,5},{5,4},{6,7},{7,6},{8,9},{9,8},{10,11... | collective-permute-start | bytes 589832 | tf_op jit(solution)/shard_map/ppermute | solution.py:439
  39.2 1.7 %collective-permute-start.7 = (bf16[64,1536]{1,0:T(8,128)(2,1)S(1)}, bf16[64,1536]{1,0:T(8,128)(2,1)S(1)}, u32[]{:S(2)}, u32[]{:S(2)}) collective-permute-start(bf16[64,1536]{1,0:T(8,128)(2,1)S(1)} %get-tuple-element.60), channel_id=1, source_target_pairs={{0,1},{1,0},{2,3},{3,2},{4,5},{5,4},{6,7},{7,6},{8,9},{9,8},{10,11... | collective-permute-start | bytes 589832 | tf_op jit(solution)/shard_map/ppermute | solution.py:439
  39.7 1.5 %collective-permute-start.8 = (bf16[64,1536]{1,0:T(8,128)(2,1)S(1)}, bf16[64,1536]{1,0:T(8,128)(2,1)S(1)}, u32[]{:S(2)}, u32[]{:S(2)}) collective-permute-start(bf16[64,1536]{1,0:T(8,128)(2,1)S(1)} %get-tuple-element.61), channel_id=1, source_target_pairs={{0,1},{1,0},{2,3},{3,2},{4,5},{5,4},{6,7},{7,6},{8,9},{9,8},{10,11... | collective-permute-start | bytes 589832 | tf_op jit(solution)/shard_map/ppermute | solution.py:439
  39.8 1.7 %collective-permute-start.9 = (bf16[64,1536]{1,0:T(8,128)(2,1)S(1)}, bf16[64,1536]{1,0:T(8,128)(2,1)S(1)}, u32[]{:S(2)}, u32[]{:S(2)}) collective-permute-start(bf16[64,1536]{1,0:T(8,128)(2,1)S(1)} %get-tuple-element.62), channel_id=1, source_target_pairs={{0,1},{1,0},{2,3},{3,2},{4,5},{5,4},{6,7},{7,6},{8,9},{9,8},{10,11... | collective-permute-start | bytes 589832 | tf_op jit(solution)/shard_map/ppermute | solution.py:439
  41.7 20.4 %collective-permute-start.15 = (bf16[64,6144]{1,0:T(8,128)(2,1)S(1)}, bf16[64,6144]{1,0:T(8,128)(2,1)S(1)}, u32[]{:S(2)}, u32[]{:S(2)}) collective-permute-start(bf16[64,6144]{1,0:T(8,128)(2,1)S(1)} %add.7.refs_6_), channel_id=1, source_target_pairs={{0,2},{1,3},{2,0},{3,1},{4,6},{5,7},{6,4},{7,5},{8,10},{9,11},{10,... | collective-permute-start | bytes 2359304 | tf_op jit(solution)/shard_map/ppermute | solution.py:442
  52.5 1.6 %collective-permute-start.11 = (bf16[64,2048]{1,0:T(8,128)(2,1)S(1)}, bf16[64,2048]{1,0:T(8,128)(2,1)S(1)}, u32[]{:S(2)}, u32[]{:S(2)}) collective-permute-start(bf16[64,2048]{1,0:T(8,128)(2,1)S(1)} %get-tuple-element.67), channel_id=1, source_target_pairs={{0,1},{1,0},{2,3},{3,2},{4,5},{5,4},{6,7},{7,6},{8,9},{9,8},{10,11... | collective-permute-start | bytes 786440 | tf_op jit(solution)/shard_map/ppermute | solution.py:439
  52.6 1.9 %collective-permute-start.12 = (bf16[64,2048]{1,0:T(8,128)(2,1)S(1)}, bf16[64,2048]{1,0:T(8,128)(2,1)S(1)}, u32[]{:S(2)}, u32[]{:S(2)}) collective-permute-start(bf16[64,2048]{1,0:T(8,128)(2,1)S(1)} %get-tuple-element.68), channel_id=1, source_target_pairs={{0,1},{1,0},{2,3},{3,2},{4,5},{5,4},{6,7},{7,6},{8,9},{9,8},{10,11... | collective-permute-start | bytes 786440 | tf_op jit(solution)/shard_map/ppermute | solution.py:439
  53.1 1.8 %collective-permute-start.13 = (bf16[64,2048]{1,0:T(8,128)(2,1)S(1)}, bf16[64,2048]{1,0:T(8,128)(2,1)S(1)}, u32[]{:S(2)}, u32[]{:S(2)}) collective-permute-start(bf16[64,2048]{1,0:T(8,128)(2,1)S(1)} %get-tuple-element.69), channel_id=1, source_target_pairs={{0,1},{1,0},{2,3},{3,2},{4,5},{5,4},{6,7},{7,6},{8,9},{9,8},{10,11... | collective-permute-start | bytes 786440 | tf_op jit(solution)/shard_map/ppermute | solution.py:439
  53.2 2.1 %collective-permute-start.14 = (bf16[64,2048]{1,0:T(8,128)(2,1)S(1)}, bf16[64,2048]{1,0:T(8,128)(2,1)S(1)}, u32[]{:S(2)}, u32[]{:S(2)}) collective-permute-start(bf16[64,2048]{1,0:T(8,128)(2,1)S(1)} %get-tuple-element.70), channel_id=1, source_target_pairs={{0,1},{1,0},{2,3},{3,2},{4,5},{5,4},{6,7},{7,6},{8,9},{9,8},{10,11... | collective-permute-start | bytes 786440 | tf_op jit(solution)/shard_map/ppermute | solution.py:439
  55.5 6.7 %copy-start.1 = (bf16[64,8192]{1,0:T(8,128)(2,1)}, bf16[64,8192]{1,0:T(8,128)(2,1)S(1)}, u32[]{:S(2)}) copy-start(bf16[64,8192]{1,0:T(8,128)(2,1)S(1)} %add.8.refs_6_) | copy-start | bytes 3145732
  55.5 28.4 %collective-permute-start.24 = (bf16[64,8192]{1,0:T(8,128)(2,1)S(1)}, bf16[64,8192]{1,0:T(8,128)(2,1)S(1)}, u32[]{:S(2)}, u32[]{:S(2)}) collective-permute-start(bf16[64,8192]{1,0:T(8,128)(2,1)S(1)} %add.8.refs_6_), channel_id=1, source_target_pairs={{0,2},{1,3},{2,0},{3,1},{4,6},{5,7},{6,4},{7,5},{8,10},{9,11},{10,... | collective-permute-start | bytes 3145736 | tf_op jit(solution)/shard_map/ppermute | solution.py:442
  68.1 0.8 copy-start.2
  78.0 4.3 %copy-start.3 = (bf16[128,1024]{1,0:T(8,128)(2,1)S(1)}, bf16[128,1024]{1,0:T(8,128)(2,1)}, u32[]{:S(2)}) copy-start(bf16[128,1024]{1,0:T(8,128)(2,1)} %get-tuple-element.78.refs_5_.refs_7_) | copy-start | bytes 786436
  78.0 1.6 %collective-permute-start.16 = (bf16[128,1024]{1,0:T(8,128)(2,1)S(1)}, bf16[128,1024]{1,0:T(8,128)(2,1)S(1)}, u32[]{:S(2)}, u32[]{:S(2)}) collective-permute-start(bf16[128,1024]{1,0:T(8,128)(2,1)S(1)} %get-tuple-element.79), channel_id=1, source_target_pairs={{0,1},{1,0},{2,3},{3,2},{4,5},{5,4},{6,7},{7,6},{8,9},{9,8},{10,11... | collective-permute-start | bytes 786440 | tf_op jit(solution)/shard_map/ppermute | solution.py:439
  78.1 1.9 %collective-permute-start.17 = (bf16[128,1024]{1,0:T(8,128)(2,1)S(1)}, bf16[128,1024]{1,0:T(8,128)(2,1)S(1)}, u32[]{:S(2)}, u32[]{:S(2)}) collective-permute-start(bf16[128,1024]{1,0:T(8,128)(2,1)S(1)} %get-tuple-element.80), channel_id=1, source_target_pairs={{0,1},{1,0},{2,3},{3,2},{4,5},{5,4},{6,7},{7,6},{8,9},{9,8},{10,11... | collective-permute-start | bytes 786440 | tf_op jit(solution)/shard_map/ppermute | solution.py:439
  78.6 1.8 %collective-permute-start.18 = (bf16[128,1024]{1,0:T(8,128)(2,1)S(1)}, bf16[128,1024]{1,0:T(8,128)(2,1)S(1)}, u32[]{:S(2)}, u32[]{:S(2)}) collective-permute-start(bf16[128,1024]{1,0:T(8,128)(2,1)S(1)} %get-tuple-element.81), channel_id=1, source_target_pairs={{0,1},{1,0},{2,3},{3,2},{4,5},{5,4},{6,7},{7,6},{8,9},{9,8},{10,11... | collective-permute-start | bytes 786440 | tf_op jit(solution)/shard_map/ppermute | solution.py:439
  78.6 2.1 %collective-permute-start.19 = (bf16[128,1024]{1,0:T(8,128)(2,1)S(1)}, bf16[128,1024]{1,0:T(8,128)(2,1)S(1)}, u32[]{:S(2)}, u32[]{:S(2)}) collective-permute-start(bf16[128,1024]{1,0:T(8,128)(2,1)S(1)} %get-tuple-element.82), channel_id=1, source_target_pairs={{0,1},{1,0},{2,3},{3,2},{4,5},{5,4},{6,7},{7,6},{8,9},{9,8},{10,11... | collective-permute-start | bytes 786440 | tf_op jit(solution)/shard_map/ppermute | solution.py:439
  79.6 2.1 %collective-permute-start.20 = (bf16[128,1024]{1,0:T(8,128)(2,1)S(1)}, bf16[128,1024]{1,0:T(8,128)(2,1)S(1)}, u32[]{:S(2)}, u32[]{:S(2)}) collective-permute-start(bf16[128,1024]{1,0:T(8,128)(2,1)S(1)} %get-tuple-element.83), channel_id=1, source_target_pairs={{0,1},{1,0},{2,3},{3,2},{4,5},{5,4},{6,7},{7,6},{8,9},{9,8},{10,11... | collective-permute-start | bytes 786440 | tf_op jit(solution)/shard_map/ppermute | solution.py:439
  80.0 1.7 %collective-permute-start.21 = (bf16[128,1024]{1,0:T(8,128)(2,1)S(1)}, bf16[128,1024]{1,0:T(8,128)(2,1)S(1)}, u32[]{:S(2)}, u32[]{:S(2)}) collective-permute-start(bf16[128,1024]{1,0:T(8,128)(2,1)S(1)} %get-tuple-element.84), channel_id=1, source_target_pairs={{0,1},{1,0},{2,3},{3,2},{4,5},{5,4},{6,7},{7,6},{8,9},{9,8},{10,11... | collective-permute-start | bytes 786440 | tf_op jit(solution)/shard_map/ppermute | solution.py:439
  80.3 1.5 %collective-permute-start.22 = (bf16[128,1024]{1,0:T(8,128)(2,1)S(1)}, bf16[128,1024]{1,0:T(8,128)(2,1)S(1)}, u32[]{:S(2)}, u32[]{:S(2)}) collective-permute-start(bf16[128,1024]{1,0:T(8,128)(2,1)S(1)} %get-tuple-element.85), channel_id=1, source_target_pairs={{0,1},{1,0},{2,3},{3,2},{4,5},{5,4},{6,7},{7,6},{8,9},{9,8},{10,11... | collective-permute-start | bytes 786440 | tf_op jit(solution)/shard_map/ppermute | solution.py:439
  80.7 1.5 %collective-permute-start.23 = (bf16[128,1024]{1,0:T(8,128)(2,1)S(1)}, bf16[128,1024]{1,0:T(8,128)(2,1)S(1)}, u32[]{:S(2)}, u32[]{:S(2)}) collective-permute-start(bf16[128,1024]{1,0:T(8,128)(2,1)S(1)} %get-tuple-element.86), channel_id=1, source_target_pairs={{0,1},{1,0},{2,3},{3,2},{4,5},{5,4},{6,7},{7,6},{8,9},{9,8},{10,11... | collective-permute-start | bytes 786440 | tf_op jit(solution)/shard_map/ppermute | solution.py:439

commit v15 on v13

--- a/solution.py
+++ b/solution.py
@@ -50,9 +50,10 @@
     ]
 
 
-def pick_kernel(rank_ref, vert_ref, k_ref, v_ref, both_ref, pair_ref):
+def pick_kernel(rank_ref, vert_ref, k_ref, v_ref, both_ref, late_ref, pair_ref):
     both_ref[:, :HS] = k_ref[...]
     both_ref[:, HS:] = v_ref[...]
+    late_ref[...] = both_ref[both_ref.shape[0] - late_ref.shape[0] :, :]
     blocks = picked_blocks(vert_ref[...], rank_ref[0], k_ref.shape[0] // BLK)
     for slot, rows in enumerate(blocks):
         picked = both_ref[rows, :]
@@ -65,10 +66,11 @@
         pick_kernel,
         out_shape=(
             jax.ShapeDtypeStruct((keys.shape[0], 2 * HS), keys.dtype),
+            jax.ShapeDtypeStruct(((SPAN - 1) * BLK - keys.shape[0], 2 * HS), keys.dtype),
             jax.ShapeDtypeStruct((copies, VMOST * BLK, 2 * HS), keys.dtype),
         ),
         in_specs=[smem(), vmem(), vmem(), vmem()],
-        out_specs=(vmem(), vmem()),
+        out_specs=(vmem(),) * 3,
         compiler_params=params(60),
         name="pick",
     )(rank, vertical, keys, values)
@@ -97,8 +99,15 @@
     return jnp.where((picked < local_blocks) & (shard >= 0), shard * local_blocks + picked, -1)
 
 
-def tables_kernel(slots, rank_ref, vert_ref, slash_ref, own_ref, table_ref, copy_ref):
+def tables_kernel(slots, rank_ref, vert_ref, slash_ref, own_ref, table_ref, copy_ref, win_ref, pool_ref):
     copy_ref[...] = own_ref[...]
+    key = lax.broadcasted_iota(jnp.int32, win_ref.shape, 0)
+    lane = lax.broadcasted_iota(jnp.int32, win_ref.shape, 1)
+    last = (key - (SPAN - 1) * BLK == lane - BLK) & (lane >= BLK)
+    win_ref[...] = jnp.where((key // BLK == lane) | last, 1.0, 0.0).astype(win_ref.dtype)
+    key = lax.broadcasted_iota(jnp.int32, pool_ref.shape, 0)
+    lane = lax.broadcasted_iota(jnp.int32, pool_ref.shape, 1)
+    pool_ref[...] = jnp.where(key // BLK == lane, 1.0, 0.0).astype(pool_ref.dtype)
     local_blocks = own_ref.shape[0] // BLK
     table_ref[0, :, : vert_ref.shape[1]] = vert_ref[...]
     table_ref[1, :, : slash_ref.shape[1]] = slash_ref[...]
@@ -112,9 +121,11 @@
         out_shape=(
             jax.ShapeDtypeStruct(shape, jnp.int32),
             jax.ShapeDtypeStruct(own.shape, own.dtype),
+            jax.ShapeDtypeStruct((SPAN * BLK, LANES), own.dtype),
+            jax.ShapeDtypeStruct((2 * slots * VMOST * BLK, LANES), own.dtype),
         ),
         in_specs=[smem(), vmem(), vmem(), vmem()],
-        out_specs=(vmem(), vmem()),
+        out_specs=(vmem(),) * 4,
         compiler_params=params(4),
         cost_estimate=SHORT,
         name="tables",
@@ -122,12 +133,12 @@
 
 
 def attend_kernel(
-    slots, tiles, sizes, place, tp_ref, ctx_ref, q_0, q_1, table_ref, own, kv_2, kv_1, *refs
+    slots, tiles, sizes, place, tp_ref, ctx_ref, q_0, q_1, table_ref, e_win, e_pool, own, kv_1, kv_2, *refs
 ):
     pairs = refs[:2]
     w_hbm = refs[2]
-    kv_win, e_win, kv_pool, e_pool, attended, weight, arrival, landed = refs[-8:]
-    outs = refs[-11:-8] if tiles else refs[-9:-8]
+    kv_win, kv_pool, attended, weight, arrival, landed = refs[-6:]
+    outs = refs[-9:-6] if tiles else refs[-7:-6]
     step = pl.program_id(0)
     heads = table_ref.shape[1]
     rows = own.shape[0]
@@ -146,9 +157,11 @@
 
     @pl.when(step == 0)
     def _():
+        reach = kv_2.shape[0]
+        places = ((kv_2, 0), (kv_1, reach), (own, reach + rows))
         copies = [
-            pltpu.make_async_copy(x, kv_win.at[pl.ds(s * rows, rows), :], landed.at[s])
-            for s, x in enumerate((kv_2, kv_1, own))
+            pltpu.make_async_copy(x, kv_win.at[pl.ds(at, x.shape[0]), :], landed.at[s])
+            for s, (x, at) in enumerate(places)
         ]
         copies += [
             pltpu.make_async_copy(
@@ -160,13 +173,6 @@
             copy.start()
         for t in range(tiles):
             fetch(t).start()
-        key = lax.broadcasted_iota(jnp.int32, e_win.shape, 0)
-        lane = lax.broadcasted_iota(jnp.int32, e_win.shape, 1)
-        last = (key - (SPAN - 1) * BLK == lane - BLK) & (lane >= BLK)
-        e_win[...] = jnp.where((key // BLK == lane) | last, 1.0, 0.0).astype(dtype)
-        key = lax.broadcasted_iota(jnp.int32, e_pool.shape, 0)
-        lane = lax.broadcasted_iota(jnp.int32, e_pool.shape, 1)
-        e_pool[...] = jnp.where(key // BLK == lane, 1.0, 0.0).astype(dtype)
         for copy in copies:
             copy.wait()
 
@@ -195,7 +201,7 @@
         far_mask = jnp.broadcast_to(far_mask[:, None, :], (heads, BLK, LANES))
         far_mask = far_mask.reshape(heads * BLK, LANES).astype(dtype)
         far_q.append(jnp.concatenate([q, far_mask], axis=1))
-        window = pl.ds(pl.multiple_of((here + 1) * BLK, BLK), SPAN * BLK)
+        window = pl.ds(pl.multiple_of(here * BLK, BLK), SPAN * BLK)
         windows.append(window)
         keys = jnp.concatenate([kv_win[window, :HS], e_win[...]], axis=1)
         near.append(
@@ -240,14 +246,14 @@
             outs[2][:, t * TILE : (t + 1) * TILE] = product[half:]
 
 
-def attend(blocks, tp, ctx, queries, table, near_kv, pairs, sizes, out_weight, tiles, after):
+def attend(blocks, tp, ctx, queries, lanes, near_kv, pairs, sizes, out_weight, tiles, after):
     width = queries.shape[1]
     rows = near_kv[0].shape[0]
+    assert near_kv[2].shape[0] + rows == (SPAN - 1) * BLK
     quarter = rows // BLK // 4
     steps = len(blocks)
     slots = pairs[1].shape[0]
     dtype = queries.dtype
-    far = 2 * slots * VMOST * BLK
 
     def place(u, g, tp):
         flip, block = blocks[-1][u]
@@ -272,14 +278,12 @@
                 pl.BlockSpec((BLK, width), lambda g, tp, ctx: (place(0, g, tp), 0)),
                 pl.BlockSpec((BLK, width), lambda g, tp, ctx: (place(1, g, tp), 0)),
             ]
-            + [whole(table.shape)]
+            + [whole(x.shape) for x in lanes]
             + [anywhere() for _ in [*near_kv, *pairs, out_weight, *after]],
             out_specs=[whole(shape) for shape in out_shapes],
             scratch_shapes=[
-                pltpu.VMEM((NEAR * rows, 2 * HS), dtype),
-                pltpu.VMEM((SPAN * BLK, LANES), dtype),
+                pltpu.VMEM((near_kv[2].shape[0] + 2 * rows, 2 * HS), dtype),
                 pltpu.VMEM((2 * slots, VMOST * BLK, 2 * HS), dtype),
-                pltpu.VMEM((far, LANES), dtype),
                 pltpu.VMEM((steps * 2 * BLK, width), dtype),
                 pltpu.VMEM((max(tiles, 1), out_weight.shape[0], TILE), dtype),
                 pltpu.SemaphoreType.DMA((max(tiles, 1),)),
@@ -289,7 +293,7 @@
         compiler_params=params(50),
         cost_estimate=SHORT,
         name="attend",
-    )(tp, ctx, queries, queries, table, *near_kv, *pairs, out_weight, *after)
+    )(tp, ctx, queries, queries, *lanes, *near_kv, *pairs, out_weight, *after)
 
 
 def project_kernel(first, a_ref, w_hbm, *refs):
@@ -298,15 +302,26 @@
     outs = refs[-2 - 2 * tiles : -2]
     half = outs[0].shape[0]
 
+    parts = arrival.shape[1]
+    rows = weight.shape[1] // parts
+
     def fetch(t):
-        return pltpu.make_async_copy(
-            w_hbm.at[:, pl.ds(first + t * tile, tile)], weight.at[t], arrival.at[t]
-        )
-
+        columns = pl.ds(first + t * tile, tile)
+        ats = [pl.ds(p * rows, rows) for p in range(parts)]
+        return [
+            pltpu.make_async_copy(w_hbm.at[at, columns], weight.at[t, at], arrival.at[t, p])
+            for p, at in enumerate(ats)
+        ]
+
+    for t in range(min(2, tiles)):
+        for copy in fetch(t):
+            copy.start()
     for t in range(tiles):
-        fetch(t).start()
-    for t in range(tiles):
-        fetch(t).wait()
+        for copy in fetch(t):
+            copy.wait()
+        if t + 2 < tiles:
+            for copy in fetch(t + 2):
+                copy.start()
         product = jnp.dot(a_ref[...], weight[t], preferred_element_type=jnp.float32)
         product = product.astype(a_ref.dtype)
         outs[t][...] = product[:half]
@@ -324,7 +339,7 @@
         out_specs=[vmem()] * (2 * tiles),
         scratch_shapes=[
             pltpu.VMEM((tiles, depth, tile), attended.dtype),
-            pltpu.SemaphoreType.DMA((tiles,)),
+            pltpu.SemaphoreType.DMA((tiles, 4)),
         ],
         compiler_params=params(50),
         cost_estimate=SHORT,
@@ -404,13 +419,13 @@
         return lax.ppermute(x, "ctx", [(r, r + by) for r in range(ctx_size - by)])
 
     half = ctx_size // 2
-    own, pair = pick(ctx, vertical, keys, values, half)
+    own, late, pair = pick(ctx, vertical, keys, values, half)
     parities = [list(range(odd, ctx_size, 2)) for odd in (0, 1)]
     pairs = [lax.all_to_all(pair, "ctx", 0, 0, axis_index_groups=parities, tiled=True)]
     needed = pairs[0][: half - 1]
     pairs.append(lax.ppermute(needed, "ctx", [(r, r ^ 1) for r in range(ctx_size)]))
-    table, own_copy = tables(ctx, vertical, slash, own, half - 1)
-    near_kv = [own_copy, shifted(own, 2), shifted(own, 1)]
+    table, own_copy, e_win, e_pool = tables(ctx, vertical, slash, own, half - 1)
+    near_kv = [own_copy, shifted(own, 1), shifted(late, 2)]
 
     def sibling(x):
         return lax.ppermute(x, "tp", [(j, j ^ 1) for j in range(4)])
@@ -421,7 +436,7 @@
     def attention(blocks, tiles, after):
         sizes = (vertical.shape[1], slash.shape[1])
         return attend(
-            blocks, tp, ctx, queries, table, near_kv, pairs, sizes, out_weight, tiles, after
+            blocks, tp, ctx, queries, (table, e_win, e_pool), near_kv, pairs, sizes, out_weight, tiles, after
         )
 
     def exchanged(send, keep):

time: 84.3 us -> 84.5 us (level)
  Pallas kernels: 39.3 us -> 41.3 us
  waiting for transfers between devices: 20.4 us -> 18.8 us
    ppermute x3, waiting for transfers between devices: 6.77 us -> 5.28 us  [across(): return lax.ppermute(x, 'tp', [(j, j ^ 2) for j in range(4)])]
    pallas_call x3, Pallas kernels: 21 us -> 22.5 us  [project(): pl.pallas_call(functools.partial(project_kernel, first), out_shape=[part]...]
  transfers between devices with their start and end apart: 24 -> 24, of which waited for: 19 -> 20; matrix products, arithmetic and copies ran while one was open for 0% -> 0% of each run, Pallas kernels for 38% -> 40%
where the time goes in v15:
time: 84.5 us; the launch traced here: 83.9 us
  Pallas kernels  41.3 us (49%)
  starting transfers between devices  20.2 us (24%)
  waiting for transfers between devices  18.8 us (22%)
  local copies, waits for them, and re-layouts  3.14 us (4%)
    pallas_call x3, Pallas kernels, project(): pl.pallas_call(functools.partial(project_kernel, first), out_shape=[part]...  22.5 us
    pallas_call x3, Pallas kernels, attend(): pl.pallas_call(functools.partial(attend_kernel, slots, tiles, sizes, plac...  13.2 us
    ppermute x2, starting transfers between devices, shifted(): return lax.ppermute(x, 'ctx', [(r, r + by) for r in range(ctx_size - by)])  6.79 us
    ppermute x17, waiting for transfers between devices, sibling(): return lax.ppermute(x, 'tp', [(j, j ^ 1) for j in range(4)])  6.25 us
    ppermute x3, waiting for transfers between devices, across(): return lax.ppermute(x, 'tp', [(j, j ^ 2) for j in range(4)])  5.28 us
    all_to_all x1, starting transfers between devices, shards(): lax.all_to_all(pair, 'ctx', 0, 0, axis_index_groups=parities, tiled=True)  5.2 us
    ppermute x2, waiting for transfers between devices, shifted(): return lax.ppermute(x, 'ctx', [(r, r + by) for r in range(ctx_size - by)])  3.86 us
    ppermute x17, starting transfers between devices, sibling(): return lax.ppermute(x, 'tp', [(j, j ^ 1) for j in range(4)])  3.86 us
  transfers between devices with their start and end apart: 24, of which 20 were waited for; matrix products, arithmetic and copies ran while one was open for 0% of the time, Pallas kernels for 40%

profile of v15, /device:TPU:16, one launch (start us, length us, event | category | flops | bytes accessed | tf_op | source)
XLA Modules:
  0.0 83.9 jit_solution(12766215586956059237)
XLA Ops:
  0.0 2.2 %pick.1 = (bf16[512,256]{1,0:T(8,128)(2,1)}, bf16[448,256]{1,0:T(8,128)(2,1)}, bf16[4,128,256]{2,1,0:T(8,128)(2,1)}) custom-call(s32[1]{0:T(128)} %bitcast.1.rank_ref.ctx_ref, s32[8,16]{1,0:T(8,128)} %vert_ref.3, bf16[512,128]{1,0:T(8,128)(2,1)} %k_ref.1, bf16[512,128]{1,0:T(8,128)(2,1)} %v_ref.1), custom_call_target="tpu_custom_call" | custom-call | tf_op jit(solution)/shard_map/pick/pallas_call | solution.py:65
  2.2 5.2 %all-to-all-start = ((bf16[4,128,256]{2,1,0:T(8,128)(2,1)}), bf16[4,128,256]{2,1,0:T(8,128)(2,1)S(1)}, u32[]{:S(2)}, u32[]{:S(2)}) async-start(bf16[4,128,256]{2,1,0:T(8,128)(2,1)} %get-tuple-element.53), calls=%async_computation | async-start | bytes 524288 | tf_op jit(solution)/shard_map/all_to_all | solution.py:424
  7.4 3.4 %collective-permute-start = (bf16[512,256]{1,0:T(8,128)(2,1)}, bf16[512,256]{1,0:T(8,128)(2,1)S(1)}, u32[]{:S(2)}, u32[]{:S(2)}) collective-permute-start(bf16[512,256]{1,0:T(8,128)(2,1)} %get-tuple-element.47.own_ref), channel_id=1, source_target_pairs={{0,4},{4,8},{8,12},{12,16},{16,20},{20,24},{24,28},{1,5},{5,9},{9,... | collective-permute-start | bytes 786440 | tf_op jit(solution)/shard_map/ppermute | solution.py:419
  10.8 3.4 %collective-permute-start.1 = (bf16[448,256]{1,0:T(8,128)(2,1)}, bf16[448,256]{1,0:T(8,128)(2,1)S(1)}, u32[]{:S(2)}, u32[]{:S(2)}) collective-permute-start(bf16[448,256]{1,0:T(8,128)(2,1)} %get-tuple-element.52), channel_id=1, source_target_pairs={{0,8},{4,12},{8,16},{12,20},{16,24},{20,28},{1,9},{5,13},{9,17},{1... | collective-permute-start | bytes 688136 | tf_op jit(solution)/shard_map/ppermute | solution.py:419
  14.2 0.6 collective-permute-start.2
  14.8 0.9 %copy-done.4 = bf16[512,256]{1,0:T(8,128)(2,1)S(1)} copy-done((bf16[512,256]{1,0:T(8,128)(2,1)S(1)}, bf16[512,256]{1,0:T(8,128)(2,1)}, u32[]{:S(2)}) %copy-start.4) | copy-done | bytes 262168
  15.8 0.7 copy-done.5
  16.5 0.7 copy-done.6
  17.2 0.2 tables.1
  17.4 2.0 %collective-permute-done.1.kv_2 = bf16[448,256]{1,0:T(8,128)(2,1)S(1)} collective-permute-done((bf16[448,256]{1,0:T(8,128)(2,1)}, bf16[448,256]{1,0:T(8,128)(2,1)S(1)}, u32[]{:S(2)}, u32[]{:S(2)}) %collective-permute-start.1) | collective-permute-done | bytes 229408 | tf_op jit(solution)/shard_map/ppermute | solution.py:419
  19.4 1.8 %collective-permute-done.kv_1 = bf16[512,256]{1,0:T(8,128)(2,1)S(1)} collective-permute-done((bf16[512,256]{1,0:T(8,128)(2,1)}, bf16[512,256]{1,0:T(8,128)(2,1)S(1)}, u32[]{:S(2)}, u32[]{:S(2)}) %collective-permute-start) | collective-permute-done | bytes 262176 | tf_op jit(solution)/shard_map/ppermute | solution.py:419
  21.3 3.4 %collective-permute-done.2.refs_1_ = bf16[3,128,256]{2,1,0:T(8,128)(2,1)S(1)} collective-permute-done((bf16[3,128,256]{2,1,0:T(8,128)(2,1)S(1)}, bf16[3,128,256]{2,1,0:T(8,128)(2,1)S(1)}, u32[]{:S(2)}, u32[]{:S(2)}) %collective-permute-start.2) | collective-permute-done | bytes 196640 | tf_op jit(solution)/shard_map/ppermute | solution.py:426
  24.7 4.4 %attend.3 = (bf16[128,1024]{1,0:T(8,128)(2,1)S(1)}, bf16[64,2048]{1,0:T(8,128)(2,1)S(1)}, bf16[64,2048]{1,0:T(8,128)(2,1)S(1)}) custom-call(s32[1]{0:T(128)} %bitcast.tp_ref, s32[1]{0:T(128)} %bitcast.1.rank_ref.ctx_ref, bf16[512,1024]{1,0:T(8,128)(2,1)S(1)} %copy-done, bf16[512,1024]{1,0:T(8,128)(2,1)S(1)} %copy-done, ...), custom_call_target="tpu_custom_call" | custom-call | tf_op jit(solution)/shard_map/attend/pallas_call | solution.py:271
  29.2 1.5 %collective-permute-done.3 = bf16[64,2048]{1,0:T(8,128)(2,1)S(1)} collective-permute-done((bf16[64,2048]{1,0:T(8,128)(2,1)S(1)}, bf16[64,2048]{1,0:T(8,128)(2,1)S(1)}, u32[]{:S(2)}, u32[]{:S(2)}) %collective-permute-start.3) | collective-permute-done | bytes 262176 | tf_op jit(solution)/shard_map/ppermute | solution.py:431
  30.8 1.6 %collective-permute-start.8 = (bf16[64,2048]{1,0:T(8,128)(2,1)S(1)}, bf16[64,2048]{1,0:T(8,128)(2,1)S(1)}, u32[]{:S(2)}, u32[]{:S(2)}) collective-permute-start(bf16[64,2048]{1,0:T(8,128)(2,1)S(1)} %add_convert_fusion.refs_0_), channel_id=1, source_target_pairs={{0,2},{1,3},{2,0},{3,1},{4,6},{5,7},{6,4},{7,5},{8,10},{9,11},{10,... | collective-permute-start | bytes 786440 | tf_op jit(solution)/shard_map/ppermute | solution.py:434
  32.3 5.6 %project.3 = (bf16[64,1536]{1,0:T(8,128)(2,1)S(1)}, bf16[64,1536]{1,0:T(8,128)(2,1)S(1)}, bf16[64,1536]{1,0:T(8,128)(2,1)S(1)}, bf16[64,1536]{1,0:T(8,128)(2,1)S...) custom-call(bf16[128,1024]{1,0:T(8,128)(2,1)S(1)} %get-tuple-element, ...), custom_call_target="tpu_custom_call" | custom-call | tf_op jit(solution)/shard_map/project/pallas_call | solution.py:335
  38.0 0.5 collective-permute-start.5
  38.5 0.4 collective-permute-start.7
  39.0 0.4 collective-permute-done.4.refs_4_
  39.4 0.3 collective-permute-done.5.refs_5_
  39.7 0.3 collective-permute-done.6.refs_6_
  40.0 0.3 collective-permute-done.7.refs_7_
  40.4 0.6 collective-permute-start.13
  41.0 3.2 %attend.4.a_ref = bf16[128,1024]{1,0:T(8,128)(2,1)S(1)} custom-call(s32[1]{0:T(128)} %bitcast.tp_ref, s32[1]{0:T(128)} %bitcast.1.rank_ref.ctx_ref, bf16[512,1024]{1,0:T(8,128)(2,1)S(1)} %copy-done, bf16[512,1024]{1,0:T(8,128)(2,1)S(1)} %copy-done, s32[3,8,128]{2,1,0:T(8,128)S(1)} %get-tuple-element.48.table_ref, ...), custom_call_target="tpu_custom_call" | custom-call | tf_op jit(solution)/shard_map/attend/pallas_call | solution.py:271
  44.3 6.9 %project.4 = (bf16[64,2048]{1,0:T(8,128)(2,1)S(1)}, bf16[64,2048]{1,0:T(8,128)(2,1)S(1)}, bf16[64,2048]{1,0:T(8,128)(2,1)S(1)}, bf16[64,2048]{1,0:T(8,128)(2,1)S...) custom-call(bf16[128,1024]{1,0:T(8,128)(2,1)S(1)} %attend.4.a_ref, ...), custom_call_target="tpu_custom_call" | custom-call | tf_op jit(solution)/shard_map/project/pallas_call | solution.py:335
  51.3 0.5 collective-permute-start.10
  51.8 0.4 collective-permute-start.12
  52.3 0.5 collective-permute-done.9.refs_4_
  52.8 0.4 collective-permute-done.10.refs_5_
  53.1 0.4 collective-permute-done.11.refs_6_
  53.5 0.4 collective-permute-done.12.refs_7_
  53.9 0.2 add.8.refs_3_
  54.2 1.6 %collective-permute-start.22 = (bf16[64,8192]{1,0:T(8,128)(2,1)S(1)}, bf16[64,8192]{1,0:T(8,128)(2,1)S(1)}, u32[]{:S(2)}, u32[]{:S(2)}) collective-permute-start(bf16[64,8192]{1,0:T(8,128)(2,1)S(1)} %add.8.refs_3_), channel_id=1, source_target_pairs={{0,2},{1,3},{2,0},{3,1},{4,6},{5,7},{6,4},{7,5},{8,10},{9,11},{10,... | collective-permute-start | bytes 3145736 | tf_op jit(solution)/shard_map/ppermute | solution.py:434
  55.7 5.2 %collective-permute-done.13.refs_4_.refs_12_ = bf16[64,6144]{1,0:T(8,128)(2,1)S(1)} collective-permute-done((bf16[64,6144]{1,0:T(8,128)(2,1)S(1)}, bf16[64,6144]{1,0:T(8,128)(2,1)S(1)}, u32[]{:S(2)}, u32[]{:S(2)}) %collective-permute-start.13) | collective-permute-done | bytes 786464 | tf_op jit(solution)/shard_map/ppermute | solution.py:434
  60.9 5.6 %attend.5.a_ref = bf16[256,1024]{1,0:T(8,128)(2,1)S(1)} custom-call(s32[1]{0:T(128)} %bitcast.tp_ref, s32[1]{0:T(128)} %bitcast.1.rank_ref.ctx_ref, bf16[512,1024]{1,0:T(8,128)(2,1)S(1)} %copy-done, bf16[512,1024]{1,0:T(8,128)(2,1)S(1)} %copy-done, s32[3,8,128]{2,1,0:T(8,128)S(1)} %get-tuple-element.48.table_ref, ...), custom_call_target="tpu_custom_call" | custom-call | tf_op jit(solution)/shard_map/attend/pallas_call | solution.py:271
  66.5 0.8 copy-done.2
  67.2 10.0 %project.5 = (bf16[128,1024]{1,0:T(8,128)(2,1)S(1)}, bf16[128,1024]{1,0:T(8,128)(2,1)S(1)}, bf16[128,1024]{1,0:T(8,128)(2,1)S(1)}, bf16[128,1024]{1,0:T(8,128)(2...) custom-call(bf16[256,1024]{1,0:T(8,128)(2,1)} %copy-done.2, ...), custom_call_target="tpu_custom_call" | custom-call | tf_op jit(solution)/shard_map/project/pallas_call | solution.py:335
  77.3 0.5 collective-permute-start.15
  77.9 0.4 collective-permute-start.17
  78.3 0.5 collective-permute-done.14.refs_2_.refs_8_
  79.0 0.2 collective-permute-done.15.refs_3_.refs_9_
  79.4 0.2 collective-permute-done.16.refs_6_.refs_10_
  79.7 0.2 collective-permute-done.17.refs_7_.refs_11_
  80.1 0.8 finish.3.refs_13_
  80.9 0.2 collective-permute-done.20.refs_10_.refs_14_
  81.1 0.4 collective-permute-done.21.refs_11_.refs_15_
  81.5 1.0 %finish.4.refs_17_ = bf16[128,8192]{1,0:T(8,128)(2,1)} custom-call(bf16[128,1024]{1,0:T(8,128)(2,1)S(1)} %get-tuple-element.75.refs_0_.refs_2_, bf16[128,1024]{1,0:T(8,128)(2,1)S(1)} %get-tuple-element.76.refs_1_.refs_3_, bf16[128,1024]{1,0:T(8,128)(2,1)S(1)} %get-tuple-element.77.refs_2_.refs_4_, ...), custom_call_target="tpu_custom_call", output_to_operand_aliasing={{}: (13, {})} | custom-call | tf_op jit(solution)/shard_map/finish/pallas_call | solution.py:396
  82.6 1.1 %finish.5 = bf16[128,8192]{1,0:T(8,128)(2,1)} custom-call(bf16[128,1024]{1,0:T(8,128)(2,1)S(1)} %get-tuple-element.73.refs_0_, bf16[128,1024]{1,0:T(8,128)(2,1)S(1)} %get-tuple-element.74.refs_1_, bf16[128,1024]{1,0:T(8,128)(2,1)S(1)} %get-tuple-element.75.refs_0_.refs_2_, ...), custom_call_target="tpu_custom_call", output_to_operand_aliasing={{}: (17, {})} | custom-call | tf_op jit(solution)/shard_map/finish/pallas_call | solution.py:396
  (29 shorter events, 1.5 us)
Async XLA Ops:
  0.0 24.7 %copy-start = (bf16[512,1024]{1,0:T(8,128)(2,1)S(1)}, bf16[512,1024]{1,0:T(8,128)(2,1)}, u32[]{:S(2)}) copy-start(bf16[512,1024]{1,0:T(8,128)(2,1)} %q_1.5) | copy-start | bytes 3145732
  2.2 12.0 %all-to-all-start = ((bf16[4,128,256]{2,1,0:T(8,128)(2,1)}), bf16[4,128,256]{2,1,0:T(8,128)(2,1)S(1)}, u32[]{:S(2)}, u32[]{:S(2)}) async-start(bf16[4,128,256]{2,1,0:T(8,128)(2,1)} %get-tuple-element.53), calls=%async_computation | async-start | bytes 524288 | tf_op jit(solution)/shard_map/all_to_all | solution.py:424
  7.4 13.9 %collective-permute-start = (bf16[512,256]{1,0:T(8,128)(2,1)}, bf16[512,256]{1,0:T(8,128)(2,1)S(1)}, u32[]{:S(2)}, u32[]{:S(2)}) collective-permute-start(bf16[512,256]{1,0:T(8,128)(2,1)} %get-tuple-element.47.own_ref), channel_id=1, source_target_pairs={{0,4},{4,8},{8,12},{12,16},{16,20},{20,24},{24,28},{1,5},{5,9},{9,... | collective-permute-start | bytes 786440 | tf_op jit(solution)/shard_map/ppermute | solution.py:419
  10.8 8.6 %collective-permute-start.1 = (bf16[448,256]{1,0:T(8,128)(2,1)}, bf16[448,256]{1,0:T(8,128)(2,1)S(1)}, u32[]{:S(2)}, u32[]{:S(2)}) collective-permute-start(bf16[448,256]{1,0:T(8,128)(2,1)} %get-tuple-element.52), channel_id=1, source_target_pairs={{0,8},{4,12},{8,16},{12,20},{16,24},{20,28},{1,9},{5,13},{9,17},{1... | collective-permute-start | bytes 688136 | tf_op jit(solution)/shard_map/ppermute | solution.py:419
  14.2 10.5 %collective-permute-start.2 = (bf16[3,128,256]{2,1,0:T(8,128)(2,1)S(1)}, bf16[3,128,256]{2,1,0:T(8,128)(2,1)S(1)}, u32[]{:S(2)}, u32[]{:S(2)}) collective-permute-start(bf16[3,128,256]{2,1,0:T(8,128)(2,1)S(1)} %slice.4), channel_id=1, source_target_pairs={{0,4},{4,0},{8,12},{12,8},{16,20},{20,16},{24,28},{28,24},{1,5},{5... | collective-permute-start | bytes 589832 | tf_op jit(solution)/shard_map/ppermute | solution.py:426
  14.8 0.9 %copy-start.4 = (bf16[512,256]{1,0:T(8,128)(2,1)S(1)}, bf16[512,256]{1,0:T(8,128)(2,1)}, u32[]{:S(2)}) copy-start(bf16[512,256]{1,0:T(8,128)(2,1)} %get-tuple-element.47.own_ref) | copy-start | bytes 786436
  15.8 0.7 copy-start.5
  16.5 0.7 copy-start.6
  29.1 1.6 %collective-permute-start.3 = (bf16[64,2048]{1,0:T(8,128)(2,1)S(1)}, bf16[64,2048]{1,0:T(8,128)(2,1)S(1)}, u32[]{:S(2)}, u32[]{:S(2)}) collective-permute-start(bf16[64,2048]{1,0:T(8,128)(2,1)S(1)} %get-tuple-element.56), channel_id=1, source_target_pairs={{0,1},{1,0},{2,3},{3,2},{4,5},{5,4},{6,7},{7,6},{8,9},{9,8},{10,11... | collective-permute-start | bytes 786440 | tf_op jit(solution)/shard_map/ppermute | solution.py:431
  30.8 13.5 %collective-permute-start.8 = (bf16[64,2048]{1,0:T(8,128)(2,1)S(1)}, bf16[64,2048]{1,0:T(8,128)(2,1)S(1)}, u32[]{:S(2)}, u32[]{:S(2)}) collective-permute-start(bf16[64,2048]{1,0:T(8,128)(2,1)S(1)} %add_convert_fusion.refs_0_), channel_id=1, source_target_pairs={{0,2},{1,3},{2,0},{3,1},{4,6},{5,7},{6,4},{7,5},{8,10},{9,11},{10,... | collective-permute-start | bytes 786440 | tf_op jit(solution)/shard_map/ppermute | solution.py:434
  37.9 1.5 %collective-permute-start.4 = (bf16[64,1536]{1,0:T(8,128)(2,1)S(1)}, bf16[64,1536]{1,0:T(8,128)(2,1)S(1)}, u32[]{:S(2)}, u32[]{:S(2)}) collective-permute-start(bf16[64,1536]{1,0:T(8,128)(2,1)S(1)} %get-tuple-element.61), channel_id=1, source_target_pairs={{0,1},{1,0},{2,3},{3,2},{4,5},{5,4},{6,7},{7,6},{8,9},{9,8},{10,11... | collective-permute-start | bytes 589832 | tf_op jit(solution)/shard_map/ppermute | solution.py:431
  38.0 1.7 %collective-permute-start.5 = (bf16[64,1536]{1,0:T(8,128)(2,1)S(1)}, bf16[64,1536]{1,0:T(8,128)(2,1)S(1)}, u32[]{:S(2)}, u32[]{:S(2)}) collective-permute-start(bf16[64,1536]{1,0:T(8,128)(2,1)S(1)} %get-tuple-element.62), channel_id=1, source_target_pairs={{0,1},{1,0},{2,3},{3,2},{4,5},{5,4},{6,7},{7,6},{8,9},{9,8},{10,11... | collective-permute-start | bytes 589832 | tf_op jit(solution)/shard_map/ppermute | solution.py:431
  38.5 1.5 %collective-permute-start.6 = (bf16[64,1536]{1,0:T(8,128)(2,1)S(1)}, bf16[64,1536]{1,0:T(8,128)(2,1)S(1)}, u32[]{:S(2)}, u32[]{:S(2)}) collective-permute-start(bf16[64,1536]{1,0:T(8,128)(2,1)S(1)} %get-tuple-element.63), channel_id=1, source_target_pairs={{0,1},{1,0},{2,3},{3,2},{4,5},{5,4},{6,7},{7,6},{8,9},{9,8},{10,11... | collective-permute-start | bytes 589832 | tf_op jit(solution)/shard_map/ppermute | solution.py:431
  38.5 1.7 %collective-permute-start.7 = (bf16[64,1536]{1,0:T(8,128)(2,1)S(1)}, bf16[64,1536]{1,0:T(8,128)(2,1)S(1)}, u32[]{:S(2)}, u32[]{:S(2)}) collective-permute-start(bf16[64,1536]{1,0:T(8,128)(2,1)S(1)} %get-tuple-element.64), channel_id=1, source_target_pairs={{0,1},{1,0},{2,3},{3,2},{4,5},{5,4},{6,7},{7,6},{8,9},{9,8},{10,11... | collective-permute-start | bytes 589832 | tf_op jit(solution)/shard_map/ppermute | solution.py:431
  40.4 20.4 %collective-permute-start.13 = (bf16[64,6144]{1,0:T(8,128)(2,1)S(1)}, bf16[64,6144]{1,0:T(8,128)(2,1)S(1)}, u32[]{:S(2)}, u32[]{:S(2)}) collective-permute-start(bf16[64,6144]{1,0:T(8,128)(2,1)S(1)} %add.7.refs_3_), channel_id=1, source_target_pairs={{0,2},{1,3},{2,0},{3,1},{4,6},{5,7},{6,4},{7,5},{8,10},{9,11},{10,... | collective-permute-start | bytes 2359304 | tf_op jit(solution)/shard_map/ppermute | solution.py:434
  51.2 1.6 %collective-permute-start.9 = (bf16[64,2048]{1,0:T(8,128)(2,1)S(1)}, bf16[64,2048]{1,0:T(8,128)(2,1)S(1)}, u32[]{:S(2)}, u32[]{:S(2)}) collective-permute-start(bf16[64,2048]{1,0:T(8,128)(2,1)S(1)} %get-tuple-element.69), channel_id=1, source_target_pairs={{0,1},{1,0},{2,3},{3,2},{4,5},{5,4},{6,7},{7,6},{8,9},{9,8},{10,11... | collective-permute-start | bytes 786440 | tf_op jit(solution)/shard_map/ppermute | solution.py:431
  51.3 1.9 %collective-permute-start.10 = (bf16[64,2048]{1,0:T(8,128)(2,1)S(1)}, bf16[64,2048]{1,0:T(8,128)(2,1)S(1)}, u32[]{:S(2)}, u32[]{:S(2)}) collective-permute-start(bf16[64,2048]{1,0:T(8,128)(2,1)S(1)} %get-tuple-element.70), channel_id=1, source_target_pairs={{0,1},{1,0},{2,3},{3,2},{4,5},{5,4},{6,7},{7,6},{8,9},{9,8},{10,11... | collective-permute-start | bytes 786440 | tf_op jit(solution)/shard_map/ppermute | solution.py:431
  51.7 1.8 %collective-permute-start.11 = (bf16[64,2048]{1,0:T(8,128)(2,1)S(1)}, bf16[64,2048]{1,0:T(8,128)(2,1)S(1)}, u32[]{:S(2)}, u32[]{:S(2)}) collective-permute-start(bf16[64,2048]{1,0:T(8,128)(2,1)S(1)} %get-tuple-element.71), channel_id=1, source_target_pairs={{0,1},{1,0},{2,3},{3,2},{4,5},{5,4},{6,7},{7,6},{8,9},{9,8},{10,11... | collective-permute-start | bytes 786440 | tf_op jit(solution)/shard_map/ppermute | solution.py:431
  51.8 2.1 %collective-permute-start.12 = (bf16[64,2048]{1,0:T(8,128)(2,1)S(1)}, bf16[64,2048]{1,0:T(8,128)(2,1)S(1)}, u32[]{:S(2)}, u32[]{:S(2)}) collective-permute-start(bf16[64,2048]{1,0:T(8,128)(2,1)S(1)} %get-tuple-element.72), channel_id=1, source_target_pairs={{0,1},{1,0},{2,3},{3,2},{4,5},{5,4},{6,7},{7,6},{8,9},{9,8},{10,11... | collective-permute-start | bytes 786440 | tf_op jit(solution)/shard_map/ppermute | solution.py:431
  54.1 6.7 %copy-start.1 = (bf16[64,8192]{1,0:T(8,128)(2,1)}, bf16[64,8192]{1,0:T(8,128)(2,1)S(1)}, u32[]{:S(2)}) copy-start(bf16[64,8192]{1,0:T(8,128)(2,1)S(1)} %add.8.refs_3_) | copy-start | bytes 3145732
  54.2 28.5 %collective-permute-start.22 = (bf16[64,8192]{1,0:T(8,128)(2,1)S(1)}, bf16[64,8192]{1,0:T(8,128)(2,1)S(1)}, u32[]{:S(2)}, u32[]{:S(2)}) collective-permute-start(bf16[64,8192]{1,0:T(8,128)(2,1)S(1)} %add.8.refs_3_), channel_id=1, source_target_pairs={{0,2},{1,3},{2,0},{3,1},{4,6},{5,7},{6,4},{7,5},{8,10},{9,11},{10,... | collective-permute-start | bytes 3145736 | tf_op jit(solution)/shard_map/ppermute | solution.py:434
  66.4 0.8 copy-start.2
  77.2 4.3 %copy-start.3 = (bf16[128,1024]{1,0:T(8,128)(2,1)S(1)}, bf16[128,1024]{1,0:T(8,128)(2,1)}, u32[]{:S(2)}) copy-start(bf16[128,1024]{1,0:T(8,128)(2,1)} %get-tuple-element.80.refs_5_.refs_7_) | copy-start | bytes 786436
  77.3 1.6 %collective-permute-start.14 = (bf16[128,1024]{1,0:T(8,128)(2,1)S(1)}, bf16[128,1024]{1,0:T(8,128)(2,1)S(1)}, u32[]{:S(2)}, u32[]{:S(2)}) collective-permute-start(bf16[128,1024]{1,0:T(8,128)(2,1)S(1)} %get-tuple-element.81), channel_id=1, source_target_pairs={{0,1},{1,0},{2,3},{3,2},{4,5},{5,4},{6,7},{7,6},{8,9},{9,8},{10,11... | collective-permute-start | bytes 786440 | tf_op jit(solution)/shard_map/ppermute | solution.py:431
  77.3 1.9 %collective-permute-start.15 = (bf16[128,1024]{1,0:T(8,128)(2,1)S(1)}, bf16[128,1024]{1,0:T(8,128)(2,1)S(1)}, u32[]{:S(2)}, u32[]{:S(2)}) collective-permute-start(bf16[128,1024]{1,0:T(8,128)(2,1)S(1)} %get-tuple-element.82), channel_id=1, source_target_pairs={{0,1},{1,0},{2,3},{3,2},{4,5},{5,4},{6,7},{7,6},{8,9},{9,8},{10,11... | collective-permute-start | bytes 786440 | tf_op jit(solution)/shard_map/ppermute | solution.py:431
  77.8 1.8 %collective-permute-start.16 = (bf16[128,1024]{1,0:T(8,128)(2,1)S(1)}, bf16[128,1024]{1,0:T(8,128)(2,1)S(1)}, u32[]{:S(2)}, u32[]{:S(2)}) collective-permute-start(bf16[128,1024]{1,0:T(8,128)(2,1)S(1)} %get-tuple-element.83), channel_id=1, source_target_pairs={{0,1},{1,0},{2,3},{3,2},{4,5},{5,4},{6,7},{7,6},{8,9},{9,8},{10,11... | collective-permute-start | bytes 786440 | tf_op jit(solution)/shard_map/ppermute | solution.py:431
  77.9 2.1 %collective-permute-start.17 = (bf16[128,1024]{1,0:T(8,128)(2,1)S(1)}, bf16[128,1024]{1,0:T(8,128)(2,1)S(1)}, u32[]{:S(2)}, u32[]{:S(2)}) collective-permute-start(bf16[128,1024]{1,0:T(8,128)(2,1)S(1)} %get-tuple-element.84), channel_id=1, source_target_pairs={{0,1},{1,0},{2,3},{3,2},{4,5},{5,4},{6,7},{7,6},{8,9},{9,8},{10,11... | collective-permute-start | bytes 786440 | tf_op jit(solution)/shard_map/ppermute | solution.py:431
  78.9 2.0 %collective-permute-start.18 = (bf16[128,1024]{1,0:T(8,128)(2,1)S(1)}, bf16[128,1024]{1,0:T(8,128)(2,1)S(1)}, u32[]{:S(2)}, u32[]{:S(2)}) collective-permute-start(bf16[128,1024]{1,0:T(8,128)(2,1)S(1)} %get-tuple-element.85), channel_id=1, source_target_pairs={{0,1},{1,0},{2,3},{3,2},{4,5},{5,4},{6,7},{7,6},{8,9},{9,8},{10,11... | collective-permute-start | bytes 786440 | tf_op jit(solution)/shard_map/ppermute | solution.py:431
  79.2 1.7 %collective-permute-start.19 = (bf16[128,1024]{1,0:T(8,128)(2,1)S(1)}, bf16[128,1024]{1,0:T(8,128)(2,1)S(1)}, u32[]{:S(2)}, u32[]{:S(2)}) collective-permute-start(bf16[128,1024]{1,0:T(8,128)(2,1)S(1)} %get-tuple-element.86), channel_id=1, source_target_pairs={{0,1},{1,0},{2,3},{3,2},{4,5},{5,4},{6,7},{7,6},{8,9},{9,8},{10,11... | collective-permute-start | bytes 786440 | tf_op jit(solution)/shard_map/ppermute | solution.py:431
  79.6 1.5 %collective-permute-start.20 = (bf16[128,1024]{1,0:T(8,128)(2,1)S(1)}, bf16[128,1024]{1,0:T(8,128)(2,1)S(1)}, u32[]{:S(2)}, u32[]{:S(2)}) collective-permute-start(bf16[128,1024]{1,0:T(8,128)(2,1)S(1)} %get-tuple-element.87), channel_id=1, source_target_pairs={{0,1},{1,0},{2,3},{3,2},{4,5},{5,4},{6,7},{7,6},{8,9},{9,8},{10,11... | collective-permute-start | bytes 786440 | tf_op jit(solution)/shard_map/ppermute | solution.py:431
  80.0 1.5 %collective-permute-start.21 = (bf16[128,1024]{1,0:T(8,128)(2,1)S(1)}, bf16[128,1024]{1,0:T(8,128)(2,1)S(1)}, u32[]{:S(2)}, u32[]{:S(2)}) collective-permute-start(bf16[128,1024]{1,0:T(8,128)(2,1)S(1)} %get-tuple-element.88), channel_id=1, source_target_pairs={{0,1},{1,0},{2,3},{3,2},{4,5},{5,4},{6,7},{7,6},{8,9},{9,8},{10,11... | collective-permute-start | bytes 786440 | tf_op jit(solution)/shard_map/ppermute | solution.py:431

commit v16 on v12

--- a/solution.py
+++ b/solution.py
@@ -50,9 +50,10 @@
     ]
 
 
-def pick_kernel(rank_ref, vert_ref, k_ref, v_ref, both_ref, pair_ref):
+def pick_kernel(rank_ref, vert_ref, k_ref, v_ref, both_ref, late_ref, pair_ref):
     both_ref[:, :HS] = k_ref[...]
     both_ref[:, HS:] = v_ref[...]
+    late_ref[...] = both_ref[both_ref.shape[0] - late_ref.shape[0] :, :]
     blocks = picked_blocks(vert_ref[...], rank_ref[0], k_ref.shape[0] // BLK)
     for slot, rows in enumerate(blocks):
         picked = both_ref[rows, :]
@@ -65,10 +66,11 @@
         pick_kernel,
         out_shape=(
             jax.ShapeDtypeStruct((keys.shape[0], 2 * HS), keys.dtype),
+            jax.ShapeDtypeStruct(((SPAN - 1) * BLK - keys.shape[0], 2 * HS), keys.dtype),
             jax.ShapeDtypeStruct((copies, VMOST * BLK, 2 * HS), keys.dtype),
         ),
         in_specs=[smem(), vmem(), vmem(), vmem()],
-        out_specs=(vmem(), vmem()),
+        out_specs=(vmem(),) * 3,
         compiler_params=params(60),
         name="pick",
     )(rank, vertical, keys, values)
@@ -146,9 +148,11 @@
 
     @pl.when(step == 0)
     def _():
+        reach = kv_2.shape[0]
+        places = ((kv_2, 0), (kv_1, reach), (own, reach + rows))
         copies = [
-            pltpu.make_async_copy(x, kv_win.at[pl.ds(s * rows, rows), :], landed.at[s])
-            for s, x in enumerate((kv_2, kv_1, own))
+            pltpu.make_async_copy(x, kv_win.at[pl.ds(at, x.shape[0]), :], landed.at[s])
+            for s, (x, at) in enumerate(places)
         ]
         copies += [
             pltpu.make_async_copy(
@@ -195,7 +199,7 @@
         far_mask = jnp.broadcast_to(far_mask[:, None, :], (heads, BLK, LANES))
         far_mask = far_mask.reshape(heads * BLK, LANES).astype(dtype)
         far_q.append(jnp.concatenate([q, far_mask], axis=1))
-        window = pl.ds(pl.multiple_of((here + 1) * BLK, BLK), SPAN * BLK)
+        window = pl.ds(pl.multiple_of(here * BLK, BLK), SPAN * BLK)
         windows.append(window)
         keys = jnp.concatenate([kv_win[window, :HS], e_win[...]], axis=1)
         near.append(
@@ -243,6 +247,7 @@
 def attend(blocks, tp, ctx, queries, table, near_kv, pairs, sizes, out_weight, tiles, after):
     width = queries.shape[1]
     rows = near_kv[0].shape[0]
+    assert near_kv[2].shape[0] + rows == (SPAN - 1) * BLK
     quarter = rows // BLK // 4
     steps = len(blocks)
     slots = pairs[1].shape[0]
@@ -276,7 +281,7 @@
             + [anywhere() for _ in [*near_kv, *pairs, out_weight, *after]],
             out_specs=[whole(shape) for shape in out_shapes],
             scratch_shapes=[
-                pltpu.VMEM((NEAR * rows, 2 * HS), dtype),
+                pltpu.VMEM((near_kv[2].shape[0] + 2 * rows, 2 * HS), dtype),
                 pltpu.VMEM((SPAN * BLK, LANES), dtype),
                 pltpu.VMEM((2 * slots, VMOST * BLK, 2 * HS), dtype),
                 pltpu.VMEM((far, LANES), dtype),
@@ -286,10 +291,38 @@
                 pltpu.SemaphoreType.DMA((NEAR + 2,)),
             ],
         ),
-        compiler_params=params(50),
+        compiler_params=params(40),
         cost_estimate=SHORT,
         name="attend",
     )(tp, ctx, queries, queries, table, *near_kv, *pairs, out_weight, *after)
+
+
+def project_staged_kernel(first, a_ref, w_ref, *refs):
+    tiles = len(refs) // 2
+    outs = refs[-2 * tiles :]
+    half, tile = outs[0].shape
+    for t in range(tiles):
+        weight = w_ref[:, first + t * tile : first + (t + 1) * tile]
+        product = jnp.dot(a_ref[...], weight, preferred_element_type=jnp.float32)
+        product = product.astype(a_ref.dtype)
+        outs[t][...] = product[:half]
+        outs[tiles + t][...] = product[half:]
+
+
+def project_staged(attended, weight, first, tiles, after):
+    rows, depth = attended.shape
+    tile = (weight.shape[1] - first) // tiles
+    part = jax.ShapeDtypeStruct((rows // 2, tile), attended.dtype)
+    outs = pl.pallas_call(
+        functools.partial(project_staged_kernel, first),
+        out_shape=[part] * (2 * tiles),
+        in_specs=[vmem(), vmem(), anywhere()],
+        out_specs=[vmem()] * (2 * tiles),
+        compiler_params=params(24),
+        cost_estimate=SHORT,
+        name="project",
+    )(attended, weight, after)
+    return outs[:tiles], outs[tiles:]
 
 
 def project_kernel(first, a_ref, w_hbm, *refs):
@@ -404,13 +437,13 @@
         return lax.ppermute(x, "ctx", [(r, r + by) for r in range(ctx_size - by)])
 
     half = ctx_size // 2
-    own, pair = pick(ctx, vertical, keys, values, half)
+    own, late, pair = pick(ctx, vertical, keys, values, half)
     parities = [list(range(odd, ctx_size, 2)) for odd in (0, 1)]
     pairs = [lax.all_to_all(pair, "ctx", 0, 0, axis_index_groups=parities, tiled=True)]
     needed = pairs[0][: half - 1]
     pairs.append(lax.ppermute(needed, "ctx", [(r, r ^ 1) for r in range(ctx_size)]))
     table, own_copy = tables(ctx, vertical, slash, own, half - 1)
-    near_kv = [own_copy, shifted(own, 1), shifted(own, 2)]
+    near_kv = [own_copy, shifted(own, 1), shifted(late, 2)]
 
     def sibling(x):
         return lax.ppermute(x, "tp", [(j, j ^ 1) for j in range(4)])
@@ -433,7 +466,7 @@
     attended, send, keep = attention((((3, 0), (2, 0)),), HEAD, ())
     total = (keep.astype(jnp.float32) + sibling(send).astype(jnp.float32)).astype(keep.dtype)
     arrived = [across(total)]
-    total = exchanged(*project(attended, out_weight, HEAD * TILE, 4, (total,)))
+    total = exchanged(*project_staged(attended, out_weight, HEAD * TILE, 4, total))
     arrived.append(across(total))
     (attended,) = attention((((3, 1), (2, 1)),), 0, (total,))
     total = exchanged(*project(attended, out_weight, 0, 4, (arrived[0],)))

time: 85.2 us -> 80.7 us (0.947)
  Pallas kernels: 39.3 us -> 36.7 us
  waiting for transfers between devices: 21.8 us -> 19.9 us
    pallas_call x3 -> x2, Pallas kernels: 21 us -> 15.7 us  [project(): pl.pallas_call(functools.partial(project_kernel, first), out_shape=[part]...]
    ppermute x2, waiting for transfers between devices: 8.77 us -> 3.94 us  [shifted(): return lax.ppermute(x, 'ctx', [(r, r + by) for r in range(ctx_size - by)])]
    ppermute x1, waiting for transfers between devices: 0.01 us -> 3.42 us  [shards(): lax.ppermute(needed, 'ctx', [(r, r ^ 1) for r in range(ctx_size)])]
    pallas_call x0 -> x1, Pallas kernels: none -> 1.86 us  [project_staged(): pl.pallas_call(functools.partial(project_staged_kernel, first), out_shape...]
  transfers between devices with their start and end apart: 24 -> 24, of which waited for: 19 -> 20; matrix products, arithmetic and copies ran while one was open for 0% -> 0% of each run, Pallas kernels for 37% -> 36%
where the time goes in v16:
time: 80.7 us; the launch traced here: 80.3 us
  Pallas kernels  36.7 us (45%)
  starting transfers between devices  20.2 us (25%)
  waiting for transfers between devices  19.9 us (25%)
  local copies, waits for them, and re-layouts  3.14 us (4%)
    pallas_call x2, Pallas kernels, project(): pl.pallas_call(functools.partial(project_kernel, first), out_shape=[part]...  15.7 us
    pallas_call x3, Pallas kernels, attend(): pl.pallas_call(functools.partial(attend_kernel, slots, tiles, sizes, plac...  13.5 us
    ppermute x2, starting transfers between devices, shifted(): return lax.ppermute(x, 'ctx', [(r, r + by) for r in range(ctx_size - by)])  6.79 us
    ppermute x3, waiting for transfers between devices, across(): return lax.ppermute(x, 'tp', [(j, j ^ 2) for j in range(4)])  6.27 us
    ppermute x17, waiting for transfers between devices, sibling(): return lax.ppermute(x, 'tp', [(j, j ^ 1) for j in range(4)])  6.24 us
    all_to_all x1, starting transfers between devices, shards(): lax.all_to_all(pair, 'ctx', 0, 0, axis_index_groups=parities, tiled=True)  5.2 us
    ppermute x2, waiting for transfers between devices, shifted(): return lax.ppermute(x, 'ctx', [(r, r + by) for r in range(ctx_size - by)])  3.94 us
    ppermute x17, starting transfers between devices, sibling(): return lax.ppermute(x, 'tp', [(j, j ^ 1) for j in range(4)])  3.87 us
  transfers between devices with their start and end apart: 24, of which 20 were waited for; matrix products, arithmetic and copies ran while one was open for 0% of the time, Pallas kernels for 36%

profile of v16, /device:TPU:16, one launch (start us, length us, event | category | flops | bytes accessed | tf_op | source)
XLA Modules:
  0.0 80.3 jit_solution(8195465380493597920)
XLA Ops:
  0.0 2.2 %pick.1 = (bf16[512,256]{1,0:T(8,128)(2,1)}, bf16[448,256]{1,0:T(8,128)(2,1)}, bf16[4,128,256]{2,1,0:T(8,128)(2,1)}) custom-call(s32[1]{0:T(128)} %bitcast.1.rank_ref.ctx_ref, s32[8,16]{1,0:T(8,128)} %vert_ref.3, bf16[512,128]{1,0:T(8,128)(2,1)} %k_ref.1, bf16[512,128]{1,0:T(8,128)(2,1)} %v_ref.1), custom_call_target="tpu_custom_call" | custom-call | tf_op jit(solution)/shard_map/pick/pallas_call | solution.py:65
  2.2 5.2 %all-to-all-start = ((bf16[4,128,256]{2,1,0:T(8,128)(2,1)}), bf16[4,128,256]{2,1,0:T(8,128)(2,1)S(1)}, u32[]{:S(2)}, u32[]{:S(2)}) async-start(bf16[4,128,256]{2,1,0:T(8,128)(2,1)} %get-tuple-element.49), calls=%async_computation | async-start | bytes 524288 | tf_op jit(solution)/shard_map/all_to_all | solution.py:442
  7.4 3.4 %collective-permute-start = (bf16[512,256]{1,0:T(8,128)(2,1)}, bf16[512,256]{1,0:T(8,128)(2,1)S(1)}, u32[]{:S(2)}, u32[]{:S(2)}) collective-permute-start(bf16[512,256]{1,0:T(8,128)(2,1)} %get-tuple-element.45.own_ref), channel_id=1, source_target_pairs={{0,4},{4,8},{8,12},{12,16},{16,20},{20,24},{24,28},{1,5},{5,9},{9,... | collective-permute-start | bytes 786440 | tf_op jit(solution)/shard_map/ppermute | solution.py:437
  10.8 3.4 %collective-permute-start.1 = (bf16[448,256]{1,0:T(8,128)(2,1)}, bf16[448,256]{1,0:T(8,128)(2,1)S(1)}, u32[]{:S(2)}, u32[]{:S(2)}) collective-permute-start(bf16[448,256]{1,0:T(8,128)(2,1)} %get-tuple-element.48), channel_id=1, source_target_pairs={{0,8},{4,12},{8,16},{12,20},{16,24},{20,28},{1,9},{5,13},{9,17},{1... | collective-permute-start | bytes 688136 | tf_op jit(solution)/shard_map/ppermute | solution.py:437
  14.2 0.6 collective-permute-start.2
  14.8 0.9 %copy-done.4 = bf16[512,256]{1,0:T(8,128)(2,1)S(1)} copy-done((bf16[512,256]{1,0:T(8,128)(2,1)S(1)}, bf16[512,256]{1,0:T(8,128)(2,1)}, u32[]{:S(2)}) %copy-start.4) | copy-done | bytes 262168
  15.8 0.7 copy-done.5
  16.5 0.7 copy-done.6
  17.3 2.1 %collective-permute-done.1.kv_2 = bf16[448,256]{1,0:T(8,128)(2,1)S(1)} collective-permute-done((bf16[448,256]{1,0:T(8,128)(2,1)}, bf16[448,256]{1,0:T(8,128)(2,1)S(1)}, u32[]{:S(2)}, u32[]{:S(2)}) %collective-permute-start.1) | collective-permute-done | bytes 229408 | tf_op jit(solution)/shard_map/ppermute | solution.py:437
  19.4 1.8 %collective-permute-done.kv_1 = bf16[512,256]{1,0:T(8,128)(2,1)S(1)} collective-permute-done((bf16[512,256]{1,0:T(8,128)(2,1)}, bf16[512,256]{1,0:T(8,128)(2,1)S(1)}, u32[]{:S(2)}, u32[]{:S(2)}) %collective-permute-start) | collective-permute-done | bytes 262176 | tf_op jit(solution)/shard_map/ppermute | solution.py:437
  21.3 3.4 %collective-permute-done.2.refs_1_ = bf16[3,128,256]{2,1,0:T(8,128)(2,1)S(1)} collective-permute-done((bf16[3,128,256]{2,1,0:T(8,128)(2,1)S(1)}, bf16[3,128,256]{2,1,0:T(8,128)(2,1)S(1)}, u32[]{:S(2)}, u32[]{:S(2)}) %collective-permute-start.2) | collective-permute-done | bytes 196640 | tf_op jit(solution)/shard_map/ppermute | solution.py:444
  24.7 4.5 %attend.3 = (bf16[128,1024]{1,0:T(8,128)(2,1)S(1)}, bf16[64,2048]{1,0:T(8,128)(2,1)S(1)}, bf16[64,2048]{1,0:T(8,128)(2,1)S(1)}) custom-call(s32[1]{0:T(128)} %bitcast.tp_ref, s32[1]{0:T(128)} %bitcast.1.rank_ref.ctx_ref, bf16[512,1024]{1,0:T(8,128)(2,1)S(1)} %copy-done.1, bf16[512,1024]{1,0:T(8,128)(2,1)S(1)} %copy-done.1, ...), custom_call_target="tpu_custom_call" | custom-call | tf_op jit(solution)/shard_map/attend/pallas_call | solution.py:270
  29.3 1.5 %collective-permute-done.3 = bf16[64,2048]{1,0:T(8,128)(2,1)S(1)} collective-permute-done((bf16[64,2048]{1,0:T(8,128)(2,1)S(1)}, bf16[64,2048]{1,0:T(8,128)(2,1)S(1)}, u32[]{:S(2)}, u32[]{:S(2)}) %collective-permute-start.3) | collective-permute-done | bytes 262176 | tf_op jit(solution)/shard_map/ppermute | solution.py:449
  30.8 1.6 %collective-permute-start.8 = (bf16[64,2048]{1,0:T(8,128)(2,1)S(1)}, bf16[64,2048]{1,0:T(8,128)(2,1)S(1)}, u32[]{:S(2)}, u32[]{:S(2)}) collective-permute-start(bf16[64,2048]{1,0:T(8,128)(2,1)S(1)} %add_convert_fusion.refs_0_), channel_id=1, source_target_pairs={{0,2},{1,3},{2,0},{3,1},{4,6},{5,7},{6,4},{7,5},{8,10},{9,11},{10,... | collective-permute-start | bytes 786440 | tf_op jit(solution)/shard_map/ppermute | solution.py:452
  32.4 1.9 %project.3 = (bf16[64,1536]{1,0:T(8,128)(2,1)S(1)}, bf16[64,1536]{1,0:T(8,128)(2,1)S(1)}, bf16[64,1536]{1,0:T(8,128)(2,1)S(1)}, bf16[64,1536]{1,0:T(8,128)(2,1)S...) custom-call(bf16[128,1024]{1,0:T(8,128)(2,1)S(1)} %get-tuple-element, ...), custom_call_target="tpu_custom_call" | custom-call | tf_op jit(solution)/shard_map/project/pallas_call | solution.py:316
  34.4 0.5 collective-permute-start.5
  34.9 0.4 collective-permute-start.7
  35.4 0.4 collective-permute-done.4.refs_4_
  35.8 0.3 collective-permute-done.5.refs_5_
  36.1 0.3 collective-permute-done.6.refs_6_
  36.4 0.3 collective-permute-done.7.refs_7_
  36.8 0.9 %collective-permute-start.13 = (bf16[64,6144]{1,0:T(8,128)(2,1)S(1)}, bf16[64,6144]{1,0:T(8,128)(2,1)S(1)}, u32[]{:S(2)}, u32[]{:S(2)}) collective-permute-start(bf16[64,6144]{1,0:T(8,128)(2,1)S(1)} %add.7.refs_3_), channel_id=1, source_target_pairs={{0,2},{1,3},{2,0},{3,1},{4,6},{5,7},{6,4},{7,5},{8,10},{9,11},{10,... | collective-permute-start | bytes 2359304 | tf_op jit(solution)/shard_map/ppermute | solution.py:452
  37.7 3.3 %attend.4.a_ref = bf16[128,1024]{1,0:T(8,128)(2,1)S(1)} custom-call(s32[1]{0:T(128)} %bitcast.tp_ref, s32[1]{0:T(128)} %bitcast.1.rank_ref.ctx_ref, bf16[512,1024]{1,0:T(8,128)(2,1)S(1)} %copy-done.1, bf16[512,1024]{1,0:T(8,128)(2,1)S(1)} %copy-done.1, s32[3,8,128]{2,1,0:T(8,128)S(1)} %get-tuple-element.46.table_ref, ...), custom_call_target="tpu_custom_call" | custom-call | tf_op jit(solution)/shard_map/attend/pallas_call | solution.py:270
  41.0 6.6 %project.4 = (bf16[64,2048]{1,0:T(8,128)(2,1)S(1)}, bf16[64,2048]{1,0:T(8,128)(2,1)S(1)}, bf16[64,2048]{1,0:T(8,128)(2,1)S(1)}, bf16[64,2048]{1,0:T(8,128)(2,1)S...) custom-call(bf16[128,1024]{1,0:T(8,128)(2,1)S(1)} %attend.4.a_ref, ...), custom_call_target="tpu_custom_call" | custom-call | tf_op jit(solution)/shard_map/project/pallas_call | solution.py:353
  47.8 0.5 collective-permute-start.10
  48.3 0.4 collective-permute-start.12
  48.8 0.5 collective-permute-done.9.refs_4_
  49.3 0.4 collective-permute-done.10.refs_5_
  49.7 0.4 collective-permute-done.11.refs_6_
  50.0 0.4 collective-permute-done.12.refs_7_
  50.4 0.2 add.8.refs_3_
  50.7 1.3 %collective-permute-start.22 = (bf16[64,8192]{1,0:T(8,128)(2,1)S(1)}, bf16[64,8192]{1,0:T(8,128)(2,1)S(1)}, u32[]{:S(2)}, u32[]{:S(2)}) collective-permute-start(bf16[64,8192]{1,0:T(8,128)(2,1)S(1)} %add.8.refs_3_), channel_id=1, source_target_pairs={{0,2},{1,3},{2,0},{3,1},{4,6},{5,7},{6,4},{7,5},{8,10},{9,11},{10,... | collective-permute-start | bytes 3145736 | tf_op jit(solution)/shard_map/ppermute | solution.py:452
  52.0 5.3 %collective-permute-done.13.refs_4_.refs_12_ = bf16[64,6144]{1,0:T(8,128)(2,1)S(1)} collective-permute-done((bf16[64,6144]{1,0:T(8,128)(2,1)S(1)}, bf16[64,6144]{1,0:T(8,128)(2,1)S(1)}, u32[]{:S(2)}, u32[]{:S(2)}) %collective-permute-start.13) | collective-permute-done | bytes 786464 | tf_op jit(solution)/shard_map/ppermute | solution.py:452
  57.3 5.7 %attend.5.a_ref = bf16[256,1024]{1,0:T(8,128)(2,1)S(1)} custom-call(s32[1]{0:T(128)} %bitcast.tp_ref, s32[1]{0:T(128)} %bitcast.1.rank_ref.ctx_ref, bf16[512,1024]{1,0:T(8,128)(2,1)S(1)} %copy-done.1, bf16[512,1024]{1,0:T(8,128)(2,1)S(1)} %copy-done.1, s32[3,8,128]{2,1,0:T(8,128)S(1)} %get-tuple-element.46.table_ref, ...), custom_call_target="tpu_custom_call" | custom-call | tf_op jit(solution)/shard_map/attend/pallas_call | solution.py:270
  62.9 0.8 copy-done.2
  63.7 9.1 %project.5 = (bf16[128,1024]{1,0:T(8,128)(2,1)S(1)}, bf16[128,1024]{1,0:T(8,128)(2,1)S(1)}, bf16[128,1024]{1,0:T(8,128)(2,1)S(1)}, bf16[128,1024]{1,0:T(8,128)(2...) custom-call(bf16[256,1024]{1,0:T(8,128)(2,1)} %copy-done.2, ...), custom_call_target="tpu_custom_call" | custom-call | tf_op jit(solution)/shard_map/project/pallas_call | solution.py:353
  72.9 0.5 collective-permute-start.15
  73.5 0.4 collective-permute-start.17
  73.9 0.5 collective-permute-done.14.refs_2_.refs_8_
  74.6 0.2 collective-permute-done.15.refs_3_.refs_9_
  74.9 0.2 collective-permute-done.16.refs_6_.refs_10_
  75.3 0.2 collective-permute-done.17.refs_7_.refs_11_
  75.7 0.8 finish.3.refs_13_
  76.5 0.2 collective-permute-done.20.refs_10_.refs_14_
  76.7 0.4 collective-permute-done.21.refs_11_.refs_15_
  77.1 1.0 %finish.4.refs_17_ = bf16[128,8192]{1,0:T(8,128)(2,1)} custom-call(bf16[128,1024]{1,0:T(8,128)(2,1)S(1)} %get-tuple-element.71.refs_0_.refs_2_, bf16[128,1024]{1,0:T(8,128)(2,1)S(1)} %get-tuple-element.72.refs_1_.refs_3_, bf16[128,1024]{1,0:T(8,128)(2,1)S(1)} %get-tuple-element.73.refs_2_.refs_4_, ...), custom_call_target="tpu_custom_call", output_to_operand_aliasing={{}: (13, {})} | custom-call | tf_op jit(solution)/shard_map/finish/pallas_call | solution.py:414
  78.1 0.9 %collective-permute-done.22.refs_16_ = bf16[64,8192]{1,0:T(8,128)(2,1)S(1)} collective-permute-done((bf16[64,8192]{1,0:T(8,128)(2,1)S(1)}, bf16[64,8192]{1,0:T(8,128)(2,1)S(1)}, u32[]{:S(2)}, u32[]{:S(2)}) %collective-permute-start.22) | collective-permute-done | bytes 1048608 | tf_op jit(solution)/shard_map/ppermute | solution.py:452
  79.0 1.1 %finish.5 = bf16[128,8192]{1,0:T(8,128)(2,1)} custom-call(bf16[128,1024]{1,0:T(8,128)(2,1)S(1)} %get-tuple-element.69.refs_0_, bf16[128,1024]{1,0:T(8,128)(2,1)S(1)} %get-tuple-element.70.refs_1_, bf16[128,1024]{1,0:T(8,128)(2,1)S(1)} %get-tuple-element.71.refs_0_.refs_2_, ...), custom_call_target="tpu_custom_call", output_to_operand_aliasing={{}: (17, {})} | custom-call | tf_op jit(solution)/shard_map/finish/pallas_call | solution.py:414
  (29 shorter events, 1.5 us)
Async XLA Ops:
  0.0 24.7 %copy-start.1 = (bf16[512,1024]{1,0:T(8,128)(2,1)S(1)}, bf16[512,1024]{1,0:T(8,128)(2,1)}, u32[]{:S(2)}) copy-start(bf16[512,1024]{1,0:T(8,128)(2,1)} %q_1.5) | copy-start | bytes 3145732
  2.2 12.0 %all-to-all-start = ((bf16[4,128,256]{2,1,0:T(8,128)(2,1)}), bf16[4,128,256]{2,1,0:T(8,128)(2,1)S(1)}, u32[]{:S(2)}, u32[]{:S(2)}) async-start(bf16[4,128,256]{2,1,0:T(8,128)(2,1)} %get-tuple-element.49), calls=%async_computation | async-start | bytes 524288 | tf_op jit(solution)/shard_map/all_to_all | solution.py:442
  7.4 13.9 %collective-permute-start = (bf16[512,256]{1,0:T(8,128)(2,1)}, bf16[512,256]{1,0:T(8,128)(2,1)S(1)}, u32[]{:S(2)}, u32[]{:S(2)}) collective-permute-start(bf16[512,256]{1,0:T(8,128)(2,1)} %get-tuple-element.45.own_ref), channel_id=1, source_target_pairs={{0,4},{4,8},{8,12},{12,16},{16,20},{20,24},{24,28},{1,5},{5,9},{9,... | collective-permute-start | bytes 786440 | tf_op jit(solution)/shard_map/ppermute | solution.py:437
  10.8 8.6 %collective-permute-start.1 = (bf16[448,256]{1,0:T(8,128)(2,1)}, bf16[448,256]{1,0:T(8,128)(2,1)S(1)}, u32[]{:S(2)}, u32[]{:S(2)}) collective-permute-start(bf16[448,256]{1,0:T(8,128)(2,1)} %get-tuple-element.48), channel_id=1, source_target_pairs={{0,8},{4,12},{8,16},{12,20},{16,24},{20,28},{1,9},{5,13},{9,17},{1... | collective-permute-start | bytes 688136 | tf_op jit(solution)/shard_map/ppermute | solution.py:437
  14.2 10.5 %collective-permute-start.2 = (bf16[3,128,256]{2,1,0:T(8,128)(2,1)S(1)}, bf16[3,128,256]{2,1,0:T(8,128)(2,1)S(1)}, u32[]{:S(2)}, u32[]{:S(2)}) collective-permute-start(bf16[3,128,256]{2,1,0:T(8,128)(2,1)S(1)} %slice.4), channel_id=1, source_target_pairs={{0,4},{4,0},{8,12},{12,8},{16,20},{20,16},{24,28},{28,24},{1,5},{5... | collective-permute-start | bytes 589832 | tf_op jit(solution)/shard_map/ppermute | solution.py:444
  14.8 0.9 %copy-start.4 = (bf16[512,256]{1,0:T(8,128)(2,1)S(1)}, bf16[512,256]{1,0:T(8,128)(2,1)}, u32[]{:S(2)}) copy-start(bf16[512,256]{1,0:T(8,128)(2,1)} %get-tuple-element.45.own_ref) | copy-start | bytes 786436
  15.8 0.7 copy-start.5
  16.5 0.7 copy-start.6
  24.7 7.7 %copy-start = (bf16[1024,8192]{1,0:T(8,128)(2,1)S(1)}, bf16[1024,8192]{1,0:T(8,128)(2,1)}, u32[]{:S(2)}) copy-start(bf16[1024,8192]{1,0:T(8,128)(2,1)} %w_hbm.3) | copy-start | bytes 50331652
  29.2 1.6 %collective-permute-start.3 = (bf16[64,2048]{1,0:T(8,128)(2,1)S(1)}, bf16[64,2048]{1,0:T(8,128)(2,1)S(1)}, u32[]{:S(2)}, u32[]{:S(2)}) collective-permute-start(bf16[64,2048]{1,0:T(8,128)(2,1)S(1)} %get-tuple-element.52), channel_id=1, source_target_pairs={{0,1},{1,0},{2,3},{3,2},{4,5},{5,4},{6,7},{7,6},{8,9},{9,8},{10,11... | collective-permute-start | bytes 786440 | tf_op jit(solution)/shard_map/ppermute | solution.py:449
  30.8 10.2 %collective-permute-start.8 = (bf16[64,2048]{1,0:T(8,128)(2,1)S(1)}, bf16[64,2048]{1,0:T(8,128)(2,1)S(1)}, u32[]{:S(2)}, u32[]{:S(2)}) collective-permute-start(bf16[64,2048]{1,0:T(8,128)(2,1)S(1)} %add_convert_fusion.refs_0_), channel_id=1, source_target_pairs={{0,2},{1,3},{2,0},{3,1},{4,6},{5,7},{6,4},{7,5},{8,10},{9,11},{10,... | collective-permute-start | bytes 786440 | tf_op jit(solution)/shard_map/ppermute | solution.py:452
  34.3 1.5 %collective-permute-start.4 = (bf16[64,1536]{1,0:T(8,128)(2,1)S(1)}, bf16[64,1536]{1,0:T(8,128)(2,1)S(1)}, u32[]{:S(2)}, u32[]{:S(2)}) collective-permute-start(bf16[64,1536]{1,0:T(8,128)(2,1)S(1)} %get-tuple-element.57), channel_id=1, source_target_pairs={{0,1},{1,0},{2,3},{3,2},{4,5},{5,4},{6,7},{7,6},{8,9},{9,8},{10,11... | collective-permute-start | bytes 589832 | tf_op jit(solution)/shard_map/ppermute | solution.py:449
  34.4 1.7 %collective-permute-start.5 = (bf16[64,1536]{1,0:T(8,128)(2,1)S(1)}, bf16[64,1536]{1,0:T(8,128)(2,1)S(1)}, u32[]{:S(2)}, u32[]{:S(2)}) collective-permute-start(bf16[64,1536]{1,0:T(8,128)(2,1)S(1)} %get-tuple-element.58), channel_id=1, source_target_pairs={{0,1},{1,0},{2,3},{3,2},{4,5},{5,4},{6,7},{7,6},{8,9},{9,8},{10,11... | collective-permute-start | bytes 589832 | tf_op jit(solution)/shard_map/ppermute | solution.py:449
  34.9 1.5 %collective-permute-start.6 = (bf16[64,1536]{1,0:T(8,128)(2,1)S(1)}, bf16[64,1536]{1,0:T(8,128)(2,1)S(1)}, u32[]{:S(2)}, u32[]{:S(2)}) collective-permute-start(bf16[64,1536]{1,0:T(8,128)(2,1)S(1)} %get-tuple-element.59), channel_id=1, source_target_pairs={{0,1},{1,0},{2,3},{3,2},{4,5},{5,4},{6,7},{7,6},{8,9},{9,8},{10,11... | collective-permute-start | bytes 589832 | tf_op jit(solution)/shard_map/ppermute | solution.py:449
  34.9 1.7 %collective-permute-start.7 = (bf16[64,1536]{1,0:T(8,128)(2,1)S(1)}, bf16[64,1536]{1,0:T(8,128)(2,1)S(1)}, u32[]{:S(2)}, u32[]{:S(2)}) collective-permute-start(bf16[64,1536]{1,0:T(8,128)(2,1)S(1)} %get-tuple-element.60), channel_id=1, source_target_pairs={{0,1},{1,0},{2,3},{3,2},{4,5},{5,4},{6,7},{7,6},{8,9},{9,8},{10,11... | collective-permute-start | bytes 589832 | tf_op jit(solution)/shard_map/ppermute | solution.py:449
  36.8 20.4 %collective-permute-start.13 = (bf16[64,6144]{1,0:T(8,128)(2,1)S(1)}, bf16[64,6144]{1,0:T(8,128)(2,1)S(1)}, u32[]{:S(2)}, u32[]{:S(2)}) collective-permute-start(bf16[64,6144]{1,0:T(8,128)(2,1)S(1)} %add.7.refs_3_), channel_id=1, source_target_pairs={{0,2},{1,3},{2,0},{3,1},{4,6},{5,7},{6,4},{7,5},{8,10},{9,11},{10,... | collective-permute-start | bytes 2359304 | tf_op jit(solution)/shard_map/ppermute | solution.py:452
  47.7 1.6 %collective-permute-start.9 = (bf16[64,2048]{1,0:T(8,128)(2,1)S(1)}, bf16[64,2048]{1,0:T(8,128)(2,1)S(1)}, u32[]{:S(2)}, u32[]{:S(2)}) collective-permute-start(bf16[64,2048]{1,0:T(8,128)(2,1)S(1)} %get-tuple-element.65), channel_id=1, source_target_pairs={{0,1},{1,0},{2,3},{3,2},{4,5},{5,4},{6,7},{7,6},{8,9},{9,8},{10,11... | collective-permute-start | bytes 786440 | tf_op jit(solution)/shard_map/ppermute | solution.py:449
  47.8 1.9 %collective-permute-start.10 = (bf16[64,2048]{1,0:T(8,128)(2,1)S(1)}, bf16[64,2048]{1,0:T(8,128)(2,1)S(1)}, u32[]{:S(2)}, u32[]{:S(2)}) collective-permute-start(bf16[64,2048]{1,0:T(8,128)(2,1)S(1)} %get-tuple-element.66), channel_id=1, source_target_pairs={{0,1},{1,0},{2,3},{3,2},{4,5},{5,4},{6,7},{7,6},{8,9},{9,8},{10,11... | collective-permute-start | bytes 786440 | tf_op jit(solution)/shard_map/ppermute | solution.py:449
  48.3 1.8 %collective-permute-start.11 = (bf16[64,2048]{1,0:T(8,128)(2,1)S(1)}, bf16[64,2048]{1,0:T(8,128)(2,1)S(1)}, u32[]{:S(2)}, u32[]{:S(2)}) collective-permute-start(bf16[64,2048]{1,0:T(8,128)(2,1)S(1)} %get-tuple-element.67), channel_id=1, source_target_pairs={{0,1},{1,0},{2,3},{3,2},{4,5},{5,4},{6,7},{7,6},{8,9},{9,8},{10,11... | collective-permute-start | bytes 786440 | tf_op jit(solution)/shard_map/ppermute | solution.py:449
  48.3 2.1 %collective-permute-start.12 = (bf16[64,2048]{1,0:T(8,128)(2,1)S(1)}, bf16[64,2048]{1,0:T(8,128)(2,1)S(1)}, u32[]{:S(2)}, u32[]{:S(2)}) collective-permute-start(bf16[64,2048]{1,0:T(8,128)(2,1)S(1)} %get-tuple-element.68), channel_id=1, source_target_pairs={{0,1},{1,0},{2,3},{3,2},{4,5},{5,4},{6,7},{7,6},{8,9},{9,8},{10,11... | collective-permute-start | bytes 786440 | tf_op jit(solution)/shard_map/ppermute | solution.py:449
  50.7 28.4 %collective-permute-start.22 = (bf16[64,8192]{1,0:T(8,128)(2,1)S(1)}, bf16[64,8192]{1,0:T(8,128)(2,1)S(1)}, u32[]{:S(2)}, u32[]{:S(2)}) collective-permute-start(bf16[64,8192]{1,0:T(8,128)(2,1)S(1)} %add.8.refs_3_), channel_id=1, source_target_pairs={{0,2},{1,3},{2,0},{3,1},{4,6},{5,7},{6,4},{7,5},{8,10},{9,11},{10,... | collective-permute-start | bytes 3145736 | tf_op jit(solution)/shard_map/ppermute | solution.py:452
  62.9 0.8 copy-start.2
  72.8 4.3 %copy-start.3 = (bf16[128,1024]{1,0:T(8,128)(2,1)S(1)}, bf16[128,1024]{1,0:T(8,128)(2,1)}, u32[]{:S(2)}) copy-start(bf16[128,1024]{1,0:T(8,128)(2,1)} %get-tuple-element.76.refs_5_.refs_7_) | copy-start | bytes 786436
  72.8 1.6 %collective-permute-start.14 = (bf16[128,1024]{1,0:T(8,128)(2,1)S(1)}, bf16[128,1024]{1,0:T(8,128)(2,1)S(1)}, u32[]{:S(2)}, u32[]{:S(2)}) collective-permute-start(bf16[128,1024]{1,0:T(8,128)(2,1)S(1)} %get-tuple-element.77), channel_id=1, source_target_pairs={{0,1},{1,0},{2,3},{3,2},{4,5},{5,4},{6,7},{7,6},{8,9},{9,8},{10,11... | collective-permute-start | bytes 786440 | tf_op jit(solution)/shard_map/ppermute | solution.py:449
  72.9 1.9 %collective-permute-start.15 = (bf16[128,1024]{1,0:T(8,128)(2,1)S(1)}, bf16[128,1024]{1,0:T(8,128)(2,1)S(1)}, u32[]{:S(2)}, u32[]{:S(2)}) collective-permute-start(bf16[128,1024]{1,0:T(8,128)(2,1)S(1)} %get-tuple-element.78), channel_id=1, source_target_pairs={{0,1},{1,0},{2,3},{3,2},{4,5},{5,4},{6,7},{7,6},{8,9},{9,8},{10,11... | collective-permute-start | bytes 786440 | tf_op jit(solution)/shard_map/ppermute | solution.py:449
  73.4 1.8 %collective-permute-start.16 = (bf16[128,1024]{1,0:T(8,128)(2,1)S(1)}, bf16[128,1024]{1,0:T(8,128)(2,1)S(1)}, u32[]{:S(2)}, u32[]{:S(2)}) collective-permute-start(bf16[128,1024]{1,0:T(8,128)(2,1)S(1)} %get-tuple-element.79), channel_id=1, source_target_pairs={{0,1},{1,0},{2,3},{3,2},{4,5},{5,4},{6,7},{7,6},{8,9},{9,8},{10,11... | collective-permute-start | bytes 786440 | tf_op jit(solution)/shard_map/ppermute | solution.py:449
  73.5 2.1 %collective-permute-start.17 = (bf16[128,1024]{1,0:T(8,128)(2,1)S(1)}, bf16[128,1024]{1,0:T(8,128)(2,1)S(1)}, u32[]{:S(2)}, u32[]{:S(2)}) collective-permute-start(bf16[128,1024]{1,0:T(8,128)(2,1)S(1)} %get-tuple-element.80), channel_id=1, source_target_pairs={{0,1},{1,0},{2,3},{3,2},{4,5},{5,4},{6,7},{7,6},{8,9},{9,8},{10,11... | collective-permute-start | bytes 786440 | tf_op jit(solution)/shard_map/ppermute | solution.py:449
  74.4 2.1 %collective-permute-start.18 = (bf16[128,1024]{1,0:T(8,128)(2,1)S(1)}, bf16[128,1024]{1,0:T(8,128)(2,1)S(1)}, u32[]{:S(2)}, u32[]{:S(2)}) collective-permute-start(bf16[128,1024]{1,0:T(8,128)(2,1)S(1)} %get-tuple-element.81), channel_id=1, source_target_pairs={{0,1},{1,0},{2,3},{3,2},{4,5},{5,4},{6,7},{7,6},{8,9},{9,8},{10,11... | collective-permute-start | bytes 786440 | tf_op jit(solution)/shard_map/ppermute | solution.py:449
  74.8 1.7 %collective-permute-start.19 = (bf16[128,1024]{1,0:T(8,128)(2,1)S(1)}, bf16[128,1024]{1,0:T(8,128)(2,1)S(1)}, u32[]{:S(2)}, u32[]{:S(2)}) collective-permute-start(bf16[128,1024]{1,0:T(8,128)(2,1)S(1)} %get-tuple-element.82), channel_id=1, source_target_pairs={{0,1},{1,0},{2,3},{3,2},{4,5},{5,4},{6,7},{7,6},{8,9},{9,8},{10,11... | collective-permute-start | bytes 786440 | tf_op jit(solution)/shard_map/ppermute | solution.py:449
  75.2 1.5 %collective-permute-start.20 = (bf16[128,1024]{1,0:T(8,128)(2,1)S(1)}, bf16[128,1024]{1,0:T(8,128)(2,1)S(1)}, u32[]{:S(2)}, u32[]{:S(2)}) collective-permute-start(bf16[128,1024]{1,0:T(8,128)(2,1)S(1)} %get-tuple-element.83), channel_id=1, source_target_pairs={{0,1},{1,0},{2,3},{3,2},{4,5},{5,4},{6,7},{7,6},{8,9},{9,8},{10,11... | collective-permute-start | bytes 786440 | tf_op jit(solution)/shard_map/ppermute | solution.py:449
  75.6 1.5 %collective-permute-start.21 = (bf16[128,1024]{1,0:T(8,128)(2,1)S(1)}, bf16[128,1024]{1,0:T(8,128)(2,1)S(1)}, u32[]{:S(2)}, u32[]{:S(2)}) collective-permute-start(bf16[128,1024]{1,0:T(8,128)(2,1)S(1)} %get-tuple-element.84), channel_id=1, source_target_pairs={{0,1},{1,0},{2,3},{3,2},{4,5},{5,4},{6,7},{7,6},{8,9},{9,8},{10,11... | collective-permute-start | bytes 786440 | tf_op jit(solution)/shard_map/ppermute | solution.py:449

commit v17 on v16

--- a/solution.py
+++ b/solution.py
@@ -146,21 +146,25 @@
             w_hbm.at[:, pl.ds(t * TILE, TILE)], weight.at[t], arrival.at[t]
         )
 
-    @pl.when(step == 0)
-    def _():
+    def window_copies():
         reach = kv_2.shape[0]
         places = ((kv_2, 0), (kv_1, reach), (own, reach + rows))
-        copies = [
+        return [
             pltpu.make_async_copy(x, kv_win.at[pl.ds(at, x.shape[0]), :], landed.at[s])
             for s, (x, at) in enumerate(places)
         ]
-        copies += [
+
+    def pool_copies():
+        return [
             pltpu.make_async_copy(
                 x.at[pl.ds(0, slots)], kv_pool.at[pl.ds(p * slots, slots)], landed.at[NEAR + p]
             )
             for p, x in enumerate(pairs)
         ]
-        for copy in copies:
+
+    @pl.when(step == 0)
+    def _():
+        for copy in pool_copies() + window_copies():
             copy.start()
         for t in range(tiles):
             fetch(t).start()
@@ -171,7 +175,7 @@
         key = lax.broadcasted_iota(jnp.int32, e_pool.shape, 0)
         lane = lax.broadcasted_iota(jnp.int32, e_pool.shape, 1)
         e_pool[...] = jnp.where(key // BLK == lane, 1.0, 0.0).astype(dtype)
-        for copy in copies:
+        for copy in pool_copies():
             copy.wait()
 
     lane = lax.broadcasted_iota(jnp.int32, (heads, LANES), 1)
@@ -185,20 +189,36 @@
     def with_ones(values):
         return jnp.concatenate([values, jnp.ones((values.shape[0], LANES), dtype)], axis=1)
 
-    near, far_q, windows = [], [], []
+    queries, far_q = [], []
     for u, q_ref in enumerate((q_0, q_1)):
-        here = place(u, step, tp_ref)
         q = q_ref[...]
         q = jnp.concatenate([q[:, h * HS : (h + 1) * HS] for h in range(heads)], axis=0)
+        queries.append(q)
+        first = rank * local_blocks + place(u, step, tp_ref) - (SPAN - 1)
+        far_mask = jnp.where(pool_ok & (block < first), 0.0, MASKED).astype(jnp.float32)
+        far_mask = jnp.broadcast_to(far_mask[:, None, :], (heads, BLK, LANES))
+        far_mask = far_mask.reshape(heads * BLK, LANES).astype(dtype)
+        far_q.append(jnp.concatenate([q, far_mask], axis=1))
+    far = lax.dot_general(
+        jnp.concatenate(far_q, axis=0),
+        jnp.concatenate([kv_pool[:, :, :HS].reshape(far_rows, HS), e_pool[...]], axis=1),
+        contract,
+        preferred_element_type=jnp.float32,
+    )
+
+    @pl.when(step == 0)
+    def _():
+        for copy in window_copies():
+            copy.wait()
+
+    near, windows = [], []
+    for u, q in enumerate(queries):
+        here = place(u, step, tp_ref)
         first = rank * local_blocks + here - (SPAN - 1)
         seen = first + lane
         ok = (seen >= 0) & (offset_ok | member(vert, seen))
         mask = jnp.where(ok | (lane >= SPAN), 0.0, MASKED).astype(jnp.float32)
         mask = (mask[:, None, :] + above[None]).reshape(heads * BLK, LANES).astype(dtype)
-        far_mask = jnp.where(pool_ok & (block < first), 0.0, MASKED).astype(jnp.float32)
-        far_mask = jnp.broadcast_to(far_mask[:, None, :], (heads, BLK, LANES))
-        far_mask = far_mask.reshape(heads * BLK, LANES).astype(dtype)
-        far_q.append(jnp.concatenate([q, far_mask], axis=1))
         window = pl.ds(pl.multiple_of(here * BLK, BLK), SPAN * BLK)
         windows.append(window)
         keys = jnp.concatenate([kv_win[window, :HS], e_win[...]], axis=1)
@@ -210,12 +230,6 @@
                 preferred_element_type=jnp.float32,
             )
         )
-    far = lax.dot_general(
-        jnp.concatenate(far_q, axis=0),
-        jnp.concatenate([kv_pool[:, :, :HS].reshape(far_rows, HS), e_pool[...]], axis=1),
-        contract,
-        preferred_element_type=jnp.float32,
-    )
     far_values = with_ones(kv_pool[:, :, HS:].reshape(far_rows, HS))
     for u in range(2):
         far_u = far[u * heads * BLK : (u + 1) * heads * BLK]

time: 80.7 us -> 81.2 us (level)
  Pallas kernels: 36.7 us -> 38.2 us
  waiting for transfers between devices: 19.9 us -> 18.6 us
    pallas_call x3, Pallas kernels: 13.5 us -> 15 us  [attend(): pl.pallas_call(functools.partial(attend_kernel, slots, tiles, sizes, plac...]
    ppermute x3, waiting for transfers between devices: 6.27 us -> 4.95 us  [across(): return lax.ppermute(x, 'tp', [(j, j ^ 2) for j in range(4)])]
  transfers between devices with their start and end apart: 24 -> 24, of which waited for: 20 -> 20; matrix products, arithmetic and copies ran while one was open for 0% -> 0% of each run, Pallas kernels for 36% -> 38%
where the time goes in v17:
time: 81.2 us; the launch traced here: 80.5 us
  Pallas kernels  38.2 us (47%)
  starting transfers between devices  20.2 us (25%)
  waiting for transfers between devices  18.6 us (23%)
  local copies, waits for them, and re-layouts  3.14 us (4%)
    pallas_call x2, Pallas kernels, project(): pl.pallas_call(functools.partial(project_kernel, first), out_shape=[part]...  15.7 us
    pallas_call x3, Pallas kernels, attend(): pl.pallas_call(functools.partial(attend_kernel, slots, tiles, sizes, plac...  15 us
    ppermute x2, starting transfers between devices, shifted(): return lax.ppermute(x, 'ctx', [(r, r + by) for r in range(ctx_size - by)])  6.79 us
    ppermute x17, waiting for transfers between devices, sibling(): return lax.ppermute(x, 'tp', [(j, j ^ 1) for j in range(4)])  6.24 us
    all_to_all x1, starting transfers between devices, shards(): lax.all_to_all(pair, 'ctx', 0, 0, axis_index_groups=parities, tiled=True)  5.2 us
    ppermute x3, waiting for transfers between devices, across(): return lax.ppermute(x, 'tp', [(j, j ^ 2) for j in range(4)])  4.95 us
    ppermute x2, waiting for transfers between devices, shifted(): return lax.ppermute(x, 'ctx', [(r, r + by) for r in range(ctx_size - by)])  3.94 us
    ppermute x17, starting transfers between devices, sibling(): return lax.ppermute(x, 'tp', [(j, j ^ 1) for j in range(4)])  3.86 us
  transfers between devices with their start and end apart: 24, of which 20 were waited for; matrix products, arithmetic and copies ran while one was open for 0% of the time, Pallas kernels for 38%

profile of v17, /device:TPU:16, one launch (start us, length us, event | category | flops | bytes accessed | tf_op | source)
XLA Modules:
  0.0 80.5 jit_solution(7174064471648120224)
XLA Ops:
  0.0 2.2 %pick.1 = (bf16[512,256]{1,0:T(8,128)(2,1)}, bf16[448,256]{1,0:T(8,128)(2,1)}, bf16[4,128,256]{2,1,0:T(8,128)(2,1)}) custom-call(s32[1]{0:T(128)} %bitcast.1.rank_ref.ctx_ref, s32[8,16]{1,0:T(8,128)} %vert_ref.3, bf16[512,128]{1,0:T(8,128)(2,1)} %k_ref.1, bf16[512,128]{1,0:T(8,128)(2,1)} %v_ref.1), custom_call_target="tpu_custom_call" | custom-call | tf_op jit(solution)/shard_map/pick/pallas_call | solution.py:65
  2.2 5.2 %all-to-all-start = ((bf16[4,128,256]{2,1,0:T(8,128)(2,1)}), bf16[4,128,256]{2,1,0:T(8,128)(2,1)S(1)}, u32[]{:S(2)}, u32[]{:S(2)}) async-start(bf16[4,128,256]{2,1,0:T(8,128)(2,1)} %get-tuple-element.49), calls=%async_computation | async-start | bytes 524288 | tf_op jit(solution)/shard_map/all_to_all | solution.py:456
  7.4 3.4 %collective-permute-start = (bf16[512,256]{1,0:T(8,128)(2,1)}, bf16[512,256]{1,0:T(8,128)(2,1)S(1)}, u32[]{:S(2)}, u32[]{:S(2)}) collective-permute-start(bf16[512,256]{1,0:T(8,128)(2,1)} %get-tuple-element.45.own_ref), channel_id=1, source_target_pairs={{0,4},{4,8},{8,12},{12,16},{16,20},{20,24},{24,28},{1,5},{5,9},{9,... | collective-permute-start | bytes 786440 | tf_op jit(solution)/shard_map/ppermute | solution.py:451
  10.8 3.4 %collective-permute-start.1 = (bf16[448,256]{1,0:T(8,128)(2,1)}, bf16[448,256]{1,0:T(8,128)(2,1)S(1)}, u32[]{:S(2)}, u32[]{:S(2)}) collective-permute-start(bf16[448,256]{1,0:T(8,128)(2,1)} %get-tuple-element.48), channel_id=1, source_target_pairs={{0,8},{4,12},{8,16},{12,20},{16,24},{20,28},{1,9},{5,13},{9,17},{1... | collective-permute-start | bytes 688136 | tf_op jit(solution)/shard_map/ppermute | solution.py:451
  14.2 0.6 collective-permute-start.2
  14.8 0.9 %copy-done.4 = bf16[512,256]{1,0:T(8,128)(2,1)S(1)} copy-done((bf16[512,256]{1,0:T(8,128)(2,1)S(1)}, bf16[512,256]{1,0:T(8,128)(2,1)}, u32[]{:S(2)}) %copy-start.4) | copy-done | bytes 262168
  15.8 0.7 copy-done.5
  16.5 0.7 copy-done.6
  17.3 2.1 %collective-permute-done.1.kv_2 = bf16[448,256]{1,0:T(8,128)(2,1)S(1)} collective-permute-done((bf16[448,256]{1,0:T(8,128)(2,1)}, bf16[448,256]{1,0:T(8,128)(2,1)S(1)}, u32[]{:S(2)}, u32[]{:S(2)}) %collective-permute-start.1) | collective-permute-done | bytes 229408 | tf_op jit(solution)/shard_map/ppermute | solution.py:451
  19.4 1.8 %collective-permute-done.kv_1 = bf16[512,256]{1,0:T(8,128)(2,1)S(1)} collective-permute-done((bf16[512,256]{1,0:T(8,128)(2,1)}, bf16[512,256]{1,0:T(8,128)(2,1)S(1)}, u32[]{:S(2)}, u32[]{:S(2)}) %collective-permute-start) | collective-permute-done | bytes 262176 | tf_op jit(solution)/shard_map/ppermute | solution.py:451
  21.3 3.4 %collective-permute-done.2.refs_1_ = bf16[3,128,256]{2,1,0:T(8,128)(2,1)S(1)} collective-permute-done((bf16[3,128,256]{2,1,0:T(8,128)(2,1)S(1)}, bf16[3,128,256]{2,1,0:T(8,128)(2,1)S(1)}, u32[]{:S(2)}, u32[]{:S(2)}) %collective-permute-start.2) | collective-permute-done | bytes 196640 | tf_op jit(solution)/shard_map/ppermute | solution.py:458
  24.7 4.7 %attend.3 = (bf16[128,1024]{1,0:T(8,128)(2,1)S(1)}, bf16[64,2048]{1,0:T(8,128)(2,1)S(1)}, bf16[64,2048]{1,0:T(8,128)(2,1)S(1)}) custom-call(s32[1]{0:T(128)} %bitcast.tp_ref, s32[1]{0:T(128)} %bitcast.1.rank_ref.ctx_ref, bf16[512,1024]{1,0:T(8,128)(2,1)S(1)} %copy-done.1, bf16[512,1024]{1,0:T(8,128)(2,1)S(1)} %copy-done.1, ...), custom_call_target="tpu_custom_call" | custom-call | tf_op jit(solution)/shard_map/attend/pallas_call | solution.py:284
  29.5 1.5 %collective-permute-done.3 = bf16[64,2048]{1,0:T(8,128)(2,1)S(1)} collective-permute-done((bf16[64,2048]{1,0:T(8,128)(2,1)S(1)}, bf16[64,2048]{1,0:T(8,128)(2,1)S(1)}, u32[]{:S(2)}, u32[]{:S(2)}) %collective-permute-start.3) | collective-permute-done | bytes 262176 | tf_op jit(solution)/shard_map/ppermute | solution.py:463
  31.1 1.6 %collective-permute-start.8 = (bf16[64,2048]{1,0:T(8,128)(2,1)S(1)}, bf16[64,2048]{1,0:T(8,128)(2,1)S(1)}, u32[]{:S(2)}, u32[]{:S(2)}) collective-permute-start(bf16[64,2048]{1,0:T(8,128)(2,1)S(1)} %add_convert_fusion.refs_0_), channel_id=1, source_target_pairs={{0,2},{1,3},{2,0},{3,1},{4,6},{5,7},{6,4},{7,5},{8,10},{9,11},{10,... | collective-permute-start | bytes 786440 | tf_op jit(solution)/shard_map/ppermute | solution.py:466
  32.6 1.9 %project.3 = (bf16[64,1536]{1,0:T(8,128)(2,1)S(1)}, bf16[64,1536]{1,0:T(8,128)(2,1)S(1)}, bf16[64,1536]{1,0:T(8,128)(2,1)S(1)}, bf16[64,1536]{1,0:T(8,128)(2,1)S...) custom-call(bf16[128,1024]{1,0:T(8,128)(2,1)S(1)} %get-tuple-element, ...), custom_call_target="tpu_custom_call" | custom-call | tf_op jit(solution)/shard_map/project/pallas_call | solution.py:330
  34.6 0.5 collective-permute-start.5
  35.1 0.4 collective-permute-start.7
  35.6 0.4 collective-permute-done.4.refs_4_
  36.0 0.3 collective-permute-done.5.refs_5_
  36.3 0.3 collective-permute-done.6.refs_6_
  36.6 0.3 collective-permute-done.7.refs_7_
  36.8 0.2 add.7.refs_3_
  37.0 0.7 collective-permute-start.13
  37.7 3.8 %attend.4.a_ref = bf16[128,1024]{1,0:T(8,128)(2,1)S(1)} custom-call(s32[1]{0:T(128)} %bitcast.tp_ref, s32[1]{0:T(128)} %bitcast.1.rank_ref.ctx_ref, bf16[512,1024]{1,0:T(8,128)(2,1)S(1)} %copy-done.1, bf16[512,1024]{1,0:T(8,128)(2,1)S(1)} %copy-done.1, s32[3,8,128]{2,1,0:T(8,128)S(1)} %get-tuple-element.46.table_ref, ...), custom_call_target="tpu_custom_call" | custom-call | tf_op jit(solution)/shard_map/attend/pallas_call | solution.py:284
  41.5 6.6 %project.4 = (bf16[64,2048]{1,0:T(8,128)(2,1)S(1)}, bf16[64,2048]{1,0:T(8,128)(2,1)S(1)}, bf16[64,2048]{1,0:T(8,128)(2,1)S(1)}, bf16[64,2048]{1,0:T(8,128)(2,1)S...) custom-call(bf16[128,1024]{1,0:T(8,128)(2,1)S(1)} %attend.4.a_ref, ...), custom_call_target="tpu_custom_call" | custom-call | tf_op jit(solution)/shard_map/project/pallas_call | solution.py:367
  48.2 0.5 collective-permute-start.10
  48.8 0.4 collective-permute-start.12
  49.2 0.5 collective-permute-done.9.refs_4_
  49.7 0.4 collective-permute-done.10.refs_5_
  50.1 0.4 collective-permute-done.11.refs_6_
  50.5 0.4 collective-permute-done.12.refs_7_
  50.9 0.2 add.8.refs_3_
  51.1 1.5 %collective-permute-start.22 = (bf16[64,8192]{1,0:T(8,128)(2,1)S(1)}, bf16[64,8192]{1,0:T(8,128)(2,1)S(1)}, u32[]{:S(2)}, u32[]{:S(2)}) collective-permute-start(bf16[64,8192]{1,0:T(8,128)(2,1)S(1)} %add.8.refs_3_), channel_id=1, source_target_pairs={{0,2},{1,3},{2,0},{3,1},{4,6},{5,7},{6,4},{7,5},{8,10},{9,11},{10,... | collective-permute-start | bytes 3145736 | tf_op jit(solution)/shard_map/ppermute | solution.py:466
  52.6 4.9 %collective-permute-done.13.refs_4_.refs_12_ = bf16[64,6144]{1,0:T(8,128)(2,1)S(1)} collective-permute-done((bf16[64,6144]{1,0:T(8,128)(2,1)S(1)}, bf16[64,6144]{1,0:T(8,128)(2,1)S(1)}, u32[]{:S(2)}, u32[]{:S(2)}) %collective-permute-start.13) | collective-permute-done | bytes 786464 | tf_op jit(solution)/shard_map/ppermute | solution.py:466
  57.5 6.5 %attend.5.a_ref = bf16[256,1024]{1,0:T(8,128)(2,1)S(1)} custom-call(s32[1]{0:T(128)} %bitcast.tp_ref, s32[1]{0:T(128)} %bitcast.1.rank_ref.ctx_ref, bf16[512,1024]{1,0:T(8,128)(2,1)S(1)} %copy-done.1, bf16[512,1024]{1,0:T(8,128)(2,1)S(1)} %copy-done.1, s32[3,8,128]{2,1,0:T(8,128)S(1)} %get-tuple-element.46.table_ref, ...), custom_call_target="tpu_custom_call" | custom-call | tf_op jit(solution)/shard_map/attend/pallas_call | solution.py:284
  64.0 0.8 copy-done.2
  64.8 9.1 %project.5 = (bf16[128,1024]{1,0:T(8,128)(2,1)S(1)}, bf16[128,1024]{1,0:T(8,128)(2,1)S(1)}, bf16[128,1024]{1,0:T(8,128)(2,1)S(1)}, bf16[128,1024]{1,0:T(8,128)(2...) custom-call(bf16[256,1024]{1,0:T(8,128)(2,1)} %copy-done.2, ...), custom_call_target="tpu_custom_call" | custom-call | tf_op jit(solution)/shard_map/project/pallas_call | solution.py:367
  74.0 0.5 collective-permute-start.15
  74.6 0.4 collective-permute-start.17
  75.0 0.5 collective-permute-done.14.refs_2_.refs_8_
  75.7 0.2 collective-permute-done.15.refs_3_.refs_9_
  76.0 0.2 collective-permute-done.16.refs_6_.refs_10_
  76.4 0.2 collective-permute-done.17.refs_7_.refs_11_
  76.8 0.8 finish.3.refs_13_
  77.6 0.2 collective-permute-done.20.refs_10_.refs_14_
  77.8 0.4 collective-permute-done.21.refs_11_.refs_15_
  78.2 1.0 %finish.4.refs_17_ = bf16[128,8192]{1,0:T(8,128)(2,1)} custom-call(bf16[128,1024]{1,0:T(8,128)(2,1)S(1)} %get-tuple-element.71.refs_0_.refs_2_, bf16[128,1024]{1,0:T(8,128)(2,1)S(1)} %get-tuple-element.72.refs_1_.refs_3_, bf16[128,1024]{1,0:T(8,128)(2,1)S(1)} %get-tuple-element.73.refs_2_.refs_4_, ...), custom_call_target="tpu_custom_call", output_to_operand_aliasing={{}: (13, {})} | custom-call | tf_op jit(solution)/shard_map/finish/pallas_call | solution.py:428
  79.2 1.1 %finish.5 = bf16[128,8192]{1,0:T(8,128)(2,1)} custom-call(bf16[128,1024]{1,0:T(8,128)(2,1)S(1)} %get-tuple-element.69.refs_0_, bf16[128,1024]{1,0:T(8,128)(2,1)S(1)} %get-tuple-element.70.refs_1_, bf16[128,1024]{1,0:T(8,128)(2,1)S(1)} %get-tuple-element.71.refs_0_.refs_2_, ...), custom_call_target="tpu_custom_call", output_to_operand_aliasing={{}: (17, {})} | custom-call | tf_op jit(solution)/shard_map/finish/pallas_call | solution.py:428
  (29 shorter events, 1.4 us)
Async XLA Ops:
  0.0 24.7 %copy-start.1 = (bf16[512,1024]{1,0:T(8,128)(2,1)S(1)}, bf16[512,1024]{1,0:T(8,128)(2,1)}, u32[]{:S(2)}) copy-start(bf16[512,1024]{1,0:T(8,128)(2,1)} %q_1.5) | copy-start | bytes 3145732
  2.2 12.0 %all-to-all-start = ((bf16[4,128,256]{2,1,0:T(8,128)(2,1)}), bf16[4,128,256]{2,1,0:T(8,128)(2,1)S(1)}, u32[]{:S(2)}, u32[]{:S(2)}) async-start(bf16[4,128,256]{2,1,0:T(8,128)(2,1)} %get-tuple-element.49), calls=%async_computation | async-start | bytes 524288 | tf_op jit(solution)/shard_map/all_to_all | solution.py:456
  7.4 13.9 %collective-permute-start = (bf16[512,256]{1,0:T(8,128)(2,1)}, bf16[512,256]{1,0:T(8,128)(2,1)S(1)}, u32[]{:S(2)}, u32[]{:S(2)}) collective-permute-start(bf16[512,256]{1,0:T(8,128)(2,1)} %get-tuple-element.45.own_ref), channel_id=1, source_target_pairs={{0,4},{4,8},{8,12},{12,16},{16,20},{20,24},{24,28},{1,5},{5,9},{9,... | collective-permute-start | bytes 786440 | tf_op jit(solution)/shard_map/ppermute | solution.py:451
  10.8 8.6 %collective-permute-start.1 = (bf16[448,256]{1,0:T(8,128)(2,1)}, bf16[448,256]{1,0:T(8,128)(2,1)S(1)}, u32[]{:S(2)}, u32[]{:S(2)}) collective-permute-start(bf16[448,256]{1,0:T(8,128)(2,1)} %get-tuple-element.48), channel_id=1, source_target_pairs={{0,8},{4,12},{8,16},{12,20},{16,24},{20,28},{1,9},{5,13},{9,17},{1... | collective-permute-start | bytes 688136 | tf_op jit(solution)/shard_map/ppermute | solution.py:451
  14.2 10.5 %collective-permute-start.2 = (bf16[3,128,256]{2,1,0:T(8,128)(2,1)S(1)}, bf16[3,128,256]{2,1,0:T(8,128)(2,1)S(1)}, u32[]{:S(2)}, u32[]{:S(2)}) collective-permute-start(bf16[3,128,256]{2,1,0:T(8,128)(2,1)S(1)} %slice.4), channel_id=1, source_target_pairs={{0,4},{4,0},{8,12},{12,8},{16,20},{20,16},{24,28},{28,24},{1,5},{5... | collective-permute-start | bytes 589832 | tf_op jit(solution)/shard_map/ppermute | solution.py:458
  14.8 0.9 %copy-start.4 = (bf16[512,256]{1,0:T(8,128)(2,1)S(1)}, bf16[512,256]{1,0:T(8,128)(2,1)}, u32[]{:S(2)}) copy-start(bf16[512,256]{1,0:T(8,128)(2,1)} %get-tuple-element.45.own_ref) | copy-start | bytes 786436
  15.8 0.7 copy-start.5
  16.5 0.7 copy-start.6
  24.7 7.9 %copy-start = (bf16[1024,8192]{1,0:T(8,128)(2,1)S(1)}, bf16[1024,8192]{1,0:T(8,128)(2,1)}, u32[]{:S(2)}) copy-start(bf16[1024,8192]{1,0:T(8,128)(2,1)} %w_hbm.3) | copy-start | bytes 50331652
  29.4 1.6 %collective-permute-start.3 = (bf16[64,2048]{1,0:T(8,128)(2,1)S(1)}, bf16[64,2048]{1,0:T(8,128)(2,1)S(1)}, u32[]{:S(2)}, u32[]{:S(2)}) collective-permute-start(bf16[64,2048]{1,0:T(8,128)(2,1)S(1)} %get-tuple-element.52), channel_id=1, source_target_pairs={{0,1},{1,0},{2,3},{3,2},{4,5},{5,4},{6,7},{7,6},{8,9},{9,8},{10,11... | collective-permute-start | bytes 786440 | tf_op jit(solution)/shard_map/ppermute | solution.py:463
  31.1 10.4 %collective-permute-start.8 = (bf16[64,2048]{1,0:T(8,128)(2,1)S(1)}, bf16[64,2048]{1,0:T(8,128)(2,1)S(1)}, u32[]{:S(2)}, u32[]{:S(2)}) collective-permute-start(bf16[64,2048]{1,0:T(8,128)(2,1)S(1)} %add_convert_fusion.refs_0_), channel_id=1, source_target_pairs={{0,2},{1,3},{2,0},{3,1},{4,6},{5,7},{6,4},{7,5},{8,10},{9,11},{10,... | collective-permute-start | bytes 786440 | tf_op jit(solution)/shard_map/ppermute | solution.py:466
  34.5 1.5 %collective-permute-start.4 = (bf16[64,1536]{1,0:T(8,128)(2,1)S(1)}, bf16[64,1536]{1,0:T(8,128)(2,1)S(1)}, u32[]{:S(2)}, u32[]{:S(2)}) collective-permute-start(bf16[64,1536]{1,0:T(8,128)(2,1)S(1)} %get-tuple-element.57), channel_id=1, source_target_pairs={{0,1},{1,0},{2,3},{3,2},{4,5},{5,4},{6,7},{7,6},{8,9},{9,8},{10,11... | collective-permute-start | bytes 589832 | tf_op jit(solution)/shard_map/ppermute | solution.py:463
  34.6 1.7 %collective-permute-start.5 = (bf16[64,1536]{1,0:T(8,128)(2,1)S(1)}, bf16[64,1536]{1,0:T(8,128)(2,1)S(1)}, u32[]{:S(2)}, u32[]{:S(2)}) collective-permute-start(bf16[64,1536]{1,0:T(8,128)(2,1)S(1)} %get-tuple-element.58), channel_id=1, source_target_pairs={{0,1},{1,0},{2,3},{3,2},{4,5},{5,4},{6,7},{7,6},{8,9},{9,8},{10,11... | collective-permute-start | bytes 589832 | tf_op jit(solution)/shard_map/ppermute | solution.py:463
  35.1 1.5 %collective-permute-start.6 = (bf16[64,1536]{1,0:T(8,128)(2,1)S(1)}, bf16[64,1536]{1,0:T(8,128)(2,1)S(1)}, u32[]{:S(2)}, u32[]{:S(2)}) collective-permute-start(bf16[64,1536]{1,0:T(8,128)(2,1)S(1)} %get-tuple-element.59), channel_id=1, source_target_pairs={{0,1},{1,0},{2,3},{3,2},{4,5},{5,4},{6,7},{7,6},{8,9},{9,8},{10,11... | collective-permute-start | bytes 589832 | tf_op jit(solution)/shard_map/ppermute | solution.py:463
  35.1 1.7 %collective-permute-start.7 = (bf16[64,1536]{1,0:T(8,128)(2,1)S(1)}, bf16[64,1536]{1,0:T(8,128)(2,1)S(1)}, u32[]{:S(2)}, u32[]{:S(2)}) collective-permute-start(bf16[64,1536]{1,0:T(8,128)(2,1)S(1)} %get-tuple-element.60), channel_id=1, source_target_pairs={{0,1},{1,0},{2,3},{3,2},{4,5},{5,4},{6,7},{7,6},{8,9},{9,8},{10,11... | collective-permute-start | bytes 589832 | tf_op jit(solution)/shard_map/ppermute | solution.py:463
  37.0 20.4 %collective-permute-start.13 = (bf16[64,6144]{1,0:T(8,128)(2,1)S(1)}, bf16[64,6144]{1,0:T(8,128)(2,1)S(1)}, u32[]{:S(2)}, u32[]{:S(2)}) collective-permute-start(bf16[64,6144]{1,0:T(8,128)(2,1)S(1)} %add.7.refs_3_), channel_id=1, source_target_pairs={{0,2},{1,3},{2,0},{3,1},{4,6},{5,7},{6,4},{7,5},{8,10},{9,11},{10,... | collective-permute-start | bytes 2359304 | tf_op jit(solution)/shard_map/ppermute | solution.py:466
  48.1 1.6 %collective-permute-start.9 = (bf16[64,2048]{1,0:T(8,128)(2,1)S(1)}, bf16[64,2048]{1,0:T(8,128)(2,1)S(1)}, u32[]{:S(2)}, u32[]{:S(2)}) collective-permute-start(bf16[64,2048]{1,0:T(8,128)(2,1)S(1)} %get-tuple-element.65), channel_id=1, source_target_pairs={{0,1},{1,0},{2,3},{3,2},{4,5},{5,4},{6,7},{7,6},{8,9},{9,8},{10,11... | collective-permute-start | bytes 786440 | tf_op jit(solution)/shard_map/ppermute | solution.py:463
  48.2 1.9 %collective-permute-start.10 = (bf16[64,2048]{1,0:T(8,128)(2,1)S(1)}, bf16[64,2048]{1,0:T(8,128)(2,1)S(1)}, u32[]{:S(2)}, u32[]{:S(2)}) collective-permute-start(bf16[64,2048]{1,0:T(8,128)(2,1)S(1)} %get-tuple-element.66), channel_id=1, source_target_pairs={{0,1},{1,0},{2,3},{3,2},{4,5},{5,4},{6,7},{7,6},{8,9},{9,8},{10,11... | collective-permute-start | bytes 786440 | tf_op jit(solution)/shard_map/ppermute | solution.py:463
  48.7 1.8 %collective-permute-start.11 = (bf16[64,2048]{1,0:T(8,128)(2,1)S(1)}, bf16[64,2048]{1,0:T(8,128)(2,1)S(1)}, u32[]{:S(2)}, u32[]{:S(2)}) collective-permute-start(bf16[64,2048]{1,0:T(8,128)(2,1)S(1)} %get-tuple-element.67), channel_id=1, source_target_pairs={{0,1},{1,0},{2,3},{3,2},{4,5},{5,4},{6,7},{7,6},{8,9},{9,8},{10,11... | collective-permute-start | bytes 786440 | tf_op jit(solution)/shard_map/ppermute | solution.py:463
  48.8 2.1 %collective-permute-start.12 = (bf16[64,2048]{1,0:T(8,128)(2,1)S(1)}, bf16[64,2048]{1,0:T(8,128)(2,1)S(1)}, u32[]{:S(2)}, u32[]{:S(2)}) collective-permute-start(bf16[64,2048]{1,0:T(8,128)(2,1)S(1)} %get-tuple-element.68), channel_id=1, source_target_pairs={{0,1},{1,0},{2,3},{3,2},{4,5},{5,4},{6,7},{7,6},{8,9},{9,8},{10,11... | collective-permute-start | bytes 786440 | tf_op jit(solution)/shard_map/ppermute | solution.py:463
  51.1 28.1 %collective-permute-start.22 = (bf16[64,8192]{1,0:T(8,128)(2,1)S(1)}, bf16[64,8192]{1,0:T(8,128)(2,1)S(1)}, u32[]{:S(2)}, u32[]{:S(2)}) collective-permute-start(bf16[64,8192]{1,0:T(8,128)(2,1)S(1)} %add.8.refs_3_), channel_id=1, source_target_pairs={{0,2},{1,3},{2,0},{3,1},{4,6},{5,7},{6,4},{7,5},{8,10},{9,11},{10,... | collective-permute-start | bytes 3145736 | tf_op jit(solution)/shard_map/ppermute | solution.py:466
  64.0 0.8 copy-start.2
  73.9 4.3 %copy-start.3 = (bf16[128,1024]{1,0:T(8,128)(2,1)S(1)}, bf16[128,1024]{1,0:T(8,128)(2,1)}, u32[]{:S(2)}) copy-start(bf16[128,1024]{1,0:T(8,128)(2,1)} %get-tuple-element.76.refs_5_.refs_7_) | copy-start | bytes 786436
  73.9 1.6 %collective-permute-start.14 = (bf16[128,1024]{1,0:T(8,128)(2,1)S(1)}, bf16[128,1024]{1,0:T(8,128)(2,1)S(1)}, u32[]{:S(2)}, u32[]{:S(2)}) collective-permute-start(bf16[128,1024]{1,0:T(8,128)(2,1)S(1)} %get-tuple-element.77), channel_id=1, source_target_pairs={{0,1},{1,0},{2,3},{3,2},{4,5},{5,4},{6,7},{7,6},{8,9},{9,8},{10,11... | collective-permute-start | bytes 786440 | tf_op jit(solution)/shard_map/ppermute | solution.py:463
  74.0 1.9 %collective-permute-start.15 = (bf16[128,1024]{1,0:T(8,128)(2,1)S(1)}, bf16[128,1024]{1,0:T(8,128)(2,1)S(1)}, u32[]{:S(2)}, u32[]{:S(2)}) collective-permute-start(bf16[128,1024]{1,0:T(8,128)(2,1)S(1)} %get-tuple-element.78), channel_id=1, source_target_pairs={{0,1},{1,0},{2,3},{3,2},{4,5},{5,4},{6,7},{7,6},{8,9},{9,8},{10,11... | collective-permute-start | bytes 786440 | tf_op jit(solution)/shard_map/ppermute | solution.py:463
  74.5 1.8 %collective-permute-start.16 = (bf16[128,1024]{1,0:T(8,128)(2,1)S(1)}, bf16[128,1024]{1,0:T(8,128)(2,1)S(1)}, u32[]{:S(2)}, u32[]{:S(2)}) collective-permute-start(bf16[128,1024]{1,0:T(8,128)(2,1)S(1)} %get-tuple-element.79), channel_id=1, source_target_pairs={{0,1},{1,0},{2,3},{3,2},{4,5},{5,4},{6,7},{7,6},{8,9},{9,8},{10,11... | collective-permute-start | bytes 786440 | tf_op jit(solution)/shard_map/ppermute | solution.py:463
  74.6 2.1 %collective-permute-start.17 = (bf16[128,1024]{1,0:T(8,128)(2,1)S(1)}, bf16[128,1024]{1,0:T(8,128)(2,1)S(1)}, u32[]{:S(2)}, u32[]{:S(2)}) collective-permute-start(bf16[128,1024]{1,0:T(8,128)(2,1)S(1)} %get-tuple-element.80), channel_id=1, source_target_pairs={{0,1},{1,0},{2,3},{3,2},{4,5},{5,4},{6,7},{7,6},{8,9},{9,8},{10,11... | collective-permute-start | bytes 786440 | tf_op jit(solution)/shard_map/ppermute | solution.py:463
  75.5 2.1 %collective-permute-start.18 = (bf16[128,1024]{1,0:T(8,128)(2,1)S(1)}, bf16[128,1024]{1,0:T(8,128)(2,1)S(1)}, u32[]{:S(2)}, u32[]{:S(2)}) collective-permute-start(bf16[128,1024]{1,0:T(8,128)(2,1)S(1)} %get-tuple-element.81), channel_id=1, source_target_pairs={{0,1},{1,0},{2,3},{3,2},{4,5},{5,4},{6,7},{7,6},{8,9},{9,8},{10,11... | collective-permute-start | bytes 786440 | tf_op jit(solution)/shard_map/ppermute | solution.py:463
  75.9 1.7 %collective-permute-start.19 = (bf16[128,1024]{1,0:T(8,128)(2,1)S(1)}, bf16[128,1024]{1,0:T(8,128)(2,1)S(1)}, u32[]{:S(2)}, u32[]{:S(2)}) collective-permute-start(bf16[128,1024]{1,0:T(8,128)(2,1)S(1)} %get-tuple-element.82), channel_id=1, source_target_pairs={{0,1},{1,0},{2,3},{3,2},{4,5},{5,4},{6,7},{7,6},{8,9},{9,8},{10,11... | collective-permute-start | bytes 786440 | tf_op jit(solution)/shard_map/ppermute | solution.py:463
  76.3 1.5 %collective-permute-start.20 = (bf16[128,1024]{1,0:T(8,128)(2,1)S(1)}, bf16[128,1024]{1,0:T(8,128)(2,1)S(1)}, u32[]{:S(2)}, u32[]{:S(2)}) collective-permute-start(bf16[128,1024]{1,0:T(8,128)(2,1)S(1)} %get-tuple-element.83), channel_id=1, source_target_pairs={{0,1},{1,0},{2,3},{3,2},{4,5},{5,4},{6,7},{7,6},{8,9},{9,8},{10,11... | collective-permute-start | bytes 786440 | tf_op jit(solution)/shard_map/ppermute | solution.py:463
  76.6 1.5 %collective-permute-start.21 = (bf16[128,1024]{1,0:T(8,128)(2,1)S(1)}, bf16[128,1024]{1,0:T(8,128)(2,1)S(1)}, u32[]{:S(2)}, u32[]{:S(2)}) collective-permute-start(bf16[128,1024]{1,0:T(8,128)(2,1)S(1)} %get-tuple-element.84), channel_id=1, source_target_pairs={{0,1},{1,0},{2,3},{3,2},{4,5},{5,4},{6,7},{7,6},{8,9},{9,8},{10,11... | collective-permute-start | bytes 786440 | tf_op jit(solution)/shard_map/ppermute | solution.py:463

commit v18 on v16

--- a/solution.py
+++ b/solution.py
@@ -427,6 +427,63 @@
     )(*keep, *got, arrived, *before)
 
 
+def own_kernel(top, *refs):
+    out_ref = refs[-1]
+    tiles = len(refs) // 2
+    rows = pl.ds(top, out_ref.shape[0])
+    for t in range(tiles):
+        total = refs[t][rows, :].astype(jnp.float32) + refs[tiles + t][rows, :].astype(jnp.float32)
+        out_ref[:, t * TILE : (t + 1) * TILE] = total
+
+
+def own_sum(keep, got, top):
+    rows = keep[0].shape[0] - top
+    return pl.pallas_call(
+        functools.partial(own_kernel, top),
+        out_shape=jax.ShapeDtypeStruct((rows, len(keep) * TILE), jnp.float32),
+        in_specs=[vmem()] * (2 * len(keep)),
+        out_specs=vmem(),
+        compiler_params=params(16),
+        cost_estimate=SHORT,
+        name="own",
+    )(*keep, *got)
+
+
+def last_kernel(top, own_ref, arrived_ref, _, out_ref, tiles_ref, sent):
+    rows = pl.ds(top, own_ref.shape[0])
+    copies = []
+    for t in range(tiles_ref.shape[0]):
+        at = slice(t * TILE, (t + 1) * TILE)
+        total = own_ref[:, at] + arrived_ref[:, at].astype(jnp.float32)
+        tiles_ref[t] = total.astype(out_ref.dtype)
+        columns = pl.ds(t * TILE, TILE)
+        copies.append(
+            pltpu.make_async_copy(tiles_ref.at[t], out_ref.at[rows, columns], sent.at[t])
+        )
+        copies[-1].start()
+    for copy in copies:
+        copy.wait()
+
+
+def finish_last(own, arrived, top, out):
+    rows, columns = arrived.shape
+    tiles = columns // TILE
+    return pl.pallas_call(
+        functools.partial(last_kernel, top),
+        out_shape=jax.ShapeDtypeStruct(out.shape, out.dtype),
+        in_specs=[vmem(), vmem(), anywhere()],
+        out_specs=anywhere(),
+        input_output_aliases={2: 0},
+        scratch_shapes=[
+            pltpu.VMEM((tiles, rows, TILE), out.dtype),
+            pltpu.SemaphoreType.DMA((tiles,)),
+        ],
+        compiler_params=params(16),
+        cost_estimate=SHORT,
+        name="last",
+    )(own, arrived, out)
+
+
 def shards(ctx_size, queries, keys, values, out_weight, vertical, slash):
     local_blocks = queries.shape[0] // BLK
     assert ctx_size % 2 == 0 and (NEAR - 1) * local_blocks >= SPAN - 1
@@ -477,7 +534,7 @@
     shape = (queries.shape[0] // 4, width)
     out = finish(keep[:HEAD], got[:HEAD], arrived[0], 0, 0, shape, None)
     out = finish(keep[HEAD:], got[HEAD:], arrived[1], HEAD, 0, shape, out)
-    return finish(keep, got, arrived[2], 0, BLK, shape, out)
+    return finish_last(own_sum(keep, got, BLK), arrived[2], BLK, out)
 
 
 def solution(mesh):

time: 80.7 us -> 80.6 us (level)
    pallas_call x0 -> x2, Pallas kernels: none -> 1.25 us  [the longest x1 1.05 us: finish_last(): pl.pallas_call(functools.partial(last_kernel, top), out_shape=jax.ShapeDt...]
    pallas_call x3 -> x2, Pallas kernels: 2.86 us -> 1.77 us  [finish(): pl.pallas_call(functools.partial(finish_kernel, tiles, first, top), out_s...]
where the time goes in v18:
time: 80.6 us; the launch traced here: 80.2 us
  Pallas kernels  36.8 us (46%)
  starting transfers between devices  20.2 us (25%)
  waiting for transfers between devices  19.6 us (24%)
  local copies, waits for them, and re-layouts  3.14 us (4%)
    pallas_call x2, Pallas kernels, project(): pl.pallas_call(functools.partial(project_kernel, first), out_shape=[part]...  15.7 us
    pallas_call x3, Pallas kernels, attend(): pl.pallas_call(functools.partial(attend_kernel, slots, tiles, sizes, plac...  13.5 us
    ppermute x2, starting transfers between devices, shifted(): return lax.ppermute(x, 'ctx', [(r, r + by) for r in range(ctx_size - by)])  6.79 us
    ppermute x17, waiting for transfers between devices, sibling(): return lax.ppermute(x, 'tp', [(j, j ^ 1) for j in range(4)])  6.24 us
    ppermute x3, waiting for transfers between devices, across(): return lax.ppermute(x, 'tp', [(j, j ^ 2) for j in range(4)])  6.05 us
    all_to_all x1, starting transfers between devices, shards(): lax.all_to_all(pair, 'ctx', 0, 0, axis_index_groups=parities, tiled=True)  5.2 us
    ppermute x2, waiting for transfers between devices, shifted(): return lax.ppermute(x, 'ctx', [(r, r + by) for r in range(ctx_size - by)])  3.94 us
    ppermute x17, starting transfers between devices, sibling(): return lax.ppermute(x, 'tp', [(j, j ^ 1) for j in range(4)])  3.87 us
  transfers between devices with their start and end apart: 24, of which 20 were waited for; matrix products, arithmetic and copies ran while one was open for 0% of the time, Pallas kernels for 36%

profile of v18, /device:TPU:16, one launch (start us, length us, event | category | flops | bytes accessed | tf_op | source)
XLA Modules:
  0.0 80.2 jit_solution(15539984926240501987)
XLA Ops:
  0.0 2.2 %pick.1 = (bf16[512,256]{1,0:T(8,128)(2,1)}, bf16[448,256]{1,0:T(8,128)(2,1)}, bf16[4,128,256]{2,1,0:T(8,128)(2,1)}) custom-call(s32[1]{0:T(128)} %bitcast.1.rank_ref.ctx_ref, s32[8,16]{1,0:T(8,128)} %vert_ref.3, bf16[512,128]{1,0:T(8,128)(2,1)} %k_ref.1, bf16[512,128]{1,0:T(8,128)(2,1)} %v_ref.1), custom_call_target="tpu_custom_call" | custom-call | tf_op jit(solution)/shard_map/pick/pallas_call | solution.py:65
  2.2 5.2 %all-to-all-start = ((bf16[4,128,256]{2,1,0:T(8,128)(2,1)}), bf16[4,128,256]{2,1,0:T(8,128)(2,1)S(1)}, u32[]{:S(2)}, u32[]{:S(2)}) async-start(bf16[4,128,256]{2,1,0:T(8,128)(2,1)} %get-tuple-element.49), calls=%async_computation | async-start | bytes 524288 | tf_op jit(solution)/shard_map/all_to_all | solution.py:499
  7.4 3.4 %collective-permute-start = (bf16[512,256]{1,0:T(8,128)(2,1)}, bf16[512,256]{1,0:T(8,128)(2,1)S(1)}, u32[]{:S(2)}, u32[]{:S(2)}) collective-permute-start(bf16[512,256]{1,0:T(8,128)(2,1)} %get-tuple-element.45.own_ref), channel_id=1, source_target_pairs={{0,4},{4,8},{8,12},{12,16},{16,20},{20,24},{24,28},{1,5},{5,9},{9,... | collective-permute-start | bytes 786440 | tf_op jit(solution)/shard_map/ppermute | solution.py:494
  10.8 3.4 %collective-permute-start.1 = (bf16[448,256]{1,0:T(8,128)(2,1)}, bf16[448,256]{1,0:T(8,128)(2,1)S(1)}, u32[]{:S(2)}, u32[]{:S(2)}) collective-permute-start(bf16[448,256]{1,0:T(8,128)(2,1)} %get-tuple-element.48), channel_id=1, source_target_pairs={{0,8},{4,12},{8,16},{12,20},{16,24},{20,28},{1,9},{5,13},{9,17},{1... | collective-permute-start | bytes 688136 | tf_op jit(solution)/shard_map/ppermute | solution.py:494
  14.2 0.6 collective-permute-start.2
  14.8 0.9 %copy-done.4 = bf16[512,256]{1,0:T(8,128)(2,1)S(1)} copy-done((bf16[512,256]{1,0:T(8,128)(2,1)S(1)}, bf16[512,256]{1,0:T(8,128)(2,1)}, u32[]{:S(2)}) %copy-start.4) | copy-done | bytes 262168
  15.8 0.7 copy-done.5
  16.5 0.7 copy-done.6
  17.3 2.1 %collective-permute-done.1.kv_2 = bf16[448,256]{1,0:T(8,128)(2,1)S(1)} collective-permute-done((bf16[448,256]{1,0:T(8,128)(2,1)}, bf16[448,256]{1,0:T(8,128)(2,1)S(1)}, u32[]{:S(2)}, u32[]{:S(2)}) %collective-permute-start.1) | collective-permute-done | bytes 229408 | tf_op jit(solution)/shard_map/ppermute | solution.py:494
  19.4 1.8 %collective-permute-done.kv_1 = bf16[512,256]{1,0:T(8,128)(2,1)S(1)} collective-permute-done((bf16[512,256]{1,0:T(8,128)(2,1)}, bf16[512,256]{1,0:T(8,128)(2,1)S(1)}, u32[]{:S(2)}, u32[]{:S(2)}) %collective-permute-start) | collective-permute-done | bytes 262176 | tf_op jit(solution)/shard_map/ppermute | solution.py:494
  21.3 3.4 %collective-permute-done.2.refs_1_ = bf16[3,128,256]{2,1,0:T(8,128)(2,1)S(1)} collective-permute-done((bf16[3,128,256]{2,1,0:T(8,128)(2,1)S(1)}, bf16[3,128,256]{2,1,0:T(8,128)(2,1)S(1)}, u32[]{:S(2)}, u32[]{:S(2)}) %collective-permute-start.2) | collective-permute-done | bytes 196640 | tf_op jit(solution)/shard_map/ppermute | solution.py:501
  24.7 4.5 %attend.3 = (bf16[128,1024]{1,0:T(8,128)(2,1)S(1)}, bf16[64,2048]{1,0:T(8,128)(2,1)S(1)}, bf16[64,2048]{1,0:T(8,128)(2,1)S(1)}) custom-call(s32[1]{0:T(128)} %bitcast.tp_ref, s32[1]{0:T(128)} %bitcast.1.rank_ref.ctx_ref, bf16[512,1024]{1,0:T(8,128)(2,1)S(1)} %copy-done.1, bf16[512,1024]{1,0:T(8,128)(2,1)S(1)} %copy-done.1, ...), custom_call_target="tpu_custom_call" | custom-call | tf_op jit(solution)/shard_map/attend/pallas_call | solution.py:270
  29.3 1.5 %collective-permute-done.3 = bf16[64,2048]{1,0:T(8,128)(2,1)S(1)} collective-permute-done((bf16[64,2048]{1,0:T(8,128)(2,1)S(1)}, bf16[64,2048]{1,0:T(8,128)(2,1)S(1)}, u32[]{:S(2)}, u32[]{:S(2)}) %collective-permute-start.3) | collective-permute-done | bytes 262176 | tf_op jit(solution)/shard_map/ppermute | solution.py:506
  30.8 1.6 %collective-permute-start.8 = (bf16[64,2048]{1,0:T(8,128)(2,1)S(1)}, bf16[64,2048]{1,0:T(8,128)(2,1)S(1)}, u32[]{:S(2)}, u32[]{:S(2)}) collective-permute-start(bf16[64,2048]{1,0:T(8,128)(2,1)S(1)} %add_convert_fusion.refs_0_), channel_id=1, source_target_pairs={{0,2},{1,3},{2,0},{3,1},{4,6},{5,7},{6,4},{7,5},{8,10},{9,11},{10,... | collective-permute-start | bytes 786440 | tf_op jit(solution)/shard_map/ppermute | solution.py:509
  32.4 1.9 %project.3 = (bf16[64,1536]{1,0:T(8,128)(2,1)S(1)}, bf16[64,1536]{1,0:T(8,128)(2,1)S(1)}, bf16[64,1536]{1,0:T(8,128)(2,1)S(1)}, bf16[64,1536]{1,0:T(8,128)(2,1)S...) custom-call(bf16[128,1024]{1,0:T(8,128)(2,1)S(1)} %get-tuple-element, ...), custom_call_target="tpu_custom_call" | custom-call | tf_op jit(solution)/shard_map/project/pallas_call | solution.py:316
  34.4 0.5 collective-permute-start.5
  34.9 0.4 collective-permute-start.7
  35.4 0.4 collective-permute-done.4.refs_4_
  35.8 0.3 collective-permute-done.5.refs_5_
  36.1 0.3 collective-permute-done.6.refs_6_
  36.4 0.3 collective-permute-done.7.refs_7_
  36.8 0.9 %collective-permute-start.13 = (bf16[64,6144]{1,0:T(8,128)(2,1)S(1)}, bf16[64,6144]{1,0:T(8,128)(2,1)S(1)}, u32[]{:S(2)}, u32[]{:S(2)}) collective-permute-start(bf16[64,6144]{1,0:T(8,128)(2,1)S(1)} %add.7.refs_3_), channel_id=1, source_target_pairs={{0,2},{1,3},{2,0},{3,1},{4,6},{5,7},{6,4},{7,5},{8,10},{9,11},{10,... | collective-permute-start | bytes 2359304 | tf_op jit(solution)/shard_map/ppermute | solution.py:509
  37.7 3.3 %attend.4.a_ref = bf16[128,1024]{1,0:T(8,128)(2,1)S(1)} custom-call(s32[1]{0:T(128)} %bitcast.tp_ref, s32[1]{0:T(128)} %bitcast.1.rank_ref.ctx_ref, bf16[512,1024]{1,0:T(8,128)(2,1)S(1)} %copy-done.1, bf16[512,1024]{1,0:T(8,128)(2,1)S(1)} %copy-done.1, s32[3,8,128]{2,1,0:T(8,128)S(1)} %get-tuple-element.46.table_ref, ...), custom_call_target="tpu_custom_call" | custom-call | tf_op jit(solution)/shard_map/attend/pallas_call | solution.py:270
  41.0 6.6 %project.4 = (bf16[64,2048]{1,0:T(8,128)(2,1)S(1)}, bf16[64,2048]{1,0:T(8,128)(2,1)S(1)}, bf16[64,2048]{1,0:T(8,128)(2,1)S(1)}, bf16[64,2048]{1,0:T(8,128)(2,1)S...) custom-call(bf16[128,1024]{1,0:T(8,128)(2,1)S(1)} %attend.4.a_ref, ...), custom_call_target="tpu_custom_call" | custom-call | tf_op jit(solution)/shard_map/project/pallas_call | solution.py:353
  47.8 0.5 collective-permute-start.10
  48.3 0.4 collective-permute-start.12
  48.8 0.5 collective-permute-done.9.refs_4_
  49.3 0.4 collective-permute-done.10.refs_5_
  49.7 0.4 collective-permute-done.11.refs_6_
  50.0 0.4 collective-permute-done.12.refs_7_
  50.4 0.2 add.8.refs_3_
  50.7 1.3 %collective-permute-start.22 = (bf16[64,8192]{1,0:T(8,128)(2,1)S(1)}, bf16[64,8192]{1,0:T(8,128)(2,1)S(1)}, u32[]{:S(2)}, u32[]{:S(2)}) collective-permute-start(bf16[64,8192]{1,0:T(8,128)(2,1)S(1)} %add.8.refs_3_), channel_id=1, source_target_pairs={{0,2},{1,3},{2,0},{3,1},{4,6},{5,7},{6,4},{7,5},{8,10},{9,11},{10,... | collective-permute-start | bytes 3145736 | tf_op jit(solution)/shard_map/ppermute | solution.py:509
  52.0 5.3 %collective-permute-done.13.refs_4_.refs_12_ = bf16[64,6144]{1,0:T(8,128)(2,1)S(1)} collective-permute-done((bf16[64,6144]{1,0:T(8,128)(2,1)S(1)}, bf16[64,6144]{1,0:T(8,128)(2,1)S(1)}, u32[]{:S(2)}, u32[]{:S(2)}) %collective-permute-start.13) | collective-permute-done | bytes 786464 | tf_op jit(solution)/shard_map/ppermute | solution.py:509
  57.3 5.7 %attend.5.a_ref = bf16[256,1024]{1,0:T(8,128)(2,1)S(1)} custom-call(s32[1]{0:T(128)} %bitcast.tp_ref, s32[1]{0:T(128)} %bitcast.1.rank_ref.ctx_ref, bf16[512,1024]{1,0:T(8,128)(2,1)S(1)} %copy-done.1, bf16[512,1024]{1,0:T(8,128)(2,1)S(1)} %copy-done.1, s32[3,8,128]{2,1,0:T(8,128)S(1)} %get-tuple-element.46.table_ref, ...), custom_call_target="tpu_custom_call" | custom-call | tf_op jit(solution)/shard_map/attend/pallas_call | solution.py:270
  62.9 0.8 copy-done.2
  63.7 9.1 %project.5 = (bf16[128,1024]{1,0:T(8,128)(2,1)S(1)}, bf16[128,1024]{1,0:T(8,128)(2,1)S(1)}, bf16[128,1024]{1,0:T(8,128)(2,1)S(1)}, bf16[128,1024]{1,0:T(8,128)(2...) custom-call(bf16[256,1024]{1,0:T(8,128)(2,1)} %copy-done.2, ...), custom_call_target="tpu_custom_call" | custom-call | tf_op jit(solution)/shard_map/project/pallas_call | solution.py:353
  72.9 0.5 collective-permute-start.15
  73.5 0.4 collective-permute-start.17
  73.9 0.5 collective-permute-done.14.refs_8_.refs_2_
  74.6 0.2 collective-permute-done.15.refs_9_.refs_3_
  74.9 0.2 collective-permute-done.16.refs_10_.refs_6_
  75.3 0.2 collective-permute-done.17.refs_11_.refs_7_
  75.7 0.8 finish.2.refs_13_
  76.5 0.2 collective-permute-done.20.refs_14_.refs_10_
  76.7 0.4 collective-permute-done.21.refs_15_.refs_11_
  77.3 1.0 %finish.3._ = bf16[128,8192]{1,0:T(8,128)(2,1)} custom-call(bf16[128,1024]{1,0:T(8,128)(2,1)S(1)} %get-tuple-element.71.refs_2_.refs_0_, bf16[128,1024]{1,0:T(8,128)(2,1)S(1)} %get-tuple-element.72.refs_3_.refs_1_, bf16[128,1024]{1,0:T(8,128)(2,1)S(1)} %get-tuple-element.73.refs_4_.refs_2_, ...), custom_call_target="tpu_custom_call", output_to_operand_aliasing={{}: (13, {})} | custom-call | tf_op jit(solution)/shard_map/finish/pallas_call | solution.py:414
  78.3 0.7 collective-permute-done.22.arrived_ref
  79.0 1.0 %last.1 = bf16[128,8192]{1,0:T(8,128)(2,1)} custom-call(f32[64,8192]{1,0:T(8,128)S(1)} %own.1.own_ref, bf16[64,8192]{1,0:T(8,128)(2,1)S(1)} %collective-permute-done.22.arrived_ref, bf16[128,8192]{1,0:T(8,128)(2,1)} %finish.3._), custom_call_target="tpu_custom_call", output_to_operand_aliasing={{}: (2, {})} | custom-call | tf_op jit(solution)/shard_map/last/pallas_call | solution.py:471
  (30 shorter events, 1.7 us)
Async XLA Ops:
  0.0 24.7 %copy-start.1 = (bf16[512,1024]{1,0:T(8,128)(2,1)S(1)}, bf16[512,1024]{1,0:T(8,128)(2,1)}, u32[]{:S(2)}) copy-start(bf16[512,1024]{1,0:T(8,128)(2,1)} %q_1.5) | copy-start | bytes 3145732
  2.2 12.0 %all-to-all-start = ((bf16[4,128,256]{2,1,0:T(8,128)(2,1)}), bf16[4,128,256]{2,1,0:T(8,128)(2,1)S(1)}, u32[]{:S(2)}, u32[]{:S(2)}) async-start(bf16[4,128,256]{2,1,0:T(8,128)(2,1)} %get-tuple-element.49), calls=%async_computation | async-start | bytes 524288 | tf_op jit(solution)/shard_map/all_to_all | solution.py:499
  7.4 13.9 %collective-permute-start = (bf16[512,256]{1,0:T(8,128)(2,1)}, bf16[512,256]{1,0:T(8,128)(2,1)S(1)}, u32[]{:S(2)}, u32[]{:S(2)}) collective-permute-start(bf16[512,256]{1,0:T(8,128)(2,1)} %get-tuple-element.45.own_ref), channel_id=1, source_target_pairs={{0,4},{4,8},{8,12},{12,16},{16,20},{20,24},{24,28},{1,5},{5,9},{9,... | collective-permute-start | bytes 786440 | tf_op jit(solution)/shard_map/ppermute | solution.py:494
  10.8 8.6 %collective-permute-start.1 = (bf16[448,256]{1,0:T(8,128)(2,1)}, bf16[448,256]{1,0:T(8,128)(2,1)S(1)}, u32[]{:S(2)}, u32[]{:S(2)}) collective-permute-start(bf16[448,256]{1,0:T(8,128)(2,1)} %get-tuple-element.48), channel_id=1, source_target_pairs={{0,8},{4,12},{8,16},{12,20},{16,24},{20,28},{1,9},{5,13},{9,17},{1... | collective-permute-start | bytes 688136 | tf_op jit(solution)/shard_map/ppermute | solution.py:494
  14.2 10.5 %collective-permute-start.2 = (bf16[3,128,256]{2,1,0:T(8,128)(2,1)S(1)}, bf16[3,128,256]{2,1,0:T(8,128)(2,1)S(1)}, u32[]{:S(2)}, u32[]{:S(2)}) collective-permute-start(bf16[3,128,256]{2,1,0:T(8,128)(2,1)S(1)} %slice.4), channel_id=1, source_target_pairs={{0,4},{4,0},{8,12},{12,8},{16,20},{20,16},{24,28},{28,24},{1,5},{5... | collective-permute-start | bytes 589832 | tf_op jit(solution)/shard_map/ppermute | solution.py:501
  14.8 0.9 %copy-start.4 = (bf16[512,256]{1,0:T(8,128)(2,1)S(1)}, bf16[512,256]{1,0:T(8,128)(2,1)}, u32[]{:S(2)}) copy-start(bf16[512,256]{1,0:T(8,128)(2,1)} %get-tuple-element.45.own_ref) | copy-start | bytes 786436
  15.8 0.7 copy-start.5
  16.5 0.7 copy-start.6
  24.7 7.7 %copy-start = (bf16[1024,8192]{1,0:T(8,128)(2,1)S(1)}, bf16[1024,8192]{1,0:T(8,128)(2,1)}, u32[]{:S(2)}) copy-start(bf16[1024,8192]{1,0:T(8,128)(2,1)} %w_hbm.3) | copy-start | bytes 50331652
  29.2 1.6 %collective-permute-start.3 = (bf16[64,2048]{1,0:T(8,128)(2,1)S(1)}, bf16[64,2048]{1,0:T(8,128)(2,1)S(1)}, u32[]{:S(2)}, u32[]{:S(2)}) collective-permute-start(bf16[64,2048]{1,0:T(8,128)(2,1)S(1)} %get-tuple-element.52), channel_id=1, source_target_pairs={{0,1},{1,0},{2,3},{3,2},{4,5},{5,4},{6,7},{7,6},{8,9},{9,8},{10,11... | collective-permute-start | bytes 786440 | tf_op jit(solution)/shard_map/ppermute | solution.py:506
  30.8 10.2 %collective-permute-start.8 = (bf16[64,2048]{1,0:T(8,128)(2,1)S(1)}, bf16[64,2048]{1,0:T(8,128)(2,1)S(1)}, u32[]{:S(2)}, u32[]{:S(2)}) collective-permute-start(bf16[64,2048]{1,0:T(8,128)(2,1)S(1)} %add_convert_fusion.refs_0_), channel_id=1, source_target_pairs={{0,2},{1,3},{2,0},{3,1},{4,6},{5,7},{6,4},{7,5},{8,10},{9,11},{10,... | collective-permute-start | bytes 786440 | tf_op jit(solution)/shard_map/ppermute | solution.py:509
  34.3 1.5 %collective-permute-start.4 = (bf16[64,1536]{1,0:T(8,128)(2,1)S(1)}, bf16[64,1536]{1,0:T(8,128)(2,1)S(1)}, u32[]{:S(2)}, u32[]{:S(2)}) collective-permute-start(bf16[64,1536]{1,0:T(8,128)(2,1)S(1)} %get-tuple-element.57), channel_id=1, source_target_pairs={{0,1},{1,0},{2,3},{3,2},{4,5},{5,4},{6,7},{7,6},{8,9},{9,8},{10,11... | collective-permute-start | bytes 589832 | tf_op jit(solution)/shard_map/ppermute | solution.py:506
  34.4 1.7 %collective-permute-start.5 = (bf16[64,1536]{1,0:T(8,128)(2,1)S(1)}, bf16[64,1536]{1,0:T(8,128)(2,1)S(1)}, u32[]{:S(2)}, u32[]{:S(2)}) collective-permute-start(bf16[64,1536]{1,0:T(8,128)(2,1)S(1)} %get-tuple-element.58), channel_id=1, source_target_pairs={{0,1},{1,0},{2,3},{3,2},{4,5},{5,4},{6,7},{7,6},{8,9},{9,8},{10,11... | collective-permute-start | bytes 589832 | tf_op jit(solution)/shard_map/ppermute | solution.py:506
  34.9 1.5 %collective-permute-start.6 = (bf16[64,1536]{1,0:T(8,128)(2,1)S(1)}, bf16[64,1536]{1,0:T(8,128)(2,1)S(1)}, u32[]{:S(2)}, u32[]{:S(2)}) collective-permute-start(bf16[64,1536]{1,0:T(8,128)(2,1)S(1)} %get-tuple-element.59), channel_id=1, source_target_pairs={{0,1},{1,0},{2,3},{3,2},{4,5},{5,4},{6,7},{7,6},{8,9},{9,8},{10,11... | collective-permute-start | bytes 589832 | tf_op jit(solution)/shard_map/ppermute | solution.py:506
  34.9 1.7 %collective-permute-start.7 = (bf16[64,1536]{1,0:T(8,128)(2,1)S(1)}, bf16[64,1536]{1,0:T(8,128)(2,1)S(1)}, u32[]{:S(2)}, u32[]{:S(2)}) collective-permute-start(bf16[64,1536]{1,0:T(8,128)(2,1)S(1)} %get-tuple-element.60), channel_id=1, source_target_pairs={{0,1},{1,0},{2,3},{3,2},{4,5},{5,4},{6,7},{7,6},{8,9},{9,8},{10,11... | collective-permute-start | bytes 589832 | tf_op jit(solution)/shard_map/ppermute | solution.py:506
  36.8 20.4 %collective-permute-start.13 = (bf16[64,6144]{1,0:T(8,128)(2,1)S(1)}, bf16[64,6144]{1,0:T(8,128)(2,1)S(1)}, u32[]{:S(2)}, u32[]{:S(2)}) collective-permute-start(bf16[64,6144]{1,0:T(8,128)(2,1)S(1)} %add.7.refs_3_), channel_id=1, source_target_pairs={{0,2},{1,3},{2,0},{3,1},{4,6},{5,7},{6,4},{7,5},{8,10},{9,11},{10,... | collective-permute-start | bytes 2359304 | tf_op jit(solution)/shard_map/ppermute | solution.py:509
  47.7 1.6 %collective-permute-start.9 = (bf16[64,2048]{1,0:T(8,128)(2,1)S(1)}, bf16[64,2048]{1,0:T(8,128)(2,1)S(1)}, u32[]{:S(2)}, u32[]{:S(2)}) collective-permute-start(bf16[64,2048]{1,0:T(8,128)(2,1)S(1)} %get-tuple-element.65), channel_id=1, source_target_pairs={{0,1},{1,0},{2,3},{3,2},{4,5},{5,4},{6,7},{7,6},{8,9},{9,8},{10,11... | collective-permute-start | bytes 786440 | tf_op jit(solution)/shard_map/ppermute | solution.py:506
  47.8 1.9 %collective-permute-start.10 = (bf16[64,2048]{1,0:T(8,128)(2,1)S(1)}, bf16[64,2048]{1,0:T(8,128)(2,1)S(1)}, u32[]{:S(2)}, u32[]{:S(2)}) collective-permute-start(bf16[64,2048]{1,0:T(8,128)(2,1)S(1)} %get-tuple-element.66), channel_id=1, source_target_pairs={{0,1},{1,0},{2,3},{3,2},{4,5},{5,4},{6,7},{7,6},{8,9},{9,8},{10,11... | collective-permute-start | bytes 786440 | tf_op jit(solution)/shard_map/ppermute | solution.py:506
  48.3 1.8 %collective-permute-start.11 = (bf16[64,2048]{1,0:T(8,128)(2,1)S(1)}, bf16[64,2048]{1,0:T(8,128)(2,1)S(1)}, u32[]{:S(2)}, u32[]{:S(2)}) collective-permute-start(bf16[64,2048]{1,0:T(8,128)(2,1)S(1)} %get-tuple-element.67), channel_id=1, source_target_pairs={{0,1},{1,0},{2,3},{3,2},{4,5},{5,4},{6,7},{7,6},{8,9},{9,8},{10,11... | collective-permute-start | bytes 786440 | tf_op jit(solution)/shard_map/ppermute | solution.py:506
  48.3 2.1 %collective-permute-start.12 = (bf16[64,2048]{1,0:T(8,128)(2,1)S(1)}, bf16[64,2048]{1,0:T(8,128)(2,1)S(1)}, u32[]{:S(2)}, u32[]{:S(2)}) collective-permute-start(bf16[64,2048]{1,0:T(8,128)(2,1)S(1)} %get-tuple-element.68), channel_id=1, source_target_pairs={{0,1},{1,0},{2,3},{3,2},{4,5},{5,4},{6,7},{7,6},{8,9},{9,8},{10,11... | collective-permute-start | bytes 786440 | tf_op jit(solution)/shard_map/ppermute | solution.py:506
  50.7 28.4 %collective-permute-start.22 = (bf16[64,8192]{1,0:T(8,128)(2,1)S(1)}, bf16[64,8192]{1,0:T(8,128)(2,1)S(1)}, u32[]{:S(2)}, u32[]{:S(2)}) collective-permute-start(bf16[64,8192]{1,0:T(8,128)(2,1)S(1)} %add.8.refs_3_), channel_id=1, source_target_pairs={{0,2},{1,3},{2,0},{3,1},{4,6},{5,7},{6,4},{7,5},{8,10},{9,11},{10,... | collective-permute-start | bytes 3145736 | tf_op jit(solution)/shard_map/ppermute | solution.py:509
  62.9 0.8 copy-start.2
  72.8 4.3 %copy-start.3 = (bf16[128,1024]{1,0:T(8,128)(2,1)S(1)}, bf16[128,1024]{1,0:T(8,128)(2,1)}, u32[]{:S(2)}) copy-start(bf16[128,1024]{1,0:T(8,128)(2,1)} %get-tuple-element.76.refs_7_.refs_5_) | copy-start | bytes 786436
  72.8 1.6 %collective-permute-start.14 = (bf16[128,1024]{1,0:T(8,128)(2,1)S(1)}, bf16[128,1024]{1,0:T(8,128)(2,1)S(1)}, u32[]{:S(2)}, u32[]{:S(2)}) collective-permute-start(bf16[128,1024]{1,0:T(8,128)(2,1)S(1)} %get-tuple-element.77), channel_id=1, source_target_pairs={{0,1},{1,0},{2,3},{3,2},{4,5},{5,4},{6,7},{7,6},{8,9},{9,8},{10,11... | collective-permute-start | bytes 786440 | tf_op jit(solution)/shard_map/ppermute | solution.py:506
  72.9 1.9 %collective-permute-start.15 = (bf16[128,1024]{1,0:T(8,128)(2,1)S(1)}, bf16[128,1024]{1,0:T(8,128)(2,1)S(1)}, u32[]{:S(2)}, u32[]{:S(2)}) collective-permute-start(bf16[128,1024]{1,0:T(8,128)(2,1)S(1)} %get-tuple-element.78), channel_id=1, source_target_pairs={{0,1},{1,0},{2,3},{3,2},{4,5},{5,4},{6,7},{7,6},{8,9},{9,8},{10,11... | collective-permute-start | bytes 786440 | tf_op jit(solution)/shard_map/ppermute | solution.py:506
  73.4 1.8 %collective-permute-start.16 = (bf16[128,1024]{1,0:T(8,128)(2,1)S(1)}, bf16[128,1024]{1,0:T(8,128)(2,1)S(1)}, u32[]{:S(2)}, u32[]{:S(2)}) collective-permute-start(bf16[128,1024]{1,0:T(8,128)(2,1)S(1)} %get-tuple-element.79), channel_id=1, source_target_pairs={{0,1},{1,0},{2,3},{3,2},{4,5},{5,4},{6,7},{7,6},{8,9},{9,8},{10,11... | collective-permute-start | bytes 786440 | tf_op jit(solution)/shard_map/ppermute | solution.py:506
  73.5 2.1 %collective-permute-start.17 = (bf16[128,1024]{1,0:T(8,128)(2,1)S(1)}, bf16[128,1024]{1,0:T(8,128)(2,1)S(1)}, u32[]{:S(2)}, u32[]{:S(2)}) collective-permute-start(bf16[128,1024]{1,0:T(8,128)(2,1)S(1)} %get-tuple-element.80), channel_id=1, source_target_pairs={{0,1},{1,0},{2,3},{3,2},{4,5},{5,4},{6,7},{7,6},{8,9},{9,8},{10,11... | collective-permute-start | bytes 786440 | tf_op jit(solution)/shard_map/ppermute | solution.py:506
  74.4 2.1 %collective-permute-start.18 = (bf16[128,1024]{1,0:T(8,128)(2,1)S(1)}, bf16[128,1024]{1,0:T(8,128)(2,1)S(1)}, u32[]{:S(2)}, u32[]{:S(2)}) collective-permute-start(bf16[128,1024]{1,0:T(8,128)(2,1)S(1)} %get-tuple-element.81), channel_id=1, source_target_pairs={{0,1},{1,0},{2,3},{3,2},{4,5},{5,4},{6,7},{7,6},{8,9},{9,8},{10,11... | collective-permute-start | bytes 786440 | tf_op jit(solution)/shard_map/ppermute | solution.py:506
  74.8 1.7 %collective-permute-start.19 = (bf16[128,1024]{1,0:T(8,128)(2,1)S(1)}, bf16[128,1024]{1,0:T(8,128)(2,1)S(1)}, u32[]{:S(2)}, u32[]{:S(2)}) collective-permute-start(bf16[128,1024]{1,0:T(8,128)(2,1)S(1)} %get-tuple-element.82), channel_id=1, source_target_pairs={{0,1},{1,0},{2,3},{3,2},{4,5},{5,4},{6,7},{7,6},{8,9},{9,8},{10,11... | collective-permute-start | bytes 786440 | tf_op jit(solution)/shard_map/ppermute | solution.py:506
  75.2 1.5 %collective-permute-start.20 = (bf16[128,1024]{1,0:T(8,128)(2,1)S(1)}, bf16[128,1024]{1,0:T(8,128)(2,1)S(1)}, u32[]{:S(2)}, u32[]{:S(2)}) collective-permute-start(bf16[128,1024]{1,0:T(8,128)(2,1)S(1)} %get-tuple-element.83), channel_id=1, source_target_pairs={{0,1},{1,0},{2,3},{3,2},{4,5},{5,4},{6,7},{7,6},{8,9},{9,8},{10,11... | collective-permute-start | bytes 786440 | tf_op jit(solution)/shard_map/ppermute | solution.py:506
  75.6 1.5 %collective-permute-start.21 = (bf16[128,1024]{1,0:T(8,128)(2,1)S(1)}, bf16[128,1024]{1,0:T(8,128)(2,1)S(1)}, u32[]{:S(2)}, u32[]{:S(2)}) collective-permute-start(bf16[128,1024]{1,0:T(8,128)(2,1)S(1)} %get-tuple-element.84), channel_id=1, source_target_pairs={{0,1},{1,0},{2,3},{3,2},{4,5},{5,4},{6,7},{7,6},{8,9},{9,8},{10,11... | collective-permute-start | bytes 786440 | tf_op jit(solution)/shard_map/ppermute | solution.py:506

commit v19 on v16

--- a/solution.py
+++ b/solution.py
@@ -141,10 +141,17 @@
     slash = table_ref[1][:, : sizes[1]]
     block = table_ref[2]
 
+    parts = arrival.shape[1]
+    depth = weight.shape[1] // parts
+
     def fetch(t):
-        return pltpu.make_async_copy(
-            w_hbm.at[:, pl.ds(t * TILE, TILE)], weight.at[t], arrival.at[t]
-        )
+        ats = [pl.ds(p * depth, depth) for p in range(parts)]
+        return [
+            pltpu.make_async_copy(
+                w_hbm.at[at, pl.ds(t * TILE, TILE)], weight.at[t, at], arrival.at[t, p]
+            )
+            for p, at in enumerate(ats)
+        ]
 
     @pl.when(step == 0)
     def _():
@@ -163,7 +170,8 @@
         for copy in copies:
             copy.start()
         for t in range(tiles):
-            fetch(t).start()
+            for copy in fetch(t):
+                copy.start()
         key = lax.broadcasted_iota(jnp.int32, e_win.shape, 0)
         lane = lax.broadcasted_iota(jnp.int32, e_win.shape, 1)
         last = (key - (SPAN - 1) * BLK == lane - BLK) & (lane >= BLK)
@@ -237,7 +245,8 @@
         outs[0][...] = attended[...]
         half = attended.shape[0] // 2
         for t in range(tiles):
-            fetch(t).wait()
+            for copy in fetch(t):
+                copy.wait()
             product = jnp.dot(attended[...], weight[t], preferred_element_type=jnp.float32)
             product = product.astype(dtype)
             outs[1][:, t * TILE : (t + 1) * TILE] = product[:half]
@@ -287,7 +296,7 @@
                 pltpu.VMEM((far, LANES), dtype),
                 pltpu.VMEM((steps * 2 * BLK, width), dtype),
                 pltpu.VMEM((max(tiles, 1), out_weight.shape[0], TILE), dtype),
-                pltpu.SemaphoreType.DMA((max(tiles, 1),)),
+                pltpu.SemaphoreType.DMA((max(tiles, 1), 4)),
                 pltpu.SemaphoreType.DMA((NEAR + 2,)),
             ],
         ),

time: 80.7 us -> 80.8 us (level)
  no operation moved by 1% of the time
where the time goes in v19:
time: 80.8 us; the launch traced here: 80.4 us
  Pallas kernels  36.8 us (46%)
  starting transfers between devices  20.2 us (25%)
  waiting for transfers between devices  19.8 us (25%)
  local copies, waits for them, and re-layouts  3.14 us (4%)
    pallas_call x2, Pallas kernels, project(): pl.pallas_call(functools.partial(project_kernel, first), out_shape=[part]...  15.7 us
    pallas_call x3, Pallas kernels, attend(): pl.pallas_call(functools.partial(attend_kernel, slots, tiles, sizes, plac...  13.6 us
    ppermute x2, starting transfers between devices, shifted(): return lax.ppermute(x, 'ctx', [(r, r + by) for r in range(ctx_size - by)])  6.79 us
    ppermute x17, waiting for transfers between devices, sibling(): return lax.ppermute(x, 'tp', [(j, j ^ 1) for j in range(4)])  6.24 us
    ppermute x3, waiting for transfers between devices, across(): return lax.ppermute(x, 'tp', [(j, j ^ 2) for j in range(4)])  6.21 us
    all_to_all x1, starting transfers between devices, shards(): lax.all_to_all(pair, 'ctx', 0, 0, axis_index_groups=parities, tiled=True)  5.2 us
    ppermute x2, waiting for transfers between devices, shifted(): return lax.ppermute(x, 'ctx', [(r, r + by) for r in range(ctx_size - by)])  3.94 us
    ppermute x17, starting transfers between devices, sibling(): return lax.ppermute(x, 'tp', [(j, j ^ 1) for j in range(4)])  3.87 us
  transfers between devices with their start and end apart: 24, of which 20 were waited for; matrix products, arithmetic and copies ran while one was open for 0% of the time, Pallas kernels for 36%

profile of v19, /device:TPU:16, one launch (start us, length us, event | category | flops | bytes accessed | tf_op | source)
XLA Modules:
  0.0 80.4 jit_solution(9553804911200741264)
XLA Ops:
  0.0 2.2 %pick.1 = (bf16[512,256]{1,0:T(8,128)(2,1)}, bf16[448,256]{1,0:T(8,128)(2,1)}, bf16[4,128,256]{2,1,0:T(8,128)(2,1)}) custom-call(s32[1]{0:T(128)} %bitcast.1.rank_ref.ctx_ref, s32[8,16]{1,0:T(8,128)} %vert_ref.3, bf16[512,128]{1,0:T(8,128)(2,1)} %k_ref.1, bf16[512,128]{1,0:T(8,128)(2,1)} %v_ref.1), custom_call_target="tpu_custom_call" | custom-call | tf_op jit(solution)/shard_map/pick/pallas_call | solution.py:65
  2.2 5.2 %all-to-all-start = ((bf16[4,128,256]{2,1,0:T(8,128)(2,1)}), bf16[4,128,256]{2,1,0:T(8,128)(2,1)S(1)}, u32[]{:S(2)}, u32[]{:S(2)}) async-start(bf16[4,128,256]{2,1,0:T(8,128)(2,1)} %get-tuple-element.49), calls=%async_computation | async-start | bytes 524288 | tf_op jit(solution)/shard_map/all_to_all | solution.py:451
  7.4 3.4 %collective-permute-start = (bf16[512,256]{1,0:T(8,128)(2,1)}, bf16[512,256]{1,0:T(8,128)(2,1)S(1)}, u32[]{:S(2)}, u32[]{:S(2)}) collective-permute-start(bf16[512,256]{1,0:T(8,128)(2,1)} %get-tuple-element.45.own_ref), channel_id=1, source_target_pairs={{0,4},{4,8},{8,12},{12,16},{16,20},{20,24},{24,28},{1,5},{5,9},{9,... | collective-permute-start | bytes 786440 | tf_op jit(solution)/shard_map/ppermute | solution.py:446
  10.8 3.4 %collective-permute-start.1 = (bf16[448,256]{1,0:T(8,128)(2,1)}, bf16[448,256]{1,0:T(8,128)(2,1)S(1)}, u32[]{:S(2)}, u32[]{:S(2)}) collective-permute-start(bf16[448,256]{1,0:T(8,128)(2,1)} %get-tuple-element.48), channel_id=1, source_target_pairs={{0,8},{4,12},{8,16},{12,20},{16,24},{20,28},{1,9},{5,13},{9,17},{1... | collective-permute-start | bytes 688136 | tf_op jit(solution)/shard_map/ppermute | solution.py:446
  14.2 0.6 collective-permute-start.2
  14.8 0.9 %copy-done.4 = bf16[512,256]{1,0:T(8,128)(2,1)S(1)} copy-done((bf16[512,256]{1,0:T(8,128)(2,1)S(1)}, bf16[512,256]{1,0:T(8,128)(2,1)}, u32[]{:S(2)}) %copy-start.4) | copy-done | bytes 262168
  15.8 0.7 copy-done.5
  16.5 0.7 copy-done.6
  17.3 2.1 %collective-permute-done.1.kv_2 = bf16[448,256]{1,0:T(8,128)(2,1)S(1)} collective-permute-done((bf16[448,256]{1,0:T(8,128)(2,1)}, bf16[448,256]{1,0:T(8,128)(2,1)S(1)}, u32[]{:S(2)}, u32[]{:S(2)}) %collective-permute-start.1) | collective-permute-done | bytes 229408 | tf_op jit(solution)/shard_map/ppermute | solution.py:446
  19.4 1.8 %collective-permute-done.kv_1 = bf16[512,256]{1,0:T(8,128)(2,1)S(1)} collective-permute-done((bf16[512,256]{1,0:T(8,128)(2,1)}, bf16[512,256]{1,0:T(8,128)(2,1)S(1)}, u32[]{:S(2)}, u32[]{:S(2)}) %collective-permute-start) | collective-permute-done | bytes 262176 | tf_op jit(solution)/shard_map/ppermute | solution.py:446
  21.3 3.4 %collective-permute-done.2.refs_1_ = bf16[3,128,256]{2,1,0:T(8,128)(2,1)S(1)} collective-permute-done((bf16[3,128,256]{2,1,0:T(8,128)(2,1)S(1)}, bf16[3,128,256]{2,1,0:T(8,128)(2,1)S(1)}, u32[]{:S(2)}, u32[]{:S(2)}) %collective-permute-start.2) | collective-permute-done | bytes 196640 | tf_op jit(solution)/shard_map/ppermute | solution.py:453
  24.7 4.6 %attend.3 = (bf16[128,1024]{1,0:T(8,128)(2,1)S(1)}, bf16[64,2048]{1,0:T(8,128)(2,1)S(1)}, bf16[64,2048]{1,0:T(8,128)(2,1)S(1)}) custom-call(s32[1]{0:T(128)} %bitcast.tp_ref, s32[1]{0:T(128)} %bitcast.1.rank_ref.ctx_ref, bf16[512,1024]{1,0:T(8,128)(2,1)S(1)} %copy-done.1, bf16[512,1024]{1,0:T(8,128)(2,1)S(1)} %copy-done.1, ...), custom_call_target="tpu_custom_call" | custom-call | tf_op jit(solution)/shard_map/attend/pallas_call | solution.py:279
  29.3 1.5 %collective-permute-done.3 = bf16[64,2048]{1,0:T(8,128)(2,1)S(1)} collective-permute-done((bf16[64,2048]{1,0:T(8,128)(2,1)S(1)}, bf16[64,2048]{1,0:T(8,128)(2,1)S(1)}, u32[]{:S(2)}, u32[]{:S(2)}) %collective-permute-start.3) | collective-permute-done | bytes 262176 | tf_op jit(solution)/shard_map/ppermute | solution.py:458
  30.9 1.6 %collective-permute-start.8 = (bf16[64,2048]{1,0:T(8,128)(2,1)S(1)}, bf16[64,2048]{1,0:T(8,128)(2,1)S(1)}, u32[]{:S(2)}, u32[]{:S(2)}) collective-permute-start(bf16[64,2048]{1,0:T(8,128)(2,1)S(1)} %add_convert_fusion.refs_0_), channel_id=1, source_target_pairs={{0,2},{1,3},{2,0},{3,1},{4,6},{5,7},{6,4},{7,5},{8,10},{9,11},{10,... | collective-permute-start | bytes 786440 | tf_op jit(solution)/shard_map/ppermute | solution.py:461
  32.5 1.9 %project.3 = (bf16[64,1536]{1,0:T(8,128)(2,1)S(1)}, bf16[64,1536]{1,0:T(8,128)(2,1)S(1)}, bf16[64,1536]{1,0:T(8,128)(2,1)S(1)}, bf16[64,1536]{1,0:T(8,128)(2,1)S...) custom-call(bf16[128,1024]{1,0:T(8,128)(2,1)S(1)} %get-tuple-element, ...), custom_call_target="tpu_custom_call" | custom-call | tf_op jit(solution)/shard_map/project/pallas_call | solution.py:325
  34.4 0.5 collective-permute-start.5
  35.0 0.4 collective-permute-start.7
  35.4 0.4 collective-permute-done.4.refs_4_
  35.9 0.3 collective-permute-done.5.refs_5_
  36.1 0.3 collective-permute-done.6.refs_6_
  36.4 0.3 collective-permute-done.7.refs_7_
  36.9 0.8 collective-permute-start.13
  37.7 3.3 %attend.4.a_ref = bf16[128,1024]{1,0:T(8,128)(2,1)S(1)} custom-call(s32[1]{0:T(128)} %bitcast.tp_ref, s32[1]{0:T(128)} %bitcast.1.rank_ref.ctx_ref, bf16[512,1024]{1,0:T(8,128)(2,1)S(1)} %copy-done.1, bf16[512,1024]{1,0:T(8,128)(2,1)S(1)} %copy-done.1, s32[3,8,128]{2,1,0:T(8,128)S(1)} %get-tuple-element.46.table_ref, ...), custom_call_target="tpu_custom_call" | custom-call | tf_op jit(solution)/shard_map/attend/pallas_call | solution.py:279
  41.1 6.6 %project.4 = (bf16[64,2048]{1,0:T(8,128)(2,1)S(1)}, bf16[64,2048]{1,0:T(8,128)(2,1)S(1)}, bf16[64,2048]{1,0:T(8,128)(2,1)S(1)}, bf16[64,2048]{1,0:T(8,128)(2,1)S...) custom-call(bf16[128,1024]{1,0:T(8,128)(2,1)S(1)} %attend.4.a_ref, ...), custom_call_target="tpu_custom_call" | custom-call | tf_op jit(solution)/shard_map/project/pallas_call | solution.py:362
  47.8 0.5 collective-permute-start.10
  48.4 0.4 collective-permute-start.12
  48.8 0.5 collective-permute-done.9.refs_4_
  49.3 0.4 collective-permute-done.10.refs_5_
  49.7 0.4 collective-permute-done.11.refs_6_
  50.1 0.4 collective-permute-done.12.refs_7_
  50.4 0.2 add.8.refs_3_
  50.7 1.4 %collective-permute-start.22 = (bf16[64,8192]{1,0:T(8,128)(2,1)S(1)}, bf16[64,8192]{1,0:T(8,128)(2,1)S(1)}, u32[]{:S(2)}, u32[]{:S(2)}) collective-permute-start(bf16[64,8192]{1,0:T(8,128)(2,1)S(1)} %add.8.refs_3_), channel_id=1, source_target_pairs={{0,2},{1,3},{2,0},{3,1},{4,6},{5,7},{6,4},{7,5},{8,10},{9,11},{10,... | collective-permute-start | bytes 3145736 | tf_op jit(solution)/shard_map/ppermute | solution.py:461
  52.0 5.3 %collective-permute-done.13.refs_4_.refs_12_ = bf16[64,6144]{1,0:T(8,128)(2,1)S(1)} collective-permute-done((bf16[64,6144]{1,0:T(8,128)(2,1)S(1)}, bf16[64,6144]{1,0:T(8,128)(2,1)S(1)}, u32[]{:S(2)}, u32[]{:S(2)}) %collective-permute-start.13) | collective-permute-done | bytes 786464 | tf_op jit(solution)/shard_map/ppermute | solution.py:461
  57.3 5.7 %attend.5.a_ref = bf16[256,1024]{1,0:T(8,128)(2,1)S(1)} custom-call(s32[1]{0:T(128)} %bitcast.tp_ref, s32[1]{0:T(128)} %bitcast.1.rank_ref.ctx_ref, bf16[512,1024]{1,0:T(8,128)(2,1)S(1)} %copy-done.1, bf16[512,1024]{1,0:T(8,128)(2,1)S(1)} %copy-done.1, s32[3,8,128]{2,1,0:T(8,128)S(1)} %get-tuple-element.46.table_ref, ...), custom_call_target="tpu_custom_call" | custom-call | tf_op jit(solution)/shard_map/attend/pallas_call | solution.py:279
  63.0 0.8 copy-done.2
  63.8 9.1 %project.5 = (bf16[128,1024]{1,0:T(8,128)(2,1)S(1)}, bf16[128,1024]{1,0:T(8,128)(2,1)S(1)}, bf16[128,1024]{1,0:T(8,128)(2,1)S(1)}, bf16[128,1024]{1,0:T(8,128)(2...) custom-call(bf16[256,1024]{1,0:T(8,128)(2,1)} %copy-done.2, ...), custom_call_target="tpu_custom_call" | custom-call | tf_op jit(solution)/shard_map/project/pallas_call | solution.py:362
  73.0 0.5 collective-permute-start.15
  73.6 0.4 collective-permute-start.17
  74.0 0.5 collective-permute-done.14.refs_2_.refs_8_
  74.7 0.2 collective-permute-done.15.refs_3_.refs_9_
  75.0 0.2 collective-permute-done.16.refs_6_.refs_10_
  75.4 0.2 collective-permute-done.17.refs_7_.refs_11_
  75.8 0.8 finish.3.refs_13_
  76.6 0.2 collective-permute-done.20.refs_10_.refs_14_
  76.8 0.4 collective-permute-done.21.refs_11_.refs_15_
  77.2 1.0 %finish.4.refs_17_ = bf16[128,8192]{1,0:T(8,128)(2,1)} custom-call(bf16[128,1024]{1,0:T(8,128)(2,1)S(1)} %get-tuple-element.71.refs_0_.refs_2_, bf16[128,1024]{1,0:T(8,128)(2,1)S(1)} %get-tuple-element.72.refs_1_.refs_3_, bf16[128,1024]{1,0:T(8,128)(2,1)S(1)} %get-tuple-element.73.refs_2_.refs_4_, ...), custom_call_target="tpu_custom_call", output_to_operand_aliasing={{}: (13, {})} | custom-call | tf_op jit(solution)/shard_map/finish/pallas_call | solution.py:423
  78.2 0.9 %collective-permute-done.22.refs_16_ = bf16[64,8192]{1,0:T(8,128)(2,1)S(1)} collective-permute-done((bf16[64,8192]{1,0:T(8,128)(2,1)S(1)}, bf16[64,8192]{1,0:T(8,128)(2,1)S(1)}, u32[]{:S(2)}, u32[]{:S(2)}) %collective-permute-start.22) | collective-permute-done | bytes 1048608 | tf_op jit(solution)/shard_map/ppermute | solution.py:461
  79.1 1.1 %finish.5 = bf16[128,8192]{1,0:T(8,128)(2,1)} custom-call(bf16[128,1024]{1,0:T(8,128)(2,1)S(1)} %get-tuple-element.69.refs_0_, bf16[128,1024]{1,0:T(8,128)(2,1)S(1)} %get-tuple-element.70.refs_1_, bf16[128,1024]{1,0:T(8,128)(2,1)S(1)} %get-tuple-element.71.refs_0_.refs_2_, ...), custom_call_target="tpu_custom_call", output_to_operand_aliasing={{}: (17, {})} | custom-call | tf_op jit(solution)/shard_map/finish/pallas_call | solution.py:423
  (29 shorter events, 1.5 us)
Async XLA Ops:
  0.0 24.7 %copy-start.1 = (bf16[512,1024]{1,0:T(8,128)(2,1)S(1)}, bf16[512,1024]{1,0:T(8,128)(2,1)}, u32[]{:S(2)}) copy-start(bf16[512,1024]{1,0:T(8,128)(2,1)} %q_1.5) | copy-start | bytes 3145732
  2.2 12.0 %all-to-all-start = ((bf16[4,128,256]{2,1,0:T(8,128)(2,1)}), bf16[4,128,256]{2,1,0:T(8,128)(2,1)S(1)}, u32[]{:S(2)}, u32[]{:S(2)}) async-start(bf16[4,128,256]{2,1,0:T(8,128)(2,1)} %get-tuple-element.49), calls=%async_computation | async-start | bytes 524288 | tf_op jit(solution)/shard_map/all_to_all | solution.py:451
  7.4 13.9 %collective-permute-start = (bf16[512,256]{1,0:T(8,128)(2,1)}, bf16[512,256]{1,0:T(8,128)(2,1)S(1)}, u32[]{:S(2)}, u32[]{:S(2)}) collective-permute-start(bf16[512,256]{1,0:T(8,128)(2,1)} %get-tuple-element.45.own_ref), channel_id=1, source_target_pairs={{0,4},{4,8},{8,12},{12,16},{16,20},{20,24},{24,28},{1,5},{5,9},{9,... | collective-permute-start | bytes 786440 | tf_op jit(solution)/shard_map/ppermute | solution.py:446
  10.8 8.6 %collective-permute-start.1 = (bf16[448,256]{1,0:T(8,128)(2,1)}, bf16[448,256]{1,0:T(8,128)(2,1)S(1)}, u32[]{:S(2)}, u32[]{:S(2)}) collective-permute-start(bf16[448,256]{1,0:T(8,128)(2,1)} %get-tuple-element.48), channel_id=1, source_target_pairs={{0,8},{4,12},{8,16},{12,20},{16,24},{20,28},{1,9},{5,13},{9,17},{1... | collective-permute-start | bytes 688136 | tf_op jit(solution)/shard_map/ppermute | solution.py:446
  14.2 10.5 %collective-permute-start.2 = (bf16[3,128,256]{2,1,0:T(8,128)(2,1)S(1)}, bf16[3,128,256]{2,1,0:T(8,128)(2,1)S(1)}, u32[]{:S(2)}, u32[]{:S(2)}) collective-permute-start(bf16[3,128,256]{2,1,0:T(8,128)(2,1)S(1)} %slice.4), channel_id=1, source_target_pairs={{0,4},{4,0},{8,12},{12,8},{16,20},{20,16},{24,28},{28,24},{1,5},{5... | collective-permute-start | bytes 589832 | tf_op jit(solution)/shard_map/ppermute | solution.py:453
  14.8 0.9 %copy-start.4 = (bf16[512,256]{1,0:T(8,128)(2,1)S(1)}, bf16[512,256]{1,0:T(8,128)(2,1)}, u32[]{:S(2)}) copy-start(bf16[512,256]{1,0:T(8,128)(2,1)} %get-tuple-element.45.own_ref) | copy-start | bytes 786436
  15.8 0.7 copy-start.5
  16.5 0.7 copy-start.6
  24.7 7.8 %copy-start = (bf16[1024,8192]{1,0:T(8,128)(2,1)S(1)}, bf16[1024,8192]{1,0:T(8,128)(2,1)}, u32[]{:S(2)}) copy-start(bf16[1024,8192]{1,0:T(8,128)(2,1)} %w_hbm.3) | copy-start | bytes 50331652
  29.2 1.6 %collective-permute-start.3 = (bf16[64,2048]{1,0:T(8,128)(2,1)S(1)}, bf16[64,2048]{1,0:T(8,128)(2,1)S(1)}, u32[]{:S(2)}, u32[]{:S(2)}) collective-permute-start(bf16[64,2048]{1,0:T(8,128)(2,1)S(1)} %get-tuple-element.52), channel_id=1, source_target_pairs={{0,1},{1,0},{2,3},{3,2},{4,5},{5,4},{6,7},{7,6},{8,9},{9,8},{10,11... | collective-permute-start | bytes 786440 | tf_op jit(solution)/shard_map/ppermute | solution.py:458
  30.9 10.1 %collective-permute-start.8 = (bf16[64,2048]{1,0:T(8,128)(2,1)S(1)}, bf16[64,2048]{1,0:T(8,128)(2,1)S(1)}, u32[]{:S(2)}, u32[]{:S(2)}) collective-permute-start(bf16[64,2048]{1,0:T(8,128)(2,1)S(1)} %add_convert_fusion.refs_0_), channel_id=1, source_target_pairs={{0,2},{1,3},{2,0},{3,1},{4,6},{5,7},{6,4},{7,5},{8,10},{9,11},{10,... | collective-permute-start | bytes 786440 | tf_op jit(solution)/shard_map/ppermute | solution.py:461
  34.3 1.5 %collective-permute-start.4 = (bf16[64,1536]{1,0:T(8,128)(2,1)S(1)}, bf16[64,1536]{1,0:T(8,128)(2,1)S(1)}, u32[]{:S(2)}, u32[]{:S(2)}) collective-permute-start(bf16[64,1536]{1,0:T(8,128)(2,1)S(1)} %get-tuple-element.57), channel_id=1, source_target_pairs={{0,1},{1,0},{2,3},{3,2},{4,5},{5,4},{6,7},{7,6},{8,9},{9,8},{10,11... | collective-permute-start | bytes 589832 | tf_op jit(solution)/shard_map/ppermute | solution.py:458
  34.4 1.7 %collective-permute-start.5 = (bf16[64,1536]{1,0:T(8,128)(2,1)S(1)}, bf16[64,1536]{1,0:T(8,128)(2,1)S(1)}, u32[]{:S(2)}, u32[]{:S(2)}) collective-permute-start(bf16[64,1536]{1,0:T(8,128)(2,1)S(1)} %get-tuple-element.58), channel_id=1, source_target_pairs={{0,1},{1,0},{2,3},{3,2},{4,5},{5,4},{6,7},{7,6},{8,9},{9,8},{10,11... | collective-permute-start | bytes 589832 | tf_op jit(solution)/shard_map/ppermute | solution.py:458
  34.9 1.5 %collective-permute-start.6 = (bf16[64,1536]{1,0:T(8,128)(2,1)S(1)}, bf16[64,1536]{1,0:T(8,128)(2,1)S(1)}, u32[]{:S(2)}, u32[]{:S(2)}) collective-permute-start(bf16[64,1536]{1,0:T(8,128)(2,1)S(1)} %get-tuple-element.59), channel_id=1, source_target_pairs={{0,1},{1,0},{2,3},{3,2},{4,5},{5,4},{6,7},{7,6},{8,9},{9,8},{10,11... | collective-permute-start | bytes 589832 | tf_op jit(solution)/shard_map/ppermute | solution.py:458
  35.0 1.7 %collective-permute-start.7 = (bf16[64,1536]{1,0:T(8,128)(2,1)S(1)}, bf16[64,1536]{1,0:T(8,128)(2,1)S(1)}, u32[]{:S(2)}, u32[]{:S(2)}) collective-permute-start(bf16[64,1536]{1,0:T(8,128)(2,1)S(1)} %get-tuple-element.60), channel_id=1, source_target_pairs={{0,1},{1,0},{2,3},{3,2},{4,5},{5,4},{6,7},{7,6},{8,9},{9,8},{10,11... | collective-permute-start | bytes 589832 | tf_op jit(solution)/shard_map/ppermute | solution.py:458
  36.9 20.4 %collective-permute-start.13 = (bf16[64,6144]{1,0:T(8,128)(2,1)S(1)}, bf16[64,6144]{1,0:T(8,128)(2,1)S(1)}, u32[]{:S(2)}, u32[]{:S(2)}) collective-permute-start(bf16[64,6144]{1,0:T(8,128)(2,1)S(1)} %add.7.refs_3_), channel_id=1, source_target_pairs={{0,2},{1,3},{2,0},{3,1},{4,6},{5,7},{6,4},{7,5},{8,10},{9,11},{10,... | collective-permute-start | bytes 2359304 | tf_op jit(solution)/shard_map/ppermute | solution.py:461
  47.7 1.6 %collective-permute-start.9 = (bf16[64,2048]{1,0:T(8,128)(2,1)S(1)}, bf16[64,2048]{1,0:T(8,128)(2,1)S(1)}, u32[]{:S(2)}, u32[]{:S(2)}) collective-permute-start(bf16[64,2048]{1,0:T(8,128)(2,1)S(1)} %get-tuple-element.65), channel_id=1, source_target_pairs={{0,1},{1,0},{2,3},{3,2},{4,5},{5,4},{6,7},{7,6},{8,9},{9,8},{10,11... | collective-permute-start | bytes 786440 | tf_op jit(solution)/shard_map/ppermute | solution.py:458
  47.8 1.9 %collective-permute-start.10 = (bf16[64,2048]{1,0:T(8,128)(2,1)S(1)}, bf16[64,2048]{1,0:T(8,128)(2,1)S(1)}, u32[]{:S(2)}, u32[]{:S(2)}) collective-permute-start(bf16[64,2048]{1,0:T(8,128)(2,1)S(1)} %get-tuple-element.66), channel_id=1, source_target_pairs={{0,1},{1,0},{2,3},{3,2},{4,5},{5,4},{6,7},{7,6},{8,9},{9,8},{10,11... | collective-permute-start | bytes 786440 | tf_op jit(solution)/shard_map/ppermute | solution.py:458
  48.3 1.8 %collective-permute-start.11 = (bf16[64,2048]{1,0:T(8,128)(2,1)S(1)}, bf16[64,2048]{1,0:T(8,128)(2,1)S(1)}, u32[]{:S(2)}, u32[]{:S(2)}) collective-permute-start(bf16[64,2048]{1,0:T(8,128)(2,1)S(1)} %get-tuple-element.67), channel_id=1, source_target_pairs={{0,1},{1,0},{2,3},{3,2},{4,5},{5,4},{6,7},{7,6},{8,9},{9,8},{10,11... | collective-permute-start | bytes 786440 | tf_op jit(solution)/shard_map/ppermute | solution.py:458
  48.4 2.1 %collective-permute-start.12 = (bf16[64,2048]{1,0:T(8,128)(2,1)S(1)}, bf16[64,2048]{1,0:T(8,128)(2,1)S(1)}, u32[]{:S(2)}, u32[]{:S(2)}) collective-permute-start(bf16[64,2048]{1,0:T(8,128)(2,1)S(1)} %get-tuple-element.68), channel_id=1, source_target_pairs={{0,1},{1,0},{2,3},{3,2},{4,5},{5,4},{6,7},{7,6},{8,9},{9,8},{10,11... | collective-permute-start | bytes 786440 | tf_op jit(solution)/shard_map/ppermute | solution.py:458
  50.7 28.4 %collective-permute-start.22 = (bf16[64,8192]{1,0:T(8,128)(2,1)S(1)}, bf16[64,8192]{1,0:T(8,128)(2,1)S(1)}, u32[]{:S(2)}, u32[]{:S(2)}) collective-permute-start(bf16[64,8192]{1,0:T(8,128)(2,1)S(1)} %add.8.refs_3_), channel_id=1, source_target_pairs={{0,2},{1,3},{2,0},{3,1},{4,6},{5,7},{6,4},{7,5},{8,10},{9,11},{10,... | collective-permute-start | bytes 3145736 | tf_op jit(solution)/shard_map/ppermute | solution.py:461
  63.0 0.8 copy-start.2
  72.9 4.3 %copy-start.3 = (bf16[128,1024]{1,0:T(8,128)(2,1)S(1)}, bf16[128,1024]{1,0:T(8,128)(2,1)}, u32[]{:S(2)}) copy-start(bf16[128,1024]{1,0:T(8,128)(2,1)} %get-tuple-element.76.refs_5_.refs_7_) | copy-start | bytes 786436
  72.9 1.6 %collective-permute-start.14 = (bf16[128,1024]{1,0:T(8,128)(2,1)S(1)}, bf16[128,1024]{1,0:T(8,128)(2,1)S(1)}, u32[]{:S(2)}, u32[]{:S(2)}) collective-permute-start(bf16[128,1024]{1,0:T(8,128)(2,1)S(1)} %get-tuple-element.77), channel_id=1, source_target_pairs={{0,1},{1,0},{2,3},{3,2},{4,5},{5,4},{6,7},{7,6},{8,9},{9,8},{10,11... | collective-permute-start | bytes 786440 | tf_op jit(solution)/shard_map/ppermute | solution.py:458
  73.0 1.9 %collective-permute-start.15 = (bf16[128,1024]{1,0:T(8,128)(2,1)S(1)}, bf16[128,1024]{1,0:T(8,128)(2,1)S(1)}, u32[]{:S(2)}, u32[]{:S(2)}) collective-permute-start(bf16[128,1024]{1,0:T(8,128)(2,1)S(1)} %get-tuple-element.78), channel_id=1, source_target_pairs={{0,1},{1,0},{2,3},{3,2},{4,5},{5,4},{6,7},{7,6},{8,9},{9,8},{10,11... | collective-permute-start | bytes 786440 | tf_op jit(solution)/shard_map/ppermute | solution.py:458
  73.5 1.8 %collective-permute-start.16 = (bf16[128,1024]{1,0:T(8,128)(2,1)S(1)}, bf16[128,1024]{1,0:T(8,128)(2,1)S(1)}, u32[]{:S(2)}, u32[]{:S(2)}) collective-permute-start(bf16[128,1024]{1,0:T(8,128)(2,1)S(1)} %get-tuple-element.79), channel_id=1, source_target_pairs={{0,1},{1,0},{2,3},{3,2},{4,5},{5,4},{6,7},{7,6},{8,9},{9,8},{10,11... | collective-permute-start | bytes 786440 | tf_op jit(solution)/shard_map/ppermute | solution.py:458
  73.6 2.1 %collective-permute-start.17 = (bf16[128,1024]{1,0:T(8,128)(2,1)S(1)}, bf16[128,1024]{1,0:T(8,128)(2,1)S(1)}, u32[]{:S(2)}, u32[]{:S(2)}) collective-permute-start(bf16[128,1024]{1,0:T(8,128)(2,1)S(1)} %get-tuple-element.80), channel_id=1, source_target_pairs={{0,1},{1,0},{2,3},{3,2},{4,5},{5,4},{6,7},{7,6},{8,9},{9,8},{10,11... | collective-permute-start | bytes 786440 | tf_op jit(solution)/shard_map/ppermute | solution.py:458
  74.5 2.1 %collective-permute-start.18 = (bf16[128,1024]{1,0:T(8,128)(2,1)S(1)}, bf16[128,1024]{1,0:T(8,128)(2,1)S(1)}, u32[]{:S(2)}, u32[]{:S(2)}) collective-permute-start(bf16[128,1024]{1,0:T(8,128)(2,1)S(1)} %get-tuple-element.81), channel_id=1, source_target_pairs={{0,1},{1,0},{2,3},{3,2},{4,5},{5,4},{6,7},{7,6},{8,9},{9,8},{10,11... | collective-permute-start | bytes 786440 | tf_op jit(solution)/shard_map/ppermute | solution.py:458
  74.9 1.7 %collective-permute-start.19 = (bf16[128,1024]{1,0:T(8,128)(2,1)S(1)}, bf16[128,1024]{1,0:T(8,128)(2,1)S(1)}, u32[]{:S(2)}, u32[]{:S(2)}) collective-permute-start(bf16[128,1024]{1,0:T(8,128)(2,1)S(1)} %get-tuple-element.82), channel_id=1, source_target_pairs={{0,1},{1,0},{2,3},{3,2},{4,5},{5,4},{6,7},{7,6},{8,9},{9,8},{10,11... | collective-permute-start | bytes 786440 | tf_op jit(solution)/shard_map/ppermute | solution.py:458
  75.3 1.5 %collective-permute-start.20 = (bf16[128,1024]{1,0:T(8,128)(2,1)S(1)}, bf16[128,1024]{1,0:T(8,128)(2,1)S(1)}, u32[]{:S(2)}, u32[]{:S(2)}) collective-permute-start(bf16[128,1024]{1,0:T(8,128)(2,1)S(1)} %get-tuple-element.83), channel_id=1, source_target_pairs={{0,1},{1,0},{2,3},{3,2},{4,5},{5,4},{6,7},{7,6},{8,9},{9,8},{10,11... | collective-permute-start | bytes 786440 | tf_op jit(solution)/shard_map/ppermute | solution.py:458
  75.6 1.5 %collective-permute-start.21 = (bf16[128,1024]{1,0:T(8,128)(2,1)S(1)}, bf16[128,1024]{1,0:T(8,128)(2,1)S(1)}, u32[]{:S(2)}, u32[]{:S(2)}) collective-permute-start(bf16[128,1024]{1,0:T(8,128)(2,1)S(1)} %get-tuple-element.84), channel_id=1, source_target_pairs={{0,1},{1,0},{2,3},{3,2},{4,5},{5,4},{6,7},{7,6},{8,9},{9,8},{10,11... | collective-permute-start | bytes 786440 | tf_op jit(solution)/shard_map/ppermute | solution.py:458

commit v20 on v16

--- a/solution.py
+++ b/solution.py
@@ -471,8 +471,8 @@
     (attended,) = attention((((3, 1), (2, 1)),), 0, (total,))
     total = exchanged(*project(attended, out_weight, 0, 4, (arrived[0],)))
     arrived.append(across(total))
-    (attended,) = attention((((1, 0), (1, 1)), ((0, 0), (0, 1))), 0, (total, arrived[1]))
-    send, keep = project(attended, out_weight, 0, tiles, ())
+    (attended,) = attention((((1, 0), (1, 1)), ((0, 0), (0, 1))), 0, (total,))
+    send, keep = project(attended, out_weight, 0, tiles, (arrived[1],))
     got = [sibling(x) for x in send]
     shape = (queries.shape[0] // 4, width)
     out = finish(keep[:HEAD], got[:HEAD], arrived[0], 0, 0, shape, None)

time: 80.7 us -> 80.7 us (level)
  waiting for transfers between devices: 19.9 us -> 19 us
  local copies, waits for them, and re-layouts: 3.14 us -> 4.02 us
    ppermute x3, waiting for transfers between devices: 6.27 us -> 5.37 us  [across(): return lax.ppermute(x, 'tp', [(j, j ^ 2) for j in range(4)])]
    unnamed x14 -> x18, local copies, waits for them, and re-layouts: 3.12 us -> 4.01 us
  transfers between devices with their start and end apart: 24 -> 24, of which waited for: 20 -> 19; matrix products, arithmetic and copies ran while one was open for 0% -> 0% of each run, Pallas kernels for 36% -> 36%
where the time goes in v20:
time: 80.7 us; the launch traced here: 80.3 us
  Pallas kernels  36.7 us (45%)
  starting transfers between devices  20.2 us (25%)
  waiting for transfers between devices  19 us (24%)
  local copies, waits for them, and re-layouts  4.02 us (5%)
    pallas_call x2, Pallas kernels, project(): pl.pallas_call(functools.partial(project_kernel, first), out_shape=[part]...  15.7 us
    pallas_call x3, Pallas kernels, attend(): pl.pallas_call(functools.partial(attend_kernel, slots, tiles, sizes, plac...  13.5 us
    ppermute x2, starting transfers between devices, shifted(): return lax.ppermute(x, 'ctx', [(r, r + by) for r in range(ctx_size - by)])  6.79 us
    ppermute x17, waiting for transfers between devices, sibling(): return lax.ppermute(x, 'tp', [(j, j ^ 1) for j in range(4)])  6.23 us
    ppermute x3, waiting for transfers between devices, across(): return lax.ppermute(x, 'tp', [(j, j ^ 2) for j in range(4)])  5.37 us
    all_to_all x1, starting transfers between devices, shards(): lax.all_to_all(pair, 'ctx', 0, 0, axis_index_groups=parities, tiled=True)  5.2 us
    unnamed x18, local copies, waits for them, and re-layouts  4.01 us
    ppermute x2, waiting for transfers between devices, shifted(): return lax.ppermute(x, 'ctx', [(r, r + by) for r in range(ctx_size - by)])  3.94 us
  transfers between devices with their start and end apart: 24, of which 19 were waited for; matrix products, arithmetic and copies ran while one was open for 0% of the time, Pallas kernels for 36%

profile of v20, /device:TPU:16, one launch (start us, length us, event | category | flops | bytes accessed | tf_op | source)
XLA Modules:
  0.0 80.3 jit_solution(13941546947989934377)
XLA Ops:
  0.0 2.2 %pick.1 = (bf16[512,256]{1,0:T(8,128)(2,1)}, bf16[448,256]{1,0:T(8,128)(2,1)}, bf16[4,128,256]{2,1,0:T(8,128)(2,1)}) custom-call(s32[1]{0:T(128)} %bitcast.1.rank_ref.ctx_ref, s32[8,16]{1,0:T(8,128)} %vert_ref.3, bf16[512,128]{1,0:T(8,128)(2,1)} %k_ref.1, bf16[512,128]{1,0:T(8,128)(2,1)} %v_ref.1), custom_call_target="tpu_custom_call" | custom-call | tf_op jit(solution)/shard_map/pick/pallas_call | solution.py:65
  2.2 5.2 %all-to-all-start = ((bf16[4,128,256]{2,1,0:T(8,128)(2,1)}), bf16[4,128,256]{2,1,0:T(8,128)(2,1)S(1)}, u32[]{:S(2)}, u32[]{:S(2)}) async-start(bf16[4,128,256]{2,1,0:T(8,128)(2,1)} %get-tuple-element.49), calls=%async_computation | async-start | bytes 524288 | tf_op jit(solution)/shard_map/all_to_all | solution.py:442
  7.4 3.4 %collective-permute-start = (bf16[512,256]{1,0:T(8,128)(2,1)}, bf16[512,256]{1,0:T(8,128)(2,1)S(1)}, u32[]{:S(2)}, u32[]{:S(2)}) collective-permute-start(bf16[512,256]{1,0:T(8,128)(2,1)} %get-tuple-element.45.own_ref), channel_id=1, source_target_pairs={{0,4},{4,8},{8,12},{12,16},{16,20},{20,24},{24,28},{1,5},{5,9},{9,... | collective-permute-start | bytes 786440 | tf_op jit(solution)/shard_map/ppermute | solution.py:437
  10.8 3.4 %collective-permute-start.1 = (bf16[448,256]{1,0:T(8,128)(2,1)}, bf16[448,256]{1,0:T(8,128)(2,1)S(1)}, u32[]{:S(2)}, u32[]{:S(2)}) collective-permute-start(bf16[448,256]{1,0:T(8,128)(2,1)} %get-tuple-element.48), channel_id=1, source_target_pairs={{0,8},{4,12},{8,16},{12,20},{16,24},{20,28},{1,9},{5,13},{9,17},{1... | collective-permute-start | bytes 688136 | tf_op jit(solution)/shard_map/ppermute | solution.py:437
  14.2 0.6 collective-permute-start.2
  14.8 0.9 %copy-done.6 = bf16[512,256]{1,0:T(8,128)(2,1)S(1)} copy-done((bf16[512,256]{1,0:T(8,128)(2,1)S(1)}, bf16[512,256]{1,0:T(8,128)(2,1)}, u32[]{:S(2)}) %copy-start.6) | copy-done | bytes 262168
  15.8 0.7 copy-done.7
  16.5 0.7 copy-done.8
  17.3 2.1 %collective-permute-done.1.kv_2 = bf16[448,256]{1,0:T(8,128)(2,1)S(1)} collective-permute-done((bf16[448,256]{1,0:T(8,128)(2,1)}, bf16[448,256]{1,0:T(8,128)(2,1)S(1)}, u32[]{:S(2)}, u32[]{:S(2)}) %collective-permute-start.1) | collective-permute-done | bytes 229408 | tf_op jit(solution)/shard_map/ppermute | solution.py:437
  19.4 1.8 %collective-permute-done.kv_1 = bf16[512,256]{1,0:T(8,128)(2,1)S(1)} collective-permute-done((bf16[512,256]{1,0:T(8,128)(2,1)}, bf16[512,256]{1,0:T(8,128)(2,1)S(1)}, u32[]{:S(2)}, u32[]{:S(2)}) %collective-permute-start) | collective-permute-done | bytes 262176 | tf_op jit(solution)/shard_map/ppermute | solution.py:437
  21.3 3.4 %collective-permute-done.2.refs_1_ = bf16[3,128,256]{2,1,0:T(8,128)(2,1)S(1)} collective-permute-done((bf16[3,128,256]{2,1,0:T(8,128)(2,1)S(1)}, bf16[3,128,256]{2,1,0:T(8,128)(2,1)S(1)}, u32[]{:S(2)}, u32[]{:S(2)}) %collective-permute-start.2) | collective-permute-done | bytes 196640 | tf_op jit(solution)/shard_map/ppermute | solution.py:444
  24.7 4.5 %attend.3 = (bf16[128,1024]{1,0:T(8,128)(2,1)S(1)}, bf16[64,2048]{1,0:T(8,128)(2,1)S(1)}, bf16[64,2048]{1,0:T(8,128)(2,1)S(1)}) custom-call(s32[1]{0:T(128)} %bitcast.tp_ref, s32[1]{0:T(128)} %bitcast.1.rank_ref.ctx_ref, bf16[512,1024]{1,0:T(8,128)(2,1)S(1)} %copy-done.1, bf16[512,1024]{1,0:T(8,128)(2,1)S(1)} %copy-done.1, ...), custom_call_target="tpu_custom_call" | custom-call | tf_op jit(solution)/shard_map/attend/pallas_call | solution.py:270
  29.3 1.5 %collective-permute-done.3 = bf16[64,2048]{1,0:T(8,128)(2,1)S(1)} collective-permute-done((bf16[64,2048]{1,0:T(8,128)(2,1)S(1)}, bf16[64,2048]{1,0:T(8,128)(2,1)S(1)}, u32[]{:S(2)}, u32[]{:S(2)}) %collective-permute-start.3) | collective-permute-done | bytes 262176 | tf_op jit(solution)/shard_map/ppermute | solution.py:449
  30.9 1.6 %collective-permute-start.8 = (bf16[64,2048]{1,0:T(8,128)(2,1)S(1)}, bf16[64,2048]{1,0:T(8,128)(2,1)S(1)}, u32[]{:S(2)}, u32[]{:S(2)}) collective-permute-start(bf16[64,2048]{1,0:T(8,128)(2,1)S(1)} %add_convert_fusion.refs_0_), channel_id=1, source_target_pairs={{0,2},{1,3},{2,0},{3,1},{4,6},{5,7},{6,4},{7,5},{8,10},{9,11},{10,... | collective-permute-start | bytes 786440 | tf_op jit(solution)/shard_map/ppermute | solution.py:452
  32.4 1.9 %project.3 = (bf16[64,1536]{1,0:T(8,128)(2,1)S(1)}, bf16[64,1536]{1,0:T(8,128)(2,1)S(1)}, bf16[64,1536]{1,0:T(8,128)(2,1)S(1)}, bf16[64,1536]{1,0:T(8,128)(2,1)S...) custom-call(bf16[128,1024]{1,0:T(8,128)(2,1)S(1)} %get-tuple-element, ...), custom_call_target="tpu_custom_call" | custom-call | tf_op jit(solution)/shard_map/project/pallas_call | solution.py:316
  34.4 0.5 collective-permute-start.5
  34.9 0.4 collective-permute-start.7
  35.4 0.4 collective-permute-done.4.refs_4_
  35.8 0.3 collective-permute-done.5.refs_5_
  36.1 0.3 collective-permute-done.6.refs_6_
  36.4 0.3 collective-permute-done.7.refs_7_
  36.8 0.9 %collective-permute-start.13 = (bf16[64,6144]{1,0:T(8,128)(2,1)S(1)}, bf16[64,6144]{1,0:T(8,128)(2,1)S(1)}, u32[]{:S(2)}, u32[]{:S(2)}) collective-permute-start(bf16[64,6144]{1,0:T(8,128)(2,1)S(1)} %add.7.refs_3_), channel_id=1, source_target_pairs={{0,2},{1,3},{2,0},{3,1},{4,6},{5,7},{6,4},{7,5},{8,10},{9,11},{10,... | collective-permute-start | bytes 2359304 | tf_op jit(solution)/shard_map/ppermute | solution.py:452
  37.7 3.3 %attend.4.a_ref = bf16[128,1024]{1,0:T(8,128)(2,1)S(1)} custom-call(s32[1]{0:T(128)} %bitcast.tp_ref, s32[1]{0:T(128)} %bitcast.1.rank_ref.ctx_ref, bf16[512,1024]{1,0:T(8,128)(2,1)S(1)} %copy-done.1, bf16[512,1024]{1,0:T(8,128)(2,1)S(1)} %copy-done.1, s32[3,8,128]{2,1,0:T(8,128)S(1)} %get-tuple-element.46.table_ref, ...), custom_call_target="tpu_custom_call" | custom-call | tf_op jit(solution)/shard_map/attend/pallas_call | solution.py:270
  41.0 6.6 %project.4 = (bf16[64,2048]{1,0:T(8,128)(2,1)S(1)}, bf16[64,2048]{1,0:T(8,128)(2,1)S(1)}, bf16[64,2048]{1,0:T(8,128)(2,1)S(1)}, bf16[64,2048]{1,0:T(8,128)(2,1)S...) custom-call(bf16[128,1024]{1,0:T(8,128)(2,1)S(1)} %attend.4.a_ref, ...), custom_call_target="tpu_custom_call" | custom-call | tf_op jit(solution)/shard_map/project/pallas_call | solution.py:353
  47.8 0.5 collective-permute-start.10
  48.4 0.4 collective-permute-start.12
  48.8 0.5 collective-permute-done.9.refs_4_
  49.3 0.4 collective-permute-done.10.refs_5_
  49.7 0.4 collective-permute-done.11.refs_6_
  50.0 0.4 collective-permute-done.12.refs_7_
  50.4 0.2 add.8.refs_3_
  50.7 1.3 %collective-permute-start.22 = (bf16[64,8192]{1,0:T(8,128)(2,1)S(1)}, bf16[64,8192]{1,0:T(8,128)(2,1)S(1)}, u32[]{:S(2)}, u32[]{:S(2)}) collective-permute-start(bf16[64,8192]{1,0:T(8,128)(2,1)S(1)} %add.8.refs_3_), channel_id=1, source_target_pairs={{0,2},{1,3},{2,0},{3,1},{4,6},{5,7},{6,4},{7,5},{8,10},{9,11},{10,... | collective-permute-start | bytes 3145736 | tf_op jit(solution)/shard_map/ppermute | solution.py:452
  52.0 5.7 %attend.5.a_ref = bf16[256,1024]{1,0:T(8,128)(2,1)S(1)} custom-call(s32[1]{0:T(128)} %bitcast.tp_ref, s32[1]{0:T(128)} %bitcast.1.rank_ref.ctx_ref, bf16[512,1024]{1,0:T(8,128)(2,1)S(1)} %copy-done.1, bf16[512,1024]{1,0:T(8,128)(2,1)S(1)} %copy-done.1, s32[3,8,128]{2,1,0:T(8,128)S(1)} %get-tuple-element.46.table_ref, ...), custom_call_target="tpu_custom_call" | custom-call | tf_op jit(solution)/shard_map/attend/pallas_call | solution.py:270
  57.6 0.8 copy-done.4
  58.4 0.9 %copy-done.2 = bf16[64,6144]{1,0:T(8,128)(2,1)} copy-done((bf16[64,6144]{1,0:T(8,128)(2,1)}, bf16[64,6144]{1,0:T(8,128)(2,1)S(1)}, u32[]{:S(2)}) %copy-start.2) | copy-done | bytes 786456
  59.3 9.1 %project.5 = (bf16[128,1024]{1,0:T(8,128)(2,1)S(1)}, bf16[128,1024]{1,0:T(8,128)(2,1)S(1)}, bf16[128,1024]{1,0:T(8,128)(2,1)S(1)}, bf16[128,1024]{1,0:T(8,128)(2...) custom-call(bf16[256,1024]{1,0:T(8,128)(2,1)} %copy-done.4, ...), custom_call_target="tpu_custom_call" | custom-call | tf_op jit(solution)/shard_map/project/pallas_call | solution.py:353
  68.5 0.5 collective-permute-start.15
  69.1 0.4 collective-permute-start.17
  69.5 0.5 collective-permute-done.14.refs_2_.refs_8_
  70.2 0.2 collective-permute-done.15.refs_3_.refs_9_
  70.5 0.2 collective-permute-done.16.refs_6_.refs_10_
  70.9 0.2 collective-permute-done.17.refs_7_.refs_11_
  71.3 0.8 finish.3.refs_13_
  72.1 0.2 collective-permute-done.20.refs_10_.refs_14_
  72.3 0.4 collective-permute-done.21.refs_11_.refs_15_
  72.7 1.0 %finish.4.refs_17_ = bf16[128,8192]{1,0:T(8,128)(2,1)} custom-call(bf16[128,1024]{1,0:T(8,128)(2,1)S(1)} %get-tuple-element.71.refs_0_.refs_2_, bf16[128,1024]{1,0:T(8,128)(2,1)S(1)} %get-tuple-element.72.refs_1_.refs_3_, bf16[128,1024]{1,0:T(8,128)(2,1)S(1)} %get-tuple-element.73.refs_2_.refs_4_, ...), custom_call_target="tpu_custom_call", output_to_operand_aliasing={{}: (13, {})} | custom-call | tf_op jit(solution)/shard_map/finish/pallas_call | solution.py:414
  73.7 5.4 %collective-permute-done.22.refs_16_ = bf16[64,8192]{1,0:T(8,128)(2,1)S(1)} collective-permute-done((bf16[64,8192]{1,0:T(8,128)(2,1)S(1)}, bf16[64,8192]{1,0:T(8,128)(2,1)S(1)}, u32[]{:S(2)}, u32[]{:S(2)}) %collective-permute-start.22) | collective-permute-done | bytes 1048608 | tf_op jit(solution)/shard_map/ppermute | solution.py:452
  79.0 1.1 %finish.5 = bf16[128,8192]{1,0:T(8,128)(2,1)} custom-call(bf16[128,1024]{1,0:T(8,128)(2,1)S(1)} %get-tuple-element.69.refs_0_, bf16[128,1024]{1,0:T(8,128)(2,1)S(1)} %get-tuple-element.70.refs_1_, bf16[128,1024]{1,0:T(8,128)(2,1)S(1)} %get-tuple-element.71.refs_0_.refs_2_, ...), custom_call_target="tpu_custom_call", output_to_operand_aliasing={{}: (17, {})} | custom-call | tf_op jit(solution)/shard_map/finish/pallas_call | solution.py:414
  (33 shorter events, 1.5 us)
Async XLA Ops:
  0.0 24.7 %copy-start.1 = (bf16[512,1024]{1,0:T(8,128)(2,1)S(1)}, bf16[512,1024]{1,0:T(8,128)(2,1)}, u32[]{:S(2)}) copy-start(bf16[512,1024]{1,0:T(8,128)(2,1)} %q_1.5) | copy-start | bytes 3145732
  2.2 12.0 %all-to-all-start = ((bf16[4,128,256]{2,1,0:T(8,128)(2,1)}), bf16[4,128,256]{2,1,0:T(8,128)(2,1)S(1)}, u32[]{:S(2)}, u32[]{:S(2)}) async-start(bf16[4,128,256]{2,1,0:T(8,128)(2,1)} %get-tuple-element.49), calls=%async_computation | async-start | bytes 524288 | tf_op jit(solution)/shard_map/all_to_all | solution.py:442
  7.4 13.9 %collective-permute-start = (bf16[512,256]{1,0:T(8,128)(2,1)}, bf16[512,256]{1,0:T(8,128)(2,1)S(1)}, u32[]{:S(2)}, u32[]{:S(2)}) collective-permute-start(bf16[512,256]{1,0:T(8,128)(2,1)} %get-tuple-element.45.own_ref), channel_id=1, source_target_pairs={{0,4},{4,8},{8,12},{12,16},{16,20},{20,24},{24,28},{1,5},{5,9},{9,... | collective-permute-start | bytes 786440 | tf_op jit(solution)/shard_map/ppermute | solution.py:437
  10.8 8.6 %collective-permute-start.1 = (bf16[448,256]{1,0:T(8,128)(2,1)}, bf16[448,256]{1,0:T(8,128)(2,1)S(1)}, u32[]{:S(2)}, u32[]{:S(2)}) collective-permute-start(bf16[448,256]{1,0:T(8,128)(2,1)} %get-tuple-element.48), channel_id=1, source_target_pairs={{0,8},{4,12},{8,16},{12,20},{16,24},{20,28},{1,9},{5,13},{9,17},{1... | collective-permute-start | bytes 688136 | tf_op jit(solution)/shard_map/ppermute | solution.py:437
  14.2 10.5 %collective-permute-start.2 = (bf16[3,128,256]{2,1,0:T(8,128)(2,1)S(1)}, bf16[3,128,256]{2,1,0:T(8,128)(2,1)S(1)}, u32[]{:S(2)}, u32[]{:S(2)}) collective-permute-start(bf16[3,128,256]{2,1,0:T(8,128)(2,1)S(1)} %slice.4), channel_id=1, source_target_pairs={{0,4},{4,0},{8,12},{12,8},{16,20},{20,16},{24,28},{28,24},{1,5},{5... | collective-permute-start | bytes 589832 | tf_op jit(solution)/shard_map/ppermute | solution.py:444
  14.8 0.9 %copy-start.6 = (bf16[512,256]{1,0:T(8,128)(2,1)S(1)}, bf16[512,256]{1,0:T(8,128)(2,1)}, u32[]{:S(2)}) copy-start(bf16[512,256]{1,0:T(8,128)(2,1)} %get-tuple-element.45.own_ref) | copy-start | bytes 786436
  15.8 0.7 copy-start.7
  16.5 0.7 copy-start.8
  24.7 7.7 %copy-start = (bf16[1024,8192]{1,0:T(8,128)(2,1)S(1)}, bf16[1024,8192]{1,0:T(8,128)(2,1)}, u32[]{:S(2)}) copy-start(bf16[1024,8192]{1,0:T(8,128)(2,1)} %w_hbm.3) | copy-start | bytes 50331652
  29.2 1.6 %collective-permute-start.3 = (bf16[64,2048]{1,0:T(8,128)(2,1)S(1)}, bf16[64,2048]{1,0:T(8,128)(2,1)S(1)}, u32[]{:S(2)}, u32[]{:S(2)}) collective-permute-start(bf16[64,2048]{1,0:T(8,128)(2,1)S(1)} %get-tuple-element.52), channel_id=1, source_target_pairs={{0,1},{1,0},{2,3},{3,2},{4,5},{5,4},{6,7},{7,6},{8,9},{9,8},{10,11... | collective-permute-start | bytes 786440 | tf_op jit(solution)/shard_map/ppermute | solution.py:449
  30.9 10.2 %collective-permute-start.8 = (bf16[64,2048]{1,0:T(8,128)(2,1)S(1)}, bf16[64,2048]{1,0:T(8,128)(2,1)S(1)}, u32[]{:S(2)}, u32[]{:S(2)}) collective-permute-start(bf16[64,2048]{1,0:T(8,128)(2,1)S(1)} %add_convert_fusion.refs_0_), channel_id=1, source_target_pairs={{0,2},{1,3},{2,0},{3,1},{4,6},{5,7},{6,4},{7,5},{8,10},{9,11},{10,... | collective-permute-start | bytes 786440 | tf_op jit(solution)/shard_map/ppermute | solution.py:452
  34.3 1.5 %collective-permute-start.4 = (bf16[64,1536]{1,0:T(8,128)(2,1)S(1)}, bf16[64,1536]{1,0:T(8,128)(2,1)S(1)}, u32[]{:S(2)}, u32[]{:S(2)}) collective-permute-start(bf16[64,1536]{1,0:T(8,128)(2,1)S(1)} %get-tuple-element.57), channel_id=1, source_target_pairs={{0,1},{1,0},{2,3},{3,2},{4,5},{5,4},{6,7},{7,6},{8,9},{9,8},{10,11... | collective-permute-start | bytes 589832 | tf_op jit(solution)/shard_map/ppermute | solution.py:449
  34.4 1.7 %collective-permute-start.5 = (bf16[64,1536]{1,0:T(8,128)(2,1)S(1)}, bf16[64,1536]{1,0:T(8,128)(2,1)S(1)}, u32[]{:S(2)}, u32[]{:S(2)}) collective-permute-start(bf16[64,1536]{1,0:T(8,128)(2,1)S(1)} %get-tuple-element.58), channel_id=1, source_target_pairs={{0,1},{1,0},{2,3},{3,2},{4,5},{5,4},{6,7},{7,6},{8,9},{9,8},{10,11... | collective-permute-start | bytes 589832 | tf_op jit(solution)/shard_map/ppermute | solution.py:449
  34.9 1.5 %collective-permute-start.6 = (bf16[64,1536]{1,0:T(8,128)(2,1)S(1)}, bf16[64,1536]{1,0:T(8,128)(2,1)S(1)}, u32[]{:S(2)}, u32[]{:S(2)}) collective-permute-start(bf16[64,1536]{1,0:T(8,128)(2,1)S(1)} %get-tuple-element.59), channel_id=1, source_target_pairs={{0,1},{1,0},{2,3},{3,2},{4,5},{5,4},{6,7},{7,6},{8,9},{9,8},{10,11... | collective-permute-start | bytes 589832 | tf_op jit(solution)/shard_map/ppermute | solution.py:449
  34.9 1.7 %collective-permute-start.7 = (bf16[64,1536]{1,0:T(8,128)(2,1)S(1)}, bf16[64,1536]{1,0:T(8,128)(2,1)S(1)}, u32[]{:S(2)}, u32[]{:S(2)}) collective-permute-start(bf16[64,1536]{1,0:T(8,128)(2,1)S(1)} %get-tuple-element.60), channel_id=1, source_target_pairs={{0,1},{1,0},{2,3},{3,2},{4,5},{5,4},{6,7},{7,6},{8,9},{9,8},{10,11... | collective-permute-start | bytes 589832 | tf_op jit(solution)/shard_map/ppermute | solution.py:449
  36.8 21.6 %collective-permute-start.13 = (bf16[64,6144]{1,0:T(8,128)(2,1)S(1)}, bf16[64,6144]{1,0:T(8,128)(2,1)S(1)}, u32[]{:S(2)}, u32[]{:S(2)}) collective-permute-start(bf16[64,6144]{1,0:T(8,128)(2,1)S(1)} %add.7.refs_3_), channel_id=1, source_target_pairs={{0,2},{1,3},{2,0},{3,1},{4,6},{5,7},{6,4},{7,5},{8,10},{9,11},{10,... | collective-permute-start | bytes 2359304 | tf_op jit(solution)/shard_map/ppermute | solution.py:452
  47.7 1.6 %collective-permute-start.9 = (bf16[64,2048]{1,0:T(8,128)(2,1)S(1)}, bf16[64,2048]{1,0:T(8,128)(2,1)S(1)}, u32[]{:S(2)}, u32[]{:S(2)}) collective-permute-start(bf16[64,2048]{1,0:T(8,128)(2,1)S(1)} %get-tuple-element.65), channel_id=1, source_target_pairs={{0,1},{1,0},{2,3},{3,2},{4,5},{5,4},{6,7},{7,6},{8,9},{9,8},{10,11... | collective-permute-start | bytes 786440 | tf_op jit(solution)/shard_map/ppermute | solution.py:449
  47.8 1.9 %collective-permute-start.10 = (bf16[64,2048]{1,0:T(8,128)(2,1)S(1)}, bf16[64,2048]{1,0:T(8,128)(2,1)S(1)}, u32[]{:S(2)}, u32[]{:S(2)}) collective-permute-start(bf16[64,2048]{1,0:T(8,128)(2,1)S(1)} %get-tuple-element.66), channel_id=1, source_target_pairs={{0,1},{1,0},{2,3},{3,2},{4,5},{5,4},{6,7},{7,6},{8,9},{9,8},{10,11... | collective-permute-start | bytes 786440 | tf_op jit(solution)/shard_map/ppermute | solution.py:449
  48.3 1.8 %collective-permute-start.11 = (bf16[64,2048]{1,0:T(8,128)(2,1)S(1)}, bf16[64,2048]{1,0:T(8,128)(2,1)S(1)}, u32[]{:S(2)}, u32[]{:S(2)}) collective-permute-start(bf16[64,2048]{1,0:T(8,128)(2,1)S(1)} %get-tuple-element.67), channel_id=1, source_target_pairs={{0,1},{1,0},{2,3},{3,2},{4,5},{5,4},{6,7},{7,6},{8,9},{9,8},{10,11... | collective-permute-start | bytes 786440 | tf_op jit(solution)/shard_map/ppermute | solution.py:449
  48.4 2.1 %collective-permute-start.12 = (bf16[64,2048]{1,0:T(8,128)(2,1)S(1)}, bf16[64,2048]{1,0:T(8,128)(2,1)S(1)}, u32[]{:S(2)}, u32[]{:S(2)}) collective-permute-start(bf16[64,2048]{1,0:T(8,128)(2,1)S(1)} %get-tuple-element.68), channel_id=1, source_target_pairs={{0,1},{1,0},{2,3},{3,2},{4,5},{5,4},{6,7},{7,6},{8,9},{9,8},{10,11... | collective-permute-start | bytes 786440 | tf_op jit(solution)/shard_map/ppermute | solution.py:449
  50.7 28.4 %collective-permute-start.22 = (bf16[64,8192]{1,0:T(8,128)(2,1)S(1)}, bf16[64,8192]{1,0:T(8,128)(2,1)S(1)}, u32[]{:S(2)}, u32[]{:S(2)}) collective-permute-start(bf16[64,8192]{1,0:T(8,128)(2,1)S(1)} %add.8.refs_3_), channel_id=1, source_target_pairs={{0,2},{1,3},{2,0},{3,1},{4,6},{5,7},{6,4},{7,5},{8,10},{9,11},{10,... | collective-permute-start | bytes 3145736 | tf_op jit(solution)/shard_map/ppermute | solution.py:452
  57.6 0.8 copy-start.4
  58.4 0.9 %copy-start.2 = (bf16[64,6144]{1,0:T(8,128)(2,1)}, bf16[64,6144]{1,0:T(8,128)(2,1)S(1)}, u32[]{:S(2)}) copy-start(bf16[64,6144]{1,0:T(8,128)(2,1)S(1)} %collective-permute-done.13.refs_0_.refs_12_) | copy-start | bytes 2359300
  68.4 4.3 %copy-start.3 = (bf16[64,6144]{1,0:T(8,128)(2,1)S(1)}, bf16[64,6144]{1,0:T(8,128)(2,1)}, u32[]{:S(2)}) copy-start(bf16[64,6144]{1,0:T(8,128)(2,1)} %copy-done.2) | copy-start | bytes 2359300
  68.4 4.3 %copy-start.5 = (bf16[128,1024]{1,0:T(8,128)(2,1)S(1)}, bf16[128,1024]{1,0:T(8,128)(2,1)}, u32[]{:S(2)}) copy-start(bf16[128,1024]{1,0:T(8,128)(2,1)} %get-tuple-element.76.refs_5_.refs_7_) | copy-start | bytes 786436
  68.4 1.6 %collective-permute-start.14 = (bf16[128,1024]{1,0:T(8,128)(2,1)S(1)}, bf16[128,1024]{1,0:T(8,128)(2,1)S(1)}, u32[]{:S(2)}, u32[]{:S(2)}) collective-permute-start(bf16[128,1024]{1,0:T(8,128)(2,1)S(1)} %get-tuple-element.77), channel_id=1, source_target_pairs={{0,1},{1,0},{2,3},{3,2},{4,5},{5,4},{6,7},{7,6},{8,9},{9,8},{10,11... | collective-permute-start | bytes 786440 | tf_op jit(solution)/shard_map/ppermute | solution.py:449
  68.5 1.9 %collective-permute-start.15 = (bf16[128,1024]{1,0:T(8,128)(2,1)S(1)}, bf16[128,1024]{1,0:T(8,128)(2,1)S(1)}, u32[]{:S(2)}, u32[]{:S(2)}) collective-permute-start(bf16[128,1024]{1,0:T(8,128)(2,1)S(1)} %get-tuple-element.78), channel_id=1, source_target_pairs={{0,1},{1,0},{2,3},{3,2},{4,5},{5,4},{6,7},{7,6},{8,9},{9,8},{10,11... | collective-permute-start | bytes 786440 | tf_op jit(solution)/shard_map/ppermute | solution.py:449
  69.0 1.8 %collective-permute-start.16 = (bf16[128,1024]{1,0:T(8,128)(2,1)S(1)}, bf16[128,1024]{1,0:T(8,128)(2,1)S(1)}, u32[]{:S(2)}, u32[]{:S(2)}) collective-permute-start(bf16[128,1024]{1,0:T(8,128)(2,1)S(1)} %get-tuple-element.79), channel_id=1, source_target_pairs={{0,1},{1,0},{2,3},{3,2},{4,5},{5,4},{6,7},{7,6},{8,9},{9,8},{10,11... | collective-permute-start | bytes 786440 | tf_op jit(solution)/shard_map/ppermute | solution.py:449
  69.1 2.1 %collective-permute-start.17 = (bf16[128,1024]{1,0:T(8,128)(2,1)S(1)}, bf16[128,1024]{1,0:T(8,128)(2,1)S(1)}, u32[]{:S(2)}, u32[]{:S(2)}) collective-permute-start(bf16[128,1024]{1,0:T(8,128)(2,1)S(1)} %get-tuple-element.80), channel_id=1, source_target_pairs={{0,1},{1,0},{2,3},{3,2},{4,5},{5,4},{6,7},{7,6},{8,9},{9,8},{10,11... | collective-permute-start | bytes 786440 | tf_op jit(solution)/shard_map/ppermute | solution.py:449
  70.0 2.1 %collective-permute-start.18 = (bf16[128,1024]{1,0:T(8,128)(2,1)S(1)}, bf16[128,1024]{1,0:T(8,128)(2,1)S(1)}, u32[]{:S(2)}, u32[]{:S(2)}) collective-permute-start(bf16[128,1024]{1,0:T(8,128)(2,1)S(1)} %get-tuple-element.81), channel_id=1, source_target_pairs={{0,1},{1,0},{2,3},{3,2},{4,5},{5,4},{6,7},{7,6},{8,9},{9,8},{10,11... | collective-permute-start | bytes 786440 | tf_op jit(solution)/shard_map/ppermute | solution.py:449
  70.4 1.7 %collective-permute-start.19 = (bf16[128,1024]{1,0:T(8,128)(2,1)S(1)}, bf16[128,1024]{1,0:T(8,128)(2,1)S(1)}, u32[]{:S(2)}, u32[]{:S(2)}) collective-permute-start(bf16[128,1024]{1,0:T(8,128)(2,1)S(1)} %get-tuple-element.82), channel_id=1, source_target_pairs={{0,1},{1,0},{2,3},{3,2},{4,5},{5,4},{6,7},{7,6},{8,9},{9,8},{10,11... | collective-permute-start | bytes 786440 | tf_op jit(solution)/shard_map/ppermute | solution.py:449
  70.8 1.5 %collective-permute-start.20 = (bf16[128,1024]{1,0:T(8,128)(2,1)S(1)}, bf16[128,1024]{1,0:T(8,128)(2,1)S(1)}, u32[]{:S(2)}, u32[]{:S(2)}) collective-permute-start(bf16[128,1024]{1,0:T(8,128)(2,1)S(1)} %get-tuple-element.83), channel_id=1, source_target_pairs={{0,1},{1,0},{2,3},{3,2},{4,5},{5,4},{6,7},{7,6},{8,9},{9,8},{10,11... | collective-permute-start | bytes 786440 | tf_op jit(solution)/shard_map/ppermute | solution.py:449
  71.1 1.5 %collective-permute-start.21 = (bf16[128,1024]{1,0:T(8,128)(2,1)S(1)}, bf16[128,1024]{1,0:T(8,128)(2,1)S(1)}, u32[]{:S(2)}, u32[]{:S(2)}) collective-permute-start(bf16[128,1024]{1,0:T(8,128)(2,1)S(1)} %get-tuple-element.84), channel_id=1, source_target_pairs={{0,1},{1,0},{2,3},{3,2},{4,5},{5,4},{6,7},{7,6},{8,9},{9,8},{10,11... | collective-permute-start | bytes 786440 | tf_op jit(solution)/shard_map/ppermute | solution.py:449
